TPU v7x, 32 devices: a whole 2x2x4 slice. The times are simulated.
32 devices in a mesh: dp: 8 (over y, x, core), section: 4 (over z).
Axes of the slice: x: 2, y: 2, z: 4, core: 2. Of those that a mesh axis runs over, the one named last changes fastest.
Arguments:
- hidden_in: bfloat16 [4, 1024, 2048], P('section', 'dp'), may hold values from -80 to 80
- queries: bfloat16 [4, 1024, 2048], P('section', 'dp'), may hold values from -20 to 20
- keys: bfloat16 [4, 1024, 512], P('section', 'dp'), may hold values from -6 to 6
- segments: int32 [8, 128], P('dp'), may hold values from 0 to 3, as said below
- value_weight: bfloat16 [4, 2048, 512], P('section'), may hold values from -0.125 to 0.125
- norm_gain: float32 [4, 2048], P('section'), may hold values from 0.25 to 1.75
- upstream: bfloat16 [1024, 2048], P('dp'), may hold values from -6 to 6
Outputs:
- input_grads: bfloat16 [4, 1024, 2048], P('section', 'dp')
- value_weight_grads: float32 [4, 2048, 512], P('section', 'dp')
- gain_grads: float32 [4, 2048], P('section', 'dp')
Inputs may be any that keep to these rules, and one draw needn't show every extreme that they name: `segments`: within each aligned block of 64 list-order tokens of a replica the list ids run from 0 to 3 in order, never falling; each of the 4 lists has 1 to 48 tokens and one has exactly 48.
All inputs are finite; a program needn't handle non-finite values.
Results may differ from a plain program's by a relative error of at most 0.03.
Values may be sent and summed in bfloat16 or wider, within the bound.
No kernel may reach another device: no remote copies, remote signals or barrier semaphores. Data moves between devices by JAX's collectives and lax.ppermute only.
A program may use at most 64 MiB of HBM per device.

v0:
```python
import jax
import jax.numpy as jnp
from jax import lax
from jax.sharding import PartitionSpec as P

KEY_VALUE_HEADS = 4
HEAD_FEATURES = 128
MICRO_ROWS = 64
MICRO = 2


epsilon = 1e-06
masked_score = -1e30


def passed_along(block, axis, distance):
    devices = range(lax.axis_size(axis))
    route = [(i - distance, i) for i in devices if i - distance in devices]
    return lax.ppermute(block, axis, route)


def attention_probs(query_tile_block, key_tile_block, list_block):
    block_row_count = query_tile_block.shape[0]
    group_width = query_tile_block.shape[1] // key_tile_block.shape[1]
    query_grid4 = query_tile_block.reshape(
        block_row_count, KEY_VALUE_HEADS, group_width, HEAD_FEATURES
    )
    key_grid3 = key_tile_block.reshape(block_row_count, KEY_VALUE_HEADS, HEAD_FEATURES)
    scores = jnp.einsum(
        "ikgd,jkd->kgij", query_grid4, key_grid3, preferred_element_type=jnp.float32
    ) * HEAD_FEATURES ** (-0.5)
    positions = lax.iota(jnp.int32, block_row_count)
    allowed = (list_block[:, None] == list_block[None, :]) & (
        positions[None, :] <= positions[:, None]
    )
    scores = jnp.where(allowed, scores, masked_score)
    exp_scores = jnp.exp(scores - jnp.max(scores, axis=-1, keepdims=True))
    return (exp_scores / jnp.sum(exp_scores, axis=-1, keepdims=True)).astype(jnp.bfloat16)


def on_device(hidden_in, queries, keys, segments, value_weight, norm_gain, upstream):
    hidden_list, query_list, key_list = (
        lax.all_to_all(hidden_in, "dp", split_axis=1, concat_axis=1, tiled=True),
        lax.all_to_all(queries, "dp", split_axis=1, concat_axis=1, tiled=True),
        lax.all_to_all(keys, "dp", split_axis=1, concat_axis=1, tiled=True),
    )
    x_rows = hidden_list[0]
    query_rows = query_list[0]
    key_rows = key_list[0]
    list_rows = segments[0]
    value_proj = value_weight[0]
    gain_row = norm_gain[0]
    row_count, model_width = x_rows.shape
    kv_width = key_rows.shape[1]
    group_width = model_width // kv_width
    section_index = lax.axis_index("section")
    section_last = lax.axis_size("section") - 1
    tick_count = MICRO + section_last
    grad_scale = float(row_count * lax.axis_size("dp")) ** (-0.5)
    x_wide = x_rows.astype(jnp.float32)
    inv_rms = lax.rsqrt(jnp.mean(x_wide * x_wide, axis=1, keepdims=True) + epsilon)
    x_norm = x_wide * inv_rms
    normed = (x_norm * gain_row).astype(jnp.bfloat16)

    def block_probs(micro_index):
        row_start = micro_index * MICRO_ROWS
        return attention_probs(
            lax.dynamic_slice_in_dim(query_rows, row_start, MICRO_ROWS, 0),
            lax.dynamic_slice_in_dim(key_rows, row_start, MICRO_ROWS, 0),
            lax.dynamic_slice_in_dim(list_rows, row_start, MICRO_ROWS, 0),
        )

    stored_probs = lax.map(block_probs, jnp.arange(MICRO, dtype=jnp.int32))

    def probs_for(micro_index):
        return lax.dynamic_index_in_dim(stored_probs, micro_index, 0, keepdims=False)

    def run_block(gradient_block, micro_index, buffers):
        input_all, values_all, gain_total, weight_total = buffers
        row_start = micro_index * MICRO_ROWS
        block_weights = probs_for(micro_index)
        gradient_grid4 = gradient_block.reshape(
            MICRO_ROWS, KEY_VALUE_HEADS, group_width, HEAD_FEATURES
        )
        value_gradient = jnp.einsum(
            "kgij,ikgd->jkd", block_weights, gradient_grid4, preferred_element_type=jnp.float32
        )
        value_gradient = value_gradient.reshape(MICRO_ROWS, kv_width).astype(jnp.bfloat16)
        x_block = lax.dynamic_slice_in_dim(x_norm, row_start, MICRO_ROWS, 0)
        inv_block = lax.dynamic_slice_in_dim(inv_rms, row_start, MICRO_ROWS, 0)
        normed_grad = lax.dot_general(
            value_gradient, value_proj, (((1,), (1,)), ((), ())), preferred_element_type=jnp.float32
        )
        scaled = normed_grad * gain_row
        inner_mean = jnp.mean(x_block * scaled, axis=1, keepdims=True)
        input_grad = (
            gradient_block.astype(jnp.float32) + inv_block * (scaled - x_block * inner_mean)
        ).astype(jnp.bfloat16)
        gain_total = gain_total + jnp.sum(x_block * normed_grad, axis=0)
        normed_block = lax.dynamic_slice_in_dim(normed, row_start, MICRO_ROWS, 0)
        weight_total = weight_total + lax.dot_general(
            normed_block,
            value_gradient,
            (((0,), (0,)), ((), ())),
            preferred_element_type=jnp.float32,
        )
        input_all = lax.dynamic_update_slice_in_dim(input_all, input_grad, row_start, 0)
        values_all = lax.dynamic_update_slice_in_dim(values_all, value_gradient, row_start, 0)
        return (input_grad, (input_all, values_all, gain_total, weight_total))

    def spare_block(gradient_block, micro_index, buffers):
        return (jnp.zeros_like(gradient_block), buffers)

    def tick_step(tick_index, loop_state):
        received, buffers = loop_state
        micro_index = tick_index - (section_last - section_index)
        is_live = (micro_index >= 0) & (micro_index < MICRO)
        micro_index = jnp.clip(micro_index, 0, MICRO - 1)
        from_top = lax.dynamic_slice_in_dim(upstream, micro_index * MICRO_ROWS, MICRO_ROWS, 0)
        gradient_block = jnp.where(section_index == section_last, from_top, received)
        handed, buffers = lax.cond(
            is_live, run_block, spare_block, gradient_block, micro_index, buffers
        )
        received = passed_along(handed, "section", -1)
        return (received, buffers)

    weight_init = jnp.zeros((model_width, kv_width), jnp.float32)
    buffers = (
        jnp.zeros((row_count, model_width), jnp.bfloat16),
        jnp.zeros((row_count, kv_width), jnp.bfloat16),
        jnp.zeros((model_width,), jnp.float32),
        weight_init,
    )
    received = jnp.zeros((MICRO_ROWS, model_width), jnp.bfloat16)
    received, buffers = lax.fori_loop(0, tick_count, tick_step, (received, buffers))
    input_all, values_all, gain_total, weight_total = buffers
    input_stored = lax.all_to_all(input_all, "dp", split_axis=0, concat_axis=0, tiled=True)
    weight_sum, gain_sum = (
        lax.psum_scatter(weight_total, "dp", scatter_dimension=0, tiled=True),
        lax.psum_scatter(gain_total, "dp", scatter_dimension=0, tiled=True),
    )
    return (input_stored[None], (weight_sum * grad_scale)[None], (gain_sum * grad_scale)[None])


def solution(mesh):
    in_specs = (
        P("section", "dp", None),
        P("section", "dp", None),
        P("section", "dp", None),
        P("dp", None),
        P("section", None, None),
        P("section", None),
        P("dp", None),
    )
    out_specs = (P("section", "dp", None), P("section", "dp", None), P("section", "dp"))
    return jax.shard_map(
        on_device, mesh=mesh, in_specs=in_specs, out_specs=out_specs, check_vma=False
    )
```

profile of v0, /device:TPU:0, one launch (start us, length us, event | category | flops | bytes accessed | tf_op | source)
XLA Modules:
  0.0 209.6 jit_solution(16432359423995353240)
XLA Ops:
  8.9 1.4 reduce.1
  11.0 5.2 %all-to-all-start.1 = ((bf16[8,2,4096]{2,1,0:T(2,128)(2,1)}), bf16[8,2,4096]{2,1,0:T(2,128)(2,1)S(1)}, u32[]{:S(2)}, u32[]{:S(2)}) async-start(bf16[8,2,4096]{2,1,0:T(2,128)(2,1)} %reshape.64), calls=%async_computation.1 | async-start | bytes 262144 | tf_op jit(solution)/shard_map/all_to_all | solution.py:45
  16.2 1.9 copy.76
  18.0 3.7 %reduce = bf16[128,2048]{1,0:T(8,128)(2,1)S(1)} reduce(bf16[128,1,2048]{2,1,0:T(2,128)(2,1)S(1)} %bitcast.84, bf16[]{:T(256)} %broadcast.58), dimensions={1}, to_apply=%bitcast.70.reduce_sub_computation | reduce | bytes 1048578
  22.9 4.2 %all-to-all-start = ((bf16[8,2,16384]{2,1,0:T(2,128)(2,1)}), bf16[8,2,16384]{2,1,0:T(2,128)(2,1)S(1)}, u32[]{:S(2)}, u32[]{:S(2)}) async-start(bf16[8,2,16384]{2,1,0:T(2,128)(2,1)} %reshape.62), calls=%async_computation | async-start | bytes 1048576 | tf_op jit(solution)/shard_map/all_to_all | solution.py:43
  27.9 3.7 %reduce.2 = bf16[128,2048]{1,0:T(8,128)(2,1)S(1)} reduce(bf16[128,1,2048]{2,1,0:T(2,128)(2,1)S(1)} %bitcast.83, bf16[]{:T(256)} %broadcast.58), dimensions={1}, to_apply=%bitcast.69.reduce_sub_computation | reduce | bytes 1048578
  32.8 4.0 %all-to-all-done = bf16[8,2,16384]{2,1,0:T(2,128)(2,1)S(1)} async-done(((bf16[8,2,16384]{2,1,0:T(2,128)(2,1)}), bf16[8,2,16384]{2,1,0:T(2,128)(2,1)S(1)}, u32[]{:S(2)}, u32[]{:S(2)}) %all-to-all-start) | async-done | bytes 524320 | tf_op jit(solution)/shard_map/all_to_all | solution.py:43
  36.9 3.5 %all-to-all-start.2 = ((bf16[8,2,16384]{2,1,0:T(2,128)(2,1)}), bf16[8,2,16384]{2,1,0:T(2,128)(2,1)S(1)}, u32[]{:S(2)}, u32[]{:S(2)}) async-start(bf16[8,2,16384]{2,1,0:T(2,128)(2,1)} %reshape.66), calls=%async_computation.2 | async-start | bytes 1048576 | tf_op jit(solution)/shard_map/all_to_all | solution.py:44
  41.7 8.3 %all-to-all-done.2 = bf16[8,2,16384]{2,1,0:T(2,128)(2,1)S(1)} async-done(((bf16[8,2,16384]{2,1,0:T(2,128)(2,1)}), bf16[8,2,16384]{2,1,0:T(2,128)(2,1)S(1)}, u32[]{:S(2)}, u32[]{:S(2)}) %all-to-all-start.2) | async-done | bytes 524320 | tf_op jit(solution)/shard_map/all_to_all | solution.py:44
  50.9 5.7 %while.31 = (s32[]{:T(128)}, bf16[2,4,4,64,64]{3,4,2,1,0:T(8,128)(2,1)}, s32[2]{0:T(128)S(1)}, s32[128]{0:T(128)S(1)}, bf16[128,512]{1,0:T(8,128)(2,1)S(1)}, /*i...) while((s32[]{:T(128)}, bf16[2,4,4,64,64]{3,4,2,1,0:T(8,128)(2,1)}, ...), condition=%wide.region_3.4_spmd, body=%wide.region_0.3_spmd.sunk | while | flops 17119364 | bytes 1910187 | solution.py:73
  56.6 2.6 %multiply_convert_fusion = (bf16[128,2048]{1,0:T(8,128)(2,1)}, f32[128,2048]{1,0:T(8,128)S(1)}) fusion(f32[2048]{0:T(1024)S(1)} %bitcast.90, f32[128]{0:T(128)S(1)} %get-tuple-element.536, bf16[1,128,2048]{2,0,1:T(2,128)(2,1)} %bitcast.80), kind=kLoop, calls=%fused_computation.46 | loop fusion | flops 1048576 | bytes 2105856 | tf_op jit(solution)/shard_map/convert_element_type | solution.py:63
  59.2 2.5 %broadcast_in_dim.43 = f32[2048,512]{1,0:T(8,128)} broadcast(f32[]{:T(128)} %constant.126.clone.1), dimensions={} | broadcast | bytes 4194308 | tf_op jit(solution)/shard_map/broadcast_in_dim | solution.py:127
  63.2 84.0 %while.32 = (s32[]{:T(128)}, bf16[64,2048]{1,0:T(8,128)(2,1)}, bf16[128,2048]{1,0:T(8,128)(2,1)}, f32[2048]{0:T(1024)S(1)}, f32[2048,512]{1,0:T(8,128)}, /*index...) while((s32[]{:T(128)}, bf16[64,2048]{1,0:T(8,128)(2,1)}, ...), condition=%wide.region_10.11_spmd, body=%wide.region_5.10_spmd.sunk | while | flops 287997952 | bytes 53463388 | solution.py:135
  63.9 1.3 collective-permute-start
  65.2 7.2 %collective-permute-done = bf16[64,2048]{1,0:T(8,128)(2,1)S(1)} collective-permute-done((bf16[64,2048]{1,0:T(8,128)(2,1)}, bf16[64,2048]{1,0:T(8,128)(2,1)S(1)}, u32[]{:S(2)}, u32[]{:S(2)}) %collective-permute-start) | collective-permute-done | bytes 262176 | tf_op jit(solution)/shard_map/while/body/eval_jaxpr/ppermute | solution.py:19
  73.8 1.3 collective-permute-start
  75.1 7.2 %collective-permute-done = bf16[64,2048]{1,0:T(8,128)(2,1)S(1)} collective-permute-done((bf16[64,2048]{1,0:T(8,128)(2,1)}, bf16[64,2048]{1,0:T(8,128)(2,1)S(1)}, u32[]{:S(2)}, u32[]{:S(2)}) %collective-permute-start) | collective-permute-done | bytes 262176 | tf_op jit(solution)/shard_map/while/body/eval_jaxpr/ppermute | solution.py:19
  83.7 1.3 collective-permute-start
  85.0 27.1 %collective-permute-done = bf16[64,2048]{1,0:T(8,128)(2,1)S(1)} collective-permute-done((bf16[64,2048]{1,0:T(8,128)(2,1)}, bf16[64,2048]{1,0:T(8,128)(2,1)S(1)}, u32[]{:S(2)}, u32[]{:S(2)}) %collective-permute-start) | collective-permute-done | bytes 262176 | tf_op jit(solution)/shard_map/while/body/eval_jaxpr/ppermute | solution.py:19
  112.8 8.0 %conditional.2 = (bf16[64,2048]{1,0:T(8,128)(2,1)}, bf16[128,2048]{1,0:T(8,128)(2,1)}, f32[2048]{0:T(1024)S(1)}, f32[2048,512]{1,0:T(8,128)}) conditional(s32[]{:T(128)} %convert_element_type.58, (bf16[128,2048]{1,0:T(8,128)(2,1)}, f32[2048]{0:T(1024)S(1)}, f32[2048,512]{1,0:T(8,128)}) %tuple.75, (pred[]{:T(512)}, s32[]{:T(128)}, ...), branch_computations={%region_6.6_spmd, %region_7.9_spmd} | conditional | flops 287997952 | bytes 51365844 | solution.py:121
  114.8 1.4 fusion.24
  119.0 1.9 copy-done.1
  120.9 1.3 collective-permute-start
  122.2 7.2 %collective-permute-done = bf16[64,2048]{1,0:T(8,128)(2,1)S(1)} collective-permute-done((bf16[64,2048]{1,0:T(8,128)(2,1)}, bf16[64,2048]{1,0:T(8,128)(2,1)S(1)}, u32[]{:S(2)}, u32[]{:S(2)}) %collective-permute-start) | collective-permute-done | bytes 262176 | tf_op jit(solution)/shard_map/while/body/eval_jaxpr/ppermute | solution.py:19
  130.0 8.0 %conditional.2 = (bf16[64,2048]{1,0:T(8,128)(2,1)}, bf16[128,2048]{1,0:T(8,128)(2,1)}, f32[2048]{0:T(1024)S(1)}, f32[2048,512]{1,0:T(8,128)}) conditional(s32[]{:T(128)} %convert_element_type.58, (bf16[128,2048]{1,0:T(8,128)(2,1)}, f32[2048]{0:T(1024)S(1)}, f32[2048,512]{1,0:T(8,128)}) %tuple.75, (pred[]{:T(512)}, s32[]{:T(128)}, ...), branch_computations={%region_6.6_spmd, %region_7.9_spmd} | conditional | flops 287997952 | bytes 51365844 | solution.py:121
  132.0 1.4 fusion.24
  136.2 1.9 copy-done.1
  139.4 7.2 %collective-permute-done = bf16[64,2048]{1,0:T(8,128)(2,1)S(1)} collective-permute-done((bf16[64,2048]{1,0:T(8,128)(2,1)}, bf16[64,2048]{1,0:T(8,128)(2,1)S(1)}, u32[]{:S(2)}, u32[]{:S(2)}) %collective-permute-start) | collective-permute-done | bytes 262176 | tf_op jit(solution)/shard_map/while/body/eval_jaxpr/ppermute | solution.py:19
  147.3 6.9 %all-to-all-start.3 = ((bf16[8,16,2048]{2,1,0:T(8,128)(2,1)}), bf16[8,16,2048]{2,1,0:T(8,128)(2,1)S(1)}, u32[]{:S(2)}, u32[]{:S(2)}) async-start(bf16[8,16,2048]{2,1,0:T(8,128)(2,1)} %bitcast.16), calls=%async_computation.3 | async-start | bytes 1048576 | tf_op jit(solution)/shard_map/all_to_all | solution.py:137
  155.4 15.3 %all-reduce = f32[2048]{0:T(1024)S(1)} all-reduce(f32[2048]{0:T(1024)S(1)} %get-tuple-element.488), channel_id=3, replica_groups=mesh['dp'=8,'section'=4] {'dp'}, use_global_device_ids=true, to_apply=%region_12.13.clone | all-reduce | flops 2048 | bytes 16384
  171.3 28.8 %reduce-scatter.2.cloned.1.call-done = f32[256,512]{1,0:T(8,128)} async-done(((f32[2048,512]{1,0:T(8,128)}), f32[256,512]{1,0:T(8,128)}) %reduce-scatter.2.cloned.1.call-update) | async-done | bytes 524304 | tf_op jit(solution)/shard_map/reduce_scatter | solution.py:139
  200.1 1.9 multiply_bitcast_fusion
  (96 shorter events, 34.1 us)
Async XLA Ops:
  7.2 19.9 %copy-start.7 = (bf16[1,128,2048]{2,1,0:T(8,128)(2,1)S(1)}, bf16[1,128,2048]{2,1,0:T(8,128)(2,1)}, u32[]{:S(2)}) copy-start(bf16[1,128,2048]{2,1,0:T(8,128)(2,1)} %param.14) | copy-start | bytes 1572868
  11.0 11.9 %all-to-all-start.1 = ((bf16[8,2,4096]{2,1,0:T(2,128)(2,1)}), bf16[8,2,4096]{2,1,0:T(2,128)(2,1)S(1)}, u32[]{:S(2)}, u32[]{:S(2)}) async-start(bf16[8,2,4096]{2,1,0:T(2,128)(2,1)} %reshape.64), calls=%async_computation.1 | async-start | bytes 262144 | tf_op jit(solution)/shard_map/all_to_all | solution.py:45
  22.9 13.9 %all-to-all-start = ((bf16[8,2,16384]{2,1,0:T(2,128)(2,1)}), bf16[8,2,16384]{2,1,0:T(2,128)(2,1)S(1)}, u32[]{:S(2)}, u32[]{:S(2)}) async-start(bf16[8,2,16384]{2,1,0:T(2,128)(2,1)} %reshape.62), calls=%async_computation | async-start | bytes 1048576 | tf_op jit(solution)/shard_map/all_to_all | solution.py:43
  31.6 19.2 %copy-start.8 = (s32[1,128]{1,0:T(1,128)S(1)}, s32[1,128]{1,0:T(1,128)}, u32[]{:S(2)}) copy-start(s32[1,128]{1,0:T(1,128)} %param.16) | copy-start | bytes 1540
  36.9 13.2 %all-to-all-start.2 = ((bf16[8,2,16384]{2,1,0:T(2,128)(2,1)}), bf16[8,2,16384]{2,1,0:T(2,128)(2,1)S(1)}, u32[]{:S(2)}, u32[]{:S(2)}) async-start(bf16[8,2,16384]{2,1,0:T(2,128)(2,1)} %reshape.66), calls=%async_computation.2 | async-start | bytes 1048576 | tf_op jit(solution)/shard_map/all_to_all | solution.py:44
  40.4 159.7 %reduce-scatter.2.cloned.1.call-start = ((), (), s32[]{:S(2)}) async-start(), calls=%async_computation.5 | async-start | bytes 4718592 | tf_op jit(solution)/shard_map/reduce_scatter | solution.py:139
  41.3 9.6 %copy-start.4 = (bf16[128,1,2048]{2,1,0:T(2,128)(2,1)}, bf16[128,1,2048]{2,1,0:T(2,128)(2,1)S(1)}, u32[]{:S(2)}) copy-start(bf16[128,1,2048]{2,1,0:T(2,128)(2,1)S(1)} %reshape.63) | copy-start | bytes 1572868
  50.9 5.7 %copy-start.6 = (f32[1,2048]{1,0:T(1,128)S(1)}, f32[1,2048]{1,0:T(1,128)}, u32[]{:S(2)}) copy-start(f32[1,2048]{1,0:T(1,128)} %param.18) | copy-start | bytes 24580
  56.6 6.6 %copy-start.2 = (bf16[1,2048,512]{2,1,0:T(8,128)(2,1)S(1)}, bf16[1,2048,512]{2,1,0:T(8,128)(2,1)}, u32[]{:S(2)}) copy-start(bf16[1,2048,512]{2,1,0:T(8,128)(2,1)} %param.17) | copy-start | bytes 6291460
  63.9 8.5 %collective-permute-start = (bf16[64,2048]{1,0:T(8,128)(2,1)}, bf16[64,2048]{1,0:T(8,128)(2,1)S(1)}, u32[]{:S(2)}, u32[]{:S(2)}) collective-permute-start(bf16[64,2048]{1,0:T(8,128)(2,1)} %get-tuple-element.664), channel_id=1, source_target_pairs={{1,0},{2,1},{3,2},{5,4},{6,5},{7,6},{9,8},{10,9},{11,10},{13,12},{... | collective-permute-start | bytes 786440 | tf_op jit(solution)/shard_map/while/body/eval_jaxpr/ppermute | solution.py:19
  72.4 0.7 copy-start.3
  73.8 8.5 %collective-permute-start = (bf16[64,2048]{1,0:T(8,128)(2,1)}, bf16[64,2048]{1,0:T(8,128)(2,1)S(1)}, u32[]{:S(2)}, u32[]{:S(2)}) collective-permute-start(bf16[64,2048]{1,0:T(8,128)(2,1)} %get-tuple-element.664), channel_id=1, source_target_pairs={{1,0},{2,1},{3,2},{5,4},{6,5},{7,6},{9,8},{10,9},{11,10},{13,12},{... | collective-permute-start | bytes 786440 | tf_op jit(solution)/shard_map/while/body/eval_jaxpr/ppermute | solution.py:19
  82.3 0.7 copy-start.3
  83.7 28.4 %collective-permute-start = (bf16[64,2048]{1,0:T(8,128)(2,1)}, bf16[64,2048]{1,0:T(8,128)(2,1)S(1)}, u32[]{:S(2)}, u32[]{:S(2)}) collective-permute-start(bf16[64,2048]{1,0:T(8,128)(2,1)} %get-tuple-element.664), channel_id=1, source_target_pairs={{1,0},{2,1},{3,2},{5,4},{6,5},{7,6},{9,8},{10,9},{11,10},{13,12},{... | collective-permute-start | bytes 786440 | tf_op jit(solution)/shard_map/while/body/eval_jaxpr/ppermute | solution.py:19
  112.1 0.7 copy-start.3
  114.8 3.4 %copy-start = (f32[2048,512]{1,0:T(8,128)S(1)}, f32[2048,512]{1,0:T(8,128)}, u32[]{:S(2)}) copy-start(f32[2048,512]{1,0:T(8,128)} %get-tuple-element.457) | copy-start | bytes 12582916 | tf_op jit(solution)/shard_map/while/body/eval_jaxpr/cond
  114.8 3.4 %copy-start.5 = (bf16[128,2048]{1,0:T(8,128)(2,1)S(1)}, bf16[128,2048]{1,0:T(8,128)(2,1)}, u32[]{:S(2)}) copy-start(bf16[128,2048]{1,0:T(8,128)(2,1)} %get-tuple-element.458) | copy-start | bytes 1572868 | tf_op jit(solution)/shard_map/while/body/eval_jaxpr/cond
  118.9 1.9 copy-start.1
  120.9 8.5 %collective-permute-start = (bf16[64,2048]{1,0:T(8,128)(2,1)}, bf16[64,2048]{1,0:T(8,128)(2,1)S(1)}, u32[]{:S(2)}, u32[]{:S(2)}) collective-permute-start(bf16[64,2048]{1,0:T(8,128)(2,1)} %get-tuple-element.664), channel_id=1, source_target_pairs={{1,0},{2,1},{3,2},{5,4},{6,5},{7,6},{9,8},{10,9},{11,10},{13,12},{... | collective-permute-start | bytes 786440 | tf_op jit(solution)/shard_map/while/body/eval_jaxpr/ppermute | solution.py:19
  129.3 0.7 copy-start.3
  132.0 3.4 %copy-start = (f32[2048,512]{1,0:T(8,128)S(1)}, f32[2048,512]{1,0:T(8,128)}, u32[]{:S(2)}) copy-start(f32[2048,512]{1,0:T(8,128)} %get-tuple-element.457) | copy-start | bytes 12582916 | tf_op jit(solution)/shard_map/while/body/eval_jaxpr/cond
  132.0 3.4 %copy-start.5 = (bf16[128,2048]{1,0:T(8,128)(2,1)S(1)}, bf16[128,2048]{1,0:T(8,128)(2,1)}, u32[]{:S(2)}) copy-start(bf16[128,2048]{1,0:T(8,128)(2,1)} %get-tuple-element.458) | copy-start | bytes 1572868 | tf_op jit(solution)/shard_map/while/body/eval_jaxpr/cond
  136.2 1.9 copy-start.1
  138.1 8.5 %collective-permute-start = (bf16[64,2048]{1,0:T(8,128)(2,1)}, bf16[64,2048]{1,0:T(8,128)(2,1)S(1)}, u32[]{:S(2)}, u32[]{:S(2)}) collective-permute-start(bf16[64,2048]{1,0:T(8,128)(2,1)} %get-tuple-element.664), channel_id=1, source_target_pairs={{1,0},{2,1},{3,2},{5,4},{6,5},{7,6},{9,8},{10,9},{11,10},{13,12},{... | collective-permute-start | bytes 786440 | tf_op jit(solution)/shard_map/while/body/eval_jaxpr/ppermute | solution.py:19
  146.6 0.7 copy-start.3
  147.3 6.9 %copy-start.9 = (u32[32]{0:T(128)S(1)}, u32[32]{0:T(128)}, u32[]{:S(2)}) copy-start(u32[32]{0:T(128)} %constant.141) | copy-start | bytes 388
  147.3 24.0 %all-to-all-start.3 = ((bf16[8,16,2048]{2,1,0:T(8,128)(2,1)}), bf16[8,16,2048]{2,1,0:T(8,128)(2,1)S(1)}, u32[]{:S(2)}, u32[]{:S(2)}) async-start(bf16[8,16,2048]{2,1,0:T(8,128)(2,1)} %bitcast.16), calls=%async_computation.3 | async-start | bytes 1048576 | tf_op jit(solution)/shard_map/all_to_all | solution.py:137
Sparse Core Ops, SparseCore 0:
  147.4 52.6 reduce-scatter.1
where the time goes:
time: 210 us
  waiting for transfers between devices  97 us (46%)
  local copies, waits for them, and re-layouts  27.6 us (13%)
  starting transfers between devices  26.3 us (13%)
  other arithmetic  18.6 us (9%)
  blocking collectives  15.3 us (7%)
  between operations  14.9 us (7%)
  matrix products  8.4 us (4%)
    ppermute x5, waiting for transfers between devices, passed_along(): return lax.ppermute(block, axis, route)  55.8 us
    reduce_scatter x1, waiting for transfers between devices, on_device(): lax.psum_scatter(weight_total, 'dp', scatter_dimension=0, tiled=True)  28.8 us
    unnamed x1, blocking collectives  15.3 us
    unnamed x26, local copies, waits for them, and re-layouts  10.3 us
    unnamed x3, other arithmetic  8.82 us
    all_to_all x1, waiting for transfers between devices, on_device(): lax.all_to_all(queries, 'dp', split_axis=1, concat_axis=1, tiled=True)  8.32 us
    all_to_all x1, starting transfers between devices, on_device(): lax.all_to_all(input_all, 'dp', split_axis=0, concat_axis=0, tiled=True)  6.85 us
    ppermute x5, starting transfers between devices, passed_along(): return lax.ppermute(block, axis, route)  6.4 us
  transfers between devices with their start and end apart: 10, of which 8 were waited for; matrix products, arithmetic and copies ran while one was open for 7% of the time, Pallas kernels for 0%

commit v1 on v0

v1 whole, which is shorter than its diff:
```python
import functools

import jax
import jax.numpy as jnp
from jax import lax
from jax.experimental import pallas as pl
from jax.experimental.pallas import tpu as pltpu
from jax.sharding import PartitionSpec as P

HEAD_FEATURES = 128
BLOCK = 64
EPSILON = 1e-06
MASKED = -1e30
UNROLLED = 8
VMEM = pl.BlockSpec(memory_space=pltpu.VMEM)
SMEM = pl.BlockSpec(memory_space=pltpu.SMEM)


def probs_kernel(model_width, kv_width, rows_ref, seg_row_ref, seg_column_ref, probs_ref, inv_ref):
    heads = model_width // kv_width
    shape = (BLOCK, heads * BLOCK)
    key_at = lax.broadcasted_iota(jnp.int32, shape, 0)
    query_at = lax.rem(lax.broadcasted_iota(jnp.int32, shape, 1), BLOCK)
    allowed = (seg_column_ref[...] == seg_row_ref[...]) & (key_at <= query_at)
    for c in range(kv_width // HEAD_FEATURES):
        first = c * heads * HEAD_FEATURES
        query_stack = jnp.concatenate(
            [
                rows_ref[:, first + h * HEAD_FEATURES : first + (h + 1) * HEAD_FEATURES]
                for h in range(heads)
            ],
            axis=0,
        )
        key_first = model_width + c * HEAD_FEATURES
        keys = rows_ref[:, key_first : key_first + HEAD_FEATURES]
        scores = lax.dot_general(
            keys, query_stack, (((1,), (1,)), ((), ())), preferred_element_type=jnp.float32
        ) * HEAD_FEATURES ** (-0.5)
        scores = jnp.where(allowed, scores, MASKED)
        exp_scores = jnp.exp(scores - jnp.max(scores, axis=0, keepdims=True))
        total = jnp.sum(exp_scores, axis=0, keepdims=True)
        probs_ref[c] = (exp_scores / total).astype(jnp.bfloat16)
    x = rows_ref[:, model_width + kv_width :].astype(jnp.float32)
    mean_square = jnp.mean(x * x, axis=1, keepdims=True)
    inv_ref[...] = jnp.broadcast_to(lax.rsqrt(mean_square + EPSILON), inv_ref.shape)


def block_probs(rows, seg, model_width, kv_width):
    heads = model_width // kv_width
    return pl.pallas_call(
        functools.partial(probs_kernel, model_width, kv_width),
        out_shape=(
            jax.ShapeDtypeStruct(
                (kv_width // HEAD_FEATURES, BLOCK, heads * BLOCK), jnp.bfloat16
            ),
            jax.ShapeDtypeStruct((BLOCK, 128), jnp.float32),
        ),
        in_specs=[VMEM, VMEM, VMEM],
        out_specs=(VMEM, VMEM),
        name="probs",
    )(rows, jnp.tile(seg, heads)[None, :], seg[:, None])


def layer_kernel(
    kv_width, live_ref, grad_ref, rows_ref, probs_ref, inv_ref, weight_ref, gain_ref, *rest
):
    out_ref, value_ref = rest[-2:]
    if len(rest) == 4:

        @pl.when(live_ref[0] == 0)
        def _():
            out_ref[...] = rest[0][...]
            value_ref[...] = rest[1][...]

    @pl.when(live_ref[0] == 1)
    def _():
        model_width = grad_ref.shape[1]
        heads = model_width // kv_width
        inv = inv_ref[:, :1]
        values = []
        for c in range(kv_width // HEAD_FEATURES):
            first = c * heads * HEAD_FEATURES
            grad_stack = jnp.concatenate(
                [
                    grad_ref[:, first + h * HEAD_FEATURES : first + (h + 1) * HEAD_FEATURES]
                    for h in range(heads)
                ],
                axis=0,
            )
            values.append(
                jnp.dot(probs_ref[c], grad_stack, preferred_element_type=jnp.float32).astype(
                    jnp.bfloat16
                )
            )
        value = jnp.concatenate(values, axis=1)
        value_ref[...] = (value.astype(jnp.float32) * inv).astype(jnp.bfloat16)
        normed_grad = lax.dot_general(
            value, weight_ref[...], (((1,), (1,)), ((), ())), preferred_element_type=jnp.float32
        )
        scaled = normed_grad * gain_ref[...]
        x_norm = rows_ref[:, model_width + kv_width :].astype(jnp.float32) * inv
        inner_mean = jnp.mean(x_norm * scaled, axis=1, keepdims=True)
        out_ref[...] = (
            grad_ref[...].astype(jnp.float32) + inv * (scaled - x_norm * inner_mean)
        ).astype(jnp.bfloat16)


def layer_step(live, grad, rows, probs, inv, weight, gain, held):
    kv_width = weight.shape[1]
    operands = [live, grad, rows, probs, inv, weight, gain]
    specs = [SMEM] + [VMEM] * 6
    if held is not None:
        operands += list(held)
        specs += [VMEM] * 2
    return pl.pallas_call(
        functools.partial(layer_kernel, kv_width),
        out_shape=(
            jax.ShapeDtypeStruct(grad.shape, jnp.bfloat16),
            jax.ShapeDtypeStruct((BLOCK, kv_width), jnp.bfloat16),
        ),
        in_specs=specs,
        out_specs=(VMEM, VMEM),
        name="layer",
    )(*operands)


def weight_kernel(scale, columns_ref, value_ref, weight_ref, gain_ref, out_ref, gain_out_ref):
    total = lax.dot_general(
        columns_ref[...], value_ref[...], (((0,), (0,)), ((), ())),
        preferred_element_type=jnp.float32,
    ) * scale
    out_ref[...] = total * gain_ref[...]
    product = total * weight_ref[...].astype(jnp.float32)
    sums = lax.dot_general(
        jnp.ones((8, product.shape[1]), jnp.float32), product, (((1,), (1,)), ((), ())),
        preferred_element_type=jnp.float32, precision=lax.Precision.HIGHEST,
    )
    gain_out_ref[...] = sums[:1]


def on_device(hidden_in, queries, keys, segments, value_weight, norm_gain, upstream):
    hidden, query, key = hidden_in[0], queries[0], keys[0]
    seg, weight = segments[0], value_weight[0]
    tokens, model_width = hidden.shape
    kv_width = key.shape[1]
    replicas = lax.axis_size("dp")
    layers = lax.axis_size("section")
    half = replicas // 2
    me = lax.axis_index("dp")
    section = lax.axis_index("section")
    side = me // half
    groups = [list(range(half)), list(range(half, replicas))]
    across = [(i, (i + half) % replicas) for i in range(replicas)]
    shares = model_width // replicas

    def rows_of(array, which, axis=0):
        at = side if which == 0 else 1 - side
        return lax.dynamic_slice_in_dim(array, at * BLOCK, BLOCK, axis)

    def regroup(array):
        return lax.all_to_all(
            array, "dp", split_axis=0, concat_axis=0, axis_index_groups=groups, tiled=True
        )

    def spread(array):
        return lax.all_to_all(array, "dp", split_axis=0, concat_axis=0, tiled=True)

    rows, probs, inv, grads, segs = [], [], [], [], []
    for which in range(2):
        up = rows_of(upstream, which)
        block_seg = rows_of(seg, which)
        if which == 1:
            up = lax.ppermute(up, "dp", across)
            block_seg = lax.ppermute(block_seg, "dp", across)
        packed = jnp.concatenate(
            [rows_of(query, which), rows_of(key, which), rows_of(hidden, which)], axis=1
        )
        rows.append(regroup(packed))
        block = block_probs(rows[which], block_seg, model_width, kv_width)
        probs.append(block[0])
        inv.append(block[1])
        grads.append(up)

    def layer(tick, which, grad, kept):
        live = (section == layers - 1 - tick).astype(jnp.int32)[None]
        return layer_step(
            live, grad, rows[which], probs[which], inv[which], weight, norm_gain, kept
        )

    held = [layer(0, which, grads[which], None) for which in range(2)]
    if layers <= UNROLLED:
        for tick in range(1, layers):
            hop = [(layers - tick, layers - 1 - tick)]
            for which in range(2):
                grad = lax.ppermute(held[which][0], "section", hop)
                held[which] = layer(tick, which, grad, held[which])
    else:
        hops = [(i, i - 1) for i in range(1, layers)]

        def tick_step(tick, held):
            grads = [lax.ppermute(kept[0], "section", hops) for kept in held]
            return [layer(tick, which, grads[which], held[which]) for which in range(2)]

        held = lax.fori_loop(1, layers, tick_step, held)

    columns, values, stored = [], [], []
    for which in range(2):
        block = rows[which][:, model_width + kv_width :]
        block = block.reshape(BLOCK, replicas, shares).transpose(1, 0, 2)
        columns.append(spread(block.reshape(replicas * BLOCK, shares)))
        out, value = held[which]
        stored.append(regroup(out))
        values.append(spread(jnp.tile(value, (replicas, 1))))
    ordered = jnp.where(
        side == 0, jnp.concatenate(stored, axis=0), jnp.concatenate(stored[::-1], axis=0)
    )
    own_weight = lax.dynamic_slice_in_dim(weight, me * shares, shares, 0)
    own_gain = lax.dynamic_slice_in_dim(norm_gain[0], me * shares, shares, 0)
    scale = float(tokens * replicas) ** (-0.5)
    weight_grad, gain_grad = pl.pallas_call(
        functools.partial(weight_kernel, scale),
        out_shape=(
            jax.ShapeDtypeStruct((shares, kv_width), jnp.float32),
            jax.ShapeDtypeStruct((1, shares), jnp.float32),
        ),
        in_specs=[VMEM] * 4,
        out_specs=(VMEM, VMEM),
        name="weight_grad",
    )(
        jnp.concatenate(columns, axis=0),
        jnp.concatenate(values, axis=0),
        own_weight,
        own_gain[:, None],
    )
    return ordered[None], weight_grad[None], gain_grad


def solution(mesh):
    in_specs = (
        P("section", "dp", None),
        P("section", "dp", None),
        P("section", "dp", None),
        P("dp", None),
        P("section", None, None),
        P("section", None),
        P("dp", None),
    )
    out_specs = (P("section", "dp", None), P("section", "dp", None), P("section", "dp"))
    return jax.shard_map(
        on_device, mesh=mesh, in_specs=in_specs, out_specs=out_specs, check_vma=False
    )
```

time: 210 us -> 130 us (0.62)
  waiting for transfers between devices: 97 us -> 30.8 us
  Pallas kernels: 0 us -> 30.6 us
  other arithmetic: 18.6 us -> 4.55 us
  between operations: 14.9 us -> 0.97 us
  local copies, waits for them, and re-layouts: 27.6 us -> 18.7 us
  matrix products: 8.4 us -> 0 us
  starting transfers between devices: 26.3 us -> 33.1 us
  blocking collectives: 15.3 us -> 9.55 us
    ppermute x5 -> x8, waiting for transfers between devices: 55.8 us -> 7.69 us  [the longest x6 4.16 us: on_device(): grad = lax.ppermute(held[which][0], 'section', hop)]
    pallas_call x0 -> x11, Pallas kernels: none -> 30.6 us  [the longest x8 23.5 us: layer_step(): pl.pallas_call(functools.partial(layer_kernel, kv_width), out_shape=(jax....]
    reduce_scatter x1 -> x0, waiting for transfers between devices: 28.8 us -> none  [on_device(): lax.psum_scatter(weight_total, 'dp', scatter_dimension=0, tiled=True)]
    unnamed x1 -> x0, blocking collectives: 15.3 us -> none
    all_to_all x4 -> x7, waiting for transfers between devices: 12.3 us -> 23.1 us  [the longest x4 14.4 us: spread(): return lax.all_to_all(array, 'dp', split_axis=0, concat_axis=0, tiled=True)]
    all_to_all x0 -> x1, blocking collectives: none -> 9.55 us  [regroup(): lax.all_to_all(array, 'dp', split_axis=0, concat_axis=0, axis_index_group...]
    unnamed x3 -> x0, other arithmetic: 8.82 us -> none
    dot_general x6 -> x0, matrix products: 6.1 us -> none  [the longest x2 2.81 us: run_block(): jnp.einsum('kgij,ikgd->jkd', block_weights, gradient_grid4, preferred_ele...]
  transfers between devices with their start and end apart: 10 -> 15, of which waited for: 8 -> 6; matrix products, arithmetic and copies ran while one was open for 7% -> 10% of each run, Pallas kernels for 0% -> 21%
where the time goes in v1:
time: 130 us; the launch traced here: 128 us
  starting transfers between devices  33.1 us (25%)
  waiting for transfers between devices  30.8 us (24%)
  Pallas kernels  30.6 us (24%)
  local copies, waits for them, and re-layouts  18.7 us (14%)
  blocking collectives  9.55 us (7%)
  other arithmetic  4.55 us (4%)
    pallas_call x8, Pallas kernels, layer_step(): pl.pallas_call(functools.partial(layer_kernel, kv_width), out_shape=(jax....  23.5 us
    all_to_all x4, starting transfers between devices, spread(): return lax.all_to_all(array, 'dp', split_axis=0, concat_axis=0, tiled=True)  14.5 us
    all_to_all x4, waiting for transfers between devices, spread(): return lax.all_to_all(array, 'dp', split_axis=0, concat_axis=0, tiled=True)  14.4 us
    all_to_all x3, starting transfers between devices, regroup(): lax.all_to_all(array, 'dp', split_axis=0, concat_axis=0, axis_index_group...  10.4 us
    all_to_all x1, blocking collectives, regroup(): lax.all_to_all(array, 'dp', split_axis=0, concat_axis=0, axis_index_group...  9.55 us
    all_to_all x3, waiting for transfers between devices, regroup(): lax.all_to_all(array, 'dp', split_axis=0, concat_axis=0, axis_index_group...  8.65 us
    unnamed x30, local copies, waits for them, and re-layouts  5.74 us
    ppermute x6, starting transfers between devices, on_device(): grad = lax.ppermute(held[which][0], 'section', hop)  5.22 us
  transfers between devices with their start and end apart: 15, of which 6 were waited for; matrix products, arithmetic and copies ran while one was open for 10% of the time, Pallas kernels for 21%

profile of v1, /device:TPU:0, one launch (start us, length us, event | category | flops | bytes accessed | tf_op | source)
XLA Modules:
  0.0 128.3 jit_solution(1942668657779779255)
XLA Ops:
  0.7 1.9 %constant_dynamic-slice_fusion.10 = (bf16[64,2048]{1,0:T(8,128)(2,1)}, bf16[64,2048]{1,0:T(8,128)(2,1)S(1)}) fusion(bf16[128,2048]{1,0:T(8,128)(2,1)} %param.13, s32[]{:T(128)S(6)} %select_n.40, s32[]{:T(128)S(6)} %select_n.41), kind=kLoop, calls=%fused_computation.18 | loop fusion | bytes 1048584 | tf_op jit(solution)/shard_map/dynamic_slice | solution.py:158
  2.6 3.0 %collective-permute-start.3 = (bf16[64,2048]{1,0:T(8,128)(2,1)S(1)}, bf16[64,2048]{1,0:T(8,128)(2,1)S(1)}, u32[]{:S(2)}, u32[]{:S(2)}) collective-permute-start(bf16[64,2048]{1,0:T(8,128)(2,1)S(1)} %get-tuple-element.52), channel_id=1, source_target_pairs={{0,16},{4,20},{8,24},{12,28},{16,0},{20,4},{24,8},{28,12},{1,17},{... | collective-permute-start | bytes 786440 | tf_op jit(solution)/shard_map/ppermute | solution.py:173
  6.5 3.5 %all-to-all-start.2 = ((bf16[4,16,4608]{2,1,0:T(8,128)(2,1)}), bf16[4,16,4608]{2,1,0:T(8,128)(2,1)S(1)}, u32[]{:S(2)}, u32[]{:S(2)}) async-start(bf16[4,16,4608]{2,1,0:T(8,128)(2,1)} %pad_maximum_fusion.2), calls=%async_computation.2 | async-start | bytes 1179648 | tf_op jit(solution)/shard_map/all_to_all | solution.py:161
  10.9 8.6 %all-to-all-done.2 = bf16[4,16,4608]{2,1,0:T(8,128)(2,1)S(1)} async-done(((bf16[4,16,4608]{2,1,0:T(8,128)(2,1)}), bf16[4,16,4608]{2,1,0:T(8,128)(2,1)S(1)}, u32[]{:S(2)}, u32[]{:S(2)}) %all-to-all-start.2) | async-done | bytes 589856 | tf_op jit(solution)/shard_map/all_to_all | solution.py:161
  19.5 3.5 %all-to-all-start = ((bf16[4,16,4608]{2,1,0:T(8,128)(2,1)}), bf16[4,16,4608]{2,1,0:T(8,128)(2,1)S(1)}, u32[]{:S(2)}, u32[]{:S(2)}) async-start(bf16[4,16,4608]{2,1,0:T(8,128)(2,1)} %pad_maximum_fusion.1), calls=%async_computation | async-start | bytes 1179648 | tf_op jit(solution)/shard_map/all_to_all | solution.py:161
  23.1 3.5 %collective-permute-done.4 = s32[64]{0:T(128)S(1)} collective-permute-done((s32[64]{0:T(128)S(1)}, s32[64]{0:T(128)S(1)}, u32[]{:S(2)}, u32[]{:S(2)}) %collective-permute-start.4) | collective-permute-done | bytes 288 | tf_op jit(solution)/shard_map/ppermute | solution.py:174
  28.0 2.0 %probs.3 = (bf16[4,64,256]{2,1,0:T(8,128)(2,1)}, f32[64,128]{1,0:T(8,128)}) custom-call(bf16[64,4608]{1,0:T(8,128)(2,1)} %bitcast.61, s32[1,256]{1,0:T(1,128)} %broadcast_in_dim_tile.7.seg_row_ref, s32[64,1]{1,0:T(8,128)} %copy.15.seg_column_ref), custom_call_target="tpu_custom_call" | custom-call | tf_op jit(solution)/shard_map/probs/pallas_call | solution.py:50
  30.7 2.7 %layer.12 = (bf16[64,2048]{1,0:T(8,128)(2,1)}, bf16[64,512]{1,0:T(8,128)(2,1)}) custom-call(s32[1]{0:T(128)} %bitcast.3.live_ref, bf16[64,2048]{1,0:T(8,128)(2,1)} %copy-done.10, bf16[64,4608]{1,0:T(8,128)(2,1)} %bitcast.62, bf16[4,64,256]{2,1,0:T(8,128)(2,1)} %get-tuple-element.34.probs_ref, f32[64,128]{1,0:T(8,128)} %get-tuple-element.35.inv_ref, ...), custom_call_target="tpu_custom_call" | custom-call | tf_op jit(solution)/shard_map/layer/pallas_call | solution.py:115
  36.3 2.0 %probs.2 = (bf16[4,64,256]{2,1,0:T(8,128)(2,1)}, f32[64,128]{1,0:T(8,128)}) custom-call(bf16[64,4608]{1,0:T(8,128)(2,1)} %bitcast.55, s32[1,256]{1,0:T(1,128)} %broadcast_in_dim_tile.6.seg_row_ref, s32[64,1]{1,0:T(8,128)} %copy.14.seg_column_ref), custom_call_target="tpu_custom_call" | custom-call | tf_op jit(solution)/shard_map/probs/pallas_call | solution.py:50
  38.3 2.6 %layer.8 = (bf16[64,2048]{1,0:T(8,128)(2,1)}, bf16[64,512]{1,0:T(8,128)(2,1)}) custom-call(s32[1]{0:T(128)} %bitcast.3.live_ref, bf16[64,2048]{1,0:T(8,128)(2,1)} %get-tuple-element.51.grad_ref, bf16[64,4608]{1,0:T(8,128)(2,1)} %bitcast.56, bf16[4,64,256]{2,1,0:T(8,128)(2,1)} %get-tuple-element.25.probs_ref, f32[64,128]{1,0:T(8,128)} %get-tuple-element.26.inv_ref, ...), custom_call_target="tpu_custom_call" | custom-call | tf_op jit(solution)/shard_map/layer/pallas_call | solution.py:115
  42.3 2.7 %layer.13 = (bf16[64,2048]{1,0:T(8,128)(2,1)}, bf16[64,512]{1,0:T(8,128)(2,1)}) custom-call(s32[1]{0:T(128)} %bitcast.2.live_ref, bf16[64,2048]{1,0:T(8,128)(2,1)} %copy-done.5, bf16[64,4608]{1,0:T(8,128)(2,1)} %bitcast.63, bf16[4,64,256]{2,1,0:T(8,128)(2,1)} %get-tuple-element.34.probs_ref, f32[64,128]{1,0:T(8,128)} %get-tuple-element.35.inv_ref, ...), custom_call_target="tpu_custom_call" | custom-call | tf_op jit(solution)/shard_map/layer/pallas_call | solution.py:115
  45.7 1.0 slice.9
  47.4 3.4 %all-to-all-start.5 = ((bf16[8,64,256]{2,1,0:T(8,128)(2,1)}), bf16[8,64,256]{2,1,0:T(8,128)(2,1)S(1)}, u32[]{:S(2)}, u32[]{:S(2)}) async-start(bf16[8,64,256]{2,1,0:T(8,128)(2,1)} %bitcast.44), calls=%async_computation.5 | async-start | bytes 524288 | tf_op jit(solution)/shard_map/all_to_all | solution.py:166
  51.5 2.7 %layer.9 = (bf16[64,2048]{1,0:T(8,128)(2,1)}, bf16[64,512]{1,0:T(8,128)(2,1)}) custom-call(s32[1]{0:T(128)} %bitcast.2.live_ref, bf16[64,2048]{1,0:T(8,128)(2,1)} %copy-done.9, bf16[64,4608]{1,0:T(8,128)(2,1)} %bitcast.57, bf16[4,64,256]{2,1,0:T(8,128)(2,1)} %get-tuple-element.25.probs_ref, f32[64,128]{1,0:T(8,128)} %get-tuple-element.26.inv_ref, ...), custom_call_target="tpu_custom_call" | custom-call | tf_op jit(solution)/shard_map/layer/pallas_call | solution.py:115
  55.6 2.7 %layer.14 = (bf16[64,2048]{1,0:T(8,128)(2,1)}, bf16[64,512]{1,0:T(8,128)(2,1)}) custom-call(s32[1]{0:T(128)} %bitcast.1.live_ref, bf16[64,2048]{1,0:T(8,128)(2,1)} %copy-done.8, bf16[64,4608]{1,0:T(8,128)(2,1)} %bitcast.65, bf16[4,64,256]{2,1,0:T(8,128)(2,1)} %get-tuple-element.34.probs_ref, f32[64,128]{1,0:T(8,128)} %get-tuple-element.35.inv_ref, ...), custom_call_target="tpu_custom_call" | custom-call | tf_op jit(solution)/shard_map/layer/pallas_call | solution.py:115
  58.3 1.3 collective-permute-start.7
  59.6 1.0 slice.8
  61.3 4.1 %all-to-all-start.4 = ((bf16[8,64,256]{2,1,0:T(8,128)(2,1)}), bf16[8,64,256]{2,1,0:T(8,128)(2,1)S(1)}, u32[]{:S(2)}, u32[]{:S(2)}) async-start(bf16[8,64,256]{2,1,0:T(8,128)(2,1)} %bitcast.46), calls=%async_computation.4 | async-start | bytes 524288 | tf_op jit(solution)/shard_map/all_to_all | solution.py:166
  66.1 2.7 %layer.10 = (bf16[64,2048]{1,0:T(8,128)(2,1)}, bf16[64,512]{1,0:T(8,128)(2,1)}) custom-call(s32[1]{0:T(128)} %bitcast.1.live_ref, bf16[64,2048]{1,0:T(8,128)(2,1)} %copy-done.6, bf16[64,4608]{1,0:T(8,128)(2,1)} %bitcast.59, bf16[4,64,256]{2,1,0:T(8,128)(2,1)} %get-tuple-element.25.probs_ref, f32[64,128]{1,0:T(8,128)} %get-tuple-element.26.inv_ref, ...), custom_call_target="tpu_custom_call" | custom-call | tf_op jit(solution)/shard_map/layer/pallas_call | solution.py:115
  68.8 1.3 collective-permute-start.2
  71.1 3.7 %layer.15 = (bf16[64,2048]{1,0:T(8,128)(2,1)}, bf16[64,512]{1,0:T(8,128)(2,1)}) custom-call(s32[1]{0:T(128)} %bitcast.live_ref, bf16[64,2048]{1,0:T(8,128)(2,1)} %copy-done.4, bf16[64,4608]{1,0:T(8,128)(2,1)} %bitcast.66, bf16[4,64,256]{2,1,0:T(8,128)(2,1)} %get-tuple-element.34.probs_ref, f32[64,128]{1,0:T(8,128)} %get-tuple-element.35.inv_ref, ...), custom_call_target="tpu_custom_call" | custom-call | tf_op jit(solution)/shard_map/layer/pallas_call | solution.py:115
  74.8 3.4 %all-to-all-start.3 = ((bf16[4,16,2048]{2,1,0:T(8,128)(2,1)}), bf16[4,16,2048]{2,1,0:T(8,128)(2,1)S(1)}, u32[]{:S(2)}, u32[]{:S(2)}) async-start(bf16[4,16,2048]{2,1,0:T(8,128)(2,1)} %bitcast.79), calls=%async_computation.3 | async-start | bytes 524288 | tf_op jit(solution)/shard_map/all_to_all | solution.py:161
  78.2 3.8 %collective-permute-done.2.grad_ref = bf16[64,2048]{1,0:T(8,128)(2,1)S(1)} collective-permute-done((bf16[64,2048]{1,0:T(8,128)(2,1)}, bf16[64,2048]{1,0:T(8,128)(2,1)S(1)}, u32[]{:S(2)}, u32[]{:S(2)}) %collective-permute-start.2) | collective-permute-done | bytes 262176 | tf_op jit(solution)/shard_map/ppermute | solution.py:195
  82.8 3.7 %layer.11 = (bf16[64,2048]{1,0:T(8,128)(2,1)}, bf16[64,512]{1,0:T(8,128)(2,1)}) custom-call(s32[1]{0:T(128)} %bitcast.live_ref, bf16[64,2048]{1,0:T(8,128)(2,1)} %copy-done.7, bf16[64,4608]{1,0:T(8,128)(2,1)} %bitcast.60, bf16[4,64,256]{2,1,0:T(8,128)(2,1)} %get-tuple-element.25.probs_ref, f32[64,128]{1,0:T(8,128)} %get-tuple-element.26.inv_ref, ...), custom_call_target="tpu_custom_call" | custom-call | tf_op jit(solution)/shard_map/layer/pallas_call | solution.py:115
  86.5 9.6 %all_to_all.70 = bf16[4,16,2048]{2,1,0:T(8,128)(2,1)S(1)} all-to-all(bf16[4,16,2048]{2,1,0:T(8,128)(2,1)} %bitcast.80), channel_id=1, replica_groups={{0,4,8,12},{16,20,24,28},{1,5,9,13},{17,21,25,29},{2,6,10,14},{18,22,26..., dimensions={0} | all-to-all | bytes 524288 | tf_op jit(solution)/shard_map/all_to_all | solution.py:161
  96.9 3.5 %all-to-all-start.7 = ((bf16[8,64,512]{2,1,0:T(8,128)(2,1)}), bf16[8,64,512]{2,1,0:T(8,128)(2,1)S(1)}, u32[]{:S(2)}, u32[]{:S(2)}) async-start(bf16[8,64,512]{2,1,0:T(8,128)(2,1)} %tile.14), calls=%async_computation.7 | async-start | bytes 1048576 | tf_op jit(solution)/shard_map/all_to_all | solution.py:166
  101.8 8.2 %all-to-all-done.7 = bf16[8,64,512]{2,1,0:T(8,128)(2,1)S(1)} async-done(((bf16[8,64,512]{2,1,0:T(8,128)(2,1)}), bf16[8,64,512]{2,1,0:T(8,128)(2,1)S(1)}, u32[]{:S(2)}, u32[]{:S(2)}) %all-to-all-start.7) | async-done | bytes 524320 | tf_op jit(solution)/shard_map/all_to_all | solution.py:166
  110.9 3.5 %all-to-all-start.6 = ((bf16[8,64,512]{2,1,0:T(8,128)(2,1)}), bf16[8,64,512]{2,1,0:T(8,128)(2,1)S(1)}, u32[]{:S(2)}, u32[]{:S(2)}) async-start(bf16[8,64,512]{2,1,0:T(8,128)(2,1)} %tile.13), calls=%async_computation.6 | async-start | bytes 1048576 | tf_op jit(solution)/shard_map/all_to_all | solution.py:166
  114.4 1.7 %dynamic-slice_bitcast_fusion.weight_ref = bf16[256,512]{1,0:T(8,128)(2,1)} fusion(bf16[1,2048,512]{2,1,0:T(8,128)(2,1)} %param.11, s32[]{:T(128)S(6)} %select_n.43), kind=kLoop, calls=%fused_computation.7 | loop fusion | bytes 524292 | tf_op jit(solution)/shard_map/dynamic_slice | solution.py:217
  117.8 6.2 %all-to-all-done.6 = bf16[8,64,512]{2,1,0:T(8,128)(2,1)S(1)} async-done(((bf16[8,64,512]{2,1,0:T(8,128)(2,1)}), bf16[8,64,512]{2,1,0:T(8,128)(2,1)S(1)}, u32[]{:S(2)}, u32[]{:S(2)}) %all-to-all-start.6) | async-done | bytes 524320 | tf_op jit(solution)/shard_map/all_to_all | solution.py:166
  124.1 1.1 pad_maximum_fusion.value_ref
  125.1 3.1 %weight_grad.1 = (f32[256,512]{1,0:T(8,128)}, f32[1,256]{1,0:T(1,128)}) custom-call(bf16[1024,256]{1,0:T(8,128)(2,1)} %pad_maximum_fusion.3.columns_ref, bf16[1024,512]{1,0:T(8,128)(2,1)} %pad_maximum_fusion.value_ref, bf16[256,512]{1,0:T(8,128)(2,1)} %dynamic-slice_bitcast_fusion.weight_ref, f32[256,1]{1,0:T(8,128)} %copy.18.gain_ref), custom_call_target="tpu_custom_call" | custom-call | tf_op jit(solution)/shard_map/weight_grad/pallas_call | solution.py:220
  (64 shorter events, 19.7 us)
Async XLA Ops:
  0.6 4.9 %copy-start.11 = (bf16[1,128,512]{2,1,0:T(8,128)(2,1)S(1)}, bf16[1,128,512]{2,1,0:T(8,128)(2,1)}, u32[]{:S(2)}) copy-start(bf16[1,128,512]{2,1,0:T(8,128)(2,1)} %param.9) | copy-start | bytes 393220
  0.6 4.9 %copy-start.2 = (bf16[1,128,2048]{2,1,0:T(8,128)(2,1)S(1)}, bf16[1,128,2048]{2,1,0:T(8,128)(2,1)}, u32[]{:S(2)}) copy-start(bf16[1,128,2048]{2,1,0:T(8,128)(2,1)} %param.7) | copy-start | bytes 1572868
  0.7 4.9 %copy-start.3 = (bf16[1,128,2048]{2,1,0:T(8,128)(2,1)S(1)}, bf16[1,128,2048]{2,1,0:T(8,128)(2,1)}, u32[]{:S(2)}) copy-start(bf16[1,128,2048]{2,1,0:T(8,128)(2,1)} %param.8) | copy-start | bytes 1572868
  2.6 27.5 %collective-permute-start.3 = (bf16[64,2048]{1,0:T(8,128)(2,1)S(1)}, bf16[64,2048]{1,0:T(8,128)(2,1)S(1)}, u32[]{:S(2)}, u32[]{:S(2)}) collective-permute-start(bf16[64,2048]{1,0:T(8,128)(2,1)S(1)} %get-tuple-element.52), channel_id=1, source_target_pairs={{0,16},{4,20},{8,24},{12,28},{16,0},{20,4},{24,8},{28,12},{1,17},{... | collective-permute-start | bytes 786440 | tf_op jit(solution)/shard_map/ppermute | solution.py:173
  6.5 13.0 %all-to-all-start.2 = ((bf16[4,16,4608]{2,1,0:T(8,128)(2,1)}), bf16[4,16,4608]{2,1,0:T(8,128)(2,1)S(1)}, u32[]{:S(2)}, u32[]{:S(2)}) async-start(bf16[4,16,4608]{2,1,0:T(8,128)(2,1)} %pad_maximum_fusion.2), calls=%async_computation.2 | async-start | bytes 1179648 | tf_op jit(solution)/shard_map/all_to_all | solution.py:161
  10.0 13.0 %copy-start.14 = (s32[1,128]{1,0:T(1,128)S(1)}, s32[1,128]{1,0:T(1,128)}, u32[]{:S(2)}) copy-start(s32[1,128]{1,0:T(1,128)} %param.10) | copy-start | bytes 1540
  19.5 8.5 %copy-start.1 = (bf16[4,16,4608]{2,1,0:T(8,128)(2,1)}, bf16[4,16,4608]{2,1,0:T(8,128)(2,1)S(1)}, u32[]{:S(2)}) copy-start(bf16[4,16,4608]{2,1,0:T(8,128)(2,1)S(1)} %all-to-all-done.2) | copy-start | bytes 1769476
  19.5 15.9 %all-to-all-start = ((bf16[4,16,4608]{2,1,0:T(8,128)(2,1)}), bf16[4,16,4608]{2,1,0:T(8,128)(2,1)S(1)}, u32[]{:S(2)}, u32[]{:S(2)}) async-start(bf16[4,16,4608]{2,1,0:T(8,128)(2,1)} %pad_maximum_fusion.1), calls=%async_computation | async-start | bytes 1179648 | tf_op jit(solution)/shard_map/all_to_all | solution.py:161
  23.1 3.5 %collective-permute-start.4 = (s32[64]{0:T(128)S(1)}, s32[64]{0:T(128)S(1)}, u32[]{:S(2)}, u32[]{:S(2)}) collective-permute-start(s32[64]{0:T(128)S(1)} %get-tuple-element.56), channel_id=1, source_target_pairs={{0,16},{4,20},{8,24},{12,28},{16,0},{20,4},{24,8},{28,12},{1,17},{... | collective-permute-start | bytes 776 | tf_op jit(solution)/shard_map/ppermute | solution.py:174
  30.0 0.7 copy-start.10
  33.4 8.2 %collective-permute-start.5 = (bf16[64,2048]{1,0:T(8,128)(2,1)}, bf16[64,2048]{1,0:T(8,128)(2,1)S(1)}, u32[]{:S(2)}, u32[]{:S(2)}) collective-permute-start(bf16[64,2048]{1,0:T(8,128)(2,1)} %get-tuple-element.36.rest_0_), channel_id=1, source_target_pairs={{3,2},{7,6},{11,10},{15,14},{19,18},{23,22},{27,26},{31,30}} | collective-permute-start | bytes 786440 | tf_op jit(solution)/shard_map/ppermute | solution.py:195
  35.5 0.8 copy-start
  40.9 9.9 %collective-permute-start = (bf16[64,2048]{1,0:T(8,128)(2,1)}, bf16[64,2048]{1,0:T(8,128)(2,1)S(1)}, u32[]{:S(2)}, u32[]{:S(2)}) collective-permute-start(bf16[64,2048]{1,0:T(8,128)(2,1)} %get-tuple-element.27.rest_0_), channel_id=1, source_target_pairs={{3,2},{7,6},{11,10},{15,14},{19,18},{23,22},{27,26},{31,30}} | collective-permute-start | bytes 786440 | tf_op jit(solution)/shard_map/ppermute | solution.py:195
  41.6 0.7 copy-start.5
  45.0 9.9 %collective-permute-start.6 = (bf16[64,2048]{1,0:T(8,128)(2,1)}, bf16[64,2048]{1,0:T(8,128)(2,1)S(1)}, u32[]{:S(2)}, u32[]{:S(2)}) collective-permute-start(bf16[64,2048]{1,0:T(8,128)(2,1)} %get-tuple-element.38.rest_0_), channel_id=1, source_target_pairs={{2,1},{6,5},{10,9},{14,13},{18,17},{22,21},{26,25},{30,29}} | collective-permute-start | bytes 786440 | tf_op jit(solution)/shard_map/ppermute | solution.py:195
  47.4 13.9 %all-to-all-start.5 = ((bf16[8,64,256]{2,1,0:T(8,128)(2,1)}), bf16[8,64,256]{2,1,0:T(8,128)(2,1)S(1)}, u32[]{:S(2)}, u32[]{:S(2)}) async-start(bf16[8,64,256]{2,1,0:T(8,128)(2,1)} %bitcast.44), calls=%async_computation.5 | async-start | bytes 524288 | tf_op jit(solution)/shard_map/all_to_all | solution.py:166
  50.8 0.7 copy-start.9
  54.2 11.2 %collective-permute-start.1 = (bf16[64,2048]{1,0:T(8,128)(2,1)}, bf16[64,2048]{1,0:T(8,128)(2,1)S(1)}, u32[]{:S(2)}, u32[]{:S(2)}) collective-permute-start(bf16[64,2048]{1,0:T(8,128)(2,1)} %get-tuple-element.29.rest_0_), channel_id=1, source_target_pairs={{2,1},{6,5},{10,9},{14,13},{18,17},{22,21},{26,25},{30,29}} | collective-permute-start | bytes 786440 | tf_op jit(solution)/shard_map/ppermute | solution.py:195
  54.9 0.7 copy-start.8
  58.3 12.1 %collective-permute-start.7 = (bf16[64,2048]{1,0:T(8,128)(2,1)}, bf16[64,2048]{1,0:T(8,128)(2,1)S(1)}, u32[]{:S(2)}, u32[]{:S(2)}) collective-permute-start(bf16[64,2048]{1,0:T(8,128)(2,1)} %get-tuple-element.40.rest_0_), channel_id=1, source_target_pairs={{1,0},{5,4},{9,8},{13,12},{17,16},{21,20},{25,24},{29,28}} | collective-permute-start | bytes 786440 | tf_op jit(solution)/shard_map/ppermute | solution.py:195
  61.3 13.5 %all-to-all-start.4 = ((bf16[8,64,256]{2,1,0:T(8,128)(2,1)}), bf16[8,64,256]{2,1,0:T(8,128)(2,1)S(1)}, u32[]{:S(2)}, u32[]{:S(2)}) async-start(bf16[8,64,256]{2,1,0:T(8,128)(2,1)} %bitcast.46), calls=%async_computation.4 | async-start | bytes 524288 | tf_op jit(solution)/shard_map/all_to_all | solution.py:166
  65.4 0.7 copy-start.6
  68.8 13.2 %collective-permute-start.2 = (bf16[64,2048]{1,0:T(8,128)(2,1)}, bf16[64,2048]{1,0:T(8,128)(2,1)S(1)}, u32[]{:S(2)}, u32[]{:S(2)}) collective-permute-start(bf16[64,2048]{1,0:T(8,128)(2,1)} %get-tuple-element.31.rest_0_), channel_id=1, source_target_pairs={{1,0},{5,4},{9,8},{13,12},{17,16},{21,20},{25,24},{29,28}} | collective-permute-start | bytes 786440 | tf_op jit(solution)/shard_map/ppermute | solution.py:195
  70.4 0.7 copy-start.4
  74.8 11.6 %all-to-all-start.3 = ((bf16[4,16,2048]{2,1,0:T(8,128)(2,1)}), bf16[4,16,2048]{2,1,0:T(8,128)(2,1)S(1)}, u32[]{:S(2)}, u32[]{:S(2)}) async-start(bf16[4,16,2048]{2,1,0:T(8,128)(2,1)} %bitcast.79), calls=%async_computation.3 | async-start | bytes 524288 | tf_op jit(solution)/shard_map/all_to_all | solution.py:161
  82.1 0.7 copy-start.7
  82.8 13.3 %copy-start.13 = (bf16[64,512]{1,0:T(8,128)(2,1)S(1)}, bf16[64,512]{1,0:T(8,128)(2,1)}, u32[]{:S(2)}) copy-start(bf16[64,512]{1,0:T(8,128)(2,1)} %get-tuple-element.44) | copy-start | bytes 196612
  86.5 23.6 %copy-start.12 = (bf16[64,512]{1,0:T(8,128)(2,1)S(1)}, bf16[64,512]{1,0:T(8,128)(2,1)}, u32[]{:S(2)}) copy-start(bf16[64,512]{1,0:T(8,128)(2,1)} %get-tuple-element.43) | copy-start | bytes 196612
  96.9 13.2 %all-to-all-start.7 = ((bf16[8,64,512]{2,1,0:T(8,128)(2,1)}), bf16[8,64,512]{2,1,0:T(8,128)(2,1)S(1)}, u32[]{:S(2)}, u32[]{:S(2)}) async-start(bf16[8,64,512]{2,1,0:T(8,128)(2,1)} %tile.14), calls=%async_computation.7 | async-start | bytes 1048576 | tf_op jit(solution)/shard_map/all_to_all | solution.py:166
  110.9 13.2 %all-to-all-start.6 = ((bf16[8,64,512]{2,1,0:T(8,128)(2,1)}), bf16[8,64,512]{2,1,0:T(8,128)(2,1)S(1)}, u32[]{:S(2)}, u32[]{:S(2)}) async-start(bf16[8,64,512]{2,1,0:T(8,128)(2,1)} %tile.13), calls=%async_computation.6 | async-start | bytes 1048576 | tf_op jit(solution)/shard_map/all_to_all | solution.py:166

commit v2 on v1

v2 whole, which is shorter than its diff:
```python
import functools

import jax
import jax.numpy as jnp
from jax import lax
from jax.experimental import pallas as pl
from jax.experimental.pallas import tpu as pltpu
from jax.sharding import PartitionSpec as P

HEAD_FEATURES = 128
BLOCK = 64
EPSILON = 1e-06
MASKED = -1e30
VMEM = pl.BlockSpec(memory_space=pltpu.VMEM)
SMEM = pl.BlockSpec(memory_space=pltpu.SMEM)


def params(flops=0, nbytes=1 << 20):
    return dict(
        compiler_params=pltpu.CompilerParams(vmem_limit_bytes=24 << 20),
        cost_estimate=pl.CostEstimate(flops=flops, bytes_accessed=nbytes, transcendentals=0),
    )


def near(array):
    return pltpu.with_memory_space_constraint(array, pltpu.VMEM)


def wide_columns(refs, first, last):
    parts = [ref[:, first:last] for ref in refs]
    return parts[0] if len(parts) == 1 else jnp.concatenate(parts, axis=0)


def probs_kernel(count, model_width, kv_width, *refs):
    pieces = refs[:count]
    code_row_ref, code_column_ref = refs[count : count + 2]
    probs_ref, inv_ref, x_ref = refs[-3:]
    heads = model_width // kv_width
    query_code, key_code = code_row_ref[...], code_column_ref[...]
    list_start = query_code - lax.rem(query_code, BLOCK)
    allowed = (key_code <= query_code) & (key_code >= list_start)
    for c in range(kv_width // HEAD_FEATURES):
        first = c * heads * HEAD_FEATURES
        query_stack = jnp.concatenate(
            [
                wide_columns(pieces, first + h * HEAD_FEATURES, first + (h + 1) * HEAD_FEATURES)
                for h in range(heads)
            ],
            axis=0,
        )
        key_first = model_width + c * HEAD_FEATURES
        keys = wide_columns(pieces, key_first, key_first + HEAD_FEATURES)
        scores = lax.dot_general(
            keys, query_stack, (((1,), (1,)), ((), ())), preferred_element_type=jnp.float32
        ) * HEAD_FEATURES ** (-0.5)
        scores = jnp.where(allowed, scores, MASKED)
        exp_scores = jnp.exp(scores - jnp.max(scores, axis=0, keepdims=True))
        total = jnp.sum(exp_scores, axis=0, keepdims=True)
        probs_ref[c] = (exp_scores / total).astype(jnp.bfloat16)
    rows = BLOCK // count
    for p, piece in enumerate(pieces):
        hidden = piece[:, model_width + kv_width :]
        x_ref[p * rows : (p + 1) * rows, :] = hidden
        x = hidden.astype(jnp.float32)
        mean_square = jnp.mean(x * x, axis=1, keepdims=True)
        inv_ref[p * rows : (p + 1) * rows, :] = jnp.broadcast_to(
            lax.rsqrt(mean_square + EPSILON), (rows, inv_ref.shape[1])
        )


def block_probs(pieces, code, model_width, kv_width, after=None):
    heads = model_width // kv_width
    key_heads = kv_width // HEAD_FEATURES
    operands = [near(piece) for piece in pieces]
    operands += [jnp.tile(code, heads)[None, :], code[:, None]]
    specs = [VMEM] * len(operands)
    if after is not None:
        operands.append(after)
        specs.append(pl.BlockSpec(memory_space=pl.ANY))
    return pl.pallas_call(
        functools.partial(probs_kernel, len(pieces), model_width, kv_width),
        out_shape=(
            jax.ShapeDtypeStruct((key_heads, BLOCK, heads * BLOCK), jnp.bfloat16),
            jax.ShapeDtypeStruct((BLOCK, 128), jnp.float32),
            jax.ShapeDtypeStruct((BLOCK, model_width), jnp.bfloat16),
        ),
        in_specs=specs,
        out_specs=(VMEM,) * 3,
        name="probs",
        **params(4 * BLOCK * BLOCK * model_width),
    )(*operands)


def layer_math(grad_ref, x_ref, probs_ref, inv_ref, weight_ref, gain_ref, scaled_ref, store, value_ref):
    model_width = grad_ref.shape[1]
    kv_width = weight_ref.shape[1]
    heads = model_width // kv_width
    chunk = min(512, model_width)
    inv = inv_ref[:, :1]
    values = []
    for c in range(kv_width // HEAD_FEATURES):
        first = c * heads * HEAD_FEATURES
        grad_stack = jnp.concatenate(
            [
                grad_ref[:, first + h * HEAD_FEATURES : first + (h + 1) * HEAD_FEATURES]
                for h in range(heads)
            ],
            axis=0,
        )
        values.append(
            jnp.dot(probs_ref[c], grad_stack, preferred_element_type=jnp.float32).astype(
                jnp.bfloat16
            )
        )
    value = jnp.concatenate(values, axis=1)
    value_ref[...] = (value.astype(jnp.float32) * inv).astype(jnp.bfloat16)
    inner = jnp.zeros((BLOCK, 1), jnp.float32)
    for first in range(0, model_width, chunk):
        columns = slice(first, first + chunk)
        normed_grad = lax.dot_general(
            value, weight_ref[columns, :], (((1,), (1,)), ((), ())),
            preferred_element_type=jnp.float32,
        )
        scaled = normed_grad * gain_ref[:, columns]
        scaled_ref[:, columns] = scaled
        x = x_ref[:, columns].astype(jnp.float32)
        inner = inner + jnp.sum(x * scaled, axis=1, keepdims=True)
    pull = inner * (inv * inv / model_width)
    for first in range(0, model_width, chunk):
        columns = slice(first, first + chunk)
        x = x_ref[:, columns].astype(jnp.float32)
        change = inv * (scaled_ref[:, columns] - x * pull)
        store(columns, (grad_ref[:, columns].astype(jnp.float32) + change).astype(jnp.bfloat16))


def layer_kernel(live_ref, grad_ref, x_ref, probs_ref, inv_ref, weight_ref, gain_ref, *rest):
    out_ref, value_ref, scaled_ref = rest[-3:]

    def store(columns, part):
        out_ref[:, columns] = part

    @pl.when(live_ref[0] == 1)
    def _():
        layer_math(
            grad_ref, x_ref, probs_ref, inv_ref, weight_ref, gain_ref, scaled_ref, store, value_ref
        )


def last_layer_kernel(
    live_ref, grad_ref, x_ref, probs_ref, inv_ref, weight_ref, gain_ref,
    first_ref, held_ref, held_value_ref, value_ref, *rest
):
    scaled_ref = rest[-1]
    pieces = rest[:-1]
    piece = BLOCK // len(pieces)

    def store(columns, part):
        for k, piece_ref in enumerate(pieces):
            piece_ref[1, :, columns] = part[k * piece : (k + 1) * piece]

    for k, piece_ref in enumerate(pieces):
        piece_ref[0] = first_ref[k * piece : (k + 1) * piece, :]

    @pl.when(live_ref[0] == 0)
    def _():
        value_ref[...] = held_value_ref[...]
        for k, piece_ref in enumerate(pieces):
            piece_ref[1] = held_ref[k * piece : (k + 1) * piece, :]

    @pl.when(live_ref[0] == 1)
    def _():
        layer_math(
            grad_ref, x_ref, probs_ref, inv_ref, weight_ref, gain_ref, scaled_ref, store, value_ref
        )


def layer_step(live, grad, x, probs, inv, weight, gain, held=None, after=None):
    model_width, kv_width = weight.shape
    operands = [live] + [near(array) for array in (grad, x, probs, inv, weight, gain)]
    specs = [SMEM] + [VMEM] * 6
    aliases = {}
    if held is not None:
        aliases = {len(operands): 0, len(operands) + 1: 1}
        operands += [near(array) for array in held]
        specs += [VMEM] * 2
    if after is not None:
        operands.append(after)
        specs.append(pl.BlockSpec(memory_space=pl.ANY))
    return pl.pallas_call(
        layer_kernel,
        out_shape=(
            pltpu.VMEM((BLOCK, model_width), jnp.bfloat16),
            pltpu.VMEM((BLOCK, kv_width), jnp.bfloat16),
        ),
        in_specs=specs,
        out_specs=(VMEM, VMEM),
        scratch_shapes=[pltpu.VMEM((BLOCK, model_width), jnp.float32)],
        input_output_aliases=aliases,
        name="layer",
        **params(2 * BLOCK * model_width * kv_width),
    )(*operands)


def last_layer_step(live, grad, x, probs, inv, weight, gain, first, held, count):
    model_width, kv_width = weight.shape
    operands = [live]
    operands += [near(array) for array in (grad, x, probs, inv, weight, gain, first, *held)]
    piece = jax.ShapeDtypeStruct((2, BLOCK // count, model_width), jnp.bfloat16)
    return pl.pallas_call(
        last_layer_kernel,
        out_shape=(jax.ShapeDtypeStruct((BLOCK, kv_width), jnp.bfloat16),) + (piece,) * count,
        in_specs=[SMEM] + [VMEM] * (len(operands) - 1),
        out_specs=(VMEM,) * (1 + count),
        scratch_shapes=[pltpu.VMEM((BLOCK, model_width), jnp.float32)],
        name="last_layer",
        **params(2 * BLOCK * model_width * kv_width),
    )(*operands)


def pack_kernel(half, piece, me_ref, query_ref, key_ref, hidden_ref, up_ref, *rest):
    sems = rest[-1]
    ups = rest[-3:-1]
    packed = rest[:-3]
    side, at = me_ref[0], me_ref[1]
    copies = []

    def copy(source, target):
        made = pltpu.make_async_copy(source, target, sems.at[len(copies)])
        made.start()
        copies.append(made)

    for block in range(2):
        for k in range(half):
            replica = (side if block == 0 else 1 - side) * half + lax.bitwise_xor(at, k)
            rows = pl.ds(pl.multiple_of(replica * piece, piece), piece)
            target = packed[block * half + k]
            first = 0
            for source in (query_ref, key_ref, hidden_ref):
                width = source.shape[1]
                copy(source.at[rows], target.at[:, pl.ds(first, width)])
                first += width
    for block in range(2):
        for k in range(half):
            replica = (side if block == 0 else 1 - side) * half + lax.bitwise_xor(at, k)
            rows = pl.ds(pl.multiple_of(replica * piece, piece), piece)
            copy(up_ref.at[rows], ups[block].at[pl.ds(k * piece, piece)])
    for made in copies:
        made.wait()


def columns_kernel(width, me_ref, first_ref, second_ref, *outs):
    pair = me_ref[0]
    for k, out_ref in enumerate(outs):
        start = pl.multiple_of(lax.bitwise_xor(pair, k) * width, width)
        out_ref[:BLOCK, :] = first_ref[:, pl.ds(start, width)]
        out_ref[BLOCK:, :] = second_ref[:, pl.ds(start, width)]


def partial_kernel(count, shares, me_ref, *refs):
    columns, first, second = refs[:count], refs[count : 2 * count], refs[2 * count : 3 * count]
    own_ref, other_ref = refs[-2:]
    value = jnp.concatenate(
        [ref[...] for pair in zip(first, second) for ref in pair], axis=0
    )
    for ref, core in ((other_ref, 1 - me_ref[0]), (own_ref, me_ref[0])):
        at = pl.ds(pl.multiple_of(core * shares, shares), shares)
        rows = jnp.concatenate([part[:, at] for part in columns], axis=0)
        ref[...] = lax.dot_general(
            rows, value, (((0,), (0,)), ((), ())), preferred_element_type=jnp.float32
        )


def finish_kernel(
    half, scale, me_ref, own_ref, other_ref, weight_ref, gain_ref, *refs
):
    pieces = refs[:half]
    rows_ref, out_ref, gain_out_ref, sems = refs[half:]
    side, at = me_ref[0], me_ref[1]
    piece = pieces[0].shape[1]
    copies = []
    for block in range(2):
        for k in range(half):
            replica = (side if block == 0 else 1 - side) * half + lax.bitwise_xor(at, k)
            rows = pl.ds(pl.multiple_of(replica * piece, piece), piece)
            made = pltpu.make_async_copy(
                pieces[k].at[block], rows_ref.at[rows], sems.at[block * half + k]
            )
            made.start()
            copies.append(made)
    shares = own_ref.shape[0]
    first = pl.multiple_of(me_ref[2] * shares, shares)
    gain = gain_ref[:, pl.ds(first, shares)]
    eye = lax.broadcasted_iota(jnp.int32, (shares, shares), 0) == lax.broadcasted_iota(
        jnp.int32, (shares, shares), 1
    )
    gain_column = jnp.sum(jnp.where(eye, gain, 0.0), axis=1, keepdims=True)
    total = (own_ref[...] + other_ref[...]) * scale
    out_ref[...] = total * gain_column
    product = total * weight_ref[pl.ds(first, shares), :].astype(jnp.float32)
    sums = lax.dot_general(
        jnp.ones((8, product.shape[1]), jnp.float32), product, (((1,), (1,)), ((), ())),
        preferred_element_type=jnp.float32, precision=lax.Precision.HIGHEST,
    )
    gain_out_ref[...] = sums[:1]
    for made in copies:
        made.wait()


def direct(hidden, query, key, seg, weight, norm_gain, upstream):
    tokens, model_width = hidden.shape
    kv_width = key.shape[1]
    replicas = lax.axis_size("dp")
    layers = lax.axis_size("section")
    half = replicas // 2
    piece = tokens // replicas
    shares = model_width // replicas
    me = lax.axis_index("dp")
    section = lax.axis_index("section")
    side, at = me // half, me % half
    place = jnp.stack([side, at, me]).astype(jnp.int32)

    def swap(array, k):
        return lax.ppermute(array, "dp", [(i, i ^ k) for i in range(replicas)])

    count = 2 * half
    bf16 = jnp.bfloat16
    packed = pl.pallas_call(
        functools.partial(pack_kernel, half, piece),
        out_shape=(jax.ShapeDtypeStruct((piece, 2 * model_width + kv_width), bf16),) * count
        + (jax.ShapeDtypeStruct((BLOCK, model_width), bf16),) * 2,
        in_specs=[SMEM] + [pl.BlockSpec(memory_space=pl.ANY)] * 4,
        out_specs=(VMEM,) * (count + 2),
        scratch_shapes=[pltpu.SemaphoreType.DMA((4 * count,))],
        name="pack",
        **params(0, 3 << 20),
    )(place, query, key, hidden, upstream)
    ups = packed[-2:]
    seg_pieces = seg.reshape(2, half, piece)
    order = jnp.bitwise_xor(at, jnp.arange(half, dtype=jnp.int32))
    place_in_block = (order[:, None] * piece + jnp.arange(piece, dtype=jnp.int32)).reshape(-1)

    def seg_of(which):
        return seg_pieces[which][order].reshape(-1)

    segs = [seg_of(side), swap(seg_of(1 - side), half)]
    codes = [block_seg * BLOCK + place_in_block for block_seg in segs]
    pieces = [
        [packed[b * half]] + [swap(packed[b * half + k], k) for k in range(1, half)]
        for b in range(2)
    ]
    grads = [ups[0], swap(ups[1], half)]
    lives = [(section == layers - 1 - tick).astype(jnp.int32)[None] for tick in range(layers)]

    blocks, held = [], []
    for b in range(2):
        after = held[0][0] if b else None
        blocks.append(block_probs(pieces[b], codes[b], model_width, kv_width, after))
        probs, inv, x = blocks[b]
        held.append(layer_step(lives[0], grads[b], x, probs, inv, weight, norm_gain))

    columns = pl.pallas_call(
        functools.partial(columns_kernel, 2 * shares),
        out_shape=(jax.ShapeDtypeStruct((2 * BLOCK, 2 * shares), bf16),) * half,
        in_specs=[SMEM, VMEM, VMEM],
        out_specs=(VMEM,) * half,
        name="columns",
        **params(0, 1 << 20),
    )((me // 2)[None], blocks[0][2], blocks[1][2])
    columns = [columns[0]] + [swap(columns[k], 2 * k) for k in range(1, half)]

    for tick in range(1, layers):
        hop = [(layers - tick, layers - 1 - tick)]
        for b in range(2):
            probs, inv, x = blocks[b]
            grad = lax.ppermute(held[b][0], "section", hop)
            if tick == layers - 1 and b == 1:
                last = last_layer_step(
                    lives[tick], grad, x, probs, inv, weight, norm_gain, held[0][0], held[1], half
                )
            else:
                after = held[0][0] if b else None
                held[b] = layer_step(
                    lives[tick], grad, x, probs, inv, weight, norm_gain, held[b], after
                )
    values = [held[0][1], last[0]]
    gathered = [[value] + [swap(value, 2 * k) for k in range(1, half)] for value in values]
    rows = [last[1]] + [swap(last[1 + k], k) for k in range(1, half)]
    own, other = pl.pallas_call(
        functools.partial(partial_kernel, half, shares),
        out_shape=(jax.ShapeDtypeStruct((shares, kv_width), jnp.float32),) * 2,
        in_specs=[SMEM] + [VMEM] * (3 * half),
        out_specs=(VMEM, VMEM),
        name="weight_partial",
        **params(4 * tokens * half * shares * kv_width),
    )((me % 2)[None], *columns, *gathered[0], *gathered[1])
    other = swap(other, 1)
    scale = float(tokens * replicas) ** (-0.5)
    input_grad, weight_grad, gain_grad = pl.pallas_call(
        functools.partial(finish_kernel, half, scale),
        out_shape=(
            jax.ShapeDtypeStruct((tokens, model_width), bf16),
            jax.ShapeDtypeStruct((shares, kv_width), jnp.float32),
            jax.ShapeDtypeStruct((1, shares), jnp.float32),
        ),
        in_specs=[SMEM] + [VMEM] * (4 + half),
        out_specs=(pl.BlockSpec(memory_space=pl.ANY), VMEM, VMEM),
        scratch_shapes=[pltpu.SemaphoreType.DMA((count,))],
        name="finish",
        **params(),
    )(place, own, other, weight, norm_gain, *rows)
    return input_grad[None], weight_grad[None], gain_grad


def weight_kernel(scale, columns_ref, value_ref, weight_ref, gain_ref, out_ref, gain_out_ref):
    total = lax.dot_general(
        columns_ref[...], value_ref[...], (((0,), (0,)), ((), ())),
        preferred_element_type=jnp.float32,
    ) * scale
    out_ref[...] = total * gain_ref[...]
    product = total * weight_ref[...].astype(jnp.float32)
    sums = lax.dot_general(
        jnp.ones((8, product.shape[1]), jnp.float32), product, (((1,), (1,)), ((), ())),
        preferred_element_type=jnp.float32, precision=lax.Precision.HIGHEST,
    )
    gain_out_ref[...] = sums[:1]


def grouped(hidden, query, key, seg, weight, norm_gain, upstream):
    tokens, model_width = hidden.shape
    kv_width = key.shape[1]
    replicas = lax.axis_size("dp")
    layers = lax.axis_size("section")
    half = replicas // 2
    me = lax.axis_index("dp")
    section = lax.axis_index("section")
    side = me // half
    groups = [list(range(half)), list(range(half, replicas))]
    across = [(i, (i + half) % replicas) for i in range(replicas)]
    shares = model_width // replicas

    def rows_of(array, which, axis=0):
        at = side if which == 0 else 1 - side
        return lax.dynamic_slice_in_dim(array, at * BLOCK, BLOCK, axis)

    def regroup(array):
        return lax.all_to_all(
            array, "dp", split_axis=0, concat_axis=0, axis_index_groups=groups, tiled=True
        )

    def spread(array):
        return lax.all_to_all(array, "dp", split_axis=0, concat_axis=0, tiled=True)

    blocks, grads = [], []
    for which in range(2):
        up = rows_of(upstream, which)
        block_seg = rows_of(seg, which)
        if which == 1:
            up = lax.ppermute(up, "dp", across)
            block_seg = lax.ppermute(block_seg, "dp", across)
        packed = jnp.concatenate(
            [rows_of(query, which), rows_of(key, which), rows_of(hidden, which)], axis=1
        )
        code = block_seg * BLOCK + jnp.arange(BLOCK, dtype=jnp.int32)
        blocks.append(block_probs([regroup(packed)], code, model_width, kv_width))
        grads.append(up)

    def layer(tick, which, grad, kept):
        live = (section == layers - 1 - tick).astype(jnp.int32)[None]
        probs, inv, x = blocks[which]
        return layer_step(live, grad, x, probs, inv, weight, norm_gain, kept)

    held = [layer(0, which, grads[which], None) for which in range(2)]
    hops = [(i, i - 1) for i in range(1, layers)]

    def tick_step(tick, held):
        grads = [lax.ppermute(kept[0], "section", hops) for kept in held]
        return [layer(tick, which, grads[which], held[which]) for which in range(2)]

    held = lax.fori_loop(1, layers, tick_step, held)

    columns, values, stored = [], [], []
    for which in range(2):
        block = blocks[which][2].reshape(BLOCK, replicas, shares).transpose(1, 0, 2)
        columns.append(spread(block.reshape(replicas * BLOCK, shares)))
        out, value = held[which]
        stored.append(regroup(out))
        values.append(spread(jnp.tile(value, (replicas, 1))))
    ordered = jnp.where(
        side == 0, jnp.concatenate(stored, axis=0), jnp.concatenate(stored[::-1], axis=0)
    )
    own_weight = lax.dynamic_slice_in_dim(weight, me * shares, shares, 0)
    own_gain = lax.dynamic_slice_in_dim(norm_gain[0], me * shares, shares, 0)
    scale = float(tokens * replicas) ** (-0.5)
    weight_grad, gain_grad = pl.pallas_call(
        functools.partial(weight_kernel, scale),
        out_shape=(
            jax.ShapeDtypeStruct((shares, kv_width), jnp.float32),
            jax.ShapeDtypeStruct((1, shares), jnp.float32),
        ),
        in_specs=[VMEM] * 4,
        out_specs=(VMEM, VMEM),
        name="weight_grad",
    )(
        jnp.concatenate(columns, axis=0),
        jnp.concatenate(values, axis=0),
        own_weight,
        own_gain[:, None],
    )
    return ordered[None], weight_grad[None], gain_grad


def on_device(hidden_in, queries, keys, segments, value_weight, norm_gain, upstream):
    replicas = lax.axis_size("dp")
    piece = hidden_in.shape[1] // replicas
    plan = direct if piece % 16 == 0 and replicas in (4, 8) else grouped
    return plan(
        hidden_in[0], queries[0], keys[0], segments[0], value_weight[0], norm_gain, upstream
    )


def solution(mesh):
    in_specs = (
        P("section", "dp", None),
        P("section", "dp", None),
        P("section", "dp", None),
        P("dp", None),
        P("section", None, None),
        P("section", None),
        P("dp", None),
    )
    out_specs = (P("section", "dp", None), P("section", "dp", None), P("section", "dp"))
    return jax.shard_map(
        on_device, mesh=mesh, in_specs=in_specs, out_specs=out_specs, check_vma=False
    )
```

time: 130 us -> 95.4 us (0.73)
  Pallas kernels: 30.6 us -> 18.1 us
  blocking collectives: 9.55 us -> 0 us
  starting transfers between devices: 33.1 us -> 27.4 us
  waiting for transfers between devices: 30.8 us -> 25.3 us
  other arithmetic: 4.55 us -> 1.55 us
  local copies, waits for them, and re-layouts: 18.7 us -> 20.4 us
    all_to_all x7 -> x0, starting transfers between devices: 24.9 us -> none  [the longest x4 14.5 us: spread(): return lax.all_to_all(array, 'dp', split_axis=0, concat_axis=0, tiled=True)]
    all_to_all x7 -> x0, waiting for transfers between devices: 23.1 us -> none  [the longest x4 14.4 us: spread(): return lax.all_to_all(array, 'dp', split_axis=0, concat_axis=0, tiled=True)]
    ppermute x8 -> x27, starting transfers between devices: 8.2 us -> 27.4 us  [the longest x21 19.4 us: swap(): return lax.ppermute(array, 'dp', [(i, i ^ k) for i in range(replicas)])]
    ppermute x8 -> x27, waiting for transfers between devices: 7.69 us -> 25.3 us  [the longest x6 12.8 us: direct(): grad = lax.ppermute(held[b][0], 'section', hop)]
    unnamed x30 -> x61, local copies, waits for them, and re-layouts: 5.74 us -> 18.6 us
    pallas_call x11 -> x14, Pallas kernels: 30.6 us -> 18.1 us  [the longest x7 5.89 us: layer_step(): pl.pallas_call(layer_kernel, out_shape=(pltpu.VMEM((BLOCK, model_width),...]
    all_to_all x1 -> x0, blocking collectives: 9.55 us -> none  [regroup(): lax.all_to_all(array, 'dp', split_axis=0, concat_axis=0, axis_index_group...]
    concatenate x4 -> x0, other arithmetic: 3.65 us -> none  [the longest x2 1.73 us: on_device(): jnp.concatenate([rows_of(query, which), rows_of(key, which), rows_of(hidd...]
  transfers between devices with their start and end apart: 15 -> 27, of which waited for: 6 -> 11; matrix products, arithmetic and copies ran while one was open for 10% -> 1% of each run, Pallas kernels for 21% -> 15%
where the time goes in v2:
time: 95.4 us; the launch traced here: 93.8 us
  starting transfers between devices  27.4 us (29%)
  waiting for transfers between devices  25.3 us (27%)
  local copies, waits for them, and re-layouts  20.4 us (21%)
  Pallas kernels  18.1 us (19%)
  other arithmetic  1.55 us (2%)
    ppermute x21, starting transfers between devices, swap(): return lax.ppermute(array, 'dp', [(i, i ^ k) for i in range(replicas)])  19.4 us
    unnamed x61, local copies, waits for them, and re-layouts  18.6 us
    ppermute x6, waiting for transfers between devices, direct(): grad = lax.ppermute(held[b][0], 'section', hop)  12.8 us
    ppermute x21, waiting for transfers between devices, swap(): return lax.ppermute(array, 'dp', [(i, i ^ k) for i in range(replicas)])  12.5 us
    ppermute x6, starting transfers between devices, direct(): grad = lax.ppermute(held[b][0], 'section', hop)  7.98 us
    pallas_call x7, Pallas kernels, layer_step(): pl.pallas_call(layer_kernel, out_shape=(pltpu.VMEM((BLOCK, model_width),...  5.89 us
    pallas_call x1, Pallas kernels, direct(): pl.pallas_call(functools.partial(pack_kernel, half, piece), out_shape=(ja...  3.14 us
    pallas_call x1, Pallas kernels, last_layer_step(): pl.pallas_call(last_layer_kernel, out_shape=(jax.ShapeDtypeStruct((BLOCK,...  2.7 us
  transfers between devices with their start and end apart: 27, of which 11 were waited for; matrix products, arithmetic and copies ran while one was open for 1% of the time, Pallas kernels for 15%

profile of v2, /device:TPU:0, one launch (start us, length us, event | category | flops | bytes accessed | tf_op | source)
XLA Modules:
  0.0 93.8 jit_solution(11699176833613232525)
XLA Ops:
  1.2 1.4 %reduce.3 = s32[128]{0:T(128)S(1)} reduce(s32[1,128]{1,0:T(1,128)} %param.10, s32[]{:T(128)} %broadcast.86), dimensions={0}, to_apply=%param.10.reduce_sub_computation.3 | reduce | bytes 1028 | tf_op args[3]
  3.3 3.0 %collective-permute-start.6 = (s32[64]{0:T(128)S(1)}, s32[64]{0:T(128)S(1)}, u32[]{:S(2)}, u32[]{:S(2)}) collective-permute-start(s32[64]{0:T(128)S(1)} %reshape.86), channel_id=1, source_target_pairs={{0,16},{4,20},{8,24},{12,28},{16,0},{20,4},{24,8},{28,12},{1,17},{... | collective-permute-start | bytes 776 | tf_op jit(solution)/shard_map/ppermute | solution.py:323
  6.4 1.0 %copy-done.6 = bf16[1,128,2048]{2,1,0:T(8,128)(2,1)S(1)} copy-done((bf16[1,128,2048]{2,1,0:T(8,128)(2,1)S(1)}, bf16[1,128,2048]{2,1,0:T(8,128)(2,1)}, u32[]{:S(2)}) %copy-start.6) | copy-done | bytes 524312
  7.4 1.0 %copy-done.7 = bf16[1,128,2048]{2,1,0:T(8,128)(2,1)S(1)} copy-done((bf16[1,128,2048]{2,1,0:T(8,128)(2,1)S(1)}, bf16[1,128,2048]{2,1,0:T(8,128)(2,1)}, u32[]{:S(2)}) %copy-start.7) | copy-done | bytes 524312
  10.4 3.1 %pack.1 = (bf16[16,4608]{1,0:T(8,128)(2,1)S(1)}, bf16[16,4608]{1,0:T(8,128)(2,1)S(1)}, bf16[16,4608]{1,0:T(8,128)(2,1)S(1)}, bf16[16,4608]{1,0:T(8,128)(2,1)}, b...) custom-call(s32[3]{0:T(128)S(1)} %pad_add_fusion.me_ref, ...), custom_call_target="tpu_custom_call" | custom-call | bytes 3145728 | tf_op jit(solution)/shard_map/pack/pallas_call | solution.py:327
  14.9 1.5 %collective-permute-start.1 = (bf16[16,4608]{1,0:T(8,128)(2,1)S(1)}, bf16[16,4608]{1,0:T(8,128)(2,1)S(1)}, u32[]{:S(2)}, u32[]{:S(2)}) collective-permute-start(bf16[16,4608]{1,0:T(8,128)(2,1)S(1)} %get-tuple-element.49), channel_id=1, source_target_pairs={{0,8},{4,12},{8,0},{12,4},{16,24},{20,28},{24,16},{28,20},{1,9},{5... | collective-permute-start | bytes 442376 | tf_op jit(solution)/shard_map/ppermute | solution.py:323
  18.0 1.6 %collective-permute-start.4 = (bf16[16,4608]{1,0:T(8,128)(2,1)}, bf16[16,4608]{1,0:T(8,128)(2,1)}, u32[]{:S(2)}, u32[]{:S(2)}) collective-permute-start(bf16[16,4608]{1,0:T(8,128)(2,1)} %get-tuple-element.54), channel_id=1, source_target_pairs={{0,8},{4,12},{8,0},{12,4},{16,24},{20,28},{24,16},{28,20},{1,9},{5... | collective-permute-start | bytes 442376 | tf_op jit(solution)/shard_map/ppermute | solution.py:323
  20.3 1.3 %collective-permute-done.1.refs_2_ = bf16[16,4608]{1,0:T(8,128)(2,1)S(1)} collective-permute-done((bf16[16,4608]{1,0:T(8,128)(2,1)S(1)}, bf16[16,4608]{1,0:T(8,128)(2,1)S(1)}, u32[]{:S(2)}, u32[]{:S(2)}) %collective-permute-start.1) | collective-permute-done | bytes 147488 | tf_op jit(solution)/shard_map/ppermute | solution.py:323
  22.4 1.5 %collective-permute-done.2.refs_3_ = bf16[16,4608]{1,0:T(8,128)(2,1)S(1)} collective-permute-done((bf16[16,4608]{1,0:T(8,128)(2,1)}, bf16[16,4608]{1,0:T(8,128)(2,1)S(1)}, u32[]{:S(2)}, u32[]{:S(2)}) %collective-permute-start.2) | collective-permute-done | bytes 147488 | tf_op jit(solution)/shard_map/ppermute | solution.py:323
  28.2 1.4 %collective-permute-start.10 = (bf16[64,2048]{1,0:T(8,128)(2,1)S(1)}, bf16[64,2048]{1,0:T(8,128)(2,1)}, u32[]{:S(2)}, u32[]{:S(2)}) collective-permute-start(bf16[64,2048]{1,0:T(8,128)(2,1)S(1)} %get-tuple-element.59.refs_6_.rest_0_), channel_id=1, source_target_pairs={{3,2},{7,6},{11,10},{15,14},{19,18},{23,22},{27,26},{31,30}} | collective-permute-start | bytes 786440 | tf_op jit(solution)/shard_map/ppermute | solution.py:375
  31.3 1.3 %probs.3 = (bf16[4,64,256]{2,1,0:T(8,128)(2,1)S(1)}, f32[64,128]{1,0:T(8,128)S(1)}, bf16[64,2048]{1,0:T(8,128)(2,1)S(1)}) custom-call(bf16[16,4608]{1,0:T(8,128)(2,1)S(1)} %copy-done.22, bf16[16,4608]{1,0:T(8,128)(2,1)} %collective-permute-done.3.refs_1_, bf16[16,4608]{1,0:T(8,128)(2,1)} %collective-permute-done.4.refs_2_, ...), custom_call_target="tpu_custom_call" | custom-call | flops 33554432 | bytes 1048576 | tf_op jit(solution)/shard_map/probs/pallas_call | solution.py:80
  34.3 1.4 %collective-permute-start.17 = (bf16[64,2048]{1,0:T(8,128)(2,1)S(1)}, bf16[64,2048]{1,0:T(8,128)(2,1)}, u32[]{:S(2)}, u32[]{:S(2)}) collective-permute-start(bf16[64,2048]{1,0:T(8,128)(2,1)S(1)} %get-tuple-element.74.rest_0_), channel_id=1, source_target_pairs={{3,2},{7,6},{11,10},{15,14},{19,18},{23,22},{27,26},{31,30}} | collective-permute-start | bytes 786440 | tf_op jit(solution)/shard_map/ppermute | solution.py:375
  37.4 1.4 %collective-permute-start.11 = (bf16[64,2048]{1,0:T(8,128)(2,1)S(1)}, bf16[64,2048]{1,0:T(8,128)(2,1)}, u32[]{:S(2)}, u32[]{:S(2)}) collective-permute-start(bf16[64,2048]{1,0:T(8,128)(2,1)S(1)} %get-tuple-element.66.rest_0_.rest_2_), channel_id=1, source_target_pairs={{2,1},{6,5},{10,9},{14,13},{18,17},{22,21},{26,25},{30,29}} | collective-permute-start | bytes 786440 | tf_op jit(solution)/shard_map/ppermute | solution.py:375
  39.7 1.4 %collective-permute-start.18 = (bf16[64,2048]{1,0:T(8,128)(2,1)S(1)}, bf16[64,2048]{1,0:T(8,128)(2,1)}, u32[]{:S(2)}, u32[]{:S(2)}) collective-permute-start(bf16[64,2048]{1,0:T(8,128)(2,1)S(1)} %get-tuple-element.76.rest_0_), channel_id=1, source_target_pairs={{2,1},{6,5},{10,9},{14,13},{18,17},{22,21},{26,25},{30,29}} | collective-permute-start | bytes 786440 | tf_op jit(solution)/shard_map/ppermute | solution.py:375
  42.8 1.3 %collective-permute-start.12 = (bf16[64,2048]{1,0:T(8,128)(2,1)S(1)}, bf16[64,2048]{1,0:T(8,128)(2,1)}, u32[]{:S(2)}, u32[]{:S(2)}) collective-permute-start(bf16[64,2048]{1,0:T(8,128)(2,1)S(1)} %get-tuple-element.68.rest_0_.rest_2_), channel_id=1, source_target_pairs={{1,0},{5,4},{9,8},{13,12},{17,16},{21,20},{25,24},{29,28}} | collective-permute-start | bytes 786440 | tf_op jit(solution)/shard_map/ppermute | solution.py:375
  45.0 1.3 %collective-permute-start.19 = (bf16[64,2048]{1,0:T(8,128)(2,1)S(1)}, bf16[64,2048]{1,0:T(8,128)(2,1)}, u32[]{:S(2)}, u32[]{:S(2)}) collective-permute-start(bf16[64,2048]{1,0:T(8,128)(2,1)S(1)} %get-tuple-element.78.held_ref), channel_id=1, source_target_pairs={{1,0},{5,4},{9,8},{13,12},{17,16},{21,20},{25,24},{29,28}} | collective-permute-start | bytes 786440 | tf_op jit(solution)/shard_map/ppermute | solution.py:375
  47.8 1.5 %collective-permute-start.7 = (bf16[128,512]{1,0:T(8,128)(2,1)}, bf16[128,512]{1,0:T(8,128)(2,1)}, u32[]{:S(2)}, u32[]{:S(2)}) collective-permute-start(bf16[128,512]{1,0:T(8,128)(2,1)} %get-tuple-element.62), channel_id=1, source_target_pairs={{0,8},{4,12},{8,0},{12,4},{16,24},{20,28},{24,16},{28,20},{1,9},{5... | collective-permute-start | bytes 393224 | tf_op jit(solution)/shard_map/ppermute | solution.py:323
  49.7 1.5 %collective-permute-start.9 = (bf16[128,512]{1,0:T(8,128)(2,1)}, bf16[128,512]{1,0:T(8,128)(2,1)}, u32[]{:S(2)}, u32[]{:S(2)}) collective-permute-start(bf16[128,512]{1,0:T(8,128)(2,1)} %get-tuple-element.64), channel_id=1, source_target_pairs={{0,24},{4,28},{8,16},{12,20},{16,8},{20,12},{24,0},{28,4},{1,25},{... | collective-permute-start | bytes 393224 | tf_op jit(solution)/shard_map/ppermute | solution.py:323
  51.2 11.4 %collective-permute-done.12.grad_ref = bf16[64,2048]{1,0:T(8,128)(2,1)} collective-permute-done((bf16[64,2048]{1,0:T(8,128)(2,1)S(1)}, bf16[64,2048]{1,0:T(8,128)(2,1)}, u32[]{:S(2)}, u32[]{:S(2)}) %collective-permute-start.12) | collective-permute-done | bytes 262176 | tf_op jit(solution)/shard_map/ppermute | solution.py:375
  63.4 2.1 %layer.10 = (bf16[64,2048]{1,0:T(8,128)(2,1)S(1)}, bf16[64,512]{1,0:T(8,128)(2,1)S(1)}) custom-call(s32[1]{0:T(128)} %bitcast.14.live_ref, bf16[64,2048]{1,0:T(8,128)(2,1)} %collective-permute-done.12.grad_ref, bf16[64,2048]{1,0:T(8,128)(2,1)S(1)} %get-tuple-element.51.x_ref.first_ref, ...), custom_call_target="tpu_custom_call", output_to_operand_aliasing={{0}: (7, {}), {1}: (8, {})} | custom-call | flops 134217728 | bytes 1048576 | tf_op jit(solution)/shard_map/layer/pallas_call | solution.py:189
  65.5 1.5 %collective-permute-start.15 = (bf16[64,512]{1,0:T(8,128)(2,1)S(1)}, bf16[64,512]{1,0:T(8,128)(2,1)S(1)}, u32[]{:S(2)}, u32[]{:S(2)}) collective-permute-start(bf16[64,512]{1,0:T(8,128)(2,1)S(1)} %get-tuple-element.70.refs_4_), channel_id=1, source_target_pairs={{0,24},{4,28},{8,16},{12,20},{16,8},{20,12},{24,0},{28,4},{1,25},{... | collective-permute-start | bytes 196616 | tf_op jit(solution)/shard_map/ppermute | solution.py:323
  67.0 1.4 %collective-permute-done.19.grad_ref = bf16[64,2048]{1,0:T(8,128)(2,1)} collective-permute-done((bf16[64,2048]{1,0:T(8,128)(2,1)S(1)}, bf16[64,2048]{1,0:T(8,128)(2,1)}, u32[]{:S(2)}, u32[]{:S(2)}) %collective-permute-start.19) | collective-permute-done | bytes 262176 | tf_op jit(solution)/shard_map/ppermute | solution.py:375
  68.9 2.7 %last_layer.1 = (bf16[64,512]{1,0:T(8,128)(2,1)}, bf16[2,16,2048]{2,1,0:T(8,128)(2,1)S(1)}, bf16[2,16,2048]{2,1,0:T(8,128)(2,1)S(1)}, bf16[2,16,2048]{2,1,0:T(8,128)(2,1)S(1)}, bf16[2,16,2048]{2,1,0:T(8,128)(2,1)S(1)}) custom-call(s32[1]{0:T(128)} %bitcast.14.live_ref, bf16[64,2048]{1,0:T(8,128)(2,1)} %collective-permute-done.19.grad_ref, ...), custom_call_target="tpu_custom_call" | custom-call | flops 134217728 | bytes 1048576 | tf_op jit(solution)/shard_map/last_layer/pallas_call | solution.py:209
  73.5 1.5 %collective-permute-start.13 = (bf16[64,512]{1,0:T(8,128)(2,1)S(1)}, bf16[64,512]{1,0:T(8,128)(2,1)S(1)}, u32[]{:S(2)}, u32[]{:S(2)}) collective-permute-start(bf16[64,512]{1,0:T(8,128)(2,1)S(1)} %get-tuple-element.70.refs_4_), channel_id=1, source_target_pairs={{0,8},{4,12},{8,0},{12,4},{16,24},{20,28},{24,16},{28,20},{1,9},{5... | collective-permute-start | bytes 196616 | tf_op jit(solution)/shard_map/ppermute | solution.py:323
  75.0 1.5 %collective-permute-start.22 = (bf16[64,512]{1,0:T(8,128)(2,1)}, bf16[64,512]{1,0:T(8,128)(2,1)S(1)}, u32[]{:S(2)}, u32[]{:S(2)}) collective-permute-start(bf16[64,512]{1,0:T(8,128)(2,1)} %get-tuple-element.81.refs_8_), channel_id=1, source_target_pairs={{0,24},{4,28},{8,16},{12,20},{16,8},{20,12},{24,0},{28,4},{1,25},{... | collective-permute-start | bytes 196616 | tf_op jit(solution)/shard_map/ppermute | solution.py:323
  77.0 1.5 %collective-permute-start.20 = (bf16[64,512]{1,0:T(8,128)(2,1)}, bf16[64,512]{1,0:T(8,128)(2,1)S(1)}, u32[]{:S(2)}, u32[]{:S(2)}) collective-permute-start(bf16[64,512]{1,0:T(8,128)(2,1)} %get-tuple-element.81.refs_8_), channel_id=1, source_target_pairs={{0,8},{4,12},{8,0},{12,4},{16,24},{20,28},{24,16},{28,20},{1,9},{5... | collective-permute-start | bytes 196616 | tf_op jit(solution)/shard_map/ppermute | solution.py:323
  78.5 1.9 %collective-permute-done.22.refs_11_ = bf16[64,512]{1,0:T(8,128)(2,1)S(1)} collective-permute-done((bf16[64,512]{1,0:T(8,128)(2,1)}, bf16[64,512]{1,0:T(8,128)(2,1)S(1)}, u32[]{:S(2)}, u32[]{:S(2)}) %collective-permute-start.22) | collective-permute-done | bytes 65568 | tf_op jit(solution)/shard_map/ppermute | solution.py:323
  81.5 1.5 %weight_partial.1 = (f32[256,512]{1,0:T(8,128)S(1)}, f32[256,512]{1,0:T(8,128)S(1)}) custom-call(s32[1]{0:T(128)} %bitcast.3.me_ref, bf16[128,512]{1,0:T(8,128)(2,1)S(1)} %copy-done.25, bf16[128,512]{1,0:T(8,128)(2,1)} %collective-permute-done.7.refs_1_, bf16[128,512]{1,0:T(8,128)(2,1)} %collective-permute-done.8.refs_2_, ...), custom_call_target="tpu_custom_call" | custom-call | flops 268435456 | bytes 1048576 | tf_op jit(solution)/shard_map/weight_partial/pallas_call | solution.py:388
  83.6 1.5 %collective-permute-start.25 = (bf16[2,16,2048]{2,1,0:T(8,128)(2,1)}, bf16[2,16,2048]{2,1,0:T(8,128)(2,1)S(1)}, u32[]{:S(2)}, u32[]{:S(2)}) collective-permute-start(bf16[2,16,2048]{2,1,0:T(8,128)(2,1)} %copy-done.28), channel_id=1, source_target_pairs={{0,8},{4,12},{8,0},{12,4},{16,24},{20,28},{24,16},{28,20},{1,9},{5... | collective-permute-start | bytes 393224 | tf_op jit(solution)/shard_map/ppermute | solution.py:323
  85.4 4.8 %collective-permute-done.25.refs_2_ = bf16[2,16,2048]{2,1,0:T(8,128)(2,1)S(1)} collective-permute-done((bf16[2,16,2048]{2,1,0:T(8,128)(2,1)}, bf16[2,16,2048]{2,1,0:T(8,128)(2,1)S(1)}, u32[]{:S(2)}, u32[]{:S(2)}) %collective-permute-start.25) | collective-permute-done | bytes 131104 | tf_op jit(solution)/shard_map/ppermute | solution.py:323
  90.1 1.1 %collective-permute-done.26.refs_3_ = bf16[2,16,2048]{2,1,0:T(8,128)(2,1)S(1)} collective-permute-done((bf16[2,16,2048]{2,1,0:T(8,128)(2,1)}, bf16[2,16,2048]{2,1,0:T(8,128)(2,1)S(1)}, u32[]{:S(2)}, u32[]{:S(2)}) %collective-permute-start.26) | collective-permute-done | bytes 131104 | tf_op jit(solution)/shard_map/ppermute | solution.py:323
  91.2 2.6 %finish.1 = (bf16[128,2048]{1,0:T(8,128)(2,1)}, f32[256,512]{1,0:T(8,128)}, f32[1,256]{1,0:T(1,128)}) custom-call(s32[3]{0:T(128)S(1)} %pad_add_fusion.me_ref, f32[256,512]{1,0:T(8,128)S(1)} %get-tuple-element.82.own_ref, f32[256,512]{1,0:T(8,128)S(1)} %collective-permute-done.23.other_ref, bf16[2048,512]{1,0:T(8,128)(2,1)S(1)} %bitcast.30, ...), custom_call_target="tpu_custom_call" | custom-call | bytes 1048576 | tf_op jit(solution)/shard_map/finish/pallas_call | solution.py:398
  (117 shorter events, 28.3 us)
Async XLA Ops:
  0.6 27.0 %copy-start.1 = (f32[1,2048]{1,0:T(1,128)S(1)}, f32[1,2048]{1,0:T(1,128)}, u32[]{:S(2)}) copy-start(f32[1,2048]{1,0:T(1,128)} %gain_ref.17) | copy-start | bytes 24580
  0.6 27.0 %copy-start = (bf16[1,2048,512]{2,1,0:T(8,128)(2,1)S(1)}, bf16[1,2048,512]{2,1,0:T(8,128)(2,1)}, u32[]{:S(2)}) copy-start(bf16[1,2048,512]{2,1,0:T(8,128)(2,1)} %param.11) | copy-start | bytes 6291460
  3.3 14.6 %collective-permute-start.6 = (s32[64]{0:T(128)S(1)}, s32[64]{0:T(128)S(1)}, u32[]{:S(2)}, u32[]{:S(2)}) collective-permute-start(s32[64]{0:T(128)S(1)} %reshape.86), channel_id=1, source_target_pairs={{0,16},{4,20},{8,24},{12,28},{16,0},{20,4},{24,8},{28,12},{1,17},{... | collective-permute-start | bytes 776 | tf_op jit(solution)/shard_map/ppermute | solution.py:323
  14.9 4.6 %collective-permute-start = (bf16[16,4608]{1,0:T(8,128)(2,1)S(1)}, bf16[16,4608]{1,0:T(8,128)(2,1)S(1)}, u32[]{:S(2)}, u32[]{:S(2)}) collective-permute-start(bf16[16,4608]{1,0:T(8,128)(2,1)S(1)} %get-tuple-element.48), channel_id=1, source_target_pairs={{0,4},{4,0},{8,12},{12,8},{16,20},{20,16},{24,28},{28,24},{1,5},{5... | collective-permute-start | bytes 442376 | tf_op jit(solution)/shard_map/ppermute | solution.py:323
  14.9 6.6 %collective-permute-start.1 = (bf16[16,4608]{1,0:T(8,128)(2,1)S(1)}, bf16[16,4608]{1,0:T(8,128)(2,1)S(1)}, u32[]{:S(2)}, u32[]{:S(2)}) collective-permute-start(bf16[16,4608]{1,0:T(8,128)(2,1)S(1)} %get-tuple-element.49), channel_id=1, source_target_pairs={{0,8},{4,12},{8,0},{12,4},{16,24},{20,28},{24,16},{28,20},{1,9},{5... | collective-permute-start | bytes 442376 | tf_op jit(solution)/shard_map/ppermute | solution.py:323
  16.4 7.5 %collective-permute-start.2 = (bf16[16,4608]{1,0:T(8,128)(2,1)}, bf16[16,4608]{1,0:T(8,128)(2,1)S(1)}, u32[]{:S(2)}, u32[]{:S(2)}) collective-permute-start(bf16[16,4608]{1,0:T(8,128)(2,1)} %get-tuple-element.50), channel_id=1, source_target_pairs={{0,12},{4,8},{8,4},{12,0},{16,28},{20,24},{24,20},{28,16},{1,13},{... | collective-permute-start | bytes 442376 | tf_op jit(solution)/shard_map/ppermute | solution.py:323
  16.8 13.0 %collective-permute-start.3 = (bf16[16,4608]{1,0:T(8,128)(2,1)}, bf16[16,4608]{1,0:T(8,128)(2,1)}, u32[]{:S(2)}, u32[]{:S(2)}) collective-permute-start(bf16[16,4608]{1,0:T(8,128)(2,1)} %get-tuple-element.53), channel_id=1, source_target_pairs={{0,4},{4,0},{8,12},{12,8},{16,20},{20,16},{24,28},{28,24},{1,5},{5... | collective-permute-start | bytes 442376 | tf_op jit(solution)/shard_map/ppermute | solution.py:323
  18.0 11.8 %collective-permute-start.4 = (bf16[16,4608]{1,0:T(8,128)(2,1)}, bf16[16,4608]{1,0:T(8,128)(2,1)}, u32[]{:S(2)}, u32[]{:S(2)}) collective-permute-start(bf16[16,4608]{1,0:T(8,128)(2,1)} %get-tuple-element.54), channel_id=1, source_target_pairs={{0,8},{4,12},{8,0},{12,4},{16,24},{20,28},{24,16},{28,20},{1,9},{5... | collective-permute-start | bytes 442376 | tf_op jit(solution)/shard_map/ppermute | solution.py:323
  20.2 10.2 %collective-permute-start.5 = (bf16[16,4608]{1,0:T(8,128)(2,1)}, bf16[16,4608]{1,0:T(8,128)(2,1)}, u32[]{:S(2)}, u32[]{:S(2)}) collective-permute-start(bf16[16,4608]{1,0:T(8,128)(2,1)} %get-tuple-element.55), channel_id=1, source_target_pairs={{0,12},{4,8},{8,4},{12,0},{16,28},{20,24},{24,20},{28,16},{1,13},{... | collective-permute-start | bytes 442376 | tf_op jit(solution)/shard_map/ppermute | solution.py:323
  22.2 10.4 %collective-permute-start.16 = (bf16[64,2048]{1,0:T(8,128)(2,1)}, bf16[64,2048]{1,0:T(8,128)(2,1)S(1)}, u32[]{:S(2)}, u32[]{:S(2)}) collective-permute-start(bf16[64,2048]{1,0:T(8,128)(2,1)} %copy-done.26), channel_id=1, source_target_pairs={{0,16},{4,20},{8,24},{12,28},{16,0},{20,4},{24,8},{28,12},{1,17},{... | collective-permute-start | bytes 786440 | tf_op jit(solution)/shard_map/ppermute | solution.py:323
  28.2 7.4 %collective-permute-start.10 = (bf16[64,2048]{1,0:T(8,128)(2,1)S(1)}, bf16[64,2048]{1,0:T(8,128)(2,1)}, u32[]{:S(2)}, u32[]{:S(2)}) collective-permute-start(bf16[64,2048]{1,0:T(8,128)(2,1)S(1)} %get-tuple-element.59.refs_6_.rest_0_), channel_id=1, source_target_pairs={{3,2},{7,6},{11,10},{15,14},{19,18},{23,22},{27,26},{31,30}} | collective-permute-start | bytes 786440 | tf_op jit(solution)/shard_map/ppermute | solution.py:375
  34.3 4.4 %collective-permute-start.17 = (bf16[64,2048]{1,0:T(8,128)(2,1)S(1)}, bf16[64,2048]{1,0:T(8,128)(2,1)}, u32[]{:S(2)}, u32[]{:S(2)}) collective-permute-start(bf16[64,2048]{1,0:T(8,128)(2,1)S(1)} %get-tuple-element.74.rest_0_), channel_id=1, source_target_pairs={{3,2},{7,6},{11,10},{15,14},{19,18},{23,22},{27,26},{31,30}} | collective-permute-start | bytes 786440 | tf_op jit(solution)/shard_map/ppermute | solution.py:375
  35.7 3.1 %copy-start.3 = (f32[64,128]{1,0:T(8,128)S(1)}, f32[64,128]{1,0:T(8,128)}, u32[]{:S(2)}) copy-start(f32[64,128]{1,0:T(8,128)} %copy-done.2) | copy-start | bytes 98308
  37.4 3.7 %collective-permute-start.11 = (bf16[64,2048]{1,0:T(8,128)(2,1)S(1)}, bf16[64,2048]{1,0:T(8,128)(2,1)}, u32[]{:S(2)}, u32[]{:S(2)}) collective-permute-start(bf16[64,2048]{1,0:T(8,128)(2,1)S(1)} %get-tuple-element.66.rest_0_.rest_2_), channel_id=1, source_target_pairs={{2,1},{6,5},{10,9},{14,13},{18,17},{22,21},{26,25},{30,29}} | collective-permute-start | bytes 786440 | tf_op jit(solution)/shard_map/ppermute | solution.py:375
  39.7 4.4 %collective-permute-start.18 = (bf16[64,2048]{1,0:T(8,128)(2,1)S(1)}, bf16[64,2048]{1,0:T(8,128)(2,1)}, u32[]{:S(2)}, u32[]{:S(2)}) collective-permute-start(bf16[64,2048]{1,0:T(8,128)(2,1)S(1)} %get-tuple-element.76.rest_0_), channel_id=1, source_target_pairs={{2,1},{6,5},{10,9},{14,13},{18,17},{22,21},{26,25},{30,29}} | collective-permute-start | bytes 786440 | tf_op jit(solution)/shard_map/ppermute | solution.py:375
  42.8 19.9 %collective-permute-start.12 = (bf16[64,2048]{1,0:T(8,128)(2,1)S(1)}, bf16[64,2048]{1,0:T(8,128)(2,1)}, u32[]{:S(2)}, u32[]{:S(2)}) collective-permute-start(bf16[64,2048]{1,0:T(8,128)(2,1)S(1)} %get-tuple-element.68.rest_0_.rest_2_), channel_id=1, source_target_pairs={{1,0},{5,4},{9,8},{13,12},{17,16},{21,20},{25,24},{29,28}} | collective-permute-start | bytes 786440 | tf_op jit(solution)/shard_map/ppermute | solution.py:375
  45.0 23.3 %collective-permute-start.19 = (bf16[64,2048]{1,0:T(8,128)(2,1)S(1)}, bf16[64,2048]{1,0:T(8,128)(2,1)}, u32[]{:S(2)}, u32[]{:S(2)}) collective-permute-start(bf16[64,2048]{1,0:T(8,128)(2,1)S(1)} %get-tuple-element.78.held_ref), channel_id=1, source_target_pairs={{1,0},{5,4},{9,8},{13,12},{17,16},{21,20},{25,24},{29,28}} | collective-permute-start | bytes 786440 | tf_op jit(solution)/shard_map/ppermute | solution.py:375
  47.8 25.8 %collective-permute-start.7 = (bf16[128,512]{1,0:T(8,128)(2,1)}, bf16[128,512]{1,0:T(8,128)(2,1)}, u32[]{:S(2)}, u32[]{:S(2)}) collective-permute-start(bf16[128,512]{1,0:T(8,128)(2,1)} %get-tuple-element.62), channel_id=1, source_target_pairs={{0,8},{4,12},{8,0},{12,4},{16,24},{20,28},{24,16},{28,20},{1,9},{5... | collective-permute-start | bytes 393224 | tf_op jit(solution)/shard_map/ppermute | solution.py:323
  49.2 25.8 %collective-permute-start.8 = (bf16[128,512]{1,0:T(8,128)(2,1)}, bf16[128,512]{1,0:T(8,128)(2,1)}, u32[]{:S(2)}, u32[]{:S(2)}) collective-permute-start(bf16[128,512]{1,0:T(8,128)(2,1)} %get-tuple-element.63), channel_id=1, source_target_pairs={{0,16},{4,20},{8,24},{12,28},{16,0},{20,4},{24,8},{28,12},{1,17},{... | collective-permute-start | bytes 393224 | tf_op jit(solution)/shard_map/ppermute | solution.py:323
  49.7 26.8 %collective-permute-start.9 = (bf16[128,512]{1,0:T(8,128)(2,1)}, bf16[128,512]{1,0:T(8,128)(2,1)}, u32[]{:S(2)}, u32[]{:S(2)}) collective-permute-start(bf16[128,512]{1,0:T(8,128)(2,1)} %get-tuple-element.64), channel_id=1, source_target_pairs={{0,24},{4,28},{8,16},{12,20},{16,8},{20,12},{24,0},{28,4},{1,25},{... | collective-permute-start | bytes 393224 | tf_op jit(solution)/shard_map/ppermute | solution.py:323
  51.2 17.6 %copy-start.5 = (f32[64,128]{1,0:T(8,128)S(1)}, f32[64,128]{1,0:T(8,128)}, u32[]{:S(2)}) copy-start(f32[64,128]{1,0:T(8,128)} %copy-done.2) | copy-start | bytes 98308
  65.5 16.0 %copy-start.25 = (bf16[128,512]{1,0:T(8,128)(2,1)S(1)}, bf16[128,512]{1,0:T(8,128)(2,1)}, u32[]{:S(2)}) copy-start(bf16[128,512]{1,0:T(8,128)(2,1)} %copy-done.24) | copy-start | bytes 393220
  65.5 11.5 %collective-permute-start.15 = (bf16[64,512]{1,0:T(8,128)(2,1)S(1)}, bf16[64,512]{1,0:T(8,128)(2,1)S(1)}, u32[]{:S(2)}, u32[]{:S(2)}) collective-permute-start(bf16[64,512]{1,0:T(8,128)(2,1)S(1)} %get-tuple-element.70.refs_4_), channel_id=1, source_target_pairs={{0,24},{4,28},{8,16},{12,20},{16,8},{20,12},{24,0},{28,4},{1,25},{... | collective-permute-start | bytes 196616 | tf_op jit(solution)/shard_map/ppermute | solution.py:323
  68.4 10.2 %collective-permute-start.14 = (bf16[64,512]{1,0:T(8,128)(2,1)S(1)}, bf16[64,512]{1,0:T(8,128)(2,1)S(1)}, u32[]{:S(2)}, u32[]{:S(2)}) collective-permute-start(bf16[64,512]{1,0:T(8,128)(2,1)S(1)} %get-tuple-element.70.refs_4_), channel_id=1, source_target_pairs={{0,16},{4,20},{8,24},{12,28},{16,0},{20,4},{24,8},{28,12},{1,17},{... | collective-permute-start | bytes 196616 | tf_op jit(solution)/shard_map/ppermute | solution.py:323
  73.5 5.0 %collective-permute-start.13 = (bf16[64,512]{1,0:T(8,128)(2,1)S(1)}, bf16[64,512]{1,0:T(8,128)(2,1)S(1)}, u32[]{:S(2)}, u32[]{:S(2)}) collective-permute-start(bf16[64,512]{1,0:T(8,128)(2,1)S(1)} %get-tuple-element.70.refs_4_), channel_id=1, source_target_pairs={{0,8},{4,12},{8,0},{12,4},{16,24},{20,28},{24,16},{28,20},{1,9},{5... | collective-permute-start | bytes 196616 | tf_op jit(solution)/shard_map/ppermute | solution.py:323
  75.0 5.4 %collective-permute-start.22 = (bf16[64,512]{1,0:T(8,128)(2,1)}, bf16[64,512]{1,0:T(8,128)(2,1)S(1)}, u32[]{:S(2)}, u32[]{:S(2)}) collective-permute-start(bf16[64,512]{1,0:T(8,128)(2,1)} %get-tuple-element.81.refs_8_), channel_id=1, source_target_pairs={{0,24},{4,28},{8,16},{12,20},{16,8},{20,12},{24,0},{28,4},{1,25},{... | collective-permute-start | bytes 196616 | tf_op jit(solution)/shard_map/ppermute | solution.py:323
  76.5 4.6 %collective-permute-start.21 = (bf16[64,512]{1,0:T(8,128)(2,1)}, bf16[64,512]{1,0:T(8,128)(2,1)S(1)}, u32[]{:S(2)}, u32[]{:S(2)}) collective-permute-start(bf16[64,512]{1,0:T(8,128)(2,1)} %get-tuple-element.81.refs_8_), channel_id=1, source_target_pairs={{0,16},{4,20},{8,24},{12,28},{16,0},{20,4},{24,8},{28,12},{1,17},{... | collective-permute-start | bytes 196616 | tf_op jit(solution)/shard_map/ppermute | solution.py:323
  77.0 4.5 %collective-permute-start.20 = (bf16[64,512]{1,0:T(8,128)(2,1)}, bf16[64,512]{1,0:T(8,128)(2,1)S(1)}, u32[]{:S(2)}, u32[]{:S(2)}) collective-permute-start(bf16[64,512]{1,0:T(8,128)(2,1)} %get-tuple-element.81.refs_8_), channel_id=1, source_target_pairs={{0,8},{4,12},{8,0},{12,4},{16,24},{20,28},{24,16},{28,20},{1,9},{5... | collective-permute-start | bytes 196616 | tf_op jit(solution)/shard_map/ppermute | solution.py:323
  83.0 8.2 %collective-permute-start.23 = (f32[256,512]{1,0:T(8,128)S(1)}, f32[256,512]{1,0:T(8,128)S(1)}, u32[]{:S(2)}, u32[]{:S(2)}) collective-permute-start(f32[256,512]{1,0:T(8,128)S(1)} %get-tuple-element.83), channel_id=1, source_target_pairs={{0,4},{4,0},{8,12},{12,8},{16,20},{20,16},{24,28},{28,24},{1,5},{5... | collective-permute-start | bytes 1572872 | tf_op jit(solution)/shard_map/ppermute | solution.py:323
  83.1 2.3 %collective-permute-start.24 = (bf16[2,16,2048]{2,1,0:T(8,128)(2,1)}, bf16[2,16,2048]{2,1,0:T(8,128)(2,1)S(1)}, u32[]{:S(2)}, u32[]{:S(2)}) collective-permute-start(bf16[2,16,2048]{2,1,0:T(8,128)(2,1)} %copy-done.29), channel_id=1, source_target_pairs={{0,4},{4,0},{8,12},{12,8},{16,20},{20,16},{24,28},{28,24},{1,5},{5... | collective-permute-start | bytes 393224 | tf_op jit(solution)/shard_map/ppermute | solution.py:323
  83.6 6.6 %collective-permute-start.25 = (bf16[2,16,2048]{2,1,0:T(8,128)(2,1)}, bf16[2,16,2048]{2,1,0:T(8,128)(2,1)S(1)}, u32[]{:S(2)}, u32[]{:S(2)}) collective-permute-start(bf16[2,16,2048]{2,1,0:T(8,128)(2,1)} %copy-done.28), channel_id=1, source_target_pairs={{0,8},{4,12},{8,0},{12,4},{16,24},{20,28},{24,16},{28,20},{1,9},{5... | collective-permute-start | bytes 393224 | tf_op jit(solution)/shard_map/ppermute | solution.py:323
  85.1 6.1 %collective-permute-start.26 = (bf16[2,16,2048]{2,1,0:T(8,128)(2,1)}, bf16[2,16,2048]{2,1,0:T(8,128)(2,1)S(1)}, u32[]{:S(2)}, u32[]{:S(2)}) collective-permute-start(bf16[2,16,2048]{2,1,0:T(8,128)(2,1)} %copy-done.27), channel_id=1, source_target_pairs={{0,12},{4,8},{8,4},{12,0},{16,28},{20,24},{24,20},{28,16},{1,13},{... | collective-permute-start | bytes 393224 | tf_op jit(solution)/shard_map/ppermute | solution.py:323
  (25 other events, 22.9 us)

commit v3 on v2

--- a/solution.py
+++ b/solution.py
@@ -15,9 +15,12 @@
 SMEM = pl.BlockSpec(memory_space=pltpu.SMEM)
 
 
+ANY = pl.BlockSpec(memory_space=pl.ANY)
+
+
 def params(flops=0, nbytes=1 << 20):
     return dict(
-        compiler_params=pltpu.CompilerParams(vmem_limit_bytes=24 << 20),
+        compiler_params=pltpu.CompilerParams(vmem_limit_bytes=16 << 20),
         cost_estimate=pl.CostEstimate(flops=flops, bytes_accessed=nbytes, transcendentals=0),
     )
 
@@ -31,14 +34,30 @@
     return parts[0] if len(parts) == 1 else jnp.concatenate(parts, axis=0)
 
 
-def probs_kernel(count, model_width, kv_width, *refs):
-    pieces = refs[:count]
-    code_row_ref, code_column_ref = refs[count : count + 2]
+def probs_kernel(count, shuffled, model_width, kv_width, *refs):
+    pieces, seg_ref = refs[:count], refs[count]
     probs_ref, inv_ref, x_ref = refs[-3:]
     heads = model_width // kv_width
-    query_code, key_code = code_row_ref[...], code_column_ref[...]
-    list_start = query_code - lax.rem(query_code, BLOCK)
-    allowed = (key_code <= query_code) & (key_code >= list_start)
+    rows = BLOCK // count
+    half = lax.axis_size("dp") // 2
+    me = lax.axis_index("dp")
+    turn = lax.rem(me, half) * rows if shuffled else 0
+
+    def iota(shape, axis):
+        return lax.broadcasted_iota(jnp.int32, shape, axis)
+
+    shape = (BLOCK, seg_ref.shape[1])
+    wanted = lax.div(me, half) * BLOCK + lax.bitwise_xor(iota(shape, 0), turn)
+    seg = seg_ref[...].astype(jnp.float32)
+    ids = jnp.sum(jnp.where(iota(shape, 1) == wanted, seg, 0.0), axis=1, keepdims=True)
+    place = lax.bitwise_xor(iota((BLOCK, 1), 0), turn)
+    key_code = ids * BLOCK + place.astype(jnp.float32)
+    list_start = ids * BLOCK
+    shape = (BLOCK, heads * BLOCK)
+    same = iota(shape, 0) == lax.rem(iota(shape, 1), BLOCK)
+    query_code = jnp.sum(jnp.where(same, key_code, 0.0), axis=0, keepdims=True)
+    query_start = jnp.sum(jnp.where(same, list_start, 0.0), axis=0, keepdims=True)
+    allowed = (key_code <= query_code) & (key_code >= query_start)
     for c in range(kv_width // HEAD_FEATURES):
         first = c * heads * HEAD_FEATURES
         query_stack = jnp.concatenate(
@@ -57,7 +76,6 @@
         exp_scores = jnp.exp(scores - jnp.max(scores, axis=0, keepdims=True))
         total = jnp.sum(exp_scores, axis=0, keepdims=True)
         probs_ref[c] = (exp_scores / total).astype(jnp.bfloat16)
-    rows = BLOCK // count
     for p, piece in enumerate(pieces):
         hidden = piece[:, model_width + kv_width :]
         x_ref[p * rows : (p + 1) * rows, :] = hidden
@@ -68,17 +86,16 @@
         )
 
 
-def block_probs(pieces, code, model_width, kv_width, after=None):
+def block_probs(pieces, seg, shuffled, model_width, kv_width, after=None):
     heads = model_width // kv_width
     key_heads = kv_width // HEAD_FEATURES
-    operands = [near(piece) for piece in pieces]
-    operands += [jnp.tile(code, heads)[None, :], code[:, None]]
+    operands = [near(piece) for piece in pieces] + [seg]
     specs = [VMEM] * len(operands)
     if after is not None:
         operands.append(after)
-        specs.append(pl.BlockSpec(memory_space=pl.ANY))
+        specs.append(ANY)
     return pl.pallas_call(
-        functools.partial(probs_kernel, len(pieces), model_width, kv_width),
+        functools.partial(probs_kernel, len(pieces), shuffled, model_width, kv_width),
         out_shape=(
             jax.ShapeDtypeStruct((key_heads, BLOCK, heads * BLOCK), jnp.bfloat16),
             jax.ShapeDtypeStruct((BLOCK, 128), jnp.float32),
@@ -139,6 +156,13 @@
     def store(columns, part):
         out_ref[:, columns] = part
 
+    if len(rest) == 5:
+
+        @pl.when(live_ref[0] == 0)
+        def _():
+            out_ref[...] = rest[0][...]
+            value_ref[...] = rest[1][...]
+
     @pl.when(live_ref[0] == 1)
     def _():
         layer_math(
@@ -146,82 +170,96 @@
         )
 
 
-def last_layer_kernel(
-    live_ref, grad_ref, x_ref, probs_ref, inv_ref, weight_ref, gain_ref,
-    first_ref, held_ref, held_value_ref, value_ref, *rest
-):
-    scaled_ref = rest[-1]
-    pieces = rest[:-1]
-    piece = BLOCK // len(pieces)
-
-    def store(columns, part):
-        for k, piece_ref in enumerate(pieces):
-            piece_ref[1, :, columns] = part[k * piece : (k + 1) * piece]
-
-    for k, piece_ref in enumerate(pieces):
-        piece_ref[0] = first_ref[k * piece : (k + 1) * piece, :]
-
-    @pl.when(live_ref[0] == 0)
-    def _():
-        value_ref[...] = held_value_ref[...]
-        for k, piece_ref in enumerate(pieces):
-            piece_ref[1] = held_ref[k * piece : (k + 1) * piece, :]
-
-    @pl.when(live_ref[0] == 1)
-    def _():
-        layer_math(
-            grad_ref, x_ref, probs_ref, inv_ref, weight_ref, gain_ref, scaled_ref, store, value_ref
-        )
-
-
-def layer_step(live, grad, x, probs, inv, weight, gain, held=None, after=None):
+def layer_step(live, grad, x, probs, inv, weight, gain, held=()):
     model_width, kv_width = weight.shape
-    operands = [live] + [near(array) for array in (grad, x, probs, inv, weight, gain)]
-    specs = [SMEM] + [VMEM] * 6
-    aliases = {}
-    if held is not None:
-        aliases = {len(operands): 0, len(operands) + 1: 1}
-        operands += [near(array) for array in held]
-        specs += [VMEM] * 2
-    if after is not None:
-        operands.append(after)
-        specs.append(pl.BlockSpec(memory_space=pl.ANY))
+    operands = [live, grad, x, probs, inv, weight, gain, *held]
     return pl.pallas_call(
         layer_kernel,
         out_shape=(
-            pltpu.VMEM((BLOCK, model_width), jnp.bfloat16),
-            pltpu.VMEM((BLOCK, kv_width), jnp.bfloat16),
+            jax.ShapeDtypeStruct((BLOCK, model_width), jnp.bfloat16),
+            jax.ShapeDtypeStruct((BLOCK, kv_width), jnp.bfloat16),
         ),
-        in_specs=specs,
+        in_specs=[SMEM] + [VMEM] * (len(operands) - 1),
         out_specs=(VMEM, VMEM),
         scratch_shapes=[pltpu.VMEM((BLOCK, model_width), jnp.float32)],
-        input_output_aliases=aliases,
         name="layer",
         **params(2 * BLOCK * model_width * kv_width),
     )(*operands)
 
 
-def last_layer_step(live, grad, x, probs, inv, weight, gain, first, held, count):
+def tick_kernel(tick, kept, pieces, *refs):
+    operands, refs = refs[:6], refs[6:]
+    earlier, refs = refs[: 2 * kept], refs[2 * kept :]
+    scaled_ref = refs[-1]
+    turn = lax.axis_size("section") - 1 - lax.axis_index("section")
+    if pieces:
+        first_ref, value_ref, outs = refs[0], refs[-2 - pieces], refs[-1 - pieces : -1]
+        rows = BLOCK // pieces
+        for k, out_ref in enumerate(outs):
+            out_ref[0] = first_ref[k * rows : (k + 1) * rows, :]
+
+        def store(columns, part):
+            for k, out_ref in enumerate(outs):
+                out_ref[1, :, columns] = part[k * rows : (k + 1) * rows]
+
+    else:
+        out_ref, value_ref = refs[-3:-1]
+
+        def store(columns, part):
+            out_ref[:, columns] = part
+
+    @pl.when(turn == tick)
+    def _():
+        layer_math(*operands, scaled_ref, store, value_ref)
+
+    for at in range(kept):
+
+        @pl.when(turn == at)
+        def _(at=at):
+            store(slice(None), earlier[2 * at][...])
+            value_ref[...] = earlier[2 * at + 1][...]
+
+
+def tick_step(tick, grad, block, weight, gain, kept=(), first=None, pieces=0, after=None):
     model_width, kv_width = weight.shape
-    operands = [live]
-    operands += [near(array) for array in (grad, x, probs, inv, weight, gain, first, *held)]
-    piece = jax.ShapeDtypeStruct((2, BLOCK // count, model_width), jnp.bfloat16)
+    probs, inv, x = block
+    operands = [near(array) for array in (grad, x, probs, inv, weight, gain)]
+    operands += [near(array) for pair in kept for array in pair]
+    if first is not None:
+        operands.append(near(first))
+    specs = [VMEM] * len(operands)
+    if after is not None:
+        operands.append(after)
+        specs.append(ANY)
+    rows = jax.ShapeDtypeStruct((BLOCK, model_width), jnp.bfloat16)
+    value = jax.ShapeDtypeStruct((BLOCK, kv_width), jnp.bfloat16)
+    if pieces:
+        piece = jax.ShapeDtypeStruct((2, BLOCK // pieces, model_width), jnp.bfloat16)
+        outs = (value,) + (piece,) * pieces
+    else:
+        outs = (rows, value)
     return pl.pallas_call(
-        last_layer_kernel,
-        out_shape=(jax.ShapeDtypeStruct((BLOCK, kv_width), jnp.bfloat16),) + (piece,) * count,
-        in_specs=[SMEM] + [VMEM] * (len(operands) - 1),
-        out_specs=(VMEM,) * (1 + count),
+        functools.partial(tick_kernel, tick, len(kept), pieces),
+        out_shape=outs,
+        in_specs=specs,
+        out_specs=(VMEM,) * len(outs),
         scratch_shapes=[pltpu.VMEM((BLOCK, model_width), jnp.float32)],
-        name="last_layer",
+        name="tick",
         **params(2 * BLOCK * model_width * kv_width),
     )(*operands)
 
 
-def pack_kernel(half, piece, me_ref, query_ref, key_ref, hidden_ref, up_ref, *rest):
+def place():
+    half = lax.axis_size("dp") // 2
+    me = lax.axis_index("dp")
+    return lax.div(me, half), lax.rem(me, half), me
+
+
+def pack_kernel(half, piece, query_ref, key_ref, hidden_ref, up_ref, *rest):
     sems = rest[-1]
     ups = rest[-3:-1]
     packed = rest[:-3]
-    side, at = me_ref[0], me_ref[1]
+    side, at, _ = place()
     copies = []
 
     def copy(source, target):
@@ -248,21 +286,22 @@
         made.wait()
 
 
-def columns_kernel(width, me_ref, first_ref, second_ref, *outs):
-    pair = me_ref[0]
+def columns_kernel(width, first_ref, second_ref, *outs):
+    pair = lax.div(place()[2], 2)
     for k, out_ref in enumerate(outs):
         start = pl.multiple_of(lax.bitwise_xor(pair, k) * width, width)
         out_ref[:BLOCK, :] = first_ref[:, pl.ds(start, width)]
         out_ref[BLOCK:, :] = second_ref[:, pl.ds(start, width)]
 
 
-def partial_kernel(count, shares, me_ref, *refs):
+def partial_kernel(count, shares, *refs):
     columns, first, second = refs[:count], refs[count : 2 * count], refs[2 * count : 3 * count]
     own_ref, other_ref = refs[-2:]
     value = jnp.concatenate(
         [ref[...] for pair in zip(first, second) for ref in pair], axis=0
     )
-    for ref, core in ((other_ref, 1 - me_ref[0]), (own_ref, me_ref[0])):
+    mine = lax.rem(place()[2], 2)
+    for ref, core in ((other_ref, 1 - mine), (own_ref, mine)):
         at = pl.ds(pl.multiple_of(core * shares, shares), shares)
         rows = jnp.concatenate([part[:, at] for part in columns], axis=0)
         ref[...] = lax.dot_general(
@@ -271,11 +310,11 @@
 
 
 def finish_kernel(
-    half, scale, me_ref, own_ref, other_ref, weight_ref, gain_ref, *refs
+    half, scale, own_ref, other_ref, weight_ref, gain_ref, *refs
 ):
     pieces = refs[:half]
     rows_ref, out_ref, gain_out_ref, sems = refs[half:]
-    side, at = me_ref[0], me_ref[1]
+    side, at, me = place()
     piece = pieces[0].shape[1]
     copies = []
     for block in range(2):
@@ -288,7 +327,7 @@
             made.start()
             copies.append(made)
     shares = own_ref.shape[0]
-    first = pl.multiple_of(me_ref[2] * shares, shares)
+    first = pl.multiple_of(me * shares, shares)
     gain = gain_ref[:, pl.ds(first, shares)]
     eye = lax.broadcasted_iota(jnp.int32, (shares, shares), 0) == lax.broadcasted_iota(
         jnp.int32, (shares, shares), 1
@@ -306,7 +345,7 @@
         made.wait()
 
 
-def direct(hidden, query, key, seg, weight, norm_gain, upstream):
+def direct(hidden, query, key, segments, weight, norm_gain, upstream):
     tokens, model_width = hidden.shape
     kv_width = key.shape[1]
     replicas = lax.axis_size("dp")
@@ -314,13 +353,12 @@
     half = replicas // 2
     piece = tokens // replicas
     shares = model_width // replicas
-    me = lax.axis_index("dp")
-    section = lax.axis_index("section")
-    side, at = me // half, me % half
-    place = jnp.stack([side, at, me]).astype(jnp.int32)
 
     def swap(array, k):
         return lax.ppermute(array, "dp", [(i, i ^ k) for i in range(replicas)])
+
+    def far(array):
+        return pltpu.with_memory_space_constraint(array, pltpu.HBM)
 
     count = 2 * half
     bf16 = jnp.bfloat16
@@ -328,71 +366,59 @@
         functools.partial(pack_kernel, half, piece),
         out_shape=(jax.ShapeDtypeStruct((piece, 2 * model_width + kv_width), bf16),) * count
         + (jax.ShapeDtypeStruct((BLOCK, model_width), bf16),) * 2,
-        in_specs=[SMEM] + [pl.BlockSpec(memory_space=pl.ANY)] * 4,
+        in_specs=[pl.BlockSpec(memory_space=pltpu.HBM)] * 4,
         out_specs=(VMEM,) * (count + 2),
         scratch_shapes=[pltpu.SemaphoreType.DMA((4 * count,))],
         name="pack",
         **params(0, 3 << 20),
-    )(place, query, key, hidden, upstream)
+    )(far(query), far(key), far(hidden), far(upstream))
     ups = packed[-2:]
-    seg_pieces = seg.reshape(2, half, piece)
-    order = jnp.bitwise_xor(at, jnp.arange(half, dtype=jnp.int32))
-    place_in_block = (order[:, None] * piece + jnp.arange(piece, dtype=jnp.int32)).reshape(-1)
-
-    def seg_of(which):
-        return seg_pieces[which][order].reshape(-1)
-
-    segs = [seg_of(side), swap(seg_of(1 - side), half)]
-    codes = [block_seg * BLOCK + place_in_block for block_seg in segs]
+    segs = [segments, swap(segments, half)]
     pieces = [
         [packed[b * half]] + [swap(packed[b * half + k], k) for k in range(1, half)]
         for b in range(2)
     ]
     grads = [ups[0], swap(ups[1], half)]
-    lives = [(section == layers - 1 - tick).astype(jnp.int32)[None] for tick in range(layers)]
-
-    blocks, held = [], []
+    blocks, kept = [], [[], []]
     for b in range(2):
-        after = held[0][0] if b else None
-        blocks.append(block_probs(pieces[b], codes[b], model_width, kv_width, after))
-        probs, inv, x = blocks[b]
-        held.append(layer_step(lives[0], grads[b], x, probs, inv, weight, norm_gain))
+        after = kept[0][0][0] if b else None
+        blocks.append(block_probs(pieces[b], segs[b], True, model_width, kv_width, after))
+        kept[b].append(tick_step(0, grads[b], blocks[b], weight, norm_gain))
 
     columns = pl.pallas_call(
         functools.partial(columns_kernel, 2 * shares),
         out_shape=(jax.ShapeDtypeStruct((2 * BLOCK, 2 * shares), bf16),) * half,
-        in_specs=[SMEM, VMEM, VMEM],
+        in_specs=[VMEM, VMEM],
         out_specs=(VMEM,) * half,
         name="columns",
         **params(0, 1 << 20),
-    )((me // 2)[None], blocks[0][2], blocks[1][2])
+    )(blocks[0][2], blocks[1][2])
     columns = [columns[0]] + [swap(columns[k], 2 * k) for k in range(1, half)]
 
     for tick in range(1, layers):
         hop = [(layers - tick, layers - 1 - tick)]
-        for b in range(2):
-            probs, inv, x = blocks[b]
-            grad = lax.ppermute(held[b][0], "section", hop)
-            if tick == layers - 1 and b == 1:
-                last = last_layer_step(
-                    lives[tick], grad, x, probs, inv, weight, norm_gain, held[0][0], held[1], half
-                )
-            else:
-                after = held[0][0] if b else None
-                held[b] = layer_step(
-                    lives[tick], grad, x, probs, inv, weight, norm_gain, held[b], after
-                )
-    values = [held[0][1], last[0]]
-    gathered = [[value] + [swap(value, 2 * k) for k in range(1, half)] for value in values]
-    rows = [last[1]] + [swap(last[1 + k], k) for k in range(1, half)]
+        grads = [lax.ppermute(kept[b][-1][0], "section", hop) for b in range(2)]
+        if tick < layers - 1:
+            kept[0].append(tick_step(tick, grads[0], blocks[0], weight, norm_gain))
+            after = kept[0][-1][0]
+            kept[1].append(tick_step(tick, grads[1], blocks[1], weight, norm_gain, after=after))
+    first, first_value = tick_step(layers - 1, grads[0], blocks[0], weight, norm_gain, kept[0])
+    last_value, *rows = tick_step(
+        layers - 1, grads[1], blocks[1], weight, norm_gain, kept[1], first, half
+    )
+    gathered = [
+        [value] + [swap(value, 2 * k) for k in range(1, half)]
+        for value in (first_value, last_value)
+    ]
+    rows = [rows[0]] + [swap(rows[k], k) for k in range(1, half)]
     own, other = pl.pallas_call(
         functools.partial(partial_kernel, half, shares),
         out_shape=(jax.ShapeDtypeStruct((shares, kv_width), jnp.float32),) * 2,
-        in_specs=[SMEM] + [VMEM] * (3 * half),
+        in_specs=[VMEM] * (3 * half),
         out_specs=(VMEM, VMEM),
         name="weight_partial",
-        **params(4 * tokens * half * shares * kv_width),
-    )((me % 2)[None], *columns, *gathered[0], *gathered[1])
+        **params(20 << 30),
+    )(*columns, *gathered[0], *gathered[1])
     other = swap(other, 1)
     scale = float(tokens * replicas) ** (-0.5)
     input_grad, weight_grad, gain_grad = pl.pallas_call(
@@ -402,12 +428,12 @@
             jax.ShapeDtypeStruct((shares, kv_width), jnp.float32),
             jax.ShapeDtypeStruct((1, shares), jnp.float32),
         ),
-        in_specs=[SMEM] + [VMEM] * (4 + half),
-        out_specs=(pl.BlockSpec(memory_space=pl.ANY), VMEM, VMEM),
+        in_specs=[VMEM] * (4 + half),
+        out_specs=(ANY, VMEM, VMEM),
         scratch_shapes=[pltpu.SemaphoreType.DMA((count,))],
         name="finish",
         **params(),
-    )(place, own, other, weight, norm_gain, *rows)
+    )(own, other, weight, norm_gain, *rows)
     return input_grad[None], weight_grad[None], gain_grad
 
 
@@ -425,7 +451,7 @@
     gain_out_ref[...] = sums[:1]
 
 
-def grouped(hidden, query, key, seg, weight, norm_gain, upstream):
+def grouped(hidden, query, key, segments, weight, norm_gain, upstream):
     tokens, model_width = hidden.shape
     kv_width = key.shape[1]
     replicas = lax.axis_size("dp")
@@ -453,15 +479,14 @@
     blocks, grads = [], []
     for which in range(2):
         up = rows_of(upstream, which)
-        block_seg = rows_of(seg, which)
+        seg = segments
         if which == 1:
             up = lax.ppermute(up, "dp", across)
-            block_seg = lax.ppermute(block_seg, "dp", across)
+            seg = lax.ppermute(seg, "dp", across)
         packed = jnp.concatenate(
             [rows_of(query, which), rows_of(key, which), rows_of(hidden, which)], axis=1
         )
-        code = block_seg * BLOCK + jnp.arange(BLOCK, dtype=jnp.int32)
-        blocks.append(block_probs([regroup(packed)], code, model_width, kv_width))
+        blocks.append(block_probs([regroup(packed)], seg, False, model_width, kv_width))
         grads.append(up)
 
     def layer(tick, which, grad, kept):
@@ -469,14 +494,14 @@
         probs, inv, x = blocks[which]
         return layer_step(live, grad, x, probs, inv, weight, norm_gain, kept)
 
-    held = [layer(0, which, grads[which], None) for which in range(2)]
+    held = [layer(0, which, grads[which], ()) for which in range(2)]
     hops = [(i, i - 1) for i in range(1, layers)]
 
-    def tick_step(tick, held):
+    def step(tick, held):
         grads = [lax.ppermute(kept[0], "section", hops) for kept in held]
         return [layer(tick, which, grads[which], held[which]) for which in range(2)]
 
-    held = lax.fori_loop(1, layers, tick_step, held)
+    held = lax.fori_loop(1, layers, step, held)
 
     columns, values, stored = [], [], []
     for which in range(2):
@@ -514,7 +539,7 @@
     piece = hidden_in.shape[1] // replicas
     plan = direct if piece % 16 == 0 and replicas in (4, 8) else grouped
     return plan(
-        hidden_in[0], queries[0], keys[0], segments[0], value_weight[0], norm_gain, upstream
+        hidden_in[0], queries[0], keys[0], segments, value_weight[0], norm_gain, upstream
     )
 
 

time: 95.4 us -> 73.1 us (0.77); the launches traced: 93.8 us -> 72.5 us
  local copies, waits for them, and re-layouts: 20.4 us -> 0.7 us
  waiting for transfers between devices: 25.3 us -> 36.1 us
  Pallas kernels: 18.1 us -> 7.31 us
  other arithmetic: 1.55 us -> 0 us
    unnamed x61 -> x6, local copies, waits for them, and re-layouts: 18.6 us -> 0.7 us
    ppermute x6, waiting for transfers between devices: 12.8 us -> 20.2 us  [direct(): grads = [lax.ppermute(kept[b][-1][0], 'section', hop) for b in range(2)]]
    pallas_call x10, Pallas kernels: 10.2 us -> 2.91 us  [the longest x8 2.35 us: tick_step(): pl.pallas_call(functools.partial(tick_kernel, tick, len(kept), pieces), o...]
    ppermute x21, waiting for transfers between devices: 12.5 us -> 16 us  [swap(): return lax.ppermute(array, 'dp', [(i, i ^ k) for i in range(replicas)])]
    ppermute x21, starting transfers between devices: 19.4 us -> 22.2 us  [swap(): return lax.ppermute(array, 'dp', [(i, i ^ k) for i in range(replicas)])]
    ppermute x6, starting transfers between devices: 7.98 us -> 5.28 us  [direct(): grads = [lax.ppermute(kept[b][-1][0], 'section', hop) for b in range(2)]]
    unnamed x1 -> x0, other arithmetic: 1.38 us -> none
    pallas_call x1, Pallas kernels: 3.14 us -> 1.88 us  [direct(): pl.pallas_call(functools.partial(pack_kernel, half, piece), out_shape=(ja...]
  transfers between devices with their start and end apart: 27 -> 27, of which waited for: 11 -> 13; matrix products, arithmetic and copies ran while one was open for 1% -> 0% of each run, Pallas kernels for 15% -> 4%
where the time goes in v3:
time: 73.1 us; the launch traced here: 72.5 us
  waiting for transfers between devices  36.1 us (49%)
  starting transfers between devices  27.5 us (38%)
  Pallas kernels  7.31 us (10%)
  between operations  0.9 us (1%)
    ppermute x21, starting transfers between devices, swap(): return lax.ppermute(array, 'dp', [(i, i ^ k) for i in range(replicas)])  22.2 us
    ppermute x6, waiting for transfers between devices, direct(): grads = [lax.ppermute(kept[b][-1][0], 'section', hop) for b in range(2)]  20.2 us
    ppermute x21, waiting for transfers between devices, swap(): return lax.ppermute(array, 'dp', [(i, i ^ k) for i in range(replicas)])  16 us
    ppermute x6, starting transfers between devices, direct(): grads = [lax.ppermute(kept[b][-1][0], 'section', hop) for b in range(2)]  5.28 us
    pallas_call x8, Pallas kernels, tick_step(): pl.pallas_call(functools.partial(tick_kernel, tick, len(kept), pieces), o...  2.35 us
    pallas_call x1, Pallas kernels, direct(): pl.pallas_call(functools.partial(finish_kernel, half, scale), out_shape=(...  1.99 us
    pallas_call x1, Pallas kernels, direct(): pl.pallas_call(functools.partial(pack_kernel, half, piece), out_shape=(ja...  1.88 us
  transfers between devices with their start and end apart: 27, of which 13 were waited for; matrix products, arithmetic and copies ran while one was open for 0% of the time, Pallas kernels for 4%

profile of v3, /device:TPU:0, one launch (start us, length us, event | category | flops | bytes accessed | tf_op | source)
XLA Modules:
  0.0 72.5 jit_solution(14749735406782309219)
XLA Ops:
  0.7 1.9 %pack.1 = (bf16[16,4608]{1,0:T(8,128)(2,1)S(1)}, bf16[16,4608]{1,0:T(8,128)(2,1)S(1)}, bf16[16,4608]{1,0:T(8,128)(2,1)S(1)}, bf16[16,4608]{1,0:T(8,128)(2,1)S(1)...) custom-call(bf16[128,2048]{1,0:T(8,128)(2,1)} %bitcast.15, ...), custom_call_target="tpu_custom_call" | custom-call | bytes 3145728 | tf_op jit(solution)/shard_map/pack/pallas_call | solution.py:365
  3.1 2.6 %collective-permute-start.1 = (bf16[16,4608]{1,0:T(8,128)(2,1)S(1)}, bf16[16,4608]{1,0:T(8,128)(2,1)S(1)}, u32[]{:S(2)}, u32[]{:S(2)}) collective-permute-start(bf16[16,4608]{1,0:T(8,128)(2,1)S(1)} %get-tuple-element.49), channel_id=1, source_target_pairs={{0,8},{4,12},{8,0},{12,4},{16,24},{20,28},{24,16},{28,20},{1,9},{5... | collective-permute-start | bytes 442376 | tf_op jit(solution)/shard_map/ppermute | solution.py:358
  5.6 1.5 %collective-permute-start.16 = (bf16[64,2048]{1,0:T(8,128)(2,1)S(1)}, bf16[64,2048]{1,0:T(8,128)(2,1)S(1)}, u32[]{:S(2)}, u32[]{:S(2)}) collective-permute-start(bf16[64,2048]{1,0:T(8,128)(2,1)S(1)} %get-tuple-element.71), channel_id=1, source_target_pairs={{0,16},{4,20},{8,24},{12,28},{16,0},{20,4},{24,8},{28,12},{1,17},{... | collective-permute-start | bytes 786440 | tf_op jit(solution)/shard_map/ppermute | solution.py:358
  7.8 1.5 %collective-permute-start.4 = (bf16[16,4608]{1,0:T(8,128)(2,1)S(1)}, bf16[16,4608]{1,0:T(8,128)(2,1)S(1)}, u32[]{:S(2)}, u32[]{:S(2)}) collective-permute-start(bf16[16,4608]{1,0:T(8,128)(2,1)S(1)} %get-tuple-element.54), channel_id=1, source_target_pairs={{0,8},{4,12},{8,0},{12,4},{16,24},{20,28},{24,16},{28,20},{1,9},{5... | collective-permute-start | bytes 442376 | tf_op jit(solution)/shard_map/ppermute | solution.py:358
  9.3 0.8 %collective-permute-done.1.refs_2_ = bf16[16,4608]{1,0:T(8,128)(2,1)S(1)} collective-permute-done((bf16[16,4608]{1,0:T(8,128)(2,1)S(1)}, bf16[16,4608]{1,0:T(8,128)(2,1)S(1)}, u32[]{:S(2)}, u32[]{:S(2)}) %collective-permute-start.1) | collective-permute-done | bytes 147488 | tf_op jit(solution)/shard_map/ppermute | solution.py:358
  10.1 1.0 %collective-permute-start.5 = (bf16[16,4608]{1,0:T(8,128)(2,1)S(1)}, bf16[16,4608]{1,0:T(8,128)(2,1)S(1)}, u32[]{:S(2)}, u32[]{:S(2)}) collective-permute-start(bf16[16,4608]{1,0:T(8,128)(2,1)S(1)} %get-tuple-element.55), channel_id=1, source_target_pairs={{0,12},{4,8},{8,4},{12,0},{16,28},{20,24},{24,20},{28,16},{1,13},{... | collective-permute-start | bytes 442376 | tf_op jit(solution)/shard_map/ppermute | solution.py:358
  11.1 2.1 %collective-permute-done.2.refs_3_ = bf16[16,4608]{1,0:T(8,128)(2,1)S(1)} collective-permute-done((bf16[16,4608]{1,0:T(8,128)(2,1)S(1)}, bf16[16,4608]{1,0:T(8,128)(2,1)S(1)}, u32[]{:S(2)}, u32[]{:S(2)}) %collective-permute-start.2) | collective-permute-done | bytes 147488 | tf_op jit(solution)/shard_map/ppermute | solution.py:358
  13.2 1.3 %collective-permute-start.6 = (s32[1,128]{1,0:T(1,128)}, s32[1,128]{1,0:T(1,128)S(1)}, u32[]{:S(2)}, u32[]{:S(2)}) collective-permute-start(s32[1,128]{1,0:T(1,128)} %refs_4_.1), channel_id=1, source_target_pairs={{0,16},{4,20},{8,24},{12,28},{16,0},{20,4},{24,8},{28,12},{1,17},{... | collective-permute-start | bytes 1544 | tf_op jit(solution)/shard_map/ppermute | solution.py:358
  14.6 0.7 copy-done.2
  15.6 1.3 %collective-permute-done.6.refs_4_ = s32[1,128]{1,0:T(1,128)S(1)} collective-permute-done((s32[1,128]{1,0:T(1,128)}, s32[1,128]{1,0:T(1,128)S(1)}, u32[]{:S(2)}, u32[]{:S(2)}) %collective-permute-start.6) | collective-permute-done | bytes 544 | tf_op jit(solution)/shard_map/ppermute | solution.py:358
  17.6 1.9 %collective-permute-done.5.refs_3_ = bf16[16,4608]{1,0:T(8,128)(2,1)S(1)} collective-permute-done((bf16[16,4608]{1,0:T(8,128)(2,1)S(1)}, bf16[16,4608]{1,0:T(8,128)(2,1)S(1)}, u32[]{:S(2)}, u32[]{:S(2)}) %collective-permute-start.5) | collective-permute-done | bytes 147488 | tf_op jit(solution)/shard_map/ppermute | solution.py:358
  19.9 0.7 collective-permute-start.17
  20.6 0.7 collective-permute-start.11
  21.3 0.7 collective-permute-start.18
  22.0 1.3 %collective-permute-start.12 = (bf16[64,2048]{1,0:T(8,128)(2,1)S(1)}, bf16[64,2048]{1,0:T(8,128)(2,1)S(1)}, u32[]{:S(2)}, u32[]{:S(2)}) collective-permute-start(bf16[64,2048]{1,0:T(8,128)(2,1)S(1)} %get-tuple-element.66.refs_10_.refs_6_), channel_id=1, source_target_pairs={{1,0},{5,4},{9,8},{13,12},{17,16},{21,20},{25,24},{29,28}} | collective-permute-start | bytes 786440 | tf_op jit(solution)/shard_map/ppermute | solution.py:400
  23.4 1.3 %collective-permute-start.19 = (bf16[64,2048]{1,0:T(8,128)(2,1)S(1)}, bf16[64,2048]{1,0:T(8,128)(2,1)S(1)}, u32[]{:S(2)}, u32[]{:S(2)}) collective-permute-start(bf16[64,2048]{1,0:T(8,128)(2,1)S(1)} %get-tuple-element.76.refs_10_), channel_id=1, source_target_pairs={{1,0},{5,4},{9,8},{13,12},{17,16},{21,20},{25,24},{29,28}} | collective-permute-start | bytes 786440 | tf_op jit(solution)/shard_map/ppermute | solution.py:400
  24.7 1.4 %collective-permute-start.7 = (bf16[128,512]{1,0:T(8,128)(2,1)S(1)}, bf16[128,512]{1,0:T(8,128)(2,1)S(1)}, u32[]{:S(2)}, u32[]{:S(2)}) collective-permute-start(bf16[128,512]{1,0:T(8,128)(2,1)S(1)} %get-tuple-element.62), channel_id=1, source_target_pairs={{0,8},{4,12},{8,0},{12,4},{16,24},{20,28},{24,16},{28,20},{1,9},{5... | collective-permute-start | bytes 393224 | tf_op jit(solution)/shard_map/ppermute | solution.py:358
  26.1 1.5 %collective-permute-start.8 = (bf16[128,512]{1,0:T(8,128)(2,1)S(1)}, bf16[128,512]{1,0:T(8,128)(2,1)S(1)}, u32[]{:S(2)}, u32[]{:S(2)}) collective-permute-start(bf16[128,512]{1,0:T(8,128)(2,1)S(1)} %get-tuple-element.63), channel_id=1, source_target_pairs={{0,16},{4,20},{8,24},{12,28},{16,0},{20,4},{24,8},{28,12},{1,17},{... | collective-permute-start | bytes 393224 | tf_op jit(solution)/shard_map/ppermute | solution.py:358
  28.3 17.0 %collective-permute-done.12.refs_0_ = bf16[64,2048]{1,0:T(8,128)(2,1)S(1)} collective-permute-done((bf16[64,2048]{1,0:T(8,128)(2,1)S(1)}, bf16[64,2048]{1,0:T(8,128)(2,1)S(1)}, u32[]{:S(2)}, u32[]{:S(2)}) %collective-permute-start.12) | collective-permute-done | bytes 262176 | tf_op jit(solution)/shard_map/ppermute | solution.py:400
  45.3 1.1 %tick.11 = (bf16[64,2048]{1,0:T(8,128)(2,1)S(1)}, bf16[64,512]{1,0:T(8,128)(2,1)S(1)}) custom-call(bf16[64,2048]{1,0:T(8,128)(2,1)S(1)} %collective-permute-done.12.refs_0_, bf16[64,2048]{1,0:T(8,128)(2,1)S(1)} %get-tuple-element.51.refs_1_.first_ref, bf16[4,64,256]{2,1,0:T(8,128)(2,1)S(1)} %get-tuple-element.57.refs_2_, ...), custom_call_target="tpu_custom_call" | custom-call | flops 134217728 | bytes 1048576 | tf_op jit(solution)/shard_map/tick/pallas_call | solution.py:241
  46.4 1.6 %collective-permute-start.15 = (bf16[64,512]{1,0:T(8,128)(2,1)S(1)}, bf16[64,512]{1,0:T(8,128)(2,1)S(1)}, u32[]{:S(2)}, u32[]{:S(2)}) collective-permute-start(bf16[64,512]{1,0:T(8,128)(2,1)S(1)} %get-tuple-element.70.refs_4_), channel_id=1, source_target_pairs={{0,24},{4,28},{8,16},{12,20},{16,8},{20,12},{24,0},{28,4},{1,25},{... | collective-permute-start | bytes 196616 | tf_op jit(solution)/shard_map/ppermute | solution.py:358
  48.1 3.1 %collective-permute-done.19.refs_0_ = bf16[64,2048]{1,0:T(8,128)(2,1)S(1)} collective-permute-done((bf16[64,2048]{1,0:T(8,128)(2,1)S(1)}, bf16[64,2048]{1,0:T(8,128)(2,1)S(1)}, u32[]{:S(2)}, u32[]{:S(2)}) %collective-permute-start.19) | collective-permute-done | bytes 262176 | tf_op jit(solution)/shard_map/ppermute | solution.py:400
  51.2 1.9 %collective-permute-start.14 = (bf16[64,512]{1,0:T(8,128)(2,1)S(1)}, bf16[64,512]{1,0:T(8,128)(2,1)S(1)}, u32[]{:S(2)}, u32[]{:S(2)}) collective-permute-start(bf16[64,512]{1,0:T(8,128)(2,1)S(1)} %get-tuple-element.70.refs_4_), channel_id=1, source_target_pairs={{0,16},{4,20},{8,24},{12,28},{16,0},{20,4},{24,8},{28,12},{1,17},{... | collective-permute-start | bytes 196616 | tf_op jit(solution)/shard_map/ppermute | solution.py:358
  53.0 1.1 %tick.15 = (bf16[64,512]{1,0:T(8,128)(2,1)S(1)}, bf16[2,16,2048]{2,1,0:T(8,128)(2,1)S(1)}, bf16[2,16,2048]{2,1,0:T(8,128)(2,1)S(1)}, bf16[2,16,2048]{2,1,0:T(8,128)(2,1)S(1)}, bf16[2,16,2048]{2,1,0:T(8,128)(2,1)S(1)}) custom-call(bf16[64,2048]{1,0:T(8,128)(2,1)S(1)} %collective-permute-done.19.refs_0_, ...), custom_call_target="tpu_custom_call" | custom-call | flops 134217728 | bytes 1048576 | tf_op jit(solution)/shard_map/tick/pallas_call | solution.py:241
  54.7 1.1 %collective-permute-start.22 = (bf16[64,512]{1,0:T(8,128)(2,1)S(1)}, bf16[64,512]{1,0:T(8,128)(2,1)S(1)}, u32[]{:S(2)}, u32[]{:S(2)}) collective-permute-start(bf16[64,512]{1,0:T(8,128)(2,1)S(1)} %get-tuple-element.81.refs_8_), channel_id=1, source_target_pairs={{0,24},{4,28},{8,16},{12,20},{16,8},{20,12},{24,0},{28,4},{1,25},{... | collective-permute-start | bytes 196616 | tf_op jit(solution)/shard_map/ppermute | solution.py:358
  55.9 1.9 %collective-permute-start.21 = (bf16[64,512]{1,0:T(8,128)(2,1)S(1)}, bf16[64,512]{1,0:T(8,128)(2,1)S(1)}, u32[]{:S(2)}, u32[]{:S(2)}) collective-permute-start(bf16[64,512]{1,0:T(8,128)(2,1)S(1)} %get-tuple-element.81.refs_8_), channel_id=1, source_target_pairs={{0,16},{4,20},{8,24},{12,28},{16,0},{20,4},{24,8},{28,12},{1,17},{... | collective-permute-start | bytes 196616 | tf_op jit(solution)/shard_map/ppermute | solution.py:358
  58.7 1.3 %collective-permute-done.22.refs_11_ = bf16[64,512]{1,0:T(8,128)(2,1)S(1)} collective-permute-done((bf16[64,512]{1,0:T(8,128)(2,1)S(1)}, bf16[64,512]{1,0:T(8,128)(2,1)S(1)}, u32[]{:S(2)}, u32[]{:S(2)}) %collective-permute-start.22) | collective-permute-done | bytes 65568 | tf_op jit(solution)/shard_map/ppermute | solution.py:358
  60.6 1.4 %collective-permute-done.20.refs_9_ = bf16[64,512]{1,0:T(8,128)(2,1)S(1)} collective-permute-done((bf16[64,512]{1,0:T(8,128)(2,1)S(1)}, bf16[64,512]{1,0:T(8,128)(2,1)S(1)}, u32[]{:S(2)}, u32[]{:S(2)}) %collective-permute-start.20) | collective-permute-done | bytes 65568 | tf_op jit(solution)/shard_map/ppermute | solution.py:358
  63.6 0.9 %collective-permute-start.26 = (bf16[2,16,2048]{2,1,0:T(8,128)(2,1)S(1)}, bf16[2,16,2048]{2,1,0:T(8,128)(2,1)S(1)}, u32[]{:S(2)}, u32[]{:S(2)}) collective-permute-start(bf16[2,16,2048]{2,1,0:T(8,128)(2,1)S(1)} %get-tuple-element.87), channel_id=1, source_target_pairs={{0,12},{4,8},{8,4},{12,0},{16,28},{20,24},{24,20},{28,16},{1,13},{... | collective-permute-start | bytes 393224 | tf_op jit(solution)/shard_map/ppermute | solution.py:358
  64.7 4.8 %collective-permute-done.25.refs_2_ = bf16[2,16,2048]{2,1,0:T(8,128)(2,1)S(1)} collective-permute-done((bf16[2,16,2048]{2,1,0:T(8,128)(2,1)S(1)}, bf16[2,16,2048]{2,1,0:T(8,128)(2,1)S(1)}, u32[]{:S(2)}, u32[]{:S(2)}) %collective-permute-start.25) | collective-permute-done | bytes 131104 | tf_op jit(solution)/shard_map/ppermute | solution.py:358
  69.4 1.1 %collective-permute-done.26.refs_3_ = bf16[2,16,2048]{2,1,0:T(8,128)(2,1)S(1)} collective-permute-done((bf16[2,16,2048]{2,1,0:T(8,128)(2,1)S(1)}, bf16[2,16,2048]{2,1,0:T(8,128)(2,1)S(1)}, u32[]{:S(2)}, u32[]{:S(2)}) %collective-permute-start.26) | collective-permute-done | bytes 131104 | tf_op jit(solution)/shard_map/ppermute | solution.py:358
  70.5 2.0 %finish.1 = (bf16[128,2048]{1,0:T(8,128)(2,1)}, f32[256,512]{1,0:T(8,128)}, f32[1,256]{1,0:T(1,128)}) custom-call(f32[256,512]{1,0:T(8,128)S(1)} %get-tuple-element.82.own_ref, f32[256,512]{1,0:T(8,128)S(1)} %collective-permute-done.23.other_ref, bf16[2048,512]{1,0:T(8,128)(2,1)S(1)} %bitcast.14, f32[1,2048]{1,0:T(1,128)S(1)} %copy-done.1, ...), custom_call_target="tpu_custom_call" | custom-call | bytes 1048576 | tf_op jit(solution)/shard_map/finish/pallas_call | solution.py:424
  (42 shorter events, 7.1 us)
Async XLA Ops:
  0.6 14.9 %copy-start.1 = (f32[1,2048]{1,0:T(1,128)S(1)}, f32[1,2048]{1,0:T(1,128)}, u32[]{:S(2)}) copy-start(f32[1,2048]{1,0:T(1,128)} %gain_ref.1) | copy-start | bytes 24580
  0.6 14.9 %copy-start = (bf16[1,2048,512]{2,1,0:T(8,128)(2,1)S(1)}, bf16[1,2048,512]{2,1,0:T(8,128)(2,1)}, u32[]{:S(2)}) copy-start(bf16[1,2048,512]{2,1,0:T(8,128)(2,1)} %param.11) | copy-start | bytes 6291460
  2.5 5.3 %collective-permute-start = (bf16[16,4608]{1,0:T(8,128)(2,1)S(1)}, bf16[16,4608]{1,0:T(8,128)(2,1)S(1)}, u32[]{:S(2)}, u32[]{:S(2)}) collective-permute-start(bf16[16,4608]{1,0:T(8,128)(2,1)S(1)} %get-tuple-element.48), channel_id=1, source_target_pairs={{0,4},{4,0},{8,12},{12,8},{16,20},{20,16},{24,28},{28,24},{1,5},{5... | collective-permute-start | bytes 442376 | tf_op jit(solution)/shard_map/ppermute | solution.py:358
  3.1 7.0 %collective-permute-start.1 = (bf16[16,4608]{1,0:T(8,128)(2,1)S(1)}, bf16[16,4608]{1,0:T(8,128)(2,1)S(1)}, u32[]{:S(2)}, u32[]{:S(2)}) collective-permute-start(bf16[16,4608]{1,0:T(8,128)(2,1)S(1)} %get-tuple-element.49), channel_id=1, source_target_pairs={{0,8},{4,12},{8,0},{12,4},{16,24},{20,28},{24,16},{28,20},{1,9},{5... | collective-permute-start | bytes 442376 | tf_op jit(solution)/shard_map/ppermute | solution.py:358
  5.6 14.2 %collective-permute-start.16 = (bf16[64,2048]{1,0:T(8,128)(2,1)S(1)}, bf16[64,2048]{1,0:T(8,128)(2,1)S(1)}, u32[]{:S(2)}, u32[]{:S(2)}) collective-permute-start(bf16[64,2048]{1,0:T(8,128)(2,1)S(1)} %get-tuple-element.71), channel_id=1, source_target_pairs={{0,16},{4,20},{8,24},{12,28},{16,0},{20,4},{24,8},{28,12},{1,17},{... | collective-permute-start | bytes 786440 | tf_op jit(solution)/shard_map/ppermute | solution.py:358
  7.1 6.1 %collective-permute-start.2 = (bf16[16,4608]{1,0:T(8,128)(2,1)S(1)}, bf16[16,4608]{1,0:T(8,128)(2,1)S(1)}, u32[]{:S(2)}, u32[]{:S(2)}) collective-permute-start(bf16[16,4608]{1,0:T(8,128)(2,1)S(1)} %get-tuple-element.50), channel_id=1, source_target_pairs={{0,12},{4,8},{8,4},{12,0},{16,28},{20,24},{24,20},{28,16},{1,13},{... | collective-permute-start | bytes 442376 | tf_op jit(solution)/shard_map/ppermute | solution.py:358
  7.2 10.4 %collective-permute-start.3 = (bf16[16,4608]{1,0:T(8,128)(2,1)S(1)}, bf16[16,4608]{1,0:T(8,128)(2,1)S(1)}, u32[]{:S(2)}, u32[]{:S(2)}) collective-permute-start(bf16[16,4608]{1,0:T(8,128)(2,1)S(1)} %get-tuple-element.53), channel_id=1, source_target_pairs={{0,4},{4,0},{8,12},{12,8},{16,20},{20,16},{24,28},{28,24},{1,5},{5... | collective-permute-start | bytes 442376 | tf_op jit(solution)/shard_map/ppermute | solution.py:358
  7.8 9.8 %collective-permute-start.4 = (bf16[16,4608]{1,0:T(8,128)(2,1)S(1)}, bf16[16,4608]{1,0:T(8,128)(2,1)S(1)}, u32[]{:S(2)}, u32[]{:S(2)}) collective-permute-start(bf16[16,4608]{1,0:T(8,128)(2,1)S(1)} %get-tuple-element.54), channel_id=1, source_target_pairs={{0,8},{4,12},{8,0},{12,4},{16,24},{20,28},{24,16},{28,20},{1,9},{5... | collective-permute-start | bytes 442376 | tf_op jit(solution)/shard_map/ppermute | solution.py:358
  10.1 9.5 %collective-permute-start.5 = (bf16[16,4608]{1,0:T(8,128)(2,1)S(1)}, bf16[16,4608]{1,0:T(8,128)(2,1)S(1)}, u32[]{:S(2)}, u32[]{:S(2)}) collective-permute-start(bf16[16,4608]{1,0:T(8,128)(2,1)S(1)} %get-tuple-element.55), channel_id=1, source_target_pairs={{0,12},{4,8},{8,4},{12,0},{16,28},{20,24},{24,20},{28,16},{1,13},{... | collective-permute-start | bytes 442376 | tf_op jit(solution)/shard_map/ppermute | solution.py:358
  13.2 3.7 %collective-permute-start.6 = (s32[1,128]{1,0:T(1,128)}, s32[1,128]{1,0:T(1,128)S(1)}, u32[]{:S(2)}, u32[]{:S(2)}) collective-permute-start(s32[1,128]{1,0:T(1,128)} %refs_4_.1), channel_id=1, source_target_pairs={{0,16},{4,20},{8,24},{12,28},{16,0},{20,4},{24,8},{28,12},{1,17},{... | collective-permute-start | bytes 1544 | tf_op jit(solution)/shard_map/ppermute | solution.py:358
  14.6 0.7 copy-start.2
  16.9 3.7 %collective-permute-start.10 = (bf16[64,2048]{1,0:T(8,128)(2,1)S(1)}, bf16[64,2048]{1,0:T(8,128)(2,1)S(1)}, u32[]{:S(2)}, u32[]{:S(2)}) collective-permute-start(bf16[64,2048]{1,0:T(8,128)(2,1)S(1)} %get-tuple-element.59.refs_5_.refs_6_), channel_id=1, source_target_pairs={{3,2},{7,6},{11,10},{15,14},{19,18},{23,22},{27,26},{31,30}} | collective-permute-start | bytes 786440 | tf_op jit(solution)/shard_map/ppermute | solution.py:400
  19.9 1.4 %collective-permute-start.17 = (bf16[64,2048]{1,0:T(8,128)(2,1)S(1)}, bf16[64,2048]{1,0:T(8,128)(2,1)S(1)}, u32[]{:S(2)}, u32[]{:S(2)}) collective-permute-start(bf16[64,2048]{1,0:T(8,128)(2,1)S(1)} %get-tuple-element.74.refs_6_), channel_id=1, source_target_pairs={{3,2},{7,6},{11,10},{15,14},{19,18},{23,22},{27,26},{31,30}} | collective-permute-start | bytes 786440 | tf_op jit(solution)/shard_map/ppermute | solution.py:400
  20.6 1.4 %collective-permute-start.11 = (bf16[64,2048]{1,0:T(8,128)(2,1)S(1)}, bf16[64,2048]{1,0:T(8,128)(2,1)S(1)}, u32[]{:S(2)}, u32[]{:S(2)}) collective-permute-start(bf16[64,2048]{1,0:T(8,128)(2,1)S(1)} %get-tuple-element.65.refs_8_.refs_6_), channel_id=1, source_target_pairs={{2,1},{6,5},{10,9},{14,13},{18,17},{22,21},{26,25},{30,29}} | collective-permute-start | bytes 786440 | tf_op jit(solution)/shard_map/ppermute | solution.py:400
  21.3 2.0 %collective-permute-start.18 = (bf16[64,2048]{1,0:T(8,128)(2,1)S(1)}, bf16[64,2048]{1,0:T(8,128)(2,1)S(1)}, u32[]{:S(2)}, u32[]{:S(2)}) collective-permute-start(bf16[64,2048]{1,0:T(8,128)(2,1)S(1)} %get-tuple-element.75.refs_8_), channel_id=1, source_target_pairs={{2,1},{6,5},{10,9},{14,13},{18,17},{22,21},{26,25},{30,29}} | collective-permute-start | bytes 786440 | tf_op jit(solution)/shard_map/ppermute | solution.py:400
  22.0 23.3 %collective-permute-start.12 = (bf16[64,2048]{1,0:T(8,128)(2,1)S(1)}, bf16[64,2048]{1,0:T(8,128)(2,1)S(1)}, u32[]{:S(2)}, u32[]{:S(2)}) collective-permute-start(bf16[64,2048]{1,0:T(8,128)(2,1)S(1)} %get-tuple-element.66.refs_10_.refs_6_), channel_id=1, source_target_pairs={{1,0},{5,4},{9,8},{13,12},{17,16},{21,20},{25,24},{29,28}} | collective-permute-start | bytes 786440 | tf_op jit(solution)/shard_map/ppermute | solution.py:400
  23.4 27.8 %collective-permute-start.19 = (bf16[64,2048]{1,0:T(8,128)(2,1)S(1)}, bf16[64,2048]{1,0:T(8,128)(2,1)S(1)}, u32[]{:S(2)}, u32[]{:S(2)}) collective-permute-start(bf16[64,2048]{1,0:T(8,128)(2,1)S(1)} %get-tuple-element.76.refs_10_), channel_id=1, source_target_pairs={{1,0},{5,4},{9,8},{13,12},{17,16},{21,20},{25,24},{29,28}} | collective-permute-start | bytes 786440 | tf_op jit(solution)/shard_map/ppermute | solution.py:400
  24.7 29.5 %collective-permute-start.7 = (bf16[128,512]{1,0:T(8,128)(2,1)S(1)}, bf16[128,512]{1,0:T(8,128)(2,1)S(1)}, u32[]{:S(2)}, u32[]{:S(2)}) collective-permute-start(bf16[128,512]{1,0:T(8,128)(2,1)S(1)} %get-tuple-element.62), channel_id=1, source_target_pairs={{0,8},{4,12},{8,0},{12,4},{16,24},{20,28},{24,16},{28,20},{1,9},{5... | collective-permute-start | bytes 393224 | tf_op jit(solution)/shard_map/ppermute | solution.py:358
  26.1 28.7 %collective-permute-start.8 = (bf16[128,512]{1,0:T(8,128)(2,1)S(1)}, bf16[128,512]{1,0:T(8,128)(2,1)S(1)}, u32[]{:S(2)}, u32[]{:S(2)}) collective-permute-start(bf16[128,512]{1,0:T(8,128)(2,1)S(1)} %get-tuple-element.63), channel_id=1, source_target_pairs={{0,16},{4,20},{8,24},{12,28},{16,0},{20,4},{24,8},{28,12},{1,17},{... | collective-permute-start | bytes 393224 | tf_op jit(solution)/shard_map/ppermute | solution.py:358
  27.6 28.3 %collective-permute-start.9 = (bf16[128,512]{1,0:T(8,128)(2,1)S(1)}, bf16[128,512]{1,0:T(8,128)(2,1)S(1)}, u32[]{:S(2)}, u32[]{:S(2)}) collective-permute-start(bf16[128,512]{1,0:T(8,128)(2,1)S(1)} %get-tuple-element.64), channel_id=1, source_target_pairs={{0,24},{4,28},{8,16},{12,20},{16,8},{20,12},{24,0},{28,4},{1,25},{... | collective-permute-start | bytes 393224 | tf_op jit(solution)/shard_map/ppermute | solution.py:358
  46.4 11.3 %collective-permute-start.15 = (bf16[64,512]{1,0:T(8,128)(2,1)S(1)}, bf16[64,512]{1,0:T(8,128)(2,1)S(1)}, u32[]{:S(2)}, u32[]{:S(2)}) collective-permute-start(bf16[64,512]{1,0:T(8,128)(2,1)S(1)} %get-tuple-element.70.refs_4_), channel_id=1, source_target_pairs={{0,24},{4,28},{8,16},{12,20},{16,8},{20,12},{24,0},{28,4},{1,25},{... | collective-permute-start | bytes 196616 | tf_op jit(solution)/shard_map/ppermute | solution.py:358
  51.2 7.1 %collective-permute-start.14 = (bf16[64,512]{1,0:T(8,128)(2,1)S(1)}, bf16[64,512]{1,0:T(8,128)(2,1)S(1)}, u32[]{:S(2)}, u32[]{:S(2)}) collective-permute-start(bf16[64,512]{1,0:T(8,128)(2,1)S(1)} %get-tuple-element.70.refs_4_), channel_id=1, source_target_pairs={{0,16},{4,20},{8,24},{12,28},{16,0},{20,4},{24,8},{28,12},{1,17},{... | collective-permute-start | bytes 196616 | tf_op jit(solution)/shard_map/ppermute | solution.py:358
  54.2 4.5 %collective-permute-start.13 = (bf16[64,512]{1,0:T(8,128)(2,1)S(1)}, bf16[64,512]{1,0:T(8,128)(2,1)S(1)}, u32[]{:S(2)}, u32[]{:S(2)}) collective-permute-start(bf16[64,512]{1,0:T(8,128)(2,1)S(1)} %get-tuple-element.70.refs_4_), channel_id=1, source_target_pairs={{0,8},{4,12},{8,0},{12,4},{16,24},{20,28},{24,16},{28,20},{1,9},{5... | collective-permute-start | bytes 196616 | tf_op jit(solution)/shard_map/ppermute | solution.py:358
  54.7 5.2 %collective-permute-start.22 = (bf16[64,512]{1,0:T(8,128)(2,1)S(1)}, bf16[64,512]{1,0:T(8,128)(2,1)S(1)}, u32[]{:S(2)}, u32[]{:S(2)}) collective-permute-start(bf16[64,512]{1,0:T(8,128)(2,1)S(1)} %get-tuple-element.81.refs_8_), channel_id=1, source_target_pairs={{0,24},{4,28},{8,16},{12,20},{16,8},{20,12},{24,0},{28,4},{1,25},{... | collective-permute-start | bytes 196616 | tf_op jit(solution)/shard_map/ppermute | solution.py:358
  55.9 4.7 %collective-permute-start.21 = (bf16[64,512]{1,0:T(8,128)(2,1)S(1)}, bf16[64,512]{1,0:T(8,128)(2,1)S(1)}, u32[]{:S(2)}, u32[]{:S(2)}) collective-permute-start(bf16[64,512]{1,0:T(8,128)(2,1)S(1)} %get-tuple-element.81.refs_8_), channel_id=1, source_target_pairs={{0,16},{4,20},{8,24},{12,28},{16,0},{20,4},{24,8},{28,12},{1,17},{... | collective-permute-start | bytes 196616 | tf_op jit(solution)/shard_map/ppermute | solution.py:358
  57.7 4.3 %collective-permute-start.20 = (bf16[64,512]{1,0:T(8,128)(2,1)S(1)}, bf16[64,512]{1,0:T(8,128)(2,1)S(1)}, u32[]{:S(2)}, u32[]{:S(2)}) collective-permute-start(bf16[64,512]{1,0:T(8,128)(2,1)S(1)} %get-tuple-element.81.refs_8_), channel_id=1, source_target_pairs={{0,8},{4,12},{8,0},{12,4},{16,24},{20,28},{24,16},{28,20},{1,9},{5... | collective-permute-start | bytes 196616 | tf_op jit(solution)/shard_map/ppermute | solution.py:358
  62.5 8.0 %collective-permute-start.23 = (f32[256,512]{1,0:T(8,128)S(1)}, f32[256,512]{1,0:T(8,128)S(1)}, u32[]{:S(2)}, u32[]{:S(2)}) collective-permute-start(f32[256,512]{1,0:T(8,128)S(1)} %get-tuple-element.83), channel_id=1, source_target_pairs={{0,4},{4,0},{8,12},{12,8},{16,20},{20,16},{24,28},{28,24},{1,5},{5... | collective-permute-start | bytes 1572872 | tf_op jit(solution)/shard_map/ppermute | solution.py:358
  62.6 2.1 %collective-permute-start.24 = (bf16[2,16,2048]{2,1,0:T(8,128)(2,1)S(1)}, bf16[2,16,2048]{2,1,0:T(8,128)(2,1)S(1)}, u32[]{:S(2)}, u32[]{:S(2)}) collective-permute-start(bf16[2,16,2048]{2,1,0:T(8,128)(2,1)S(1)} %get-tuple-element.85), channel_id=1, source_target_pairs={{0,4},{4,0},{8,12},{12,8},{16,20},{20,16},{24,28},{28,24},{1,5},{5... | collective-permute-start | bytes 393224 | tf_op jit(solution)/shard_map/ppermute | solution.py:358
  63.1 6.4 %collective-permute-start.25 = (bf16[2,16,2048]{2,1,0:T(8,128)(2,1)S(1)}, bf16[2,16,2048]{2,1,0:T(8,128)(2,1)S(1)}, u32[]{:S(2)}, u32[]{:S(2)}) collective-permute-start(bf16[2,16,2048]{2,1,0:T(8,128)(2,1)S(1)} %get-tuple-element.86), channel_id=1, source_target_pairs={{0,8},{4,12},{8,0},{12,4},{16,24},{20,28},{24,16},{28,20},{1,9},{5... | collective-permute-start | bytes 393224 | tf_op jit(solution)/shard_map/ppermute | solution.py:358
  63.6 6.9 %collective-permute-start.26 = (bf16[2,16,2048]{2,1,0:T(8,128)(2,1)S(1)}, bf16[2,16,2048]{2,1,0:T(8,128)(2,1)S(1)}, u32[]{:S(2)}, u32[]{:S(2)}) collective-permute-start(bf16[2,16,2048]{2,1,0:T(8,128)(2,1)S(1)} %get-tuple-element.87), channel_id=1, source_target_pairs={{0,12},{4,8},{8,4},{12,0},{16,28},{20,24},{24,20},{28,16},{1,13},{... | collective-permute-start | bytes 393224 | tf_op jit(solution)/shard_map/ppermute | solution.py:358

commit v4 on v3

v4 whole, which is shorter than its diff:
```python
import functools

import jax
import jax.numpy as jnp
from jax import lax
from jax.experimental import pallas as pl
from jax.experimental.pallas import tpu as pltpu
from jax.sharding import PartitionSpec as P

HEAD_FEATURES = 128
BLOCK = 64
UNIT = 32
EPSILON = 1e-06
MASKED = -1e30
VMEM = pl.BlockSpec(memory_space=pltpu.VMEM)
SMEM = pl.BlockSpec(memory_space=pltpu.SMEM)


ANY = pl.BlockSpec(memory_space=pl.ANY)


LATE, EARLY = slice(UNIT, BLOCK), slice(0, UNIT)


def params(flops=0, nbytes=1 << 20):
    return dict(
        compiler_params=pltpu.CompilerParams(vmem_limit_bytes=16 << 20),
        cost_estimate=pl.CostEstimate(flops=flops, bytes_accessed=nbytes, transcendentals=0),
    )


def near(array):
    return pltpu.with_memory_space_constraint(array, pltpu.VMEM)


def place():
    half = lax.axis_size("dp") // 2
    me = lax.axis_index("dp")
    return lax.div(me, half), lax.rem(me, half), me


def probs_kernel(count, seg_row, model_width, kv_width, *refs):
    pieces, seg_ref = refs[:count], refs[count]
    late_ref, early_ref, inv_ref, x_ref, rows_ref = refs[-5:]
    heads = model_width // kv_width
    rows = BLOCK // count
    side, at, _ = place()
    for k, piece in enumerate(pieces):
        if count == 1:
            rows_ref[...] = piece[...]
        else:
            first = pl.multiple_of(lax.bitwise_xor(at, k) * rows, rows)
            rows_ref[pl.ds(first, rows), :] = piece[...]

    def iota(shape, axis):
        return lax.broadcasted_iota(jnp.int32, shape, axis)

    seg = seg_ref[seg_row : seg_row + 16, : 2 * BLOCK].astype(jnp.float32)[:1]
    shape = (BLOCK, 2 * BLOCK)
    wanted = iota(shape, 1) == side * BLOCK + iota(shape, 0)
    ids = jnp.sum(jnp.where(wanted, seg, 0.0), axis=1, keepdims=True)
    key_code = ids * BLOCK + iota((BLOCK, 1), 0).astype(jnp.float32)
    list_start = ids * BLOCK
    shape = (BLOCK, heads * BLOCK)
    column = iota(shape, 1)
    query_at = lax.rem(column, UNIT) + jnp.where(column < heads * UNIT, UNIT, 0)
    same = iota(shape, 0) == query_at
    query_code = jnp.sum(jnp.where(same, key_code, 0.0), axis=0, keepdims=True)
    query_start = jnp.sum(jnp.where(same, list_start, 0.0), axis=0, keepdims=True)
    allowed = (key_code <= query_code) & (key_code >= query_start)
    for c in range(kv_width // HEAD_FEATURES):
        first = c * heads * HEAD_FEATURES
        query_stack = jnp.concatenate(
            [
                rows_ref[part, first + h * HEAD_FEATURES : first + (h + 1) * HEAD_FEATURES]
                for part in (LATE, EARLY)
                for h in range(heads)
            ],
            axis=0,
        )
        key_first = model_width + c * HEAD_FEATURES
        keys = rows_ref[:, key_first : key_first + HEAD_FEATURES]
        scores = lax.dot_general(
            keys, query_stack, (((1,), (1,)), ((), ())), preferred_element_type=jnp.float32
        ) * HEAD_FEATURES ** (-0.5)
        scores = jnp.where(allowed, scores, MASKED)
        exp_scores = jnp.exp(scores - jnp.max(scores, axis=0, keepdims=True))
        total = jnp.sum(exp_scores, axis=0, keepdims=True)
        probs = (exp_scores / total).astype(jnp.bfloat16)
        late_ref[c] = probs[LATE, : heads * UNIT]
        early_ref[c] = probs[EARLY]
    hidden = rows_ref[:, model_width + kv_width :]
    x_ref[...] = hidden
    x = hidden.astype(jnp.float32)
    mean_square = jnp.mean(x * x, axis=1, keepdims=True)
    inv_ref[...] = jnp.broadcast_to(lax.rsqrt(mean_square + EPSILON), inv_ref.shape)


def block_probs(pieces, seg, seg_row, model_width, kv_width, after=None):
    heads = model_width // kv_width
    key_heads = kv_width // HEAD_FEATURES
    operands = [near(piece) for piece in pieces] + [near(seg)]
    specs = [VMEM] * len(operands)
    if after is not None:
        operands.append(after)
        specs.append(ANY)
    return pl.pallas_call(
        functools.partial(probs_kernel, len(pieces), seg_row, model_width, kv_width),
        out_shape=(
            jax.ShapeDtypeStruct((key_heads, UNIT, heads * UNIT), jnp.bfloat16),
            jax.ShapeDtypeStruct((key_heads, UNIT, heads * BLOCK), jnp.bfloat16),
            jax.ShapeDtypeStruct((BLOCK, 128), jnp.float32),
            jax.ShapeDtypeStruct((BLOCK, model_width), jnp.bfloat16),
        ),
        in_specs=specs,
        out_specs=(VMEM,) * 4,
        scratch_shapes=[pltpu.VMEM((BLOCK, 2 * model_width + kv_width), jnp.bfloat16)],
        name="probs",
        **params(4 * BLOCK * BLOCK * model_width),
    )(*operands)


def unit_math(rows, grads, probs_ref, x_ref, inv_ref, weight_ref, gain_ref, scaled_ref, store, value_ref):
    model_width = x_ref.shape[1]
    kv_width = weight_ref.shape[1]
    heads = model_width // kv_width
    chunk = min(512, model_width)
    inv = inv_ref[rows, :1]
    values = []
    for c in range(kv_width // HEAD_FEATURES):
        first = c * heads * HEAD_FEATURES
        grad_stack = jnp.concatenate(
            [
                grad_ref[part, first + h * HEAD_FEATURES : first + (h + 1) * HEAD_FEATURES]
                for grad_ref, part in grads
                for h in range(heads)
            ],
            axis=0,
        )
        values.append(
            jnp.dot(probs_ref[c], grad_stack, preferred_element_type=jnp.float32).astype(
                jnp.bfloat16
            )
        )
    value = jnp.concatenate(values, axis=1)
    value_ref[...] = (value.astype(jnp.float32) * inv).astype(jnp.bfloat16)
    inner = jnp.zeros((UNIT, 1), jnp.float32)
    for first in range(0, model_width, chunk):
        columns = slice(first, first + chunk)
        normed_grad = lax.dot_general(
            value, weight_ref[columns, :], (((1,), (1,)), ((), ())),
            preferred_element_type=jnp.float32,
        )
        scaled = normed_grad * gain_ref[:, columns]
        scaled_ref[:, columns] = scaled
        x = x_ref[rows, columns].astype(jnp.float32)
        inner = inner + jnp.sum(x * scaled, axis=1, keepdims=True)
    pull = inner * (inv * inv / model_width)
    grad_ref, part = grads[-1]
    for first in range(0, model_width, chunk):
        columns = slice(first, first + chunk)
        x = x_ref[rows, columns].astype(jnp.float32)
        change = inv * (scaled_ref[:, columns] - x * pull)
        grad = grad_ref[part, columns].astype(jnp.float32)
        store(columns, (grad + change).astype(jnp.bfloat16))


def layer_kernel(
    live_ref, grad_ref, late_ref, early_ref, inv_ref, x_ref, weight_ref, gain_ref, *rest
):
    out_ref, value_ref, scaled_ref = rest[-3:]
    if len(rest) == 5:

        @pl.when(live_ref[0] == 0)
        def _():
            out_ref[...] = rest[0][...]
            value_ref[...] = rest[1][...]

    @pl.when(live_ref[0] == 1)
    def _():
        for rows, parts, probs_ref in ((LATE, [LATE], late_ref), (EARLY, [LATE, EARLY], early_ref)):

            def store(columns, part, rows=rows):
                out_ref[rows, columns] = part

            grads = [(grad_ref, part) for part in parts]
            unit_math(
                rows, grads, probs_ref, x_ref, inv_ref, weight_ref, gain_ref, scaled_ref, store,
                value_ref.at[rows],
            )


def layer_step(live, grad, block, weight, gain, held=()):
    model_width, kv_width = weight.shape
    operands = [live, grad, *block, weight, gain, *held]
    return pl.pallas_call(
        layer_kernel,
        out_shape=(
            jax.ShapeDtypeStruct((BLOCK, model_width), jnp.bfloat16),
            jax.ShapeDtypeStruct((BLOCK, kv_width), jnp.bfloat16),
        ),
        in_specs=[SMEM] + [VMEM] * (len(operands) - 1),
        out_specs=(VMEM, VMEM),
        scratch_shapes=[pltpu.VMEM((UNIT, model_width), jnp.float32)],
        name="layer",
        **params(2 * BLOCK * model_width * kv_width),
    )(*operands)


def tick_kernel(tick, rows, parts, kept, final, *refs):
    grads = list(zip(refs, parts))
    probs_ref, inv_ref, x_ref, weight_ref, gain_ref = refs[len(parts) : len(parts) + 5]
    refs = refs[len(parts) + 5 :]
    earlier, refs = refs[: 2 * kept], refs[2 * kept :]
    model_width, kv_width = x_ref.shape[1], weight_ref.shape[1]
    turn = lax.axis_size("section") - 1 - lax.axis_index("section")
    if final:
        late_ref, late_value_ref = refs[:2]
        values_ref, *outs = refs[-8:-3]
        scaled_ref, block_ref, value_ref = refs[-3:]

        def store(columns, part):
            block_ref[EARLY, columns] = part

    else:
        out_ref, value_ref, scaled_ref = refs[-3:]

        def store(columns, part):
            out_ref[:, columns] = part

    @pl.when(turn == tick)
    def _():
        unit_math(
            rows, grads, probs_ref, x_ref, inv_ref, weight_ref, gain_ref, scaled_ref, store,
            value_ref,
        )

    for at in range(kept):

        @pl.when(turn == at)
        def _(at=at):
            store(slice(None), earlier[2 * at][...])
            value_ref[...] = earlier[2 * at + 1][...]

    if final:
        block_ref[LATE, :] = late_ref[...]
        at = place()[1]
        piece = outs[0].shape[0]
        for k, out_ref in enumerate(outs):
            first = pl.multiple_of(lax.bitwise_xor(at, k) * piece, piece)
            out_ref[:piece, :] = block_ref[pl.ds(first, piece), :]
        values = [value_ref[...], late_value_ref[...]]
        if final == 2:
            values = [refs[2][...]] + values
            groups = model_width // kv_width
            whole = jnp.concatenate(values, axis=0)
            values_ref[...] = whole
            share = 2 * BLOCK // groups
            for g in range(groups):
                outs[2][piece:, g * kv_width : (g + 1) * kv_width] = whole[
                    g * share : (g + 1) * share
                ]
        else:
            values_ref[...] = jnp.concatenate(values, axis=0)


def tick_step(tick, grads, block, weight, gain, kept=(), late=(), after=()):
    model_width, kv_width = weight.shape
    low = len(grads) == 2
    final = len(late) - 1 if late else 0
    arrays = [grad for grad, _ in grads]
    arrays += [block[1] if low else block[0], block[2], block[3], weight, gain]
    arrays += [array for pair in kept for array in pair]
    arrays += late
    operands = [near(array) for array in arrays]
    specs = [VMEM] * len(operands) + [ANY] * len(after)
    bf16 = jnp.bfloat16
    scratch = [pltpu.VMEM((UNIT, model_width), jnp.float32)]
    if final:
        scratch += [pltpu.VMEM((BLOCK, model_width), bf16), pltpu.VMEM((UNIT, kv_width), bf16)]
        half = lax.axis_size("dp") // 2
        piece = BLOCK // half
        heights = [piece] * half
        if final == 2:
            heights[2] += 2 * BLOCK * kv_width // model_width
        outs = (jax.ShapeDtypeStruct((final * BLOCK, kv_width), bf16),)
        outs += tuple(jax.ShapeDtypeStruct((rows, model_width), bf16) for rows in heights)
    else:
        outs = (
            jax.ShapeDtypeStruct((UNIT, model_width), bf16),
            jax.ShapeDtypeStruct((UNIT, kv_width), bf16),
        )
    return pl.pallas_call(
        functools.partial(
            tick_kernel, tick, EARLY if low else LATE, [part for _, part in grads], len(kept), final
        ),
        out_shape=outs,
        in_specs=specs,
        out_specs=(VMEM,) * len(outs),
        scratch_shapes=scratch,
        name="tick",
        **params(2 * UNIT * model_width * kv_width),
    )(*operands, *after)


def pack_kernel(half, piece, query_ref, key_ref, hidden_ref, up_ref, seg_ref, *rest):
    sems = rest[-1]
    seg_out_ref, own_up_ref, across_ref = rest[-4:-1]
    packed = rest[:-4]
    side, at, _ = place()
    copies = []

    def copy(source, target):
        made = pltpu.make_async_copy(source, target, sems.at[len(copies)])
        made.start()
        copies.append(made)

    for block in range(2):
        for k in range(half):
            replica = (side if block == 0 else 1 - side) * half + lax.bitwise_xor(at, k)
            rows = pl.ds(pl.multiple_of(replica * piece, piece), piece)
            target = packed[block * half + k]
            first = 0
            for source in (query_ref, key_ref, hidden_ref):
                width = source.shape[1]
                copy(source.at[rows], target.at[:, pl.ds(first, width)])
                first += width
    for there, target in ((side, own_up_ref), (1 - side, across_ref.at[pl.ds(0, BLOCK)])):
        copy(up_ref.at[pl.ds(pl.multiple_of(there * BLOCK, BLOCK), BLOCK)], target)
    ids = jnp.broadcast_to(seg_ref[...].astype(jnp.float32), seg_out_ref.shape).astype(jnp.bfloat16)
    seg_out_ref[...] = ids
    across_ref[BLOCK:, :] = jnp.zeros((16, across_ref.shape[1]), jnp.bfloat16)
    across_ref[BLOCK:, : ids.shape[1]] = ids
    for made in copies:
        made.wait()


def columns_kernel(width, first_ref, second_ref, *outs):
    pair = lax.div(place()[2], 2)
    for k, out_ref in enumerate(outs):
        start = pl.multiple_of(lax.bitwise_xor(pair, k) * width, width)
        out_ref[:BLOCK, :] = first_ref[:, pl.ds(start, width)]
        out_ref[BLOCK:, :] = second_ref[:, pl.ds(start, width)]


def partial_kernel(count, shares, piece, *refs):
    columns, values = refs[:count], refs[count : 2 * count]
    own_ref, other_ref = refs[-2:]
    kv_width = values[0].shape[1]
    parts = []
    for k, ref in enumerate(values):
        if k == 1:
            parts += [
                ref[piece:, first : first + kv_width] for first in range(0, ref.shape[1], kv_width)
            ]
        else:
            parts.append(ref[...])
    value = jnp.concatenate(parts, axis=0)
    mine = lax.rem(place()[2], 2)
    for ref, core in ((other_ref, 1 - mine), (own_ref, mine)):
        at = pl.ds(pl.multiple_of(core * shares, shares), shares)
        rows = jnp.concatenate([part[:, at] for part in columns], axis=0)
        ref[...] = lax.dot_general(
            rows, value, (((0,), (0,)), ((), ())), preferred_element_type=jnp.float32
        )


def finish_kernel(
    half, scale, own_ref, other_ref, weight_ref, gain_ref, *refs
):
    pieces = refs[: 2 * half]
    rows_ref, out_ref, gain_out_ref, sems = refs[2 * half :]
    side, at, me = place()
    piece = pieces[0].shape[0]
    copies = []
    for block in range(2):
        for k in range(half):
            replica = (side if block == 0 else 1 - side) * half + lax.bitwise_xor(at, k)
            rows = pl.ds(pl.multiple_of(replica * piece, piece), piece)
            source = pieces[block * half + k].at[pl.ds(0, piece)]
            made = pltpu.make_async_copy(source, rows_ref.at[rows], sems.at[block * half + k])
            made.start()
            copies.append(made)
    shares = own_ref.shape[0]
    first = pl.multiple_of(me * shares, shares)
    gain = gain_ref[:, pl.ds(first, shares)]
    eye = lax.broadcasted_iota(jnp.int32, (shares, shares), 0) == lax.broadcasted_iota(
        jnp.int32, (shares, shares), 1
    )
    gain_column = jnp.sum(jnp.where(eye, gain, 0.0), axis=1, keepdims=True)
    total = (own_ref[...] + other_ref[...]) * scale
    out_ref[...] = total * gain_column
    product = total * weight_ref[pl.ds(first, shares), :].astype(jnp.float32)
    sums = lax.dot_general(
        jnp.ones((8, product.shape[1]), jnp.float32), product, (((1,), (1,)), ((), ())),
        preferred_element_type=jnp.float32, precision=lax.Precision.HIGHEST,
    )
    gain_out_ref[...] = sums[:1]
    for made in copies:
        made.wait()


def direct(hidden, query, key, segments, weight, norm_gain, upstream):
    tokens, model_width = hidden.shape
    kv_width = key.shape[1]
    replicas = lax.axis_size("dp")
    layers = lax.axis_size("section")
    half = replicas // 2
    piece = tokens // replicas
    shares = model_width // replicas

    def swap(array, k):
        return lax.ppermute(array, "dp", [(i, i ^ k) for i in range(replicas)])

    def far(array):
        return pltpu.with_memory_space_constraint(array, pltpu.HBM)

    count = 2 * half
    bf16 = jnp.bfloat16
    packed = pl.pallas_call(
        functools.partial(pack_kernel, half, piece),
        out_shape=(jax.ShapeDtypeStruct((piece, 2 * model_width + kv_width), bf16),) * count
        + (
            jax.ShapeDtypeStruct((16, segments.shape[1]), bf16),
            jax.ShapeDtypeStruct((BLOCK, model_width), bf16),
            jax.ShapeDtypeStruct((BLOCK + 16, model_width), bf16),
        ),
        in_specs=[pl.BlockSpec(memory_space=pltpu.HBM)] * 4 + [VMEM],
        out_specs=(VMEM,) * (count + 3),
        scratch_shapes=[pltpu.SemaphoreType.DMA((3 * count + 2,))],
        name="pack",
        **params(0, 3 << 20),
    )(far(query), far(key), far(hidden), far(upstream), segments)
    pieces = [
        [packed[b * half]] + [swap(packed[b * half + k], k) for k in range(1, half)]
        for b in range(2)
    ]
    across = swap(packed[-1], half)
    grads, segs = [packed[-2], across], [(packed[-3], 0), (across, BLOCK)]
    blocks, kept, after = [], [], ()
    for b in range(2):
        block = block_probs(pieces[b], *segs[b], model_width, kv_width, *after)
        late, early = (grads[b], LATE), (grads[b], EARLY)
        first = tick_step(0, [late], block, weight, norm_gain)
        second = tick_step(0, [late, early], block, weight, norm_gain, after=[first[0]])
        blocks.append(block)
        kept += [[first], [second]]
        after = [second[0]]

    columns = pl.pallas_call(
        functools.partial(columns_kernel, 2 * shares),
        out_shape=(jax.ShapeDtypeStruct((2 * BLOCK, 2 * shares), bf16),) * half,
        in_specs=[VMEM, VMEM],
        out_specs=(VMEM,) * half,
        name="columns",
        **params(0, 1 << 20),
    )(blocks[0][3], blocks[1][3])
    columns = [columns[0]] + [swap(columns[k], 2 * k) for k in range(1, half)]

    whole = slice(0, UNIT)
    for tick in range(1, layers):
        hop = [(layers - tick, layers - 1 - tick)]
        grads = [(lax.ppermute(unit[-1][0], "section", hop), whole) for unit in kept]
        last = tick == layers - 1
        after, done = [], []
        for u in range(4):
            needs = grads[u - 1 : u + 1] if u % 2 else grads[u : u + 1]
            late = []
            if last and u % 2:
                late = list(done[u - 1]) + ([done[1][0]] if u == 3 else [])
            done.append(
                tick_step(
                    tick, needs, blocks[u // 2], weight, norm_gain, kept[u] if last else (), late,
                    after,
                )
            )
            after = [done[u][0]]
            kept[u].append(done[u])
    first_rows = done[1][1:]
    values, *last_rows = done[3]
    first_rows = [first_rows[0]] + [swap(first_rows[k], k) for k in range(1, half)]
    last_rows = [last_rows[0]] + [swap(last_rows[k], k) for k in range(1, half)]
    gathered = [values, last_rows[2]] + [swap(values, 2 * k) for k in range(2, half)]
    rows = first_rows + last_rows
    own, other = pl.pallas_call(
        functools.partial(partial_kernel, half, shares, piece),
        out_shape=(jax.ShapeDtypeStruct((shares, kv_width), jnp.float32),) * 2,
        in_specs=[VMEM] * (2 * half),
        out_specs=(VMEM, VMEM),
        name="weight_partial",
        **params(4 * tokens * half * shares * kv_width),
    )(*columns, *gathered)
    other = swap(other, 1)
    scale = float(tokens * replicas) ** (-0.5)
    input_grad, weight_grad, gain_grad = pl.pallas_call(
        functools.partial(finish_kernel, half, scale),
        out_shape=(
            jax.ShapeDtypeStruct((tokens, model_width), bf16),
            jax.ShapeDtypeStruct((shares, kv_width), jnp.float32),
            jax.ShapeDtypeStruct((1, shares), jnp.float32),
        ),
        in_specs=[VMEM] * (4 + count),
        out_specs=(ANY, VMEM, VMEM),
        scratch_shapes=[pltpu.SemaphoreType.DMA((count,))],
        name="finish",
        **params(),
    )(own, other, weight, norm_gain, *rows)
    return input_grad[None], weight_grad[None], gain_grad


def weight_kernel(scale, columns_ref, value_ref, weight_ref, gain_ref, out_ref, gain_out_ref):
    total = lax.dot_general(
        columns_ref[...], value_ref[...], (((0,), (0,)), ((), ())),
        preferred_element_type=jnp.float32,
    ) * scale
    out_ref[...] = total * gain_ref[...]
    product = total * weight_ref[...].astype(jnp.float32)
    sums = lax.dot_general(
        jnp.ones((8, product.shape[1]), jnp.float32), product, (((1,), (1,)), ((), ())),
        preferred_element_type=jnp.float32, precision=lax.Precision.HIGHEST,
    )
    gain_out_ref[...] = sums[:1]


def grouped(hidden, query, key, segments, weight, norm_gain, upstream):
    tokens, model_width = hidden.shape
    kv_width = key.shape[1]
    replicas = lax.axis_size("dp")
    layers = lax.axis_size("section")
    half = replicas // 2
    me = lax.axis_index("dp")
    section = lax.axis_index("section")
    side = me // half
    groups = [list(range(half)), list(range(half, replicas))]
    across = [(i, (i + half) % replicas) for i in range(replicas)]
    shares = model_width // replicas

    def rows_of(array, which, axis=0):
        at = side if which == 0 else 1 - side
        return lax.dynamic_slice_in_dim(array, at * BLOCK, BLOCK, axis)

    def regroup(array):
        return lax.all_to_all(
            array, "dp", split_axis=0, concat_axis=0, axis_index_groups=groups, tiled=True
        )

    def spread(array):
        return lax.all_to_all(array, "dp", split_axis=0, concat_axis=0, tiled=True)

    blocks, grads = [], []
    for which in range(2):
        up = rows_of(upstream, which)
        seg = jnp.broadcast_to(segments, (16, 2 * BLOCK)).astype(jnp.bfloat16)
        if which == 1:
            up = lax.ppermute(up, "dp", across)
            seg = lax.ppermute(seg, "dp", across)
        packed = jnp.concatenate(
            [rows_of(query, which), rows_of(key, which), rows_of(hidden, which)], axis=1
        )
        blocks.append(block_probs([regroup(packed)], seg, 0, model_width, kv_width))
        grads.append(up)

    def layer(tick, which, grad, kept):
        live = (section == layers - 1 - tick).astype(jnp.int32)[None]
        return layer_step(live, grad, blocks[which], weight, norm_gain, kept)

    held = [layer(0, which, grads[which], ()) for which in range(2)]
    hops = [(i, i - 1) for i in range(1, layers)]

    def step(tick, held):
        grads = [lax.ppermute(kept[0], "section", hops) for kept in held]
        return [layer(tick, which, grads[which], held[which]) for which in range(2)]

    held = lax.fori_loop(1, layers, step, held)

    columns, values, stored = [], [], []
    for which in range(2):
        block = blocks[which][3].reshape(BLOCK, replicas, shares).transpose(1, 0, 2)
        columns.append(spread(block.reshape(replicas * BLOCK, shares)))
        out, value = held[which]
        stored.append(regroup(out))
        values.append(spread(jnp.tile(value, (replicas, 1))))
    ordered = jnp.where(
        side == 0, jnp.concatenate(stored, axis=0), jnp.concatenate(stored[::-1], axis=0)
    )
    own_weight = lax.dynamic_slice_in_dim(weight, me * shares, shares, 0)
    own_gain = lax.dynamic_slice_in_dim(norm_gain[0], me * shares, shares, 0)
    scale = float(tokens * replicas) ** (-0.5)
    weight_grad, gain_grad = pl.pallas_call(
        functools.partial(weight_kernel, scale),
        out_shape=(
            jax.ShapeDtypeStruct((shares, kv_width), jnp.float32),
            jax.ShapeDtypeStruct((1, shares), jnp.float32),
        ),
        in_specs=[VMEM] * 4,
        out_specs=(VMEM, VMEM),
        name="weight_grad",
    )(
        jnp.concatenate(columns, axis=0),
        jnp.concatenate(values, axis=0),
        own_weight,
        own_gain[:, None],
    )
    return ordered[None], weight_grad[None], gain_grad


def on_device(hidden_in, queries, keys, segments, value_weight, norm_gain, upstream):
    replicas = lax.axis_size("dp")
    piece = hidden_in.shape[1] // replicas
    plan = direct if piece % 16 == 0 and replicas == 8 else grouped
    return plan(
        hidden_in[0], queries[0], keys[0], segments, value_weight[0], norm_gain, upstream
    )


def solution(mesh):
    in_specs = (
        P("section", "dp", None),
        P("section", "dp", None),
        P("section", "dp", None),
        P("dp", None),
        P("section", None, None),
        P("section", None),
        P("dp", None),
    )
    out_specs = (P("section", "dp", None), P("section", "dp", None), P("section", "dp"))
    return jax.shard_map(
        on_device, mesh=mesh, in_specs=in_specs, out_specs=out_specs, check_vma=False
    )
```

time: 73.1 us -> 74.3 us (1.016)
  waiting for transfers between devices: 36.1 us -> 34 us
  Pallas kernels: 7.31 us -> 9.32 us
  starting transfers between devices: 27.5 us -> 28.8 us
    ppermute x6 -> x12, waiting for transfers between devices: 20.2 us -> 12.3 us  [direct(): lax.ppermute(unit[-1][0], 'section', hop)]
    ppermute x21 -> x19, waiting for transfers between devices: 16 us -> 21.7 us  [swap(): return lax.ppermute(array, 'dp', [(i, i ^ k) for i in range(replicas)])]
    ppermute x6 -> x12, starting transfers between devices: 5.28 us -> 10.5 us  [direct(): lax.ppermute(unit[-1][0], 'section', hop)]
    ppermute x21 -> x19, starting transfers between devices: 22.2 us -> 18.3 us  [swap(): return lax.ppermute(array, 'dp', [(i, i ^ k) for i in range(replicas)])]
    pallas_call x11 -> x19, Pallas kernels: 3.39 us -> 5.5 us  [the longest x16 4.37 us: tick_step(): pl.pallas_call(functools.partial(tick_kernel, tick, EARLY if low else LAT...]
  transfers between devices with their start and end apart: 27 -> 31, of which waited for: 13 -> 13; matrix products, arithmetic and copies ran while one was open for 0% -> 0% of each run, Pallas kernels for 4% -> 7%
where the time goes in v4:
time: 74.3 us; the launch traced here: 74 us
  waiting for transfers between devices  34 us (46%)
  starting transfers between devices  28.8 us (39%)
  Pallas kernels  9.32 us (13%)
  between operations  1.03 us (1%)
  local copies, waits for them, and re-layouts  0.81 us (1%)
    ppermute x19, waiting for transfers between devices, swap(): return lax.ppermute(array, 'dp', [(i, i ^ k) for i in range(replicas)])  21.7 us
    ppermute x19, starting transfers between devices, swap(): return lax.ppermute(array, 'dp', [(i, i ^ k) for i in range(replicas)])  18.3 us
    ppermute x12, waiting for transfers between devices, direct(): lax.ppermute(unit[-1][0], 'section', hop)  12.3 us
    ppermute x12, starting transfers between devices, direct(): lax.ppermute(unit[-1][0], 'section', hop)  10.5 us
    pallas_call x16, Pallas kernels, tick_step(): pl.pallas_call(functools.partial(tick_kernel, tick, EARLY if low else LAT...  4.37 us
    pallas_call x1, Pallas kernels, direct(): pl.pallas_call(functools.partial(finish_kernel, half, scale), out_shape=(...  2.01 us
    pallas_call x1, Pallas kernels, direct(): pl.pallas_call(functools.partial(pack_kernel, half, piece), out_shape=(ja...  1.75 us
  transfers between devices with their start and end apart: 31, of which 13 were waited for; matrix products, arithmetic and copies ran while one was open for 0% of the time, Pallas kernels for 7%

profile of v4, /device:TPU:0, one launch (start us, length us, event | category | flops | bytes accessed | tf_op | source)
XLA Modules:
  0.0 74.0 jit_solution(1301576026503961474)
XLA Ops:
  0.7 0.8 %copy-done.2 = s32[1,128]{1,0:T(1,128)S(1)} copy-done((s32[1,128]{1,0:T(1,128)S(1)}, s32[1,128]{1,0:T(1,128)}, u32[]{:S(2)}) %copy-start.2) | copy-done | bytes 536
  1.5 1.8 %pack.1 = (bf16[16,4608]{1,0:T(8,128)(2,1)S(1)}, bf16[16,4608]{1,0:T(8,128)(2,1)S(1)}, bf16[16,4608]{1,0:T(8,128)(2,1)S(1)}, bf16[16,4608]{1,0:T(8,128)(2,1)S(1)...) custom-call(bf16[128,2048]{1,0:T(8,128)(2,1)} %bitcast.23, ...), custom_call_target="tpu_custom_call" | custom-call | bytes 3145728 | tf_op jit(solution)/shard_map/pack/pallas_call | solution.py:420
  3.2 3.0 %collective-permute-start.6 = (bf16[80,2048]{1,0:T(8,128)(2,1)S(1)}, bf16[80,2048]{1,0:T(8,128)(2,1)S(1)}, u32[]{:S(2)}, u32[]{:S(2)}) collective-permute-start(bf16[80,2048]{1,0:T(8,128)(2,1)S(1)} %get-tuple-element.79), channel_id=1, source_target_pairs={{0,16},{4,20},{8,24},{12,28},{16,0},{20,4},{24,8},{28,12},{1,17},{... | collective-permute-start | bytes 983048 | tf_op jit(solution)/shard_map/ppermute | solution.py:413
  6.3 1.5 %collective-permute-start.1 = (bf16[16,4608]{1,0:T(8,128)(2,1)S(1)}, bf16[16,4608]{1,0:T(8,128)(2,1)S(1)}, u32[]{:S(2)}, u32[]{:S(2)}) collective-permute-start(bf16[16,4608]{1,0:T(8,128)(2,1)S(1)} %get-tuple-element.71), channel_id=1, source_target_pairs={{0,8},{4,12},{8,0},{12,4},{16,24},{20,28},{24,16},{28,20},{1,9},{5... | collective-permute-start | bytes 442376 | tf_op jit(solution)/shard_map/ppermute | solution.py:413
  8.4 1.5 %collective-permute-start.4 = (bf16[16,4608]{1,0:T(8,128)(2,1)S(1)}, bf16[16,4608]{1,0:T(8,128)(2,1)S(1)}, u32[]{:S(2)}, u32[]{:S(2)}) collective-permute-start(bf16[16,4608]{1,0:T(8,128)(2,1)S(1)} %get-tuple-element.77), channel_id=1, source_target_pairs={{0,8},{4,12},{8,0},{12,4},{16,24},{20,28},{24,16},{28,20},{1,9},{5... | collective-permute-start | bytes 442376 | tf_op jit(solution)/shard_map/ppermute | solution.py:413
  9.9 3.0 %collective-permute-done.1.refs_2_ = bf16[16,4608]{1,0:T(8,128)(2,1)S(1)} collective-permute-done((bf16[16,4608]{1,0:T(8,128)(2,1)S(1)}, bf16[16,4608]{1,0:T(8,128)(2,1)S(1)}, u32[]{:S(2)}, u32[]{:S(2)}) %collective-permute-start.1) | collective-permute-done | bytes 147488 | tf_op jit(solution)/shard_map/ppermute | solution.py:413
  13.3 1.9 %collective-permute-done.2.refs_3_ = bf16[16,4608]{1,0:T(8,128)(2,1)S(1)} collective-permute-done((bf16[16,4608]{1,0:T(8,128)(2,1)S(1)}, bf16[16,4608]{1,0:T(8,128)(2,1)S(1)}, u32[]{:S(2)}, u32[]{:S(2)}) %collective-permute-start.2) | collective-permute-done | bytes 147488 | tf_op jit(solution)/shard_map/ppermute | solution.py:413
  17.0 2.2 %collective-permute-done.4.refs_2_ = bf16[16,4608]{1,0:T(8,128)(2,1)S(1)} collective-permute-done((bf16[16,4608]{1,0:T(8,128)(2,1)S(1)}, bf16[16,4608]{1,0:T(8,128)(2,1)S(1)}, u32[]{:S(2)}, u32[]{:S(2)}) %collective-permute-start.4) | collective-permute-done | bytes 147488 | tf_op jit(solution)/shard_map/ppermute | solution.py:413
  19.2 2.4 %collective-permute-done.5.refs_3_ = bf16[16,4608]{1,0:T(8,128)(2,1)S(1)} collective-permute-done((bf16[16,4608]{1,0:T(8,128)(2,1)S(1)}, bf16[16,4608]{1,0:T(8,128)(2,1)S(1)}, u32[]{:S(2)}, u32[]{:S(2)}) %collective-permute-start.5) | collective-permute-done | bytes 147488 | tf_op jit(solution)/shard_map/ppermute | solution.py:413
  26.2 1.3 %collective-permute-start.20 = (bf16[32,2048]{1,0:T(8,128)(2,1)S(1)}, bf16[32,2048]{1,0:T(8,128)(2,1)S(1)}, u32[]{:S(2)}, u32[]{:S(2)}) collective-permute-start(bf16[32,2048]{1,0:T(8,128)(2,1)S(1)} %get-tuple-element.97.refs_7_.refs_10_), channel_id=1, source_target_pairs={{1,0},{5,4},{9,8},{13,12},{17,16},{21,20},{25,24},{29,28}} | collective-permute-start | bytes 393224 | tf_op jit(solution)/shard_map/ppermute | solution.py:463
  27.5 1.3 %collective-permute-start.21 = (bf16[32,2048]{1,0:T(8,128)(2,1)S(1)}, bf16[32,2048]{1,0:T(8,128)(2,1)S(1)}, u32[]{:S(2)}, u32[]{:S(2)}) collective-permute-start(bf16[32,2048]{1,0:T(8,128)(2,1)S(1)} %get-tuple-element.98.refs_6_.refs_11_), channel_id=1, source_target_pairs={{1,0},{5,4},{9,8},{13,12},{17,16},{21,20},{25,24},{29,28}} | collective-permute-start | bytes 393224 | tf_op jit(solution)/shard_map/ppermute | solution.py:463
  28.9 1.3 %collective-permute-start.16 = (bf16[32,2048]{1,0:T(8,128)(2,1)S(1)}, bf16[32,2048]{1,0:T(8,128)(2,1)S(1)}, u32[]{:S(2)}, u32[]{:S(2)}) collective-permute-start(bf16[32,2048]{1,0:T(8,128)(2,1)S(1)} %get-tuple-element.99.refs_7_.refs_10_), channel_id=1, source_target_pairs={{1,0},{5,4},{9,8},{13,12},{17,16},{21,20},{25,24},{29,28}} | collective-permute-start | bytes 393224 | tf_op jit(solution)/shard_map/ppermute | solution.py:463
  30.2 1.3 %collective-permute-start.19 = (bf16[32,2048]{1,0:T(8,128)(2,1)S(1)}, bf16[32,2048]{1,0:T(8,128)(2,1)S(1)}, u32[]{:S(2)}, u32[]{:S(2)}) collective-permute-start(bf16[32,2048]{1,0:T(8,128)(2,1)S(1)} %get-tuple-element.103.refs_11_), channel_id=1, source_target_pairs={{1,0},{5,4},{9,8},{13,12},{17,16},{21,20},{25,24},{29,28}} | collective-permute-start | bytes 393224 | tf_op jit(solution)/shard_map/ppermute | solution.py:463
  31.6 1.6 %collective-permute-start.7 = (bf16[128,512]{1,0:T(8,128)(2,1)S(1)}, bf16[128,512]{1,0:T(8,128)(2,1)S(1)}, u32[]{:S(2)}, u32[]{:S(2)}) collective-permute-start(bf16[128,512]{1,0:T(8,128)(2,1)S(1)} %get-tuple-element.88), channel_id=1, source_target_pairs={{0,8},{4,12},{8,0},{12,4},{16,24},{20,28},{24,16},{28,20},{1,9},{5... | collective-permute-start | bytes 393224 | tf_op jit(solution)/shard_map/ppermute | solution.py:413
  33.1 7.0 %collective-permute-done.20.refs_0_ = bf16[32,2048]{1,0:T(8,128)(2,1)S(1)} collective-permute-done((bf16[32,2048]{1,0:T(8,128)(2,1)S(1)}, bf16[32,2048]{1,0:T(8,128)(2,1)S(1)}, u32[]{:S(2)}, u32[]{:S(2)}) %collective-permute-start.20) | collective-permute-done | bytes 131104 | tf_op jit(solution)/shard_map/ppermute | solution.py:463
  40.1 1.0 %tick.28 = (bf16[32,2048]{1,0:T(8,128)(2,1)S(1)}, bf16[32,512]{1,0:T(8,128)(2,1)S(1)}) custom-call(bf16[32,2048]{1,0:T(8,128)(2,1)S(1)} %collective-permute-done.20.refs_0_, bf16[4,32,128]{2,1,0:T(8,128)(2,1)S(1)} %get-tuple-element.83.refs_1_, f32[64,128]{1,0:T(8,128)S(1)} %get-tuple-element.82.refs_2_.refs_3_, ...), custom_call_target="tpu_custom_call" | custom-call | flops 67108864 | bytes 1048576 | tf_op jit(solution)/shard_map/tick/pallas_call | solution.py:293
  41.1 1.8 %collective-permute-done.21.refs_1_ = bf16[32,2048]{1,0:T(8,128)(2,1)S(1)} collective-permute-done((bf16[32,2048]{1,0:T(8,128)(2,1)S(1)}, bf16[32,2048]{1,0:T(8,128)(2,1)S(1)}, u32[]{:S(2)}, u32[]{:S(2)}) %collective-permute-start.21) | collective-permute-done | bytes 131104 | tf_op jit(solution)/shard_map/ppermute | solution.py:463
  42.9 1.1 %tick.29 = (bf16[64,512]{1,0:T(8,128)(2,1)S(1)}, bf16[16,2048]{1,0:T(8,128)(2,1)S(1)}, bf16[16,2048]{1,0:T(8,128)(2,1)S(1)}, bf16[16,2048]{1,0:T(8,128)(2,1)S(1)}, bf16[16,2048]{1,0:T(8,128)(2,1)S(1)}) custom-call(bf16[32,2048]{1,0:T(8,128)(2,1)S(1)} %collective-permute-done.20.refs_0_, bf16[32,2048]{1,0:T(8,128)(2,1)S(1)} %collective-permute-done.21.refs_1_, ...), custom_call_target="tpu_custom_call" | custom-call | flops 67108864 | bytes 1048576 | tf_op jit(solution)/shard_map/tick/pallas_call | solution.py:293
  44.0 1.7 %collective-permute-done.16.refs_0_ = bf16[32,2048]{1,0:T(8,128)(2,1)S(1)} collective-permute-done((bf16[32,2048]{1,0:T(8,128)(2,1)S(1)}, bf16[32,2048]{1,0:T(8,128)(2,1)S(1)}, u32[]{:S(2)}, u32[]{:S(2)}) %collective-permute-start.16) | collective-permute-done | bytes 131104 | tf_op jit(solution)/shard_map/ppermute | solution.py:463
  45.7 1.0 %tick.30 = (bf16[32,2048]{1,0:T(8,128)(2,1)S(1)}, bf16[32,512]{1,0:T(8,128)(2,1)S(1)}) custom-call(bf16[32,2048]{1,0:T(8,128)(2,1)S(1)} %collective-permute-done.16.refs_0_, bf16[4,32,128]{2,1,0:T(8,128)(2,1)S(1)} %get-tuple-element.91.refs_1_, f32[64,128]{1,0:T(8,128)S(1)} %get-tuple-element.92.refs_2_.refs_3_, ...), custom_call_target="tpu_custom_call" | custom-call | flops 67108864 | bytes 1048576 | tf_op jit(solution)/shard_map/tick/pallas_call | solution.py:293
  46.8 1.8 %collective-permute-done.19.refs_1_ = bf16[32,2048]{1,0:T(8,128)(2,1)S(1)} collective-permute-done((bf16[32,2048]{1,0:T(8,128)(2,1)S(1)}, bf16[32,2048]{1,0:T(8,128)(2,1)S(1)}, u32[]{:S(2)}, u32[]{:S(2)}) %collective-permute-start.19) | collective-permute-done | bytes 131104 | tf_op jit(solution)/shard_map/ppermute | solution.py:463
  48.5 1.1 %tick.31 = (bf16[128,512]{1,0:T(8,128)(2,1)S(1)}, bf16[16,2048]{1,0:T(8,128)(2,1)S(1)}, bf16[16,2048]{1,0:T(8,128)(2,1)S(1)}, bf16[48,2048]{1,0:T(8,128)(2,1)S(1)}, bf16[16,2048]{1,0:T(8,128)(2,1)S(1)}) custom-call(bf16[32,2048]{1,0:T(8,128)(2,1)S(1)} %collective-permute-done.16.refs_0_, bf16[32,2048]{1,0:T(8,128)(2,1)S(1)} %collective-permute-done.19.refs_1_, ...), custom_call_target="tpu_custom_call" | custom-call | flops 67108864 | bytes 1048576 | tf_op jit(solution)/shard_map/tick/pallas_call | solution.py:293
  49.6 1.5 %collective-permute-start.22 = (bf16[48,2048]{1,0:T(8,128)(2,1)S(1)}, bf16[48,2048]{1,0:T(8,128)(2,1)S(1)}, u32[]{:S(2)}, u32[]{:S(2)}) collective-permute-start(bf16[48,2048]{1,0:T(8,128)(2,1)S(1)} %get-tuple-element.122), channel_id=1, source_target_pairs={{0,8},{4,12},{8,0},{12,4},{16,24},{20,28},{24,16},{28,20},{1,9},{5... | collective-permute-start | bytes 589832 | tf_op jit(solution)/shard_map/ppermute | solution.py:413
  51.7 1.5 %collective-permute-start.9 = (bf16[128,512]{1,0:T(8,128)(2,1)S(1)}, bf16[128,512]{1,0:T(8,128)(2,1)S(1)}, u32[]{:S(2)}, u32[]{:S(2)}) collective-permute-start(bf16[128,512]{1,0:T(8,128)(2,1)S(1)} %get-tuple-element.90), channel_id=1, source_target_pairs={{0,24},{4,28},{8,16},{12,20},{16,8},{20,12},{24,0},{28,4},{1,25},{... | collective-permute-start | bytes 393224 | tf_op jit(solution)/shard_map/ppermute | solution.py:413
  53.2 1.4 %collective-permute-start.24 = (bf16[128,512]{1,0:T(8,128)(2,1)S(1)}, bf16[128,512]{1,0:T(8,128)(2,1)S(1)}, u32[]{:S(2)}, u32[]{:S(2)}) collective-permute-start(bf16[128,512]{1,0:T(8,128)(2,1)S(1)} %get-tuple-element.121.refs_4_), channel_id=1, source_target_pairs={{0,24},{4,28},{8,16},{12,20},{16,8},{20,12},{24,0},{28,4},{1,25},{... | collective-permute-start | bytes 393224 | tf_op jit(solution)/shard_map/ppermute | solution.py:413
  54.6 1.5 %collective-permute-start.23 = (bf16[128,512]{1,0:T(8,128)(2,1)S(1)}, bf16[128,512]{1,0:T(8,128)(2,1)S(1)}, u32[]{:S(2)}, u32[]{:S(2)}) collective-permute-start(bf16[128,512]{1,0:T(8,128)(2,1)S(1)} %get-tuple-element.121.refs_4_), channel_id=1, source_target_pairs={{0,16},{4,20},{8,24},{12,28},{16,0},{20,4},{24,8},{28,12},{1,17},{... | collective-permute-start | bytes 393224 | tf_op jit(solution)/shard_map/ppermute | solution.py:413
  56.1 6.4 %collective-permute-done.8.refs_2_ = bf16[128,512]{1,0:T(8,128)(2,1)S(1)} collective-permute-done((bf16[128,512]{1,0:T(8,128)(2,1)S(1)}, bf16[128,512]{1,0:T(8,128)(2,1)S(1)}, u32[]{:S(2)}, u32[]{:S(2)}) %collective-permute-start.8) | collective-permute-done | bytes 131104 | tf_op jit(solution)/shard_map/ppermute | solution.py:413
  62.6 1.7 %collective-permute-done.23.refs_6_ = bf16[128,512]{1,0:T(8,128)(2,1)S(1)} collective-permute-done((bf16[128,512]{1,0:T(8,128)(2,1)S(1)}, bf16[128,512]{1,0:T(8,128)(2,1)S(1)}, u32[]{:S(2)}, u32[]{:S(2)}) %collective-permute-start.23) | collective-permute-done | bytes 131104 | tf_op jit(solution)/shard_map/ppermute | solution.py:413
  65.4 0.8 %collective-permute-start.27 = (bf16[16,2048]{1,0:T(8,128)(2,1)S(1)}, bf16[16,2048]{1,0:T(8,128)(2,1)S(1)}, u32[]{:S(2)}, u32[]{:S(2)}) collective-permute-start(bf16[16,2048]{1,0:T(8,128)(2,1)S(1)} %get-tuple-element.127), channel_id=1, source_target_pairs={{0,8},{4,12},{8,0},{12,4},{16,24},{20,28},{24,16},{28,20},{1,9},{5... | collective-permute-start | bytes 196616 | tf_op jit(solution)/shard_map/ppermute | solution.py:413
  67.9 2.2 %collective-permute-done.27.refs_2_ = bf16[16,2048]{1,0:T(8,128)(2,1)S(1)} collective-permute-done((bf16[16,2048]{1,0:T(8,128)(2,1)S(1)}, bf16[16,2048]{1,0:T(8,128)(2,1)S(1)}, u32[]{:S(2)}, u32[]{:S(2)}) %collective-permute-start.27) | collective-permute-done | bytes 65568 | tf_op jit(solution)/shard_map/ppermute | solution.py:413
  70.6 1.4 %collective-permute-done.30.refs_7_ = bf16[16,2048]{1,0:T(8,128)(2,1)S(1)} collective-permute-done((bf16[16,2048]{1,0:T(8,128)(2,1)S(1)}, bf16[16,2048]{1,0:T(8,128)(2,1)S(1)}, u32[]{:S(2)}, u32[]{:S(2)}) %collective-permute-start.30) | collective-permute-done | bytes 65568 | tf_op jit(solution)/shard_map/ppermute | solution.py:413
  72.0 2.0 %finish.1 = (bf16[128,2048]{1,0:T(8,128)(2,1)}, f32[256,512]{1,0:T(8,128)}, f32[1,256]{1,0:T(1,128)}) custom-call(f32[256,512]{1,0:T(8,128)S(1)} %get-tuple-element.123.own_ref, f32[256,512]{1,0:T(8,128)S(1)} %collective-permute-done.25.other_ref, bf16[2048,512]{1,0:T(8,128)(2,1)S(1)} %bitcast.22, f32[1,2048]{1,0:T(1,128)S(1)} %copy-done.1, ...), custom_call_target="tpu_custom_call" | custom-call | bytes 1048576 | tf_op jit(solution)/shard_map/finish/pallas_call | solution.py:495
  (58 shorter events, 11.2 us)
Async XLA Ops:
  0.6 15.0 %copy-start.1 = (f32[1,2048]{1,0:T(1,128)S(1)}, f32[1,2048]{1,0:T(1,128)}, u32[]{:S(2)}) copy-start(f32[1,2048]{1,0:T(1,128)} %gain_ref.1) | copy-start | bytes 24580
  3.2 18.4 %collective-permute-start.6 = (bf16[80,2048]{1,0:T(8,128)(2,1)S(1)}, bf16[80,2048]{1,0:T(8,128)(2,1)S(1)}, u32[]{:S(2)}, u32[]{:S(2)}) collective-permute-start(bf16[80,2048]{1,0:T(8,128)(2,1)S(1)} %get-tuple-element.79), channel_id=1, source_target_pairs={{0,16},{4,20},{8,24},{12,28},{16,0},{20,4},{24,8},{28,12},{1,17},{... | collective-permute-start | bytes 983048 | tf_op jit(solution)/shard_map/ppermute | solution.py:413
  6.2 2.1 %collective-permute-start = (bf16[16,4608]{1,0:T(8,128)(2,1)S(1)}, bf16[16,4608]{1,0:T(8,128)(2,1)S(1)}, u32[]{:S(2)}, u32[]{:S(2)}) collective-permute-start(bf16[16,4608]{1,0:T(8,128)(2,1)S(1)} %get-tuple-element.70), channel_id=1, source_target_pairs={{0,4},{4,0},{8,12},{12,8},{16,20},{20,16},{24,28},{28,24},{1,5},{5... | collective-permute-start | bytes 442376 | tf_op jit(solution)/shard_map/ppermute | solution.py:413
  6.3 6.6 %collective-permute-start.1 = (bf16[16,4608]{1,0:T(8,128)(2,1)S(1)}, bf16[16,4608]{1,0:T(8,128)(2,1)S(1)}, u32[]{:S(2)}, u32[]{:S(2)}) collective-permute-start(bf16[16,4608]{1,0:T(8,128)(2,1)S(1)} %get-tuple-element.71), channel_id=1, source_target_pairs={{0,8},{4,12},{8,0},{12,4},{16,24},{20,28},{24,16},{28,20},{1,9},{5... | collective-permute-start | bytes 442376 | tf_op jit(solution)/shard_map/ppermute | solution.py:413
  7.7 7.5 %collective-permute-start.2 = (bf16[16,4608]{1,0:T(8,128)(2,1)S(1)}, bf16[16,4608]{1,0:T(8,128)(2,1)S(1)}, u32[]{:S(2)}, u32[]{:S(2)}) collective-permute-start(bf16[16,4608]{1,0:T(8,128)(2,1)S(1)} %get-tuple-element.72), channel_id=1, source_target_pairs={{0,12},{4,8},{8,4},{12,0},{16,28},{20,24},{24,20},{28,16},{1,13},{... | collective-permute-start | bytes 442376 | tf_op jit(solution)/shard_map/ppermute | solution.py:413
  8.1 8.2 %collective-permute-start.3 = (bf16[16,4608]{1,0:T(8,128)(2,1)S(1)}, bf16[16,4608]{1,0:T(8,128)(2,1)S(1)}, u32[]{:S(2)}, u32[]{:S(2)}) collective-permute-start(bf16[16,4608]{1,0:T(8,128)(2,1)S(1)} %get-tuple-element.76), channel_id=1, source_target_pairs={{0,4},{4,0},{8,12},{12,8},{16,20},{20,16},{24,28},{28,24},{1,5},{5... | collective-permute-start | bytes 442376 | tf_op jit(solution)/shard_map/ppermute | solution.py:413
  8.4 10.8 %collective-permute-start.4 = (bf16[16,4608]{1,0:T(8,128)(2,1)S(1)}, bf16[16,4608]{1,0:T(8,128)(2,1)S(1)}, u32[]{:S(2)}, u32[]{:S(2)}) collective-permute-start(bf16[16,4608]{1,0:T(8,128)(2,1)S(1)} %get-tuple-element.77), channel_id=1, source_target_pairs={{0,8},{4,12},{8,0},{12,4},{16,24},{20,28},{24,16},{28,20},{1,9},{5... | collective-permute-start | bytes 442376 | tf_op jit(solution)/shard_map/ppermute | solution.py:413
  12.9 8.7 %collective-permute-start.5 = (bf16[16,4608]{1,0:T(8,128)(2,1)S(1)}, bf16[16,4608]{1,0:T(8,128)(2,1)S(1)}, u32[]{:S(2)}, u32[]{:S(2)}) collective-permute-start(bf16[16,4608]{1,0:T(8,128)(2,1)S(1)} %get-tuple-element.78), channel_id=1, source_target_pairs={{0,12},{4,8},{8,4},{12,0},{16,28},{20,24},{24,20},{28,16},{1,13},{... | collective-permute-start | bytes 442376 | tf_op jit(solution)/shard_map/ppermute | solution.py:413
  15.7 7.7 %collective-permute-start.11 = (bf16[32,2048]{1,0:T(8,128)(2,1)S(1)}, bf16[32,2048]{1,0:T(8,128)(2,1)S(1)}, u32[]{:S(2)}, u32[]{:S(2)}) collective-permute-start(bf16[32,2048]{1,0:T(8,128)(2,1)S(1)} %get-tuple-element.84.refs_7_.refs_6_), channel_id=1, source_target_pairs={{3,2},{7,6},{11,10},{15,14},{19,18},{23,22},{27,26},{31,30}} | collective-permute-start | bytes 393224 | tf_op jit(solution)/shard_map/ppermute | solution.py:463
  16.4 7.7 %collective-permute-start.12 = (bf16[32,2048]{1,0:T(8,128)(2,1)S(1)}, bf16[32,2048]{1,0:T(8,128)(2,1)S(1)}, u32[]{:S(2)}, u32[]{:S(2)}) collective-permute-start(bf16[32,2048]{1,0:T(8,128)(2,1)S(1)} %get-tuple-element.85.refs_5_.refs_7_), channel_id=1, source_target_pairs={{3,2},{7,6},{11,10},{15,14},{19,18},{23,22},{27,26},{31,30}} | collective-permute-start | bytes 393224 | tf_op jit(solution)/shard_map/ppermute | solution.py:463
  22.0 2.8 %collective-permute-start.10 = (bf16[32,2048]{1,0:T(8,128)(2,1)S(1)}, bf16[32,2048]{1,0:T(8,128)(2,1)S(1)}, u32[]{:S(2)}, u32[]{:S(2)}) collective-permute-start(bf16[32,2048]{1,0:T(8,128)(2,1)S(1)} %get-tuple-element.93.refs_7_.refs_6_), channel_id=1, source_target_pairs={{3,2},{7,6},{11,10},{15,14},{19,18},{23,22},{27,26},{31,30}} | collective-permute-start | bytes 393224 | tf_op jit(solution)/shard_map/ppermute | solution.py:463
  22.7 2.8 %collective-permute-start.17 = (bf16[32,2048]{1,0:T(8,128)(2,1)S(1)}, bf16[32,2048]{1,0:T(8,128)(2,1)S(1)}, u32[]{:S(2)}, u32[]{:S(2)}) collective-permute-start(bf16[32,2048]{1,0:T(8,128)(2,1)S(1)} %get-tuple-element.101.refs_7_), channel_id=1, source_target_pairs={{3,2},{7,6},{11,10},{15,14},{19,18},{23,22},{27,26},{31,30}} | collective-permute-start | bytes 393224 | tf_op jit(solution)/shard_map/ppermute | solution.py:463
  23.4 2.8 %collective-permute-start.14 = (bf16[32,2048]{1,0:T(8,128)(2,1)S(1)}, bf16[32,2048]{1,0:T(8,128)(2,1)S(1)}, u32[]{:S(2)}, u32[]{:S(2)}) collective-permute-start(bf16[32,2048]{1,0:T(8,128)(2,1)S(1)} %get-tuple-element.94.refs_7_.refs_8_), channel_id=1, source_target_pairs={{2,1},{6,5},{10,9},{14,13},{18,17},{22,21},{26,25},{30,29}} | collective-permute-start | bytes 393224 | tf_op jit(solution)/shard_map/ppermute | solution.py:463
  24.1 3.4 %collective-permute-start.15 = (bf16[32,2048]{1,0:T(8,128)(2,1)S(1)}, bf16[32,2048]{1,0:T(8,128)(2,1)S(1)}, u32[]{:S(2)}, u32[]{:S(2)}) collective-permute-start(bf16[32,2048]{1,0:T(8,128)(2,1)S(1)} %get-tuple-element.95.refs_6_.refs_9_), channel_id=1, source_target_pairs={{2,1},{6,5},{10,9},{14,13},{18,17},{22,21},{26,25},{30,29}} | collective-permute-start | bytes 393224 | tf_op jit(solution)/shard_map/ppermute | solution.py:463
  24.8 4.1 %collective-permute-start.13 = (bf16[32,2048]{1,0:T(8,128)(2,1)S(1)}, bf16[32,2048]{1,0:T(8,128)(2,1)S(1)}, u32[]{:S(2)}, u32[]{:S(2)}) collective-permute-start(bf16[32,2048]{1,0:T(8,128)(2,1)S(1)} %get-tuple-element.96.refs_7_.refs_8_), channel_id=1, source_target_pairs={{2,1},{6,5},{10,9},{14,13},{18,17},{22,21},{26,25},{30,29}} | collective-permute-start | bytes 393224 | tf_op jit(solution)/shard_map/ppermute | solution.py:463
  25.5 4.7 %collective-permute-start.18 = (bf16[32,2048]{1,0:T(8,128)(2,1)S(1)}, bf16[32,2048]{1,0:T(8,128)(2,1)S(1)}, u32[]{:S(2)}, u32[]{:S(2)}) collective-permute-start(bf16[32,2048]{1,0:T(8,128)(2,1)S(1)} %get-tuple-element.102.refs_9_), channel_id=1, source_target_pairs={{2,1},{6,5},{10,9},{14,13},{18,17},{22,21},{26,25},{30,29}} | collective-permute-start | bytes 393224 | tf_op jit(solution)/shard_map/ppermute | solution.py:463
  26.2 13.9 %collective-permute-start.20 = (bf16[32,2048]{1,0:T(8,128)(2,1)S(1)}, bf16[32,2048]{1,0:T(8,128)(2,1)S(1)}, u32[]{:S(2)}, u32[]{:S(2)}) collective-permute-start(bf16[32,2048]{1,0:T(8,128)(2,1)S(1)} %get-tuple-element.97.refs_7_.refs_10_), channel_id=1, source_target_pairs={{1,0},{5,4},{9,8},{13,12},{17,16},{21,20},{25,24},{29,28}} | collective-permute-start | bytes 393224 | tf_op jit(solution)/shard_map/ppermute | solution.py:463
  27.5 15.4 %collective-permute-start.21 = (bf16[32,2048]{1,0:T(8,128)(2,1)S(1)}, bf16[32,2048]{1,0:T(8,128)(2,1)S(1)}, u32[]{:S(2)}, u32[]{:S(2)}) collective-permute-start(bf16[32,2048]{1,0:T(8,128)(2,1)S(1)} %get-tuple-element.98.refs_6_.refs_11_), channel_id=1, source_target_pairs={{1,0},{5,4},{9,8},{13,12},{17,16},{21,20},{25,24},{29,28}} | collective-permute-start | bytes 393224 | tf_op jit(solution)/shard_map/ppermute | solution.py:463
  28.9 16.8 %collective-permute-start.16 = (bf16[32,2048]{1,0:T(8,128)(2,1)S(1)}, bf16[32,2048]{1,0:T(8,128)(2,1)S(1)}, u32[]{:S(2)}, u32[]{:S(2)}) collective-permute-start(bf16[32,2048]{1,0:T(8,128)(2,1)S(1)} %get-tuple-element.99.refs_7_.refs_10_), channel_id=1, source_target_pairs={{1,0},{5,4},{9,8},{13,12},{17,16},{21,20},{25,24},{29,28}} | collective-permute-start | bytes 393224 | tf_op jit(solution)/shard_map/ppermute | solution.py:463
  30.2 18.3 %collective-permute-start.19 = (bf16[32,2048]{1,0:T(8,128)(2,1)S(1)}, bf16[32,2048]{1,0:T(8,128)(2,1)S(1)}, u32[]{:S(2)}, u32[]{:S(2)}) collective-permute-start(bf16[32,2048]{1,0:T(8,128)(2,1)S(1)} %get-tuple-element.103.refs_11_), channel_id=1, source_target_pairs={{1,0},{5,4},{9,8},{13,12},{17,16},{21,20},{25,24},{29,28}} | collective-permute-start | bytes 393224 | tf_op jit(solution)/shard_map/ppermute | solution.py:463
  31.6 23.0 %collective-permute-start.7 = (bf16[128,512]{1,0:T(8,128)(2,1)S(1)}, bf16[128,512]{1,0:T(8,128)(2,1)S(1)}, u32[]{:S(2)}, u32[]{:S(2)}) collective-permute-start(bf16[128,512]{1,0:T(8,128)(2,1)S(1)} %get-tuple-element.88), channel_id=1, source_target_pairs={{0,8},{4,12},{8,0},{12,4},{16,24},{20,28},{24,16},{28,20},{1,9},{5... | collective-permute-start | bytes 393224 | tf_op jit(solution)/shard_map/ppermute | solution.py:413
  49.6 14.7 %collective-permute-start.22 = (bf16[48,2048]{1,0:T(8,128)(2,1)S(1)}, bf16[48,2048]{1,0:T(8,128)(2,1)S(1)}, u32[]{:S(2)}, u32[]{:S(2)}) collective-permute-start(bf16[48,2048]{1,0:T(8,128)(2,1)S(1)} %get-tuple-element.122), channel_id=1, source_target_pairs={{0,8},{4,12},{8,0},{12,4},{16,24},{20,28},{24,16},{28,20},{1,9},{5... | collective-permute-start | bytes 589832 | tf_op jit(solution)/shard_map/ppermute | solution.py:413
  51.2 11.4 %collective-permute-start.8 = (bf16[128,512]{1,0:T(8,128)(2,1)S(1)}, bf16[128,512]{1,0:T(8,128)(2,1)S(1)}, u32[]{:S(2)}, u32[]{:S(2)}) collective-permute-start(bf16[128,512]{1,0:T(8,128)(2,1)S(1)} %get-tuple-element.89), channel_id=1, source_target_pairs={{0,16},{4,20},{8,24},{12,28},{16,0},{20,4},{24,8},{28,12},{1,17},{... | collective-permute-start | bytes 393224 | tf_op jit(solution)/shard_map/ppermute | solution.py:413
  51.7 10.9 %collective-permute-start.9 = (bf16[128,512]{1,0:T(8,128)(2,1)S(1)}, bf16[128,512]{1,0:T(8,128)(2,1)S(1)}, u32[]{:S(2)}, u32[]{:S(2)}) collective-permute-start(bf16[128,512]{1,0:T(8,128)(2,1)S(1)} %get-tuple-element.90), channel_id=1, source_target_pairs={{0,24},{4,28},{8,16},{12,20},{16,8},{20,12},{24,0},{28,4},{1,25},{... | collective-permute-start | bytes 393224 | tf_op jit(solution)/shard_map/ppermute | solution.py:413
  53.2 9.4 %collective-permute-start.24 = (bf16[128,512]{1,0:T(8,128)(2,1)S(1)}, bf16[128,512]{1,0:T(8,128)(2,1)S(1)}, u32[]{:S(2)}, u32[]{:S(2)}) collective-permute-start(bf16[128,512]{1,0:T(8,128)(2,1)S(1)} %get-tuple-element.121.refs_4_), channel_id=1, source_target_pairs={{0,24},{4,28},{8,16},{12,20},{16,8},{20,12},{24,0},{28,4},{1,25},{... | collective-permute-start | bytes 393224 | tf_op jit(solution)/shard_map/ppermute | solution.py:413
  54.6 9.7 %collective-permute-start.23 = (bf16[128,512]{1,0:T(8,128)(2,1)S(1)}, bf16[128,512]{1,0:T(8,128)(2,1)S(1)}, u32[]{:S(2)}, u32[]{:S(2)}) collective-permute-start(bf16[128,512]{1,0:T(8,128)(2,1)S(1)} %get-tuple-element.121.refs_4_), channel_id=1, source_target_pairs={{0,16},{4,20},{8,24},{12,28},{16,0},{20,4},{24,8},{28,12},{1,17},{... | collective-permute-start | bytes 393224 | tf_op jit(solution)/shard_map/ppermute | solution.py:413
  64.8 7.2 %collective-permute-start.25 = (f32[256,512]{1,0:T(8,128)S(1)}, f32[256,512]{1,0:T(8,128)S(1)}, u32[]{:S(2)}, u32[]{:S(2)}) collective-permute-start(f32[256,512]{1,0:T(8,128)S(1)} %get-tuple-element.124), channel_id=1, source_target_pairs={{0,4},{4,0},{8,12},{12,8},{16,20},{20,16},{24,28},{28,24},{1,5},{5... | collective-permute-start | bytes 1572872 | tf_op jit(solution)/shard_map/ppermute | solution.py:413
  64.9 2.6 %collective-permute-start.26 = (bf16[16,2048]{1,0:T(8,128)(2,1)S(1)}, bf16[16,2048]{1,0:T(8,128)(2,1)S(1)}, u32[]{:S(2)}, u32[]{:S(2)}) collective-permute-start(bf16[16,2048]{1,0:T(8,128)(2,1)S(1)} %get-tuple-element.126), channel_id=1, source_target_pairs={{0,4},{4,0},{8,12},{12,8},{16,20},{20,16},{24,28},{28,24},{1,5},{5... | collective-permute-start | bytes 196616 | tf_op jit(solution)/shard_map/ppermute | solution.py:413
  65.4 4.7 %collective-permute-start.27 = (bf16[16,2048]{1,0:T(8,128)(2,1)S(1)}, bf16[16,2048]{1,0:T(8,128)(2,1)S(1)}, u32[]{:S(2)}, u32[]{:S(2)}) collective-permute-start(bf16[16,2048]{1,0:T(8,128)(2,1)S(1)} %get-tuple-element.127), channel_id=1, source_target_pairs={{0,8},{4,12},{8,0},{12,4},{16,24},{20,28},{24,16},{28,20},{1,9},{5... | collective-permute-start | bytes 196616 | tf_op jit(solution)/shard_map/ppermute | solution.py:413
  66.2 4.4 %collective-permute-start.28 = (bf16[16,2048]{1,0:T(8,128)(2,1)S(1)}, bf16[16,2048]{1,0:T(8,128)(2,1)S(1)}, u32[]{:S(2)}, u32[]{:S(2)}) collective-permute-start(bf16[16,2048]{1,0:T(8,128)(2,1)S(1)} %get-tuple-element.128), channel_id=1, source_target_pairs={{0,12},{4,8},{8,4},{12,0},{16,28},{20,24},{24,20},{28,16},{1,13},{... | collective-permute-start | bytes 196616 | tf_op jit(solution)/shard_map/ppermute | solution.py:413
  66.8 3.8 %collective-permute-start.29 = (bf16[16,2048]{1,0:T(8,128)(2,1)S(1)}, bf16[16,2048]{1,0:T(8,128)(2,1)S(1)}, u32[]{:S(2)}, u32[]{:S(2)}) collective-permute-start(bf16[16,2048]{1,0:T(8,128)(2,1)S(1)} %get-tuple-element.130), channel_id=1, source_target_pairs={{0,4},{4,0},{8,12},{12,8},{16,20},{20,16},{24,28},{28,24},{1,5},{5... | collective-permute-start | bytes 196616 | tf_op jit(solution)/shard_map/ppermute | solution.py:413
  67.5 4.5 %collective-permute-start.30 = (bf16[16,2048]{1,0:T(8,128)(2,1)S(1)}, bf16[16,2048]{1,0:T(8,128)(2,1)S(1)}, u32[]{:S(2)}, u32[]{:S(2)}) collective-permute-start(bf16[16,2048]{1,0:T(8,128)(2,1)S(1)} %get-tuple-element.131), channel_id=1, source_target_pairs={{0,12},{4,8},{8,4},{12,0},{16,28},{20,24},{24,20},{28,16},{1,13},{... | collective-permute-start | bytes 196616 | tf_op jit(solution)/shard_map/ppermute | solution.py:413
  (2 other events, 15.8 us)

commit v5 on v4

--- a/solution.py
+++ b/solution.py
@@ -22,10 +22,11 @@
 LATE, EARLY = slice(UNIT, BLOCK), slice(0, UNIT)
 
 
-def params(flops=0, nbytes=1 << 20):
+def params(microseconds):
+    flops = int(microseconds * 1.15e9)
     return dict(
         compiler_params=pltpu.CompilerParams(vmem_limit_bytes=16 << 20),
-        cost_estimate=pl.CostEstimate(flops=flops, bytes_accessed=nbytes, transcendentals=0),
+        cost_estimate=pl.CostEstimate(flops=flops, bytes_accessed=0, transcendentals=0),
     )
 
 
@@ -96,14 +97,12 @@
     inv_ref[...] = jnp.broadcast_to(lax.rsqrt(mean_square + EPSILON), inv_ref.shape)
 
 
-def block_probs(pieces, seg, seg_row, model_width, kv_width, after=None):
+def block_probs(pieces, seg, seg_row, model_width, kv_width, after=()):
     heads = model_width // kv_width
     key_heads = kv_width // HEAD_FEATURES
     operands = [near(piece) for piece in pieces] + [near(seg)]
-    specs = [VMEM] * len(operands)
-    if after is not None:
-        operands.append(after)
-        specs.append(ANY)
+    specs = [VMEM] * len(operands) + [ANY] * len(after)
+    operands += after
     return pl.pallas_call(
         functools.partial(probs_kernel, len(pieces), seg_row, model_width, kv_width),
         out_shape=(
@@ -116,13 +115,12 @@
         out_specs=(VMEM,) * 4,
         scratch_shapes=[pltpu.VMEM((BLOCK, 2 * model_width + kv_width), jnp.bfloat16)],
         name="probs",
-        **params(4 * BLOCK * BLOCK * model_width),
+        **params(0.35),
     )(*operands)
 
 
-def unit_math(rows, grads, probs_ref, x_ref, inv_ref, weight_ref, gain_ref, scaled_ref, store, value_ref):
-    model_width = x_ref.shape[1]
-    kv_width = weight_ref.shape[1]
+def unit_math(rows, grads, probs_ref, x_ref, inv_ref, turned_ref, gain_ref, scaled_ref, store, value_ref):
+    kv_width, model_width = turned_ref.shape
     heads = model_width // kv_width
     chunk = min(512, model_width)
     inv = inv_ref[rows, :1]
@@ -147,10 +145,7 @@
     inner = jnp.zeros((UNIT, 1), jnp.float32)
     for first in range(0, model_width, chunk):
         columns = slice(first, first + chunk)
-        normed_grad = lax.dot_general(
-            value, weight_ref[columns, :], (((1,), (1,)), ((), ())),
-            preferred_element_type=jnp.float32,
-        )
+        normed_grad = jnp.dot(value, turned_ref[:, columns], preferred_element_type=jnp.float32)
         scaled = normed_grad * gain_ref[:, columns]
         scaled_ref[:, columns] = scaled
         x = x_ref[rows, columns].astype(jnp.float32)
@@ -165,8 +160,26 @@
         store(columns, (grad + change).astype(jnp.bfloat16))
 
 
+def turn_kernel(weight_ref, *refs):
+    turned_ref = refs[-1]
+    step = min(256, weight_ref.shape[0])
+    for first in range(0, weight_ref.shape[0], step):
+        turned_ref[:, first : first + step] = weight_ref[first : first + step, :].T
+
+
+def turn(weight, after=()):
+    return pl.pallas_call(
+        turn_kernel,
+        out_shape=jax.ShapeDtypeStruct(weight.shape[::-1], weight.dtype),
+        in_specs=[VMEM] + [ANY] * len(after),
+        out_specs=VMEM,
+        name="turn",
+        **params(1.5),
+    )(near(weight), *after)
+
+
 def layer_kernel(
-    live_ref, grad_ref, late_ref, early_ref, inv_ref, x_ref, weight_ref, gain_ref, *rest
+    live_ref, grad_ref, late_ref, early_ref, inv_ref, x_ref, turned_ref, gain_ref, *rest
 ):
     out_ref, value_ref, scaled_ref = rest[-3:]
     if len(rest) == 5:
@@ -185,14 +198,14 @@
 
             grads = [(grad_ref, part) for part in parts]
             unit_math(
-                rows, grads, probs_ref, x_ref, inv_ref, weight_ref, gain_ref, scaled_ref, store,
+                rows, grads, probs_ref, x_ref, inv_ref, turned_ref, gain_ref, scaled_ref, store,
                 value_ref.at[rows],
             )
 
 
-def layer_step(live, grad, block, weight, gain, held=()):
-    model_width, kv_width = weight.shape
-    operands = [live, grad, *block, weight, gain, *held]
+def layer_step(live, grad, block, turned, gain, held=()):
+    kv_width, model_width = turned.shape
+    operands = [live, grad, *block, turned, gain, *held]
     return pl.pallas_call(
         layer_kernel,
         out_shape=(
@@ -203,16 +216,16 @@
         out_specs=(VMEM, VMEM),
         scratch_shapes=[pltpu.VMEM((UNIT, model_width), jnp.float32)],
         name="layer",
-        **params(2 * BLOCK * model_width * kv_width),
+        **params(1.1),
     )(*operands)
 
 
 def tick_kernel(tick, rows, parts, kept, final, *refs):
     grads = list(zip(refs, parts))
-    probs_ref, inv_ref, x_ref, weight_ref, gain_ref = refs[len(parts) : len(parts) + 5]
+    probs_ref, inv_ref, x_ref, turned_ref, gain_ref = refs[len(parts) : len(parts) + 5]
     refs = refs[len(parts) + 5 :]
     earlier, refs = refs[: 2 * kept], refs[2 * kept :]
-    model_width, kv_width = x_ref.shape[1], weight_ref.shape[1]
+    kv_width, model_width = turned_ref.shape
     turn = lax.axis_size("section") - 1 - lax.axis_index("section")
     if final:
         late_ref, late_value_ref = refs[:2]
@@ -231,7 +244,7 @@
     @pl.when(turn == tick)
     def _():
         unit_math(
-            rows, grads, probs_ref, x_ref, inv_ref, weight_ref, gain_ref, scaled_ref, store,
+            rows, grads, probs_ref, x_ref, inv_ref, turned_ref, gain_ref, scaled_ref, store,
             value_ref,
         )
 
@@ -264,12 +277,12 @@
             values_ref[...] = jnp.concatenate(values, axis=0)
 
 
-def tick_step(tick, grads, block, weight, gain, kept=(), late=(), after=()):
-    model_width, kv_width = weight.shape
+def tick_step(tick, grads, block, turned, gain, kept=(), late=(), after=()):
+    kv_width, model_width = turned.shape
     low = len(grads) == 2
     final = len(late) - 1 if late else 0
     arrays = [grad for grad, _ in grads]
-    arrays += [block[1] if low else block[0], block[2], block[3], weight, gain]
+    arrays += [block[1] if low else block[0], block[2], block[3], turned, gain]
     arrays += [array for pair in kept for array in pair]
     arrays += late
     operands = [near(array) for array in arrays]
@@ -299,15 +312,15 @@
         out_specs=(VMEM,) * len(outs),
         scratch_shapes=scratch,
         name="tick",
-        **params(2 * UNIT * model_width * kv_width),
+        **params(0.2),
     )(*operands, *after)
 
 
-def pack_kernel(half, piece, query_ref, key_ref, hidden_ref, up_ref, seg_ref, *rest):
-    sems = rest[-1]
-    seg_out_ref, own_up_ref, across_ref = rest[-4:-1]
-    packed = rest[:-4]
+def pack_kernel(block, half, piece, query_ref, key_ref, hidden_ref, up_ref, seg_ref, *rest):
+    late_ref, early_ref, seg_in_ref, sems = rest[-4:]
+    packed = rest[-4 - half : -4]
     side, at, _ = place()
+    there = side if block == 0 else 1 - side
     copies = []
 
     def copy(source, target):
@@ -315,24 +328,48 @@
         made.start()
         copies.append(made)
 
-    for block in range(2):
-        for k in range(half):
-            replica = (side if block == 0 else 1 - side) * half + lax.bitwise_xor(at, k)
-            rows = pl.ds(pl.multiple_of(replica * piece, piece), piece)
-            target = packed[block * half + k]
-            first = 0
-            for source in (query_ref, key_ref, hidden_ref):
-                width = source.shape[1]
-                copy(source.at[rows], target.at[:, pl.ds(first, width)])
-                first += width
-    for there, target in ((side, own_up_ref), (1 - side, across_ref.at[pl.ds(0, BLOCK)])):
-        copy(up_ref.at[pl.ds(pl.multiple_of(there * BLOCK, BLOCK), BLOCK)], target)
-    ids = jnp.broadcast_to(seg_ref[...].astype(jnp.float32), seg_out_ref.shape).astype(jnp.bfloat16)
-    seg_out_ref[...] = ids
-    across_ref[BLOCK:, :] = jnp.zeros((16, across_ref.shape[1]), jnp.bfloat16)
-    across_ref[BLOCK:, : ids.shape[1]] = ids
-    for made in copies:
+    copy(seg_ref, seg_in_ref)
+    for k in range(half):
+        replica = there * half + lax.bitwise_xor(at, k)
+        rows = pl.ds(pl.multiple_of(replica * piece, piece), piece)
+        first = 0
+        for source in (query_ref, key_ref, hidden_ref):
+            width = source.shape[1]
+            copy(source.at[rows], packed[k].at[:, pl.ds(first, width)])
+            first += width
+    for first, target in ((0, early_ref), (UNIT, late_ref.at[pl.ds(0, UNIT)])):
+        copy(up_ref.at[pl.ds(pl.multiple_of(there * BLOCK + first, UNIT), UNIT)], target)
+    late_ref[UNIT:, :] = jnp.zeros((16, late_ref.shape[1]), jnp.bfloat16)
+    copies[0].wait()
+    ids = seg_in_ref[...].astype(jnp.float32)
+    late_ref[UNIT:, : ids.shape[1]] = jnp.broadcast_to(ids, (16, ids.shape[1])).astype(
+        jnp.bfloat16
+    )
+    for made in copies[1:]:
         made.wait()
+
+
+def pack(block, half, piece, sources):
+    model_width = sources[0].shape[1]
+    width = sum(source.shape[1] for source in sources[:3])
+    bf16 = jnp.bfloat16
+    operands = [pltpu.with_memory_space_constraint(array, pltpu.HBM) for array in sources]
+    return pl.pallas_call(
+        functools.partial(pack_kernel, block, half, piece),
+        out_shape=(jax.ShapeDtypeStruct((piece, width), bf16),) * half
+        + (
+            jax.ShapeDtypeStruct((UNIT + 16, model_width), bf16),
+            jax.ShapeDtypeStruct((UNIT, model_width), bf16),
+        ),
+        in_specs=[pl.BlockSpec(memory_space=pltpu.HBM)] * len(sources),
+        out_specs=(VMEM,) * (half + 2),
+        scratch_shapes=[
+            pltpu.VMEM(sources[-1].shape, jnp.int32),
+            pltpu.SemaphoreType.DMA((3 * half + 3,)),
+        ],
+        name="pack",
+        **params(1.2),
+    )(*operands)
 
 
 def columns_kernel(width, first_ref, second_ref, *outs):
@@ -412,37 +449,22 @@
     def swap(array, k):
         return lax.ppermute(array, "dp", [(i, i ^ k) for i in range(replicas)])
 
-    def far(array):
-        return pltpu.with_memory_space_constraint(array, pltpu.HBM)
-
     count = 2 * half
     bf16 = jnp.bfloat16
-    packed = pl.pallas_call(
-        functools.partial(pack_kernel, half, piece),
-        out_shape=(jax.ShapeDtypeStruct((piece, 2 * model_width + kv_width), bf16),) * count
-        + (
-            jax.ShapeDtypeStruct((16, segments.shape[1]), bf16),
-            jax.ShapeDtypeStruct((BLOCK, model_width), bf16),
-            jax.ShapeDtypeStruct((BLOCK + 16, model_width), bf16),
-        ),
-        in_specs=[pl.BlockSpec(memory_space=pltpu.HBM)] * 4 + [VMEM],
-        out_specs=(VMEM,) * (count + 3),
-        scratch_shapes=[pltpu.SemaphoreType.DMA((3 * count + 2,))],
-        name="pack",
-        **params(0, 3 << 20),
-    )(far(query), far(key), far(hidden), far(upstream), segments)
-    pieces = [
-        [packed[b * half]] + [swap(packed[b * half + k], k) for k in range(1, half)]
-        for b in range(2)
-    ]
-    across = swap(packed[-1], half)
-    grads, segs = [packed[-2], across], [(packed[-3], 0), (across, BLOCK)]
-    blocks, kept, after = [], [], ()
+    sources = (query, key, hidden, upstream, segments)
+    pieces, ups = [], []
     for b in range(2):
-        block = block_probs(pieces[b], *segs[b], model_width, kv_width, *after)
-        late, early = (grads[b], LATE), (grads[b], EARLY)
-        first = tick_step(0, [late], block, weight, norm_gain)
-        second = tick_step(0, [late, early], block, weight, norm_gain, after=[first[0]])
+        *packed, late, early = pack(b, half, piece, sources)
+        pieces.append([packed[0]] + [swap(packed[k], k) for k in range(1, half)])
+        ups.append([swap(part, half) for part in (late, early)] if b else [late, early])
+    whole = slice(0, UNIT)
+    turned = turn(weight)
+    blocks, kept, after = [], [], [turned]
+    for b in range(2):
+        block = block_probs(pieces[b], ups[b][0], UNIT, model_width, kv_width, after)
+        late, early = [(part, whole) for part in ups[b]]
+        first = tick_step(0, [late], block, turned, norm_gain)
+        second = tick_step(0, [late, early], block, turned, norm_gain, after=[first[0]])
         blocks.append(block)
         kept += [[first], [second]]
         after = [second[0]]
@@ -453,43 +475,42 @@
         in_specs=[VMEM, VMEM],
         out_specs=(VMEM,) * half,
         name="columns",
-        **params(0, 1 << 20),
+        **params(0.4),
     )(blocks[0][3], blocks[1][3])
     columns = [columns[0]] + [swap(columns[k], 2 * k) for k in range(1, half)]
 
-    whole = slice(0, UNIT)
     for tick in range(1, layers):
         hop = [(layers - tick, layers - 1 - tick)]
         grads = [(lax.ppermute(unit[-1][0], "section", hop), whole) for unit in kept]
         last = tick == layers - 1
-        after, done = [], []
+        after, done = (columns if last else []), []
         for u in range(4):
             needs = grads[u - 1 : u + 1] if u % 2 else grads[u : u + 1]
             late = []
             if last and u % 2:
                 late = list(done[u - 1]) + ([done[1][0]] if u == 3 else [])
+            if last and u == 3:
+                rows = [done[1][1]] + [swap(done[1][1 + k], k) for k in range(1, half)]
+                after = after + rows[1:]
             done.append(
                 tick_step(
-                    tick, needs, blocks[u // 2], weight, norm_gain, kept[u] if last else (), late,
+                    tick, needs, blocks[u // 2], turned, norm_gain, kept[u] if last else (), late,
                     after,
                 )
             )
             after = [done[u][0]]
             kept[u].append(done[u])
-    first_rows = done[1][1:]
     values, *last_rows = done[3]
-    first_rows = [first_rows[0]] + [swap(first_rows[k], k) for k in range(1, half)]
     last_rows = [last_rows[0]] + [swap(last_rows[k], k) for k in range(1, half)]
     gathered = [values, last_rows[2]] + [swap(values, 2 * k) for k in range(2, half)]
-    rows = first_rows + last_rows
     own, other = pl.pallas_call(
         functools.partial(partial_kernel, half, shares, piece),
         out_shape=(jax.ShapeDtypeStruct((shares, kv_width), jnp.float32),) * 2,
-        in_specs=[VMEM] * (2 * half),
+        in_specs=[VMEM] * (2 * half) + [ANY] * 2,
         out_specs=(VMEM, VMEM),
         name="weight_partial",
-        **params(4 * tokens * half * shares * kv_width),
-    )(*columns, *gathered)
+        **params(0.5),
+    )(*columns, *gathered, last_rows[1], last_rows[3])
     other = swap(other, 1)
     scale = float(tokens * replicas) ** (-0.5)
     input_grad, weight_grad, gain_grad = pl.pallas_call(
@@ -503,8 +524,8 @@
         out_specs=(ANY, VMEM, VMEM),
         scratch_shapes=[pltpu.SemaphoreType.DMA((count,))],
         name="finish",
-        **params(),
-    )(own, other, weight, norm_gain, *rows)
+        **params(2.0),
+    )(own, other, weight, norm_gain, *rows, *last_rows)
     return input_grad[None], weight_grad[None], gain_grad
 
 
@@ -547,6 +568,7 @@
     def spread(array):
         return lax.all_to_all(array, "dp", split_axis=0, concat_axis=0, tiled=True)
 
+    turned = turn(weight)
     blocks, grads = [], []
     for which in range(2):
         up = rows_of(upstream, which)
@@ -562,7 +584,7 @@
 
     def layer(tick, which, grad, kept):
         live = (section == layers - 1 - tick).astype(jnp.int32)[None]
-        return layer_step(live, grad, blocks[which], weight, norm_gain, kept)
+        return layer_step(live, grad, blocks[which], turned, norm_gain, kept)
 
     held = [layer(0, which, grads[which], ()) for which in range(2)]
     hops = [(i, i - 1) for i in range(1, layers)]

time: 74.3 us -> 65.9 us (0.89)
  waiting for transfers between devices: 34 us -> 23 us
  starting transfers between devices: 28.8 us -> 31.5 us
  local copies, waits for them, and re-layouts: 0.81 us -> 0.01 us
  Pallas kernels: 9.32 us -> 10.1 us
    ppermute x19 -> x20, waiting for transfers between devices: 21.7 us -> 14.3 us  [swap(): return lax.ppermute(array, 'dp', [(i, i ^ k) for i in range(replicas)])]
    ppermute x12, waiting for transfers between devices: 12.3 us -> 8.71 us  [direct(): lax.ppermute(unit[-1][0], 'section', hop)]
    ppermute x19 -> x20, starting transfers between devices: 18.3 us -> 21 us  [swap(): return lax.ppermute(array, 'dp', [(i, i ^ k) for i in range(replicas)])]
    pallas_call x1 -> x3, Pallas kernels: 1.75 us -> 3.54 us  [the longest x2 2.91 us: pack(): pl.pallas_call(functools.partial(pack_kernel, block, half, piece), out_sh...]
    pallas_call x16, Pallas kernels: 4.37 us -> 3.38 us  [tick_step(): pl.pallas_call(functools.partial(tick_kernel, tick, EARLY if low else LAT...]
    unnamed x6 -> x4, local copies, waits for them, and re-layouts: 0.81 us -> 0.01 us
  transfers between devices with their start and end apart: 31 -> 32, of which waited for: 13 -> 14; matrix products, arithmetic and copies ran while one was open for 0% -> 0% of each run, Pallas kernels for 7% -> 8%
where the time goes in v5:
time: 65.9 us; the launch traced here: 65.6 us
  starting transfers between devices  31.5 us (48%)
  waiting for transfers between devices  23 us (35%)
  Pallas kernels  10.1 us (15%)
  between operations  1.01 us (2%)
    ppermute x20, starting transfers between devices, swap(): return lax.ppermute(array, 'dp', [(i, i ^ k) for i in range(replicas)])  21 us
    ppermute x20, waiting for transfers between devices, swap(): return lax.ppermute(array, 'dp', [(i, i ^ k) for i in range(replicas)])  14.3 us
    ppermute x12, starting transfers between devices, direct(): lax.ppermute(unit[-1][0], 'section', hop)  10.5 us
    ppermute x12, waiting for transfers between devices, direct(): lax.ppermute(unit[-1][0], 'section', hop)  8.71 us
    pallas_call x16, Pallas kernels, tick_step(): pl.pallas_call(functools.partial(tick_kernel, tick, EARLY if low else LAT...  3.38 us
    pallas_call x2, Pallas kernels, pack(): pl.pallas_call(functools.partial(pack_kernel, block, half, piece), out_sh...  2.91 us
    pallas_call x1, Pallas kernels, direct(): pl.pallas_call(functools.partial(finish_kernel, half, scale), out_shape=(...  2 us
  transfers between devices with their start and end apart: 32, of which 14 were waited for; matrix products, arithmetic and copies ran while one was open for 0% of the time, Pallas kernels for 8%

profile of v5, /device:TPU:0, one launch (start us, length us, event | category | flops | bytes accessed | tf_op | source)
XLA Modules:
  0.0 65.6 jit_solution(12288571033565032995)
XLA Ops:
  0.6 1.4 %pack.2 = (bf16[16,4608]{1,0:T(8,128)(2,1)S(1)}, bf16[16,4608]{1,0:T(8,128)(2,1)S(1)}, bf16[16,4608]{1,0:T(8,128)(2,1)S(1)}, bf16[16,4608]{1,0:T(8,128)(2,1)S(1)...) custom-call(bf16[128,2048]{1,0:T(8,128)(2,1)} %bitcast.8, bf16[128,512]{1,0:T(8,128)(2,1)} %bitcast.12, ...), custom_call_target="tpu_custom_call" | custom-call | flops 1380000000 | tf_op jit(solution)/shard_map/pack/pallas_call | solution.py:357
  2.6 2.6 %collective-permute-start.1 = (bf16[16,4608]{1,0:T(8,128)(2,1)S(1)}, bf16[16,4608]{1,0:T(8,128)(2,1)S(1)}, u32[]{:S(2)}, u32[]{:S(2)}) collective-permute-start(bf16[16,4608]{1,0:T(8,128)(2,1)S(1)} %get-tuple-element.72), channel_id=1, source_target_pairs={{0,8},{4,12},{8,0},{12,4},{16,24},{20,28},{24,16},{28,20},{1,9},{5... | collective-permute-start | bytes 442376 | tf_op jit(solution)/shard_map/ppermute | solution.py:450
  5.2 1.5 %pack.3 = (bf16[16,4608]{1,0:T(8,128)(2,1)S(1)}, bf16[16,4608]{1,0:T(8,128)(2,1)S(1)}, bf16[16,4608]{1,0:T(8,128)(2,1)S(1)}, bf16[16,4608]{1,0:T(8,128)(2,1)S(1)...) custom-call(bf16[128,2048]{1,0:T(8,128)(2,1)} %bitcast.9, bf16[128,512]{1,0:T(8,128)(2,1)} %bitcast.13, ...), custom_call_target="tpu_custom_call" | custom-call | flops 1380000000 | tf_op jit(solution)/shard_map/pack/pallas_call | solution.py:357
  6.7 1.8 %collective-permute-start.6 = (bf16[48,2048]{1,0:T(8,128)(2,1)S(1)}, bf16[48,2048]{1,0:T(8,128)(2,1)S(1)}, u32[]{:S(2)}, u32[]{:S(2)}) collective-permute-start(bf16[48,2048]{1,0:T(8,128)(2,1)S(1)} %get-tuple-element.80), channel_id=1, source_target_pairs={{0,16},{4,20},{8,24},{12,28},{16,0},{20,4},{24,8},{28,12},{1,17},{... | collective-permute-start | bytes 589832 | tf_op jit(solution)/shard_map/ppermute | solution.py:450
  8.6 1.4 %collective-permute-start.4 = (bf16[16,4608]{1,0:T(8,128)(2,1)S(1)}, bf16[16,4608]{1,0:T(8,128)(2,1)S(1)}, u32[]{:S(2)}, u32[]{:S(2)}) collective-permute-start(bf16[16,4608]{1,0:T(8,128)(2,1)S(1)} %get-tuple-element.78), channel_id=1, source_target_pairs={{0,8},{4,12},{8,0},{12,4},{16,24},{20,28},{24,16},{28,20},{1,9},{5... | collective-permute-start | bytes 442376 | tf_op jit(solution)/shard_map/ppermute | solution.py:450
  11.2 1.2 %collective-permute-done.2.refs_3_ = bf16[16,4608]{1,0:T(8,128)(2,1)S(1)} collective-permute-done((bf16[16,4608]{1,0:T(8,128)(2,1)S(1)}, bf16[16,4608]{1,0:T(8,128)(2,1)S(1)}, u32[]{:S(2)}, u32[]{:S(2)}) %collective-permute-start.2) | collective-permute-done | bytes 147488 | tf_op jit(solution)/shard_map/ppermute | solution.py:450
  12.5 1.6 %collective-permute-start.17 = (bf16[32,2048]{1,0:T(8,128)(2,1)S(1)}, bf16[32,2048]{1,0:T(8,128)(2,1)S(1)}, u32[]{:S(2)}, u32[]{:S(2)}) collective-permute-start(bf16[32,2048]{1,0:T(8,128)(2,1)S(1)} %get-tuple-element.101), channel_id=1, source_target_pairs={{0,16},{4,20},{8,24},{12,28},{16,0},{20,4},{24,8},{28,12},{1,17},{... | collective-permute-start | bytes 393224 | tf_op jit(solution)/shard_map/ppermute | solution.py:450
  14.4 0.7 %collective-permute-start.11 = (bf16[32,2048]{1,0:T(8,128)(2,1)S(1)}, bf16[32,2048]{1,0:T(8,128)(2,1)S(1)}, u32[]{:S(2)}, u32[]{:S(2)}) collective-permute-start(bf16[32,2048]{1,0:T(8,128)(2,1)S(1)} %get-tuple-element.85.refs_7_.refs_6_), channel_id=1, source_target_pairs={{3,2},{7,6},{11,10},{15,14},{19,18},{23,22},{27,26},{31,30}} | collective-permute-start | bytes 393224 | tf_op jit(solution)/shard_map/ppermute | solution.py:484
  15.1 1.0 %collective-permute-done.4.refs_2_ = bf16[16,4608]{1,0:T(8,128)(2,1)S(1)} collective-permute-done((bf16[16,4608]{1,0:T(8,128)(2,1)S(1)}, bf16[16,4608]{1,0:T(8,128)(2,1)S(1)}, u32[]{:S(2)}, u32[]{:S(2)}) %collective-permute-start.4) | collective-permute-done | bytes 147488 | tf_op jit(solution)/shard_map/ppermute | solution.py:450
  16.8 2.0 %collective-permute-done.5.refs_3_ = bf16[16,4608]{1,0:T(8,128)(2,1)S(1)} collective-permute-done((bf16[16,4608]{1,0:T(8,128)(2,1)S(1)}, bf16[16,4608]{1,0:T(8,128)(2,1)S(1)}, u32[]{:S(2)}, u32[]{:S(2)}) %collective-permute-start.5) | collective-permute-done | bytes 147488 | tf_op jit(solution)/shard_map/ppermute | solution.py:450
  21.3 1.6 %collective-permute-start.7 = (bf16[128,512]{1,0:T(8,128)(2,1)S(1)}, bf16[128,512]{1,0:T(8,128)(2,1)S(1)}, u32[]{:S(2)}, u32[]{:S(2)}) collective-permute-start(bf16[128,512]{1,0:T(8,128)(2,1)S(1)} %get-tuple-element.89), channel_id=1, source_target_pairs={{0,8},{4,12},{8,0},{12,4},{16,24},{20,28},{24,16},{28,20},{1,9},{5... | collective-permute-start | bytes 393224 | tf_op jit(solution)/shard_map/ppermute | solution.py:450
  25.0 1.6 %collective-permute-start.8 = (bf16[128,512]{1,0:T(8,128)(2,1)S(1)}, bf16[128,512]{1,0:T(8,128)(2,1)S(1)}, u32[]{:S(2)}, u32[]{:S(2)}) collective-permute-start(bf16[128,512]{1,0:T(8,128)(2,1)S(1)} %get-tuple-element.90), channel_id=1, source_target_pairs={{0,16},{4,20},{8,24},{12,28},{16,0},{20,4},{24,8},{28,12},{1,17},{... | collective-permute-start | bytes 393224 | tf_op jit(solution)/shard_map/ppermute | solution.py:450
  26.9 2.7 %collective-permute-start.9 = (bf16[128,512]{1,0:T(8,128)(2,1)S(1)}, bf16[128,512]{1,0:T(8,128)(2,1)S(1)}, u32[]{:S(2)}, u32[]{:S(2)}) collective-permute-start(bf16[128,512]{1,0:T(8,128)(2,1)S(1)} %get-tuple-element.91), channel_id=1, source_target_pairs={{0,24},{4,28},{8,16},{12,20},{16,8},{20,12},{24,0},{28,4},{1,25},{... | collective-permute-start | bytes 393224 | tf_op jit(solution)/shard_map/ppermute | solution.py:450
  29.6 1.3 %collective-permute-start.21 = (bf16[32,2048]{1,0:T(8,128)(2,1)S(1)}, bf16[32,2048]{1,0:T(8,128)(2,1)S(1)}, u32[]{:S(2)}, u32[]{:S(2)}) collective-permute-start(bf16[32,2048]{1,0:T(8,128)(2,1)S(1)} %get-tuple-element.98.refs_7_.refs_10_), channel_id=1, source_target_pairs={{1,0},{5,4},{9,8},{13,12},{17,16},{21,20},{25,24},{29,28}} | collective-permute-start | bytes 393224 | tf_op jit(solution)/shard_map/ppermute | solution.py:484
  30.9 1.3 %collective-permute-start.22 = (bf16[32,2048]{1,0:T(8,128)(2,1)S(1)}, bf16[32,2048]{1,0:T(8,128)(2,1)S(1)}, u32[]{:S(2)}, u32[]{:S(2)}) collective-permute-start(bf16[32,2048]{1,0:T(8,128)(2,1)S(1)} %get-tuple-element.99.refs_6_.refs_11_), channel_id=1, source_target_pairs={{1,0},{5,4},{9,8},{13,12},{17,16},{21,20},{25,24},{29,28}} | collective-permute-start | bytes 393224 | tf_op jit(solution)/shard_map/ppermute | solution.py:484
  32.2 1.3 %collective-permute-start.16 = (bf16[32,2048]{1,0:T(8,128)(2,1)S(1)}, bf16[32,2048]{1,0:T(8,128)(2,1)S(1)}, u32[]{:S(2)}, u32[]{:S(2)}) collective-permute-start(bf16[32,2048]{1,0:T(8,128)(2,1)S(1)} %get-tuple-element.100.refs_7_.refs_10_), channel_id=1, source_target_pairs={{1,0},{5,4},{9,8},{13,12},{17,16},{21,20},{25,24},{29,28}} | collective-permute-start | bytes 393224 | tf_op jit(solution)/shard_map/ppermute | solution.py:484
  33.6 1.3 %collective-permute-start.20 = (bf16[32,2048]{1,0:T(8,128)(2,1)S(1)}, bf16[32,2048]{1,0:T(8,128)(2,1)S(1)}, u32[]{:S(2)}, u32[]{:S(2)}) collective-permute-start(bf16[32,2048]{1,0:T(8,128)(2,1)S(1)} %get-tuple-element.105.refs_11_), channel_id=1, source_target_pairs={{1,0},{5,4},{9,8},{13,12},{17,16},{21,20},{25,24},{29,28}} | collective-permute-start | bytes 393224 | tf_op jit(solution)/shard_map/ppermute | solution.py:484
  34.9 5.1 %collective-permute-done.21.refs_0_ = bf16[32,2048]{1,0:T(8,128)(2,1)S(1)} collective-permute-done((bf16[32,2048]{1,0:T(8,128)(2,1)S(1)}, bf16[32,2048]{1,0:T(8,128)(2,1)S(1)}, u32[]{:S(2)}, u32[]{:S(2)}) %collective-permute-start.21) | collective-permute-done | bytes 131104 | tf_op jit(solution)/shard_map/ppermute | solution.py:484
  39.9 0.8 %tick.28 = (bf16[32,2048]{1,0:T(8,128)(2,1)S(1)}, bf16[32,512]{1,0:T(8,128)(2,1)S(1)}) custom-call(bf16[32,2048]{1,0:T(8,128)(2,1)S(1)} %collective-permute-done.21.refs_0_, bf16[4,32,128]{2,1,0:T(8,128)(2,1)S(1)} %get-tuple-element.84.refs_1_, f32[64,128]{1,0:T(8,128)S(1)} %get-tuple-element.83.refs_2_.refs_3_, ...), custom_call_target="tpu_custom_call" | custom-call | flops 230000000 | tf_op jit(solution)/shard_map/tick/pallas_call | solution.py:306
  40.7 1.9 %collective-permute-done.22.refs_1_ = bf16[32,2048]{1,0:T(8,128)(2,1)S(1)} collective-permute-done((bf16[32,2048]{1,0:T(8,128)(2,1)S(1)}, bf16[32,2048]{1,0:T(8,128)(2,1)S(1)}, u32[]{:S(2)}, u32[]{:S(2)}) %collective-permute-start.22) | collective-permute-done | bytes 131104 | tf_op jit(solution)/shard_map/ppermute | solution.py:484
  42.6 0.8 %tick.29 = (bf16[64,512]{1,0:T(8,128)(2,1)S(1)}, bf16[16,2048]{1,0:T(8,128)(2,1)S(1)}, bf16[16,2048]{1,0:T(8,128)(2,1)S(1)}, bf16[16,2048]{1,0:T(8,128)(2,1)S(1)}, bf16[16,2048]{1,0:T(8,128)(2,1)S(1)}) custom-call(bf16[32,2048]{1,0:T(8,128)(2,1)S(1)} %collective-permute-done.21.refs_0_, bf16[32,2048]{1,0:T(8,128)(2,1)S(1)} %collective-permute-done.22.refs_1_, ...), custom_call_target="tpu_custom_call" | custom-call | flops 230000000 | tf_op jit(solution)/shard_map/tick/pallas_call | solution.py:306
  43.6 1.8 %collective-permute-start.25 = (bf16[16,2048]{1,0:T(8,128)(2,1)S(1)}, bf16[16,2048]{1,0:T(8,128)(2,1)S(1)}, u32[]{:S(2)}, u32[]{:S(2)}) collective-permute-start(bf16[16,2048]{1,0:T(8,128)(2,1)S(1)} %get-tuple-element.125), channel_id=1, source_target_pairs={{0,12},{4,8},{8,4},{12,0},{16,28},{20,24},{24,20},{28,16},{1,13},{... | collective-permute-start | bytes 196616 | tf_op jit(solution)/shard_map/ppermute | solution.py:450
  45.9 0.8 %tick.30 = (bf16[32,2048]{1,0:T(8,128)(2,1)S(1)}, bf16[32,512]{1,0:T(8,128)(2,1)S(1)}) custom-call(bf16[32,2048]{1,0:T(8,128)(2,1)S(1)} %collective-permute-done.16.refs_0_, bf16[4,32,128]{2,1,0:T(8,128)(2,1)S(1)} %get-tuple-element.92.refs_1_, f32[64,128]{1,0:T(8,128)S(1)} %get-tuple-element.93.refs_2_.refs_3_, ...), custom_call_target="tpu_custom_call" | custom-call | flops 230000000 | tf_op jit(solution)/shard_map/tick/pallas_call | solution.py:306
  46.7 1.2 %collective-permute-done.20.refs_1_ = bf16[32,2048]{1,0:T(8,128)(2,1)S(1)} collective-permute-done((bf16[32,2048]{1,0:T(8,128)(2,1)S(1)}, bf16[32,2048]{1,0:T(8,128)(2,1)S(1)}, u32[]{:S(2)}, u32[]{:S(2)}) %collective-permute-start.20) | collective-permute-done | bytes 131104 | tf_op jit(solution)/shard_map/ppermute | solution.py:484
  49.0 0.8 %tick.31 = (bf16[128,512]{1,0:T(8,128)(2,1)S(1)}, bf16[16,2048]{1,0:T(8,128)(2,1)S(1)}, bf16[16,2048]{1,0:T(8,128)(2,1)S(1)}, bf16[48,2048]{1,0:T(8,128)(2,1)S(1)}, bf16[16,2048]{1,0:T(8,128)(2,1)S(1)}) custom-call(bf16[32,2048]{1,0:T(8,128)(2,1)S(1)} %collective-permute-done.16.refs_0_, bf16[32,2048]{1,0:T(8,128)(2,1)S(1)} %collective-permute-done.20.refs_1_, ...), custom_call_target="tpu_custom_call" | custom-call | flops 230000000 | tf_op jit(solution)/shard_map/tick/pallas_call | solution.py:306
  49.8 0.7 %collective-permute-start.26 = (bf16[48,2048]{1,0:T(8,128)(2,1)S(1)}, bf16[48,2048]{1,0:T(8,128)(2,1)S(1)}, u32[]{:S(2)}, u32[]{:S(2)}) collective-permute-start(bf16[48,2048]{1,0:T(8,128)(2,1)S(1)} %get-tuple-element.127), channel_id=1, source_target_pairs={{0,8},{4,12},{8,0},{12,4},{16,24},{20,28},{24,16},{28,20},{1,9},{5... | collective-permute-start | bytes 589832 | tf_op jit(solution)/shard_map/ppermute | solution.py:450
  50.6 1.6 %collective-permute-start.27 = (bf16[128,512]{1,0:T(8,128)(2,1)S(1)}, bf16[128,512]{1,0:T(8,128)(2,1)S(1)}, u32[]{:S(2)}, u32[]{:S(2)}) collective-permute-start(bf16[128,512]{1,0:T(8,128)(2,1)S(1)} %get-tuple-element.126.refs_4_), channel_id=1, source_target_pairs={{0,16},{4,20},{8,24},{12,28},{16,0},{20,4},{24,8},{28,12},{1,17},{... | collective-permute-start | bytes 393224 | tf_op jit(solution)/shard_map/ppermute | solution.py:450
  52.1 1.3 %collective-permute-start.28 = (bf16[128,512]{1,0:T(8,128)(2,1)S(1)}, bf16[128,512]{1,0:T(8,128)(2,1)S(1)}, u32[]{:S(2)}, u32[]{:S(2)}) collective-permute-start(bf16[128,512]{1,0:T(8,128)(2,1)S(1)} %get-tuple-element.126.refs_4_), channel_id=1, source_target_pairs={{0,24},{4,28},{8,16},{12,20},{16,8},{20,12},{24,0},{28,4},{1,25},{... | collective-permute-start | bytes 393224 | tf_op jit(solution)/shard_map/ppermute | solution.py:450
  53.4 0.8 %collective-permute-start.30 = (bf16[16,2048]{1,0:T(8,128)(2,1)S(1)}, bf16[16,2048]{1,0:T(8,128)(2,1)S(1)}, u32[]{:S(2)}, u32[]{:S(2)}) collective-permute-start(bf16[16,2048]{1,0:T(8,128)(2,1)S(1)} %get-tuple-element.129), channel_id=1, source_target_pairs={{0,12},{4,8},{8,4},{12,0},{16,28},{20,24},{24,20},{28,16},{1,13},{... | collective-permute-start | bytes 196616 | tf_op jit(solution)/shard_map/ppermute | solution.py:450
  54.6 5.9 %collective-permute-done.30.refs_9_.refs_7_ = bf16[16,2048]{1,0:T(8,128)(2,1)S(1)} collective-permute-done((bf16[16,2048]{1,0:T(8,128)(2,1)S(1)}, bf16[16,2048]{1,0:T(8,128)(2,1)S(1)}, u32[]{:S(2)}, u32[]{:S(2)}) %collective-permute-start.30) | collective-permute-done | bytes 65568 | tf_op jit(solution)/shard_map/ppermute | solution.py:450
  61.8 1.8 %collective-permute-done.31.other_ref = f32[256,512]{1,0:T(8,128)S(1)} collective-permute-done((f32[256,512]{1,0:T(8,128)S(1)}, f32[256,512]{1,0:T(8,128)S(1)}, u32[]{:S(2)}, u32[]{:S(2)}) %collective-permute-start.31) | collective-permute-done | bytes 524320 | tf_op jit(solution)/shard_map/ppermute | solution.py:450
  63.6 2.0 %finish.1 = (bf16[128,2048]{1,0:T(8,128)(2,1)}, f32[256,512]{1,0:T(8,128)}, f32[1,256]{1,0:T(1,128)}) custom-call(f32[256,512]{1,0:T(8,128)S(1)} %get-tuple-element.130.own_ref, f32[256,512]{1,0:T(8,128)S(1)} %collective-permute-done.31.other_ref, bf16[2048,512]{1,0:T(8,128)(2,1)S(1)} %bitcast.7, f32[1,2048]{1,0:T(1,128)S(1)} %copy-done, ...), custom_call_target="tpu_custom_call" | custom-call | flops 2300000000 | tf_op jit(solution)/shard_map/finish/pallas_call | solution.py:516
  (60 shorter events, 11.2 us)
Async XLA Ops:
  2.0 6.6 %collective-permute-start = (bf16[16,4608]{1,0:T(8,128)(2,1)S(1)}, bf16[16,4608]{1,0:T(8,128)(2,1)S(1)}, u32[]{:S(2)}, u32[]{:S(2)}) collective-permute-start(bf16[16,4608]{1,0:T(8,128)(2,1)S(1)} %get-tuple-element.71), channel_id=1, source_target_pairs={{0,4},{4,0},{8,12},{12,8},{16,20},{20,16},{24,28},{28,24},{1,5},{5... | collective-permute-start | bytes 442376 | tf_op jit(solution)/shard_map/ppermute | solution.py:450
  2.6 7.4 %collective-permute-start.1 = (bf16[16,4608]{1,0:T(8,128)(2,1)S(1)}, bf16[16,4608]{1,0:T(8,128)(2,1)S(1)}, u32[]{:S(2)}, u32[]{:S(2)}) collective-permute-start(bf16[16,4608]{1,0:T(8,128)(2,1)S(1)} %get-tuple-element.72), channel_id=1, source_target_pairs={{0,8},{4,12},{8,0},{12,4},{16,24},{20,28},{24,16},{28,20},{1,9},{5... | collective-permute-start | bytes 442376 | tf_op jit(solution)/shard_map/ppermute | solution.py:450
  5.1 7.3 %collective-permute-start.2 = (bf16[16,4608]{1,0:T(8,128)(2,1)S(1)}, bf16[16,4608]{1,0:T(8,128)(2,1)S(1)}, u32[]{:S(2)}, u32[]{:S(2)}) collective-permute-start(bf16[16,4608]{1,0:T(8,128)(2,1)S(1)} %get-tuple-element.73), channel_id=1, source_target_pairs={{0,12},{4,8},{8,4},{12,0},{16,28},{20,24},{24,20},{28,16},{1,13},{... | collective-permute-start | bytes 442376 | tf_op jit(solution)/shard_map/ppermute | solution.py:450
  6.7 12.1 %collective-permute-start.6 = (bf16[48,2048]{1,0:T(8,128)(2,1)S(1)}, bf16[48,2048]{1,0:T(8,128)(2,1)S(1)}, u32[]{:S(2)}, u32[]{:S(2)}) collective-permute-start(bf16[48,2048]{1,0:T(8,128)(2,1)S(1)} %get-tuple-element.80), channel_id=1, source_target_pairs={{0,16},{4,20},{8,24},{12,28},{16,0},{20,4},{24,8},{28,12},{1,17},{... | collective-permute-start | bytes 589832 | tf_op jit(solution)/shard_map/ppermute | solution.py:450
  8.6 5.9 %collective-permute-start.3 = (bf16[16,4608]{1,0:T(8,128)(2,1)S(1)}, bf16[16,4608]{1,0:T(8,128)(2,1)S(1)}, u32[]{:S(2)}, u32[]{:S(2)}) collective-permute-start(bf16[16,4608]{1,0:T(8,128)(2,1)S(1)} %get-tuple-element.77), channel_id=1, source_target_pairs={{0,4},{4,0},{8,12},{12,8},{16,20},{20,16},{24,28},{28,24},{1,5},{5... | collective-permute-start | bytes 442376 | tf_op jit(solution)/shard_map/ppermute | solution.py:450
  8.6 7.5 %collective-permute-start.4 = (bf16[16,4608]{1,0:T(8,128)(2,1)S(1)}, bf16[16,4608]{1,0:T(8,128)(2,1)S(1)}, u32[]{:S(2)}, u32[]{:S(2)}) collective-permute-start(bf16[16,4608]{1,0:T(8,128)(2,1)S(1)} %get-tuple-element.78), channel_id=1, source_target_pairs={{0,8},{4,12},{8,0},{12,4},{16,24},{20,28},{24,16},{28,20},{1,9},{5... | collective-permute-start | bytes 442376 | tf_op jit(solution)/shard_map/ppermute | solution.py:450
  10.0 8.8 %collective-permute-start.5 = (bf16[16,4608]{1,0:T(8,128)(2,1)S(1)}, bf16[16,4608]{1,0:T(8,128)(2,1)S(1)}, u32[]{:S(2)}, u32[]{:S(2)}) collective-permute-start(bf16[16,4608]{1,0:T(8,128)(2,1)S(1)} %get-tuple-element.79), channel_id=1, source_target_pairs={{0,12},{4,8},{8,4},{12,0},{16,28},{20,24},{24,20},{28,16},{1,13},{... | collective-permute-start | bytes 442376 | tf_op jit(solution)/shard_map/ppermute | solution.py:450
  12.5 7.4 %collective-permute-start.17 = (bf16[32,2048]{1,0:T(8,128)(2,1)S(1)}, bf16[32,2048]{1,0:T(8,128)(2,1)S(1)}, u32[]{:S(2)}, u32[]{:S(2)}) collective-permute-start(bf16[32,2048]{1,0:T(8,128)(2,1)S(1)} %get-tuple-element.101), channel_id=1, source_target_pairs={{0,16},{4,20},{8,24},{12,28},{16,0},{20,4},{24,8},{28,12},{1,17},{... | collective-permute-start | bytes 393224 | tf_op jit(solution)/shard_map/ppermute | solution.py:450
  14.4 6.1 %collective-permute-start.11 = (bf16[32,2048]{1,0:T(8,128)(2,1)S(1)}, bf16[32,2048]{1,0:T(8,128)(2,1)S(1)}, u32[]{:S(2)}, u32[]{:S(2)}) collective-permute-start(bf16[32,2048]{1,0:T(8,128)(2,1)S(1)} %get-tuple-element.85.refs_7_.refs_6_), channel_id=1, source_target_pairs={{3,2},{7,6},{11,10},{15,14},{19,18},{23,22},{27,26},{31,30}} | collective-permute-start | bytes 393224 | tf_op jit(solution)/shard_map/ppermute | solution.py:484
  16.1 6.8 %collective-permute-start.12 = (bf16[32,2048]{1,0:T(8,128)(2,1)S(1)}, bf16[32,2048]{1,0:T(8,128)(2,1)S(1)}, u32[]{:S(2)}, u32[]{:S(2)}) collective-permute-start(bf16[32,2048]{1,0:T(8,128)(2,1)S(1)} %get-tuple-element.86.refs_5_.refs_7_), channel_id=1, source_target_pairs={{3,2},{7,6},{11,10},{15,14},{19,18},{23,22},{27,26},{31,30}} | collective-permute-start | bytes 393224 | tf_op jit(solution)/shard_map/ppermute | solution.py:484
  19.1 4.5 %collective-permute-start.10 = (bf16[32,2048]{1,0:T(8,128)(2,1)S(1)}, bf16[32,2048]{1,0:T(8,128)(2,1)S(1)}, u32[]{:S(2)}, u32[]{:S(2)}) collective-permute-start(bf16[32,2048]{1,0:T(8,128)(2,1)S(1)} %get-tuple-element.94.refs_7_.refs_6_), channel_id=1, source_target_pairs={{3,2},{7,6},{11,10},{15,14},{19,18},{23,22},{27,26},{31,30}} | collective-permute-start | bytes 393224 | tf_op jit(solution)/shard_map/ppermute | solution.py:484
  19.8 4.5 %collective-permute-start.18 = (bf16[32,2048]{1,0:T(8,128)(2,1)S(1)}, bf16[32,2048]{1,0:T(8,128)(2,1)S(1)}, u32[]{:S(2)}, u32[]{:S(2)}) collective-permute-start(bf16[32,2048]{1,0:T(8,128)(2,1)S(1)} %get-tuple-element.103.refs_7_), channel_id=1, source_target_pairs={{3,2},{7,6},{11,10},{15,14},{19,18},{23,22},{27,26},{31,30}} | collective-permute-start | bytes 393224 | tf_op jit(solution)/shard_map/ppermute | solution.py:484
  20.6 4.5 %collective-permute-start.14 = (bf16[32,2048]{1,0:T(8,128)(2,1)S(1)}, bf16[32,2048]{1,0:T(8,128)(2,1)S(1)}, u32[]{:S(2)}, u32[]{:S(2)}) collective-permute-start(bf16[32,2048]{1,0:T(8,128)(2,1)S(1)} %get-tuple-element.95.refs_7_.refs_8_), channel_id=1, source_target_pairs={{2,1},{6,5},{10,9},{14,13},{18,17},{22,21},{26,25},{30,29}} | collective-permute-start | bytes 393224 | tf_op jit(solution)/shard_map/ppermute | solution.py:484
  21.3 5.6 %collective-permute-start.7 = (bf16[128,512]{1,0:T(8,128)(2,1)S(1)}, bf16[128,512]{1,0:T(8,128)(2,1)S(1)}, u32[]{:S(2)}, u32[]{:S(2)}) collective-permute-start(bf16[128,512]{1,0:T(8,128)(2,1)S(1)} %get-tuple-element.89), channel_id=1, source_target_pairs={{0,8},{4,12},{8,0},{12,4},{16,24},{20,28},{24,16},{28,20},{1,9},{5... | collective-permute-start | bytes 393224 | tf_op jit(solution)/shard_map/ppermute | solution.py:450
  22.9 6.6 %collective-permute-start.15 = (bf16[32,2048]{1,0:T(8,128)(2,1)S(1)}, bf16[32,2048]{1,0:T(8,128)(2,1)S(1)}, u32[]{:S(2)}, u32[]{:S(2)}) collective-permute-start(bf16[32,2048]{1,0:T(8,128)(2,1)S(1)} %get-tuple-element.96.refs_6_.refs_9_), channel_id=1, source_target_pairs={{2,1},{6,5},{10,9},{14,13},{18,17},{22,21},{26,25},{30,29}} | collective-permute-start | bytes 393224 | tf_op jit(solution)/shard_map/ppermute | solution.py:484
  23.6 7.2 %collective-permute-start.13 = (bf16[32,2048]{1,0:T(8,128)(2,1)S(1)}, bf16[32,2048]{1,0:T(8,128)(2,1)S(1)}, u32[]{:S(2)}, u32[]{:S(2)}) collective-permute-start(bf16[32,2048]{1,0:T(8,128)(2,1)S(1)} %get-tuple-element.97.refs_7_.refs_8_), channel_id=1, source_target_pairs={{2,1},{6,5},{10,9},{14,13},{18,17},{22,21},{26,25},{30,29}} | collective-permute-start | bytes 393224 | tf_op jit(solution)/shard_map/ppermute | solution.py:484
  24.3 7.9 %collective-permute-start.19 = (bf16[32,2048]{1,0:T(8,128)(2,1)S(1)}, bf16[32,2048]{1,0:T(8,128)(2,1)S(1)}, u32[]{:S(2)}, u32[]{:S(2)}) collective-permute-start(bf16[32,2048]{1,0:T(8,128)(2,1)S(1)} %get-tuple-element.104.refs_9_), channel_id=1, source_target_pairs={{2,1},{6,5},{10,9},{14,13},{18,17},{22,21},{26,25},{30,29}} | collective-permute-start | bytes 393224 | tf_op jit(solution)/shard_map/ppermute | solution.py:484
  25.0 8.5 %collective-permute-start.8 = (bf16[128,512]{1,0:T(8,128)(2,1)S(1)}, bf16[128,512]{1,0:T(8,128)(2,1)S(1)}, u32[]{:S(2)}, u32[]{:S(2)}) collective-permute-start(bf16[128,512]{1,0:T(8,128)(2,1)S(1)} %get-tuple-element.90), channel_id=1, source_target_pairs={{0,16},{4,20},{8,24},{12,28},{16,0},{20,4},{24,8},{28,12},{1,17},{... | collective-permute-start | bytes 393224 | tf_op jit(solution)/shard_map/ppermute | solution.py:450
  26.9 8.0 %collective-permute-start.9 = (bf16[128,512]{1,0:T(8,128)(2,1)S(1)}, bf16[128,512]{1,0:T(8,128)(2,1)S(1)}, u32[]{:S(2)}, u32[]{:S(2)}) collective-permute-start(bf16[128,512]{1,0:T(8,128)(2,1)S(1)} %get-tuple-element.91), channel_id=1, source_target_pairs={{0,24},{4,28},{8,16},{12,20},{16,8},{20,12},{24,0},{28,4},{1,25},{... | collective-permute-start | bytes 393224 | tf_op jit(solution)/shard_map/ppermute | solution.py:450
  29.6 10.4 %collective-permute-start.21 = (bf16[32,2048]{1,0:T(8,128)(2,1)S(1)}, bf16[32,2048]{1,0:T(8,128)(2,1)S(1)}, u32[]{:S(2)}, u32[]{:S(2)}) collective-permute-start(bf16[32,2048]{1,0:T(8,128)(2,1)S(1)} %get-tuple-element.98.refs_7_.refs_10_), channel_id=1, source_target_pairs={{1,0},{5,4},{9,8},{13,12},{17,16},{21,20},{25,24},{29,28}} | collective-permute-start | bytes 393224 | tf_op jit(solution)/shard_map/ppermute | solution.py:484
  30.9 11.7 %collective-permute-start.22 = (bf16[32,2048]{1,0:T(8,128)(2,1)S(1)}, bf16[32,2048]{1,0:T(8,128)(2,1)S(1)}, u32[]{:S(2)}, u32[]{:S(2)}) collective-permute-start(bf16[32,2048]{1,0:T(8,128)(2,1)S(1)} %get-tuple-element.99.refs_6_.refs_11_), channel_id=1, source_target_pairs={{1,0},{5,4},{9,8},{13,12},{17,16},{21,20},{25,24},{29,28}} | collective-permute-start | bytes 393224 | tf_op jit(solution)/shard_map/ppermute | solution.py:484
  32.2 13.7 %collective-permute-start.16 = (bf16[32,2048]{1,0:T(8,128)(2,1)S(1)}, bf16[32,2048]{1,0:T(8,128)(2,1)S(1)}, u32[]{:S(2)}, u32[]{:S(2)}) collective-permute-start(bf16[32,2048]{1,0:T(8,128)(2,1)S(1)} %get-tuple-element.100.refs_7_.refs_10_), channel_id=1, source_target_pairs={{1,0},{5,4},{9,8},{13,12},{17,16},{21,20},{25,24},{29,28}} | collective-permute-start | bytes 393224 | tf_op jit(solution)/shard_map/ppermute | solution.py:484
  33.6 14.4 %collective-permute-start.20 = (bf16[32,2048]{1,0:T(8,128)(2,1)S(1)}, bf16[32,2048]{1,0:T(8,128)(2,1)S(1)}, u32[]{:S(2)}, u32[]{:S(2)}) collective-permute-start(bf16[32,2048]{1,0:T(8,128)(2,1)S(1)} %get-tuple-element.105.refs_11_), channel_id=1, source_target_pairs={{1,0},{5,4},{9,8},{13,12},{17,16},{21,20},{25,24},{29,28}} | collective-permute-start | bytes 393224 | tf_op jit(solution)/shard_map/ppermute | solution.py:484
  43.4 4.5 %collective-permute-start.23 = (bf16[16,2048]{1,0:T(8,128)(2,1)S(1)}, bf16[16,2048]{1,0:T(8,128)(2,1)S(1)}, u32[]{:S(2)}, u32[]{:S(2)}) collective-permute-start(bf16[16,2048]{1,0:T(8,128)(2,1)S(1)} %get-tuple-element.123), channel_id=1, source_target_pairs={{0,4},{4,0},{8,12},{12,8},{16,20},{20,16},{24,28},{28,24},{1,5},{5... | collective-permute-start | bytes 196616 | tf_op jit(solution)/shard_map/ppermute | solution.py:450
  43.5 5.0 %collective-permute-start.24 = (bf16[16,2048]{1,0:T(8,128)(2,1)S(1)}, bf16[16,2048]{1,0:T(8,128)(2,1)S(1)}, u32[]{:S(2)}, u32[]{:S(2)}) collective-permute-start(bf16[16,2048]{1,0:T(8,128)(2,1)S(1)} %get-tuple-element.124), channel_id=1, source_target_pairs={{0,8},{4,12},{8,0},{12,4},{16,24},{20,28},{24,16},{28,20},{1,9},{5... | collective-permute-start | bytes 196616 | tf_op jit(solution)/shard_map/ppermute | solution.py:450
  43.6 5.4 %collective-permute-start.25 = (bf16[16,2048]{1,0:T(8,128)(2,1)S(1)}, bf16[16,2048]{1,0:T(8,128)(2,1)S(1)}, u32[]{:S(2)}, u32[]{:S(2)}) collective-permute-start(bf16[16,2048]{1,0:T(8,128)(2,1)S(1)} %get-tuple-element.125), channel_id=1, source_target_pairs={{0,12},{4,8},{8,4},{12,0},{16,28},{20,24},{24,20},{28,16},{1,13},{... | collective-permute-start | bytes 196616 | tf_op jit(solution)/shard_map/ppermute | solution.py:450
  49.8 11.3 %collective-permute-start.26 = (bf16[48,2048]{1,0:T(8,128)(2,1)S(1)}, bf16[48,2048]{1,0:T(8,128)(2,1)S(1)}, u32[]{:S(2)}, u32[]{:S(2)}) collective-permute-start(bf16[48,2048]{1,0:T(8,128)(2,1)S(1)} %get-tuple-element.127), channel_id=1, source_target_pairs={{0,8},{4,12},{8,0},{12,4},{16,24},{20,28},{24,16},{28,20},{1,9},{5... | collective-permute-start | bytes 589832 | tf_op jit(solution)/shard_map/ppermute | solution.py:450
  50.6 10.0 %collective-permute-start.27 = (bf16[128,512]{1,0:T(8,128)(2,1)S(1)}, bf16[128,512]{1,0:T(8,128)(2,1)S(1)}, u32[]{:S(2)}, u32[]{:S(2)}) collective-permute-start(bf16[128,512]{1,0:T(8,128)(2,1)S(1)} %get-tuple-element.126.refs_4_), channel_id=1, source_target_pairs={{0,16},{4,20},{8,24},{12,28},{16,0},{20,4},{24,8},{28,12},{1,17},{... | collective-permute-start | bytes 393224 | tf_op jit(solution)/shard_map/ppermute | solution.py:450
  52.1 9.0 %collective-permute-start.28 = (bf16[128,512]{1,0:T(8,128)(2,1)S(1)}, bf16[128,512]{1,0:T(8,128)(2,1)S(1)}, u32[]{:S(2)}, u32[]{:S(2)}) collective-permute-start(bf16[128,512]{1,0:T(8,128)(2,1)S(1)} %get-tuple-element.126.refs_4_), channel_id=1, source_target_pairs={{0,24},{4,28},{8,16},{12,20},{16,8},{20,12},{24,0},{28,4},{1,25},{... | collective-permute-start | bytes 393224 | tf_op jit(solution)/shard_map/ppermute | solution.py:450
  53.4 1.3 %collective-permute-start.29 = (bf16[16,2048]{1,0:T(8,128)(2,1)S(1)}, bf16[16,2048]{1,0:T(8,128)(2,1)S(1)}, u32[]{:S(2)}, u32[]{:S(2)}) collective-permute-start(bf16[16,2048]{1,0:T(8,128)(2,1)S(1)} %get-tuple-element.128), channel_id=1, source_target_pairs={{0,4},{4,0},{8,12},{12,8},{16,20},{20,16},{24,28},{28,24},{1,5},{5... | collective-permute-start | bytes 196616 | tf_op jit(solution)/shard_map/ppermute | solution.py:450
  53.4 7.2 %collective-permute-start.30 = (bf16[16,2048]{1,0:T(8,128)(2,1)S(1)}, bf16[16,2048]{1,0:T(8,128)(2,1)S(1)}, u32[]{:S(2)}, u32[]{:S(2)}) collective-permute-start(bf16[16,2048]{1,0:T(8,128)(2,1)S(1)} %get-tuple-element.129), channel_id=1, source_target_pairs={{0,12},{4,8},{8,4},{12,0},{16,28},{20,24},{24,20},{28,16},{1,13},{... | collective-permute-start | bytes 196616 | tf_op jit(solution)/shard_map/ppermute | solution.py:450
  61.6 2.0 %collective-permute-start.31 = (f32[256,512]{1,0:T(8,128)S(1)}, f32[256,512]{1,0:T(8,128)S(1)}, u32[]{:S(2)}, u32[]{:S(2)}) collective-permute-start(f32[256,512]{1,0:T(8,128)S(1)} %get-tuple-element.131), channel_id=1, source_target_pairs={{0,4},{4,0},{8,12},{12,8},{16,20},{20,16},{24,28},{28,24},{1,5},{5... | collective-permute-start | bytes 1572872 | tf_op jit(solution)/shard_map/ppermute | solution.py:450
  (2 other events, 8.6 us)

commit v6 on v5

--- a/solution.py
+++ b/solution.py
@@ -101,19 +101,22 @@
     heads = model_width // kv_width
     key_heads = kv_width // HEAD_FEATURES
     operands = [near(piece) for piece in pieces] + [near(seg)]
-    specs = [VMEM] * len(operands) + [ANY] * len(after)
+    specs = [VMEM] * len(operands)
+    outs = [
+        jax.ShapeDtypeStruct((key_heads, UNIT, heads * UNIT), jnp.bfloat16),
+        jax.ShapeDtypeStruct((key_heads, UNIT, heads * BLOCK), jnp.bfloat16),
+        jax.ShapeDtypeStruct((BLOCK, 128), jnp.float32),
+        jax.ShapeDtypeStruct((BLOCK, model_width), jnp.bfloat16),
+    ]
+    scratch = [pltpu.VMEM((BLOCK, 2 * model_width + kv_width), jnp.bfloat16)]
     operands += after
+    specs += [ANY] * len(after)
     return pl.pallas_call(
         functools.partial(probs_kernel, len(pieces), seg_row, model_width, kv_width),
-        out_shape=(
-            jax.ShapeDtypeStruct((key_heads, UNIT, heads * UNIT), jnp.bfloat16),
-            jax.ShapeDtypeStruct((key_heads, UNIT, heads * BLOCK), jnp.bfloat16),
-            jax.ShapeDtypeStruct((BLOCK, 128), jnp.float32),
-            jax.ShapeDtypeStruct((BLOCK, model_width), jnp.bfloat16),
-        ),
+        out_shape=tuple(outs),
         in_specs=specs,
-        out_specs=(VMEM,) * 4,
-        scratch_shapes=[pltpu.VMEM((BLOCK, 2 * model_width + kv_width), jnp.bfloat16)],
+        out_specs=(VMEM,) * len(outs),
+        scratch_shapes=scratch,
         name="probs",
         **params(0.35),
     )(*operands)
@@ -220,7 +223,7 @@
     )(*operands)
 
 
-def tick_kernel(tick, rows, parts, kept, final, *refs):
+def tick_kernel(tick, rows, parts, kept, final, send, *refs):
     grads = list(zip(refs, parts))
     probs_ref, inv_ref, x_ref, turned_ref, gain_ref = refs[len(parts) : len(parts) + 5]
     refs = refs[len(parts) + 5 :]
@@ -236,6 +239,12 @@
             block_ref[EARLY, columns] = part
 
     else:
+        if send:
+            up_ref, across_ref, sem = refs[0], refs[-3], refs[-1]
+            refs = refs[:-3] + refs[-2:-1]
+            first = pl.multiple_of((1 - place()[0]) * BLOCK, BLOCK)
+            made = pltpu.make_async_copy(up_ref.at[pl.ds(first, UNIT)], across_ref, sem)
+            made.start()
         out_ref, value_ref, scaled_ref = refs[-3:]
 
         def store(columns, part):
@@ -248,6 +257,8 @@
             value_ref,
         )
 
+    if send:
+        made.wait()
     for at in range(kept):
 
         @pl.when(turn == at)
@@ -277,7 +288,7 @@
             values_ref[...] = jnp.concatenate(values, axis=0)
 
 
-def tick_step(tick, grads, block, turned, gain, kept=(), late=(), after=()):
+def tick_step(tick, grads, block, turned, gain, kept=(), late=(), after=(), up=None):
     kv_width, model_width = turned.shape
     low = len(grads) == 2
     final = len(late) - 1 if late else 0
@@ -286,7 +297,11 @@
     arrays += [array for pair in kept for array in pair]
     arrays += late
     operands = [near(array) for array in arrays]
-    specs = [VMEM] * len(operands) + [ANY] * len(after)
+    specs = [VMEM] * len(operands)
+    if up is not None:
+        operands.append(pltpu.with_memory_space_constraint(up, pltpu.HBM))
+        specs.append(pl.BlockSpec(memory_space=pltpu.HBM))
+    specs += [ANY] * len(after)
     bf16 = jnp.bfloat16
     scratch = [pltpu.VMEM((UNIT, model_width), jnp.float32)]
     if final:
@@ -303,9 +318,13 @@
             jax.ShapeDtypeStruct((UNIT, model_width), bf16),
             jax.ShapeDtypeStruct((UNIT, kv_width), bf16),
         )
+        if up is not None:
+            outs += (jax.ShapeDtypeStruct((UNIT, model_width), bf16),)
+            scratch.append(pltpu.SemaphoreType.DMA)
+    parts = [part for _, part in grads]
     return pl.pallas_call(
         functools.partial(
-            tick_kernel, tick, EARLY if low else LATE, [part for _, part in grads], len(kept), final
+            tick_kernel, tick, EARLY if low else LATE, parts, len(kept), final, up is not None
         ),
         out_shape=outs,
         in_specs=specs,
@@ -317,8 +336,9 @@
 
 
 def pack_kernel(block, half, piece, query_ref, key_ref, hidden_ref, up_ref, seg_ref, *rest):
-    late_ref, early_ref, seg_in_ref, sems = rest[-4:]
-    packed = rest[-4 - half : -4]
+    late_ref, *early, seg_in_ref, sems = rest[-4 + block :]
+    packed = rest[-4 + block - half : -4 + block]
+    rest = rest[: -4 + block - half]
     side, at, _ = place()
     there = side if block == 0 else 1 - side
     copies = []
@@ -337,47 +357,64 @@
             width = source.shape[1]
             copy(source.at[rows], packed[k].at[:, pl.ds(first, width)])
             first += width
-    for first, target in ((0, early_ref), (UNIT, late_ref.at[pl.ds(0, UNIT)])):
-        copy(up_ref.at[pl.ds(pl.multiple_of(there * BLOCK + first, UNIT), UNIT)], target)
+    for first, target in [(UNIT, late_ref)] + [(0, ref) for ref in early]:
+        rows = pl.ds(pl.multiple_of(there * BLOCK + first, UNIT), UNIT)
+        copy(up_ref.at[rows], target.at[pl.ds(0, UNIT)])
     late_ref[UNIT:, :] = jnp.zeros((16, late_ref.shape[1]), jnp.bfloat16)
     copies[0].wait()
     ids = seg_in_ref[...].astype(jnp.float32)
     late_ref[UNIT:, : ids.shape[1]] = jnp.broadcast_to(ids, (16, ids.shape[1])).astype(
         jnp.bfloat16
     )
+    if rest:
+        turn_kernel(rest[0], rest[-1])
     for made in copies[1:]:
         made.wait()
 
 
-def pack(block, half, piece, sources):
+def pack(block, half, piece, sources, weight=None):
     model_width = sources[0].shape[1]
     width = sum(source.shape[1] for source in sources[:3])
     bf16 = jnp.bfloat16
     operands = [pltpu.with_memory_space_constraint(array, pltpu.HBM) for array in sources]
+    specs = [pl.BlockSpec(memory_space=pltpu.HBM)] * len(sources)
+    outs = [jax.ShapeDtypeStruct((piece, width), bf16)] * half
+    outs += [
+        jax.ShapeDtypeStruct((rows, model_width), bf16) for rows in (UNIT + 16, UNIT)[: 2 - block]
+    ]
+    if weight is not None:
+        operands.append(near(weight))
+        specs.append(VMEM)
+        outs = [jax.ShapeDtypeStruct(weight.shape[::-1], bf16)] + outs
     return pl.pallas_call(
         functools.partial(pack_kernel, block, half, piece),
-        out_shape=(jax.ShapeDtypeStruct((piece, width), bf16),) * half
-        + (
-            jax.ShapeDtypeStruct((UNIT + 16, model_width), bf16),
-            jax.ShapeDtypeStruct((UNIT, model_width), bf16),
-        ),
-        in_specs=[pl.BlockSpec(memory_space=pltpu.HBM)] * len(sources),
-        out_specs=(VMEM,) * (half + 2),
+        out_shape=tuple(outs),
+        in_specs=specs,
+        out_specs=(VMEM,) * len(outs),
         scratch_shapes=[
             pltpu.VMEM(sources[-1].shape, jnp.int32),
-            pltpu.SemaphoreType.DMA((3 * half + 3,)),
+            pltpu.SemaphoreType.DMA((3 * half + 3 - block,)),
         ],
         name="pack",
         **params(1.2),
     )(*operands)
 
 
-def columns_kernel(width, first_ref, second_ref, *outs):
-    pair = lax.div(place()[2], 2)
+def columns_kernel(
+    width, scale, first_ref, second_ref, weight_ref, gain_ref, after_ref, weight_out_ref,
+    gain_out_ref, *outs
+):
+    me = place()[2]
     for k, out_ref in enumerate(outs):
-        start = pl.multiple_of(lax.bitwise_xor(pair, k) * width, width)
+        start = pl.multiple_of(lax.bitwise_xor(lax.div(me, 2), k) * width, width)
         out_ref[:BLOCK, :] = first_ref[:, pl.ds(start, width)]
         out_ref[BLOCK:, :] = second_ref[:, pl.ds(start, width)]
+    shares = weight_out_ref.shape[0]
+    first = pl.multiple_of(me * shares, shares)
+    weight_out_ref[...] = weight_ref[pl.ds(first, shares), :].astype(jnp.float32) * scale
+    gain = gain_ref[:, pl.ds(first, shares)]
+    column = jnp.sum(jnp.where(diagonal(shares), gain, 0.0), axis=1, keepdims=True)
+    gain_out_ref[...] = jnp.broadcast_to(column * scale, gain_out_ref.shape)
 
 
 def partial_kernel(count, shares, piece, *refs):
@@ -399,15 +436,13 @@
         rows = jnp.concatenate([part[:, at] for part in columns], axis=0)
         ref[...] = lax.dot_general(
             rows, value, (((0,), (0,)), ((), ())), preferred_element_type=jnp.float32
-        )
-
-
-def finish_kernel(
-    half, scale, own_ref, other_ref, weight_ref, gain_ref, *refs
-):
+        ).astype(ref.dtype)
+
+
+def rows_kernel(half, *refs):
     pieces = refs[: 2 * half]
-    rows_ref, out_ref, gain_out_ref, sems = refs[2 * half :]
-    side, at, me = place()
+    rows_ref, sems = refs[-2:]
+    side, at, _ = place()
     piece = pieces[0].shape[0]
     copies = []
     for block in range(2):
@@ -418,23 +453,23 @@
             made = pltpu.make_async_copy(source, rows_ref.at[rows], sems.at[block * half + k])
             made.start()
             copies.append(made)
-    shares = own_ref.shape[0]
-    first = pl.multiple_of(me * shares, shares)
-    gain = gain_ref[:, pl.ds(first, shares)]
-    eye = lax.broadcasted_iota(jnp.int32, (shares, shares), 0) == lax.broadcasted_iota(
-        jnp.int32, (shares, shares), 1
-    )
-    gain_column = jnp.sum(jnp.where(eye, gain, 0.0), axis=1, keepdims=True)
-    total = (own_ref[...] + other_ref[...]) * scale
-    out_ref[...] = total * gain_column
-    product = total * weight_ref[pl.ds(first, shares), :].astype(jnp.float32)
-    sums = lax.dot_general(
-        jnp.ones((8, product.shape[1]), jnp.float32), product, (((1,), (1,)), ((), ())),
-        preferred_element_type=jnp.float32, precision=lax.Precision.HIGHEST,
-    )
-    gain_out_ref[...] = sums[:1]
     for made in copies:
         made.wait()
+
+
+def diagonal(size):
+    return lax.broadcasted_iota(jnp.int32, (size, size), 0) == lax.broadcasted_iota(
+        jnp.int32, (size, size), 1
+    )
+
+
+def finish_kernel(own_ref, other_ref, weight_ref, gain_ref, rows_ref, out_ref, gain_out_ref):
+    total = own_ref[...] + other_ref[...].astype(jnp.float32)
+    out_ref[...] = total * gain_ref[:, :1]
+    sums = jnp.sum(total * weight_ref[...], axis=1, keepdims=True)
+    gain_out_ref[...] = jnp.sum(
+        jnp.where(diagonal(total.shape[0]), sums, 0.0), axis=0, keepdims=True
+    )
 
 
 def direct(hidden, query, key, segments, weight, norm_gain, upstream):
@@ -454,41 +489,54 @@
     sources = (query, key, hidden, upstream, segments)
     pieces, ups = [], []
     for b in range(2):
-        *packed, late, early = pack(b, half, piece, sources)
+        if b:
+            turned, *packed, late = pack(b, half, piece, sources, weight)
+        else:
+            *packed, late, early = pack(b, half, piece, sources)
         pieces.append([packed[0]] + [swap(packed[k], k) for k in range(1, half)])
-        ups.append([swap(part, half) for part in (late, early)] if b else [late, early])
+        ups.append([swap(late, half)] if b else [late, early])
     whole = slice(0, UNIT)
-    turned = turn(weight)
-    blocks, kept, after = [], [], [turned]
+    scale = float(tokens * replicas) ** (-0.5)
+    blocks, kept, after = [], [], []
     for b in range(2):
         block = block_probs(pieces[b], ups[b][0], UNIT, model_width, kv_width, after)
         late, early = [(part, whole) for part in ups[b]]
         first = tick_step(0, [late], block, turned, norm_gain)
-        second = tick_step(0, [late, early], block, turned, norm_gain, after=[first[0]])
+        up = None if b else upstream
+        second = tick_step(0, [late, early], block, turned, norm_gain, after=[first[0]], up=up)
+        if b == 0:
+            *second, rows = second
+            ups[1].append(swap(rows, half))
         blocks.append(block)
         kept += [[first], [second]]
         after = [second[0]]
-
-    columns = pl.pallas_call(
-        functools.partial(columns_kernel, 2 * shares),
-        out_shape=(jax.ShapeDtypeStruct((2 * BLOCK, 2 * shares), bf16),) * half,
-        in_specs=[VMEM, VMEM],
-        out_specs=(VMEM,) * half,
-        name="columns",
-        **params(0.4),
-    )(blocks[0][3], blocks[1][3])
-    columns = [columns[0]] + [swap(columns[k], 2 * k) for k in range(1, half)]
 
     for tick in range(1, layers):
         hop = [(layers - tick, layers - 1 - tick)]
         grads = [(lax.ppermute(unit[-1][0], "section", hop), whole) for unit in kept]
         last = tick == layers - 1
-        after, done = (columns if last else []), []
+        after, done = [], []
+        if last:
+            own_weight, own_gain, *columns = pl.pallas_call(
+                functools.partial(columns_kernel, 2 * shares, scale),
+                out_shape=(
+                    jax.ShapeDtypeStruct((shares, kv_width), jnp.float32),
+                    jax.ShapeDtypeStruct((shares, 128), jnp.float32),
+                )
+                + (jax.ShapeDtypeStruct((2 * BLOCK, 2 * shares), bf16),) * half,
+                in_specs=[VMEM] * 4 + [ANY],
+                out_specs=(VMEM,) * (2 + half),
+                name="columns",
+                **params(0.4),
+            )(blocks[0][3], blocks[1][3], near(weight), norm_gain, kept[3][-1][0])
+            columns = [columns[0]] + [swap(columns[k], 2 * k) for k in range(1, half)]
         for u in range(4):
             needs = grads[u - 1 : u + 1] if u % 2 else grads[u : u + 1]
             late = []
             if last and u % 2:
                 late = list(done[u - 1]) + ([done[1][0]] if u == 3 else [])
+            if last and u == 1:
+                after = after + columns[1:]
             if last and u == 3:
                 rows = [done[1][1]] + [swap(done[1][1 + k], k) for k in range(1, half)]
                 after = after + rows[1:]
@@ -505,27 +553,36 @@
     gathered = [values, last_rows[2]] + [swap(values, 2 * k) for k in range(2, half)]
     own, other = pl.pallas_call(
         functools.partial(partial_kernel, half, shares, piece),
-        out_shape=(jax.ShapeDtypeStruct((shares, kv_width), jnp.float32),) * 2,
+        out_shape=(
+            jax.ShapeDtypeStruct((shares, kv_width), jnp.float32),
+            jax.ShapeDtypeStruct((shares, kv_width), bf16),
+        ),
         in_specs=[VMEM] * (2 * half) + [ANY] * 2,
         out_specs=(VMEM, VMEM),
         name="weight_partial",
         **params(0.5),
     )(*columns, *gathered, last_rows[1], last_rows[3])
     other = swap(other, 1)
-    scale = float(tokens * replicas) ** (-0.5)
-    input_grad, weight_grad, gain_grad = pl.pallas_call(
-        functools.partial(finish_kernel, half, scale),
+    input_grad = pl.pallas_call(
+        functools.partial(rows_kernel, half),
+        out_shape=jax.ShapeDtypeStruct((tokens, model_width), bf16),
+        in_specs=[VMEM] * count + [ANY],
+        out_specs=ANY,
+        scratch_shapes=[pltpu.SemaphoreType.DMA((count,))],
+        name="rows",
+        **params(1.2),
+    )(*rows, *last_rows, own)
+    weight_grad, gain_grad = pl.pallas_call(
+        finish_kernel,
         out_shape=(
-            jax.ShapeDtypeStruct((tokens, model_width), bf16),
             jax.ShapeDtypeStruct((shares, kv_width), jnp.float32),
             jax.ShapeDtypeStruct((1, shares), jnp.float32),
         ),
-        in_specs=[VMEM] * (4 + count),
-        out_specs=(ANY, VMEM, VMEM),
-        scratch_shapes=[pltpu.SemaphoreType.DMA((count,))],
+        in_specs=[VMEM] * 4 + [ANY],
+        out_specs=(VMEM, VMEM),
         name="finish",
-        **params(2.0),
-    )(own, other, weight, norm_gain, *rows, *last_rows)
+        **params(1.0),
+    )(own, other, own_weight, own_gain, input_grad)
     return input_grad[None], weight_grad[None], gain_grad
 
 

time: 65.9 us -> 69.2 us (1.050)
  the two profiles are of different devices: /device:TPU:0 before, /device:TPU:9 now
where the time goes in v6:
time: 69.2 us; the launch traced here: 68.9 us
  starting transfers between devices  33.5 us (48%)
  waiting for transfers between devices  22.9 us (33%)
  Pallas kernels  10.4 us (15%)
  local copies, waits for them, and re-layouts  1.05 us (2%)
  between operations  1.01 us (1%)
    ppermute x20, starting transfers between devices, swap(): return lax.ppermute(array, 'dp', [(i, i ^ k) for i in range(replicas)])  20.5 us
    ppermute x20, waiting for transfers between devices, swap(): return lax.ppermute(array, 'dp', [(i, i ^ k) for i in range(replicas)])  16 us
    ppermute x12, starting transfers between devices, direct(): lax.ppermute(unit[-1][0], 'section', hop)  13 us
    ppermute x12, waiting for transfers between devices, direct(): lax.ppermute(unit[-1][0], 'section', hop)  6.95 us
    pallas_call x16, Pallas kernels, tick_step(): pl.pallas_call(functools.partial(tick_kernel, tick, EARLY if low else LAT...  4.29 us
    pallas_call x2, Pallas kernels, pack(): pl.pallas_call(functools.partial(pack_kernel, block, half, piece), out_sh...  2.98 us
  transfers between devices with their start and end apart: 32, of which 12 were waited for; matrix products, arithmetic and copies ran while one was open for 0% of the time, Pallas kernels for 11%

profile of v6, /device:TPU:9, one launch (start us, length us, event | category | flops | bytes accessed | tf_op | source)
XLA Modules:
  0.0 68.9 jit_solution(9277887221073855854)
XLA Ops:
  0.6 1.5 %pack.2 = (bf16[16,4608]{1,0:T(8,128)(2,1)S(1)}, bf16[16,4608]{1,0:T(8,128)(2,1)S(1)}, bf16[16,4608]{1,0:T(8,128)(2,1)S(1)}, bf16[16,4608]{1,0:T(8,128)(2,1)S(1)...) custom-call(bf16[128,2048]{1,0:T(8,128)(2,1)} %bitcast.9, bf16[128,512]{1,0:T(8,128)(2,1)} %bitcast.13, ...), custom_call_target="tpu_custom_call" | custom-call | flops 1380000000 | tf_op jit(solution)/shard_map/pack/pallas_call | solution.py:389
  2.9 1.2 %collective-permute-start.1 = (bf16[16,4608]{1,0:T(8,128)(2,1)S(1)}, bf16[16,4608]{1,0:T(8,128)(2,1)S(1)}, u32[]{:S(2)}, u32[]{:S(2)}) collective-permute-start(bf16[16,4608]{1,0:T(8,128)(2,1)S(1)} %get-tuple-element.75), channel_id=1, source_target_pairs={{0,8},{4,12},{8,0},{12,4},{16,24},{20,28},{24,16},{28,20},{1,9},{5... | collective-permute-start | bytes 442376 | tf_op jit(solution)/shard_map/ppermute | solution.py:485
  4.6 1.5 %pack.3 = (bf16[512,2048]{1,0:T(8,128)(2,1)S(1)}, bf16[16,4608]{1,0:T(8,128)(2,1)S(1)}, bf16[16,4608]{1,0:T(8,128)(2,1)S(1)}, bf16[16,4608]{1,0:T(8,128)(2,1)S(1...) custom-call(bf16[128,2048]{1,0:T(8,128)(2,1)} %bitcast.10, bf16[128,512]{1,0:T(8,128)(2,1)} %bitcast.14, ...), custom_call_target="tpu_custom_call" | custom-call | flops 1380000000 | tf_op jit(solution)/shard_map/pack/pallas_call | solution.py:389
  6.1 1.3 %collective-permute-start.12 = (bf16[48,2048]{1,0:T(8,128)(2,1)S(1)}, bf16[48,2048]{1,0:T(8,128)(2,1)S(1)}, u32[]{:S(2)}, u32[]{:S(2)}) collective-permute-start(bf16[48,2048]{1,0:T(8,128)(2,1)S(1)} %get-tuple-element.101), channel_id=1, source_target_pairs={{0,16},{4,20},{8,24},{12,28},{16,0},{20,4},{24,8},{28,12},{1,17},{... | collective-permute-start | bytes 589832 | tf_op jit(solution)/shard_map/ppermute | solution.py:485
  7.8 1.2 %collective-permute-start.10 = (bf16[16,4608]{1,0:T(8,128)(2,1)S(1)}, bf16[16,4608]{1,0:T(8,128)(2,1)S(1)}, u32[]{:S(2)}, u32[]{:S(2)}) collective-permute-start(bf16[16,4608]{1,0:T(8,128)(2,1)S(1)} %get-tuple-element.99), channel_id=1, source_target_pairs={{0,8},{4,12},{8,0},{12,4},{16,24},{20,28},{24,16},{28,20},{1,9},{5... | collective-permute-start | bytes 442376 | tf_op jit(solution)/shard_map/ppermute | solution.py:485
  9.1 1.7 %collective-permute-start.11 = (bf16[16,4608]{1,0:T(8,128)(2,1)S(1)}, bf16[16,4608]{1,0:T(8,128)(2,1)S(1)}, u32[]{:S(2)}, u32[]{:S(2)}) collective-permute-start(bf16[16,4608]{1,0:T(8,128)(2,1)S(1)} %get-tuple-element.100), channel_id=1, source_target_pairs={{0,12},{4,8},{8,4},{12,0},{16,28},{20,24},{24,20},{28,16},{1,13},{... | collective-permute-start | bytes 442376 | tf_op jit(solution)/shard_map/ppermute | solution.py:485
  10.7 1.7 %collective-permute-done.2.refs_3_ = bf16[16,4608]{1,0:T(8,128)(2,1)S(1)} collective-permute-done((bf16[16,4608]{1,0:T(8,128)(2,1)S(1)}, bf16[16,4608]{1,0:T(8,128)(2,1)S(1)}, u32[]{:S(2)}, u32[]{:S(2)}) %collective-permute-start.2) | collective-permute-done | bytes 147488 | tf_op jit(solution)/shard_map/ppermute | solution.py:485
  12.8 0.9 %tick.19 = (bf16[32,2048]{1,0:T(8,128)(2,1)S(1)}, bf16[32,512]{1,0:T(8,128)(2,1)S(1)}, bf16[32,2048]{1,0:T(8,128)(2,1)S(1)}) custom-call(bf16[48,2048]{1,0:T(8,128)(2,1)S(1)} %get-tuple-element.72.refs_4_.refs_0_, bf16[32,2048]{1,0:T(8,128)(2,1)S(1)} %get-tuple-element.84.refs_1_, bf16[4,32,256]{2,1,0:T(8,128)(2,1)S(1)} %get-tuple-element.85.refs_2_, ...), custom_call_target="tpu_custom_call" | custom-call | flops 230000000 | tf_op jit(solution)/shard_map/tick/pallas_call | solution.py:325
  13.7 1.3 %collective-permute-start.15 = (bf16[32,2048]{1,0:T(8,128)(2,1)S(1)}, bf16[32,2048]{1,0:T(8,128)(2,1)S(1)}, u32[]{:S(2)}, u32[]{:S(2)}) collective-permute-start(bf16[32,2048]{1,0:T(8,128)(2,1)S(1)} %get-tuple-element.107), channel_id=1, source_target_pairs={{0,16},{4,20},{8,24},{12,28},{16,0},{20,4},{24,8},{28,12},{1,17},{... | collective-permute-start | bytes 393224 | tf_op jit(solution)/shard_map/ppermute | solution.py:485
  16.4 1.9 %collective-permute-done.11.refs_3_ = bf16[16,4608]{1,0:T(8,128)(2,1)S(1)} collective-permute-done((bf16[16,4608]{1,0:T(8,128)(2,1)S(1)}, bf16[16,4608]{1,0:T(8,128)(2,1)S(1)}, u32[]{:S(2)}, u32[]{:S(2)}) %collective-permute-start.11) | collective-permute-done | bytes 147488 | tf_op jit(solution)/shard_map/ppermute | solution.py:485
  20.1 1.3 %collective-permute-start.4 = (bf16[32,2048]{1,0:T(8,128)(2,1)S(1)}, bf16[32,2048]{1,0:T(8,128)(2,1)S(1)}, u32[]{:S(2)}, u32[]{:S(2)}) collective-permute-start(bf16[32,2048]{1,0:T(8,128)(2,1)S(1)} %get-tuple-element.82.refs_7_.refs_8_), channel_id=1, source_target_pairs={{2,1},{6,5},{10,9},{14,13},{18,17},{22,21},{26,25},{30,29}} | collective-permute-start | bytes 393224 | tf_op jit(solution)/shard_map/ppermute | solution.py:516
  21.4 1.3 %collective-permute-start.7 = (bf16[32,2048]{1,0:T(8,128)(2,1)S(1)}, bf16[32,2048]{1,0:T(8,128)(2,1)S(1)}, u32[]{:S(2)}, u32[]{:S(2)}) collective-permute-start(bf16[32,2048]{1,0:T(8,128)(2,1)S(1)} %get-tuple-element.87.refs_6_.refs_9_), channel_id=1, source_target_pairs={{2,1},{6,5},{10,9},{14,13},{18,17},{22,21},{26,25},{30,29}} | collective-permute-start | bytes 393224 | tf_op jit(solution)/shard_map/ppermute | solution.py:516
  22.7 1.3 %collective-permute-start.14 = (bf16[32,2048]{1,0:T(8,128)(2,1)S(1)}, bf16[32,2048]{1,0:T(8,128)(2,1)S(1)}, u32[]{:S(2)}, u32[]{:S(2)}) collective-permute-start(bf16[32,2048]{1,0:T(8,128)(2,1)S(1)} %get-tuple-element.106.refs_7_.refs_8_), channel_id=1, source_target_pairs={{2,1},{6,5},{10,9},{14,13},{18,17},{22,21},{26,25},{30,29}} | collective-permute-start | bytes 393224 | tf_op jit(solution)/shard_map/ppermute | solution.py:516
  24.1 1.3 %collective-permute-start.17 = (bf16[32,2048]{1,0:T(8,128)(2,1)S(1)}, bf16[32,2048]{1,0:T(8,128)(2,1)S(1)}, u32[]{:S(2)}, u32[]{:S(2)}) collective-permute-start(bf16[32,2048]{1,0:T(8,128)(2,1)S(1)} %get-tuple-element.110.refs_9_), channel_id=1, source_target_pairs={{2,1},{6,5},{10,9},{14,13},{18,17},{22,21},{26,25},{30,29}} | collective-permute-start | bytes 393224 | tf_op jit(solution)/shard_map/ppermute | solution.py:516
  25.4 3.2 %collective-permute-done.4.refs_0_ = bf16[32,2048]{1,0:T(8,128)(2,1)S(1)} collective-permute-done((bf16[32,2048]{1,0:T(8,128)(2,1)S(1)}, bf16[32,2048]{1,0:T(8,128)(2,1)S(1)}, u32[]{:S(2)}, u32[]{:S(2)}) %collective-permute-start.4) | collective-permute-done | bytes 131104 | tf_op jit(solution)/shard_map/ppermute | solution.py:516
  29.3 1.3 %collective-permute-start.5 = (bf16[32,2048]{1,0:T(8,128)(2,1)S(1)}, bf16[32,2048]{1,0:T(8,128)(2,1)S(1)}, u32[]{:S(2)}, u32[]{:S(2)}) collective-permute-start(bf16[32,2048]{1,0:T(8,128)(2,1)S(1)} %get-tuple-element.83.refs_7_.refs_10_), channel_id=1, source_target_pairs={{1,0},{5,4},{9,8},{13,12},{17,16},{21,20},{25,24},{29,28}} | collective-permute-start | bytes 393224 | tf_op jit(solution)/shard_map/ppermute | solution.py:516
  32.2 1.3 %collective-permute-start.8 = (bf16[32,2048]{1,0:T(8,128)(2,1)S(1)}, bf16[32,2048]{1,0:T(8,128)(2,1)S(1)}, u32[]{:S(2)}, u32[]{:S(2)}) collective-permute-start(bf16[32,2048]{1,0:T(8,128)(2,1)S(1)} %get-tuple-element.88.refs_6_.refs_11_), channel_id=1, source_target_pairs={{1,0},{5,4},{9,8},{13,12},{17,16},{21,20},{25,24},{29,28}} | collective-permute-start | bytes 393224 | tf_op jit(solution)/shard_map/ppermute | solution.py:516
  35.0 2.3 %collective-permute-done.17.refs_1_ = bf16[32,2048]{1,0:T(8,128)(2,1)S(1)} collective-permute-done((bf16[32,2048]{1,0:T(8,128)(2,1)S(1)}, bf16[32,2048]{1,0:T(8,128)(2,1)S(1)}, u32[]{:S(2)}, u32[]{:S(2)}) %collective-permute-start.17) | collective-permute-done | bytes 131104 | tf_op jit(solution)/shard_map/ppermute | solution.py:516
  38.2 1.3 %collective-permute-start.18 = (bf16[128,512]{1,0:T(8,128)(2,1)S(1)}, bf16[128,512]{1,0:T(8,128)(2,1)S(1)}, u32[]{:S(2)}, u32[]{:S(2)}) collective-permute-start(bf16[128,512]{1,0:T(8,128)(2,1)S(1)} %get-tuple-element.113), channel_id=1, source_target_pairs={{0,8},{4,12},{8,0},{12,4},{16,24},{20,28},{24,16},{28,20},{1,9},{5... | collective-permute-start | bytes 393224 | tf_op jit(solution)/shard_map/ppermute | solution.py:485
  39.9 1.0 %collective-permute-start.20 = (bf16[128,512]{1,0:T(8,128)(2,1)S(1)}, bf16[128,512]{1,0:T(8,128)(2,1)S(1)}, u32[]{:S(2)}, u32[]{:S(2)}) collective-permute-start(bf16[128,512]{1,0:T(8,128)(2,1)S(1)} %get-tuple-element.115), channel_id=1, source_target_pairs={{0,24},{4,28},{8,16},{12,20},{16,8},{20,12},{24,0},{28,4},{1,25},{... | collective-permute-start | bytes 393224 | tf_op jit(solution)/shard_map/ppermute | solution.py:485
  40.9 1.3 %collective-permute-start.24 = (bf16[32,2048]{1,0:T(8,128)(2,1)S(1)}, bf16[32,2048]{1,0:T(8,128)(2,1)S(1)}, u32[]{:S(2)}, u32[]{:S(2)}) collective-permute-start(bf16[32,2048]{1,0:T(8,128)(2,1)S(1)} %get-tuple-element.111.refs_7_.refs_10_), channel_id=1, source_target_pairs={{1,0},{5,4},{9,8},{13,12},{17,16},{21,20},{25,24},{29,28}} | collective-permute-start | bytes 393224 | tf_op jit(solution)/shard_map/ppermute | solution.py:516
  42.2 1.3 %collective-permute-start.25 = (bf16[32,2048]{1,0:T(8,128)(2,1)S(1)}, bf16[32,2048]{1,0:T(8,128)(2,1)S(1)}, u32[]{:S(2)}, u32[]{:S(2)}) collective-permute-start(bf16[32,2048]{1,0:T(8,128)(2,1)S(1)} %get-tuple-element.112.after_ref.refs_11_), channel_id=1, source_target_pairs={{1,0},{5,4},{9,8},{13,12},{17,16},{21,20},{25,24},{29,28}} | collective-permute-start | bytes 393224 | tf_op jit(solution)/shard_map/ppermute | solution.py:516
  43.6 1.6 %collective-permute-done.20.refs_18_.refs_3_ = bf16[128,512]{1,0:T(8,128)(2,1)S(1)} collective-permute-done((bf16[128,512]{1,0:T(8,128)(2,1)S(1)}, bf16[128,512]{1,0:T(8,128)(2,1)S(1)}, u32[]{:S(2)}, u32[]{:S(2)}) %collective-permute-start.20) | collective-permute-done | bytes 131104 | tf_op jit(solution)/shard_map/ppermute | solution.py:485
  45.3 3.2 %collective-permute-start.21 = (bf16[16,2048]{1,0:T(8,128)(2,1)S(1)}, bf16[16,2048]{1,0:T(8,128)(2,1)S(1)}, u32[]{:S(2)}, u32[]{:S(2)}) collective-permute-start(bf16[16,2048]{1,0:T(8,128)(2,1)S(1)} %get-tuple-element.117), channel_id=1, source_target_pairs={{0,4},{4,0},{8,12},{12,8},{16,20},{20,16},{24,28},{28,24},{1,5},{5... | collective-permute-start | bytes 196616 | tf_op jit(solution)/shard_map/ppermute | solution.py:485
  48.8 1.5 %collective-permute-start.23 = (bf16[16,2048]{1,0:T(8,128)(2,1)S(1)}, bf16[16,2048]{1,0:T(8,128)(2,1)S(1)}, u32[]{:S(2)}, u32[]{:S(2)}) collective-permute-start(bf16[16,2048]{1,0:T(8,128)(2,1)S(1)} %get-tuple-element.119), channel_id=1, source_target_pairs={{0,12},{4,8},{8,4},{12,0},{16,28},{20,24},{24,20},{28,16},{1,13},{... | collective-permute-start | bytes 196616 | tf_op jit(solution)/shard_map/ppermute | solution.py:485
  50.3 1.9 %collective-permute-done.22.refs_18_.refs_2_ = bf16[16,2048]{1,0:T(8,128)(2,1)S(1)} collective-permute-done((bf16[16,2048]{1,0:T(8,128)(2,1)S(1)}, bf16[16,2048]{1,0:T(8,128)(2,1)S(1)}, u32[]{:S(2)}, u32[]{:S(2)}) %collective-permute-start.22) | collective-permute-done | bytes 65568 | tf_op jit(solution)/shard_map/ppermute | solution.py:485
  52.2 1.6 %collective-permute-done.23.refs_19_.refs_3_ = bf16[16,2048]{1,0:T(8,128)(2,1)S(1)} collective-permute-done((bf16[16,2048]{1,0:T(8,128)(2,1)S(1)}, bf16[16,2048]{1,0:T(8,128)(2,1)S(1)}, u32[]{:S(2)}, u32[]{:S(2)}) %collective-permute-start.23) | collective-permute-done | bytes 65568 | tf_op jit(solution)/shard_map/ppermute | solution.py:485
  54.9 1.6 %collective-permute-start.30 = (bf16[128,512]{1,0:T(8,128)(2,1)S(1)}, bf16[128,512]{1,0:T(8,128)(2,1)S(1)}, u32[]{:S(2)}, u32[]{:S(2)}) collective-permute-start(bf16[128,512]{1,0:T(8,128)(2,1)S(1)} %get-tuple-element.134.refs_4_), channel_id=1, source_target_pairs={{0,24},{4,28},{8,16},{12,20},{16,8},{20,12},{24,0},{28,4},{1,25},{... | collective-permute-start | bytes 393224 | tf_op jit(solution)/shard_map/ppermute | solution.py:485
  56.6 1.1 %collective-permute-start.26 = (bf16[16,2048]{1,0:T(8,128)(2,1)S(1)}, bf16[16,2048]{1,0:T(8,128)(2,1)S(1)}, u32[]{:S(2)}, u32[]{:S(2)}) collective-permute-start(bf16[16,2048]{1,0:T(8,128)(2,1)S(1)} %get-tuple-element.130), channel_id=1, source_target_pairs={{0,4},{4,0},{8,12},{12,8},{16,20},{20,16},{24,28},{28,24},{1,5},{5... | collective-permute-start | bytes 196616 | tf_op jit(solution)/shard_map/ppermute | solution.py:485
  58.5 6.2 %collective-permute-done.28.refs_9_.refs_7_ = bf16[16,2048]{1,0:T(8,128)(2,1)S(1)} collective-permute-done((bf16[16,2048]{1,0:T(8,128)(2,1)S(1)}, bf16[16,2048]{1,0:T(8,128)(2,1)S(1)}, u32[]{:S(2)}, u32[]{:S(2)}) %collective-permute-start.28) | collective-permute-done | bytes 65568 | tf_op jit(solution)/shard_map/ppermute | solution.py:485
  66.8 1.0 %copy-done.2 = bf16[128,2048]{1,0:T(8,128)(2,1)S(1)} copy-done((bf16[128,2048]{1,0:T(8,128)(2,1)S(1)}, bf16[128,2048]{1,0:T(8,128)(2,1)}, u32[]{:S(2)}) %copy-start.2) | copy-done | bytes 524312
  67.9 1.0 %finish.1 = (f32[256,512]{1,0:T(8,128)}, f32[1,256]{1,0:T(1,128)}) custom-call(f32[256,512]{1,0:T(8,128)S(1)} %get-tuple-element.135.refs_8_.own_ref, bf16[256,512]{1,0:T(8,128)(2,1)S(1)} %collective-permute-done.31.other_ref, f32[256,512]{1,0:T(8,128)S(1)} %get-tuple-element.137.weight_ref, f32[256,128]{1,0:T(8,128)S(1)} %get-tuple-element.138.gain_ref, ...), custom_call_target="tpu_custom_call" | custom-call | flops 1150000000 | tf_op jit(solution)/shard_map/finish/pallas_call | solution.py:575
  (62 shorter events, 14.8 us)
Async XLA Ops:
  2.2 5.7 %collective-permute-start = (bf16[16,4608]{1,0:T(8,128)(2,1)S(1)}, bf16[16,4608]{1,0:T(8,128)(2,1)S(1)}, u32[]{:S(2)}, u32[]{:S(2)}) collective-permute-start(bf16[16,4608]{1,0:T(8,128)(2,1)S(1)} %get-tuple-element.74), channel_id=1, source_target_pairs={{0,4},{4,0},{8,12},{12,8},{16,20},{20,16},{24,28},{28,24},{1,5},{5... | collective-permute-start | bytes 442376 | tf_op jit(solution)/shard_map/ppermute | solution.py:485
  2.9 6.2 %collective-permute-start.1 = (bf16[16,4608]{1,0:T(8,128)(2,1)S(1)}, bf16[16,4608]{1,0:T(8,128)(2,1)S(1)}, u32[]{:S(2)}, u32[]{:S(2)}) collective-permute-start(bf16[16,4608]{1,0:T(8,128)(2,1)S(1)} %get-tuple-element.75), channel_id=1, source_target_pairs={{0,8},{4,12},{8,0},{12,4},{16,24},{20,28},{24,16},{28,20},{1,9},{5... | collective-permute-start | bytes 442376 | tf_op jit(solution)/shard_map/ppermute | solution.py:485
  4.1 8.3 %collective-permute-start.2 = (bf16[16,4608]{1,0:T(8,128)(2,1)S(1)}, bf16[16,4608]{1,0:T(8,128)(2,1)S(1)}, u32[]{:S(2)}, u32[]{:S(2)}) collective-permute-start(bf16[16,4608]{1,0:T(8,128)(2,1)S(1)} %get-tuple-element.76), channel_id=1, source_target_pairs={{0,12},{4,8},{8,4},{12,0},{16,28},{20,24},{24,20},{28,16},{1,13},{... | collective-permute-start | bytes 442376 | tf_op jit(solution)/shard_map/ppermute | solution.py:485
  6.1 12.2 %collective-permute-start.12 = (bf16[48,2048]{1,0:T(8,128)(2,1)S(1)}, bf16[48,2048]{1,0:T(8,128)(2,1)S(1)}, u32[]{:S(2)}, u32[]{:S(2)}) collective-permute-start(bf16[48,2048]{1,0:T(8,128)(2,1)S(1)} %get-tuple-element.101), channel_id=1, source_target_pairs={{0,16},{4,20},{8,24},{12,28},{16,0},{20,4},{24,8},{28,12},{1,17},{... | collective-permute-start | bytes 589832 | tf_op jit(solution)/shard_map/ppermute | solution.py:485
  7.4 7.6 %collective-permute-start.9 = (bf16[16,4608]{1,0:T(8,128)(2,1)S(1)}, bf16[16,4608]{1,0:T(8,128)(2,1)S(1)}, u32[]{:S(2)}, u32[]{:S(2)}) collective-permute-start(bf16[16,4608]{1,0:T(8,128)(2,1)S(1)} %get-tuple-element.98), channel_id=1, source_target_pairs={{0,4},{4,0},{8,12},{12,8},{16,20},{20,16},{24,28},{28,24},{1,5},{5... | collective-permute-start | bytes 442376 | tf_op jit(solution)/shard_map/ppermute | solution.py:485
  7.8 7.8 %collective-permute-start.10 = (bf16[16,4608]{1,0:T(8,128)(2,1)S(1)}, bf16[16,4608]{1,0:T(8,128)(2,1)S(1)}, u32[]{:S(2)}, u32[]{:S(2)}) collective-permute-start(bf16[16,4608]{1,0:T(8,128)(2,1)S(1)} %get-tuple-element.99), channel_id=1, source_target_pairs={{0,8},{4,12},{8,0},{12,4},{16,24},{20,28},{24,16},{28,20},{1,9},{5... | collective-permute-start | bytes 442376 | tf_op jit(solution)/shard_map/ppermute | solution.py:485
  9.1 9.2 %collective-permute-start.11 = (bf16[16,4608]{1,0:T(8,128)(2,1)S(1)}, bf16[16,4608]{1,0:T(8,128)(2,1)S(1)}, u32[]{:S(2)}, u32[]{:S(2)}) collective-permute-start(bf16[16,4608]{1,0:T(8,128)(2,1)S(1)} %get-tuple-element.100), channel_id=1, source_target_pairs={{0,12},{4,8},{8,4},{12,0},{16,28},{20,24},{24,20},{28,16},{1,13},{... | collective-permute-start | bytes 442376 | tf_op jit(solution)/shard_map/ppermute | solution.py:485
  13.7 5.6 %collective-permute-start.15 = (bf16[32,2048]{1,0:T(8,128)(2,1)S(1)}, bf16[32,2048]{1,0:T(8,128)(2,1)S(1)}, u32[]{:S(2)}, u32[]{:S(2)}) collective-permute-start(bf16[32,2048]{1,0:T(8,128)(2,1)S(1)} %get-tuple-element.107), channel_id=1, source_target_pairs={{0,16},{4,20},{8,24},{12,28},{16,0},{20,4},{24,8},{28,12},{1,17},{... | collective-permute-start | bytes 393224 | tf_op jit(solution)/shard_map/ppermute | solution.py:485
  15.0 5.0 %collective-permute-start.3 = (bf16[32,2048]{1,0:T(8,128)(2,1)S(1)}, bf16[32,2048]{1,0:T(8,128)(2,1)S(1)}, u32[]{:S(2)}, u32[]{:S(2)}) collective-permute-start(bf16[32,2048]{1,0:T(8,128)(2,1)S(1)} %get-tuple-element.81.refs_8_.refs_6_), channel_id=1, source_target_pairs={{3,2},{7,6},{11,10},{15,14},{19,18},{23,22},{27,26},{31,30}} | collective-permute-start | bytes 393224 | tf_op jit(solution)/shard_map/ppermute | solution.py:516
  15.7 5.7 %collective-permute-start.6 = (bf16[32,2048]{1,0:T(8,128)(2,1)S(1)}, bf16[32,2048]{1,0:T(8,128)(2,1)S(1)}, u32[]{:S(2)}, u32[]{:S(2)}) collective-permute-start(bf16[32,2048]{1,0:T(8,128)(2,1)S(1)} %get-tuple-element.86.refs_5_.refs_7_), channel_id=1, source_target_pairs={{3,2},{7,6},{11,10},{15,14},{19,18},{23,22},{27,26},{31,30}} | collective-permute-start | bytes 393224 | tf_op jit(solution)/shard_map/ppermute | solution.py:516
  18.6 4.1 %collective-permute-start.13 = (bf16[32,2048]{1,0:T(8,128)(2,1)S(1)}, bf16[32,2048]{1,0:T(8,128)(2,1)S(1)}, u32[]{:S(2)}, u32[]{:S(2)}) collective-permute-start(bf16[32,2048]{1,0:T(8,128)(2,1)S(1)} %get-tuple-element.105.refs_7_.refs_6_), channel_id=1, source_target_pairs={{3,2},{7,6},{11,10},{15,14},{19,18},{23,22},{27,26},{31,30}} | collective-permute-start | bytes 393224 | tf_op jit(solution)/shard_map/ppermute | solution.py:516
  19.3 4.7 %collective-permute-start.16 = (bf16[32,2048]{1,0:T(8,128)(2,1)S(1)}, bf16[32,2048]{1,0:T(8,128)(2,1)S(1)}, u32[]{:S(2)}, u32[]{:S(2)}) collective-permute-start(bf16[32,2048]{1,0:T(8,128)(2,1)S(1)} %get-tuple-element.109.refs_7_), channel_id=1, source_target_pairs={{3,2},{7,6},{11,10},{15,14},{19,18},{23,22},{27,26},{31,30}} | collective-permute-start | bytes 393224 | tf_op jit(solution)/shard_map/ppermute | solution.py:516
  20.1 8.5 %collective-permute-start.4 = (bf16[32,2048]{1,0:T(8,128)(2,1)S(1)}, bf16[32,2048]{1,0:T(8,128)(2,1)S(1)}, u32[]{:S(2)}, u32[]{:S(2)}) collective-permute-start(bf16[32,2048]{1,0:T(8,128)(2,1)S(1)} %get-tuple-element.82.refs_7_.refs_8_), channel_id=1, source_target_pairs={{2,1},{6,5},{10,9},{14,13},{18,17},{22,21},{26,25},{30,29}} | collective-permute-start | bytes 393224 | tf_op jit(solution)/shard_map/ppermute | solution.py:516
  21.4 10.0 %collective-permute-start.7 = (bf16[32,2048]{1,0:T(8,128)(2,1)S(1)}, bf16[32,2048]{1,0:T(8,128)(2,1)S(1)}, u32[]{:S(2)}, u32[]{:S(2)}) collective-permute-start(bf16[32,2048]{1,0:T(8,128)(2,1)S(1)} %get-tuple-element.87.refs_6_.refs_9_), channel_id=1, source_target_pairs={{2,1},{6,5},{10,9},{14,13},{18,17},{22,21},{26,25},{30,29}} | collective-permute-start | bytes 393224 | tf_op jit(solution)/shard_map/ppermute | solution.py:516
  22.7 11.5 %collective-permute-start.14 = (bf16[32,2048]{1,0:T(8,128)(2,1)S(1)}, bf16[32,2048]{1,0:T(8,128)(2,1)S(1)}, u32[]{:S(2)}, u32[]{:S(2)}) collective-permute-start(bf16[32,2048]{1,0:T(8,128)(2,1)S(1)} %get-tuple-element.106.refs_7_.refs_8_), channel_id=1, source_target_pairs={{2,1},{6,5},{10,9},{14,13},{18,17},{22,21},{26,25},{30,29}} | collective-permute-start | bytes 393224 | tf_op jit(solution)/shard_map/ppermute | solution.py:516
  24.1 13.2 %collective-permute-start.17 = (bf16[32,2048]{1,0:T(8,128)(2,1)S(1)}, bf16[32,2048]{1,0:T(8,128)(2,1)S(1)}, u32[]{:S(2)}, u32[]{:S(2)}) collective-permute-start(bf16[32,2048]{1,0:T(8,128)(2,1)S(1)} %get-tuple-element.110.refs_9_), channel_id=1, source_target_pairs={{2,1},{6,5},{10,9},{14,13},{18,17},{22,21},{26,25},{30,29}} | collective-permute-start | bytes 393224 | tf_op jit(solution)/shard_map/ppermute | solution.py:516
  29.3 11.6 %collective-permute-start.5 = (bf16[32,2048]{1,0:T(8,128)(2,1)S(1)}, bf16[32,2048]{1,0:T(8,128)(2,1)S(1)}, u32[]{:S(2)}, u32[]{:S(2)}) collective-permute-start(bf16[32,2048]{1,0:T(8,128)(2,1)S(1)} %get-tuple-element.83.refs_7_.refs_10_), channel_id=1, source_target_pairs={{1,0},{5,4},{9,8},{13,12},{17,16},{21,20},{25,24},{29,28}} | collective-permute-start | bytes 393224 | tf_op jit(solution)/shard_map/ppermute | solution.py:516
  32.2 10.1 %collective-permute-start.8 = (bf16[32,2048]{1,0:T(8,128)(2,1)S(1)}, bf16[32,2048]{1,0:T(8,128)(2,1)S(1)}, u32[]{:S(2)}, u32[]{:S(2)}) collective-permute-start(bf16[32,2048]{1,0:T(8,128)(2,1)S(1)} %get-tuple-element.88.refs_6_.refs_11_), channel_id=1, source_target_pairs={{1,0},{5,4},{9,8},{13,12},{17,16},{21,20},{25,24},{29,28}} | collective-permute-start | bytes 393224 | tf_op jit(solution)/shard_map/ppermute | solution.py:516
  38.2 5.4 %collective-permute-start.18 = (bf16[128,512]{1,0:T(8,128)(2,1)S(1)}, bf16[128,512]{1,0:T(8,128)(2,1)S(1)}, u32[]{:S(2)}, u32[]{:S(2)}) collective-permute-start(bf16[128,512]{1,0:T(8,128)(2,1)S(1)} %get-tuple-element.113), channel_id=1, source_target_pairs={{0,8},{4,12},{8,0},{12,4},{16,24},{20,28},{24,16},{28,20},{1,9},{5... | collective-permute-start | bytes 393224 | tf_op jit(solution)/shard_map/ppermute | solution.py:485
  39.5 4.1 %collective-permute-start.19 = (bf16[128,512]{1,0:T(8,128)(2,1)S(1)}, bf16[128,512]{1,0:T(8,128)(2,1)S(1)}, u32[]{:S(2)}, u32[]{:S(2)}) collective-permute-start(bf16[128,512]{1,0:T(8,128)(2,1)S(1)} %get-tuple-element.114), channel_id=1, source_target_pairs={{0,16},{4,20},{8,24},{12,28},{16,0},{20,4},{24,8},{28,12},{1,17},{... | collective-permute-start | bytes 393224 | tf_op jit(solution)/shard_map/ppermute | solution.py:485
  39.9 5.3 %collective-permute-start.20 = (bf16[128,512]{1,0:T(8,128)(2,1)S(1)}, bf16[128,512]{1,0:T(8,128)(2,1)S(1)}, u32[]{:S(2)}, u32[]{:S(2)}) collective-permute-start(bf16[128,512]{1,0:T(8,128)(2,1)S(1)} %get-tuple-element.115), channel_id=1, source_target_pairs={{0,24},{4,28},{8,16},{12,20},{16,8},{20,12},{24,0},{28,4},{1,25},{... | collective-permute-start | bytes 393224 | tf_op jit(solution)/shard_map/ppermute | solution.py:485
  40.9 9.3 %collective-permute-start.24 = (bf16[32,2048]{1,0:T(8,128)(2,1)S(1)}, bf16[32,2048]{1,0:T(8,128)(2,1)S(1)}, u32[]{:S(2)}, u32[]{:S(2)}) collective-permute-start(bf16[32,2048]{1,0:T(8,128)(2,1)S(1)} %get-tuple-element.111.refs_7_.refs_10_), channel_id=1, source_target_pairs={{1,0},{5,4},{9,8},{13,12},{17,16},{21,20},{25,24},{29,28}} | collective-permute-start | bytes 393224 | tf_op jit(solution)/shard_map/ppermute | solution.py:516
  42.2 8.0 %collective-permute-start.25 = (bf16[32,2048]{1,0:T(8,128)(2,1)S(1)}, bf16[32,2048]{1,0:T(8,128)(2,1)S(1)}, u32[]{:S(2)}, u32[]{:S(2)}) collective-permute-start(bf16[32,2048]{1,0:T(8,128)(2,1)S(1)} %get-tuple-element.112.after_ref.refs_11_), channel_id=1, source_target_pairs={{1,0},{5,4},{9,8},{13,12},{17,16},{21,20},{25,24},{29,28}} | collective-permute-start | bytes 393224 | tf_op jit(solution)/shard_map/ppermute | solution.py:516
  45.3 5.0 %collective-permute-start.21 = (bf16[16,2048]{1,0:T(8,128)(2,1)S(1)}, bf16[16,2048]{1,0:T(8,128)(2,1)S(1)}, u32[]{:S(2)}, u32[]{:S(2)}) collective-permute-start(bf16[16,2048]{1,0:T(8,128)(2,1)S(1)} %get-tuple-element.117), channel_id=1, source_target_pairs={{0,4},{4,0},{8,12},{12,8},{16,20},{20,16},{24,28},{28,24},{1,5},{5... | collective-permute-start | bytes 196616 | tf_op jit(solution)/shard_map/ppermute | solution.py:485
  48.5 3.7 %collective-permute-start.22 = (bf16[16,2048]{1,0:T(8,128)(2,1)S(1)}, bf16[16,2048]{1,0:T(8,128)(2,1)S(1)}, u32[]{:S(2)}, u32[]{:S(2)}) collective-permute-start(bf16[16,2048]{1,0:T(8,128)(2,1)S(1)} %get-tuple-element.118), channel_id=1, source_target_pairs={{0,8},{4,12},{8,0},{12,4},{16,24},{20,28},{24,16},{28,20},{1,9},{5... | collective-permute-start | bytes 196616 | tf_op jit(solution)/shard_map/ppermute | solution.py:485
  48.8 5.0 %collective-permute-start.23 = (bf16[16,2048]{1,0:T(8,128)(2,1)S(1)}, bf16[16,2048]{1,0:T(8,128)(2,1)S(1)}, u32[]{:S(2)}, u32[]{:S(2)}) collective-permute-start(bf16[16,2048]{1,0:T(8,128)(2,1)S(1)} %get-tuple-element.119), channel_id=1, source_target_pairs={{0,12},{4,8},{8,4},{12,0},{16,28},{20,24},{24,20},{28,16},{1,13},{... | collective-permute-start | bytes 196616 | tf_op jit(solution)/shard_map/ppermute | solution.py:485
  53.8 10.9 %collective-permute-start.27 = (bf16[48,2048]{1,0:T(8,128)(2,1)S(1)}, bf16[48,2048]{1,0:T(8,128)(2,1)S(1)}, u32[]{:S(2)}, u32[]{:S(2)}) collective-permute-start(bf16[48,2048]{1,0:T(8,128)(2,1)S(1)} %get-tuple-element.131), channel_id=1, source_target_pairs={{0,8},{4,12},{8,0},{12,4},{16,24},{20,28},{24,16},{28,20},{1,9},{5... | collective-permute-start | bytes 589832 | tf_op jit(solution)/shard_map/ppermute | solution.py:485
  54.2 10.6 %collective-permute-start.29 = (bf16[128,512]{1,0:T(8,128)(2,1)S(1)}, bf16[128,512]{1,0:T(8,128)(2,1)S(1)}, u32[]{:S(2)}, u32[]{:S(2)}) collective-permute-start(bf16[128,512]{1,0:T(8,128)(2,1)S(1)} %get-tuple-element.134.refs_4_), channel_id=1, source_target_pairs={{0,16},{4,20},{8,24},{12,28},{16,0},{20,4},{24,8},{28,12},{1,17},{... | collective-permute-start | bytes 393224 | tf_op jit(solution)/shard_map/ppermute | solution.py:485
  54.9 9.8 %collective-permute-start.30 = (bf16[128,512]{1,0:T(8,128)(2,1)S(1)}, bf16[128,512]{1,0:T(8,128)(2,1)S(1)}, u32[]{:S(2)}, u32[]{:S(2)}) collective-permute-start(bf16[128,512]{1,0:T(8,128)(2,1)S(1)} %get-tuple-element.134.refs_4_), channel_id=1, source_target_pairs={{0,24},{4,28},{8,16},{12,20},{16,8},{20,12},{24,0},{28,4},{1,25},{... | collective-permute-start | bytes 393224 | tf_op jit(solution)/shard_map/ppermute | solution.py:485
  56.6 2.0 %collective-permute-start.26 = (bf16[16,2048]{1,0:T(8,128)(2,1)S(1)}, bf16[16,2048]{1,0:T(8,128)(2,1)S(1)}, u32[]{:S(2)}, u32[]{:S(2)}) collective-permute-start(bf16[16,2048]{1,0:T(8,128)(2,1)S(1)} %get-tuple-element.130), channel_id=1, source_target_pairs={{0,4},{4,0},{8,12},{12,8},{16,20},{20,16},{24,28},{28,24},{1,5},{5... | collective-permute-start | bytes 196616 | tf_op jit(solution)/shard_map/ppermute | solution.py:485
  57.6 7.1 %collective-permute-start.28 = (bf16[16,2048]{1,0:T(8,128)(2,1)S(1)}, bf16[16,2048]{1,0:T(8,128)(2,1)S(1)}, u32[]{:S(2)}, u32[]{:S(2)}) collective-permute-start(bf16[16,2048]{1,0:T(8,128)(2,1)S(1)} %get-tuple-element.132), channel_id=1, source_target_pairs={{0,12},{4,8},{8,4},{12,0},{16,28},{20,24},{24,20},{28,16},{1,13},{... | collective-permute-start | bytes 196616 | tf_op jit(solution)/shard_map/ppermute | solution.py:485
  65.2 1.6 %collective-permute-start.31 = (bf16[256,512]{1,0:T(8,128)(2,1)S(1)}, bf16[256,512]{1,0:T(8,128)(2,1)S(1)}, u32[]{:S(2)}, u32[]{:S(2)}) collective-permute-start(bf16[256,512]{1,0:T(8,128)(2,1)S(1)} %get-tuple-element.136), channel_id=1, source_target_pairs={{0,4},{4,0},{8,12},{12,8},{16,20},{20,16},{24,28},{28,24},{1,5},{5... | collective-permute-start | bytes 786440 | tf_op jit(solution)/shard_map/ppermute | solution.py:485
  (3 other events, 13.1 us)

commit v7 on v6

--- a/solution.py
+++ b/solution.py
@@ -12,6 +12,7 @@
 UNIT = 32
 EPSILON = 1e-06
 MASKED = -1e30
+UNITS = ("a_late", "a_early", "b_late", "b_early")
 VMEM = pl.BlockSpec(memory_space=pltpu.VMEM)
 SMEM = pl.BlockSpec(memory_space=pltpu.SMEM)
 
@@ -101,24 +102,21 @@
     heads = model_width // kv_width
     key_heads = kv_width // HEAD_FEATURES
     operands = [near(piece) for piece in pieces] + [near(seg)]
-    specs = [VMEM] * len(operands)
-    outs = [
-        jax.ShapeDtypeStruct((key_heads, UNIT, heads * UNIT), jnp.bfloat16),
-        jax.ShapeDtypeStruct((key_heads, UNIT, heads * BLOCK), jnp.bfloat16),
-        jax.ShapeDtypeStruct((BLOCK, 128), jnp.float32),
-        jax.ShapeDtypeStruct((BLOCK, model_width), jnp.bfloat16),
-    ]
-    scratch = [pltpu.VMEM((BLOCK, 2 * model_width + kv_width), jnp.bfloat16)]
+    specs = [VMEM] * len(operands) + [ANY] * len(after)
     operands += after
-    specs += [ANY] * len(after)
     return pl.pallas_call(
         functools.partial(probs_kernel, len(pieces), seg_row, model_width, kv_width),
-        out_shape=tuple(outs),
+        out_shape=(
+            jax.ShapeDtypeStruct((key_heads, UNIT, heads * UNIT), jnp.bfloat16),
+            jax.ShapeDtypeStruct((key_heads, UNIT, heads * BLOCK), jnp.bfloat16),
+            jax.ShapeDtypeStruct((BLOCK, 128), jnp.float32),
+            jax.ShapeDtypeStruct((BLOCK, model_width), jnp.bfloat16),
+        ),
         in_specs=specs,
-        out_specs=(VMEM,) * len(outs),
-        scratch_shapes=scratch,
+        out_specs=(VMEM,) * 4,
+        scratch_shapes=[pltpu.VMEM((BLOCK, 2 * model_width + kv_width), jnp.bfloat16)],
         name="probs",
-        **params(0.35),
+        **params(0.35 if after else 2.0),
     )(*operands)
 
 
@@ -223,7 +221,7 @@
     )(*operands)
 
 
-def tick_kernel(tick, rows, parts, kept, final, send, *refs):
+def tick_kernel(tick, rows, parts, kept, final, *refs):
     grads = list(zip(refs, parts))
     probs_ref, inv_ref, x_ref, turned_ref, gain_ref = refs[len(parts) : len(parts) + 5]
     refs = refs[len(parts) + 5 :]
@@ -239,12 +237,6 @@
             block_ref[EARLY, columns] = part
 
     else:
-        if send:
-            up_ref, across_ref, sem = refs[0], refs[-3], refs[-1]
-            refs = refs[:-3] + refs[-2:-1]
-            first = pl.multiple_of((1 - place()[0]) * BLOCK, BLOCK)
-            made = pltpu.make_async_copy(up_ref.at[pl.ds(first, UNIT)], across_ref, sem)
-            made.start()
         out_ref, value_ref, scaled_ref = refs[-3:]
 
         def store(columns, part):
@@ -257,8 +249,6 @@
             value_ref,
         )
 
-    if send:
-        made.wait()
     for at in range(kept):
 
         @pl.when(turn == at)
@@ -288,7 +278,7 @@
             values_ref[...] = jnp.concatenate(values, axis=0)
 
 
-def tick_step(tick, grads, block, turned, gain, kept=(), late=(), after=(), up=None):
+def tick_step(tick, grads, block, turned, gain, kept=(), late=(), after=(), name=""):
     kv_width, model_width = turned.shape
     low = len(grads) == 2
     final = len(late) - 1 if late else 0
@@ -297,11 +287,7 @@
     arrays += [array for pair in kept for array in pair]
     arrays += late
     operands = [near(array) for array in arrays]
-    specs = [VMEM] * len(operands)
-    if up is not None:
-        operands.append(pltpu.with_memory_space_constraint(up, pltpu.HBM))
-        specs.append(pl.BlockSpec(memory_space=pltpu.HBM))
-    specs += [ANY] * len(after)
+    specs = [VMEM] * len(operands) + [ANY] * len(after)
     bf16 = jnp.bfloat16
     scratch = [pltpu.VMEM((UNIT, model_width), jnp.float32)]
     if final:
@@ -318,27 +304,23 @@
             jax.ShapeDtypeStruct((UNIT, model_width), bf16),
             jax.ShapeDtypeStruct((UNIT, kv_width), bf16),
         )
-        if up is not None:
-            outs += (jax.ShapeDtypeStruct((UNIT, model_width), bf16),)
-            scratch.append(pltpu.SemaphoreType.DMA)
-    parts = [part for _, part in grads]
     return pl.pallas_call(
         functools.partial(
-            tick_kernel, tick, EARLY if low else LATE, parts, len(kept), final, up is not None
+            tick_kernel, tick, EARLY if low else LATE, [part for _, part in grads], len(kept), final
         ),
         out_shape=outs,
         in_specs=specs,
         out_specs=(VMEM,) * len(outs),
         scratch_shapes=scratch,
-        name="tick",
-        **params(0.2),
+        name=f"tick{tick}_{name}",
+        **params(0.0),
     )(*operands, *after)
 
 
 def pack_kernel(block, half, piece, query_ref, key_ref, hidden_ref, up_ref, seg_ref, *rest):
-    late_ref, *early, seg_in_ref, sems = rest[-4 + block :]
-    packed = rest[-4 + block - half : -4 + block]
-    rest = rest[: -4 + block - half]
+    up_out_ref, seg_in_ref, sems = rest[-3:]
+    packed = rest[-3 - half : -3]
+    rest = rest[: -3 - half]
     side, at, _ = place()
     there = side if block == 0 else 1 - side
     copies = []
@@ -357,16 +339,15 @@
             width = source.shape[1]
             copy(source.at[rows], packed[k].at[:, pl.ds(first, width)])
             first += width
-    for first, target in [(UNIT, late_ref)] + [(0, ref) for ref in early]:
-        rows = pl.ds(pl.multiple_of(there * BLOCK + first, UNIT), UNIT)
-        copy(up_ref.at[rows], target.at[pl.ds(0, UNIT)])
-    late_ref[UNIT:, :] = jnp.zeros((16, late_ref.shape[1]), jnp.bfloat16)
+    rows = pl.ds(pl.multiple_of(there * BLOCK, BLOCK), BLOCK)
+    copy(up_ref.at[rows], up_out_ref.at[pl.ds(0, BLOCK)])
+    up_out_ref[BLOCK:, :] = jnp.zeros((16, up_out_ref.shape[1]), jnp.bfloat16)
     copies[0].wait()
     ids = seg_in_ref[...].astype(jnp.float32)
-    late_ref[UNIT:, : ids.shape[1]] = jnp.broadcast_to(ids, (16, ids.shape[1])).astype(
+    up_out_ref[BLOCK:, : ids.shape[1]] = jnp.broadcast_to(ids, (16, ids.shape[1])).astype(
         jnp.bfloat16
     )
-    if rest:
+    if block == 1:
         turn_kernel(rest[0], rest[-1])
     for made in copies[1:]:
         made.wait()
@@ -379,9 +360,7 @@
     operands = [pltpu.with_memory_space_constraint(array, pltpu.HBM) for array in sources]
     specs = [pl.BlockSpec(memory_space=pltpu.HBM)] * len(sources)
     outs = [jax.ShapeDtypeStruct((piece, width), bf16)] * half
-    outs += [
-        jax.ShapeDtypeStruct((rows, model_width), bf16) for rows in (UNIT + 16, UNIT)[: 2 - block]
-    ]
+    outs.append(jax.ShapeDtypeStruct((BLOCK + 16, model_width), bf16))
     if weight is not None:
         operands.append(near(weight))
         specs.append(VMEM)
@@ -393,7 +372,7 @@
         out_specs=(VMEM,) * len(outs),
         scratch_shapes=[
             pltpu.VMEM(sources[-1].shape, jnp.int32),
-            pltpu.SemaphoreType.DMA((3 * half + 3 - block,)),
+            pltpu.SemaphoreType.DMA((3 * half + 2,)),
         ],
         name="pack",
         **params(1.2),
@@ -402,13 +381,13 @@
 
 def columns_kernel(
     width, scale, first_ref, second_ref, weight_ref, gain_ref, after_ref, weight_out_ref,
-    gain_out_ref, *outs
+    gain_out_ref, out_ref
 ):
     me = place()[2]
-    for k, out_ref in enumerate(outs):
-        start = pl.multiple_of(lax.bitwise_xor(lax.div(me, 2), k) * width, width)
-        out_ref[:BLOCK, :] = first_ref[:, pl.ds(start, width)]
-        out_ref[BLOCK:, :] = second_ref[:, pl.ds(start, width)]
+    for block, block_ref in enumerate((first_ref, second_ref)):
+        for pair in range(out_ref.shape[0] // (2 * BLOCK)):
+            row = (2 * pair + block) * BLOCK
+            out_ref[row : row + BLOCK, :] = block_ref[:, pair * width : (pair + 1) * width]
     shares = weight_out_ref.shape[0]
     first = pl.multiple_of(me * shares, shares)
     weight_out_ref[...] = weight_ref[pl.ds(first, shares), :].astype(jnp.float32) * scale
@@ -418,7 +397,7 @@
 
 
 def partial_kernel(count, shares, piece, *refs):
-    columns, values = refs[:count], refs[count : 2 * count]
+    columns_ref, values = refs[0], refs[1 : 1 + count]
     own_ref, other_ref = refs[-2:]
     kv_width = values[0].shape[1]
     parts = []
@@ -430,10 +409,20 @@
         else:
             parts.append(ref[...])
     value = jnp.concatenate(parts, axis=0)
-    mine = lax.rem(place()[2], 2)
+    me = place()[2]
+    pair, mine = lax.div(me, 2), lax.rem(me, 2)
+    tokens = 2 * BLOCK
     for ref, core in ((other_ref, 1 - mine), (own_ref, mine)):
         at = pl.ds(pl.multiple_of(core * shares, shares), shares)
-        rows = jnp.concatenate([part[:, at] for part in columns], axis=0)
+        rows = jnp.concatenate(
+            [
+                columns_ref[
+                    pl.ds(pl.multiple_of(lax.bitwise_xor(pair, k) * tokens, tokens), tokens), at
+                ]
+                for k in range(count)
+            ],
+            axis=0,
+        )
         ref[...] = lax.dot_general(
             rows, value, (((0,), (0,)), ((), ())), preferred_element_type=jnp.float32
         ).astype(ref.dtype)
@@ -441,7 +430,8 @@
 
 def rows_kernel(half, *refs):
     pieces = refs[: 2 * half]
-    rows_ref, sems = refs[-2:]
+    rows_ref, token_ref, sems = refs[-3:]
+    token_ref[...] = jnp.zeros_like(token_ref)
     side, at, _ = place()
     piece = pieces[0].shape[0]
     copies = []
@@ -463,7 +453,7 @@
     )
 
 
-def finish_kernel(own_ref, other_ref, weight_ref, gain_ref, rows_ref, out_ref, gain_out_ref):
+def finish_kernel(own_ref, other_ref, weight_ref, gain_ref, after_ref, out_ref, gain_out_ref):
     total = own_ref[...] + other_ref[...].astype(jnp.float32)
     out_ref[...] = total * gain_ref[:, :1]
     sums = jnp.sum(total * weight_ref[...], axis=1, keepdims=True)
@@ -489,24 +479,21 @@
     sources = (query, key, hidden, upstream, segments)
     pieces, ups = [], []
     for b in range(2):
+        *packed, up = pack(b, half, piece, sources, weight if b else None)
         if b:
-            turned, *packed, late = pack(b, half, piece, sources, weight)
-        else:
-            *packed, late, early = pack(b, half, piece, sources)
+            turned, *packed = packed
         pieces.append([packed[0]] + [swap(packed[k], k) for k in range(1, half)])
-        ups.append([swap(late, half)] if b else [late, early])
+        ups.append(swap(up, half) if b else up)
     whole = slice(0, UNIT)
     scale = float(tokens * replicas) ** (-0.5)
     blocks, kept, after = [], [], []
     for b in range(2):
-        block = block_probs(pieces[b], ups[b][0], UNIT, model_width, kv_width, after)
-        late, early = [(part, whole) for part in ups[b]]
-        first = tick_step(0, [late], block, turned, norm_gain)
-        up = None if b else upstream
-        second = tick_step(0, [late, early], block, turned, norm_gain, after=[first[0]], up=up)
-        if b == 0:
-            *second, rows = second
-            ups[1].append(swap(rows, half))
+        block = block_probs(pieces[b], ups[b], BLOCK, model_width, kv_width, after)
+        late, early = (ups[b], LATE), (ups[b], EARLY)
+        first = tick_step(0, [late], block, turned, norm_gain, name=UNITS[2 * b])
+        second = tick_step(
+            0, [late, early], block, turned, norm_gain, after=[first[0]], name=UNITS[2 * b + 1]
+        )
         blocks.append(block)
         kept += [[first], [second]]
         after = [second[0]]
@@ -515,35 +502,38 @@
         hop = [(layers - tick, layers - 1 - tick)]
         grads = [(lax.ppermute(unit[-1][0], "section", hop), whole) for unit in kept]
         last = tick == layers - 1
-        after, done = [], []
+        after, done = [kept[3][-1][0]], []
         if last:
-            own_weight, own_gain, *columns = pl.pallas_call(
+            own_weight, own_gain, columns = pl.pallas_call(
                 functools.partial(columns_kernel, 2 * shares, scale),
                 out_shape=(
                     jax.ShapeDtypeStruct((shares, kv_width), jnp.float32),
                     jax.ShapeDtypeStruct((shares, 128), jnp.float32),
                 )
-                + (jax.ShapeDtypeStruct((2 * BLOCK, 2 * shares), bf16),) * half,
+                + (jax.ShapeDtypeStruct((half * 2 * BLOCK, 2 * shares), bf16),),
                 in_specs=[VMEM] * 4 + [ANY],
-                out_specs=(VMEM,) * (2 + half),
+                out_specs=(VMEM,) * 3,
                 name="columns",
                 **params(0.4),
             )(blocks[0][3], blocks[1][3], near(weight), norm_gain, kept[3][-1][0])
-            columns = [columns[0]] + [swap(columns[k], 2 * k) for k in range(1, half)]
+            parities = [list(range(parity, replicas, 2)) for parity in range(2)]
+            columns = lax.all_to_all(
+                columns, "dp", split_axis=0, concat_axis=0, axis_index_groups=parities, tiled=True
+            )
         for u in range(4):
             needs = grads[u - 1 : u + 1] if u % 2 else grads[u : u + 1]
             late = []
             if last and u % 2:
                 late = list(done[u - 1]) + ([done[1][0]] if u == 3 else [])
-            if last and u == 1:
-                after = after + columns[1:]
+            if last and u == 0:
+                after = after + [columns]
             if last and u == 3:
                 rows = [done[1][1]] + [swap(done[1][1 + k], k) for k in range(1, half)]
                 after = after + rows[1:]
             done.append(
                 tick_step(
                     tick, needs, blocks[u // 2], turned, norm_gain, kept[u] if last else (), late,
-                    after,
+                    after, name=UNITS[u],
                 )
             )
             after = [done[u][0]]
@@ -557,17 +547,20 @@
             jax.ShapeDtypeStruct((shares, kv_width), jnp.float32),
             jax.ShapeDtypeStruct((shares, kv_width), bf16),
         ),
-        in_specs=[VMEM] * (2 * half) + [ANY] * 2,
+        in_specs=[VMEM] * (1 + half) + [ANY] * 2,
         out_specs=(VMEM, VMEM),
         name="weight_partial",
         **params(0.5),
-    )(*columns, *gathered, last_rows[1], last_rows[3])
+    )(columns, *gathered, last_rows[1], last_rows[3])
     other = swap(other, 1)
-    input_grad = pl.pallas_call(
+    input_grad, token = pl.pallas_call(
         functools.partial(rows_kernel, half),
-        out_shape=jax.ShapeDtypeStruct((tokens, model_width), bf16),
+        out_shape=(
+            jax.ShapeDtypeStruct((tokens, model_width), bf16),
+            jax.ShapeDtypeStruct((8, 128), jnp.float32),
+        ),
         in_specs=[VMEM] * count + [ANY],
-        out_specs=ANY,
+        out_specs=(ANY, VMEM),
         scratch_shapes=[pltpu.SemaphoreType.DMA((count,))],
         name="rows",
         **params(1.2),
@@ -582,7 +575,7 @@
         out_specs=(VMEM, VMEM),
         name="finish",
         **params(1.0),
-    )(own, other, own_weight, own_gain, input_grad)
+    )(own, other, own_weight, own_gain, token)
     return input_grad[None], weight_grad[None], gain_grad
 
 

time: 69.2 us -> 86.7 us (1.25)
  the two profiles are of different devices: /device:TPU:9 before, /device:TPU:0 now
where the time goes in v7:
time: 86.7 us; the launch traced here: 85.9 us
  starting transfers between devices  28.7 us (33%)
  waiting for transfers between devices  28.7 us (33%)
  local copies, waits for them, and re-layouts  14.8 us (17%)
  Pallas kernels  12.3 us (14%)
  between operations  1.4 us (2%)
    unnamed x112, local copies, waits for them, and re-layouts  14.8 us
    ppermute x12, waiting for transfers between devices, direct(): lax.ppermute(unit[-1][0], 'section', hop)  14.5 us
    ppermute x16, starting transfers between devices, swap(): return lax.ppermute(array, 'dp', [(i, i ^ k) for i in range(replicas)])  14.4 us
    ppermute x16, waiting for transfers between devices, swap(): return lax.ppermute(array, 'dp', [(i, i ^ k) for i in range(replicas)])  14.2 us
    ppermute x12, starting transfers between devices, direct(): lax.ppermute(unit[-1][0], 'section', hop)  10.4 us
    pallas_call x16, Pallas kernels, tick_step(): pl.pallas_call(functools.partial(tick_kernel, tick, EARLY if low else LAT...  6.2 us
    all_to_all x1, starting transfers between devices, direct(): lax.all_to_all(columns, 'dp', split_axis=0, concat_axis=0, axis_index_gro...  3.79 us
    pallas_call x2, Pallas kernels, pack(): pl.pallas_call(functools.partial(pack_kernel, block, half, piece), out_sh...  2.97 us
  transfers between devices with their start and end apart: 29, of which 9 were waited for; matrix products, arithmetic and copies ran while one was open for 0% of the time, Pallas kernels for 9%

profile of v7, /device:TPU:0, one launch (start us, length us, event | category | flops | bytes accessed | tf_op | source)
XLA Modules:
  0.0 85.9 jit_solution(15894802688303997196)
XLA Ops:
  0.6 1.5 %pack.2 = (bf16[16,4608]{1,0:T(8,128)(2,1)S(1)}, bf16[16,4608]{1,0:T(8,128)(2,1)S(1)}, bf16[16,4608]{1,0:T(8,128)(2,1)S(1)}, bf16[16,4608]{1,0:T(8,128)(2,1)S(1)}, bf16[80,2048]{1,0:T(8,128)(2,1)S(1)}) custom-call(bf16[128,2048]{1,0:T(8,128)(2,1)} %bitcast.13, bf16[128,512]{1,0:T(8,128)(2,1)} %bitcast.17, bf16[128,2048]{1,0:T(8,128)(2,1)} %bitcast.15, ...), custom_call_target="tpu_custom_call" | custom-call | flops 1380000000 | tf_op jit(solution)/shard_map/pack/pallas_call | solution.py:368
  2.7 2.6 %collective-permute-start.1 = (bf16[16,4608]{1,0:T(8,128)(2,1)S(1)}, bf16[16,4608]{1,0:T(8,128)(2,1)S(1)}, u32[]{:S(2)}, u32[]{:S(2)}) collective-permute-start(bf16[16,4608]{1,0:T(8,128)(2,1)S(1)} %get-tuple-element.72), channel_id=1, source_target_pairs={{0,8},{4,12},{8,0},{12,4},{16,24},{20,28},{24,16},{28,20},{1,9},{5... | collective-permute-start | bytes 442376 | tf_op jit(solution)/shard_map/ppermute | solution.py:475
  5.3 1.4 %pack.3 = (bf16[512,2048]{1,0:T(8,128)(2,1)S(1)}, bf16[16,4608]{1,0:T(8,128)(2,1)S(1)}, bf16[16,4608]{1,0:T(8,128)(2,1)S(1)}, bf16[16,4608]{1,0:T(8,128)(2,1)S(1...) custom-call(bf16[128,2048]{1,0:T(8,128)(2,1)} %bitcast.14, bf16[128,512]{1,0:T(8,128)(2,1)} %bitcast.18, ...), custom_call_target="tpu_custom_call" | custom-call | flops 1380000000 | tf_op jit(solution)/shard_map/pack/pallas_call | solution.py:368
  6.8 1.8 %collective-permute-start.4 = (bf16[80,2048]{1,0:T(8,128)(2,1)S(1)}, bf16[80,2048]{1,0:T(8,128)(2,1)S(1)}, u32[]{:S(2)}, u32[]{:S(2)}) collective-permute-start(bf16[80,2048]{1,0:T(8,128)(2,1)S(1)} %get-tuple-element.79), channel_id=1, source_target_pairs={{0,16},{4,20},{8,24},{12,28},{16,0},{20,4},{24,8},{28,12},{1,17},{... | collective-permute-start | bytes 983048 | tf_op jit(solution)/shard_map/ppermute | solution.py:475
  8.7 1.5 %collective-permute-start.6 = (bf16[16,4608]{1,0:T(8,128)(2,1)S(1)}, bf16[16,4608]{1,0:T(8,128)(2,1)S(1)}, u32[]{:S(2)}, u32[]{:S(2)}) collective-permute-start(bf16[16,4608]{1,0:T(8,128)(2,1)S(1)} %get-tuple-element.82), channel_id=1, source_target_pairs={{0,8},{4,12},{8,0},{12,4},{16,24},{20,28},{24,16},{28,20},{1,9},{5... | collective-permute-start | bytes 442376 | tf_op jit(solution)/shard_map/ppermute | solution.py:475
  10.7 1.9 %collective-permute-done.2.refs_3_ = bf16[16,4608]{1,0:T(8,128)(2,1)S(1)} collective-permute-done((bf16[16,4608]{1,0:T(8,128)(2,1)S(1)}, bf16[16,4608]{1,0:T(8,128)(2,1)S(1)}, u32[]{:S(2)}, u32[]{:S(2)}) %collective-permute-start.2) | collective-permute-done | bytes 147488 | tf_op jit(solution)/shard_map/ppermute | solution.py:475
  16.3 2.6 %collective-permute-done.7.refs_3_ = bf16[16,4608]{1,0:T(8,128)(2,1)S(1)} collective-permute-done((bf16[16,4608]{1,0:T(8,128)(2,1)S(1)}, bf16[16,4608]{1,0:T(8,128)(2,1)S(1)}, u32[]{:S(2)}, u32[]{:S(2)}) %collective-permute-start.7) | collective-permute-done | bytes 147488 | tf_op jit(solution)/shard_map/ppermute | solution.py:475
  28.1 0.8 copy-done.52
  30.4 3.8 %all-to-all-start = ((bf16[4,128,512]{2,1,0:T(8,128)(2,1)}), bf16[4,128,512]{2,1,0:T(8,128)(2,1)S(1)}, u32[]{:S(2)}, u32[]{:S(2)}) async-start(bf16[4,128,512]{2,1,0:T(8,128)(2,1)} %bitcast.12), calls=%async_computation | async-start | bytes 1048576 | tf_op jit(solution)/shard_map/all_to_all | solution.py:520
  34.2 1.3 %collective-permute-start.12 = (bf16[32,2048]{1,0:T(8,128)(2,1)}, bf16[32,2048]{1,0:T(8,128)(2,1)S(1)}, u32[]{:S(2)}, u32[]{:S(2)}) collective-permute-start(bf16[32,2048]{1,0:T(8,128)(2,1)} %copy-done.12), channel_id=1, source_target_pairs={{1,0},{5,4},{9,8},{13,12},{17,16},{21,20},{25,24},{29,28}} | collective-permute-start | bytes 393224 | tf_op jit(solution)/shard_map/ppermute | solution.py:503
  35.4 1.3 %collective-permute-start.14 = (bf16[32,2048]{1,0:T(8,128)(2,1)}, bf16[32,2048]{1,0:T(8,128)(2,1)}, u32[]{:S(2)}, u32[]{:S(2)}) collective-permute-start(bf16[32,2048]{1,0:T(8,128)(2,1)} %copy-done.24), channel_id=1, source_target_pairs={{1,0},{5,4},{9,8},{13,12},{17,16},{21,20},{25,24},{29,28}} | collective-permute-start | bytes 393224 | tf_op jit(solution)/shard_map/ppermute | solution.py:503
  36.7 1.3 %collective-permute-start.20 = (bf16[32,2048]{1,0:T(8,128)(2,1)}, bf16[32,2048]{1,0:T(8,128)(2,1)}, u32[]{:S(2)}, u32[]{:S(2)}) collective-permute-start(bf16[32,2048]{1,0:T(8,128)(2,1)} %copy-done.10), channel_id=1, source_target_pairs={{1,0},{5,4},{9,8},{13,12},{17,16},{21,20},{25,24},{29,28}} | collective-permute-start | bytes 393224 | tf_op jit(solution)/shard_map/ppermute | solution.py:503
  38.0 1.3 %collective-permute-start.21 = (bf16[32,2048]{1,0:T(8,128)(2,1)S(1)}, bf16[32,2048]{1,0:T(8,128)(2,1)}, u32[]{:S(2)}, u32[]{:S(2)}) collective-permute-start(bf16[32,2048]{1,0:T(8,128)(2,1)S(1)} %get-tuple-element.105.after_ref.refs_12_.refs_11_), channel_id=1, source_target_pairs={{1,0},{5,4},{9,8},{13,12},{17,16},{21,20},{25,24},{29,28}} | collective-permute-start | bytes 393224 | tf_op jit(solution)/shard_map/ppermute | solution.py:503
  39.3 14.5 %collective-permute-done.12.refs_0_ = bf16[32,2048]{1,0:T(8,128)(2,1)S(1)} collective-permute-done((bf16[32,2048]{1,0:T(8,128)(2,1)}, bf16[32,2048]{1,0:T(8,128)(2,1)S(1)}, u32[]{:S(2)}, u32[]{:S(2)}) %collective-permute-start.12) | collective-permute-done | bytes 131104 | tf_op jit(solution)/shard_map/ppermute | solution.py:503
  54.5 0.9 %copy-done.5 = bf16[32,2048]{1,0:T(8,128)(2,1)S(1)} copy-done((bf16[32,2048]{1,0:T(8,128)(2,1)S(1)}, bf16[32,2048]{1,0:T(8,128)(2,1)}, u32[]{:S(2)}) %copy-start.5) | copy-done | bytes 131096
  55.4 0.9 %copy-done.9 = bf16[32,2048]{1,0:T(8,128)(2,1)S(1)} copy-done((bf16[32,2048]{1,0:T(8,128)(2,1)S(1)}, bf16[32,2048]{1,0:T(8,128)(2,1)}, u32[]{:S(2)}) %copy-start.9) | copy-done | bytes 131096
  56.3 0.9 %copy-done.13 = bf16[32,2048]{1,0:T(8,128)(2,1)S(1)} copy-done((bf16[32,2048]{1,0:T(8,128)(2,1)S(1)}, bf16[32,2048]{1,0:T(8,128)(2,1)}, u32[]{:S(2)}) %copy-start.13) | copy-done | bytes 131096
  57.2 0.9 %copy-done.20 = bf16[32,2048]{1,0:T(8,128)(2,1)S(1)} copy-done((bf16[32,2048]{1,0:T(8,128)(2,1)S(1)}, bf16[32,2048]{1,0:T(8,128)(2,1)}, u32[]{:S(2)}) %copy-start.20) | copy-done | bytes 131096
  60.4 0.8 tick3_a_late.1
  61.5 1.7 %tick3_a_early.1 = (bf16[64,512]{1,0:T(8,128)(2,1)S(1)}, bf16[16,2048]{1,0:T(8,128)(2,1)S(1)}, bf16[16,2048]{1,0:T(8,128)(2,1)S(1)}, bf16[16,2048]{1,0:T(8,128)(2,1)S(1)}, bf16[16,2048]{1,0:T(8,128)(2,1)S(1)}) custom-call(bf16[32,2048]{1,0:T(8,128)(2,1)S(1)} %copy-done.21, bf16[32,2048]{1,0:T(8,128)(2,1)} %collective-permute-done.14.refs_1_, ...), custom_call_target="tpu_custom_call" | custom-call | tf_op jit(solution)/shard_map/tick3_a_early/pallas_call | solution.py:307
  63.3 2.1 %collective-permute-start.18 = (bf16[16,2048]{1,0:T(8,128)(2,1)S(1)}, bf16[16,2048]{1,0:T(8,128)(2,1)S(1)}, u32[]{:S(2)}, u32[]{:S(2)}) collective-permute-start(bf16[16,2048]{1,0:T(8,128)(2,1)S(1)} %get-tuple-element.111), channel_id=1, source_target_pairs={{0,8},{4,12},{8,0},{12,4},{16,24},{20,28},{24,16},{28,20},{1,9},{5... | collective-permute-start | bytes 196616 | tf_op jit(solution)/shard_map/ppermute | solution.py:475
  65.6 1.7 %tick3_b_late.1 = (bf16[32,2048]{1,0:T(8,128)(2,1)S(1)}, bf16[32,512]{1,0:T(8,128)(2,1)S(1)}) custom-call(bf16[32,2048]{1,0:T(8,128)(2,1)} %collective-permute-done.20.refs_0_, bf16[4,32,128]{2,1,0:T(8,128)(2,1)S(1)} %get-tuple-element.89.refs_1_, f32[64,128]{1,0:T(8,128)S(1)} %get-tuple-element.87.refs_2_.refs_3_, ...), custom_call_target="tpu_custom_call" | custom-call | tf_op jit(solution)/shard_map/tick3_b_late/pallas_call | solution.py:307
  67.3 0.8 collective-permute-done.18.refs_18_.refs_2_
  68.2 1.4 %collective-permute-done.19.refs_19_.refs_3_ = bf16[16,2048]{1,0:T(8,128)(2,1)S(1)} collective-permute-done((bf16[16,2048]{1,0:T(8,128)(2,1)S(1)}, bf16[16,2048]{1,0:T(8,128)(2,1)S(1)}, u32[]{:S(2)}, u32[]{:S(2)}) %collective-permute-start.19) | collective-permute-done | bytes 65568 | tf_op jit(solution)/shard_map/ppermute | solution.py:475
  69.6 1.8 %tick3_b_early.1 = (bf16[128,512]{1,0:T(8,128)(2,1)S(1)}, bf16[16,2048]{1,0:T(8,128)(2,1)S(1)}, bf16[16,2048]{1,0:T(8,128)(2,1)S(1)}, bf16[48,2048]{1,0:T(8,128)(2,1)S(1)}, bf16[16,2048]{1,0:T(8,128)(2,1)S(1)}) custom-call(bf16[32,2048]{1,0:T(8,128)(2,1)} %collective-permute-done.20.refs_0_, bf16[32,2048]{1,0:T(8,128)(2,1)} %collective-permute-done.21.refs_1_, ...), custom_call_target="tpu_custom_call" | custom-call | tf_op jit(solution)/shard_map/tick3_b_early/pallas_call | solution.py:307
  71.4 1.4 %collective-permute-start.23 = (bf16[48,2048]{1,0:T(8,128)(2,1)S(1)}, bf16[48,2048]{1,0:T(8,128)(2,1)S(1)}, u32[]{:S(2)}, u32[]{:S(2)}) collective-permute-start(bf16[48,2048]{1,0:T(8,128)(2,1)S(1)} %get-tuple-element.124), channel_id=1, source_target_pairs={{0,8},{4,12},{8,0},{12,4},{16,24},{20,28},{24,16},{28,20},{1,9},{5... | collective-permute-start | bytes 589832 | tf_op jit(solution)/shard_map/ppermute | solution.py:475
  72.8 1.5 %collective-permute-start.25 = (bf16[128,512]{1,0:T(8,128)(2,1)S(1)}, bf16[128,512]{1,0:T(8,128)(2,1)S(1)}, u32[]{:S(2)}, u32[]{:S(2)}) collective-permute-start(bf16[128,512]{1,0:T(8,128)(2,1)S(1)} %get-tuple-element.126.refs_1_), channel_id=1, source_target_pairs={{0,16},{4,20},{8,24},{12,28},{16,0},{20,4},{24,8},{28,12},{1,17},{... | collective-permute-start | bytes 393224 | tf_op jit(solution)/shard_map/ppermute | solution.py:475
  74.9 1.5 %collective-permute-start.24 = (bf16[16,2048]{1,0:T(8,128)(2,1)S(1)}, bf16[16,2048]{1,0:T(8,128)(2,1)S(1)}, u32[]{:S(2)}, u32[]{:S(2)}) collective-permute-start(bf16[16,2048]{1,0:T(8,128)(2,1)S(1)} %get-tuple-element.125), channel_id=1, source_target_pairs={{0,12},{4,8},{8,4},{12,0},{16,28},{20,24},{24,20},{28,16},{1,13},{... | collective-permute-start | bytes 196616 | tf_op jit(solution)/shard_map/ppermute | solution.py:475
  76.4 5.5 %collective-permute-done.24.refs_6_.refs_7_ = bf16[16,2048]{1,0:T(8,128)(2,1)S(1)} collective-permute-done((bf16[16,2048]{1,0:T(8,128)(2,1)S(1)}, bf16[16,2048]{1,0:T(8,128)(2,1)S(1)}, u32[]{:S(2)}, u32[]{:S(2)}) %collective-permute-start.24) | collective-permute-done | bytes 65568 | tf_op jit(solution)/shard_map/ppermute | solution.py:475
  81.9 1.0 %collective-permute-done.26.refs_4_ = bf16[128,512]{1,0:T(8,128)(2,1)S(1)} collective-permute-done((bf16[128,512]{1,0:T(8,128)(2,1)S(1)}, bf16[128,512]{1,0:T(8,128)(2,1)S(1)}, u32[]{:S(2)}, u32[]{:S(2)}) %collective-permute-start.26) | collective-permute-done | bytes 131104 | tf_op jit(solution)/shard_map/ppermute | solution.py:475
  83.4 0.9 %rows.1 = (bf16[128,2048]{1,0:T(8,128)(2,1)}, f32[8,128]{1,0:T(8,128)S(1)}) custom-call(bf16[16,2048]{1,0:T(8,128)(2,1)S(1)} %get-tuple-element.109.refs_0_, bf16[16,2048]{1,0:T(8,128)(2,1)S(1)} %collective-permute-done.17.refs_17_.refs_1_, bf16[16,2048]{1,0:T(8,128)(2,1)S(1)} %collective-permute-done.18.refs_18_.refs_2_, ...), custom_call_target="tpu_custom_call" | custom-call | flops 1380000000 | tf_op jit(solution)/shard_map/rows/pallas_call | solution.py:556
  84.9 1.0 %finish.1 = (f32[256,512]{1,0:T(8,128)}, f32[1,256]{1,0:T(1,128)}) custom-call(f32[256,512]{1,0:T(8,128)S(1)} %get-tuple-element.127.refs_8_.own_ref, bf16[256,512]{1,0:T(8,128)(2,1)S(1)} %collective-permute-done.27.other_ref, f32[256,512]{1,0:T(8,128)S(1)} %copy-done.53, f32[256,128]{1,0:T(8,128)S(1)} %copy-done.55, f32[8,128]{1,0:T(8,128)S(1)} %get-tuple-element.132.after_ref), custom_call_target="tpu_custom_call" | custom-call | flops 1150000000 | tf_op jit(solution)/shard_map/finish/pallas_call | solution.py:568
  (162 shorter events, 20.4 us)
Async XLA Ops:
  2.2 6.5 %collective-permute-start = (bf16[16,4608]{1,0:T(8,128)(2,1)S(1)}, bf16[16,4608]{1,0:T(8,128)(2,1)S(1)}, u32[]{:S(2)}, u32[]{:S(2)}) collective-permute-start(bf16[16,4608]{1,0:T(8,128)(2,1)S(1)} %get-tuple-element.71), channel_id=1, source_target_pairs={{0,4},{4,0},{8,12},{12,8},{16,20},{20,16},{24,28},{28,24},{1,5},{5... | collective-permute-start | bytes 442376 | tf_op jit(solution)/shard_map/ppermute | solution.py:475
  2.7 7.5 %collective-permute-start.1 = (bf16[16,4608]{1,0:T(8,128)(2,1)S(1)}, bf16[16,4608]{1,0:T(8,128)(2,1)S(1)}, u32[]{:S(2)}, u32[]{:S(2)}) collective-permute-start(bf16[16,4608]{1,0:T(8,128)(2,1)S(1)} %get-tuple-element.72), channel_id=1, source_target_pairs={{0,8},{4,12},{8,0},{12,4},{16,24},{20,28},{24,16},{28,20},{1,9},{5... | collective-permute-start | bytes 442376 | tf_op jit(solution)/shard_map/ppermute | solution.py:475
  5.3 7.3 %collective-permute-start.2 = (bf16[16,4608]{1,0:T(8,128)(2,1)S(1)}, bf16[16,4608]{1,0:T(8,128)(2,1)S(1)}, u32[]{:S(2)}, u32[]{:S(2)}) collective-permute-start(bf16[16,4608]{1,0:T(8,128)(2,1)S(1)} %get-tuple-element.73), channel_id=1, source_target_pairs={{0,12},{4,8},{8,4},{12,0},{16,28},{20,24},{24,20},{28,16},{1,13},{... | collective-permute-start | bytes 442376 | tf_op jit(solution)/shard_map/ppermute | solution.py:475
  6.8 12.1 %collective-permute-start.4 = (bf16[80,2048]{1,0:T(8,128)(2,1)S(1)}, bf16[80,2048]{1,0:T(8,128)(2,1)S(1)}, u32[]{:S(2)}, u32[]{:S(2)}) collective-permute-start(bf16[80,2048]{1,0:T(8,128)(2,1)S(1)} %get-tuple-element.79), channel_id=1, source_target_pairs={{0,16},{4,20},{8,24},{12,28},{16,0},{20,4},{24,8},{28,12},{1,17},{... | collective-permute-start | bytes 983048 | tf_op jit(solution)/shard_map/ppermute | solution.py:475
  8.6 6.6 %collective-permute-start.5 = (bf16[16,4608]{1,0:T(8,128)(2,1)S(1)}, bf16[16,4608]{1,0:T(8,128)(2,1)S(1)}, u32[]{:S(2)}, u32[]{:S(2)}) collective-permute-start(bf16[16,4608]{1,0:T(8,128)(2,1)S(1)} %get-tuple-element.81), channel_id=1, source_target_pairs={{0,4},{4,0},{8,12},{12,8},{16,20},{20,16},{24,28},{28,24},{1,5},{5... | collective-permute-start | bytes 442376 | tf_op jit(solution)/shard_map/ppermute | solution.py:475
  8.7 7.6 %collective-permute-start.6 = (bf16[16,4608]{1,0:T(8,128)(2,1)S(1)}, bf16[16,4608]{1,0:T(8,128)(2,1)S(1)}, u32[]{:S(2)}, u32[]{:S(2)}) collective-permute-start(bf16[16,4608]{1,0:T(8,128)(2,1)S(1)} %get-tuple-element.82), channel_id=1, source_target_pairs={{0,8},{4,12},{8,0},{12,4},{16,24},{20,28},{24,16},{28,20},{1,9},{5... | collective-permute-start | bytes 442376 | tf_op jit(solution)/shard_map/ppermute | solution.py:475
  10.2 8.7 %collective-permute-start.7 = (bf16[16,4608]{1,0:T(8,128)(2,1)S(1)}, bf16[16,4608]{1,0:T(8,128)(2,1)S(1)}, u32[]{:S(2)}, u32[]{:S(2)}) collective-permute-start(bf16[16,4608]{1,0:T(8,128)(2,1)S(1)} %get-tuple-element.83), channel_id=1, source_target_pairs={{0,12},{4,8},{8,4},{12,0},{16,28},{20,24},{24,20},{28,16},{1,13},{... | collective-permute-start | bytes 442376 | tf_op jit(solution)/shard_map/ppermute | solution.py:475
  13.9 8.0 %collective-permute-start.3 = (bf16[32,2048]{1,0:T(8,128)(2,1)S(1)}, bf16[32,2048]{1,0:T(8,128)(2,1)S(1)}, u32[]{:S(2)}, u32[]{:S(2)}) collective-permute-start(bf16[32,2048]{1,0:T(8,128)(2,1)S(1)} %get-tuple-element.78.refs_7_.refs_6_), channel_id=1, source_target_pairs={{3,2},{7,6},{11,10},{15,14},{19,18},{23,22},{27,26},{31,30}} | collective-permute-start | bytes 393224 | tf_op jit(solution)/shard_map/ppermute | solution.py:503
  15.2 7.4 %collective-permute-start.11 = (bf16[32,2048]{1,0:T(8,128)(2,1)S(1)}, bf16[32,2048]{1,0:T(8,128)(2,1)S(1)}, u32[]{:S(2)}, u32[]{:S(2)}) collective-permute-start(bf16[32,2048]{1,0:T(8,128)(2,1)S(1)} %get-tuple-element.85.refs_5_.refs_7_), channel_id=1, source_target_pairs={{3,2},{7,6},{11,10},{15,14},{19,18},{23,22},{27,26},{31,30}} | collective-permute-start | bytes 393224 | tf_op jit(solution)/shard_map/ppermute | solution.py:503
  19.9 4.0 %collective-permute-start.9 = (bf16[32,2048]{1,0:T(8,128)(2,1)S(1)}, bf16[32,2048]{1,0:T(8,128)(2,1)S(1)}, u32[]{:S(2)}, u32[]{:S(2)}) collective-permute-start(bf16[32,2048]{1,0:T(8,128)(2,1)S(1)} %get-tuple-element.90.refs_7_.refs_6_), channel_id=1, source_target_pairs={{3,2},{7,6},{11,10},{15,14},{19,18},{23,22},{27,26},{31,30}} | collective-permute-start | bytes 393224 | tf_op jit(solution)/shard_map/ppermute | solution.py:503
  21.2 4.0 %collective-permute-start.10 = (bf16[32,2048]{1,0:T(8,128)(2,1)S(1)}, bf16[32,2048]{1,0:T(8,128)(2,1)S(1)}, u32[]{:S(2)}, u32[]{:S(2)}) collective-permute-start(bf16[32,2048]{1,0:T(8,128)(2,1)S(1)} %get-tuple-element.91.refs_6_.refs_7_), channel_id=1, source_target_pairs={{3,2},{7,6},{11,10},{15,14},{19,18},{23,22},{27,26},{31,30}} | collective-permute-start | bytes 393224 | tf_op jit(solution)/shard_map/ppermute | solution.py:503
  21.9 4.1 %collective-permute-start.8 = (bf16[32,2048]{1,0:T(8,128)(2,1)S(1)}, bf16[32,2048]{1,0:T(8,128)(2,1)S(1)}, u32[]{:S(2)}, u32[]{:S(2)}) collective-permute-start(bf16[32,2048]{1,0:T(8,128)(2,1)S(1)} %get-tuple-element.92.refs_7_.refs_8_), channel_id=1, source_target_pairs={{2,1},{6,5},{10,9},{14,13},{18,17},{22,21},{26,25},{30,29}} | collective-permute-start | bytes 393224 | tf_op jit(solution)/shard_map/ppermute | solution.py:503
  23.2 3.4 %collective-permute-start.13 = (bf16[32,2048]{1,0:T(8,128)(2,1)S(1)}, bf16[32,2048]{1,0:T(8,128)(2,1)S(1)}, u32[]{:S(2)}, u32[]{:S(2)}) collective-permute-start(bf16[32,2048]{1,0:T(8,128)(2,1)S(1)} %get-tuple-element.93.refs_6_.refs_9_), channel_id=1, source_target_pairs={{2,1},{6,5},{10,9},{14,13},{18,17},{22,21},{26,25},{30,29}} | collective-permute-start | bytes 393224 | tf_op jit(solution)/shard_map/ppermute | solution.py:503
  24.6 2.1 %collective-permute-start.15 = (bf16[32,2048]{1,0:T(8,128)(2,1)S(1)}, bf16[32,2048]{1,0:T(8,128)(2,1)S(1)}, u32[]{:S(2)}, u32[]{:S(2)}) collective-permute-start(bf16[32,2048]{1,0:T(8,128)(2,1)S(1)} %get-tuple-element.94.refs_7_.refs_8_), channel_id=1, source_target_pairs={{2,1},{6,5},{10,9},{14,13},{18,17},{22,21},{26,25},{30,29}} | collective-permute-start | bytes 393224 | tf_op jit(solution)/shard_map/ppermute | solution.py:503
  25.3 2.0 %collective-permute-start.16 = (bf16[32,2048]{1,0:T(8,128)(2,1)S(1)}, bf16[32,2048]{1,0:T(8,128)(2,1)S(1)}, u32[]{:S(2)}, u32[]{:S(2)}) collective-permute-start(bf16[32,2048]{1,0:T(8,128)(2,1)S(1)} %get-tuple-element.95.refs_6_.refs_9_), channel_id=1, source_target_pairs={{2,1},{6,5},{10,9},{14,13},{18,17},{22,21},{26,25},{30,29}} | collective-permute-start | bytes 393224 | tf_op jit(solution)/shard_map/ppermute | solution.py:503
  30.4 24.1 %all-to-all-start = ((bf16[4,128,512]{2,1,0:T(8,128)(2,1)}), bf16[4,128,512]{2,1,0:T(8,128)(2,1)S(1)}, u32[]{:S(2)}, u32[]{:S(2)}) async-start(bf16[4,128,512]{2,1,0:T(8,128)(2,1)} %bitcast.12), calls=%async_computation | async-start | bytes 1048576 | tf_op jit(solution)/shard_map/all_to_all | solution.py:520
  34.2 19.7 %collective-permute-start.12 = (bf16[32,2048]{1,0:T(8,128)(2,1)}, bf16[32,2048]{1,0:T(8,128)(2,1)S(1)}, u32[]{:S(2)}, u32[]{:S(2)}) collective-permute-start(bf16[32,2048]{1,0:T(8,128)(2,1)} %copy-done.12), channel_id=1, source_target_pairs={{1,0},{5,4},{9,8},{13,12},{17,16},{21,20},{25,24},{29,28}} | collective-permute-start | bytes 393224 | tf_op jit(solution)/shard_map/ppermute | solution.py:503
  35.4 25.8 %collective-permute-start.14 = (bf16[32,2048]{1,0:T(8,128)(2,1)}, bf16[32,2048]{1,0:T(8,128)(2,1)}, u32[]{:S(2)}, u32[]{:S(2)}) collective-permute-start(bf16[32,2048]{1,0:T(8,128)(2,1)} %copy-done.24), channel_id=1, source_target_pairs={{1,0},{5,4},{9,8},{13,12},{17,16},{21,20},{25,24},{29,28}} | collective-permute-start | bytes 393224 | tf_op jit(solution)/shard_map/ppermute | solution.py:503
  36.7 28.8 %collective-permute-start.20 = (bf16[32,2048]{1,0:T(8,128)(2,1)}, bf16[32,2048]{1,0:T(8,128)(2,1)}, u32[]{:S(2)}, u32[]{:S(2)}) collective-permute-start(bf16[32,2048]{1,0:T(8,128)(2,1)} %copy-done.10), channel_id=1, source_target_pairs={{1,0},{5,4},{9,8},{13,12},{17,16},{21,20},{25,24},{29,28}} | collective-permute-start | bytes 393224 | tf_op jit(solution)/shard_map/ppermute | solution.py:503
  38.0 29.3 %collective-permute-start.21 = (bf16[32,2048]{1,0:T(8,128)(2,1)S(1)}, bf16[32,2048]{1,0:T(8,128)(2,1)}, u32[]{:S(2)}, u32[]{:S(2)}) collective-permute-start(bf16[32,2048]{1,0:T(8,128)(2,1)S(1)} %get-tuple-element.105.after_ref.refs_12_.refs_11_), channel_id=1, source_target_pairs={{1,0},{5,4},{9,8},{13,12},{17,16},{21,20},{25,24},{29,28}} | collective-permute-start | bytes 393224 | tf_op jit(solution)/shard_map/ppermute | solution.py:503
  63.2 6.3 %copy-start.16 = (bf16[32,2048]{1,0:T(8,128)(2,1)S(1)}, bf16[32,2048]{1,0:T(8,128)(2,1)}, u32[]{:S(2)}) copy-start(bf16[32,2048]{1,0:T(8,128)(2,1)} %copy-done.15) | copy-start | bytes 393220
  63.2 6.3 %copy-start.18 = (bf16[32,2048]{1,0:T(8,128)(2,1)S(1)}, bf16[32,2048]{1,0:T(8,128)(2,1)}, u32[]{:S(2)}) copy-start(bf16[32,2048]{1,0:T(8,128)(2,1)} %copy-done.17) | copy-start | bytes 393220
  63.2 6.3 %copy-start.29 = (bf16[32,512]{1,0:T(8,128)(2,1)S(1)}, bf16[32,512]{1,0:T(8,128)(2,1)}, u32[]{:S(2)}) copy-start(bf16[32,512]{1,0:T(8,128)(2,1)} %copy-done.28) | copy-start | bytes 98308
  63.3 4.1 %collective-permute-start.17 = (bf16[16,2048]{1,0:T(8,128)(2,1)S(1)}, bf16[16,2048]{1,0:T(8,128)(2,1)S(1)}, u32[]{:S(2)}, u32[]{:S(2)}) collective-permute-start(bf16[16,2048]{1,0:T(8,128)(2,1)S(1)} %get-tuple-element.110), channel_id=1, source_target_pairs={{0,4},{4,0},{8,12},{12,8},{16,20},{20,16},{24,28},{28,24},{1,5},{5... | collective-permute-start | bytes 196616 | tf_op jit(solution)/shard_map/ppermute | solution.py:475
  63.3 4.8 %collective-permute-start.18 = (bf16[16,2048]{1,0:T(8,128)(2,1)S(1)}, bf16[16,2048]{1,0:T(8,128)(2,1)S(1)}, u32[]{:S(2)}, u32[]{:S(2)}) collective-permute-start(bf16[16,2048]{1,0:T(8,128)(2,1)S(1)} %get-tuple-element.111), channel_id=1, source_target_pairs={{0,8},{4,12},{8,0},{12,4},{16,24},{20,28},{24,16},{28,20},{1,9},{5... | collective-permute-start | bytes 196616 | tf_op jit(solution)/shard_map/ppermute | solution.py:475
  65.5 4.0 %collective-permute-start.19 = (bf16[16,2048]{1,0:T(8,128)(2,1)S(1)}, bf16[16,2048]{1,0:T(8,128)(2,1)S(1)}, u32[]{:S(2)}, u32[]{:S(2)}) collective-permute-start(bf16[16,2048]{1,0:T(8,128)(2,1)S(1)} %get-tuple-element.112), channel_id=1, source_target_pairs={{0,12},{4,8},{8,4},{12,0},{16,28},{20,24},{24,20},{28,16},{1,13},{... | collective-permute-start | bytes 196616 | tf_op jit(solution)/shard_map/ppermute | solution.py:475
  71.4 11.4 %collective-permute-start.23 = (bf16[48,2048]{1,0:T(8,128)(2,1)S(1)}, bf16[48,2048]{1,0:T(8,128)(2,1)S(1)}, u32[]{:S(2)}, u32[]{:S(2)}) collective-permute-start(bf16[48,2048]{1,0:T(8,128)(2,1)S(1)} %get-tuple-element.124), channel_id=1, source_target_pairs={{0,8},{4,12},{8,0},{12,4},{16,24},{20,28},{24,16},{28,20},{1,9},{5... | collective-permute-start | bytes 589832 | tf_op jit(solution)/shard_map/ppermute | solution.py:475
  72.8 9.1 %collective-permute-start.25 = (bf16[128,512]{1,0:T(8,128)(2,1)S(1)}, bf16[128,512]{1,0:T(8,128)(2,1)S(1)}, u32[]{:S(2)}, u32[]{:S(2)}) collective-permute-start(bf16[128,512]{1,0:T(8,128)(2,1)S(1)} %get-tuple-element.126.refs_1_), channel_id=1, source_target_pairs={{0,16},{4,20},{8,24},{12,28},{16,0},{20,4},{24,8},{28,12},{1,17},{... | collective-permute-start | bytes 393224 | tf_op jit(solution)/shard_map/ppermute | solution.py:475
  74.2 8.6 %collective-permute-start.26 = (bf16[128,512]{1,0:T(8,128)(2,1)S(1)}, bf16[128,512]{1,0:T(8,128)(2,1)S(1)}, u32[]{:S(2)}, u32[]{:S(2)}) collective-permute-start(bf16[128,512]{1,0:T(8,128)(2,1)S(1)} %get-tuple-element.126.refs_1_), channel_id=1, source_target_pairs={{0,24},{4,28},{8,16},{12,20},{16,8},{20,12},{24,0},{28,4},{1,25},{... | collective-permute-start | bytes 393224 | tf_op jit(solution)/shard_map/ppermute | solution.py:475
  74.9 1.5 %collective-permute-start.22 = (bf16[16,2048]{1,0:T(8,128)(2,1)S(1)}, bf16[16,2048]{1,0:T(8,128)(2,1)S(1)}, u32[]{:S(2)}, u32[]{:S(2)}) collective-permute-start(bf16[16,2048]{1,0:T(8,128)(2,1)S(1)} %get-tuple-element.123), channel_id=1, source_target_pairs={{0,4},{4,0},{8,12},{12,8},{16,20},{20,16},{24,28},{28,24},{1,5},{5... | collective-permute-start | bytes 196616 | tf_op jit(solution)/shard_map/ppermute | solution.py:475
  74.9 6.9 %collective-permute-start.24 = (bf16[16,2048]{1,0:T(8,128)(2,1)S(1)}, bf16[16,2048]{1,0:T(8,128)(2,1)S(1)}, u32[]{:S(2)}, u32[]{:S(2)}) collective-permute-start(bf16[16,2048]{1,0:T(8,128)(2,1)S(1)} %get-tuple-element.125), channel_id=1, source_target_pairs={{0,12},{4,8},{8,4},{12,0},{16,28},{20,24},{24,20},{28,16},{1,13},{... | collective-permute-start | bytes 196616 | tf_op jit(solution)/shard_map/ppermute | solution.py:475
  83.3 1.6 %collective-permute-start.27 = (bf16[256,512]{1,0:T(8,128)(2,1)S(1)}, bf16[256,512]{1,0:T(8,128)(2,1)S(1)}, u32[]{:S(2)}, u32[]{:S(2)}) collective-permute-start(bf16[256,512]{1,0:T(8,128)(2,1)S(1)} %get-tuple-element.129), channel_id=1, source_target_pairs={{0,4},{4,0},{8,12},{12,8},{16,20},{20,16},{24,28},{28,24},{1,5},{5... | collective-permute-start | bytes 786440 | tf_op jit(solution)/shard_map/ppermute | solution.py:475
  (53 other events, 99.8 us)

commit v8 on v7

--- a/solution.py
+++ b/solution.py
@@ -12,6 +12,7 @@
 UNIT = 32
 EPSILON = 1e-06
 MASKED = -1e30
+OUTS = {1: 2, 5: 6}
 UNITS = ("a_late", "a_early", "b_late", "b_early")
 VMEM = pl.BlockSpec(memory_space=pltpu.VMEM)
 SMEM = pl.BlockSpec(memory_space=pltpu.SMEM)
@@ -221,26 +222,28 @@
     )(*operands)
 
 
-def tick_kernel(tick, rows, parts, kept, final, *refs):
+def tick_kernel(tick, rows, parts, kept, late, *refs):
     grads = list(zip(refs, parts))
     probs_ref, inv_ref, x_ref, turned_ref, gain_ref = refs[len(parts) : len(parts) + 5]
     refs = refs[len(parts) + 5 :]
     earlier, refs = refs[: 2 * kept], refs[2 * kept :]
+    late_refs = refs[:late]
     kv_width, model_width = turned_ref.shape
     turn = lax.axis_size("section") - 1 - lax.axis_index("section")
-    if final:
-        late_ref, late_value_ref = refs[:2]
-        values_ref, *outs = refs[-8:-3]
-        scaled_ref, block_ref, value_ref = refs[-3:]
+    if late:
+        outs, (scaled_ref, blocks_ref, value_ref) = refs[-3 - OUTS[late] : -3], refs[-3:]
+    else:
+        outs, scaled_ref = refs[-3:-1], refs[-1]
+        value_ref = outs[1]
+    if late > 1:
 
         def store(columns, part):
-            block_ref[EARLY, columns] = part
+            blocks_ref[BLOCK : BLOCK + UNIT, columns] = part
 
     else:
-        out_ref, value_ref, scaled_ref = refs[-3:]
 
         def store(columns, part):
-            out_ref[:, columns] = part
+            outs[0][:, columns] = part
 
     @pl.when(turn == tick)
     def _():
@@ -256,32 +259,34 @@
             store(slice(None), earlier[2 * at][...])
             value_ref[...] = earlier[2 * at + 1][...]
 
-    if final:
-        block_ref[LATE, :] = late_ref[...]
+    if late:
+        values = jnp.concatenate([value_ref[...], late_refs[0][...]], axis=0)
+        outs[1][...] = values
+    if late > 1:
+        late_a_ref, early_a_ref, late_b_ref, value_a_ref = late_refs[1:]
+        outs[0][:BLOCK, :] = value_a_ref[...]
+        outs[0][BLOCK:, :] = values
+        blocks_ref[EARLY, :] = early_a_ref[...]
+        blocks_ref[LATE, :] = late_a_ref[...]
+        blocks_ref[BLOCK + UNIT :, :] = late_b_ref[...]
         at = place()[1]
-        piece = outs[0].shape[0]
-        for k, out_ref in enumerate(outs):
+        half = len(outs) - 2
+        piece = BLOCK // half
+        for k, out_ref in enumerate(outs[2:]):
             first = pl.multiple_of(lax.bitwise_xor(at, k) * piece, piece)
-            out_ref[:piece, :] = block_ref[pl.ds(first, piece), :]
-        values = [value_ref[...], late_value_ref[...]]
-        if final == 2:
-            values = [refs[2][...]] + values
-            groups = model_width // kv_width
-            whole = jnp.concatenate(values, axis=0)
-            values_ref[...] = whole
-            share = 2 * BLOCK // groups
-            for g in range(groups):
-                outs[2][piece:, g * kv_width : (g + 1) * kv_width] = whole[
-                    g * share : (g + 1) * share
-                ]
-        else:
-            values_ref[...] = jnp.concatenate(values, axis=0)
+            out_ref[:piece, :] = blocks_ref[pl.ds(first, piece), :]
+            out_ref[piece : 2 * piece, :] = blocks_ref[pl.ds(BLOCK + first, piece), :]
+        groups = model_width // kv_width
+        share = BLOCK // groups
+        for g in range(groups):
+            outs[4][2 * piece :, g * kv_width : (g + 1) * kv_width] = values[
+                g * share : (g + 1) * share
+            ]
 
 
 def tick_step(tick, grads, block, turned, gain, kept=(), late=(), after=(), name=""):
     kv_width, model_width = turned.shape
     low = len(grads) == 2
-    final = len(late) - 1 if late else 0
     arrays = [grad for grad, _ in grads]
     arrays += [block[1] if low else block[0], block[2], block[3], turned, gain]
     arrays += [array for pair in kept for array in pair]
@@ -290,30 +295,27 @@
     specs = [VMEM] * len(operands) + [ANY] * len(after)
     bf16 = jnp.bfloat16
     scratch = [pltpu.VMEM((UNIT, model_width), jnp.float32)]
-    if final:
-        scratch += [pltpu.VMEM((BLOCK, model_width), bf16), pltpu.VMEM((UNIT, kv_width), bf16)]
+    rows, value = (UNIT, model_width), (UNIT, kv_width)
+    shapes = [rows, value]
+    if late:
+        scratch += [pltpu.VMEM((2 * BLOCK, model_width), bf16), pltpu.VMEM(value, bf16)]
+        shapes = [rows, (BLOCK, kv_width)]
+    if len(late) > 1:
         half = lax.axis_size("dp") // 2
-        piece = BLOCK // half
-        heights = [piece] * half
-        if final == 2:
-            heights[2] += 2 * BLOCK * kv_width // model_width
-        outs = (jax.ShapeDtypeStruct((final * BLOCK, kv_width), bf16),)
-        outs += tuple(jax.ShapeDtypeStruct((rows, model_width), bf16) for rows in heights)
-    else:
-        outs = (
-            jax.ShapeDtypeStruct((UNIT, model_width), bf16),
-            jax.ShapeDtypeStruct((UNIT, kv_width), bf16),
-        )
+        shapes = [(2 * BLOCK // half, model_width)] * half
+        shapes[2] = (2 * BLOCK // half + BLOCK * kv_width // model_width, model_width)
+        shapes = [(2 * BLOCK, kv_width), (BLOCK, kv_width)] + shapes
+    parts = [part for _, part in grads]
     return pl.pallas_call(
         functools.partial(
-            tick_kernel, tick, EARLY if low else LATE, [part for _, part in grads], len(kept), final
+            tick_kernel, tick, EARLY if low else LATE, parts, len(kept), len(late)
         ),
-        out_shape=outs,
+        out_shape=tuple(jax.ShapeDtypeStruct(shape, bf16) for shape in shapes),
         in_specs=specs,
-        out_specs=(VMEM,) * len(outs),
+        out_specs=(VMEM,) * len(shapes),
         scratch_shapes=scratch,
         name=f"tick{tick}_{name}",
-        **params(0.0),
+        **params(1.0 if kept else 0.0),
     )(*operands, *after)
 
 
@@ -379,67 +381,74 @@
     )(*operands)
 
 
-def columns_kernel(
-    width, scale, first_ref, second_ref, weight_ref, gain_ref, after_ref, weight_out_ref,
-    gain_out_ref, out_ref
-):
-    me = place()[2]
-    for block, block_ref in enumerate((first_ref, second_ref)):
-        for pair in range(out_ref.shape[0] // (2 * BLOCK)):
-            row = (2 * pair + block) * BLOCK
-            out_ref[row : row + BLOCK, :] = block_ref[:, pair * width : (pair + 1) * width]
+def columns_kernel(width, distance, first_ref, second_ref, *refs):
+    out_ref = refs[-1]
+    there = lax.div(lax.bitwise_xor(place()[2], distance), 2)
+    out_ref[:BLOCK, :] = first_ref[:, columns_of(there, width)]
+    out_ref[BLOCK:, :] = second_ref[:, columns_of(there, width)]
+
+
+def columns_for(distance, blocks, after):
+    model_width = blocks[0][3].shape[1]
+    width = 2 * model_width // lax.axis_size("dp")
+    return pl.pallas_call(
+        functools.partial(columns_kernel, width, distance),
+        out_shape=jax.ShapeDtypeStruct((2 * BLOCK, width), jnp.bfloat16),
+        in_specs=[VMEM] * 2 + [ANY] * len(after),
+        out_specs=VMEM,
+        name=f"columns{distance}",
+        **params(0.0),
+    )(blocks[0][3], blocks[1][3], *after)
+
+
+def own_kernel(scale, weight_ref, gain_ref, after_ref, weight_out_ref, gain_out_ref):
     shares = weight_out_ref.shape[0]
-    first = pl.multiple_of(me * shares, shares)
+    first = pl.multiple_of(place()[2] * shares, shares)
     weight_out_ref[...] = weight_ref[pl.ds(first, shares), :].astype(jnp.float32) * scale
     gain = gain_ref[:, pl.ds(first, shares)]
     column = jnp.sum(jnp.where(diagonal(shares), gain, 0.0), axis=1, keepdims=True)
     gain_out_ref[...] = jnp.broadcast_to(column * scale, gain_out_ref.shape)
 
 
-def partial_kernel(count, shares, piece, *refs):
-    columns_ref, values = refs[0], refs[1 : 1 + count]
-    own_ref, other_ref = refs[-2:]
-    kv_width = values[0].shape[1]
-    parts = []
-    for k, ref in enumerate(values):
-        if k == 1:
-            parts += [
-                ref[piece:, first : first + kv_width] for first in range(0, ref.shape[1], kv_width)
-            ]
-        else:
-            parts.append(ref[...])
+def columns_of(pair, width):
+    return pl.ds(pl.multiple_of(pair * width, width), width)
+
+
+def partial_kernel(shares, first, *refs):
+    columns, refs = refs[:4], refs[4:]
+    own_out_ref, *other_refs = refs[6:]
+    kv_width = own_out_ref.shape[1]
+    parts = [ref[...] for ref in refs[:6]]
+    packed = refs[2]
+    parts[2:3] = [packed[first:, at : at + kv_width] for at in range(0, packed.shape[1], kv_width)]
     value = jnp.concatenate(parts, axis=0)
-    me = place()[2]
-    pair, mine = lax.div(me, 2), lax.rem(me, 2)
-    tokens = 2 * BLOCK
-    for ref, core in ((other_ref, 1 - mine), (own_ref, mine)):
+    mine = lax.rem(place()[2], 2)
+
+    def share(core):
         at = pl.ds(pl.multiple_of(core * shares, shares), shares)
-        rows = jnp.concatenate(
-            [
-                columns_ref[
-                    pl.ds(pl.multiple_of(lax.bitwise_xor(pair, k) * tokens, tokens), tokens), at
-                ]
-                for k in range(count)
-            ],
-            axis=0,
+        rows = jnp.concatenate([ref[:, at] for ref in columns], axis=0)
+        return lax.dot_general(
+            rows, value, (((0,), (0,)), ((), ())), preferred_element_type=jnp.float32
         )
-        ref[...] = lax.dot_general(
-            rows, value, (((0,), (0,)), ((), ())), preferred_element_type=jnp.float32
-        ).astype(ref.dtype)
+
+    other = share(1 - mine).astype(jnp.bfloat16)
+    for part, ref in enumerate(other_refs):
+        ref[...] = other[part * (shares // 2) : (part + 1) * (shares // 2)]
+    own_out_ref[...] = share(mine)
 
 
 def rows_kernel(half, *refs):
-    pieces = refs[: 2 * half]
+    pieces = refs[:half]
     rows_ref, token_ref, sems = refs[-3:]
     token_ref[...] = jnp.zeros_like(token_ref)
     side, at, _ = place()
-    piece = pieces[0].shape[0]
+    piece = BLOCK // half
     copies = []
     for block in range(2):
         for k in range(half):
             replica = (side if block == 0 else 1 - side) * half + lax.bitwise_xor(at, k)
             rows = pl.ds(pl.multiple_of(replica * piece, piece), piece)
-            source = pieces[block * half + k].at[pl.ds(0, piece)]
+            source = pieces[k].at[pl.ds(block * piece, piece)]
             made = pltpu.make_async_copy(source, rows_ref.at[rows], sems.at[block * half + k])
             made.start()
             copies.append(made)
@@ -453,8 +462,11 @@
     )
 
 
-def finish_kernel(own_ref, other_ref, weight_ref, gain_ref, after_ref, out_ref, gain_out_ref):
-    total = own_ref[...] + other_ref[...].astype(jnp.float32)
+def finish_kernel(
+    own_ref, first_ref, second_ref, weight_ref, gain_ref, after_ref, out_ref, gain_out_ref
+):
+    other = jnp.concatenate([first_ref[...], second_ref[...]], axis=0)
+    total = own_ref[...] + other.astype(jnp.float32)
     out_ref[...] = total * gain_ref[:, :1]
     sums = jnp.sum(total * weight_ref[...], axis=1, keepdims=True)
     gain_out_ref[...] = jnp.sum(
@@ -503,33 +515,32 @@
         grads = [(lax.ppermute(unit[-1][0], "section", hop), whole) for unit in kept]
         last = tick == layers - 1
         after, done = [kept[3][-1][0]], []
-        if last:
-            own_weight, own_gain, columns = pl.pallas_call(
-                functools.partial(columns_kernel, 2 * shares, scale),
+        if tick == layers - 2:
+            own_weight, own_gain = pl.pallas_call(
+                functools.partial(own_kernel, scale),
                 out_shape=(
                     jax.ShapeDtypeStruct((shares, kv_width), jnp.float32),
                     jax.ShapeDtypeStruct((shares, 128), jnp.float32),
-                )
-                + (jax.ShapeDtypeStruct((half * 2 * BLOCK, 2 * shares), bf16),),
-                in_specs=[VMEM] * 4 + [ANY],
-                out_specs=(VMEM,) * 3,
-                name="columns",
-                **params(0.4),
-            )(blocks[0][3], blocks[1][3], near(weight), norm_gain, kept[3][-1][0])
-            parities = [list(range(parity, replicas, 2)) for parity in range(2)]
-            columns = lax.all_to_all(
-                columns, "dp", split_axis=0, concat_axis=0, axis_index_groups=parities, tiled=True
-            )
+                ),
+                in_specs=[VMEM, VMEM, ANY],
+                out_specs=(VMEM, VMEM),
+                name="own",
+                **params(0.0),
+            )(near(weight), norm_gain, *after)
+            columns = {6: swap(columns_for(6, blocks, after + [own_gain]), 6)}
+        if last:
+            columns[2] = swap(columns_for(2, blocks, after + [columns[6]]), 2)
         for u in range(4):
             needs = grads[u - 1 : u + 1] if u % 2 else grads[u : u + 1]
             late = []
-            if last and u % 2:
-                late = list(done[u - 1]) + ([done[1][0]] if u == 3 else [])
-            if last and u == 0:
-                after = after + [columns]
+            if last and u == 1:
+                late = [done[0][1]]
             if last and u == 3:
-                rows = [done[1][1]] + [swap(done[1][1 + k], k) for k in range(1, half)]
-                after = after + rows[1:]
+                late = [done[2][1], done[0][0], done[1][0], done[2][0], done[1][1]]
+                first_values = {k: swap(done[1][1], k) for k in (2, 6)}
+                columns[0] = columns_for(0, blocks, after)
+                columns[4] = swap(columns_for(4, blocks, [done[1][0], columns[2]]), 4)
+                after = after + [columns[4], first_values[2], first_values[6]]
             done.append(
                 tick_step(
                     tick, needs, blocks[u // 2], turned, norm_gain, kept[u] if last else (), late,
@@ -538,44 +549,43 @@
             )
             after = [done[u][0]]
             kept[u].append(done[u])
-    values, *last_rows = done[3]
-    last_rows = [last_rows[0]] + [swap(last_rows[k], k) for k in range(1, half)]
-    gathered = [values, last_rows[2]] + [swap(values, 2 * k) for k in range(2, half)]
-    own, other = pl.pallas_call(
-        functools.partial(partial_kernel, half, shares, piece),
-        out_shape=(
-            jax.ShapeDtypeStruct((shares, kv_width), jnp.float32),
-            jax.ShapeDtypeStruct((shares, kv_width), bf16),
-        ),
-        in_specs=[VMEM] * (1 + half) + [ANY] * 2,
-        out_specs=(VMEM, VMEM),
+    values, last_value, *rows = done[3]
+    rows = [rows[0]] + [swap(rows[k], k) for k in range(1, half)]
+    values = [values, first_values[2], rows[2], swap(values, 4)]
+    values += [first_values[6], swap(last_value, 6)]
+    own, *other = pl.pallas_call(
+        functools.partial(partial_kernel, shares, 2 * piece),
+        out_shape=(jax.ShapeDtypeStruct((shares, kv_width), jnp.float32),)
+        + (jax.ShapeDtypeStruct((shares // 2, kv_width), bf16),) * 2,
+        in_specs=[VMEM] * 10,
+        out_specs=(VMEM,) * 3,
         name="weight_partial",
-        **params(0.5),
-    )(columns, *gathered, last_rows[1], last_rows[3])
-    other = swap(other, 1)
+        **params(0.0),
+    )(*[columns[k] for k in (0, 2, 4, 6)], *values)
+    other = [swap(part, 1) for part in other]
     input_grad, token = pl.pallas_call(
         functools.partial(rows_kernel, half),
         out_shape=(
             jax.ShapeDtypeStruct((tokens, model_width), bf16),
             jax.ShapeDtypeStruct((8, 128), jnp.float32),
         ),
-        in_specs=[VMEM] * count + [ANY],
+        in_specs=[VMEM] * half + [ANY],
         out_specs=(ANY, VMEM),
         scratch_shapes=[pltpu.SemaphoreType.DMA((count,))],
         name="rows",
-        **params(1.2),
-    )(*rows, *last_rows, own)
+        **params(0.0),
+    )(*rows, own)
     weight_grad, gain_grad = pl.pallas_call(
         finish_kernel,
         out_shape=(
             jax.ShapeDtypeStruct((shares, kv_width), jnp.float32),
             jax.ShapeDtypeStruct((1, shares), jnp.float32),
         ),
-        in_specs=[VMEM] * 4 + [ANY],
+        in_specs=[VMEM] * 5 + [ANY],
         out_specs=(VMEM, VMEM),
         name="finish",
-        **params(1.0),
-    )(own, other, own_weight, own_gain, token)
+        **params(0.0),
+    )(own, *other, own_weight, own_gain, token)
     return input_grad[None], weight_grad[None], gain_grad
 
 

time: 86.7 us -> 63.5 us (0.73)
  the two profiles are of different devices: /device:TPU:0 before, /device:TPU:9 now
where the time goes in v8:
time: 63.5 us; the launch traced here: 63.2 us
  starting transfers between devices  36.8 us (58%)
  waiting for transfers between devices  15.4 us (24%)
  Pallas kernels  9.53 us (15%)
  between operations  1.01 us (2%)
    ppermute x19, starting transfers between devices, swap(): return lax.ppermute(array, 'dp', [(i, i ^ k) for i in range(replicas)])  23.8 us
    ppermute x12, starting transfers between devices, direct(): lax.ppermute(unit[-1][0], 'section', hop)  13 us
    ppermute x19, waiting for transfers between devices, swap(): return lax.ppermute(array, 'dp', [(i, i ^ k) for i in range(replicas)])  12.3 us
    pallas_call x16, Pallas kernels, tick_step(): pl.pallas_call(functools.partial(tick_kernel, tick, EARLY if low else LAT...  3.37 us
    ppermute x12, waiting for transfers between devices, direct(): lax.ppermute(unit[-1][0], 'section', hop)  3.14 us
    pallas_call x2, Pallas kernels, pack(): pl.pallas_call(functools.partial(pack_kernel, block, half, piece), out_sh...  2.97 us
  transfers between devices with their start and end apart: 31, of which 11 were waited for; matrix products, arithmetic and copies ran while one was open for 0% of the time, Pallas kernels for 11%

profile of v8, /device:TPU:9, one launch (start us, length us, event | category | flops | bytes accessed | tf_op | source)
XLA Modules:
  0.0 63.2 jit_solution(8641427883071142363)
XLA Ops:
  0.6 1.5 %pack.3 = (bf16[16,4608]{1,0:T(8,128)(2,1)S(1)}, bf16[16,4608]{1,0:T(8,128)(2,1)S(1)}, bf16[16,4608]{1,0:T(8,128)(2,1)S(1)}, bf16[16,4608]{1,0:T(8,128)(2,1)S(1)}, bf16[80,2048]{1,0:T(8,128)(2,1)S(1)}) custom-call(bf16[128,2048]{1,0:T(8,128)(2,1)} %bitcast.8, bf16[128,512]{1,0:T(8,128)(2,1)} %bitcast.14, bf16[128,2048]{1,0:T(8,128)(2,1)} %bitcast.10, ...), custom_call_target="tpu_custom_call" | custom-call | flops 1380000000 | tf_op jit(solution)/shard_map/pack/pallas_call | solution.py:370
  2.9 1.2 %collective-permute-start.5 = (bf16[16,4608]{1,0:T(8,128)(2,1)S(1)}, bf16[16,4608]{1,0:T(8,128)(2,1)S(1)}, u32[]{:S(2)}, u32[]{:S(2)}) collective-permute-start(bf16[16,4608]{1,0:T(8,128)(2,1)S(1)} %get-tuple-element.75), channel_id=1, source_target_pairs={{0,8},{4,12},{8,0},{12,4},{16,24},{20,28},{24,16},{28,20},{1,9},{5... | collective-permute-start | bytes 442376 | tf_op jit(solution)/shard_map/ppermute | solution.py:487
  4.6 1.4 %pack.2 = (bf16[512,2048]{1,0:T(8,128)(2,1)S(1)}, bf16[16,4608]{1,0:T(8,128)(2,1)S(1)}, bf16[16,4608]{1,0:T(8,128)(2,1)S(1)}, bf16[16,4608]{1,0:T(8,128)(2,1)S(1...) custom-call(bf16[128,2048]{1,0:T(8,128)(2,1)} %bitcast.9, bf16[128,512]{1,0:T(8,128)(2,1)} %bitcast.15, ...), custom_call_target="tpu_custom_call" | custom-call | flops 1380000000 | tf_op jit(solution)/shard_map/pack/pallas_call | solution.py:370
  6.1 1.3 %collective-permute-start = (bf16[80,2048]{1,0:T(8,128)(2,1)S(1)}, bf16[80,2048]{1,0:T(8,128)(2,1)S(1)}, u32[]{:S(2)}, u32[]{:S(2)}) collective-permute-start(bf16[80,2048]{1,0:T(8,128)(2,1)S(1)} %get-tuple-element.67), channel_id=1, source_target_pairs={{0,16},{4,20},{8,24},{12,28},{16,0},{20,4},{24,8},{28,12},{1,17},{... | collective-permute-start | bytes 983048 | tf_op jit(solution)/shard_map/ppermute | solution.py:487
  7.8 1.2 %collective-permute-start.2 = (bf16[16,4608]{1,0:T(8,128)(2,1)S(1)}, bf16[16,4608]{1,0:T(8,128)(2,1)S(1)}, u32[]{:S(2)}, u32[]{:S(2)}) collective-permute-start(bf16[16,4608]{1,0:T(8,128)(2,1)S(1)} %get-tuple-element.70), channel_id=1, source_target_pairs={{0,8},{4,12},{8,0},{12,4},{16,24},{20,28},{24,16},{28,20},{1,9},{5... | collective-permute-start | bytes 442376 | tf_op jit(solution)/shard_map/ppermute | solution.py:487
  9.0 1.7 %collective-permute-start.3 = (bf16[16,4608]{1,0:T(8,128)(2,1)S(1)}, bf16[16,4608]{1,0:T(8,128)(2,1)S(1)}, u32[]{:S(2)}, u32[]{:S(2)}) collective-permute-start(bf16[16,4608]{1,0:T(8,128)(2,1)S(1)} %get-tuple-element.71), channel_id=1, source_target_pairs={{0,12},{4,8},{8,4},{12,0},{16,28},{20,24},{24,20},{28,16},{1,13},{... | collective-permute-start | bytes 442376 | tf_op jit(solution)/shard_map/ppermute | solution.py:487
  10.7 1.7 %collective-permute-done.6.refs_3_ = bf16[16,4608]{1,0:T(8,128)(2,1)S(1)} collective-permute-done((bf16[16,4608]{1,0:T(8,128)(2,1)S(1)}, bf16[16,4608]{1,0:T(8,128)(2,1)S(1)}, u32[]{:S(2)}, u32[]{:S(2)}) %collective-permute-start.6) | collective-permute-done | bytes 147488 | tf_op jit(solution)/shard_map/ppermute | solution.py:487
  14.7 3.3 %collective-permute-done.3.refs_3_ = bf16[16,4608]{1,0:T(8,128)(2,1)S(1)} collective-permute-done((bf16[16,4608]{1,0:T(8,128)(2,1)S(1)}, bf16[16,4608]{1,0:T(8,128)(2,1)S(1)}, u32[]{:S(2)}, u32[]{:S(2)}) %collective-permute-start.3) | collective-permute-done | bytes 147488 | tf_op jit(solution)/shard_map/ppermute | solution.py:487
  19.7 1.3 %collective-permute-start.11 = (bf16[32,2048]{1,0:T(8,128)(2,1)S(1)}, bf16[32,2048]{1,0:T(8,128)(2,1)S(1)}, u32[]{:S(2)}, u32[]{:S(2)}) collective-permute-start(bf16[32,2048]{1,0:T(8,128)(2,1)S(1)} %get-tuple-element.90.refs_7_.refs_8_), channel_id=1, source_target_pairs={{2,1},{6,5},{10,9},{14,13},{18,17},{22,21},{26,25},{30,29}} | collective-permute-start | bytes 393224 | tf_op jit(solution)/shard_map/ppermute | solution.py:515
  21.1 1.3 %collective-permute-start.12 = (bf16[32,2048]{1,0:T(8,128)(2,1)S(1)}, bf16[32,2048]{1,0:T(8,128)(2,1)S(1)}, u32[]{:S(2)}, u32[]{:S(2)}) collective-permute-start(bf16[32,2048]{1,0:T(8,128)(2,1)S(1)} %get-tuple-element.91.refs_6_.refs_9_), channel_id=1, source_target_pairs={{2,1},{6,5},{10,9},{14,13},{18,17},{22,21},{26,25},{30,29}} | collective-permute-start | bytes 393224 | tf_op jit(solution)/shard_map/ppermute | solution.py:515
  22.4 1.3 %collective-permute-start.10 = (bf16[32,2048]{1,0:T(8,128)(2,1)S(1)}, bf16[32,2048]{1,0:T(8,128)(2,1)S(1)}, u32[]{:S(2)}, u32[]{:S(2)}) collective-permute-start(bf16[32,2048]{1,0:T(8,128)(2,1)S(1)} %get-tuple-element.92.refs_7_.refs_8_), channel_id=1, source_target_pairs={{2,1},{6,5},{10,9},{14,13},{18,17},{22,21},{26,25},{30,29}} | collective-permute-start | bytes 393224 | tf_op jit(solution)/shard_map/ppermute | solution.py:515
  23.7 1.3 %collective-permute-start.15 = (bf16[32,2048]{1,0:T(8,128)(2,1)S(1)}, bf16[32,2048]{1,0:T(8,128)(2,1)S(1)}, u32[]{:S(2)}, u32[]{:S(2)}) collective-permute-start(bf16[32,2048]{1,0:T(8,128)(2,1)S(1)} %get-tuple-element.93.refs_6_.after_ref.refs_0_.refs_9_), channel_id=1, source_target_pairs={{2,1},{6,5},{10,9},{14,13},{18,17},{22,21},{26,25},{30,29}} | collective-permute-start | bytes 393224 | tf_op jit(solution)/shard_map/ppermute | solution.py:515
  25.2 2.2 %collective-permute-start.19 = (bf16[128,512]{1,0:T(8,128)(2,1)S(1)}, bf16[128,512]{1,0:T(8,128)(2,1)S(1)}, u32[]{:S(2)}, u32[]{:S(2)}) collective-permute-start(bf16[128,512]{1,0:T(8,128)(2,1)S(1)} %columns6.1), channel_id=1, source_target_pairs={{0,24},{4,28},{8,16},{12,20},{16,8},{20,12},{24,0},{28,4},{1,25},{... | collective-permute-start | bytes 393224 | tf_op jit(solution)/shard_map/ppermute | solution.py:487
  27.5 1.1 %collective-permute-done.11.refs_0_ = bf16[32,2048]{1,0:T(8,128)(2,1)S(1)} collective-permute-done((bf16[32,2048]{1,0:T(8,128)(2,1)S(1)}, bf16[32,2048]{1,0:T(8,128)(2,1)S(1)}, u32[]{:S(2)}, u32[]{:S(2)}) %collective-permute-start.11) | collective-permute-done | bytes 131104 | tf_op jit(solution)/shard_map/ppermute | solution.py:515
  29.3 1.3 %collective-permute-start.17 = (bf16[32,2048]{1,0:T(8,128)(2,1)S(1)}, bf16[32,2048]{1,0:T(8,128)(2,1)S(1)}, u32[]{:S(2)}, u32[]{:S(2)}) collective-permute-start(bf16[32,2048]{1,0:T(8,128)(2,1)S(1)} %get-tuple-element.94.refs_7_.refs_10_), channel_id=1, source_target_pairs={{1,0},{5,4},{9,8},{13,12},{17,16},{21,20},{25,24},{29,28}} | collective-permute-start | bytes 393224 | tf_op jit(solution)/shard_map/ppermute | solution.py:515
  31.4 0.8 %tick2_a_early.1 = (bf16[32,2048]{1,0:T(8,128)(2,1)S(1)}, bf16[32,512]{1,0:T(8,128)(2,1)S(1)}) custom-call(bf16[32,2048]{1,0:T(8,128)(2,1)S(1)} %collective-permute-done.11.refs_0_, bf16[32,2048]{1,0:T(8,128)(2,1)S(1)} %collective-permute-done.12.refs_1_, bf16[4,32,256]{2,1,0:T(8,128)(2,1)S(1)} %get-tuple-element.77.refs_2_, ...), custom_call_target="tpu_custom_call" | custom-call | tf_op jit(solution)/shard_map/tick2_a_early/pallas_call | solution.py:309
  32.2 1.3 %collective-permute-start.18 = (bf16[32,2048]{1,0:T(8,128)(2,1)S(1)}, bf16[32,2048]{1,0:T(8,128)(2,1)S(1)}, u32[]{:S(2)}, u32[]{:S(2)}) collective-permute-start(bf16[32,2048]{1,0:T(8,128)(2,1)S(1)} %get-tuple-element.95.refs_6_.refs_11_), channel_id=1, source_target_pairs={{1,0},{5,4},{9,8},{13,12},{17,16},{21,20},{25,24},{29,28}} | collective-permute-start | bytes 393224 | tf_op jit(solution)/shard_map/ppermute | solution.py:515
  34.8 1.3 %collective-permute-start.14 = (bf16[32,2048]{1,0:T(8,128)(2,1)S(1)}, bf16[32,2048]{1,0:T(8,128)(2,1)S(1)}, u32[]{:S(2)}, u32[]{:S(2)}) collective-permute-start(bf16[32,2048]{1,0:T(8,128)(2,1)S(1)} %get-tuple-element.96.refs_7_.refs_10_), channel_id=1, source_target_pairs={{1,0},{5,4},{9,8},{13,12},{17,16},{21,20},{25,24},{29,28}} | collective-permute-start | bytes 393224 | tf_op jit(solution)/shard_map/ppermute | solution.py:515
  36.9 0.8 %tick2_b_early.1 = (bf16[32,2048]{1,0:T(8,128)(2,1)S(1)}, bf16[32,512]{1,0:T(8,128)(2,1)S(1)}) custom-call(bf16[32,2048]{1,0:T(8,128)(2,1)S(1)} %collective-permute-done.10.refs_0_, bf16[32,2048]{1,0:T(8,128)(2,1)S(1)} %collective-permute-done.15.refs_1_, bf16[4,32,256]{2,1,0:T(8,128)(2,1)S(1)} %get-tuple-element.88.refs_2_, ...), custom_call_target="tpu_custom_call" | custom-call | tf_op jit(solution)/shard_map/tick2_b_early/pallas_call | solution.py:309
  37.6 1.3 %collective-permute-start.16 = (bf16[32,2048]{1,0:T(8,128)(2,1)S(1)}, bf16[32,2048]{1,0:T(8,128)(2,1)S(1)}, u32[]{:S(2)}, u32[]{:S(2)}) collective-permute-start(bf16[32,2048]{1,0:T(8,128)(2,1)S(1)} %get-tuple-element.97.refs_12_.refs_0_.refs_11_), channel_id=1, source_target_pairs={{1,0},{5,4},{9,8},{13,12},{17,16},{21,20},{25,24},{29,28}} | collective-permute-start | bytes 393224 | tf_op jit(solution)/shard_map/ppermute | solution.py:515
  39.0 1.3 %collective-permute-start.20 = (bf16[128,512]{1,0:T(8,128)(2,1)S(1)}, bf16[128,512]{1,0:T(8,128)(2,1)S(1)}, u32[]{:S(2)}, u32[]{:S(2)}) collective-permute-start(bf16[128,512]{1,0:T(8,128)(2,1)S(1)} %columns2.1), channel_id=1, source_target_pairs={{0,8},{4,12},{8,0},{12,4},{16,24},{20,28},{24,16},{28,20},{1,9},{5... | collective-permute-start | bytes 393224 | tf_op jit(solution)/shard_map/ppermute | solution.py:487
  40.4 3.1 %collective-permute-done.20.refs_1_ = bf16[128,512]{1,0:T(8,128)(2,1)S(1)} collective-permute-done((bf16[128,512]{1,0:T(8,128)(2,1)S(1)}, bf16[128,512]{1,0:T(8,128)(2,1)S(1)}, u32[]{:S(2)}, u32[]{:S(2)}) %collective-permute-start.20) | collective-permute-done | bytes 131104 | tf_op jit(solution)/shard_map/ppermute | solution.py:487
  43.5 1.3 %collective-permute-start.21 = (bf16[128,512]{1,0:T(8,128)(2,1)S(1)}, bf16[128,512]{1,0:T(8,128)(2,1)S(1)}, u32[]{:S(2)}, u32[]{:S(2)}) collective-permute-start(bf16[128,512]{1,0:T(8,128)(2,1)S(1)} %columns4.1), channel_id=1, source_target_pairs={{0,16},{4,20},{8,24},{12,28},{16,0},{20,4},{24,8},{28,12},{1,17},{... | collective-permute-start | bytes 393224 | tf_op jit(solution)/shard_map/ppermute | solution.py:487
  44.8 1.2 %collective-permute-start.23 = (bf16[64,512]{1,0:T(8,128)(2,1)S(1)}, bf16[64,512]{1,0:T(8,128)(2,1)S(1)}, u32[]{:S(2)}, u32[]{:S(2)}) collective-permute-start(bf16[64,512]{1,0:T(8,128)(2,1)S(1)} %get-tuple-element.115.refs_17_), channel_id=1, source_target_pairs={{0,24},{4,28},{8,16},{12,20},{16,8},{20,12},{24,0},{28,4},{1,25},{... | collective-permute-start | bytes 196616 | tf_op jit(solution)/shard_map/ppermute | solution.py:487
  46.2 2.7 %collective-permute-done.23.refs_21_.refs_8_ = bf16[64,512]{1,0:T(8,128)(2,1)S(1)} collective-permute-done((bf16[64,512]{1,0:T(8,128)(2,1)S(1)}, bf16[64,512]{1,0:T(8,128)(2,1)S(1)}, u32[]{:S(2)}, u32[]{:S(2)}) %collective-permute-start.23) | collective-permute-done | bytes 65568 | tf_op jit(solution)/shard_map/ppermute | solution.py:487
  49.4 0.9 %collective-permute-start.25 = (bf16[48,2048]{1,0:T(8,128)(2,1)S(1)}, bf16[48,2048]{1,0:T(8,128)(2,1)S(1)}, u32[]{:S(2)}, u32[]{:S(2)}) collective-permute-start(bf16[48,2048]{1,0:T(8,128)(2,1)S(1)} %get-tuple-element.119), channel_id=1, source_target_pairs={{0,8},{4,12},{8,0},{12,4},{16,24},{20,28},{24,16},{28,20},{1,9},{5... | collective-permute-start | bytes 589832 | tf_op jit(solution)/shard_map/ppermute | solution.py:487
  50.3 1.1 %collective-permute-start.27 = (bf16[128,512]{1,0:T(8,128)(2,1)S(1)}, bf16[128,512]{1,0:T(8,128)(2,1)S(1)}, u32[]{:S(2)}, u32[]{:S(2)}) collective-permute-start(bf16[128,512]{1,0:T(8,128)(2,1)S(1)} %get-tuple-element.121.refs_4_), channel_id=1, source_target_pairs={{0,16},{4,20},{8,24},{12,28},{16,0},{20,4},{24,8},{28,12},{1,17},{... | collective-permute-start | bytes 393224 | tf_op jit(solution)/shard_map/ppermute | solution.py:487
  52.2 3.8 %collective-permute-start.24 = (bf16[32,2048]{1,0:T(8,128)(2,1)S(1)}, bf16[32,2048]{1,0:T(8,128)(2,1)S(1)}, u32[]{:S(2)}, u32[]{:S(2)}) collective-permute-start(bf16[32,2048]{1,0:T(8,128)(2,1)S(1)} %get-tuple-element.118), channel_id=1, source_target_pairs={{0,4},{4,0},{8,12},{12,8},{16,20},{20,16},{24,28},{28,24},{1,5},{5... | collective-permute-start | bytes 393224 | tf_op jit(solution)/shard_map/ppermute | solution.py:487
  57.2 3.2 %collective-permute-start.29 = (bf16[128,512]{1,0:T(8,128)(2,1)S(1)}, bf16[128,512]{1,0:T(8,128)(2,1)S(1)}, u32[]{:S(2)}, u32[]{:S(2)}) collective-permute-start(bf16[128,512]{1,0:T(8,128)(2,1)S(1)} %get-tuple-element.125), channel_id=1, source_target_pairs={{0,4},{4,0},{8,12},{12,8},{16,20},{20,16},{24,28},{28,24},{1,5},{5... | collective-permute-start | bytes 393224 | tf_op jit(solution)/shard_map/ppermute | solution.py:487
  60.5 0.8 %collective-permute-done.26.refs_3_ = bf16[32,2048]{1,0:T(8,128)(2,1)S(1)} collective-permute-done((bf16[32,2048]{1,0:T(8,128)(2,1)S(1)}, bf16[32,2048]{1,0:T(8,128)(2,1)S(1)}, u32[]{:S(2)}, u32[]{:S(2)}) %collective-permute-start.26) | collective-permute-done | bytes 131104 | tf_op jit(solution)/shard_map/ppermute | solution.py:487
  61.3 0.8 %rows.1 = (bf16[128,2048]{1,0:T(8,128)(2,1)}, f32[8,128]{1,0:T(8,128)S(1)}) custom-call(bf16[32,2048]{1,0:T(8,128)(2,1)S(1)} %get-tuple-element.117.refs_0_, bf16[32,2048]{1,0:T(8,128)(2,1)S(1)} %collective-permute-done.24.refs_1_, bf16[48,2048]{1,0:T(8,128)(2,1)S(1)} %collective-permute-done.25.refs_6_.refs_2_, ...), custom_call_target="tpu_custom_call" | custom-call | tf_op jit(solution)/shard_map/rows/pallas_call | solution.py:566
  62.2 1.0 %finish.1 = (f32[256,512]{1,0:T(8,128)}, f32[1,256]{1,0:T(1,128)}) custom-call(f32[256,512]{1,0:T(8,128)S(1)} %get-tuple-element.123.refs_4_.own_ref, bf16[128,512]{1,0:T(8,128)(2,1)S(1)} %collective-permute-done.29.first_ref, bf16[128,512]{1,0:T(8,128)(2,1)S(1)} %collective-permute-done.30.second_ref, f32[256,512]{1,0:T(8,128)S(1)} %get-tuple-element.127.weight_ref, ...), custom_call_target="tpu_custom_call" | custom-call | tf_op jit(solution)/shard_map/finish/pallas_call | solution.py:578
  (62 shorter events, 12.3 us)
Async XLA Ops:
  0.6 4.0 %copy-start = (bf16[1,2048,512]{2,1,0:T(8,128)(2,1)S(1)}, bf16[1,2048,512]{2,1,0:T(8,128)(2,1)}, u32[]{:S(2)}) copy-start(bf16[1,2048,512]{2,1,0:T(8,128)(2,1)} %param.11) | copy-start | bytes 6291460
  2.2 5.7 %collective-permute-start.4 = (bf16[16,4608]{1,0:T(8,128)(2,1)S(1)}, bf16[16,4608]{1,0:T(8,128)(2,1)S(1)}, u32[]{:S(2)}, u32[]{:S(2)}) collective-permute-start(bf16[16,4608]{1,0:T(8,128)(2,1)S(1)} %get-tuple-element.74), channel_id=1, source_target_pairs={{0,4},{4,0},{8,12},{12,8},{16,20},{20,16},{24,28},{28,24},{1,5},{5... | collective-permute-start | bytes 442376 | tf_op jit(solution)/shard_map/ppermute | solution.py:487
  2.9 6.1 %collective-permute-start.5 = (bf16[16,4608]{1,0:T(8,128)(2,1)S(1)}, bf16[16,4608]{1,0:T(8,128)(2,1)S(1)}, u32[]{:S(2)}, u32[]{:S(2)}) collective-permute-start(bf16[16,4608]{1,0:T(8,128)(2,1)S(1)} %get-tuple-element.75), channel_id=1, source_target_pairs={{0,8},{4,12},{8,0},{12,4},{16,24},{20,28},{24,16},{28,20},{1,9},{5... | collective-permute-start | bytes 442376 | tf_op jit(solution)/shard_map/ppermute | solution.py:487
  4.1 8.3 %collective-permute-start.6 = (bf16[16,4608]{1,0:T(8,128)(2,1)S(1)}, bf16[16,4608]{1,0:T(8,128)(2,1)S(1)}, u32[]{:S(2)}, u32[]{:S(2)}) collective-permute-start(bf16[16,4608]{1,0:T(8,128)(2,1)S(1)} %get-tuple-element.76), channel_id=1, source_target_pairs={{0,12},{4,8},{8,4},{12,0},{16,28},{20,24},{24,20},{28,16},{1,13},{... | collective-permute-start | bytes 442376 | tf_op jit(solution)/shard_map/ppermute | solution.py:487
  6.1 11.9 %collective-permute-start = (bf16[80,2048]{1,0:T(8,128)(2,1)S(1)}, bf16[80,2048]{1,0:T(8,128)(2,1)S(1)}, u32[]{:S(2)}, u32[]{:S(2)}) collective-permute-start(bf16[80,2048]{1,0:T(8,128)(2,1)S(1)} %get-tuple-element.67), channel_id=1, source_target_pairs={{0,16},{4,20},{8,24},{12,28},{16,0},{20,4},{24,8},{28,12},{1,17},{... | collective-permute-start | bytes 983048 | tf_op jit(solution)/shard_map/ppermute | solution.py:487
  7.4 6.4 %collective-permute-start.1 = (bf16[16,4608]{1,0:T(8,128)(2,1)S(1)}, bf16[16,4608]{1,0:T(8,128)(2,1)S(1)}, u32[]{:S(2)}, u32[]{:S(2)}) collective-permute-start(bf16[16,4608]{1,0:T(8,128)(2,1)S(1)} %get-tuple-element.69), channel_id=1, source_target_pairs={{0,4},{4,0},{8,12},{12,8},{16,20},{20,16},{24,28},{28,24},{1,5},{5... | collective-permute-start | bytes 442376 | tf_op jit(solution)/shard_map/ppermute | solution.py:487
  7.8 6.8 %collective-permute-start.2 = (bf16[16,4608]{1,0:T(8,128)(2,1)S(1)}, bf16[16,4608]{1,0:T(8,128)(2,1)S(1)}, u32[]{:S(2)}, u32[]{:S(2)}) collective-permute-start(bf16[16,4608]{1,0:T(8,128)(2,1)S(1)} %get-tuple-element.70), channel_id=1, source_target_pairs={{0,8},{4,12},{8,0},{12,4},{16,24},{20,28},{24,16},{28,20},{1,9},{5... | collective-permute-start | bytes 442376 | tf_op jit(solution)/shard_map/ppermute | solution.py:487
  9.0 8.9 %collective-permute-start.3 = (bf16[16,4608]{1,0:T(8,128)(2,1)S(1)}, bf16[16,4608]{1,0:T(8,128)(2,1)S(1)}, u32[]{:S(2)}, u32[]{:S(2)}) collective-permute-start(bf16[16,4608]{1,0:T(8,128)(2,1)S(1)} %get-tuple-element.71), channel_id=1, source_target_pairs={{0,12},{4,8},{8,4},{12,0},{16,28},{20,24},{24,20},{28,16},{1,13},{... | collective-permute-start | bytes 442376 | tf_op jit(solution)/shard_map/ppermute | solution.py:487
  13.1 6.6 %collective-permute-start.8 = (bf16[32,2048]{1,0:T(8,128)(2,1)S(1)}, bf16[32,2048]{1,0:T(8,128)(2,1)S(1)}, u32[]{:S(2)}, u32[]{:S(2)}) collective-permute-start(bf16[32,2048]{1,0:T(8,128)(2,1)S(1)} %get-tuple-element.82.refs_7_.refs_6_), channel_id=1, source_target_pairs={{3,2},{7,6},{11,10},{15,14},{19,18},{23,22},{27,26},{31,30}} | collective-permute-start | bytes 393224 | tf_op jit(solution)/shard_map/ppermute | solution.py:515
  13.8 7.2 %collective-permute-start.9 = (bf16[32,2048]{1,0:T(8,128)(2,1)S(1)}, bf16[32,2048]{1,0:T(8,128)(2,1)S(1)}, u32[]{:S(2)}, u32[]{:S(2)}) collective-permute-start(bf16[32,2048]{1,0:T(8,128)(2,1)S(1)} %get-tuple-element.83.refs_5_.refs_7_), channel_id=1, source_target_pairs={{3,2},{7,6},{11,10},{15,14},{19,18},{23,22},{27,26},{31,30}} | collective-permute-start | bytes 393224 | tf_op jit(solution)/shard_map/ppermute | solution.py:515
  18.3 4.0 %collective-permute-start.7 = (bf16[32,2048]{1,0:T(8,128)(2,1)S(1)}, bf16[32,2048]{1,0:T(8,128)(2,1)S(1)}, u32[]{:S(2)}, u32[]{:S(2)}) collective-permute-start(bf16[32,2048]{1,0:T(8,128)(2,1)S(1)} %get-tuple-element.87.refs_7_.refs_6_), channel_id=1, source_target_pairs={{3,2},{7,6},{11,10},{15,14},{19,18},{23,22},{27,26},{31,30}} | collective-permute-start | bytes 393224 | tf_op jit(solution)/shard_map/ppermute | solution.py:515
  19.0 4.7 %collective-permute-start.13 = (bf16[32,2048]{1,0:T(8,128)(2,1)S(1)}, bf16[32,2048]{1,0:T(8,128)(2,1)S(1)}, u32[]{:S(2)}, u32[]{:S(2)}) collective-permute-start(bf16[32,2048]{1,0:T(8,128)(2,1)S(1)} %get-tuple-element.89.refs_6_.refs_7_), channel_id=1, source_target_pairs={{3,2},{7,6},{11,10},{15,14},{19,18},{23,22},{27,26},{31,30}} | collective-permute-start | bytes 393224 | tf_op jit(solution)/shard_map/ppermute | solution.py:515
  19.7 8.8 %collective-permute-start.11 = (bf16[32,2048]{1,0:T(8,128)(2,1)S(1)}, bf16[32,2048]{1,0:T(8,128)(2,1)S(1)}, u32[]{:S(2)}, u32[]{:S(2)}) collective-permute-start(bf16[32,2048]{1,0:T(8,128)(2,1)S(1)} %get-tuple-element.90.refs_7_.refs_8_), channel_id=1, source_target_pairs={{2,1},{6,5},{10,9},{14,13},{18,17},{22,21},{26,25},{30,29}} | collective-permute-start | bytes 393224 | tf_op jit(solution)/shard_map/ppermute | solution.py:515
  21.1 10.3 %collective-permute-start.12 = (bf16[32,2048]{1,0:T(8,128)(2,1)S(1)}, bf16[32,2048]{1,0:T(8,128)(2,1)S(1)}, u32[]{:S(2)}, u32[]{:S(2)}) collective-permute-start(bf16[32,2048]{1,0:T(8,128)(2,1)S(1)} %get-tuple-element.91.refs_6_.refs_9_), channel_id=1, source_target_pairs={{2,1},{6,5},{10,9},{14,13},{18,17},{22,21},{26,25},{30,29}} | collective-permute-start | bytes 393224 | tf_op jit(solution)/shard_map/ppermute | solution.py:515
  22.4 11.6 %collective-permute-start.10 = (bf16[32,2048]{1,0:T(8,128)(2,1)S(1)}, bf16[32,2048]{1,0:T(8,128)(2,1)S(1)}, u32[]{:S(2)}, u32[]{:S(2)}) collective-permute-start(bf16[32,2048]{1,0:T(8,128)(2,1)S(1)} %get-tuple-element.92.refs_7_.refs_8_), channel_id=1, source_target_pairs={{2,1},{6,5},{10,9},{14,13},{18,17},{22,21},{26,25},{30,29}} | collective-permute-start | bytes 393224 | tf_op jit(solution)/shard_map/ppermute | solution.py:515
  23.7 13.1 %collective-permute-start.15 = (bf16[32,2048]{1,0:T(8,128)(2,1)S(1)}, bf16[32,2048]{1,0:T(8,128)(2,1)S(1)}, u32[]{:S(2)}, u32[]{:S(2)}) collective-permute-start(bf16[32,2048]{1,0:T(8,128)(2,1)S(1)} %get-tuple-element.93.refs_6_.after_ref.refs_0_.refs_9_), channel_id=1, source_target_pairs={{2,1},{6,5},{10,9},{14,13},{18,17},{22,21},{26,25},{30,29}} | collective-permute-start | bytes 393224 | tf_op jit(solution)/shard_map/ppermute | solution.py:515
  25.2 13.7 %collective-permute-start.19 = (bf16[128,512]{1,0:T(8,128)(2,1)S(1)}, bf16[128,512]{1,0:T(8,128)(2,1)S(1)}, u32[]{:S(2)}, u32[]{:S(2)}) collective-permute-start(bf16[128,512]{1,0:T(8,128)(2,1)S(1)} %columns6.1), channel_id=1, source_target_pairs={{0,24},{4,28},{8,16},{12,20},{16,8},{20,12},{24,0},{28,4},{1,25},{... | collective-permute-start | bytes 393224 | tf_op jit(solution)/shard_map/ppermute | solution.py:487
  29.3 10.9 %collective-permute-start.17 = (bf16[32,2048]{1,0:T(8,128)(2,1)S(1)}, bf16[32,2048]{1,0:T(8,128)(2,1)S(1)}, u32[]{:S(2)}, u32[]{:S(2)}) collective-permute-start(bf16[32,2048]{1,0:T(8,128)(2,1)S(1)} %get-tuple-element.94.refs_7_.refs_10_), channel_id=1, source_target_pairs={{1,0},{5,4},{9,8},{13,12},{17,16},{21,20},{25,24},{29,28}} | collective-permute-start | bytes 393224 | tf_op jit(solution)/shard_map/ppermute | solution.py:515
  32.2 8.1 %collective-permute-start.18 = (bf16[32,2048]{1,0:T(8,128)(2,1)S(1)}, bf16[32,2048]{1,0:T(8,128)(2,1)S(1)}, u32[]{:S(2)}, u32[]{:S(2)}) collective-permute-start(bf16[32,2048]{1,0:T(8,128)(2,1)S(1)} %get-tuple-element.95.refs_6_.refs_11_), channel_id=1, source_target_pairs={{1,0},{5,4},{9,8},{13,12},{17,16},{21,20},{25,24},{29,28}} | collective-permute-start | bytes 393224 | tf_op jit(solution)/shard_map/ppermute | solution.py:515
  34.8 11.4 %collective-permute-start.14 = (bf16[32,2048]{1,0:T(8,128)(2,1)S(1)}, bf16[32,2048]{1,0:T(8,128)(2,1)S(1)}, u32[]{:S(2)}, u32[]{:S(2)}) collective-permute-start(bf16[32,2048]{1,0:T(8,128)(2,1)S(1)} %get-tuple-element.96.refs_7_.refs_10_), channel_id=1, source_target_pairs={{1,0},{5,4},{9,8},{13,12},{17,16},{21,20},{25,24},{29,28}} | collective-permute-start | bytes 393224 | tf_op jit(solution)/shard_map/ppermute | solution.py:515
  37.6 11.7 %collective-permute-start.16 = (bf16[32,2048]{1,0:T(8,128)(2,1)S(1)}, bf16[32,2048]{1,0:T(8,128)(2,1)S(1)}, u32[]{:S(2)}, u32[]{:S(2)}) collective-permute-start(bf16[32,2048]{1,0:T(8,128)(2,1)S(1)} %get-tuple-element.97.refs_12_.refs_0_.refs_11_), channel_id=1, source_target_pairs={{1,0},{5,4},{9,8},{13,12},{17,16},{21,20},{25,24},{29,28}} | collective-permute-start | bytes 393224 | tf_op jit(solution)/shard_map/ppermute | solution.py:515
  39.0 4.5 %collective-permute-start.20 = (bf16[128,512]{1,0:T(8,128)(2,1)S(1)}, bf16[128,512]{1,0:T(8,128)(2,1)S(1)}, u32[]{:S(2)}, u32[]{:S(2)}) collective-permute-start(bf16[128,512]{1,0:T(8,128)(2,1)S(1)} %columns2.1), channel_id=1, source_target_pairs={{0,8},{4,12},{8,0},{12,4},{16,24},{20,28},{24,16},{28,20},{1,9},{5... | collective-permute-start | bytes 393224 | tf_op jit(solution)/shard_map/ppermute | solution.py:487
  43.5 5.9 %collective-permute-start.21 = (bf16[128,512]{1,0:T(8,128)(2,1)S(1)}, bf16[128,512]{1,0:T(8,128)(2,1)S(1)}, u32[]{:S(2)}, u32[]{:S(2)}) collective-permute-start(bf16[128,512]{1,0:T(8,128)(2,1)S(1)} %columns4.1), channel_id=1, source_target_pairs={{0,16},{4,20},{8,24},{12,28},{16,0},{20,4},{24,8},{28,12},{1,17},{... | collective-permute-start | bytes 393224 | tf_op jit(solution)/shard_map/ppermute | solution.py:487
  44.8 4.1 %collective-permute-start.23 = (bf16[64,512]{1,0:T(8,128)(2,1)S(1)}, bf16[64,512]{1,0:T(8,128)(2,1)S(1)}, u32[]{:S(2)}, u32[]{:S(2)}) collective-permute-start(bf16[64,512]{1,0:T(8,128)(2,1)S(1)} %get-tuple-element.115.refs_17_), channel_id=1, source_target_pairs={{0,24},{4,28},{8,16},{12,20},{16,8},{20,12},{24,0},{28,4},{1,25},{... | collective-permute-start | bytes 196616 | tf_op jit(solution)/shard_map/ppermute | solution.py:487
  45.9 3.4 %collective-permute-start.22 = (bf16[64,512]{1,0:T(8,128)(2,1)S(1)}, bf16[64,512]{1,0:T(8,128)(2,1)S(1)}, u32[]{:S(2)}, u32[]{:S(2)}) collective-permute-start(bf16[64,512]{1,0:T(8,128)(2,1)S(1)} %get-tuple-element.115.refs_17_), channel_id=1, source_target_pairs={{0,8},{4,12},{8,0},{12,4},{16,24},{20,28},{24,16},{28,20},{1,9},{5... | collective-permute-start | bytes 196616 | tf_op jit(solution)/shard_map/ppermute | solution.py:487
  49.4 7.3 %collective-permute-start.25 = (bf16[48,2048]{1,0:T(8,128)(2,1)S(1)}, bf16[48,2048]{1,0:T(8,128)(2,1)S(1)}, u32[]{:S(2)}, u32[]{:S(2)}) collective-permute-start(bf16[48,2048]{1,0:T(8,128)(2,1)S(1)} %get-tuple-element.119), channel_id=1, source_target_pairs={{0,8},{4,12},{8,0},{12,4},{16,24},{20,28},{24,16},{28,20},{1,9},{5... | collective-permute-start | bytes 589832 | tf_op jit(solution)/shard_map/ppermute | solution.py:487
  50.3 6.4 %collective-permute-start.27 = (bf16[128,512]{1,0:T(8,128)(2,1)S(1)}, bf16[128,512]{1,0:T(8,128)(2,1)S(1)}, u32[]{:S(2)}, u32[]{:S(2)}) collective-permute-start(bf16[128,512]{1,0:T(8,128)(2,1)S(1)} %get-tuple-element.121.refs_4_), channel_id=1, source_target_pairs={{0,16},{4,20},{8,24},{12,28},{16,0},{20,4},{24,8},{28,12},{1,17},{... | collective-permute-start | bytes 393224 | tf_op jit(solution)/shard_map/ppermute | solution.py:487
  51.5 5.2 %collective-permute-start.28 = (bf16[64,512]{1,0:T(8,128)(2,1)S(1)}, bf16[64,512]{1,0:T(8,128)(2,1)S(1)}, u32[]{:S(2)}, u32[]{:S(2)}) collective-permute-start(bf16[64,512]{1,0:T(8,128)(2,1)S(1)} %get-tuple-element.122), channel_id=1, source_target_pairs={{0,24},{4,28},{8,16},{12,20},{16,8},{20,12},{24,0},{28,4},{1,25},{... | collective-permute-start | bytes 196616 | tf_op jit(solution)/shard_map/ppermute | solution.py:487
  52.2 8.3 %collective-permute-start.24 = (bf16[32,2048]{1,0:T(8,128)(2,1)S(1)}, bf16[32,2048]{1,0:T(8,128)(2,1)S(1)}, u32[]{:S(2)}, u32[]{:S(2)}) collective-permute-start(bf16[32,2048]{1,0:T(8,128)(2,1)S(1)} %get-tuple-element.118), channel_id=1, source_target_pairs={{0,4},{4,0},{8,12},{12,8},{16,20},{20,16},{24,28},{28,24},{1,5},{5... | collective-permute-start | bytes 393224 | tf_op jit(solution)/shard_map/ppermute | solution.py:487
  56.0 5.3 %collective-permute-start.26 = (bf16[32,2048]{1,0:T(8,128)(2,1)S(1)}, bf16[32,2048]{1,0:T(8,128)(2,1)S(1)}, u32[]{:S(2)}, u32[]{:S(2)}) collective-permute-start(bf16[32,2048]{1,0:T(8,128)(2,1)S(1)} %get-tuple-element.120), channel_id=1, source_target_pairs={{0,12},{4,8},{8,4},{12,0},{16,28},{20,24},{24,20},{28,16},{1,13},{... | collective-permute-start | bytes 393224 | tf_op jit(solution)/shard_map/ppermute | solution.py:487
  57.2 5.0 %collective-permute-start.29 = (bf16[128,512]{1,0:T(8,128)(2,1)S(1)}, bf16[128,512]{1,0:T(8,128)(2,1)S(1)}, u32[]{:S(2)}, u32[]{:S(2)}) collective-permute-start(bf16[128,512]{1,0:T(8,128)(2,1)S(1)} %get-tuple-element.125), channel_id=1, source_target_pairs={{0,4},{4,0},{8,12},{12,8},{16,20},{20,16},{24,28},{28,24},{1,5},{5... | collective-permute-start | bytes 393224 | tf_op jit(solution)/shard_map/ppermute | solution.py:487
  60.4 1.8 %collective-permute-start.30 = (bf16[128,512]{1,0:T(8,128)(2,1)S(1)}, bf16[128,512]{1,0:T(8,128)(2,1)S(1)}, u32[]{:S(2)}, u32[]{:S(2)}) collective-permute-start(bf16[128,512]{1,0:T(8,128)(2,1)S(1)} %get-tuple-element.126), channel_id=1, source_target_pairs={{0,4},{4,0},{8,12},{12,8},{16,20},{20,16},{24,28},{28,24},{1,5},{5... | collective-permute-start | bytes 393224 | tf_op jit(solution)/shard_map/ppermute | solution.py:487
  (1 other events, 0.7 us)

commit v9 on v8

--- a/solution.py
+++ b/solution.py
@@ -437,10 +437,15 @@
     own_out_ref[...] = share(mine)
 
 
-def rows_kernel(half, *refs):
+def diagonal(size):
+    return lax.broadcasted_iota(jnp.int32, (size, size), 0) == lax.broadcasted_iota(
+        jnp.int32, (size, size), 1
+    )
+
+
+def finish_kernel(half, own_ref, first_ref, second_ref, weight_ref, gain_ref, *refs):
     pieces = refs[:half]
-    rows_ref, token_ref, sems = refs[-3:]
-    token_ref[...] = jnp.zeros_like(token_ref)
+    rows_ref, out_ref, gain_out_ref, sems = refs[half:]
     side, at, _ = place()
     piece = BLOCK // half
     copies = []
@@ -452,19 +457,6 @@
             made = pltpu.make_async_copy(source, rows_ref.at[rows], sems.at[block * half + k])
             made.start()
             copies.append(made)
-    for made in copies:
-        made.wait()
-
-
-def diagonal(size):
-    return lax.broadcasted_iota(jnp.int32, (size, size), 0) == lax.broadcasted_iota(
-        jnp.int32, (size, size), 1
-    )
-
-
-def finish_kernel(
-    own_ref, first_ref, second_ref, weight_ref, gain_ref, after_ref, out_ref, gain_out_ref
-):
     other = jnp.concatenate([first_ref[...], second_ref[...]], axis=0)
     total = own_ref[...] + other.astype(jnp.float32)
     out_ref[...] = total * gain_ref[:, :1]
@@ -472,6 +464,8 @@
     gain_out_ref[...] = jnp.sum(
         jnp.where(diagonal(total.shape[0]), sums, 0.0), axis=0, keepdims=True
     )
+    for made in copies:
+        made.wait()
 
 
 def direct(hidden, query, key, segments, weight, norm_gain, upstream):
@@ -529,7 +523,8 @@
             )(near(weight), norm_gain, *after)
             columns = {6: swap(columns_for(6, blocks, after + [own_gain]), 6)}
         if last:
-            columns[2] = swap(columns_for(2, blocks, after + [columns[6]]), 2)
+            waits = after + [columns[6]]
+            columns.update({k: swap(columns_for(k, blocks, waits), k) for k in (2, 4)})
         for u in range(4):
             needs = grads[u - 1 : u + 1] if u % 2 else grads[u : u + 1]
             late = []
@@ -539,8 +534,7 @@
                 late = [done[2][1], done[0][0], done[1][0], done[2][0], done[1][1]]
                 first_values = {k: swap(done[1][1], k) for k in (2, 6)}
                 columns[0] = columns_for(0, blocks, after)
-                columns[4] = swap(columns_for(4, blocks, [done[1][0], columns[2]]), 4)
-                after = after + [columns[4], first_values[2], first_values[6]]
+                after = after + [columns[2], columns[4], first_values[2], first_values[6]]
             done.append(
                 tick_step(
                     tick, needs, blocks[u // 2], turned, norm_gain, kept[u] if last else (), late,
@@ -563,29 +557,19 @@
         **params(0.0),
     )(*[columns[k] for k in (0, 2, 4, 6)], *values)
     other = [swap(part, 1) for part in other]
-    input_grad, token = pl.pallas_call(
-        functools.partial(rows_kernel, half),
+    input_grad, weight_grad, gain_grad = pl.pallas_call(
+        functools.partial(finish_kernel, half),
         out_shape=(
             jax.ShapeDtypeStruct((tokens, model_width), bf16),
-            jax.ShapeDtypeStruct((8, 128), jnp.float32),
-        ),
-        in_specs=[VMEM] * half + [ANY],
-        out_specs=(ANY, VMEM),
-        scratch_shapes=[pltpu.SemaphoreType.DMA((count,))],
-        name="rows",
-        **params(0.0),
-    )(*rows, own)
-    weight_grad, gain_grad = pl.pallas_call(
-        finish_kernel,
-        out_shape=(
             jax.ShapeDtypeStruct((shares, kv_width), jnp.float32),
             jax.ShapeDtypeStruct((1, shares), jnp.float32),
         ),
-        in_specs=[VMEM] * 5 + [ANY],
-        out_specs=(VMEM, VMEM),
+        in_specs=[VMEM] * (5 + half),
+        out_specs=(ANY, VMEM, VMEM),
+        scratch_shapes=[pltpu.SemaphoreType.DMA((count,))],
         name="finish",
         **params(0.0),
-    )(own, *other, own_weight, own_gain, token)
+    )(own, *other, own_weight, own_gain, *rows)
     return input_grad[None], weight_grad[None], gain_grad
 
 

time: 63.5 us -> 61 us (0.961)
  the two profiles are of different devices: /device:TPU:9 before, /device:TPU:0 now
where the time goes in v9:
time: 61 us; the launch traced here: 60.7 us
  starting transfers between devices  31 us (51%)
  waiting for transfers between devices  18.7 us (31%)
  Pallas kernels  9.48 us (16%)
  between operations  1.02 us (2%)
    ppermute x19, starting transfers between devices, swap(): return lax.ppermute(array, 'dp', [(i, i ^ k) for i in range(replicas)])  20.5 us
    ppermute x19, waiting for transfers between devices, swap(): return lax.ppermute(array, 'dp', [(i, i ^ k) for i in range(replicas)])  13.2 us
    ppermute x12, starting transfers between devices, direct(): lax.ppermute(unit[-1][0], 'section', hop)  10.5 us
    ppermute x12, waiting for transfers between devices, direct(): lax.ppermute(unit[-1][0], 'section', hop)  5.5 us
    pallas_call x16, Pallas kernels, tick_step(): pl.pallas_call(functools.partial(tick_kernel, tick, EARLY if low else LAT...  3.42 us
    pallas_call x2, Pallas kernels, pack(): pl.pallas_call(functools.partial(pack_kernel, block, half, piece), out_sh...  2.97 us
    pallas_call x1, Pallas kernels, direct(): pl.pallas_call(functools.partial(finish_kernel, half), out_shape=(jax.Sha...  1.74 us
  transfers between devices with their start and end apart: 31, of which 10 were waited for; matrix products, arithmetic and copies ran while one was open for 0% of the time, Pallas kernels for 9%

profile of v9, /device:TPU:0, one launch (start us, length us, event | category | flops | bytes accessed | tf_op | source)
XLA Modules:
  0.0 60.7 jit_solution(17153813612774468940)
XLA Ops:
  0.6 1.5 %pack.2 = (bf16[16,4608]{1,0:T(8,128)(2,1)S(1)}, bf16[16,4608]{1,0:T(8,128)(2,1)S(1)}, bf16[16,4608]{1,0:T(8,128)(2,1)S(1)}, bf16[16,4608]{1,0:T(8,128)(2,1)S(1)}, bf16[80,2048]{1,0:T(8,128)(2,1)S(1)}) custom-call(bf16[128,2048]{1,0:T(8,128)(2,1)} %bitcast.8, bf16[128,512]{1,0:T(8,128)(2,1)} %bitcast.14, bf16[128,2048]{1,0:T(8,128)(2,1)} %bitcast.10, ...), custom_call_target="tpu_custom_call" | custom-call | flops 1380000000 | tf_op jit(solution)/shard_map/pack/pallas_call | solution.py:370
  2.7 2.6 %collective-permute-start.1 = (bf16[16,4608]{1,0:T(8,128)(2,1)S(1)}, bf16[16,4608]{1,0:T(8,128)(2,1)S(1)}, u32[]{:S(2)}, u32[]{:S(2)}) collective-permute-start(bf16[16,4608]{1,0:T(8,128)(2,1)S(1)} %get-tuple-element.68), channel_id=1, source_target_pairs={{0,8},{4,12},{8,0},{12,4},{16,24},{20,28},{24,16},{28,20},{1,9},{5... | collective-permute-start | bytes 442376 | tf_op jit(solution)/shard_map/ppermute | solution.py:481
  5.3 1.4 %pack.3 = (bf16[512,2048]{1,0:T(8,128)(2,1)S(1)}, bf16[16,4608]{1,0:T(8,128)(2,1)S(1)}, bf16[16,4608]{1,0:T(8,128)(2,1)S(1)}, bf16[16,4608]{1,0:T(8,128)(2,1)S(1...) custom-call(bf16[128,2048]{1,0:T(8,128)(2,1)} %bitcast.9, bf16[128,512]{1,0:T(8,128)(2,1)} %bitcast.15, ...), custom_call_target="tpu_custom_call" | custom-call | flops 1380000000 | tf_op jit(solution)/shard_map/pack/pallas_call | solution.py:370
  6.8 1.8 %collective-permute-start.6 = (bf16[80,2048]{1,0:T(8,128)(2,1)S(1)}, bf16[80,2048]{1,0:T(8,128)(2,1)S(1)}, u32[]{:S(2)}, u32[]{:S(2)}) collective-permute-start(bf16[80,2048]{1,0:T(8,128)(2,1)S(1)} %get-tuple-element.76), channel_id=1, source_target_pairs={{0,16},{4,20},{8,24},{12,28},{16,0},{20,4},{24,8},{28,12},{1,17},{... | collective-permute-start | bytes 983048 | tf_op jit(solution)/shard_map/ppermute | solution.py:481
  8.7 1.5 %collective-permute-start.4 = (bf16[16,4608]{1,0:T(8,128)(2,1)S(1)}, bf16[16,4608]{1,0:T(8,128)(2,1)S(1)}, u32[]{:S(2)}, u32[]{:S(2)}) collective-permute-start(bf16[16,4608]{1,0:T(8,128)(2,1)S(1)} %get-tuple-element.74), channel_id=1, source_target_pairs={{0,8},{4,12},{8,0},{12,4},{16,24},{20,28},{24,16},{28,20},{1,9},{5... | collective-permute-start | bytes 442376 | tf_op jit(solution)/shard_map/ppermute | solution.py:481
  10.7 1.9 %collective-permute-done.2.refs_3_ = bf16[16,4608]{1,0:T(8,128)(2,1)S(1)} collective-permute-done((bf16[16,4608]{1,0:T(8,128)(2,1)S(1)}, bf16[16,4608]{1,0:T(8,128)(2,1)S(1)}, u32[]{:S(2)}, u32[]{:S(2)}) %collective-permute-start.2) | collective-permute-done | bytes 147488 | tf_op jit(solution)/shard_map/ppermute | solution.py:481
  14.7 1.6 %collective-permute-done.4.refs_2_ = bf16[16,4608]{1,0:T(8,128)(2,1)S(1)} collective-permute-done((bf16[16,4608]{1,0:T(8,128)(2,1)S(1)}, bf16[16,4608]{1,0:T(8,128)(2,1)S(1)}, u32[]{:S(2)}, u32[]{:S(2)}) %collective-permute-start.4) | collective-permute-done | bytes 147488 | tf_op jit(solution)/shard_map/ppermute | solution.py:481
  16.3 2.6 %collective-permute-done.5.refs_3_ = bf16[16,4608]{1,0:T(8,128)(2,1)S(1)} collective-permute-done((bf16[16,4608]{1,0:T(8,128)(2,1)S(1)}, bf16[16,4608]{1,0:T(8,128)(2,1)S(1)}, u32[]{:S(2)}, u32[]{:S(2)}) %collective-permute-start.5) | collective-permute-done | bytes 147488 | tf_op jit(solution)/shard_map/ppermute | solution.py:481
  21.4 0.7 %collective-permute-start.12 = (bf16[32,2048]{1,0:T(8,128)(2,1)S(1)}, bf16[32,2048]{1,0:T(8,128)(2,1)S(1)}, u32[]{:S(2)}, u32[]{:S(2)}) collective-permute-start(bf16[32,2048]{1,0:T(8,128)(2,1)S(1)} %get-tuple-element.90.refs_6_.refs_9_), channel_id=1, source_target_pairs={{2,1},{6,5},{10,9},{14,13},{18,17},{22,21},{26,25},{30,29}} | collective-permute-start | bytes 393224 | tf_op jit(solution)/shard_map/ppermute | solution.py:509
  22.8 0.7 %collective-permute-start.17 = (bf16[32,2048]{1,0:T(8,128)(2,1)S(1)}, bf16[32,2048]{1,0:T(8,128)(2,1)S(1)}, u32[]{:S(2)}, u32[]{:S(2)}) collective-permute-start(bf16[32,2048]{1,0:T(8,128)(2,1)S(1)} %get-tuple-element.92.refs_6_.after_ref.refs_0_.refs_9_), channel_id=1, source_target_pairs={{2,1},{6,5},{10,9},{14,13},{18,17},{22,21},{26,25},{30,29}} | collective-permute-start | bytes 393224 | tf_op jit(solution)/shard_map/ppermute | solution.py:509
  23.7 2.6 %collective-permute-start.18 = (bf16[128,512]{1,0:T(8,128)(2,1)S(1)}, bf16[128,512]{1,0:T(8,128)(2,1)S(1)}, u32[]{:S(2)}, u32[]{:S(2)}) collective-permute-start(bf16[128,512]{1,0:T(8,128)(2,1)S(1)} %columns6.1), channel_id=1, source_target_pairs={{0,24},{4,28},{8,16},{12,20},{16,8},{20,12},{24,0},{28,4},{1,25},{... | collective-permute-start | bytes 393224 | tf_op jit(solution)/shard_map/ppermute | solution.py:481
  26.3 1.3 %collective-permute-start.15 = (bf16[32,2048]{1,0:T(8,128)(2,1)S(1)}, bf16[32,2048]{1,0:T(8,128)(2,1)S(1)}, u32[]{:S(2)}, u32[]{:S(2)}) collective-permute-start(bf16[32,2048]{1,0:T(8,128)(2,1)S(1)} %get-tuple-element.93.refs_7_.refs_10_), channel_id=1, source_target_pairs={{1,0},{5,4},{9,8},{13,12},{17,16},{21,20},{25,24},{29,28}} | collective-permute-start | bytes 393224 | tf_op jit(solution)/shard_map/ppermute | solution.py:509
  27.6 1.3 %collective-permute-start.16 = (bf16[32,2048]{1,0:T(8,128)(2,1)S(1)}, bf16[32,2048]{1,0:T(8,128)(2,1)S(1)}, u32[]{:S(2)}, u32[]{:S(2)}) collective-permute-start(bf16[32,2048]{1,0:T(8,128)(2,1)S(1)} %get-tuple-element.94.refs_6_.refs_11_), channel_id=1, source_target_pairs={{1,0},{5,4},{9,8},{13,12},{17,16},{21,20},{25,24},{29,28}} | collective-permute-start | bytes 393224 | tf_op jit(solution)/shard_map/ppermute | solution.py:509
  28.9 1.3 %collective-permute-start.14 = (bf16[32,2048]{1,0:T(8,128)(2,1)S(1)}, bf16[32,2048]{1,0:T(8,128)(2,1)S(1)}, u32[]{:S(2)}, u32[]{:S(2)}) collective-permute-start(bf16[32,2048]{1,0:T(8,128)(2,1)S(1)} %get-tuple-element.95.refs_7_.refs_10_), channel_id=1, source_target_pairs={{1,0},{5,4},{9,8},{13,12},{17,16},{21,20},{25,24},{29,28}} | collective-permute-start | bytes 393224 | tf_op jit(solution)/shard_map/ppermute | solution.py:509
  30.3 1.3 %collective-permute-start.21 = (bf16[32,2048]{1,0:T(8,128)(2,1)S(1)}, bf16[32,2048]{1,0:T(8,128)(2,1)S(1)}, u32[]{:S(2)}, u32[]{:S(2)}) collective-permute-start(bf16[32,2048]{1,0:T(8,128)(2,1)S(1)} %get-tuple-element.105.refs_12_.refs_0_.refs_11_), channel_id=1, source_target_pairs={{1,0},{5,4},{9,8},{13,12},{17,16},{21,20},{25,24},{29,28}} | collective-permute-start | bytes 393224 | tf_op jit(solution)/shard_map/ppermute | solution.py:509
  32.2 4.9 %collective-permute-done.15.refs_0_ = bf16[32,2048]{1,0:T(8,128)(2,1)S(1)} collective-permute-done((bf16[32,2048]{1,0:T(8,128)(2,1)S(1)}, bf16[32,2048]{1,0:T(8,128)(2,1)S(1)}, u32[]{:S(2)}, u32[]{:S(2)}) %collective-permute-start.15) | collective-permute-done | bytes 131104 | tf_op jit(solution)/shard_map/ppermute | solution.py:509
  37.1 1.5 %collective-permute-start.20 = (bf16[128,512]{1,0:T(8,128)(2,1)S(1)}, bf16[128,512]{1,0:T(8,128)(2,1)S(1)}, u32[]{:S(2)}, u32[]{:S(2)}) collective-permute-start(bf16[128,512]{1,0:T(8,128)(2,1)S(1)} %columns4.1), channel_id=1, source_target_pairs={{0,16},{4,20},{8,24},{12,28},{16,0},{20,4},{24,8},{28,12},{1,17},{... | collective-permute-start | bytes 393224 | tf_op jit(solution)/shard_map/ppermute | solution.py:481
  38.7 0.8 %tick3_a_late.1 = (bf16[32,2048]{1,0:T(8,128)(2,1)S(1)}, bf16[32,512]{1,0:T(8,128)(2,1)S(1)}) custom-call(bf16[32,2048]{1,0:T(8,128)(2,1)S(1)} %collective-permute-done.15.refs_0_, bf16[4,32,128]{2,1,0:T(8,128)(2,1)S(1)} %get-tuple-element.80.refs_1_, f32[64,128]{1,0:T(8,128)S(1)} %get-tuple-element.78.refs_2_.refs_3_, ...), custom_call_target="tpu_custom_call" | custom-call | flops 1150000000 | tf_op jit(solution)/shard_map/tick3_a_late/pallas_call | solution.py:309
  40.0 0.8 %tick3_a_early.1 = (bf16[32,2048]{1,0:T(8,128)(2,1)S(1)}, bf16[64,512]{1,0:T(8,128)(2,1)S(1)}) custom-call(bf16[32,2048]{1,0:T(8,128)(2,1)S(1)} %collective-permute-done.15.refs_0_, bf16[32,2048]{1,0:T(8,128)(2,1)S(1)} %collective-permute-done.16.refs_1_, bf16[4,32,256]{2,1,0:T(8,128)(2,1)S(1)} %get-tuple-element.77.refs_2_, ...), custom_call_target="tpu_custom_call" | custom-call | flops 1150000000 | tf_op jit(solution)/shard_map/tick3_a_early/pallas_call | solution.py:309
  40.8 2.5 %collective-permute-start.23 = (bf16[64,512]{1,0:T(8,128)(2,1)S(1)}, bf16[64,512]{1,0:T(8,128)(2,1)S(1)}, u32[]{:S(2)}, u32[]{:S(2)}) collective-permute-start(bf16[64,512]{1,0:T(8,128)(2,1)S(1)} %get-tuple-element.115.refs_17_), channel_id=1, source_target_pairs={{0,24},{4,28},{8,16},{12,20},{16,8},{20,12},{24,0},{28,4},{1,25},{... | collective-permute-start | bytes 196616 | tf_op jit(solution)/shard_map/ppermute | solution.py:481
  43.3 1.0 %collective-permute-start.22 = (bf16[64,512]{1,0:T(8,128)(2,1)S(1)}, bf16[64,512]{1,0:T(8,128)(2,1)S(1)}, u32[]{:S(2)}, u32[]{:S(2)}) collective-permute-start(bf16[64,512]{1,0:T(8,128)(2,1)S(1)} %get-tuple-element.115.refs_17_), channel_id=1, source_target_pairs={{0,8},{4,12},{8,0},{12,4},{16,24},{20,28},{24,16},{28,20},{1,9},{5... | collective-permute-start | bytes 196616 | tf_op jit(solution)/shard_map/ppermute | solution.py:481
  44.3 0.8 %tick3_b_late.1 = (bf16[32,2048]{1,0:T(8,128)(2,1)S(1)}, bf16[32,512]{1,0:T(8,128)(2,1)S(1)}) custom-call(bf16[32,2048]{1,0:T(8,128)(2,1)S(1)} %collective-permute-done.14.refs_0_, bf16[4,32,128]{2,1,0:T(8,128)(2,1)S(1)} %get-tuple-element.84.refs_1_, f32[64,128]{1,0:T(8,128)S(1)} %get-tuple-element.85.refs_2_.refs_3_, ...), custom_call_target="tpu_custom_call" | custom-call | flops 1150000000 | tf_op jit(solution)/shard_map/tick3_b_late/pallas_call | solution.py:309
  45.1 1.5 %collective-permute-done.23.refs_22_.refs_8_ = bf16[64,512]{1,0:T(8,128)(2,1)S(1)} collective-permute-done((bf16[64,512]{1,0:T(8,128)(2,1)S(1)}, bf16[64,512]{1,0:T(8,128)(2,1)S(1)}, u32[]{:S(2)}, u32[]{:S(2)}) %collective-permute-start.23) | collective-permute-done | bytes 65568 | tf_op jit(solution)/shard_map/ppermute | solution.py:481
  46.6 1.0 %collective-permute-done.22.refs_21_.refs_5_ = bf16[64,512]{1,0:T(8,128)(2,1)S(1)} collective-permute-done((bf16[64,512]{1,0:T(8,128)(2,1)S(1)}, bf16[64,512]{1,0:T(8,128)(2,1)S(1)}, u32[]{:S(2)}, u32[]{:S(2)}) %collective-permute-start.22) | collective-permute-done | bytes 65568 | tf_op jit(solution)/shard_map/ppermute | solution.py:481
  47.6 0.9 %tick3_b_early.1 = (bf16[128,512]{1,0:T(8,128)(2,1)S(1)}, bf16[64,512]{1,0:T(8,128)(2,1)S(1)}, bf16[32,2048]{1,0:T(8,128)(2,1)S(1)}, bf16[32,2048]{1,0:T(8,128)(...) custom-call(bf16[32,2048]{1,0:T(8,128)(2,1)S(1)} %collective-permute-done.14.refs_0_, ...), custom_call_target="tpu_custom_call" | custom-call | flops 1150000000 | tf_op jit(solution)/shard_map/tick3_b_early/pallas_call | solution.py:309
  48.5 1.0 %collective-permute-start.24 = (bf16[48,2048]{1,0:T(8,128)(2,1)S(1)}, bf16[48,2048]{1,0:T(8,128)(2,1)S(1)}, u32[]{:S(2)}, u32[]{:S(2)}) collective-permute-start(bf16[48,2048]{1,0:T(8,128)(2,1)S(1)} %get-tuple-element.117), channel_id=1, source_target_pairs={{0,8},{4,12},{8,0},{12,4},{16,24},{20,28},{24,16},{28,20},{1,9},{5... | collective-permute-start | bytes 589832 | tf_op jit(solution)/shard_map/ppermute | solution.py:481
  49.6 1.5 %collective-permute-start.25 = (bf16[128,512]{1,0:T(8,128)(2,1)S(1)}, bf16[128,512]{1,0:T(8,128)(2,1)S(1)}, u32[]{:S(2)}, u32[]{:S(2)}) collective-permute-start(bf16[128,512]{1,0:T(8,128)(2,1)S(1)} %get-tuple-element.116.refs_4_), channel_id=1, source_target_pairs={{0,16},{4,20},{8,24},{12,28},{16,0},{20,4},{24,8},{28,12},{1,17},{... | collective-permute-start | bytes 393224 | tf_op jit(solution)/shard_map/ppermute | solution.py:481
  51.1 1.0 %collective-permute-start.26 = (bf16[64,512]{1,0:T(8,128)(2,1)S(1)}, bf16[64,512]{1,0:T(8,128)(2,1)S(1)}, u32[]{:S(2)}, u32[]{:S(2)}) collective-permute-start(bf16[64,512]{1,0:T(8,128)(2,1)S(1)} %get-tuple-element.118), channel_id=1, source_target_pairs={{0,24},{4,28},{8,16},{12,20},{16,8},{20,12},{24,0},{28,4},{1,25},{... | collective-permute-start | bytes 196616 | tf_op jit(solution)/shard_map/ppermute | solution.py:481
  52.2 1.1 %collective-permute-start.30 = (bf16[32,2048]{1,0:T(8,128)(2,1)S(1)}, bf16[32,2048]{1,0:T(8,128)(2,1)S(1)}, u32[]{:S(2)}, u32[]{:S(2)}) collective-permute-start(bf16[32,2048]{1,0:T(8,128)(2,1)S(1)} %get-tuple-element.125), channel_id=1, source_target_pairs={{0,12},{4,8},{8,4},{12,0},{16,28},{20,24},{24,20},{28,16},{1,13},{... | collective-permute-start | bytes 393224 | tf_op jit(solution)/shard_map/ppermute | solution.py:481
  53.3 3.6 %collective-permute-done.26.refs_9_ = bf16[64,512]{1,0:T(8,128)(2,1)S(1)} collective-permute-done((bf16[64,512]{1,0:T(8,128)(2,1)S(1)}, bf16[64,512]{1,0:T(8,128)(2,1)S(1)}, u32[]{:S(2)}, u32[]{:S(2)}) %collective-permute-start.26) | collective-permute-done | bytes 65568 | tf_op jit(solution)/shard_map/ppermute | solution.py:481
  57.9 0.8 %collective-permute-done.27.first_ref = bf16[128,512]{1,0:T(8,128)(2,1)S(1)} collective-permute-done((bf16[128,512]{1,0:T(8,128)(2,1)S(1)}, bf16[128,512]{1,0:T(8,128)(2,1)S(1)}, u32[]{:S(2)}, u32[]{:S(2)}) %collective-permute-start.27) | collective-permute-done | bytes 131104 | tf_op jit(solution)/shard_map/ppermute | solution.py:481
  58.9 1.7 %finish.1 = (bf16[128,2048]{1,0:T(8,128)(2,1)}, f32[256,512]{1,0:T(8,128)}, f32[1,256]{1,0:T(1,128)}) custom-call(f32[256,512]{1,0:T(8,128)S(1)} %get-tuple-element.119.own_ref, bf16[128,512]{1,0:T(8,128)(2,1)S(1)} %collective-permute-done.27.first_ref, bf16[128,512]{1,0:T(8,128)(2,1)S(1)} %collective-permute-done.28.second_ref, ...), custom_call_target="tpu_custom_call" | custom-call | tf_op jit(solution)/shard_map/finish/pallas_call | solution.py:560
  (61 shorter events, 9.1 us)
Async XLA Ops:
  0.6 4.7 %copy-start = (bf16[1,2048,512]{2,1,0:T(8,128)(2,1)S(1)}, bf16[1,2048,512]{2,1,0:T(8,128)(2,1)}, u32[]{:S(2)}) copy-start(bf16[1,2048,512]{2,1,0:T(8,128)(2,1)} %param.11) | copy-start | bytes 6291460
  2.2 6.5 %collective-permute-start = (bf16[16,4608]{1,0:T(8,128)(2,1)S(1)}, bf16[16,4608]{1,0:T(8,128)(2,1)S(1)}, u32[]{:S(2)}, u32[]{:S(2)}) collective-permute-start(bf16[16,4608]{1,0:T(8,128)(2,1)S(1)} %get-tuple-element.67), channel_id=1, source_target_pairs={{0,4},{4,0},{8,12},{12,8},{16,20},{20,16},{24,28},{28,24},{1,5},{5... | collective-permute-start | bytes 442376 | tf_op jit(solution)/shard_map/ppermute | solution.py:481
  2.7 7.5 %collective-permute-start.1 = (bf16[16,4608]{1,0:T(8,128)(2,1)S(1)}, bf16[16,4608]{1,0:T(8,128)(2,1)S(1)}, u32[]{:S(2)}, u32[]{:S(2)}) collective-permute-start(bf16[16,4608]{1,0:T(8,128)(2,1)S(1)} %get-tuple-element.68), channel_id=1, source_target_pairs={{0,8},{4,12},{8,0},{12,4},{16,24},{20,28},{24,16},{28,20},{1,9},{5... | collective-permute-start | bytes 442376 | tf_op jit(solution)/shard_map/ppermute | solution.py:481
  5.3 7.3 %collective-permute-start.2 = (bf16[16,4608]{1,0:T(8,128)(2,1)S(1)}, bf16[16,4608]{1,0:T(8,128)(2,1)S(1)}, u32[]{:S(2)}, u32[]{:S(2)}) collective-permute-start(bf16[16,4608]{1,0:T(8,128)(2,1)S(1)} %get-tuple-element.69), channel_id=1, source_target_pairs={{0,12},{4,8},{8,4},{12,0},{16,28},{20,24},{24,20},{28,16},{1,13},{... | collective-permute-start | bytes 442376 | tf_op jit(solution)/shard_map/ppermute | solution.py:481
  6.8 12.1 %collective-permute-start.6 = (bf16[80,2048]{1,0:T(8,128)(2,1)S(1)}, bf16[80,2048]{1,0:T(8,128)(2,1)S(1)}, u32[]{:S(2)}, u32[]{:S(2)}) collective-permute-start(bf16[80,2048]{1,0:T(8,128)(2,1)S(1)} %get-tuple-element.76), channel_id=1, source_target_pairs={{0,16},{4,20},{8,24},{12,28},{16,0},{20,4},{24,8},{28,12},{1,17},{... | collective-permute-start | bytes 983048 | tf_op jit(solution)/shard_map/ppermute | solution.py:481
  8.6 5.4 %collective-permute-start.3 = (bf16[16,4608]{1,0:T(8,128)(2,1)S(1)}, bf16[16,4608]{1,0:T(8,128)(2,1)S(1)}, u32[]{:S(2)}, u32[]{:S(2)}) collective-permute-start(bf16[16,4608]{1,0:T(8,128)(2,1)S(1)} %get-tuple-element.73), channel_id=1, source_target_pairs={{0,4},{4,0},{8,12},{12,8},{16,20},{20,16},{24,28},{28,24},{1,5},{5... | collective-permute-start | bytes 442376 | tf_op jit(solution)/shard_map/ppermute | solution.py:481
  8.7 7.6 %collective-permute-start.4 = (bf16[16,4608]{1,0:T(8,128)(2,1)S(1)}, bf16[16,4608]{1,0:T(8,128)(2,1)S(1)}, u32[]{:S(2)}, u32[]{:S(2)}) collective-permute-start(bf16[16,4608]{1,0:T(8,128)(2,1)S(1)} %get-tuple-element.74), channel_id=1, source_target_pairs={{0,8},{4,12},{8,0},{12,4},{16,24},{20,28},{24,16},{28,20},{1,9},{5... | collective-permute-start | bytes 442376 | tf_op jit(solution)/shard_map/ppermute | solution.py:481
  10.2 8.7 %collective-permute-start.5 = (bf16[16,4608]{1,0:T(8,128)(2,1)S(1)}, bf16[16,4608]{1,0:T(8,128)(2,1)S(1)}, u32[]{:S(2)}, u32[]{:S(2)}) collective-permute-start(bf16[16,4608]{1,0:T(8,128)(2,1)S(1)} %get-tuple-element.75), channel_id=1, source_target_pairs={{0,12},{4,8},{8,4},{12,0},{16,28},{20,24},{24,20},{28,16},{1,13},{... | collective-permute-start | bytes 442376 | tf_op jit(solution)/shard_map/ppermute | solution.py:481
  13.3 7.4 %collective-permute-start.8 = (bf16[32,2048]{1,0:T(8,128)(2,1)S(1)}, bf16[32,2048]{1,0:T(8,128)(2,1)S(1)}, u32[]{:S(2)}, u32[]{:S(2)}) collective-permute-start(bf16[32,2048]{1,0:T(8,128)(2,1)S(1)} %get-tuple-element.81.refs_7_.refs_6_), channel_id=1, source_target_pairs={{3,2},{7,6},{11,10},{15,14},{19,18},{23,22},{27,26},{31,30}} | collective-permute-start | bytes 393224 | tf_op jit(solution)/shard_map/ppermute | solution.py:509
  14.0 7.4 %collective-permute-start.9 = (bf16[32,2048]{1,0:T(8,128)(2,1)S(1)}, bf16[32,2048]{1,0:T(8,128)(2,1)S(1)}, u32[]{:S(2)}, u32[]{:S(2)}) collective-permute-start(bf16[32,2048]{1,0:T(8,128)(2,1)S(1)} %get-tuple-element.82.refs_5_.refs_7_), channel_id=1, source_target_pairs={{3,2},{7,6},{11,10},{15,14},{19,18},{23,22},{27,26},{31,30}} | collective-permute-start | bytes 393224 | tf_op jit(solution)/shard_map/ppermute | solution.py:509
  19.3 2.8 %collective-permute-start.7 = (bf16[32,2048]{1,0:T(8,128)(2,1)S(1)}, bf16[32,2048]{1,0:T(8,128)(2,1)S(1)}, u32[]{:S(2)}, u32[]{:S(2)}) collective-permute-start(bf16[32,2048]{1,0:T(8,128)(2,1)S(1)} %get-tuple-element.86.refs_7_.refs_6_), channel_id=1, source_target_pairs={{3,2},{7,6},{11,10},{15,14},{19,18},{23,22},{27,26},{31,30}} | collective-permute-start | bytes 393224 | tf_op jit(solution)/shard_map/ppermute | solution.py:509
  20.0 2.8 %collective-permute-start.13 = (bf16[32,2048]{1,0:T(8,128)(2,1)S(1)}, bf16[32,2048]{1,0:T(8,128)(2,1)S(1)}, u32[]{:S(2)}, u32[]{:S(2)}) collective-permute-start(bf16[32,2048]{1,0:T(8,128)(2,1)S(1)} %get-tuple-element.88.refs_6_.refs_7_), channel_id=1, source_target_pairs={{3,2},{7,6},{11,10},{15,14},{19,18},{23,22},{27,26},{31,30}} | collective-permute-start | bytes 393224 | tf_op jit(solution)/shard_map/ppermute | solution.py:509
  20.7 5.6 %collective-permute-start.11 = (bf16[32,2048]{1,0:T(8,128)(2,1)S(1)}, bf16[32,2048]{1,0:T(8,128)(2,1)S(1)}, u32[]{:S(2)}, u32[]{:S(2)}) collective-permute-start(bf16[32,2048]{1,0:T(8,128)(2,1)S(1)} %get-tuple-element.89.refs_7_.refs_8_), channel_id=1, source_target_pairs={{2,1},{6,5},{10,9},{14,13},{18,17},{22,21},{26,25},{30,29}} | collective-permute-start | bytes 393224 | tf_op jit(solution)/shard_map/ppermute | solution.py:509
  21.4 6.2 %collective-permute-start.12 = (bf16[32,2048]{1,0:T(8,128)(2,1)S(1)}, bf16[32,2048]{1,0:T(8,128)(2,1)S(1)}, u32[]{:S(2)}, u32[]{:S(2)}) collective-permute-start(bf16[32,2048]{1,0:T(8,128)(2,1)S(1)} %get-tuple-element.90.refs_6_.refs_9_), channel_id=1, source_target_pairs={{2,1},{6,5},{10,9},{14,13},{18,17},{22,21},{26,25},{30,29}} | collective-permute-start | bytes 393224 | tf_op jit(solution)/shard_map/ppermute | solution.py:509
  22.1 6.8 %collective-permute-start.10 = (bf16[32,2048]{1,0:T(8,128)(2,1)S(1)}, bf16[32,2048]{1,0:T(8,128)(2,1)S(1)}, u32[]{:S(2)}, u32[]{:S(2)}) collective-permute-start(bf16[32,2048]{1,0:T(8,128)(2,1)S(1)} %get-tuple-element.91.refs_7_.refs_8_), channel_id=1, source_target_pairs={{2,1},{6,5},{10,9},{14,13},{18,17},{22,21},{26,25},{30,29}} | collective-permute-start | bytes 393224 | tf_op jit(solution)/shard_map/ppermute | solution.py:509
  22.8 7.4 %collective-permute-start.17 = (bf16[32,2048]{1,0:T(8,128)(2,1)S(1)}, bf16[32,2048]{1,0:T(8,128)(2,1)S(1)}, u32[]{:S(2)}, u32[]{:S(2)}) collective-permute-start(bf16[32,2048]{1,0:T(8,128)(2,1)S(1)} %get-tuple-element.92.refs_6_.after_ref.refs_0_.refs_9_), channel_id=1, source_target_pairs={{2,1},{6,5},{10,9},{14,13},{18,17},{22,21},{26,25},{30,29}} | collective-permute-start | bytes 393224 | tf_op jit(solution)/shard_map/ppermute | solution.py:509
  23.7 7.9 %collective-permute-start.18 = (bf16[128,512]{1,0:T(8,128)(2,1)S(1)}, bf16[128,512]{1,0:T(8,128)(2,1)S(1)}, u32[]{:S(2)}, u32[]{:S(2)}) collective-permute-start(bf16[128,512]{1,0:T(8,128)(2,1)S(1)} %columns6.1), channel_id=1, source_target_pairs={{0,24},{4,28},{8,16},{12,20},{16,8},{20,12},{24,0},{28,4},{1,25},{... | collective-permute-start | bytes 393224 | tf_op jit(solution)/shard_map/ppermute | solution.py:481
  26.3 10.9 %collective-permute-start.15 = (bf16[32,2048]{1,0:T(8,128)(2,1)S(1)}, bf16[32,2048]{1,0:T(8,128)(2,1)S(1)}, u32[]{:S(2)}, u32[]{:S(2)}) collective-permute-start(bf16[32,2048]{1,0:T(8,128)(2,1)S(1)} %get-tuple-element.93.refs_7_.refs_10_), channel_id=1, source_target_pairs={{1,0},{5,4},{9,8},{13,12},{17,16},{21,20},{25,24},{29,28}} | collective-permute-start | bytes 393224 | tf_op jit(solution)/shard_map/ppermute | solution.py:509
  27.6 12.4 %collective-permute-start.16 = (bf16[32,2048]{1,0:T(8,128)(2,1)S(1)}, bf16[32,2048]{1,0:T(8,128)(2,1)S(1)}, u32[]{:S(2)}, u32[]{:S(2)}) collective-permute-start(bf16[32,2048]{1,0:T(8,128)(2,1)S(1)} %get-tuple-element.94.refs_6_.refs_11_), channel_id=1, source_target_pairs={{1,0},{5,4},{9,8},{13,12},{17,16},{21,20},{25,24},{29,28}} | collective-permute-start | bytes 393224 | tf_op jit(solution)/shard_map/ppermute | solution.py:509
  28.9 14.4 %collective-permute-start.14 = (bf16[32,2048]{1,0:T(8,128)(2,1)S(1)}, bf16[32,2048]{1,0:T(8,128)(2,1)S(1)}, u32[]{:S(2)}, u32[]{:S(2)}) collective-permute-start(bf16[32,2048]{1,0:T(8,128)(2,1)S(1)} %get-tuple-element.95.refs_7_.refs_10_), channel_id=1, source_target_pairs={{1,0},{5,4},{9,8},{13,12},{17,16},{21,20},{25,24},{29,28}} | collective-permute-start | bytes 393224 | tf_op jit(solution)/shard_map/ppermute | solution.py:509
  30.3 17.3 %collective-permute-start.21 = (bf16[32,2048]{1,0:T(8,128)(2,1)S(1)}, bf16[32,2048]{1,0:T(8,128)(2,1)S(1)}, u32[]{:S(2)}, u32[]{:S(2)}) collective-permute-start(bf16[32,2048]{1,0:T(8,128)(2,1)S(1)} %get-tuple-element.105.refs_12_.refs_0_.refs_11_), channel_id=1, source_target_pairs={{1,0},{5,4},{9,8},{13,12},{17,16},{21,20},{25,24},{29,28}} | collective-permute-start | bytes 393224 | tf_op jit(solution)/shard_map/ppermute | solution.py:509
  31.6 16.0 %collective-permute-start.19 = (bf16[128,512]{1,0:T(8,128)(2,1)S(1)}, bf16[128,512]{1,0:T(8,128)(2,1)S(1)}, u32[]{:S(2)}, u32[]{:S(2)}) collective-permute-start(bf16[128,512]{1,0:T(8,128)(2,1)S(1)} %columns2.1), channel_id=1, source_target_pairs={{0,8},{4,12},{8,0},{12,4},{16,24},{20,28},{24,16},{28,20},{1,9},{5... | collective-permute-start | bytes 393224 | tf_op jit(solution)/shard_map/ppermute | solution.py:481
  37.1 10.5 %collective-permute-start.20 = (bf16[128,512]{1,0:T(8,128)(2,1)S(1)}, bf16[128,512]{1,0:T(8,128)(2,1)S(1)}, u32[]{:S(2)}, u32[]{:S(2)}) collective-permute-start(bf16[128,512]{1,0:T(8,128)(2,1)S(1)} %columns4.1), channel_id=1, source_target_pairs={{0,16},{4,20},{8,24},{12,28},{16,0},{20,4},{24,8},{28,12},{1,17},{... | collective-permute-start | bytes 393224 | tf_op jit(solution)/shard_map/ppermute | solution.py:481
  40.8 5.8 %collective-permute-start.23 = (bf16[64,512]{1,0:T(8,128)(2,1)S(1)}, bf16[64,512]{1,0:T(8,128)(2,1)S(1)}, u32[]{:S(2)}, u32[]{:S(2)}) collective-permute-start(bf16[64,512]{1,0:T(8,128)(2,1)S(1)} %get-tuple-element.115.refs_17_), channel_id=1, source_target_pairs={{0,24},{4,28},{8,16},{12,20},{16,8},{20,12},{24,0},{28,4},{1,25},{... | collective-permute-start | bytes 196616 | tf_op jit(solution)/shard_map/ppermute | solution.py:481
  43.3 4.3 %collective-permute-start.22 = (bf16[64,512]{1,0:T(8,128)(2,1)S(1)}, bf16[64,512]{1,0:T(8,128)(2,1)S(1)}, u32[]{:S(2)}, u32[]{:S(2)}) collective-permute-start(bf16[64,512]{1,0:T(8,128)(2,1)S(1)} %get-tuple-element.115.refs_17_), channel_id=1, source_target_pairs={{0,8},{4,12},{8,0},{12,4},{16,24},{20,28},{24,16},{28,20},{1,9},{5... | collective-permute-start | bytes 196616 | tf_op jit(solution)/shard_map/ppermute | solution.py:481
  48.5 8.3 %collective-permute-start.24 = (bf16[48,2048]{1,0:T(8,128)(2,1)S(1)}, bf16[48,2048]{1,0:T(8,128)(2,1)S(1)}, u32[]{:S(2)}, u32[]{:S(2)}) collective-permute-start(bf16[48,2048]{1,0:T(8,128)(2,1)S(1)} %get-tuple-element.117), channel_id=1, source_target_pairs={{0,8},{4,12},{8,0},{12,4},{16,24},{20,28},{24,16},{28,20},{1,9},{5... | collective-permute-start | bytes 589832 | tf_op jit(solution)/shard_map/ppermute | solution.py:481
  49.6 7.3 %collective-permute-start.25 = (bf16[128,512]{1,0:T(8,128)(2,1)S(1)}, bf16[128,512]{1,0:T(8,128)(2,1)S(1)}, u32[]{:S(2)}, u32[]{:S(2)}) collective-permute-start(bf16[128,512]{1,0:T(8,128)(2,1)S(1)} %get-tuple-element.116.refs_4_), channel_id=1, source_target_pairs={{0,16},{4,20},{8,24},{12,28},{16,0},{20,4},{24,8},{28,12},{1,17},{... | collective-permute-start | bytes 393224 | tf_op jit(solution)/shard_map/ppermute | solution.py:481
  51.1 5.7 %collective-permute-start.26 = (bf16[64,512]{1,0:T(8,128)(2,1)S(1)}, bf16[64,512]{1,0:T(8,128)(2,1)S(1)}, u32[]{:S(2)}, u32[]{:S(2)}) collective-permute-start(bf16[64,512]{1,0:T(8,128)(2,1)S(1)} %get-tuple-element.118), channel_id=1, source_target_pairs={{0,24},{4,28},{8,16},{12,20},{16,8},{20,12},{24,0},{28,4},{1,25},{... | collective-permute-start | bytes 196616 | tf_op jit(solution)/shard_map/ppermute | solution.py:481
  52.1 5.8 %collective-permute-start.29 = (bf16[32,2048]{1,0:T(8,128)(2,1)S(1)}, bf16[32,2048]{1,0:T(8,128)(2,1)S(1)}, u32[]{:S(2)}, u32[]{:S(2)}) collective-permute-start(bf16[32,2048]{1,0:T(8,128)(2,1)S(1)} %get-tuple-element.124), channel_id=1, source_target_pairs={{0,4},{4,0},{8,12},{12,8},{16,20},{20,16},{24,28},{28,24},{1,5},{5... | collective-permute-start | bytes 393224 | tf_op jit(solution)/shard_map/ppermute | solution.py:481
  52.2 5.7 %collective-permute-start.30 = (bf16[32,2048]{1,0:T(8,128)(2,1)S(1)}, bf16[32,2048]{1,0:T(8,128)(2,1)S(1)}, u32[]{:S(2)}, u32[]{:S(2)}) collective-permute-start(bf16[32,2048]{1,0:T(8,128)(2,1)S(1)} %get-tuple-element.125), channel_id=1, source_target_pairs={{0,12},{4,8},{8,4},{12,0},{16,28},{20,24},{24,20},{28,16},{1,13},{... | collective-permute-start | bytes 393224 | tf_op jit(solution)/shard_map/ppermute | solution.py:481
  57.3 1.4 %collective-permute-start.27 = (bf16[128,512]{1,0:T(8,128)(2,1)S(1)}, bf16[128,512]{1,0:T(8,128)(2,1)S(1)}, u32[]{:S(2)}, u32[]{:S(2)}) collective-permute-start(bf16[128,512]{1,0:T(8,128)(2,1)S(1)} %get-tuple-element.120), channel_id=1, source_target_pairs={{0,4},{4,0},{8,12},{12,8},{16,20},{20,16},{24,28},{28,24},{1,5},{5... | collective-permute-start | bytes 393224 | tf_op jit(solution)/shard_map/ppermute | solution.py:481
  57.4 1.5 %collective-permute-start.28 = (bf16[128,512]{1,0:T(8,128)(2,1)S(1)}, bf16[128,512]{1,0:T(8,128)(2,1)S(1)}, u32[]{:S(2)}, u32[]{:S(2)}) collective-permute-start(bf16[128,512]{1,0:T(8,128)(2,1)S(1)} %get-tuple-element.121), channel_id=1, source_target_pairs={{0,4},{4,0},{8,12},{12,8},{16,20},{20,16},{24,28},{28,24},{1,5},{5... | collective-permute-start | bytes 393224 | tf_op jit(solution)/shard_map/ppermute | solution.py:481
  (1 other events, 0.7 us)

commit v10 on v9

--- a/solution.py
+++ b/solution.py
@@ -12,7 +12,7 @@
 UNIT = 32
 EPSILON = 1e-06
 MASKED = -1e30
-OUTS = {1: 2, 5: 6}
+OUTS = {2: 3, 5: 6}
 UNITS = ("a_late", "a_early", "b_late", "b_early")
 VMEM = pl.BlockSpec(memory_space=pltpu.VMEM)
 SMEM = pl.BlockSpec(memory_space=pltpu.SMEM)
@@ -231,18 +231,17 @@
     kv_width, model_width = turned_ref.shape
     turn = lax.axis_size("section") - 1 - lax.axis_index("section")
     if late:
-        outs, (scaled_ref, blocks_ref, value_ref) = refs[-3 - OUTS[late] : -3], refs[-3:]
+        outs, (scaled_ref, blocks_ref, value_ref) = refs[late : -3], refs[-3:]
+        outs = outs[len(outs) - OUTS[late] :]
     else:
         outs, scaled_ref = refs[-3:-1], refs[-1]
         value_ref = outs[1]
-    if late > 1:
-
-        def store(columns, part):
-            blocks_ref[BLOCK : BLOCK + UNIT, columns] = part
-
-    else:
-
-        def store(columns, part):
+    first_row = BLOCK if late > 2 else 0
+
+    def store(columns, part):
+        if late:
+            blocks_ref[first_row : first_row + UNIT, columns] = part
+        if late <= 2:
             outs[0][:, columns] = part
 
     @pl.when(turn == tick)
@@ -259,29 +258,32 @@
             store(slice(None), earlier[2 * at][...])
             value_ref[...] = earlier[2 * at + 1][...]
 
-    if late:
-        values = jnp.concatenate([value_ref[...], late_refs[0][...]], axis=0)
-        outs[1][...] = values
-    if late > 1:
-        late_a_ref, early_a_ref, late_b_ref, value_a_ref = late_refs[1:]
+    if not late:
+        return
+    values = jnp.concatenate([value_ref[...], late_refs[0][...]], axis=0)
+    blocks_ref[first_row + UNIT : first_row + BLOCK, :] = late_refs[1][...]
+    outs[1][...] = values
+    if late > 2:
+        late_a_ref, early_a_ref, value_a_ref = late_refs[2:]
+        blocks_ref[EARLY, :] = early_a_ref[...]
+        blocks_ref[LATE, :] = late_a_ref[...]
         outs[0][:BLOCK, :] = value_a_ref[...]
         outs[0][BLOCK:, :] = values
-        blocks_ref[EARLY, :] = early_a_ref[...]
-        blocks_ref[LATE, :] = late_a_ref[...]
-        blocks_ref[BLOCK + UNIT :, :] = late_b_ref[...]
-        at = place()[1]
-        half = len(outs) - 2
-        piece = BLOCK // half
-        for k, out_ref in enumerate(outs[2:]):
-            first = pl.multiple_of(lax.bitwise_xor(at, k) * piece, piece)
+    at = place()[1]
+    pieces = {2: outs[2]} if late == 2 else dict(enumerate(outs[2:]))
+    piece = BLOCK * kv_width // model_width
+    for k, out_ref in pieces.items():
+        first = pl.multiple_of(lax.bitwise_xor(at, k) * piece, piece)
+        here = blocks_ref[pl.ds(first_row + first, piece), :]
+        if k == 2:
+            out_ref[:piece, :] = here
+            for g in range(model_width // kv_width):
+                out_ref[piece:, g * kv_width : (g + 1) * kv_width] = values[
+                    g * piece : (g + 1) * piece
+                ]
+        else:
             out_ref[:piece, :] = blocks_ref[pl.ds(first, piece), :]
-            out_ref[piece : 2 * piece, :] = blocks_ref[pl.ds(BLOCK + first, piece), :]
-        groups = model_width // kv_width
-        share = BLOCK // groups
-        for g in range(groups):
-            outs[4][2 * piece :, g * kv_width : (g + 1) * kv_width] = values[
-                g * share : (g + 1) * share
-            ]
+            out_ref[piece:, :] = here
 
 
 def tick_step(tick, grads, block, turned, gain, kept=(), late=(), after=(), name=""):
@@ -298,13 +300,12 @@
     rows, value = (UNIT, model_width), (UNIT, kv_width)
     shapes = [rows, value]
     if late:
+        half = lax.axis_size("dp") // 2
         scratch += [pltpu.VMEM((2 * BLOCK, model_width), bf16), pltpu.VMEM(value, bf16)]
-        shapes = [rows, (BLOCK, kv_width)]
-    if len(late) > 1:
-        half = lax.axis_size("dp") // 2
-        shapes = [(2 * BLOCK // half, model_width)] * half
-        shapes[2] = (2 * BLOCK // half + BLOCK * kv_width // model_width, model_width)
-        shapes = [(2 * BLOCK, kv_width), (BLOCK, kv_width)] + shapes
+        pieces = (2 * BLOCK // half, model_width)
+        shapes = [rows, (BLOCK, kv_width), pieces]
+    if len(late) > 2:
+        shapes = [(2 * BLOCK, kv_width), (BLOCK, kv_width)] + [pieces] * half
     parts = [part for _, part in grads]
     return pl.pallas_call(
         functools.partial(
@@ -418,9 +419,10 @@
     columns, refs = refs[:4], refs[4:]
     own_out_ref, *other_refs = refs[6:]
     kv_width = own_out_ref.shape[1]
-    parts = [ref[...] for ref in refs[:6]]
-    packed = refs[2]
-    parts[2:3] = [packed[first:, at : at + kv_width] for at in range(0, packed.shape[1], kv_width)]
+    parts = []
+    for ref in refs[:6]:
+        for at in range(0, ref.shape[1], kv_width):
+            parts.append(ref[first:, at : at + kv_width] if ref.shape[1] > kv_width else ref[...])
     value = jnp.concatenate(parts, axis=0)
     mine = lax.rem(place()[2], 2)
 
@@ -444,25 +446,35 @@
 
 
 def finish_kernel(half, own_ref, first_ref, second_ref, weight_ref, gain_ref, *refs):
-    pieces = refs[:half]
-    rows_ref, out_ref, gain_out_ref, sems = refs[half:]
+    first_rows_ref, pieces = refs[0], refs[1 : 1 + half]
+    rows_ref, out_ref, gain_out_ref, sums_ref, sems = refs[1 + half :]
     side, at, _ = place()
     piece = BLOCK // half
     copies = []
+
+    def copy(source, target):
+        made = pltpu.make_async_copy(source, target, sems.at[len(copies)])
+        made.start()
+        copies.append(made)
+
     for block in range(2):
         for k in range(half):
             replica = (side if block == 0 else 1 - side) * half + lax.bitwise_xor(at, k)
             rows = pl.ds(pl.multiple_of(replica * piece, piece), piece)
-            source = pieces[k].at[pl.ds(block * piece, piece)]
-            made = pltpu.make_async_copy(source, rows_ref.at[rows], sems.at[block * half + k])
-            made.start()
-            copies.append(made)
-    other = jnp.concatenate([first_ref[...], second_ref[...]], axis=0)
-    total = own_ref[...] + other.astype(jnp.float32)
-    out_ref[...] = total * gain_ref[:, :1]
-    sums = jnp.sum(total * weight_ref[...], axis=1, keepdims=True)
+            source, first = pieces[k], block * piece
+            if k == 2:
+                source, first = (pieces[k] if block else first_rows_ref), 0
+            copy(source.at[pl.ds(first, piece)], rows_ref.at[rows])
+    shares = own_ref.shape[0]
+    gain_sums = []
+    for part, ref in enumerate((first_ref, second_ref)):
+        rows = slice(part * (shares // 2), (part + 1) * (shares // 2))
+        total = own_ref[rows, :] + ref[...].astype(jnp.float32)
+        sums_ref[rows, :] = total * gain_ref[rows, :1]
+        copy(sums_ref.at[rows], out_ref.at[rows])
+        gain_sums.append(jnp.sum(total * weight_ref[rows, :], axis=1, keepdims=True))
     gain_out_ref[...] = jnp.sum(
-        jnp.where(diagonal(total.shape[0]), sums, 0.0), axis=0, keepdims=True
+        jnp.where(diagonal(shares), jnp.concatenate(gain_sums, axis=0), 0.0), axis=0, keepdims=True
     )
     for made in copies:
         made.wait()
@@ -529,12 +541,11 @@
             needs = grads[u - 1 : u + 1] if u % 2 else grads[u : u + 1]
             late = []
             if last and u == 1:
-                late = [done[0][1]]
+                late = [done[0][1], done[0][0]]
             if last and u == 3:
-                late = [done[2][1], done[0][0], done[1][0], done[2][0], done[1][1]]
-                first_values = {k: swap(done[1][1], k) for k in (2, 6)}
-                columns[0] = columns_for(0, blocks, after)
-                after = after + [columns[2], columns[4], first_values[2], first_values[6]]
+                late = [done[2][1], done[2][0], done[0][0], done[1][0], done[1][1]]
+                first_value, first_rows = swap(done[1][1], 6), swap(done[1][2], 2)
+                after = after + [columns[2], columns[4], first_value]
             done.append(
                 tick_step(
                     tick, needs, blocks[u // 2], turned, norm_gain, kept[u] if last else (), late,
@@ -545,10 +556,10 @@
             kept[u].append(done[u])
     values, last_value, *rows = done[3]
     rows = [rows[0]] + [swap(rows[k], k) for k in range(1, half)]
-    values = [values, first_values[2], rows[2], swap(values, 4)]
-    values += [first_values[6], swap(last_value, 6)]
+    columns[0] = columns_for(0, blocks, [values, first_rows])
+    values = [values, first_rows, rows[2], swap(values, 4), first_value, swap(last_value, 6)]
     own, *other = pl.pallas_call(
-        functools.partial(partial_kernel, shares, 2 * piece),
+        functools.partial(partial_kernel, shares, piece),
         out_shape=(jax.ShapeDtypeStruct((shares, kv_width), jnp.float32),)
         + (jax.ShapeDtypeStruct((shares // 2, kv_width), bf16),) * 2,
         in_specs=[VMEM] * 10,
@@ -564,12 +575,15 @@
             jax.ShapeDtypeStruct((shares, kv_width), jnp.float32),
             jax.ShapeDtypeStruct((1, shares), jnp.float32),
         ),
-        in_specs=[VMEM] * (5 + half),
-        out_specs=(ANY, VMEM, VMEM),
-        scratch_shapes=[pltpu.SemaphoreType.DMA((count,))],
+        in_specs=[VMEM] * (6 + half),
+        out_specs=(ANY, ANY, VMEM),
+        scratch_shapes=[
+            pltpu.VMEM((shares, kv_width), jnp.float32),
+            pltpu.SemaphoreType.DMA((count + 2,)),
+        ],
         name="finish",
         **params(0.0),
-    )(own, *other, own_weight, own_gain, *rows)
+    )(own, *other, own_weight, own_gain, first_rows, *rows)
     return input_grad[None], weight_grad[None], gain_grad
 
 

time: 61 us -> 60.5 us (level)
  waiting for transfers between devices: 18.7 us -> 17.8 us
    ppermute x19, waiting for transfers between devices: 13.2 us -> 12.3 us  [swap(): return lax.ppermute(array, 'dp', [(i, i ^ k) for i in range(replicas)])]
  transfers between devices with their start and end apart: 31 -> 31, of which waited for: 10 -> 9; matrix products, arithmetic and copies ran while one was open for 0% -> 0% of each run, Pallas kernels for 9% -> 10%
where the time goes in v10:
time: 60.5 us; the launch traced here: 60.1 us
  starting transfers between devices  31.5 us (52%)
  waiting for transfers between devices  17.8 us (29%)
  Pallas kernels  9.46 us (16%)
  between operations  1.01 us (2%)
    ppermute x19, starting transfers between devices, swap(): return lax.ppermute(array, 'dp', [(i, i ^ k) for i in range(replicas)])  21 us
    ppermute x19, waiting for transfers between devices, swap(): return lax.ppermute(array, 'dp', [(i, i ^ k) for i in range(replicas)])  12.3 us
    ppermute x12, starting transfers between devices, direct(): lax.ppermute(unit[-1][0], 'section', hop)  10.5 us
    ppermute x12, waiting for transfers between devices, direct(): lax.ppermute(unit[-1][0], 'section', hop)  5.51 us
    pallas_call x16, Pallas kernels, tick_step(): pl.pallas_call(functools.partial(tick_kernel, tick, EARLY if low else LAT...  3.44 us
    pallas_call x2, Pallas kernels, pack(): pl.pallas_call(functools.partial(pack_kernel, block, half, piece), out_sh...  2.97 us
    pallas_call x1, Pallas kernels, direct(): pl.pallas_call(functools.partial(finish_kernel, half), out_shape=(jax.Sha...  1.7 us
  transfers between devices with their start and end apart: 31, of which 9 were waited for; matrix products, arithmetic and copies ran while one was open for 0% of the time, Pallas kernels for 10%

profile of v10, /device:TPU:0, one launch (start us, length us, event | category | flops | bytes accessed | tf_op | source)
XLA Modules:
  0.0 60.1 jit_solution(16466360595073428510)
XLA Ops:
  0.6 1.5 %pack.2 = (bf16[16,4608]{1,0:T(8,128)(2,1)S(1)}, bf16[16,4608]{1,0:T(8,128)(2,1)S(1)}, bf16[16,4608]{1,0:T(8,128)(2,1)S(1)}, bf16[16,4608]{1,0:T(8,128)(2,1)S(1)}, bf16[80,2048]{1,0:T(8,128)(2,1)S(1)}) custom-call(bf16[128,2048]{1,0:T(8,128)(2,1)} %bitcast.8, bf16[128,512]{1,0:T(8,128)(2,1)} %bitcast.14, bf16[128,2048]{1,0:T(8,128)(2,1)} %bitcast.10, ...), custom_call_target="tpu_custom_call" | custom-call | flops 1380000000 | tf_op jit(solution)/shard_map/pack/pallas_call | solution.py:371
  2.7 2.6 %collective-permute-start.1 = (bf16[16,4608]{1,0:T(8,128)(2,1)S(1)}, bf16[16,4608]{1,0:T(8,128)(2,1)S(1)}, u32[]{:S(2)}, u32[]{:S(2)}) collective-permute-start(bf16[16,4608]{1,0:T(8,128)(2,1)S(1)} %get-tuple-element.69), channel_id=1, source_target_pairs={{0,8},{4,12},{8,0},{12,4},{16,24},{20,28},{24,16},{28,20},{1,9},{5... | collective-permute-start | bytes 442376 | tf_op jit(solution)/shard_map/ppermute | solution.py:493
  5.3 1.4 %pack.3 = (bf16[512,2048]{1,0:T(8,128)(2,1)S(1)}, bf16[16,4608]{1,0:T(8,128)(2,1)S(1)}, bf16[16,4608]{1,0:T(8,128)(2,1)S(1)}, bf16[16,4608]{1,0:T(8,128)(2,1)S(1...) custom-call(bf16[128,2048]{1,0:T(8,128)(2,1)} %bitcast.9, bf16[128,512]{1,0:T(8,128)(2,1)} %bitcast.15, ...), custom_call_target="tpu_custom_call" | custom-call | flops 1380000000 | tf_op jit(solution)/shard_map/pack/pallas_call | solution.py:371
  6.8 1.8 %collective-permute-start.6 = (bf16[80,2048]{1,0:T(8,128)(2,1)S(1)}, bf16[80,2048]{1,0:T(8,128)(2,1)S(1)}, u32[]{:S(2)}, u32[]{:S(2)}) collective-permute-start(bf16[80,2048]{1,0:T(8,128)(2,1)S(1)} %get-tuple-element.77), channel_id=1, source_target_pairs={{0,16},{4,20},{8,24},{12,28},{16,0},{20,4},{24,8},{28,12},{1,17},{... | collective-permute-start | bytes 983048 | tf_op jit(solution)/shard_map/ppermute | solution.py:493
  8.7 1.5 %collective-permute-start.4 = (bf16[16,4608]{1,0:T(8,128)(2,1)S(1)}, bf16[16,4608]{1,0:T(8,128)(2,1)S(1)}, u32[]{:S(2)}, u32[]{:S(2)}) collective-permute-start(bf16[16,4608]{1,0:T(8,128)(2,1)S(1)} %get-tuple-element.75), channel_id=1, source_target_pairs={{0,8},{4,12},{8,0},{12,4},{16,24},{20,28},{24,16},{28,20},{1,9},{5... | collective-permute-start | bytes 442376 | tf_op jit(solution)/shard_map/ppermute | solution.py:493
  10.7 1.9 %collective-permute-done.2.refs_3_ = bf16[16,4608]{1,0:T(8,128)(2,1)S(1)} collective-permute-done((bf16[16,4608]{1,0:T(8,128)(2,1)S(1)}, bf16[16,4608]{1,0:T(8,128)(2,1)S(1)}, u32[]{:S(2)}, u32[]{:S(2)}) %collective-permute-start.2) | collective-permute-done | bytes 147488 | tf_op jit(solution)/shard_map/ppermute | solution.py:493
  14.0 0.7 %collective-permute-start.9 = (bf16[32,2048]{1,0:T(8,128)(2,1)S(1)}, bf16[32,2048]{1,0:T(8,128)(2,1)S(1)}, u32[]{:S(2)}, u32[]{:S(2)}) collective-permute-start(bf16[32,2048]{1,0:T(8,128)(2,1)S(1)} %get-tuple-element.83.refs_5_.refs_7_), channel_id=1, source_target_pairs={{3,2},{7,6},{11,10},{15,14},{19,18},{23,22},{27,26},{31,30}} | collective-permute-start | bytes 393224 | tf_op jit(solution)/shard_map/ppermute | solution.py:521
  14.7 1.6 %collective-permute-done.4.refs_2_ = bf16[16,4608]{1,0:T(8,128)(2,1)S(1)} collective-permute-done((bf16[16,4608]{1,0:T(8,128)(2,1)S(1)}, bf16[16,4608]{1,0:T(8,128)(2,1)S(1)}, u32[]{:S(2)}, u32[]{:S(2)}) %collective-permute-start.4) | collective-permute-done | bytes 147488 | tf_op jit(solution)/shard_map/ppermute | solution.py:493
  16.3 2.6 %collective-permute-done.5.refs_3_ = bf16[16,4608]{1,0:T(8,128)(2,1)S(1)} collective-permute-done((bf16[16,4608]{1,0:T(8,128)(2,1)S(1)}, bf16[16,4608]{1,0:T(8,128)(2,1)S(1)}, u32[]{:S(2)}, u32[]{:S(2)}) %collective-permute-start.5) | collective-permute-done | bytes 147488 | tf_op jit(solution)/shard_map/ppermute | solution.py:493
  19.3 0.7 %collective-permute-start.7 = (bf16[32,2048]{1,0:T(8,128)(2,1)S(1)}, bf16[32,2048]{1,0:T(8,128)(2,1)S(1)}, u32[]{:S(2)}, u32[]{:S(2)}) collective-permute-start(bf16[32,2048]{1,0:T(8,128)(2,1)S(1)} %get-tuple-element.87.refs_7_.refs_6_), channel_id=1, source_target_pairs={{3,2},{7,6},{11,10},{15,14},{19,18},{23,22},{27,26},{31,30}} | collective-permute-start | bytes 393224 | tf_op jit(solution)/shard_map/ppermute | solution.py:521
  21.4 0.7 %collective-permute-start.12 = (bf16[32,2048]{1,0:T(8,128)(2,1)S(1)}, bf16[32,2048]{1,0:T(8,128)(2,1)S(1)}, u32[]{:S(2)}, u32[]{:S(2)}) collective-permute-start(bf16[32,2048]{1,0:T(8,128)(2,1)S(1)} %get-tuple-element.91.refs_6_.refs_9_), channel_id=1, source_target_pairs={{2,1},{6,5},{10,9},{14,13},{18,17},{22,21},{26,25},{30,29}} | collective-permute-start | bytes 393224 | tf_op jit(solution)/shard_map/ppermute | solution.py:521
  22.8 0.7 %collective-permute-start.15 = (bf16[32,2048]{1,0:T(8,128)(2,1)S(1)}, bf16[32,2048]{1,0:T(8,128)(2,1)S(1)}, u32[]{:S(2)}, u32[]{:S(2)}) collective-permute-start(bf16[32,2048]{1,0:T(8,128)(2,1)S(1)} %get-tuple-element.93.refs_6_.after_ref.refs_0_.refs_9_), channel_id=1, source_target_pairs={{2,1},{6,5},{10,9},{14,13},{18,17},{22,21},{26,25},{30,29}} | collective-permute-start | bytes 393224 | tf_op jit(solution)/shard_map/ppermute | solution.py:521
  23.7 2.6 %collective-permute-start.19 = (bf16[128,512]{1,0:T(8,128)(2,1)S(1)}, bf16[128,512]{1,0:T(8,128)(2,1)S(1)}, u32[]{:S(2)}, u32[]{:S(2)}) collective-permute-start(bf16[128,512]{1,0:T(8,128)(2,1)S(1)} %columns6.1), channel_id=1, source_target_pairs={{0,24},{4,28},{8,16},{12,20},{16,8},{20,12},{24,0},{28,4},{1,25},{... | collective-permute-start | bytes 393224 | tf_op jit(solution)/shard_map/ppermute | solution.py:493
  26.3 1.3 %collective-permute-start.17 = (bf16[32,2048]{1,0:T(8,128)(2,1)S(1)}, bf16[32,2048]{1,0:T(8,128)(2,1)S(1)}, u32[]{:S(2)}, u32[]{:S(2)}) collective-permute-start(bf16[32,2048]{1,0:T(8,128)(2,1)S(1)} %get-tuple-element.94.refs_7_.refs_10_), channel_id=1, source_target_pairs={{1,0},{5,4},{9,8},{13,12},{17,16},{21,20},{25,24},{29,28}} | collective-permute-start | bytes 393224 | tf_op jit(solution)/shard_map/ppermute | solution.py:521
  27.6 1.3 %collective-permute-start.18 = (bf16[32,2048]{1,0:T(8,128)(2,1)S(1)}, bf16[32,2048]{1,0:T(8,128)(2,1)S(1)}, u32[]{:S(2)}, u32[]{:S(2)}) collective-permute-start(bf16[32,2048]{1,0:T(8,128)(2,1)S(1)} %get-tuple-element.95.refs_6_.refs_11_), channel_id=1, source_target_pairs={{1,0},{5,4},{9,8},{13,12},{17,16},{21,20},{25,24},{29,28}} | collective-permute-start | bytes 393224 | tf_op jit(solution)/shard_map/ppermute | solution.py:521
  28.9 1.3 %collective-permute-start.14 = (bf16[32,2048]{1,0:T(8,128)(2,1)S(1)}, bf16[32,2048]{1,0:T(8,128)(2,1)S(1)}, u32[]{:S(2)}, u32[]{:S(2)}) collective-permute-start(bf16[32,2048]{1,0:T(8,128)(2,1)S(1)} %get-tuple-element.96.refs_7_.refs_10_), channel_id=1, source_target_pairs={{1,0},{5,4},{9,8},{13,12},{17,16},{21,20},{25,24},{29,28}} | collective-permute-start | bytes 393224 | tf_op jit(solution)/shard_map/ppermute | solution.py:521
  30.3 1.3 %collective-permute-start.16 = (bf16[32,2048]{1,0:T(8,128)(2,1)S(1)}, bf16[32,2048]{1,0:T(8,128)(2,1)S(1)}, u32[]{:S(2)}, u32[]{:S(2)}) collective-permute-start(bf16[32,2048]{1,0:T(8,128)(2,1)S(1)} %get-tuple-element.97.refs_12_.refs_0_.refs_11_), channel_id=1, source_target_pairs={{1,0},{5,4},{9,8},{13,12},{17,16},{21,20},{25,24},{29,28}} | collective-permute-start | bytes 393224 | tf_op jit(solution)/shard_map/ppermute | solution.py:521
  32.2 4.9 %collective-permute-done.17.refs_0_ = bf16[32,2048]{1,0:T(8,128)(2,1)S(1)} collective-permute-done((bf16[32,2048]{1,0:T(8,128)(2,1)S(1)}, bf16[32,2048]{1,0:T(8,128)(2,1)S(1)}, u32[]{:S(2)}, u32[]{:S(2)}) %collective-permute-start.17) | collective-permute-done | bytes 131104 | tf_op jit(solution)/shard_map/ppermute | solution.py:521
  37.1 1.5 %collective-permute-start.21 = (bf16[128,512]{1,0:T(8,128)(2,1)S(1)}, bf16[128,512]{1,0:T(8,128)(2,1)S(1)}, u32[]{:S(2)}, u32[]{:S(2)}) collective-permute-start(bf16[128,512]{1,0:T(8,128)(2,1)S(1)} %columns4.1), channel_id=1, source_target_pairs={{0,16},{4,20},{8,24},{12,28},{16,0},{20,4},{24,8},{28,12},{1,17},{... | collective-permute-start | bytes 393224 | tf_op jit(solution)/shard_map/ppermute | solution.py:493
  38.7 0.8 %tick3_a_late.1 = (bf16[32,2048]{1,0:T(8,128)(2,1)S(1)}, bf16[32,512]{1,0:T(8,128)(2,1)S(1)}) custom-call(bf16[32,2048]{1,0:T(8,128)(2,1)S(1)} %collective-permute-done.17.refs_0_, bf16[4,32,128]{2,1,0:T(8,128)(2,1)S(1)} %get-tuple-element.81.refs_1_, f32[64,128]{1,0:T(8,128)S(1)} %get-tuple-element.79.refs_2_.refs_3_, ...), custom_call_target="tpu_custom_call" | custom-call | flops 1150000000 | tf_op jit(solution)/shard_map/tick3_a_late/pallas_call | solution.py:310
  40.0 0.8 %tick3_a_early.1 = (bf16[32,2048]{1,0:T(8,128)(2,1)S(1)}, bf16[64,512]{1,0:T(8,128)(2,1)S(1)}, bf16[32,2048]{1,0:T(8,128)(2,1)S(1)}) custom-call(bf16[32,2048]{1,0:T(8,128)(2,1)S(1)} %collective-permute-done.17.refs_0_, bf16[32,2048]{1,0:T(8,128)(2,1)S(1)} %collective-permute-done.18.refs_1_, bf16[4,32,256]{2,1,0:T(8,128)(2,1)S(1)} %get-tuple-element.78.refs_2_, ...), custom_call_target="tpu_custom_call" | custom-call | flops 1150000000 | tf_op jit(solution)/shard_map/tick3_a_early/pallas_call | solution.py:310
  40.8 2.5 %collective-permute-start.22 = (bf16[64,512]{1,0:T(8,128)(2,1)S(1)}, bf16[64,512]{1,0:T(8,128)(2,1)S(1)}, u32[]{:S(2)}, u32[]{:S(2)}) collective-permute-start(bf16[64,512]{1,0:T(8,128)(2,1)S(1)} %get-tuple-element.115.refs_17_), channel_id=1, source_target_pairs={{0,24},{4,28},{8,16},{12,20},{16,8},{20,12},{24,0},{28,4},{1,25},{... | collective-permute-start | bytes 196616 | tf_op jit(solution)/shard_map/ppermute | solution.py:493
  43.4 1.0 %collective-permute-start.23 = (bf16[32,2048]{1,0:T(8,128)(2,1)S(1)}, bf16[32,2048]{1,0:T(8,128)(2,1)S(1)}, u32[]{:S(2)}, u32[]{:S(2)}) collective-permute-start(bf16[32,2048]{1,0:T(8,128)(2,1)S(1)} %get-tuple-element.118), channel_id=1, source_target_pairs={{0,8},{4,12},{8,0},{12,4},{16,24},{20,28},{24,16},{28,20},{1,9},{5... | collective-permute-start | bytes 393224 | tf_op jit(solution)/shard_map/ppermute | solution.py:493
  44.3 0.8 %tick3_b_late.1 = (bf16[32,2048]{1,0:T(8,128)(2,1)S(1)}, bf16[32,512]{1,0:T(8,128)(2,1)S(1)}) custom-call(bf16[32,2048]{1,0:T(8,128)(2,1)S(1)} %collective-permute-done.14.refs_0_, bf16[4,32,128]{2,1,0:T(8,128)(2,1)S(1)} %get-tuple-element.85.refs_1_, f32[64,128]{1,0:T(8,128)S(1)} %get-tuple-element.86.refs_2_.refs_3_, ...), custom_call_target="tpu_custom_call" | custom-call | flops 1150000000 | tf_op jit(solution)/shard_map/tick3_b_late/pallas_call | solution.py:310
  45.1 1.6 %collective-permute-done.22.refs_21_.refs_8_ = bf16[64,512]{1,0:T(8,128)(2,1)S(1)} collective-permute-done((bf16[64,512]{1,0:T(8,128)(2,1)S(1)}, bf16[64,512]{1,0:T(8,128)(2,1)S(1)}, u32[]{:S(2)}, u32[]{:S(2)}) %collective-permute-start.22) | collective-permute-done | bytes 65568 | tf_op jit(solution)/shard_map/ppermute | solution.py:493
  46.7 0.9 %tick3_b_early.1 = (bf16[128,512]{1,0:T(8,128)(2,1)S(1)}, bf16[64,512]{1,0:T(8,128)(2,1)S(1)}, bf16[32,2048]{1,0:T(8,128)(2,1)S(1)}, bf16[32,2048]{1,0:T(8,128)(...) custom-call(bf16[32,2048]{1,0:T(8,128)(2,1)S(1)} %collective-permute-done.14.refs_0_, ...), custom_call_target="tpu_custom_call" | custom-call | flops 1150000000 | tf_op jit(solution)/shard_map/tick3_b_early/pallas_call | solution.py:310
  47.6 1.6 %collective-permute-start.24 = (bf16[32,2048]{1,0:T(8,128)(2,1)S(1)}, bf16[32,2048]{1,0:T(8,128)(2,1)S(1)}, u32[]{:S(2)}, u32[]{:S(2)}) collective-permute-start(bf16[32,2048]{1,0:T(8,128)(2,1)S(1)} %get-tuple-element.119), channel_id=1, source_target_pairs={{0,8},{4,12},{8,0},{12,4},{16,24},{20,28},{24,16},{28,20},{1,9},{5... | collective-permute-start | bytes 393224 | tf_op jit(solution)/shard_map/ppermute | solution.py:493
  49.1 1.4 %collective-permute-start.25 = (bf16[128,512]{1,0:T(8,128)(2,1)S(1)}, bf16[128,512]{1,0:T(8,128)(2,1)S(1)}, u32[]{:S(2)}, u32[]{:S(2)}) collective-permute-start(bf16[128,512]{1,0:T(8,128)(2,1)S(1)} %get-tuple-element.117.refs_0_.refs_4_), channel_id=1, source_target_pairs={{0,16},{4,20},{8,24},{12,28},{16,0},{20,4},{24,8},{28,12},{1,17},{... | collective-permute-start | bytes 393224 | tf_op jit(solution)/shard_map/ppermute | solution.py:493
  51.1 1.6 %collective-permute-start.30 = (bf16[32,2048]{1,0:T(8,128)(2,1)S(1)}, bf16[32,2048]{1,0:T(8,128)(2,1)S(1)}, u32[]{:S(2)}, u32[]{:S(2)}) collective-permute-start(bf16[32,2048]{1,0:T(8,128)(2,1)S(1)} %get-tuple-element.127), channel_id=1, source_target_pairs={{0,12},{4,8},{8,4},{12,0},{16,28},{20,24},{24,20},{28,16},{1,13},{... | collective-permute-start | bytes 393224 | tf_op jit(solution)/shard_map/ppermute | solution.py:493
  52.8 3.6 %collective-permute-done.26.refs_9_ = bf16[64,512]{1,0:T(8,128)(2,1)S(1)} collective-permute-done((bf16[64,512]{1,0:T(8,128)(2,1)S(1)}, bf16[64,512]{1,0:T(8,128)(2,1)S(1)}, u32[]{:S(2)}, u32[]{:S(2)}) %collective-permute-start.26) | collective-permute-done | bytes 65568 | tf_op jit(solution)/shard_map/ppermute | solution.py:493
  57.4 0.8 %collective-permute-done.27.first_ref = bf16[128,512]{1,0:T(8,128)(2,1)S(1)} collective-permute-done((bf16[128,512]{1,0:T(8,128)(2,1)S(1)}, bf16[128,512]{1,0:T(8,128)(2,1)S(1)}, u32[]{:S(2)}, u32[]{:S(2)}) %collective-permute-start.27) | collective-permute-done | bytes 131104 | tf_op jit(solution)/shard_map/ppermute | solution.py:493
  58.4 1.7 %finish.1 = (bf16[128,2048]{1,0:T(8,128)(2,1)}, f32[256,512]{1,0:T(8,128)}, f32[1,256]{1,0:T(1,128)}) custom-call(f32[256,512]{1,0:T(8,128)S(1)} %get-tuple-element.121.own_ref, bf16[128,512]{1,0:T(8,128)(2,1)S(1)} %collective-permute-done.27.first_ref, bf16[128,512]{1,0:T(8,128)(2,1)S(1)} %collective-permute-done.28.second_ref, ...), custom_call_target="tpu_custom_call" | custom-call | tf_op jit(solution)/shard_map/finish/pallas_call | solution.py:571
  (61 shorter events, 8.3 us)
Async XLA Ops:
  0.6 4.7 %copy-start = (bf16[1,2048,512]{2,1,0:T(8,128)(2,1)S(1)}, bf16[1,2048,512]{2,1,0:T(8,128)(2,1)}, u32[]{:S(2)}) copy-start(bf16[1,2048,512]{2,1,0:T(8,128)(2,1)} %param.11) | copy-start | bytes 6291460
  2.2 6.5 %collective-permute-start = (bf16[16,4608]{1,0:T(8,128)(2,1)S(1)}, bf16[16,4608]{1,0:T(8,128)(2,1)S(1)}, u32[]{:S(2)}, u32[]{:S(2)}) collective-permute-start(bf16[16,4608]{1,0:T(8,128)(2,1)S(1)} %get-tuple-element.68), channel_id=1, source_target_pairs={{0,4},{4,0},{8,12},{12,8},{16,20},{20,16},{24,28},{28,24},{1,5},{5... | collective-permute-start | bytes 442376 | tf_op jit(solution)/shard_map/ppermute | solution.py:493
  2.7 7.5 %collective-permute-start.1 = (bf16[16,4608]{1,0:T(8,128)(2,1)S(1)}, bf16[16,4608]{1,0:T(8,128)(2,1)S(1)}, u32[]{:S(2)}, u32[]{:S(2)}) collective-permute-start(bf16[16,4608]{1,0:T(8,128)(2,1)S(1)} %get-tuple-element.69), channel_id=1, source_target_pairs={{0,8},{4,12},{8,0},{12,4},{16,24},{20,28},{24,16},{28,20},{1,9},{5... | collective-permute-start | bytes 442376 | tf_op jit(solution)/shard_map/ppermute | solution.py:493
  5.3 7.3 %collective-permute-start.2 = (bf16[16,4608]{1,0:T(8,128)(2,1)S(1)}, bf16[16,4608]{1,0:T(8,128)(2,1)S(1)}, u32[]{:S(2)}, u32[]{:S(2)}) collective-permute-start(bf16[16,4608]{1,0:T(8,128)(2,1)S(1)} %get-tuple-element.70), channel_id=1, source_target_pairs={{0,12},{4,8},{8,4},{12,0},{16,28},{20,24},{24,20},{28,16},{1,13},{... | collective-permute-start | bytes 442376 | tf_op jit(solution)/shard_map/ppermute | solution.py:493
  6.8 12.1 %collective-permute-start.6 = (bf16[80,2048]{1,0:T(8,128)(2,1)S(1)}, bf16[80,2048]{1,0:T(8,128)(2,1)S(1)}, u32[]{:S(2)}, u32[]{:S(2)}) collective-permute-start(bf16[80,2048]{1,0:T(8,128)(2,1)S(1)} %get-tuple-element.77), channel_id=1, source_target_pairs={{0,16},{4,20},{8,24},{12,28},{16,0},{20,4},{24,8},{28,12},{1,17},{... | collective-permute-start | bytes 983048 | tf_op jit(solution)/shard_map/ppermute | solution.py:493
  8.6 5.4 %collective-permute-start.3 = (bf16[16,4608]{1,0:T(8,128)(2,1)S(1)}, bf16[16,4608]{1,0:T(8,128)(2,1)S(1)}, u32[]{:S(2)}, u32[]{:S(2)}) collective-permute-start(bf16[16,4608]{1,0:T(8,128)(2,1)S(1)} %get-tuple-element.74), channel_id=1, source_target_pairs={{0,4},{4,0},{8,12},{12,8},{16,20},{20,16},{24,28},{28,24},{1,5},{5... | collective-permute-start | bytes 442376 | tf_op jit(solution)/shard_map/ppermute | solution.py:493
  8.7 7.6 %collective-permute-start.4 = (bf16[16,4608]{1,0:T(8,128)(2,1)S(1)}, bf16[16,4608]{1,0:T(8,128)(2,1)S(1)}, u32[]{:S(2)}, u32[]{:S(2)}) collective-permute-start(bf16[16,4608]{1,0:T(8,128)(2,1)S(1)} %get-tuple-element.75), channel_id=1, source_target_pairs={{0,8},{4,12},{8,0},{12,4},{16,24},{20,28},{24,16},{28,20},{1,9},{5... | collective-permute-start | bytes 442376 | tf_op jit(solution)/shard_map/ppermute | solution.py:493
  10.2 8.7 %collective-permute-start.5 = (bf16[16,4608]{1,0:T(8,128)(2,1)S(1)}, bf16[16,4608]{1,0:T(8,128)(2,1)S(1)}, u32[]{:S(2)}, u32[]{:S(2)}) collective-permute-start(bf16[16,4608]{1,0:T(8,128)(2,1)S(1)} %get-tuple-element.76), channel_id=1, source_target_pairs={{0,12},{4,8},{8,4},{12,0},{16,28},{20,24},{24,20},{28,16},{1,13},{... | collective-permute-start | bytes 442376 | tf_op jit(solution)/shard_map/ppermute | solution.py:493
  13.3 7.4 %collective-permute-start.8 = (bf16[32,2048]{1,0:T(8,128)(2,1)S(1)}, bf16[32,2048]{1,0:T(8,128)(2,1)S(1)}, u32[]{:S(2)}, u32[]{:S(2)}) collective-permute-start(bf16[32,2048]{1,0:T(8,128)(2,1)S(1)} %get-tuple-element.82.refs_7_.refs_6_), channel_id=1, source_target_pairs={{3,2},{7,6},{11,10},{15,14},{19,18},{23,22},{27,26},{31,30}} | collective-permute-start | bytes 393224 | tf_op jit(solution)/shard_map/ppermute | solution.py:521
  14.0 7.4 %collective-permute-start.9 = (bf16[32,2048]{1,0:T(8,128)(2,1)S(1)}, bf16[32,2048]{1,0:T(8,128)(2,1)S(1)}, u32[]{:S(2)}, u32[]{:S(2)}) collective-permute-start(bf16[32,2048]{1,0:T(8,128)(2,1)S(1)} %get-tuple-element.83.refs_5_.refs_7_), channel_id=1, source_target_pairs={{3,2},{7,6},{11,10},{15,14},{19,18},{23,22},{27,26},{31,30}} | collective-permute-start | bytes 393224 | tf_op jit(solution)/shard_map/ppermute | solution.py:521
  19.3 2.8 %collective-permute-start.7 = (bf16[32,2048]{1,0:T(8,128)(2,1)S(1)}, bf16[32,2048]{1,0:T(8,128)(2,1)S(1)}, u32[]{:S(2)}, u32[]{:S(2)}) collective-permute-start(bf16[32,2048]{1,0:T(8,128)(2,1)S(1)} %get-tuple-element.87.refs_7_.refs_6_), channel_id=1, source_target_pairs={{3,2},{7,6},{11,10},{15,14},{19,18},{23,22},{27,26},{31,30}} | collective-permute-start | bytes 393224 | tf_op jit(solution)/shard_map/ppermute | solution.py:521
  20.0 2.8 %collective-permute-start.13 = (bf16[32,2048]{1,0:T(8,128)(2,1)S(1)}, bf16[32,2048]{1,0:T(8,128)(2,1)S(1)}, u32[]{:S(2)}, u32[]{:S(2)}) collective-permute-start(bf16[32,2048]{1,0:T(8,128)(2,1)S(1)} %get-tuple-element.89.refs_6_.refs_7_), channel_id=1, source_target_pairs={{3,2},{7,6},{11,10},{15,14},{19,18},{23,22},{27,26},{31,30}} | collective-permute-start | bytes 393224 | tf_op jit(solution)/shard_map/ppermute | solution.py:521
  20.7 5.6 %collective-permute-start.11 = (bf16[32,2048]{1,0:T(8,128)(2,1)S(1)}, bf16[32,2048]{1,0:T(8,128)(2,1)S(1)}, u32[]{:S(2)}, u32[]{:S(2)}) collective-permute-start(bf16[32,2048]{1,0:T(8,128)(2,1)S(1)} %get-tuple-element.90.refs_7_.refs_8_), channel_id=1, source_target_pairs={{2,1},{6,5},{10,9},{14,13},{18,17},{22,21},{26,25},{30,29}} | collective-permute-start | bytes 393224 | tf_op jit(solution)/shard_map/ppermute | solution.py:521
  21.4 6.2 %collective-permute-start.12 = (bf16[32,2048]{1,0:T(8,128)(2,1)S(1)}, bf16[32,2048]{1,0:T(8,128)(2,1)S(1)}, u32[]{:S(2)}, u32[]{:S(2)}) collective-permute-start(bf16[32,2048]{1,0:T(8,128)(2,1)S(1)} %get-tuple-element.91.refs_6_.refs_9_), channel_id=1, source_target_pairs={{2,1},{6,5},{10,9},{14,13},{18,17},{22,21},{26,25},{30,29}} | collective-permute-start | bytes 393224 | tf_op jit(solution)/shard_map/ppermute | solution.py:521
  22.1 6.8 %collective-permute-start.10 = (bf16[32,2048]{1,0:T(8,128)(2,1)S(1)}, bf16[32,2048]{1,0:T(8,128)(2,1)S(1)}, u32[]{:S(2)}, u32[]{:S(2)}) collective-permute-start(bf16[32,2048]{1,0:T(8,128)(2,1)S(1)} %get-tuple-element.92.refs_7_.refs_8_), channel_id=1, source_target_pairs={{2,1},{6,5},{10,9},{14,13},{18,17},{22,21},{26,25},{30,29}} | collective-permute-start | bytes 393224 | tf_op jit(solution)/shard_map/ppermute | solution.py:521
  22.8 7.4 %collective-permute-start.15 = (bf16[32,2048]{1,0:T(8,128)(2,1)S(1)}, bf16[32,2048]{1,0:T(8,128)(2,1)S(1)}, u32[]{:S(2)}, u32[]{:S(2)}) collective-permute-start(bf16[32,2048]{1,0:T(8,128)(2,1)S(1)} %get-tuple-element.93.refs_6_.after_ref.refs_0_.refs_9_), channel_id=1, source_target_pairs={{2,1},{6,5},{10,9},{14,13},{18,17},{22,21},{26,25},{30,29}} | collective-permute-start | bytes 393224 | tf_op jit(solution)/shard_map/ppermute | solution.py:521
  23.7 7.9 %collective-permute-start.19 = (bf16[128,512]{1,0:T(8,128)(2,1)S(1)}, bf16[128,512]{1,0:T(8,128)(2,1)S(1)}, u32[]{:S(2)}, u32[]{:S(2)}) collective-permute-start(bf16[128,512]{1,0:T(8,128)(2,1)S(1)} %columns6.1), channel_id=1, source_target_pairs={{0,24},{4,28},{8,16},{12,20},{16,8},{20,12},{24,0},{28,4},{1,25},{... | collective-permute-start | bytes 393224 | tf_op jit(solution)/shard_map/ppermute | solution.py:493
  26.3 10.9 %collective-permute-start.17 = (bf16[32,2048]{1,0:T(8,128)(2,1)S(1)}, bf16[32,2048]{1,0:T(8,128)(2,1)S(1)}, u32[]{:S(2)}, u32[]{:S(2)}) collective-permute-start(bf16[32,2048]{1,0:T(8,128)(2,1)S(1)} %get-tuple-element.94.refs_7_.refs_10_), channel_id=1, source_target_pairs={{1,0},{5,4},{9,8},{13,12},{17,16},{21,20},{25,24},{29,28}} | collective-permute-start | bytes 393224 | tf_op jit(solution)/shard_map/ppermute | solution.py:521
  27.6 12.4 %collective-permute-start.18 = (bf16[32,2048]{1,0:T(8,128)(2,1)S(1)}, bf16[32,2048]{1,0:T(8,128)(2,1)S(1)}, u32[]{:S(2)}, u32[]{:S(2)}) collective-permute-start(bf16[32,2048]{1,0:T(8,128)(2,1)S(1)} %get-tuple-element.95.refs_6_.refs_11_), channel_id=1, source_target_pairs={{1,0},{5,4},{9,8},{13,12},{17,16},{21,20},{25,24},{29,28}} | collective-permute-start | bytes 393224 | tf_op jit(solution)/shard_map/ppermute | solution.py:521
  28.9 14.4 %collective-permute-start.14 = (bf16[32,2048]{1,0:T(8,128)(2,1)S(1)}, bf16[32,2048]{1,0:T(8,128)(2,1)S(1)}, u32[]{:S(2)}, u32[]{:S(2)}) collective-permute-start(bf16[32,2048]{1,0:T(8,128)(2,1)S(1)} %get-tuple-element.96.refs_7_.refs_10_), channel_id=1, source_target_pairs={{1,0},{5,4},{9,8},{13,12},{17,16},{21,20},{25,24},{29,28}} | collective-permute-start | bytes 393224 | tf_op jit(solution)/shard_map/ppermute | solution.py:521
  30.3 16.4 %collective-permute-start.16 = (bf16[32,2048]{1,0:T(8,128)(2,1)S(1)}, bf16[32,2048]{1,0:T(8,128)(2,1)S(1)}, u32[]{:S(2)}, u32[]{:S(2)}) collective-permute-start(bf16[32,2048]{1,0:T(8,128)(2,1)S(1)} %get-tuple-element.97.refs_12_.refs_0_.refs_11_), channel_id=1, source_target_pairs={{1,0},{5,4},{9,8},{13,12},{17,16},{21,20},{25,24},{29,28}} | collective-permute-start | bytes 393224 | tf_op jit(solution)/shard_map/ppermute | solution.py:521
  31.6 15.1 %collective-permute-start.20 = (bf16[128,512]{1,0:T(8,128)(2,1)S(1)}, bf16[128,512]{1,0:T(8,128)(2,1)S(1)}, u32[]{:S(2)}, u32[]{:S(2)}) collective-permute-start(bf16[128,512]{1,0:T(8,128)(2,1)S(1)} %columns2.1), channel_id=1, source_target_pairs={{0,8},{4,12},{8,0},{12,4},{16,24},{20,28},{24,16},{28,20},{1,9},{5... | collective-permute-start | bytes 393224 | tf_op jit(solution)/shard_map/ppermute | solution.py:493
  37.1 9.5 %collective-permute-start.21 = (bf16[128,512]{1,0:T(8,128)(2,1)S(1)}, bf16[128,512]{1,0:T(8,128)(2,1)S(1)}, u32[]{:S(2)}, u32[]{:S(2)}) collective-permute-start(bf16[128,512]{1,0:T(8,128)(2,1)S(1)} %columns4.1), channel_id=1, source_target_pairs={{0,16},{4,20},{8,24},{12,28},{16,0},{20,4},{24,8},{28,12},{1,17},{... | collective-permute-start | bytes 393224 | tf_op jit(solution)/shard_map/ppermute | solution.py:493
  40.8 5.8 %collective-permute-start.22 = (bf16[64,512]{1,0:T(8,128)(2,1)S(1)}, bf16[64,512]{1,0:T(8,128)(2,1)S(1)}, u32[]{:S(2)}, u32[]{:S(2)}) collective-permute-start(bf16[64,512]{1,0:T(8,128)(2,1)S(1)} %get-tuple-element.115.refs_17_), channel_id=1, source_target_pairs={{0,24},{4,28},{8,16},{12,20},{16,8},{20,12},{24,0},{28,4},{1,25},{... | collective-permute-start | bytes 196616 | tf_op jit(solution)/shard_map/ppermute | solution.py:493
  43.4 7.8 %collective-permute-start.23 = (bf16[32,2048]{1,0:T(8,128)(2,1)S(1)}, bf16[32,2048]{1,0:T(8,128)(2,1)S(1)}, u32[]{:S(2)}, u32[]{:S(2)}) collective-permute-start(bf16[32,2048]{1,0:T(8,128)(2,1)S(1)} %get-tuple-element.118), channel_id=1, source_target_pairs={{0,8},{4,12},{8,0},{12,4},{16,24},{20,28},{24,16},{28,20},{1,9},{5... | collective-permute-start | bytes 393224 | tf_op jit(solution)/shard_map/ppermute | solution.py:493
  47.6 8.8 %collective-permute-start.24 = (bf16[32,2048]{1,0:T(8,128)(2,1)S(1)}, bf16[32,2048]{1,0:T(8,128)(2,1)S(1)}, u32[]{:S(2)}, u32[]{:S(2)}) collective-permute-start(bf16[32,2048]{1,0:T(8,128)(2,1)S(1)} %get-tuple-element.119), channel_id=1, source_target_pairs={{0,8},{4,12},{8,0},{12,4},{16,24},{20,28},{24,16},{28,20},{1,9},{5... | collective-permute-start | bytes 393224 | tf_op jit(solution)/shard_map/ppermute | solution.py:493
  49.1 7.2 %collective-permute-start.25 = (bf16[128,512]{1,0:T(8,128)(2,1)S(1)}, bf16[128,512]{1,0:T(8,128)(2,1)S(1)}, u32[]{:S(2)}, u32[]{:S(2)}) collective-permute-start(bf16[128,512]{1,0:T(8,128)(2,1)S(1)} %get-tuple-element.117.refs_0_.refs_4_), channel_id=1, source_target_pairs={{0,16},{4,20},{8,24},{12,28},{16,0},{20,4},{24,8},{28,12},{1,17},{... | collective-permute-start | bytes 393224 | tf_op jit(solution)/shard_map/ppermute | solution.py:493
  50.6 5.8 %collective-permute-start.26 = (bf16[64,512]{1,0:T(8,128)(2,1)S(1)}, bf16[64,512]{1,0:T(8,128)(2,1)S(1)}, u32[]{:S(2)}, u32[]{:S(2)}) collective-permute-start(bf16[64,512]{1,0:T(8,128)(2,1)S(1)} %get-tuple-element.120), channel_id=1, source_target_pairs={{0,24},{4,28},{8,16},{12,20},{16,8},{20,12},{24,0},{28,4},{1,25},{... | collective-permute-start | bytes 196616 | tf_op jit(solution)/shard_map/ppermute | solution.py:493
  51.1 6.3 %collective-permute-start.29 = (bf16[32,2048]{1,0:T(8,128)(2,1)S(1)}, bf16[32,2048]{1,0:T(8,128)(2,1)S(1)}, u32[]{:S(2)}, u32[]{:S(2)}) collective-permute-start(bf16[32,2048]{1,0:T(8,128)(2,1)S(1)} %get-tuple-element.126), channel_id=1, source_target_pairs={{0,4},{4,0},{8,12},{12,8},{16,20},{20,16},{24,28},{28,24},{1,5},{5... | collective-permute-start | bytes 393224 | tf_op jit(solution)/shard_map/ppermute | solution.py:493
  51.1 6.3 %collective-permute-start.30 = (bf16[32,2048]{1,0:T(8,128)(2,1)S(1)}, bf16[32,2048]{1,0:T(8,128)(2,1)S(1)}, u32[]{:S(2)}, u32[]{:S(2)}) collective-permute-start(bf16[32,2048]{1,0:T(8,128)(2,1)S(1)} %get-tuple-element.127), channel_id=1, source_target_pairs={{0,12},{4,8},{8,4},{12,0},{16,28},{20,24},{24,20},{28,16},{1,13},{... | collective-permute-start | bytes 393224 | tf_op jit(solution)/shard_map/ppermute | solution.py:493
  56.8 1.4 %collective-permute-start.27 = (bf16[128,512]{1,0:T(8,128)(2,1)S(1)}, bf16[128,512]{1,0:T(8,128)(2,1)S(1)}, u32[]{:S(2)}, u32[]{:S(2)}) collective-permute-start(bf16[128,512]{1,0:T(8,128)(2,1)S(1)} %get-tuple-element.122), channel_id=1, source_target_pairs={{0,4},{4,0},{8,12},{12,8},{16,20},{20,16},{24,28},{28,24},{1,5},{5... | collective-permute-start | bytes 393224 | tf_op jit(solution)/shard_map/ppermute | solution.py:493
  56.9 1.5 %collective-permute-start.28 = (bf16[128,512]{1,0:T(8,128)(2,1)S(1)}, bf16[128,512]{1,0:T(8,128)(2,1)S(1)}, u32[]{:S(2)}, u32[]{:S(2)}) collective-permute-start(bf16[128,512]{1,0:T(8,128)(2,1)S(1)} %get-tuple-element.123), channel_id=1, source_target_pairs={{0,4},{4,0},{8,12},{12,8},{16,20},{20,16},{24,28},{28,24},{1,5},{5... | collective-permute-start | bytes 393224 | tf_op jit(solution)/shard_map/ppermute | solution.py:493
  (1 other events, 0.7 us)

commit v11 on v10

--- a/solution.py
+++ b/solution.py
@@ -321,11 +321,11 @@
 
 
 def pack_kernel(block, half, piece, query_ref, key_ref, hidden_ref, up_ref, seg_ref, *rest):
-    up_out_ref, seg_in_ref, sems = rest[-3:]
-    packed = rest[-3 - half : -3]
-    rest = rest[: -3 - half]
+    up_out_ref, seg_in_ref, rows_ref, sems = rest[-4:]
+    packed = rest[-4 - half : -4]
     side, at, _ = place()
     there = side if block == 0 else 1 - side
+    rows = pl.ds(pl.multiple_of(there * BLOCK, BLOCK), BLOCK)
     copies = []
 
     def copy(source, target):
@@ -333,27 +333,26 @@
         made.start()
         copies.append(made)
 
+    first = 0
+    for source in (query_ref, key_ref, hidden_ref):
+        width = source.shape[1]
+        copy(source.at[rows], rows_ref.at[:, pl.ds(first, width)])
+        first += width
     copy(seg_ref, seg_in_ref)
-    for k in range(half):
-        replica = there * half + lax.bitwise_xor(at, k)
-        rows = pl.ds(pl.multiple_of(replica * piece, piece), piece)
-        first = 0
-        for source in (query_ref, key_ref, hidden_ref):
-            width = source.shape[1]
-            copy(source.at[rows], packed[k].at[:, pl.ds(first, width)])
-            first += width
-    rows = pl.ds(pl.multiple_of(there * BLOCK, BLOCK), BLOCK)
     copy(up_ref.at[rows], up_out_ref.at[pl.ds(0, BLOCK)])
     up_out_ref[BLOCK:, :] = jnp.zeros((16, up_out_ref.shape[1]), jnp.bfloat16)
-    copies[0].wait()
+    if block == 1:
+        turn_kernel(rest[0], rest[-5 - half])
+    for made in copies[:4]:
+        made.wait()
     ids = seg_in_ref[...].astype(jnp.float32)
     up_out_ref[BLOCK:, : ids.shape[1]] = jnp.broadcast_to(ids, (16, ids.shape[1])).astype(
         jnp.bfloat16
     )
-    if block == 1:
-        turn_kernel(rest[0], rest[-1])
-    for made in copies[1:]:
-        made.wait()
+    for k in range(half):
+        first = pl.multiple_of(lax.bitwise_xor(at, k) * piece, piece)
+        packed[k][...] = rows_ref[pl.ds(first, piece), :]
+    copies[4].wait()
 
 
 def pack(block, half, piece, sources, weight=None):
@@ -375,7 +374,8 @@
         out_specs=(VMEM,) * len(outs),
         scratch_shapes=[
             pltpu.VMEM(sources[-1].shape, jnp.int32),
-            pltpu.SemaphoreType.DMA((3 * half + 2,)),
+            pltpu.VMEM((BLOCK, width), bf16),
+            pltpu.SemaphoreType.DMA((5,)),
         ],
         name="pack",
         **params(1.2),
@@ -398,7 +398,7 @@
         in_specs=[VMEM] * 2 + [ANY] * len(after),
         out_specs=VMEM,
         name=f"columns{distance}",
-        **params(0.0),
+        **params(0.0 if distance else 1.0),
     )(blocks[0][3], blocks[1][3], *after)
 
 
@@ -447,16 +447,9 @@
 
 def finish_kernel(half, own_ref, first_ref, second_ref, weight_ref, gain_ref, *refs):
     first_rows_ref, pieces = refs[0], refs[1 : 1 + half]
-    rows_ref, out_ref, gain_out_ref, sums_ref, sems = refs[1 + half :]
+    rows_ref, out_ref, gain_out_ref = refs[1 + half :]
     side, at, _ = place()
     piece = BLOCK // half
-    copies = []
-
-    def copy(source, target):
-        made = pltpu.make_async_copy(source, target, sems.at[len(copies)])
-        made.start()
-        copies.append(made)
-
     for block in range(2):
         for k in range(half):
             replica = (side if block == 0 else 1 - side) * half + lax.bitwise_xor(at, k)
@@ -464,20 +457,14 @@
             source, first = pieces[k], block * piece
             if k == 2:
                 source, first = (pieces[k] if block else first_rows_ref), 0
-            copy(source.at[pl.ds(first, piece)], rows_ref.at[rows])
-    shares = own_ref.shape[0]
-    gain_sums = []
-    for part, ref in enumerate((first_ref, second_ref)):
-        rows = slice(part * (shares // 2), (part + 1) * (shares // 2))
-        total = own_ref[rows, :] + ref[...].astype(jnp.float32)
-        sums_ref[rows, :] = total * gain_ref[rows, :1]
-        copy(sums_ref.at[rows], out_ref.at[rows])
-        gain_sums.append(jnp.sum(total * weight_ref[rows, :], axis=1, keepdims=True))
+            rows_ref[rows, :] = source[first : first + piece, :]
+    other = jnp.concatenate([first_ref[...], second_ref[...]], axis=0)
+    total = own_ref[...] + other.astype(jnp.float32)
+    out_ref[...] = total * gain_ref[:, :1]
+    sums = jnp.sum(total * weight_ref[...], axis=1, keepdims=True)
     gain_out_ref[...] = jnp.sum(
-        jnp.where(diagonal(shares), jnp.concatenate(gain_sums, axis=0), 0.0), axis=0, keepdims=True
-    )
-    for made in copies:
-        made.wait()
+        jnp.where(diagonal(total.shape[0]), sums, 0.0), axis=0, keepdims=True
+    )
 
 
 def direct(hidden, query, key, segments, weight, norm_gain, upstream):
@@ -556,8 +543,9 @@
             kept[u].append(done[u])
     values, last_value, *rows = done[3]
     rows = [rows[0]] + [swap(rows[k], k) for k in range(1, half)]
-    columns[0] = columns_for(0, blocks, [values, first_rows])
-    values = [values, first_rows, rows[2], swap(values, 4), first_value, swap(last_value, 6)]
+    last_value = swap(last_value, 6)
+    columns[0] = columns_for(0, blocks, [values, first_rows, last_value])
+    values = [values, first_rows, rows[2], swap(values, 4), first_value, last_value]
     own, *other = pl.pallas_call(
         functools.partial(partial_kernel, shares, piece),
         out_shape=(jax.ShapeDtypeStruct((shares, kv_width), jnp.float32),)
@@ -576,11 +564,7 @@
             jax.ShapeDtypeStruct((1, shares), jnp.float32),
         ),
         in_specs=[VMEM] * (6 + half),
-        out_specs=(ANY, ANY, VMEM),
-        scratch_shapes=[
-            pltpu.VMEM((shares, kv_width), jnp.float32),
-            pltpu.SemaphoreType.DMA((count + 2,)),
-        ],
+        out_specs=(VMEM,) * 3,
         name="finish",
         **params(0.0),
     )(own, *other, own_weight, own_gain, first_rows, *rows)

time: 60.5 us -> 59.2 us (0.979)
  Pallas kernels: 9.46 us -> 8.49 us
  transfers between devices with their start and end apart: 31 -> 31, of which waited for: 9 -> 10; matrix products, arithmetic and copies ran while one was open for 0% -> 0% of each run, Pallas kernels for 10% -> 10%
where the time goes in v11:
time: 59.2 us; the launch traced here: 58.9 us
  starting transfers between devices  31.7 us (54%)
  waiting for transfers between devices  17.4 us (29%)
  Pallas kernels  8.49 us (14%)
  between operations  1.01 us (2%)
    ppermute x19, starting transfers between devices, swap(): return lax.ppermute(array, 'dp', [(i, i ^ k) for i in range(replicas)])  21.2 us
    ppermute x19, waiting for transfers between devices, swap(): return lax.ppermute(array, 'dp', [(i, i ^ k) for i in range(replicas)])  11.8 us
    ppermute x12, starting transfers between devices, direct(): lax.ppermute(unit[-1][0], 'section', hop)  10.5 us
    ppermute x12, waiting for transfers between devices, direct(): lax.ppermute(unit[-1][0], 'section', hop)  5.51 us
    pallas_call x16, Pallas kernels, tick_step(): pl.pallas_call(functools.partial(tick_kernel, tick, EARLY if low else LAT...  3.43 us
    pallas_call x2, Pallas kernels, pack(): pl.pallas_call(functools.partial(pack_kernel, block, half, piece), out_sh...  2.58 us
  transfers between devices with their start and end apart: 31, of which 10 were waited for; matrix products, arithmetic and copies ran while one was open for 0% of the time, Pallas kernels for 10%

profile of v11, /device:TPU:0, one launch (start us, length us, event | category | flops | bytes accessed | tf_op | source)
XLA Modules:
  0.0 58.9 jit_solution(14044885062162028551)
XLA Ops:
  0.6 1.4 %pack.2 = (bf16[16,4608]{1,0:T(8,128)(2,1)S(1)}, bf16[16,4608]{1,0:T(8,128)(2,1)S(1)}, bf16[16,4608]{1,0:T(8,128)(2,1)S(1)}, bf16[16,4608]{1,0:T(8,128)(2,1)S(1)}, bf16[80,2048]{1,0:T(8,128)(2,1)S(1)}) custom-call(bf16[128,2048]{1,0:T(8,128)(2,1)} %bitcast.8, bf16[128,512]{1,0:T(8,128)(2,1)} %bitcast.14, bf16[128,2048]{1,0:T(8,128)(2,1)} %bitcast.10, ...), custom_call_target="tpu_custom_call" | custom-call | flops 1380000000 | tf_op jit(solution)/shard_map/pack/pallas_call | solution.py:370
  2.5 2.6 %collective-permute-start.1 = (bf16[16,4608]{1,0:T(8,128)(2,1)S(1)}, bf16[16,4608]{1,0:T(8,128)(2,1)S(1)}, u32[]{:S(2)}, u32[]{:S(2)}) collective-permute-start(bf16[16,4608]{1,0:T(8,128)(2,1)S(1)} %get-tuple-element.69), channel_id=1, source_target_pairs={{0,8},{4,12},{8,0},{12,4},{16,24},{20,28},{24,16},{28,20},{1,9},{5... | collective-permute-start | bytes 442376 | tf_op jit(solution)/shard_map/ppermute | solution.py:480
  5.2 1.2 %pack.3 = (bf16[512,2048]{1,0:T(8,128)(2,1)S(1)}, bf16[16,4608]{1,0:T(8,128)(2,1)S(1)}, bf16[16,4608]{1,0:T(8,128)(2,1)S(1)}, bf16[16,4608]{1,0:T(8,128)(2,1)S(1...) custom-call(bf16[128,2048]{1,0:T(8,128)(2,1)} %bitcast.9, bf16[128,512]{1,0:T(8,128)(2,1)} %bitcast.15, ...), custom_call_target="tpu_custom_call" | custom-call | flops 1380000000 | tf_op jit(solution)/shard_map/pack/pallas_call | solution.py:370
  6.4 1.8 %collective-permute-start.6 = (bf16[80,2048]{1,0:T(8,128)(2,1)S(1)}, bf16[80,2048]{1,0:T(8,128)(2,1)S(1)}, u32[]{:S(2)}, u32[]{:S(2)}) collective-permute-start(bf16[80,2048]{1,0:T(8,128)(2,1)S(1)} %get-tuple-element.77), channel_id=1, source_target_pairs={{0,16},{4,20},{8,24},{12,28},{16,0},{20,4},{24,8},{28,12},{1,17},{... | collective-permute-start | bytes 983048 | tf_op jit(solution)/shard_map/ppermute | solution.py:480
  8.3 1.5 %collective-permute-start.4 = (bf16[16,4608]{1,0:T(8,128)(2,1)S(1)}, bf16[16,4608]{1,0:T(8,128)(2,1)S(1)}, u32[]{:S(2)}, u32[]{:S(2)}) collective-permute-start(bf16[16,4608]{1,0:T(8,128)(2,1)S(1)} %get-tuple-element.75), channel_id=1, source_target_pairs={{0,8},{4,12},{8,0},{12,4},{16,24},{20,28},{24,16},{28,20},{1,9},{5... | collective-permute-start | bytes 442376 | tf_op jit(solution)/shard_map/ppermute | solution.py:480
  9.8 0.8 %collective-permute-start.5 = (bf16[16,4608]{1,0:T(8,128)(2,1)S(1)}, bf16[16,4608]{1,0:T(8,128)(2,1)S(1)}, u32[]{:S(2)}, u32[]{:S(2)}) collective-permute-start(bf16[16,4608]{1,0:T(8,128)(2,1)S(1)} %get-tuple-element.76), channel_id=1, source_target_pairs={{0,12},{4,8},{8,4},{12,0},{16,28},{20,24},{24,20},{28,16},{1,13},{... | collective-permute-start | bytes 442376 | tf_op jit(solution)/shard_map/ppermute | solution.py:480
  10.6 1.9 %collective-permute-done.2.refs_3_ = bf16[16,4608]{1,0:T(8,128)(2,1)S(1)} collective-permute-done((bf16[16,4608]{1,0:T(8,128)(2,1)S(1)}, bf16[16,4608]{1,0:T(8,128)(2,1)S(1)}, u32[]{:S(2)}, u32[]{:S(2)}) %collective-permute-start.2) | collective-permute-done | bytes 147488 | tf_op jit(solution)/shard_map/ppermute | solution.py:480
  13.8 0.7 %collective-permute-start.9 = (bf16[32,2048]{1,0:T(8,128)(2,1)S(1)}, bf16[32,2048]{1,0:T(8,128)(2,1)S(1)}, u32[]{:S(2)}, u32[]{:S(2)}) collective-permute-start(bf16[32,2048]{1,0:T(8,128)(2,1)S(1)} %get-tuple-element.83.refs_5_.refs_7_), channel_id=1, source_target_pairs={{3,2},{7,6},{11,10},{15,14},{19,18},{23,22},{27,26},{31,30}} | collective-permute-start | bytes 393224 | tf_op jit(solution)/shard_map/ppermute | solution.py:508
  14.5 1.6 %collective-permute-done.4.refs_2_ = bf16[16,4608]{1,0:T(8,128)(2,1)S(1)} collective-permute-done((bf16[16,4608]{1,0:T(8,128)(2,1)S(1)}, bf16[16,4608]{1,0:T(8,128)(2,1)S(1)}, u32[]{:S(2)}, u32[]{:S(2)}) %collective-permute-start.4) | collective-permute-done | bytes 147488 | tf_op jit(solution)/shard_map/ppermute | solution.py:480
  16.1 2.6 %collective-permute-done.5.refs_3_ = bf16[16,4608]{1,0:T(8,128)(2,1)S(1)} collective-permute-done((bf16[16,4608]{1,0:T(8,128)(2,1)S(1)}, bf16[16,4608]{1,0:T(8,128)(2,1)S(1)}, u32[]{:S(2)}, u32[]{:S(2)}) %collective-permute-start.5) | collective-permute-done | bytes 147488 | tf_op jit(solution)/shard_map/ppermute | solution.py:480
  19.8 0.7 %collective-permute-start.13 = (bf16[32,2048]{1,0:T(8,128)(2,1)S(1)}, bf16[32,2048]{1,0:T(8,128)(2,1)S(1)}, u32[]{:S(2)}, u32[]{:S(2)}) collective-permute-start(bf16[32,2048]{1,0:T(8,128)(2,1)S(1)} %get-tuple-element.89.refs_6_.refs_7_), channel_id=1, source_target_pairs={{3,2},{7,6},{11,10},{15,14},{19,18},{23,22},{27,26},{31,30}} | collective-permute-start | bytes 393224 | tf_op jit(solution)/shard_map/ppermute | solution.py:508
  21.2 0.7 %collective-permute-start.12 = (bf16[32,2048]{1,0:T(8,128)(2,1)S(1)}, bf16[32,2048]{1,0:T(8,128)(2,1)S(1)}, u32[]{:S(2)}, u32[]{:S(2)}) collective-permute-start(bf16[32,2048]{1,0:T(8,128)(2,1)S(1)} %get-tuple-element.91.refs_6_.refs_9_), channel_id=1, source_target_pairs={{2,1},{6,5},{10,9},{14,13},{18,17},{22,21},{26,25},{30,29}} | collective-permute-start | bytes 393224 | tf_op jit(solution)/shard_map/ppermute | solution.py:508
  23.5 2.6 %collective-permute-start.19 = (bf16[128,512]{1,0:T(8,128)(2,1)S(1)}, bf16[128,512]{1,0:T(8,128)(2,1)S(1)}, u32[]{:S(2)}, u32[]{:S(2)}) collective-permute-start(bf16[128,512]{1,0:T(8,128)(2,1)S(1)} %columns6.1), channel_id=1, source_target_pairs={{0,24},{4,28},{8,16},{12,20},{16,8},{20,12},{24,0},{28,4},{1,25},{... | collective-permute-start | bytes 393224 | tf_op jit(solution)/shard_map/ppermute | solution.py:480
  26.1 1.3 %collective-permute-start.17 = (bf16[32,2048]{1,0:T(8,128)(2,1)S(1)}, bf16[32,2048]{1,0:T(8,128)(2,1)S(1)}, u32[]{:S(2)}, u32[]{:S(2)}) collective-permute-start(bf16[32,2048]{1,0:T(8,128)(2,1)S(1)} %get-tuple-element.94.refs_7_.refs_10_), channel_id=1, source_target_pairs={{1,0},{5,4},{9,8},{13,12},{17,16},{21,20},{25,24},{29,28}} | collective-permute-start | bytes 393224 | tf_op jit(solution)/shard_map/ppermute | solution.py:508
  27.4 1.3 %collective-permute-start.18 = (bf16[32,2048]{1,0:T(8,128)(2,1)S(1)}, bf16[32,2048]{1,0:T(8,128)(2,1)S(1)}, u32[]{:S(2)}, u32[]{:S(2)}) collective-permute-start(bf16[32,2048]{1,0:T(8,128)(2,1)S(1)} %get-tuple-element.95.refs_6_.refs_11_), channel_id=1, source_target_pairs={{1,0},{5,4},{9,8},{13,12},{17,16},{21,20},{25,24},{29,28}} | collective-permute-start | bytes 393224 | tf_op jit(solution)/shard_map/ppermute | solution.py:508
  28.8 1.3 %collective-permute-start.14 = (bf16[32,2048]{1,0:T(8,128)(2,1)S(1)}, bf16[32,2048]{1,0:T(8,128)(2,1)S(1)}, u32[]{:S(2)}, u32[]{:S(2)}) collective-permute-start(bf16[32,2048]{1,0:T(8,128)(2,1)S(1)} %get-tuple-element.96.refs_7_.refs_10_), channel_id=1, source_target_pairs={{1,0},{5,4},{9,8},{13,12},{17,16},{21,20},{25,24},{29,28}} | collective-permute-start | bytes 393224 | tf_op jit(solution)/shard_map/ppermute | solution.py:508
  30.1 1.3 %collective-permute-start.16 = (bf16[32,2048]{1,0:T(8,128)(2,1)S(1)}, bf16[32,2048]{1,0:T(8,128)(2,1)S(1)}, u32[]{:S(2)}, u32[]{:S(2)}) collective-permute-start(bf16[32,2048]{1,0:T(8,128)(2,1)S(1)} %get-tuple-element.97.refs_12_.refs_0_.refs_11_), channel_id=1, source_target_pairs={{1,0},{5,4},{9,8},{13,12},{17,16},{21,20},{25,24},{29,28}} | collective-permute-start | bytes 393224 | tf_op jit(solution)/shard_map/ppermute | solution.py:508
  32.1 4.9 %collective-permute-done.17.refs_0_ = bf16[32,2048]{1,0:T(8,128)(2,1)S(1)} collective-permute-done((bf16[32,2048]{1,0:T(8,128)(2,1)S(1)}, bf16[32,2048]{1,0:T(8,128)(2,1)S(1)}, u32[]{:S(2)}, u32[]{:S(2)}) %collective-permute-start.17) | collective-permute-done | bytes 131104 | tf_op jit(solution)/shard_map/ppermute | solution.py:508
  37.0 1.5 %collective-permute-start.21 = (bf16[128,512]{1,0:T(8,128)(2,1)S(1)}, bf16[128,512]{1,0:T(8,128)(2,1)S(1)}, u32[]{:S(2)}, u32[]{:S(2)}) collective-permute-start(bf16[128,512]{1,0:T(8,128)(2,1)S(1)} %columns4.1), channel_id=1, source_target_pairs={{0,16},{4,20},{8,24},{12,28},{16,0},{20,4},{24,8},{28,12},{1,17},{... | collective-permute-start | bytes 393224 | tf_op jit(solution)/shard_map/ppermute | solution.py:480
  38.5 0.8 %tick3_a_late.1 = (bf16[32,2048]{1,0:T(8,128)(2,1)S(1)}, bf16[32,512]{1,0:T(8,128)(2,1)S(1)}) custom-call(bf16[32,2048]{1,0:T(8,128)(2,1)S(1)} %collective-permute-done.17.refs_0_, bf16[4,32,128]{2,1,0:T(8,128)(2,1)S(1)} %get-tuple-element.81.refs_1_, f32[64,128]{1,0:T(8,128)S(1)} %get-tuple-element.79.refs_2_.refs_3_, ...), custom_call_target="tpu_custom_call" | custom-call | flops 1150000000 | tf_op jit(solution)/shard_map/tick3_a_late/pallas_call | solution.py:310
  39.9 0.8 %tick3_a_early.1 = (bf16[32,2048]{1,0:T(8,128)(2,1)S(1)}, bf16[64,512]{1,0:T(8,128)(2,1)S(1)}, bf16[32,2048]{1,0:T(8,128)(2,1)S(1)}) custom-call(bf16[32,2048]{1,0:T(8,128)(2,1)S(1)} %collective-permute-done.17.refs_0_, bf16[32,2048]{1,0:T(8,128)(2,1)S(1)} %collective-permute-done.18.refs_1_, bf16[4,32,256]{2,1,0:T(8,128)(2,1)S(1)} %get-tuple-element.78.refs_2_, ...), custom_call_target="tpu_custom_call" | custom-call | flops 1150000000 | tf_op jit(solution)/shard_map/tick3_a_early/pallas_call | solution.py:310
  40.7 2.5 %collective-permute-start.22 = (bf16[64,512]{1,0:T(8,128)(2,1)S(1)}, bf16[64,512]{1,0:T(8,128)(2,1)S(1)}, u32[]{:S(2)}, u32[]{:S(2)}) collective-permute-start(bf16[64,512]{1,0:T(8,128)(2,1)S(1)} %get-tuple-element.115.refs_17_), channel_id=1, source_target_pairs={{0,24},{4,28},{8,16},{12,20},{16,8},{20,12},{24,0},{28,4},{1,25},{... | collective-permute-start | bytes 196616 | tf_op jit(solution)/shard_map/ppermute | solution.py:480
  43.2 0.9 %collective-permute-start.23 = (bf16[32,2048]{1,0:T(8,128)(2,1)S(1)}, bf16[32,2048]{1,0:T(8,128)(2,1)S(1)}, u32[]{:S(2)}, u32[]{:S(2)}) collective-permute-start(bf16[32,2048]{1,0:T(8,128)(2,1)S(1)} %get-tuple-element.118), channel_id=1, source_target_pairs={{0,8},{4,12},{8,0},{12,4},{16,24},{20,28},{24,16},{28,20},{1,9},{5... | collective-permute-start | bytes 393224 | tf_op jit(solution)/shard_map/ppermute | solution.py:480
  44.1 0.8 %tick3_b_late.1 = (bf16[32,2048]{1,0:T(8,128)(2,1)S(1)}, bf16[32,512]{1,0:T(8,128)(2,1)S(1)}) custom-call(bf16[32,2048]{1,0:T(8,128)(2,1)S(1)} %collective-permute-done.14.refs_0_, bf16[4,32,128]{2,1,0:T(8,128)(2,1)S(1)} %get-tuple-element.85.refs_1_, f32[64,128]{1,0:T(8,128)S(1)} %get-tuple-element.86.refs_2_.refs_3_, ...), custom_call_target="tpu_custom_call" | custom-call | flops 1150000000 | tf_op jit(solution)/shard_map/tick3_b_late/pallas_call | solution.py:310
  44.9 1.6 %collective-permute-done.22.refs_21_.refs_8_ = bf16[64,512]{1,0:T(8,128)(2,1)S(1)} collective-permute-done((bf16[64,512]{1,0:T(8,128)(2,1)S(1)}, bf16[64,512]{1,0:T(8,128)(2,1)S(1)}, u32[]{:S(2)}, u32[]{:S(2)}) %collective-permute-start.22) | collective-permute-done | bytes 65568 | tf_op jit(solution)/shard_map/ppermute | solution.py:480
  46.5 0.9 %tick3_b_early.1 = (bf16[128,512]{1,0:T(8,128)(2,1)S(1)}, bf16[64,512]{1,0:T(8,128)(2,1)S(1)}, bf16[32,2048]{1,0:T(8,128)(2,1)S(1)}, bf16[32,2048]{1,0:T(8,128)(...) custom-call(bf16[32,2048]{1,0:T(8,128)(2,1)S(1)} %collective-permute-done.14.refs_0_, ...), custom_call_target="tpu_custom_call" | custom-call | flops 1150000000 | tf_op jit(solution)/shard_map/tick3_b_early/pallas_call | solution.py:310
  47.4 2.4 %collective-permute-start.24 = (bf16[64,512]{1,0:T(8,128)(2,1)S(1)}, bf16[64,512]{1,0:T(8,128)(2,1)S(1)}, u32[]{:S(2)}, u32[]{:S(2)}) collective-permute-start(bf16[64,512]{1,0:T(8,128)(2,1)S(1)} %get-tuple-element.119), channel_id=1, source_target_pairs={{0,24},{4,28},{8,16},{12,20},{16,8},{20,12},{24,0},{28,4},{1,25},{... | collective-permute-start | bytes 196616 | tf_op jit(solution)/shard_map/ppermute | solution.py:480
  49.8 0.7 %collective-permute-start.25 = (bf16[32,2048]{1,0:T(8,128)(2,1)S(1)}, bf16[32,2048]{1,0:T(8,128)(2,1)S(1)}, u32[]{:S(2)}, u32[]{:S(2)}) collective-permute-start(bf16[32,2048]{1,0:T(8,128)(2,1)S(1)} %get-tuple-element.120), channel_id=1, source_target_pairs={{0,8},{4,12},{8,0},{12,4},{16,24},{20,28},{24,16},{28,20},{1,9},{5... | collective-permute-start | bytes 393224 | tf_op jit(solution)/shard_map/ppermute | solution.py:480
  51.0 1.6 %collective-permute-start.30 = (bf16[32,2048]{1,0:T(8,128)(2,1)S(1)}, bf16[32,2048]{1,0:T(8,128)(2,1)S(1)}, u32[]{:S(2)}, u32[]{:S(2)}) collective-permute-start(bf16[32,2048]{1,0:T(8,128)(2,1)S(1)} %get-tuple-element.127), channel_id=1, source_target_pairs={{0,12},{4,8},{8,4},{12,0},{16,28},{20,24},{24,20},{28,16},{1,13},{... | collective-permute-start | bytes 393224 | tf_op jit(solution)/shard_map/ppermute | solution.py:480
  52.8 2.9 %collective-permute-done.25.refs_6_.refs_3_ = bf16[32,2048]{1,0:T(8,128)(2,1)S(1)} collective-permute-done((bf16[32,2048]{1,0:T(8,128)(2,1)S(1)}, bf16[32,2048]{1,0:T(8,128)(2,1)S(1)}, u32[]{:S(2)}, u32[]{:S(2)}) %collective-permute-start.25) | collective-permute-done | bytes 131104 | tf_op jit(solution)/shard_map/ppermute | solution.py:480
  56.7 0.8 %collective-permute-done.27.first_ref = bf16[128,512]{1,0:T(8,128)(2,1)S(1)} collective-permute-done((bf16[128,512]{1,0:T(8,128)(2,1)S(1)}, bf16[128,512]{1,0:T(8,128)(2,1)S(1)}, u32[]{:S(2)}, u32[]{:S(2)}) %collective-permute-start.27) | collective-permute-done | bytes 131104 | tf_op jit(solution)/shard_map/ppermute | solution.py:480
  57.8 1.1 %finish.1 = (bf16[128,2048]{1,0:T(8,128)(2,1)}, f32[256,512]{1,0:T(8,128)}, f32[1,256]{1,0:T(1,128)}) custom-call(f32[256,512]{1,0:T(8,128)S(1)} %get-tuple-element.121.own_ref, bf16[128,512]{1,0:T(8,128)(2,1)S(1)} %collective-permute-done.27.first_ref, bf16[128,512]{1,0:T(8,128)(2,1)S(1)} %collective-permute-done.28.second_ref, ...), custom_call_target="tpu_custom_call" | custom-call | tf_op jit(solution)/shard_map/finish/pallas_call | solution.py:559
  (61 shorter events, 8.5 us)
Async XLA Ops:
  0.6 4.5 %copy-start = (bf16[1,2048,512]{2,1,0:T(8,128)(2,1)S(1)}, bf16[1,2048,512]{2,1,0:T(8,128)(2,1)}, u32[]{:S(2)}) copy-start(bf16[1,2048,512]{2,1,0:T(8,128)(2,1)} %param.11) | copy-start | bytes 6291460
  2.0 6.3 %collective-permute-start = (bf16[16,4608]{1,0:T(8,128)(2,1)S(1)}, bf16[16,4608]{1,0:T(8,128)(2,1)S(1)}, u32[]{:S(2)}, u32[]{:S(2)}) collective-permute-start(bf16[16,4608]{1,0:T(8,128)(2,1)S(1)} %get-tuple-element.68), channel_id=1, source_target_pairs={{0,4},{4,0},{8,12},{12,8},{16,20},{20,16},{24,28},{28,24},{1,5},{5... | collective-permute-start | bytes 442376 | tf_op jit(solution)/shard_map/ppermute | solution.py:480
  2.5 7.3 %collective-permute-start.1 = (bf16[16,4608]{1,0:T(8,128)(2,1)S(1)}, bf16[16,4608]{1,0:T(8,128)(2,1)S(1)}, u32[]{:S(2)}, u32[]{:S(2)}) collective-permute-start(bf16[16,4608]{1,0:T(8,128)(2,1)S(1)} %get-tuple-element.69), channel_id=1, source_target_pairs={{0,8},{4,12},{8,0},{12,4},{16,24},{20,28},{24,16},{28,20},{1,9},{5... | collective-permute-start | bytes 442376 | tf_op jit(solution)/shard_map/ppermute | solution.py:480
  5.1 7.3 %collective-permute-start.2 = (bf16[16,4608]{1,0:T(8,128)(2,1)S(1)}, bf16[16,4608]{1,0:T(8,128)(2,1)S(1)}, u32[]{:S(2)}, u32[]{:S(2)}) collective-permute-start(bf16[16,4608]{1,0:T(8,128)(2,1)S(1)} %get-tuple-element.70), channel_id=1, source_target_pairs={{0,12},{4,8},{8,4},{12,0},{16,28},{20,24},{24,20},{28,16},{1,13},{... | collective-permute-start | bytes 442376 | tf_op jit(solution)/shard_map/ppermute | solution.py:480
  6.4 12.4 %collective-permute-start.6 = (bf16[80,2048]{1,0:T(8,128)(2,1)S(1)}, bf16[80,2048]{1,0:T(8,128)(2,1)S(1)}, u32[]{:S(2)}, u32[]{:S(2)}) collective-permute-start(bf16[80,2048]{1,0:T(8,128)(2,1)S(1)} %get-tuple-element.77), channel_id=1, source_target_pairs={{0,16},{4,20},{8,24},{12,28},{16,0},{20,4},{24,8},{28,12},{1,17},{... | collective-permute-start | bytes 983048 | tf_op jit(solution)/shard_map/ppermute | solution.py:480
  8.2 5.6 %collective-permute-start.3 = (bf16[16,4608]{1,0:T(8,128)(2,1)S(1)}, bf16[16,4608]{1,0:T(8,128)(2,1)S(1)}, u32[]{:S(2)}, u32[]{:S(2)}) collective-permute-start(bf16[16,4608]{1,0:T(8,128)(2,1)S(1)} %get-tuple-element.74), channel_id=1, source_target_pairs={{0,4},{4,0},{8,12},{12,8},{16,20},{20,16},{24,28},{28,24},{1,5},{5... | collective-permute-start | bytes 442376 | tf_op jit(solution)/shard_map/ppermute | solution.py:480
  8.3 7.8 %collective-permute-start.4 = (bf16[16,4608]{1,0:T(8,128)(2,1)S(1)}, bf16[16,4608]{1,0:T(8,128)(2,1)S(1)}, u32[]{:S(2)}, u32[]{:S(2)}) collective-permute-start(bf16[16,4608]{1,0:T(8,128)(2,1)S(1)} %get-tuple-element.75), channel_id=1, source_target_pairs={{0,8},{4,12},{8,0},{12,4},{16,24},{20,28},{24,16},{28,20},{1,9},{5... | collective-permute-start | bytes 442376 | tf_op jit(solution)/shard_map/ppermute | solution.py:480
  9.8 9.0 %collective-permute-start.5 = (bf16[16,4608]{1,0:T(8,128)(2,1)S(1)}, bf16[16,4608]{1,0:T(8,128)(2,1)S(1)}, u32[]{:S(2)}, u32[]{:S(2)}) collective-permute-start(bf16[16,4608]{1,0:T(8,128)(2,1)S(1)} %get-tuple-element.76), channel_id=1, source_target_pairs={{0,12},{4,8},{8,4},{12,0},{16,28},{20,24},{24,20},{28,16},{1,13},{... | collective-permute-start | bytes 442376 | tf_op jit(solution)/shard_map/ppermute | solution.py:480
  13.1 7.4 %collective-permute-start.8 = (bf16[32,2048]{1,0:T(8,128)(2,1)S(1)}, bf16[32,2048]{1,0:T(8,128)(2,1)S(1)}, u32[]{:S(2)}, u32[]{:S(2)}) collective-permute-start(bf16[32,2048]{1,0:T(8,128)(2,1)S(1)} %get-tuple-element.82.refs_7_.refs_6_), channel_id=1, source_target_pairs={{3,2},{7,6},{11,10},{15,14},{19,18},{23,22},{27,26},{31,30}} | collective-permute-start | bytes 393224 | tf_op jit(solution)/shard_map/ppermute | solution.py:508
  13.8 7.4 %collective-permute-start.9 = (bf16[32,2048]{1,0:T(8,128)(2,1)S(1)}, bf16[32,2048]{1,0:T(8,128)(2,1)S(1)}, u32[]{:S(2)}, u32[]{:S(2)}) collective-permute-start(bf16[32,2048]{1,0:T(8,128)(2,1)S(1)} %get-tuple-element.83.refs_5_.refs_7_), channel_id=1, source_target_pairs={{3,2},{7,6},{11,10},{15,14},{19,18},{23,22},{27,26},{31,30}} | collective-permute-start | bytes 393224 | tf_op jit(solution)/shard_map/ppermute | solution.py:508
  19.1 2.8 %collective-permute-start.7 = (bf16[32,2048]{1,0:T(8,128)(2,1)S(1)}, bf16[32,2048]{1,0:T(8,128)(2,1)S(1)}, u32[]{:S(2)}, u32[]{:S(2)}) collective-permute-start(bf16[32,2048]{1,0:T(8,128)(2,1)S(1)} %get-tuple-element.87.refs_7_.refs_6_), channel_id=1, source_target_pairs={{3,2},{7,6},{11,10},{15,14},{19,18},{23,22},{27,26},{31,30}} | collective-permute-start | bytes 393224 | tf_op jit(solution)/shard_map/ppermute | solution.py:508
  19.8 2.8 %collective-permute-start.13 = (bf16[32,2048]{1,0:T(8,128)(2,1)S(1)}, bf16[32,2048]{1,0:T(8,128)(2,1)S(1)}, u32[]{:S(2)}, u32[]{:S(2)}) collective-permute-start(bf16[32,2048]{1,0:T(8,128)(2,1)S(1)} %get-tuple-element.89.refs_6_.refs_7_), channel_id=1, source_target_pairs={{3,2},{7,6},{11,10},{15,14},{19,18},{23,22},{27,26},{31,30}} | collective-permute-start | bytes 393224 | tf_op jit(solution)/shard_map/ppermute | solution.py:508
  20.5 5.6 %collective-permute-start.11 = (bf16[32,2048]{1,0:T(8,128)(2,1)S(1)}, bf16[32,2048]{1,0:T(8,128)(2,1)S(1)}, u32[]{:S(2)}, u32[]{:S(2)}) collective-permute-start(bf16[32,2048]{1,0:T(8,128)(2,1)S(1)} %get-tuple-element.90.refs_7_.refs_8_), channel_id=1, source_target_pairs={{2,1},{6,5},{10,9},{14,13},{18,17},{22,21},{26,25},{30,29}} | collective-permute-start | bytes 393224 | tf_op jit(solution)/shard_map/ppermute | solution.py:508
  21.2 6.2 %collective-permute-start.12 = (bf16[32,2048]{1,0:T(8,128)(2,1)S(1)}, bf16[32,2048]{1,0:T(8,128)(2,1)S(1)}, u32[]{:S(2)}, u32[]{:S(2)}) collective-permute-start(bf16[32,2048]{1,0:T(8,128)(2,1)S(1)} %get-tuple-element.91.refs_6_.refs_9_), channel_id=1, source_target_pairs={{2,1},{6,5},{10,9},{14,13},{18,17},{22,21},{26,25},{30,29}} | collective-permute-start | bytes 393224 | tf_op jit(solution)/shard_map/ppermute | solution.py:508
  21.9 6.8 %collective-permute-start.10 = (bf16[32,2048]{1,0:T(8,128)(2,1)S(1)}, bf16[32,2048]{1,0:T(8,128)(2,1)S(1)}, u32[]{:S(2)}, u32[]{:S(2)}) collective-permute-start(bf16[32,2048]{1,0:T(8,128)(2,1)S(1)} %get-tuple-element.92.refs_7_.refs_8_), channel_id=1, source_target_pairs={{2,1},{6,5},{10,9},{14,13},{18,17},{22,21},{26,25},{30,29}} | collective-permute-start | bytes 393224 | tf_op jit(solution)/shard_map/ppermute | solution.py:508
  22.6 7.4 %collective-permute-start.15 = (bf16[32,2048]{1,0:T(8,128)(2,1)S(1)}, bf16[32,2048]{1,0:T(8,128)(2,1)S(1)}, u32[]{:S(2)}, u32[]{:S(2)}) collective-permute-start(bf16[32,2048]{1,0:T(8,128)(2,1)S(1)} %get-tuple-element.93.refs_6_.after_ref.refs_0_.refs_9_), channel_id=1, source_target_pairs={{2,1},{6,5},{10,9},{14,13},{18,17},{22,21},{26,25},{30,29}} | collective-permute-start | bytes 393224 | tf_op jit(solution)/shard_map/ppermute | solution.py:508
  23.5 7.9 %collective-permute-start.19 = (bf16[128,512]{1,0:T(8,128)(2,1)S(1)}, bf16[128,512]{1,0:T(8,128)(2,1)S(1)}, u32[]{:S(2)}, u32[]{:S(2)}) collective-permute-start(bf16[128,512]{1,0:T(8,128)(2,1)S(1)} %columns6.1), channel_id=1, source_target_pairs={{0,24},{4,28},{8,16},{12,20},{16,8},{20,12},{24,0},{28,4},{1,25},{... | collective-permute-start | bytes 393224 | tf_op jit(solution)/shard_map/ppermute | solution.py:480
  26.1 10.9 %collective-permute-start.17 = (bf16[32,2048]{1,0:T(8,128)(2,1)S(1)}, bf16[32,2048]{1,0:T(8,128)(2,1)S(1)}, u32[]{:S(2)}, u32[]{:S(2)}) collective-permute-start(bf16[32,2048]{1,0:T(8,128)(2,1)S(1)} %get-tuple-element.94.refs_7_.refs_10_), channel_id=1, source_target_pairs={{1,0},{5,4},{9,8},{13,12},{17,16},{21,20},{25,24},{29,28}} | collective-permute-start | bytes 393224 | tf_op jit(solution)/shard_map/ppermute | solution.py:508
  27.4 12.4 %collective-permute-start.18 = (bf16[32,2048]{1,0:T(8,128)(2,1)S(1)}, bf16[32,2048]{1,0:T(8,128)(2,1)S(1)}, u32[]{:S(2)}, u32[]{:S(2)}) collective-permute-start(bf16[32,2048]{1,0:T(8,128)(2,1)S(1)} %get-tuple-element.95.refs_6_.refs_11_), channel_id=1, source_target_pairs={{1,0},{5,4},{9,8},{13,12},{17,16},{21,20},{25,24},{29,28}} | collective-permute-start | bytes 393224 | tf_op jit(solution)/shard_map/ppermute | solution.py:508
  28.8 14.4 %collective-permute-start.14 = (bf16[32,2048]{1,0:T(8,128)(2,1)S(1)}, bf16[32,2048]{1,0:T(8,128)(2,1)S(1)}, u32[]{:S(2)}, u32[]{:S(2)}) collective-permute-start(bf16[32,2048]{1,0:T(8,128)(2,1)S(1)} %get-tuple-element.96.refs_7_.refs_10_), channel_id=1, source_target_pairs={{1,0},{5,4},{9,8},{13,12},{17,16},{21,20},{25,24},{29,28}} | collective-permute-start | bytes 393224 | tf_op jit(solution)/shard_map/ppermute | solution.py:508
  30.1 16.4 %collective-permute-start.16 = (bf16[32,2048]{1,0:T(8,128)(2,1)S(1)}, bf16[32,2048]{1,0:T(8,128)(2,1)S(1)}, u32[]{:S(2)}, u32[]{:S(2)}) collective-permute-start(bf16[32,2048]{1,0:T(8,128)(2,1)S(1)} %get-tuple-element.97.refs_12_.refs_0_.refs_11_), channel_id=1, source_target_pairs={{1,0},{5,4},{9,8},{13,12},{17,16},{21,20},{25,24},{29,28}} | collective-permute-start | bytes 393224 | tf_op jit(solution)/shard_map/ppermute | solution.py:508
  31.5 15.1 %collective-permute-start.20 = (bf16[128,512]{1,0:T(8,128)(2,1)S(1)}, bf16[128,512]{1,0:T(8,128)(2,1)S(1)}, u32[]{:S(2)}, u32[]{:S(2)}) collective-permute-start(bf16[128,512]{1,0:T(8,128)(2,1)S(1)} %columns2.1), channel_id=1, source_target_pairs={{0,8},{4,12},{8,0},{12,4},{16,24},{20,28},{24,16},{28,20},{1,9},{5... | collective-permute-start | bytes 393224 | tf_op jit(solution)/shard_map/ppermute | solution.py:480
  37.0 9.5 %collective-permute-start.21 = (bf16[128,512]{1,0:T(8,128)(2,1)S(1)}, bf16[128,512]{1,0:T(8,128)(2,1)S(1)}, u32[]{:S(2)}, u32[]{:S(2)}) collective-permute-start(bf16[128,512]{1,0:T(8,128)(2,1)S(1)} %columns4.1), channel_id=1, source_target_pairs={{0,16},{4,20},{8,24},{12,28},{16,0},{20,4},{24,8},{28,12},{1,17},{... | collective-permute-start | bytes 393224 | tf_op jit(solution)/shard_map/ppermute | solution.py:480
  40.7 5.8 %collective-permute-start.22 = (bf16[64,512]{1,0:T(8,128)(2,1)S(1)}, bf16[64,512]{1,0:T(8,128)(2,1)S(1)}, u32[]{:S(2)}, u32[]{:S(2)}) collective-permute-start(bf16[64,512]{1,0:T(8,128)(2,1)S(1)} %get-tuple-element.115.refs_17_), channel_id=1, source_target_pairs={{0,24},{4,28},{8,16},{12,20},{16,8},{20,12},{24,0},{28,4},{1,25},{... | collective-permute-start | bytes 196616 | tf_op jit(solution)/shard_map/ppermute | solution.py:480
  43.2 7.8 %collective-permute-start.23 = (bf16[32,2048]{1,0:T(8,128)(2,1)S(1)}, bf16[32,2048]{1,0:T(8,128)(2,1)S(1)}, u32[]{:S(2)}, u32[]{:S(2)}) collective-permute-start(bf16[32,2048]{1,0:T(8,128)(2,1)S(1)} %get-tuple-element.118), channel_id=1, source_target_pairs={{0,8},{4,12},{8,0},{12,4},{16,24},{20,28},{24,16},{28,20},{1,9},{5... | collective-permute-start | bytes 393224 | tf_op jit(solution)/shard_map/ppermute | solution.py:480
  47.4 5.3 %collective-permute-start.24 = (bf16[64,512]{1,0:T(8,128)(2,1)S(1)}, bf16[64,512]{1,0:T(8,128)(2,1)S(1)}, u32[]{:S(2)}, u32[]{:S(2)}) collective-permute-start(bf16[64,512]{1,0:T(8,128)(2,1)S(1)} %get-tuple-element.119), channel_id=1, source_target_pairs={{0,24},{4,28},{8,16},{12,20},{16,8},{20,12},{24,0},{28,4},{1,25},{... | collective-permute-start | bytes 196616 | tf_op jit(solution)/shard_map/ppermute | solution.py:480
  49.8 5.8 %collective-permute-start.25 = (bf16[32,2048]{1,0:T(8,128)(2,1)S(1)}, bf16[32,2048]{1,0:T(8,128)(2,1)S(1)}, u32[]{:S(2)}, u32[]{:S(2)}) collective-permute-start(bf16[32,2048]{1,0:T(8,128)(2,1)S(1)} %get-tuple-element.120), channel_id=1, source_target_pairs={{0,8},{4,12},{8,0},{12,4},{16,24},{20,28},{24,16},{28,20},{1,9},{5... | collective-permute-start | bytes 393224 | tf_op jit(solution)/shard_map/ppermute | solution.py:480
  50.5 5.2 %collective-permute-start.26 = (bf16[128,512]{1,0:T(8,128)(2,1)S(1)}, bf16[128,512]{1,0:T(8,128)(2,1)S(1)}, u32[]{:S(2)}, u32[]{:S(2)}) collective-permute-start(bf16[128,512]{1,0:T(8,128)(2,1)S(1)} %get-tuple-element.117.refs_0_.refs_4_), channel_id=1, source_target_pairs={{0,16},{4,20},{8,24},{12,28},{16,0},{20,4},{24,8},{28,12},{1,17},{... | collective-permute-start | bytes 393224 | tf_op jit(solution)/shard_map/ppermute | solution.py:480
  51.0 5.8 %collective-permute-start.29 = (bf16[32,2048]{1,0:T(8,128)(2,1)S(1)}, bf16[32,2048]{1,0:T(8,128)(2,1)S(1)}, u32[]{:S(2)}, u32[]{:S(2)}) collective-permute-start(bf16[32,2048]{1,0:T(8,128)(2,1)S(1)} %get-tuple-element.126), channel_id=1, source_target_pairs={{0,4},{4,0},{8,12},{12,8},{16,20},{20,16},{24,28},{28,24},{1,5},{5... | collective-permute-start | bytes 393224 | tf_op jit(solution)/shard_map/ppermute | solution.py:480
  51.0 5.8 %collective-permute-start.30 = (bf16[32,2048]{1,0:T(8,128)(2,1)S(1)}, bf16[32,2048]{1,0:T(8,128)(2,1)S(1)}, u32[]{:S(2)}, u32[]{:S(2)}) collective-permute-start(bf16[32,2048]{1,0:T(8,128)(2,1)S(1)} %get-tuple-element.127), channel_id=1, source_target_pairs={{0,12},{4,8},{8,4},{12,0},{16,28},{20,24},{24,20},{28,16},{1,13},{... | collective-permute-start | bytes 393224 | tf_op jit(solution)/shard_map/ppermute | solution.py:480
  56.2 1.4 %collective-permute-start.27 = (bf16[128,512]{1,0:T(8,128)(2,1)S(1)}, bf16[128,512]{1,0:T(8,128)(2,1)S(1)}, u32[]{:S(2)}, u32[]{:S(2)}) collective-permute-start(bf16[128,512]{1,0:T(8,128)(2,1)S(1)} %get-tuple-element.122), channel_id=1, source_target_pairs={{0,4},{4,0},{8,12},{12,8},{16,20},{20,16},{24,28},{28,24},{1,5},{5... | collective-permute-start | bytes 393224 | tf_op jit(solution)/shard_map/ppermute | solution.py:480
  56.2 1.5 %collective-permute-start.28 = (bf16[128,512]{1,0:T(8,128)(2,1)S(1)}, bf16[128,512]{1,0:T(8,128)(2,1)S(1)}, u32[]{:S(2)}, u32[]{:S(2)}) collective-permute-start(bf16[128,512]{1,0:T(8,128)(2,1)S(1)} %get-tuple-element.123), channel_id=1, source_target_pairs={{0,4},{4,0},{8,12},{12,8},{16,20},{20,16},{24,28},{28,24},{1,5},{5... | collective-permute-start | bytes 393224 | tf_op jit(solution)/shard_map/ppermute | solution.py:480
  (1 other events, 0.7 us)

commit v12 on v11

--- a/solution.py
+++ b/solution.py
@@ -272,18 +272,26 @@
     at = place()[1]
     pieces = {2: outs[2]} if late == 2 else dict(enumerate(outs[2:]))
     piece = BLOCK * kv_width // model_width
+
+    def rows_for(k, block):
+        first = pl.multiple_of(lax.bitwise_xor(at, k) * piece, piece)
+        return blocks_ref[pl.ds(block * BLOCK + first, piece), :]
+
+    block = 0 if late == 2 else 1
     for k, out_ref in pieces.items():
-        first = pl.multiple_of(lax.bitwise_xor(at, k) * piece, piece)
-        here = blocks_ref[pl.ds(first_row + first, piece), :]
         if k == 2:
-            out_ref[:piece, :] = here
+            out_ref[:piece, :] = rows_for(2, block)
             for g in range(model_width // kv_width):
-                out_ref[piece:, g * kv_width : (g + 1) * kv_width] = values[
+                out_ref[piece : 2 * piece, g * kv_width : (g + 1) * kv_width] = values[
                     g * piece : (g + 1) * piece
                 ]
+            if block == 0:
+                out_ref[2 * piece :, :] = rows_for(3, 0)
+        elif k == 3:
+            out_ref[...] = rows_for(3, 1)
         else:
-            out_ref[:piece, :] = blocks_ref[pl.ds(first, piece), :]
-            out_ref[piece:, :] = here
+            out_ref[:piece, :] = rows_for(k, 0)
+            out_ref[piece:, :] = rows_for(k, 1)
 
 
 def tick_step(tick, grads, block, turned, gain, kept=(), late=(), after=(), name=""):
@@ -302,10 +310,11 @@
     if late:
         half = lax.axis_size("dp") // 2
         scratch += [pltpu.VMEM((2 * BLOCK, model_width), bf16), pltpu.VMEM(value, bf16)]
-        pieces = (2 * BLOCK // half, model_width)
-        shapes = [rows, (BLOCK, kv_width), pieces]
+        piece = BLOCK // half
+        shapes = [rows, (BLOCK, kv_width), (3 * piece, model_width)]
     if len(late) > 2:
-        shapes = [(2 * BLOCK, kv_width), (BLOCK, kv_width)] + [pieces] * half
+        shapes = [(2 * BLOCK, kv_width), (BLOCK, kv_width)]
+        shapes += [(2 * piece, model_width)] * 3 + [(piece, model_width)]
     parts = [part for _, part in grads]
     return pl.pallas_call(
         functools.partial(
@@ -342,7 +351,8 @@
     copy(up_ref.at[rows], up_out_ref.at[pl.ds(0, BLOCK)])
     up_out_ref[BLOCK:, :] = jnp.zeros((16, up_out_ref.shape[1]), jnp.bfloat16)
     if block == 1:
-        turn_kernel(rest[0], rest[-5 - half])
+        rest[2][...] = rest[1][...]
+        turn_kernel(rest[0], rest[3])
     for made in copies[:4]:
         made.wait()
     ids = seg_in_ref[...].astype(jnp.float32)
@@ -355,7 +365,7 @@
     copies[4].wait()
 
 
-def pack(block, half, piece, sources, weight=None):
+def pack(block, half, piece, sources, weight=None, gain=None):
     model_width = sources[0].shape[1]
     width = sum(source.shape[1] for source in sources[:3])
     bf16 = jnp.bfloat16
@@ -364,9 +374,12 @@
     outs = [jax.ShapeDtypeStruct((piece, width), bf16)] * half
     outs.append(jax.ShapeDtypeStruct((BLOCK + 16, model_width), bf16))
     if weight is not None:
-        operands.append(near(weight))
-        specs.append(VMEM)
-        outs = [jax.ShapeDtypeStruct(weight.shape[::-1], bf16)] + outs
+        operands += [near(weight), gain]
+        specs += [VMEM, VMEM]
+        outs = [
+            jax.ShapeDtypeStruct(gain.shape, gain.dtype),
+            jax.ShapeDtypeStruct(weight.shape[::-1], bf16),
+        ] + outs
     return pl.pallas_call(
         functools.partial(pack_kernel, block, half, piece),
         out_shape=tuple(outs),
@@ -384,22 +397,28 @@
 
 def columns_kernel(width, distance, first_ref, second_ref, *refs):
     out_ref = refs[-1]
+    if distance == 0:
+        came_ref, out_ref, handed_ref = refs[0], refs[-2], refs[-1]
+        handed_ref[...] = came_ref[came_ref.shape[0] - handed_ref.shape[0] :, :]
     there = lax.div(lax.bitwise_xor(place()[2], distance), 2)
     out_ref[:BLOCK, :] = first_ref[:, columns_of(there, width)]
     out_ref[BLOCK:, :] = second_ref[:, columns_of(there, width)]
 
 
-def columns_for(distance, blocks, after):
+def columns_for(distance, blocks, after, came=()):
     model_width = blocks[0][3].shape[1]
     width = 2 * model_width // lax.axis_size("dp")
-    return pl.pallas_call(
+    shapes = [(2 * BLOCK, width)] + [(array.shape[0] // 3, model_width) for array in came]
+    outs = [jax.ShapeDtypeStruct(shape, jnp.bfloat16) for shape in shapes]
+    results = pl.pallas_call(
         functools.partial(columns_kernel, width, distance),
-        out_shape=jax.ShapeDtypeStruct((2 * BLOCK, width), jnp.bfloat16),
-        in_specs=[VMEM] * 2 + [ANY] * len(after),
-        out_specs=VMEM,
+        out_shape=tuple(outs),
+        in_specs=[VMEM] * (2 + len(came)) + [ANY] * len(after),
+        out_specs=(VMEM,) * len(outs),
         name=f"columns{distance}",
         **params(0.0 if distance else 1.0),
-    )(blocks[0][3], blocks[1][3], *after)
+    )(blocks[0][3], blocks[1][3], *came, *after)
+    return results if came else results[0]
 
 
 def own_kernel(scale, weight_ref, gain_ref, after_ref, weight_out_ref, gain_out_ref):
@@ -421,8 +440,9 @@
     kv_width = own_out_ref.shape[1]
     parts = []
     for ref in refs[:6]:
-        for at in range(0, ref.shape[1], kv_width):
-            parts.append(ref[first:, at : at + kv_width] if ref.shape[1] > kv_width else ref[...])
+        beside = ref.shape[1] > kv_width
+        rows = slice(first, 2 * first) if beside else slice(0, ref.shape[0])
+        parts += [ref[rows, at : at + kv_width] for at in range(0, ref.shape[1], kv_width)]
     value = jnp.concatenate(parts, axis=0)
     mine = lax.rem(place()[2], 2)
 
@@ -445,9 +465,9 @@
     )
 
 
-def finish_kernel(half, own_ref, first_ref, second_ref, weight_ref, gain_ref, *refs):
-    first_rows_ref, pieces = refs[0], refs[1 : 1 + half]
-    rows_ref, out_ref, gain_out_ref = refs[1 + half :]
+def rows_kernel(half, first_rows_ref, handed_ref, *refs):
+    pieces = refs[:half]
+    rows_ref, token_ref = refs[half:]
     side, at, _ = place()
     piece = BLOCK // half
     for block in range(2):
@@ -457,7 +477,15 @@
             source, first = pieces[k], block * piece
             if k == 2:
                 source, first = (pieces[k] if block else first_rows_ref), 0
+            if k == 3:
+                source, first = (pieces[k] if block else handed_ref), 0
             rows_ref[rows, :] = source[first : first + piece, :]
+    token_ref[...] = jnp.zeros_like(token_ref)
+
+
+def finish_kernel(
+    own_ref, first_ref, second_ref, weight_ref, gain_ref, after_ref, out_ref, gain_out_ref
+):
     other = jnp.concatenate([first_ref[...], second_ref[...]], axis=0)
     total = own_ref[...] + other.astype(jnp.float32)
     out_ref[...] = total * gain_ref[:, :1]
@@ -484,9 +512,10 @@
     sources = (query, key, hidden, upstream, segments)
     pieces, ups = [], []
     for b in range(2):
-        *packed, up = pack(b, half, piece, sources, weight if b else None)
+        extra = (weight, norm_gain) if b else ()
+        *packed, up = pack(b, half, piece, sources, *extra)
         if b:
-            turned, *packed = packed
+            gain, turned, *packed = packed
         pieces.append([packed[0]] + [swap(packed[k], k) for k in range(1, half)])
         ups.append(swap(up, half) if b else up)
     whole = slice(0, UNIT)
@@ -495,9 +524,9 @@
     for b in range(2):
         block = block_probs(pieces[b], ups[b], BLOCK, model_width, kv_width, after)
         late, early = (ups[b], LATE), (ups[b], EARLY)
-        first = tick_step(0, [late], block, turned, norm_gain, name=UNITS[2 * b])
+        first = tick_step(0, [late], block, turned, gain, name=UNITS[2 * b])
         second = tick_step(
-            0, [late, early], block, turned, norm_gain, after=[first[0]], name=UNITS[2 * b + 1]
+            0, [late, early], block, turned, gain, after=[first[0]], name=UNITS[2 * b + 1]
         )
         blocks.append(block)
         kept += [[first], [second]]
@@ -519,7 +548,7 @@
                 out_specs=(VMEM, VMEM),
                 name="own",
                 **params(0.0),
-            )(near(weight), norm_gain, *after)
+            )(near(weight), near(gain), *after)
             columns = {6: swap(columns_for(6, blocks, after + [own_gain]), 6)}
         if last:
             waits = after + [columns[6]]
@@ -535,7 +564,7 @@
                 after = after + [columns[2], columns[4], first_value]
             done.append(
                 tick_step(
-                    tick, needs, blocks[u // 2], turned, norm_gain, kept[u] if last else (), late,
+                    tick, needs, blocks[u // 2], turned, gain, kept[u] if last else (), late,
                     after, name=UNITS[u],
                 )
             )
@@ -544,7 +573,8 @@
     values, last_value, *rows = done[3]
     rows = [rows[0]] + [swap(rows[k], k) for k in range(1, half)]
     last_value = swap(last_value, 6)
-    columns[0] = columns_for(0, blocks, [values, first_rows, last_value])
+    columns[0], handed = columns_for(0, blocks, [values, last_value], [first_rows])
+    handed = swap(handed, 1)
     values = [values, first_rows, rows[2], swap(values, 4), first_value, last_value]
     own, *other = pl.pallas_call(
         functools.partial(partial_kernel, shares, piece),
@@ -556,18 +586,28 @@
         **params(0.0),
     )(*[columns[k] for k in (0, 2, 4, 6)], *values)
     other = [swap(part, 1) for part in other]
-    input_grad, weight_grad, gain_grad = pl.pallas_call(
-        functools.partial(finish_kernel, half),
+    input_grad, token = pl.pallas_call(
+        functools.partial(rows_kernel, half),
         out_shape=(
             jax.ShapeDtypeStruct((tokens, model_width), bf16),
+            jax.ShapeDtypeStruct((8, 128), jnp.float32),
+        ),
+        in_specs=[VMEM] * (2 + half),
+        out_specs=(VMEM, VMEM),
+        name="rows",
+        **params(0.8),
+    )(first_rows, handed, *rows)
+    weight_grad, gain_grad = pl.pallas_call(
+        finish_kernel,
+        out_shape=(
             jax.ShapeDtypeStruct((shares, kv_width), jnp.float32),
             jax.ShapeDtypeStruct((1, shares), jnp.float32),
         ),
-        in_specs=[VMEM] * (6 + half),
-        out_specs=(VMEM,) * 3,
+        in_specs=[VMEM] * 5 + [ANY],
+        out_specs=(VMEM, VMEM),
         name="finish",
         **params(0.0),
-    )(own, *other, own_weight, own_gain, first_rows, *rows)
+    )(own, *other, own_weight, own_gain, token)
     return input_grad[None], weight_grad[None], gain_grad
 
 

time: 59.2 us -> 59.1 us (level)
  Pallas kernels: 8.49 us -> 9.7 us
  waiting for transfers between devices: 17.4 us -> 16.6 us
    pallas_call x1 -> x2, Pallas kernels: 1.12 us -> 1.83 us  [the longest x1 0.99 us: direct(): pl.pallas_call(finish_kernel, out_shape=(jax.ShapeDtypeStruct((shares, kv...]
    ppermute x19 -> x20, waiting for transfers between devices: 11.8 us -> 11.2 us  [swap(): return lax.ppermute(array, 'dp', [(i, i ^ k) for i in range(replicas)])]
    ppermute x19 -> x20, starting transfers between devices: 21.2 us -> 20.8 us  [swap(): return lax.ppermute(array, 'dp', [(i, i ^ k) for i in range(replicas)])]
  transfers between devices with their start and end apart: 31 -> 32, of which waited for: 10 -> 9; matrix products, arithmetic and copies ran while one was open for 0% -> 0% of each run, Pallas kernels for 10% -> 13%
where the time goes in v12:
time: 59.1 us; the launch traced here: 58.7 us
  starting transfers between devices  31.3 us (53%)
  waiting for transfers between devices  16.6 us (28%)
  Pallas kernels  9.7 us (16%)
  between operations  1.04 us (2%)
    ppermute x20, starting transfers between devices, swap(): return lax.ppermute(array, 'dp', [(i, i ^ k) for i in range(replicas)])  20.8 us
    ppermute x20, waiting for transfers between devices, swap(): return lax.ppermute(array, 'dp', [(i, i ^ k) for i in range(replicas)])  11.2 us
    ppermute x12, starting transfers between devices, direct(): lax.ppermute(unit[-1][0], 'section', hop)  10.5 us
    ppermute x12, waiting for transfers between devices, direct(): lax.ppermute(unit[-1][0], 'section', hop)  5.44 us
    pallas_call x16, Pallas kernels, tick_step(): pl.pallas_call(functools.partial(tick_kernel, tick, EARLY if low else LAT...  3.45 us
    pallas_call x2, Pallas kernels, pack(): pl.pallas_call(functools.partial(pack_kernel, block, half, piece), out_sh...  3.06 us
  transfers between devices with their start and end apart: 32, of which 9 were waited for; matrix products, arithmetic and copies ran while one was open for 0% of the time, Pallas kernels for 13%

profile of v12, /device:TPU:0, one launch (start us, length us, event | category | flops | bytes accessed | tf_op | source)
XLA Modules:
  0.0 58.7 jit_solution(9995061981847405539)
XLA Ops:
  0.7 1.4 %pack.2 = (bf16[16,4608]{1,0:T(8,128)(2,1)S(1)}, bf16[16,4608]{1,0:T(8,128)(2,1)S(1)}, bf16[16,4608]{1,0:T(8,128)(2,1)S(1)}, bf16[16,4608]{1,0:T(8,128)(2,1)S(1)}, bf16[80,2048]{1,0:T(8,128)(2,1)S(1)}) custom-call(bf16[128,2048]{1,0:T(8,128)(2,1)} %bitcast.8, bf16[128,512]{1,0:T(8,128)(2,1)} %bitcast.13, bf16[128,2048]{1,0:T(8,128)(2,1)} %bitcast.10, ...), custom_call_target="tpu_custom_call" | custom-call | flops 1380000000 | tf_op jit(solution)/shard_map/pack/pallas_call | solution.py:383
  2.5 2.6 %collective-permute-start.1 = (bf16[16,4608]{1,0:T(8,128)(2,1)S(1)}, bf16[16,4608]{1,0:T(8,128)(2,1)S(1)}, u32[]{:S(2)}, u32[]{:S(2)}) collective-permute-start(bf16[16,4608]{1,0:T(8,128)(2,1)S(1)} %get-tuple-element.74), channel_id=1, source_target_pairs={{0,8},{4,12},{8,0},{12,4},{16,24},{20,28},{24,16},{28,20},{1,9},{5... | collective-permute-start | bytes 442376 | tf_op jit(solution)/shard_map/ppermute | solution.py:508
  5.2 1.7 %pack.3 = (f32[1,2048]{1,0:T(1,128)S(1)}, bf16[512,2048]{1,0:T(8,128)(2,1)S(1)}, bf16[16,4608]{1,0:T(8,128)(2,1)S(1)}, bf16[16,4608]{1,0:T(8,128)(2,1)S(1)}, bf1...) custom-call(bf16[128,2048]{1,0:T(8,128)(2,1)} %bitcast.9, ...), custom_call_target="tpu_custom_call" | custom-call | flops 1380000000 | tf_op jit(solution)/shard_map/pack/pallas_call | solution.py:383
  6.9 1.8 %collective-permute-start.4 = (bf16[80,2048]{1,0:T(8,128)(2,1)S(1)}, bf16[80,2048]{1,0:T(8,128)(2,1)S(1)}, u32[]{:S(2)}, u32[]{:S(2)}) collective-permute-start(bf16[80,2048]{1,0:T(8,128)(2,1)S(1)} %get-tuple-element.82), channel_id=1, source_target_pairs={{0,16},{4,20},{8,24},{12,28},{16,0},{20,4},{24,8},{28,12},{1,17},{... | collective-permute-start | bytes 983048 | tf_op jit(solution)/shard_map/ppermute | solution.py:508
  8.8 1.5 %collective-permute-start.6 = (bf16[16,4608]{1,0:T(8,128)(2,1)S(1)}, bf16[16,4608]{1,0:T(8,128)(2,1)S(1)}, u32[]{:S(2)}, u32[]{:S(2)}) collective-permute-start(bf16[16,4608]{1,0:T(8,128)(2,1)S(1)} %get-tuple-element.85), channel_id=1, source_target_pairs={{0,8},{4,12},{8,0},{12,4},{16,24},{20,28},{24,16},{28,20},{1,9},{5... | collective-permute-start | bytes 442376 | tf_op jit(solution)/shard_map/ppermute | solution.py:508
  10.6 1.9 %collective-permute-done.2.refs_3_ = bf16[16,4608]{1,0:T(8,128)(2,1)S(1)} collective-permute-done((bf16[16,4608]{1,0:T(8,128)(2,1)S(1)}, bf16[16,4608]{1,0:T(8,128)(2,1)S(1)}, u32[]{:S(2)}, u32[]{:S(2)}) %collective-permute-start.2) | collective-permute-done | bytes 147488 | tf_op jit(solution)/shard_map/ppermute | solution.py:508
  12.8 0.7 %collective-permute-start.3 = (bf16[32,2048]{1,0:T(8,128)(2,1)S(1)}, bf16[32,2048]{1,0:T(8,128)(2,1)S(1)}, u32[]{:S(2)}, u32[]{:S(2)}) collective-permute-start(bf16[32,2048]{1,0:T(8,128)(2,1)S(1)} %get-tuple-element.81.refs_7_.refs_6_), channel_id=1, source_target_pairs={{3,2},{7,6},{11,10},{15,14},{19,18},{23,22},{27,26},{31,30}} | collective-permute-start | bytes 393224 | tf_op jit(solution)/shard_map/ppermute | solution.py:537
  13.5 0.7 %collective-permute-start.11 = (bf16[32,2048]{1,0:T(8,128)(2,1)S(1)}, bf16[32,2048]{1,0:T(8,128)(2,1)S(1)}, u32[]{:S(2)}, u32[]{:S(2)}) collective-permute-start(bf16[32,2048]{1,0:T(8,128)(2,1)S(1)} %get-tuple-element.88.refs_5_.refs_7_), channel_id=1, source_target_pairs={{3,2},{7,6},{11,10},{15,14},{19,18},{23,22},{27,26},{31,30}} | collective-permute-start | bytes 393224 | tf_op jit(solution)/shard_map/ppermute | solution.py:537
  14.2 1.9 %collective-permute-done.6.refs_2_ = bf16[16,4608]{1,0:T(8,128)(2,1)S(1)} collective-permute-done((bf16[16,4608]{1,0:T(8,128)(2,1)S(1)}, bf16[16,4608]{1,0:T(8,128)(2,1)S(1)}, u32[]{:S(2)}, u32[]{:S(2)}) %collective-permute-start.6) | collective-permute-done | bytes 147488 | tf_op jit(solution)/shard_map/ppermute | solution.py:508
  16.1 2.6 %collective-permute-done.7.refs_3_ = bf16[16,4608]{1,0:T(8,128)(2,1)S(1)} collective-permute-done((bf16[16,4608]{1,0:T(8,128)(2,1)S(1)}, bf16[16,4608]{1,0:T(8,128)(2,1)S(1)}, u32[]{:S(2)}, u32[]{:S(2)}) %collective-permute-start.7) | collective-permute-done | bytes 147488 | tf_op jit(solution)/shard_map/ppermute | solution.py:508
  19.1 0.7 %collective-permute-start.9 = (bf16[32,2048]{1,0:T(8,128)(2,1)S(1)}, bf16[32,2048]{1,0:T(8,128)(2,1)S(1)}, u32[]{:S(2)}, u32[]{:S(2)}) collective-permute-start(bf16[32,2048]{1,0:T(8,128)(2,1)S(1)} %get-tuple-element.93.refs_7_.refs_6_), channel_id=1, source_target_pairs={{3,2},{7,6},{11,10},{15,14},{19,18},{23,22},{27,26},{31,30}} | collective-permute-start | bytes 393224 | tf_op jit(solution)/shard_map/ppermute | solution.py:537
  19.8 0.7 %collective-permute-start.10 = (bf16[32,2048]{1,0:T(8,128)(2,1)S(1)}, bf16[32,2048]{1,0:T(8,128)(2,1)S(1)}, u32[]{:S(2)}, u32[]{:S(2)}) collective-permute-start(bf16[32,2048]{1,0:T(8,128)(2,1)S(1)} %get-tuple-element.94.refs_6_.refs_7_), channel_id=1, source_target_pairs={{3,2},{7,6},{11,10},{15,14},{19,18},{23,22},{27,26},{31,30}} | collective-permute-start | bytes 393224 | tf_op jit(solution)/shard_map/ppermute | solution.py:537
  21.2 0.7 %collective-permute-start.13 = (bf16[32,2048]{1,0:T(8,128)(2,1)S(1)}, bf16[32,2048]{1,0:T(8,128)(2,1)S(1)}, u32[]{:S(2)}, u32[]{:S(2)}) collective-permute-start(bf16[32,2048]{1,0:T(8,128)(2,1)S(1)} %get-tuple-element.96.refs_6_.refs_9_), channel_id=1, source_target_pairs={{2,1},{6,5},{10,9},{14,13},{18,17},{22,21},{26,25},{30,29}} | collective-permute-start | bytes 393224 | tf_op jit(solution)/shard_map/ppermute | solution.py:537
  23.5 2.6 %collective-permute-start.20 = (bf16[128,512]{1,0:T(8,128)(2,1)S(1)}, bf16[128,512]{1,0:T(8,128)(2,1)S(1)}, u32[]{:S(2)}, u32[]{:S(2)}) collective-permute-start(bf16[128,512]{1,0:T(8,128)(2,1)S(1)} %columns6.1), channel_id=1, source_target_pairs={{0,24},{4,28},{8,16},{12,20},{16,8},{20,12},{24,0},{28,4},{1,25},{... | collective-permute-start | bytes 393224 | tf_op jit(solution)/shard_map/ppermute | solution.py:508
  26.1 1.3 %collective-permute-start.12 = (bf16[32,2048]{1,0:T(8,128)(2,1)S(1)}, bf16[32,2048]{1,0:T(8,128)(2,1)S(1)}, u32[]{:S(2)}, u32[]{:S(2)}) collective-permute-start(bf16[32,2048]{1,0:T(8,128)(2,1)S(1)} %get-tuple-element.99.refs_7_.refs_10_), channel_id=1, source_target_pairs={{1,0},{5,4},{9,8},{13,12},{17,16},{21,20},{25,24},{29,28}} | collective-permute-start | bytes 393224 | tf_op jit(solution)/shard_map/ppermute | solution.py:537
  27.4 1.3 %collective-permute-start.14 = (bf16[32,2048]{1,0:T(8,128)(2,1)S(1)}, bf16[32,2048]{1,0:T(8,128)(2,1)S(1)}, u32[]{:S(2)}, u32[]{:S(2)}) collective-permute-start(bf16[32,2048]{1,0:T(8,128)(2,1)S(1)} %get-tuple-element.100.refs_6_.refs_11_), channel_id=1, source_target_pairs={{1,0},{5,4},{9,8},{13,12},{17,16},{21,20},{25,24},{29,28}} | collective-permute-start | bytes 393224 | tf_op jit(solution)/shard_map/ppermute | solution.py:537
  28.8 1.3 %collective-permute-start.18 = (bf16[32,2048]{1,0:T(8,128)(2,1)S(1)}, bf16[32,2048]{1,0:T(8,128)(2,1)S(1)}, u32[]{:S(2)}, u32[]{:S(2)}) collective-permute-start(bf16[32,2048]{1,0:T(8,128)(2,1)S(1)} %get-tuple-element.107.refs_7_.refs_10_), channel_id=1, source_target_pairs={{1,0},{5,4},{9,8},{13,12},{17,16},{21,20},{25,24},{29,28}} | collective-permute-start | bytes 393224 | tf_op jit(solution)/shard_map/ppermute | solution.py:537
  30.1 1.3 %collective-permute-start.19 = (bf16[32,2048]{1,0:T(8,128)(2,1)S(1)}, bf16[32,2048]{1,0:T(8,128)(2,1)S(1)}, u32[]{:S(2)}, u32[]{:S(2)}) collective-permute-start(bf16[32,2048]{1,0:T(8,128)(2,1)S(1)} %get-tuple-element.108.refs_12_.refs_0_.refs_11_), channel_id=1, source_target_pairs={{1,0},{5,4},{9,8},{13,12},{17,16},{21,20},{25,24},{29,28}} | collective-permute-start | bytes 393224 | tf_op jit(solution)/shard_map/ppermute | solution.py:537
  32.1 4.9 %collective-permute-done.12.refs_0_ = bf16[32,2048]{1,0:T(8,128)(2,1)S(1)} collective-permute-done((bf16[32,2048]{1,0:T(8,128)(2,1)S(1)}, bf16[32,2048]{1,0:T(8,128)(2,1)S(1)}, u32[]{:S(2)}, u32[]{:S(2)}) %collective-permute-start.12) | collective-permute-done | bytes 131104 | tf_op jit(solution)/shard_map/ppermute | solution.py:537
  37.0 1.5 %collective-permute-start.22 = (bf16[128,512]{1,0:T(8,128)(2,1)S(1)}, bf16[128,512]{1,0:T(8,128)(2,1)S(1)}, u32[]{:S(2)}, u32[]{:S(2)}) collective-permute-start(bf16[128,512]{1,0:T(8,128)(2,1)S(1)} %columns4.1), channel_id=1, source_target_pairs={{0,16},{4,20},{8,24},{12,28},{16,0},{20,4},{24,8},{28,12},{1,17},{... | collective-permute-start | bytes 393224 | tf_op jit(solution)/shard_map/ppermute | solution.py:508
  38.5 0.8 %tick3_a_late.1 = (bf16[32,2048]{1,0:T(8,128)(2,1)S(1)}, bf16[32,512]{1,0:T(8,128)(2,1)S(1)}) custom-call(bf16[32,2048]{1,0:T(8,128)(2,1)S(1)} %collective-permute-done.12.refs_0_, bf16[4,32,128]{2,1,0:T(8,128)(2,1)S(1)} %get-tuple-element.76.refs_1_, f32[64,128]{1,0:T(8,128)S(1)} %get-tuple-element.77.refs_2_.refs_3_, ...), custom_call_target="tpu_custom_call" | custom-call | flops 1150000000 | tf_op jit(solution)/shard_map/tick3_a_late/pallas_call | solution.py:319
  39.8 0.8 %tick3_a_early.1 = (bf16[32,2048]{1,0:T(8,128)(2,1)S(1)}, bf16[64,512]{1,0:T(8,128)(2,1)S(1)}, bf16[48,2048]{1,0:T(8,128)(2,1)S(1)}) custom-call(bf16[32,2048]{1,0:T(8,128)(2,1)S(1)} %collective-permute-done.12.refs_0_, bf16[32,2048]{1,0:T(8,128)(2,1)S(1)} %collective-permute-done.14.refs_1_, bf16[4,32,256]{2,1,0:T(8,128)(2,1)S(1)} %get-tuple-element.87.refs_2_, ...), custom_call_target="tpu_custom_call" | custom-call | flops 1150000000 | tf_op jit(solution)/shard_map/tick3_a_early/pallas_call | solution.py:319
  40.6 2.5 %collective-permute-start.23 = (bf16[64,512]{1,0:T(8,128)(2,1)S(1)}, bf16[64,512]{1,0:T(8,128)(2,1)S(1)}, u32[]{:S(2)}, u32[]{:S(2)}) collective-permute-start(bf16[64,512]{1,0:T(8,128)(2,1)S(1)} %get-tuple-element.121.refs_17_), channel_id=1, source_target_pairs={{0,24},{4,28},{8,16},{12,20},{16,8},{20,12},{24,0},{28,4},{1,25},{... | collective-permute-start | bytes 196616 | tf_op jit(solution)/shard_map/ppermute | solution.py:508
  43.1 1.0 %collective-permute-start.17 = (bf16[48,2048]{1,0:T(8,128)(2,1)S(1)}, bf16[48,2048]{1,0:T(8,128)(2,1)S(1)}, u32[]{:S(2)}, u32[]{:S(2)}) collective-permute-start(bf16[48,2048]{1,0:T(8,128)(2,1)S(1)} %get-tuple-element.111), channel_id=1, source_target_pairs={{0,8},{4,12},{8,0},{12,4},{16,24},{20,28},{24,16},{28,20},{1,9},{5... | collective-permute-start | bytes 589832 | tf_op jit(solution)/shard_map/ppermute | solution.py:508
  44.1 0.8 %tick3_b_late.1 = (bf16[32,2048]{1,0:T(8,128)(2,1)S(1)}, bf16[32,512]{1,0:T(8,128)(2,1)S(1)}) custom-call(bf16[32,2048]{1,0:T(8,128)(2,1)S(1)} %collective-permute-done.18.refs_0_, bf16[4,32,128]{2,1,0:T(8,128)(2,1)S(1)} %get-tuple-element.92.refs_1_, f32[64,128]{1,0:T(8,128)S(1)} %get-tuple-element.90.refs_2_.refs_3_, ...), custom_call_target="tpu_custom_call" | custom-call | flops 1150000000 | tf_op jit(solution)/shard_map/tick3_b_late/pallas_call | solution.py:319
  44.9 1.3 %collective-permute-done.23.refs_21_.refs_8_ = bf16[64,512]{1,0:T(8,128)(2,1)S(1)} collective-permute-done((bf16[64,512]{1,0:T(8,128)(2,1)S(1)}, bf16[64,512]{1,0:T(8,128)(2,1)S(1)}, u32[]{:S(2)}, u32[]{:S(2)}) %collective-permute-start.23) | collective-permute-done | bytes 65568 | tf_op jit(solution)/shard_map/ppermute | solution.py:508
  46.2 0.9 %tick3_b_early.1 = (bf16[128,512]{1,0:T(8,128)(2,1)S(1)}, bf16[64,512]{1,0:T(8,128)(2,1)S(1)}, bf16[32,2048]{1,0:T(8,128)(2,1)S(1)}, bf16[32,2048]{1,0:T(8,128)(...) custom-call(bf16[32,2048]{1,0:T(8,128)(2,1)S(1)} %collective-permute-done.18.refs_0_, ...), custom_call_target="tpu_custom_call" | custom-call | flops 1150000000 | tf_op jit(solution)/shard_map/tick3_b_early/pallas_call | solution.py:319
  47.1 2.8 %collective-permute-start.24 = (bf16[64,512]{1,0:T(8,128)(2,1)S(1)}, bf16[64,512]{1,0:T(8,128)(2,1)S(1)}, u32[]{:S(2)}, u32[]{:S(2)}) collective-permute-start(bf16[64,512]{1,0:T(8,128)(2,1)S(1)} %get-tuple-element.124), channel_id=1, source_target_pairs={{0,24},{4,28},{8,16},{12,20},{16,8},{20,12},{24,0},{28,4},{1,25},{... | collective-permute-start | bytes 196616 | tf_op jit(solution)/shard_map/ppermute | solution.py:508
  50.7 1.6 %collective-permute-start.26 = (bf16[32,2048]{1,0:T(8,128)(2,1)S(1)}, bf16[32,2048]{1,0:T(8,128)(2,1)S(1)}, u32[]{:S(2)}, u32[]{:S(2)}) collective-permute-start(bf16[32,2048]{1,0:T(8,128)(2,1)S(1)} %get-tuple-element.127), channel_id=1, source_target_pairs={{0,4},{4,0},{8,12},{12,8},{16,20},{20,16},{24,28},{28,24},{1,5},{5... | collective-permute-start | bytes 393224 | tf_op jit(solution)/shard_map/ppermute | solution.py:508
  53.0 2.6 %collective-permute-done.27.refs_2_.refs_6_ = bf16[32,2048]{1,0:T(8,128)(2,1)S(1)} collective-permute-done((bf16[32,2048]{1,0:T(8,128)(2,1)S(1)}, bf16[32,2048]{1,0:T(8,128)(2,1)S(1)}, u32[]{:S(2)}, u32[]{:S(2)}) %collective-permute-start.27) | collective-permute-done | bytes 131104 | tf_op jit(solution)/shard_map/ppermute | solution.py:508
  56.7 0.8 %rows.1 = (bf16[128,2048]{1,0:T(8,128)(2,1)}, f32[8,128]{1,0:T(8,128)S(1)}) custom-call(bf16[48,2048]{1,0:T(8,128)(2,1)S(1)} %collective-permute-done.17.refs_0_.first_rows_ref.refs_5_, bf16[16,2048]{1,0:T(8,128)(2,1)S(1)} %collective-permute-done.25.handed_ref, bf16[32,2048]{1,0:T(8,128)(2,1)S(1)} %get-tuple-element.126.refs_0_, ...), custom_call_target="tpu_custom_call" | custom-call | flops 920000000 | tf_op jit(solution)/shard_map/rows/pallas_call | solution.py:589
  57.7 1.0 %finish.1 = (f32[256,512]{1,0:T(8,128)}, f32[1,256]{1,0:T(1,128)}) custom-call(f32[256,512]{1,0:T(8,128)S(1)} %get-tuple-element.132.own_ref, bf16[128,512]{1,0:T(8,128)(2,1)S(1)} %collective-permute-done.30.first_ref, bf16[128,512]{1,0:T(8,128)(2,1)S(1)} %collective-permute-done.31.second_ref, f32[256,512]{1,0:T(8,128)S(1)} %get-tuple-element.135.weight_ref, ...), custom_call_target="tpu_custom_call" | custom-call | tf_op jit(solution)/shard_map/finish/pallas_call | solution.py:600
  (64 shorter events, 7.9 us)
Async XLA Ops:
  2.0 6.8 %collective-permute-start = (bf16[16,4608]{1,0:T(8,128)(2,1)S(1)}, bf16[16,4608]{1,0:T(8,128)(2,1)S(1)}, u32[]{:S(2)}, u32[]{:S(2)}) collective-permute-start(bf16[16,4608]{1,0:T(8,128)(2,1)S(1)} %get-tuple-element.73), channel_id=1, source_target_pairs={{0,4},{4,0},{8,12},{12,8},{16,20},{20,16},{24,28},{28,24},{1,5},{5... | collective-permute-start | bytes 442376 | tf_op jit(solution)/shard_map/ppermute | solution.py:508
  2.5 7.7 %collective-permute-start.1 = (bf16[16,4608]{1,0:T(8,128)(2,1)S(1)}, bf16[16,4608]{1,0:T(8,128)(2,1)S(1)}, u32[]{:S(2)}, u32[]{:S(2)}) collective-permute-start(bf16[16,4608]{1,0:T(8,128)(2,1)S(1)} %get-tuple-element.74), channel_id=1, source_target_pairs={{0,8},{4,12},{8,0},{12,4},{16,24},{20,28},{24,16},{28,20},{1,9},{5... | collective-permute-start | bytes 442376 | tf_op jit(solution)/shard_map/ppermute | solution.py:508
  5.1 7.3 %collective-permute-start.2 = (bf16[16,4608]{1,0:T(8,128)(2,1)S(1)}, bf16[16,4608]{1,0:T(8,128)(2,1)S(1)}, u32[]{:S(2)}, u32[]{:S(2)}) collective-permute-start(bf16[16,4608]{1,0:T(8,128)(2,1)S(1)} %get-tuple-element.75), channel_id=1, source_target_pairs={{0,12},{4,8},{8,4},{12,0},{16,28},{20,24},{24,20},{28,16},{1,13},{... | collective-permute-start | bytes 442376 | tf_op jit(solution)/shard_map/ppermute | solution.py:508
  6.9 11.9 %collective-permute-start.4 = (bf16[80,2048]{1,0:T(8,128)(2,1)S(1)}, bf16[80,2048]{1,0:T(8,128)(2,1)S(1)}, u32[]{:S(2)}, u32[]{:S(2)}) collective-permute-start(bf16[80,2048]{1,0:T(8,128)(2,1)S(1)} %get-tuple-element.82), channel_id=1, source_target_pairs={{0,16},{4,20},{8,24},{12,28},{16,0},{20,4},{24,8},{28,12},{1,17},{... | collective-permute-start | bytes 983048 | tf_op jit(solution)/shard_map/ppermute | solution.py:508
  8.7 4.8 %collective-permute-start.5 = (bf16[16,4608]{1,0:T(8,128)(2,1)S(1)}, bf16[16,4608]{1,0:T(8,128)(2,1)S(1)}, u32[]{:S(2)}, u32[]{:S(2)}) collective-permute-start(bf16[16,4608]{1,0:T(8,128)(2,1)S(1)} %get-tuple-element.84), channel_id=1, source_target_pairs={{0,4},{4,0},{8,12},{12,8},{16,20},{20,16},{24,28},{28,24},{1,5},{5... | collective-permute-start | bytes 442376 | tf_op jit(solution)/shard_map/ppermute | solution.py:508
  8.8 7.3 %collective-permute-start.6 = (bf16[16,4608]{1,0:T(8,128)(2,1)S(1)}, bf16[16,4608]{1,0:T(8,128)(2,1)S(1)}, u32[]{:S(2)}, u32[]{:S(2)}) collective-permute-start(bf16[16,4608]{1,0:T(8,128)(2,1)S(1)} %get-tuple-element.85), channel_id=1, source_target_pairs={{0,8},{4,12},{8,0},{12,4},{16,24},{20,28},{24,16},{28,20},{1,9},{5... | collective-permute-start | bytes 442376 | tf_op jit(solution)/shard_map/ppermute | solution.py:508
  10.3 8.5 %collective-permute-start.7 = (bf16[16,4608]{1,0:T(8,128)(2,1)S(1)}, bf16[16,4608]{1,0:T(8,128)(2,1)S(1)}, u32[]{:S(2)}, u32[]{:S(2)}) collective-permute-start(bf16[16,4608]{1,0:T(8,128)(2,1)S(1)} %get-tuple-element.86), channel_id=1, source_target_pairs={{0,12},{4,8},{8,4},{12,0},{16,28},{20,24},{24,20},{28,16},{1,13},{... | collective-permute-start | bytes 442376 | tf_op jit(solution)/shard_map/ppermute | solution.py:508
  12.8 7.7 %collective-permute-start.3 = (bf16[32,2048]{1,0:T(8,128)(2,1)S(1)}, bf16[32,2048]{1,0:T(8,128)(2,1)S(1)}, u32[]{:S(2)}, u32[]{:S(2)}) collective-permute-start(bf16[32,2048]{1,0:T(8,128)(2,1)S(1)} %get-tuple-element.81.refs_7_.refs_6_), channel_id=1, source_target_pairs={{3,2},{7,6},{11,10},{15,14},{19,18},{23,22},{27,26},{31,30}} | collective-permute-start | bytes 393224 | tf_op jit(solution)/shard_map/ppermute | solution.py:537
  13.5 7.7 %collective-permute-start.11 = (bf16[32,2048]{1,0:T(8,128)(2,1)S(1)}, bf16[32,2048]{1,0:T(8,128)(2,1)S(1)}, u32[]{:S(2)}, u32[]{:S(2)}) collective-permute-start(bf16[32,2048]{1,0:T(8,128)(2,1)S(1)} %get-tuple-element.88.refs_5_.refs_7_), channel_id=1, source_target_pairs={{3,2},{7,6},{11,10},{15,14},{19,18},{23,22},{27,26},{31,30}} | collective-permute-start | bytes 393224 | tf_op jit(solution)/shard_map/ppermute | solution.py:537
  19.1 2.8 %collective-permute-start.9 = (bf16[32,2048]{1,0:T(8,128)(2,1)S(1)}, bf16[32,2048]{1,0:T(8,128)(2,1)S(1)}, u32[]{:S(2)}, u32[]{:S(2)}) collective-permute-start(bf16[32,2048]{1,0:T(8,128)(2,1)S(1)} %get-tuple-element.93.refs_7_.refs_6_), channel_id=1, source_target_pairs={{3,2},{7,6},{11,10},{15,14},{19,18},{23,22},{27,26},{31,30}} | collective-permute-start | bytes 393224 | tf_op jit(solution)/shard_map/ppermute | solution.py:537
  19.8 2.8 %collective-permute-start.10 = (bf16[32,2048]{1,0:T(8,128)(2,1)S(1)}, bf16[32,2048]{1,0:T(8,128)(2,1)S(1)}, u32[]{:S(2)}, u32[]{:S(2)}) collective-permute-start(bf16[32,2048]{1,0:T(8,128)(2,1)S(1)} %get-tuple-element.94.refs_6_.refs_7_), channel_id=1, source_target_pairs={{3,2},{7,6},{11,10},{15,14},{19,18},{23,22},{27,26},{31,30}} | collective-permute-start | bytes 393224 | tf_op jit(solution)/shard_map/ppermute | solution.py:537
  20.5 5.6 %collective-permute-start.8 = (bf16[32,2048]{1,0:T(8,128)(2,1)S(1)}, bf16[32,2048]{1,0:T(8,128)(2,1)S(1)}, u32[]{:S(2)}, u32[]{:S(2)}) collective-permute-start(bf16[32,2048]{1,0:T(8,128)(2,1)S(1)} %get-tuple-element.95.refs_7_.refs_8_), channel_id=1, source_target_pairs={{2,1},{6,5},{10,9},{14,13},{18,17},{22,21},{26,25},{30,29}} | collective-permute-start | bytes 393224 | tf_op jit(solution)/shard_map/ppermute | solution.py:537
  21.2 6.2 %collective-permute-start.13 = (bf16[32,2048]{1,0:T(8,128)(2,1)S(1)}, bf16[32,2048]{1,0:T(8,128)(2,1)S(1)}, u32[]{:S(2)}, u32[]{:S(2)}) collective-permute-start(bf16[32,2048]{1,0:T(8,128)(2,1)S(1)} %get-tuple-element.96.refs_6_.refs_9_), channel_id=1, source_target_pairs={{2,1},{6,5},{10,9},{14,13},{18,17},{22,21},{26,25},{30,29}} | collective-permute-start | bytes 393224 | tf_op jit(solution)/shard_map/ppermute | solution.py:537
  21.9 6.8 %collective-permute-start.15 = (bf16[32,2048]{1,0:T(8,128)(2,1)S(1)}, bf16[32,2048]{1,0:T(8,128)(2,1)S(1)}, u32[]{:S(2)}, u32[]{:S(2)}) collective-permute-start(bf16[32,2048]{1,0:T(8,128)(2,1)S(1)} %get-tuple-element.97.refs_7_.refs_8_), channel_id=1, source_target_pairs={{2,1},{6,5},{10,9},{14,13},{18,17},{22,21},{26,25},{30,29}} | collective-permute-start | bytes 393224 | tf_op jit(solution)/shard_map/ppermute | solution.py:537
  22.7 7.4 %collective-permute-start.16 = (bf16[32,2048]{1,0:T(8,128)(2,1)S(1)}, bf16[32,2048]{1,0:T(8,128)(2,1)S(1)}, u32[]{:S(2)}, u32[]{:S(2)}) collective-permute-start(bf16[32,2048]{1,0:T(8,128)(2,1)S(1)} %get-tuple-element.98.refs_6_.after_ref.refs_0_.refs_9_), channel_id=1, source_target_pairs={{2,1},{6,5},{10,9},{14,13},{18,17},{22,21},{26,25},{30,29}} | collective-permute-start | bytes 393224 | tf_op jit(solution)/shard_map/ppermute | solution.py:537
  23.5 7.9 %collective-permute-start.20 = (bf16[128,512]{1,0:T(8,128)(2,1)S(1)}, bf16[128,512]{1,0:T(8,128)(2,1)S(1)}, u32[]{:S(2)}, u32[]{:S(2)}) collective-permute-start(bf16[128,512]{1,0:T(8,128)(2,1)S(1)} %columns6.1), channel_id=1, source_target_pairs={{0,24},{4,28},{8,16},{12,20},{16,8},{20,12},{24,0},{28,4},{1,25},{... | collective-permute-start | bytes 393224 | tf_op jit(solution)/shard_map/ppermute | solution.py:508
  26.1 10.9 %collective-permute-start.12 = (bf16[32,2048]{1,0:T(8,128)(2,1)S(1)}, bf16[32,2048]{1,0:T(8,128)(2,1)S(1)}, u32[]{:S(2)}, u32[]{:S(2)}) collective-permute-start(bf16[32,2048]{1,0:T(8,128)(2,1)S(1)} %get-tuple-element.99.refs_7_.refs_10_), channel_id=1, source_target_pairs={{1,0},{5,4},{9,8},{13,12},{17,16},{21,20},{25,24},{29,28}} | collective-permute-start | bytes 393224 | tf_op jit(solution)/shard_map/ppermute | solution.py:537
  27.4 12.4 %collective-permute-start.14 = (bf16[32,2048]{1,0:T(8,128)(2,1)S(1)}, bf16[32,2048]{1,0:T(8,128)(2,1)S(1)}, u32[]{:S(2)}, u32[]{:S(2)}) collective-permute-start(bf16[32,2048]{1,0:T(8,128)(2,1)S(1)} %get-tuple-element.100.refs_6_.refs_11_), channel_id=1, source_target_pairs={{1,0},{5,4},{9,8},{13,12},{17,16},{21,20},{25,24},{29,28}} | collective-permute-start | bytes 393224 | tf_op jit(solution)/shard_map/ppermute | solution.py:537
  28.8 14.4 %collective-permute-start.18 = (bf16[32,2048]{1,0:T(8,128)(2,1)S(1)}, bf16[32,2048]{1,0:T(8,128)(2,1)S(1)}, u32[]{:S(2)}, u32[]{:S(2)}) collective-permute-start(bf16[32,2048]{1,0:T(8,128)(2,1)S(1)} %get-tuple-element.107.refs_7_.refs_10_), channel_id=1, source_target_pairs={{1,0},{5,4},{9,8},{13,12},{17,16},{21,20},{25,24},{29,28}} | collective-permute-start | bytes 393224 | tf_op jit(solution)/shard_map/ppermute | solution.py:537
  30.1 16.1 %collective-permute-start.19 = (bf16[32,2048]{1,0:T(8,128)(2,1)S(1)}, bf16[32,2048]{1,0:T(8,128)(2,1)S(1)}, u32[]{:S(2)}, u32[]{:S(2)}) collective-permute-start(bf16[32,2048]{1,0:T(8,128)(2,1)S(1)} %get-tuple-element.108.refs_12_.refs_0_.refs_11_), channel_id=1, source_target_pairs={{1,0},{5,4},{9,8},{13,12},{17,16},{21,20},{25,24},{29,28}} | collective-permute-start | bytes 393224 | tf_op jit(solution)/shard_map/ppermute | solution.py:537
  31.5 14.8 %collective-permute-start.21 = (bf16[128,512]{1,0:T(8,128)(2,1)S(1)}, bf16[128,512]{1,0:T(8,128)(2,1)S(1)}, u32[]{:S(2)}, u32[]{:S(2)}) collective-permute-start(bf16[128,512]{1,0:T(8,128)(2,1)S(1)} %columns2.1), channel_id=1, source_target_pairs={{0,8},{4,12},{8,0},{12,4},{16,24},{20,28},{24,16},{28,20},{1,9},{5... | collective-permute-start | bytes 393224 | tf_op jit(solution)/shard_map/ppermute | solution.py:508
  37.0 9.2 %collective-permute-start.22 = (bf16[128,512]{1,0:T(8,128)(2,1)S(1)}, bf16[128,512]{1,0:T(8,128)(2,1)S(1)}, u32[]{:S(2)}, u32[]{:S(2)}) collective-permute-start(bf16[128,512]{1,0:T(8,128)(2,1)S(1)} %columns4.1), channel_id=1, source_target_pairs={{0,16},{4,20},{8,24},{12,28},{16,0},{20,4},{24,8},{28,12},{1,17},{... | collective-permute-start | bytes 393224 | tf_op jit(solution)/shard_map/ppermute | solution.py:508
  40.6 5.6 %collective-permute-start.23 = (bf16[64,512]{1,0:T(8,128)(2,1)S(1)}, bf16[64,512]{1,0:T(8,128)(2,1)S(1)}, u32[]{:S(2)}, u32[]{:S(2)}) collective-permute-start(bf16[64,512]{1,0:T(8,128)(2,1)S(1)} %get-tuple-element.121.refs_17_), channel_id=1, source_target_pairs={{0,24},{4,28},{8,16},{12,20},{16,8},{20,12},{24,0},{28,4},{1,25},{... | collective-permute-start | bytes 196616 | tf_op jit(solution)/shard_map/ppermute | solution.py:508
  43.1 7.5 %collective-permute-start.17 = (bf16[48,2048]{1,0:T(8,128)(2,1)S(1)}, bf16[48,2048]{1,0:T(8,128)(2,1)S(1)}, u32[]{:S(2)}, u32[]{:S(2)}) collective-permute-start(bf16[48,2048]{1,0:T(8,128)(2,1)S(1)} %get-tuple-element.111), channel_id=1, source_target_pairs={{0,8},{4,12},{8,0},{12,4},{16,24},{20,28},{24,16},{28,20},{1,9},{5... | collective-permute-start | bytes 589832 | tf_op jit(solution)/shard_map/ppermute | solution.py:508
  47.1 5.8 %collective-permute-start.24 = (bf16[64,512]{1,0:T(8,128)(2,1)S(1)}, bf16[64,512]{1,0:T(8,128)(2,1)S(1)}, u32[]{:S(2)}, u32[]{:S(2)}) collective-permute-start(bf16[64,512]{1,0:T(8,128)(2,1)S(1)} %get-tuple-element.124), channel_id=1, source_target_pairs={{0,24},{4,28},{8,16},{12,20},{16,8},{20,12},{24,0},{28,4},{1,25},{... | collective-permute-start | bytes 196616 | tf_op jit(solution)/shard_map/ppermute | solution.py:508
  49.9 5.7 %collective-permute-start.27 = (bf16[32,2048]{1,0:T(8,128)(2,1)S(1)}, bf16[32,2048]{1,0:T(8,128)(2,1)S(1)}, u32[]{:S(2)}, u32[]{:S(2)}) collective-permute-start(bf16[32,2048]{1,0:T(8,128)(2,1)S(1)} %get-tuple-element.128), channel_id=1, source_target_pairs={{0,8},{4,12},{8,0},{12,4},{16,24},{20,28},{24,16},{28,20},{1,9},{5... | collective-permute-start | bytes 393224 | tf_op jit(solution)/shard_map/ppermute | solution.py:508
  50.4 5.2 %collective-permute-start.29 = (bf16[128,512]{1,0:T(8,128)(2,1)S(1)}, bf16[128,512]{1,0:T(8,128)(2,1)S(1)}, u32[]{:S(2)}, u32[]{:S(2)}) collective-permute-start(bf16[128,512]{1,0:T(8,128)(2,1)S(1)} %get-tuple-element.123.refs_1_.refs_4_), channel_id=1, source_target_pairs={{0,16},{4,20},{8,24},{12,28},{16,0},{20,4},{24,8},{28,12},{1,17},{... | collective-permute-start | bytes 393224 | tf_op jit(solution)/shard_map/ppermute | solution.py:508
  50.7 6.0 %collective-permute-start.28 = (bf16[16,2048]{1,0:T(8,128)(2,1)S(1)}, bf16[16,2048]{1,0:T(8,128)(2,1)S(1)}, u32[]{:S(2)}, u32[]{:S(2)}) collective-permute-start(bf16[16,2048]{1,0:T(8,128)(2,1)S(1)} %get-tuple-element.129), channel_id=1, source_target_pairs={{0,12},{4,8},{8,4},{12,0},{16,28},{20,24},{24,20},{28,16},{1,13},{... | collective-permute-start | bytes 196616 | tf_op jit(solution)/shard_map/ppermute | solution.py:508
  50.7 6.0 %collective-permute-start.26 = (bf16[32,2048]{1,0:T(8,128)(2,1)S(1)}, bf16[32,2048]{1,0:T(8,128)(2,1)S(1)}, u32[]{:S(2)}, u32[]{:S(2)}) collective-permute-start(bf16[32,2048]{1,0:T(8,128)(2,1)S(1)} %get-tuple-element.127), channel_id=1, source_target_pairs={{0,4},{4,0},{8,12},{12,8},{16,20},{20,16},{24,28},{28,24},{1,5},{5... | collective-permute-start | bytes 393224 | tf_op jit(solution)/shard_map/ppermute | solution.py:508
  53.0 3.7 %collective-permute-start.25 = (bf16[16,2048]{1,0:T(8,128)(2,1)S(1)}, bf16[16,2048]{1,0:T(8,128)(2,1)S(1)}, u32[]{:S(2)}, u32[]{:S(2)}) collective-permute-start(bf16[16,2048]{1,0:T(8,128)(2,1)S(1)} %get-tuple-element.125), channel_id=1, source_target_pairs={{0,4},{4,0},{8,12},{12,8},{16,20},{20,16},{24,28},{28,24},{1,5},{5... | collective-permute-start | bytes 196616 | tf_op jit(solution)/shard_map/ppermute | solution.py:508
  56.1 1.4 %collective-permute-start.30 = (bf16[128,512]{1,0:T(8,128)(2,1)S(1)}, bf16[128,512]{1,0:T(8,128)(2,1)S(1)}, u32[]{:S(2)}, u32[]{:S(2)}) collective-permute-start(bf16[128,512]{1,0:T(8,128)(2,1)S(1)} %get-tuple-element.133), channel_id=1, source_target_pairs={{0,4},{4,0},{8,12},{12,8},{16,20},{20,16},{24,28},{28,24},{1,5},{5... | collective-permute-start | bytes 393224 | tf_op jit(solution)/shard_map/ppermute | solution.py:508
  56.2 1.5 %collective-permute-start.31 = (bf16[128,512]{1,0:T(8,128)(2,1)S(1)}, bf16[128,512]{1,0:T(8,128)(2,1)S(1)}, u32[]{:S(2)}, u32[]{:S(2)}) collective-permute-start(bf16[128,512]{1,0:T(8,128)(2,1)S(1)} %get-tuple-element.134), channel_id=1, source_target_pairs={{0,4},{4,0},{8,12},{12,8},{16,20},{20,16},{24,28},{28,24},{1,5},{5... | collective-permute-start | bytes 393224 | tf_op jit(solution)/shard_map/ppermute | solution.py:508
  (2 other events, 9.1 us)

commit v13 on v12

--- a/solution.py
+++ b/solution.py
@@ -12,7 +12,7 @@
 UNIT = 32
 EPSILON = 1e-06
 MASKED = -1e30
-OUTS = {2: 3, 5: 6}
+OUTS = {2: 3, 4: 5}
 UNITS = ("a_late", "a_early", "b_late", "b_early")
 VMEM = pl.BlockSpec(memory_space=pltpu.VMEM)
 SMEM = pl.BlockSpec(memory_space=pltpu.SMEM)
@@ -262,15 +262,13 @@
         return
     values = jnp.concatenate([value_ref[...], late_refs[0][...]], axis=0)
     blocks_ref[first_row + UNIT : first_row + BLOCK, :] = late_refs[1][...]
-    outs[1][...] = values
+    outs[1 if late == 2 else 0][...] = values
     if late > 2:
-        late_a_ref, early_a_ref, value_a_ref = late_refs[2:]
+        late_a_ref, early_a_ref = late_refs[2:]
         blocks_ref[EARLY, :] = early_a_ref[...]
         blocks_ref[LATE, :] = late_a_ref[...]
-        outs[0][:BLOCK, :] = value_a_ref[...]
-        outs[0][BLOCK:, :] = values
     at = place()[1]
-    pieces = {2: outs[2]} if late == 2 else dict(enumerate(outs[2:]))
+    pieces = {2: outs[2]} if late == 2 else dict(enumerate(outs[1:]))
     piece = BLOCK * kv_width // model_width
 
     def rows_for(k, block):
@@ -313,7 +311,7 @@
         piece = BLOCK // half
         shapes = [rows, (BLOCK, kv_width), (3 * piece, model_width)]
     if len(late) > 2:
-        shapes = [(2 * BLOCK, kv_width), (BLOCK, kv_width)]
+        shapes = [(BLOCK, kv_width)]
         shapes += [(2 * piece, model_width)] * 3 + [(piece, model_width)]
     parts = [part for _, part in grads]
     return pl.pallas_call(
@@ -400,15 +398,21 @@
     if distance == 0:
         came_ref, out_ref, handed_ref = refs[0], refs[-2], refs[-1]
         handed_ref[...] = came_ref[came_ref.shape[0] - handed_ref.shape[0] :, :]
+    if distance == 4:
+        out_ref[2 * BLOCK :, :] = refs[0][...]
     there = lax.div(lax.bitwise_xor(place()[2], distance), 2)
     out_ref[:BLOCK, :] = first_ref[:, columns_of(there, width)]
-    out_ref[BLOCK:, :] = second_ref[:, columns_of(there, width)]
+    out_ref[BLOCK : 2 * BLOCK, :] = second_ref[:, columns_of(there, width)]
 
 
 def columns_for(distance, blocks, after, came=()):
     model_width = blocks[0][3].shape[1]
     width = 2 * model_width // lax.axis_size("dp")
-    shapes = [(2 * BLOCK, width)] + [(array.shape[0] // 3, model_width) for array in came]
+    shapes = [(2 * BLOCK, width)]
+    if distance == 0:
+        shapes.append((came[0].shape[0] // 3, model_width))
+    if distance == 4:
+        shapes = [(3 * BLOCK, width)]
     outs = [jax.ShapeDtypeStruct(shape, jnp.bfloat16) for shape in shapes]
     results = pl.pallas_call(
         functools.partial(columns_kernel, width, distance),
@@ -418,7 +422,7 @@
         name=f"columns{distance}",
         **params(0.0 if distance else 1.0),
     )(blocks[0][3], blocks[1][3], *came, *after)
-    return results if came else results[0]
+    return results if distance == 0 else results[0]
 
 
 def own_kernel(scale, weight_ref, gain_ref, after_ref, weight_out_ref, gain_out_ref):
@@ -435,20 +439,20 @@
 
 
 def partial_kernel(shares, first, *refs):
-    columns, refs = refs[:4], refs[4:]
-    own_out_ref, *other_refs = refs[6:]
+    columns, values, (own_out_ref, *other_refs) = refs[:4], refs[4:-3], refs[-3:]
     kv_width = own_out_ref.shape[1]
     parts = []
-    for ref in refs[:6]:
+    for ref in values:
         beside = ref.shape[1] > kv_width
         rows = slice(first, 2 * first) if beside else slice(0, ref.shape[0])
         parts += [ref[rows, at : at + kv_width] for at in range(0, ref.shape[1], kv_width)]
+    parts.insert(len(parts) - 3, columns[2][2 * BLOCK :, :])
     value = jnp.concatenate(parts, axis=0)
     mine = lax.rem(place()[2], 2)
 
     def share(core):
         at = pl.ds(pl.multiple_of(core * shares, shares), shares)
-        rows = jnp.concatenate([ref[:, at] for ref in columns], axis=0)
+        rows = jnp.concatenate([ref[: 2 * BLOCK, at] for ref in columns], axis=0)
         return lax.dot_general(
             rows, value, (((0,), (0,)), ((), ())), preferred_element_type=jnp.float32
         )
@@ -551,17 +555,17 @@
             )(near(weight), near(gain), *after)
             columns = {6: swap(columns_for(6, blocks, after + [own_gain]), 6)}
         if last:
-            waits = after + [columns[6]]
-            columns.update({k: swap(columns_for(k, blocks, waits), k) for k in (2, 4)})
+            columns[2] = swap(columns_for(2, blocks, after + [columns[6]]), 2)
         for u in range(4):
             needs = grads[u - 1 : u + 1] if u % 2 else grads[u : u + 1]
             late = []
             if last and u == 1:
                 late = [done[0][1], done[0][0]]
             if last and u == 3:
-                late = [done[2][1], done[2][0], done[0][0], done[1][0], done[1][1]]
+                late = [done[2][1], done[2][0], done[0][0], done[1][0]]
                 first_value, first_rows = swap(done[1][1], 6), swap(done[1][2], 2)
-                after = after + [columns[2], columns[4], first_value]
+                columns[4] = swap(columns_for(4, blocks, [], [done[1][1]]), 4)
+                after = after + [columns[2], first_value]
             done.append(
                 tick_step(
                     tick, needs, blocks[u // 2], turned, gain, kept[u] if last else (), late,
@@ -570,17 +574,18 @@
             )
             after = [done[u][0]]
             kept[u].append(done[u])
-    values, last_value, *rows = done[3]
+    own_value, *rows = done[3]
+    own_first = done[1][1]
     rows = [rows[0]] + [swap(rows[k], k) for k in range(1, half)]
-    last_value = swap(last_value, 6)
-    columns[0], handed = columns_for(0, blocks, [values, last_value], [first_rows])
+    last_value = swap(own_value, 6)
+    columns[0], handed = columns_for(0, blocks, [own_value, columns[4]], [first_rows])
     handed = swap(handed, 1)
-    values = [values, first_rows, rows[2], swap(values, 4), first_value, last_value]
+    values = [own_first, own_value, first_rows, rows[2], swap(own_value, 4), first_value, last_value]
     own, *other = pl.pallas_call(
         functools.partial(partial_kernel, shares, piece),
         out_shape=(jax.ShapeDtypeStruct((shares, kv_width), jnp.float32),)
         + (jax.ShapeDtypeStruct((shares // 2, kv_width), bf16),) * 2,
-        in_specs=[VMEM] * 10,
+        in_specs=[VMEM] * 11,
         out_specs=(VMEM,) * 3,
         name="weight_partial",
         **params(0.0),

time: 59.1 us -> 59.8 us (1.012)
  waiting for transfers between devices: 16.6 us -> 18.9 us
  starting transfers between devices: 31.3 us -> 29.9 us
    ppermute x12, waiting for transfers between devices: 5.44 us -> 6.97 us  [direct(): lax.ppermute(unit[-1][0], 'section', hop)]
    ppermute x20, starting transfers between devices: 20.8 us -> 19.4 us  [swap(): return lax.ppermute(array, 'dp', [(i, i ^ k) for i in range(replicas)])]
    ppermute x20, waiting for transfers between devices: 11.2 us -> 11.9 us  [swap(): return lax.ppermute(array, 'dp', [(i, i ^ k) for i in range(replicas)])]
  transfers between devices with their start and end apart: 32 -> 32, of which waited for: 9 -> 10; matrix products, arithmetic and copies ran while one was open for 0% -> 0% of each run, Pallas kernels for 13% -> 12%
where the time goes in v13:
time: 59.8 us; the launch traced here: 59.5 us
  starting transfers between devices  29.9 us (50%)
  waiting for transfers between devices  18.9 us (32%)
  Pallas kernels  9.69 us (16%)
  between operations  1.03 us (2%)
    ppermute x20, starting transfers between devices, swap(): return lax.ppermute(array, 'dp', [(i, i ^ k) for i in range(replicas)])  19.4 us
    ppermute x20, waiting for transfers between devices, swap(): return lax.ppermute(array, 'dp', [(i, i ^ k) for i in range(replicas)])  11.9 us
    ppermute x12, starting transfers between devices, direct(): lax.ppermute(unit[-1][0], 'section', hop)  10.5 us
    ppermute x12, waiting for transfers between devices, direct(): lax.ppermute(unit[-1][0], 'section', hop)  6.97 us
    pallas_call x16, Pallas kernels, tick_step(): pl.pallas_call(functools.partial(tick_kernel, tick, EARLY if low else LAT...  3.42 us
    pallas_call x2, Pallas kernels, pack(): pl.pallas_call(functools.partial(pack_kernel, block, half, piece), out_sh...  3.06 us
  transfers between devices with their start and end apart: 32, of which 10 were waited for; matrix products, arithmetic and copies ran while one was open for 0% of the time, Pallas kernels for 12%

profile of v13, /device:TPU:0, one launch (start us, length us, event | category | flops | bytes accessed | tf_op | source)
XLA Modules:
  0.0 59.5 jit_solution(3965342067523983113)
XLA Ops:
  0.7 1.4 %pack.2 = (bf16[16,4608]{1,0:T(8,128)(2,1)S(1)}, bf16[16,4608]{1,0:T(8,128)(2,1)S(1)}, bf16[16,4608]{1,0:T(8,128)(2,1)S(1)}, bf16[16,4608]{1,0:T(8,128)(2,1)S(1)}, bf16[80,2048]{1,0:T(8,128)(2,1)S(1)}) custom-call(bf16[128,2048]{1,0:T(8,128)(2,1)} %bitcast.8, bf16[128,512]{1,0:T(8,128)(2,1)} %bitcast.13, bf16[128,2048]{1,0:T(8,128)(2,1)} %bitcast.10, ...), custom_call_target="tpu_custom_call" | custom-call | flops 1380000000 | tf_op jit(solution)/shard_map/pack/pallas_call | solution.py:381
  2.5 2.6 %collective-permute-start.1 = (bf16[16,4608]{1,0:T(8,128)(2,1)S(1)}, bf16[16,4608]{1,0:T(8,128)(2,1)S(1)}, u32[]{:S(2)}, u32[]{:S(2)}) collective-permute-start(bf16[16,4608]{1,0:T(8,128)(2,1)S(1)} %get-tuple-element.73), channel_id=1, source_target_pairs={{0,8},{4,12},{8,0},{12,4},{16,24},{20,28},{24,16},{28,20},{1,9},{5... | collective-permute-start | bytes 442376 | tf_op jit(solution)/shard_map/ppermute | solution.py:512
  5.2 1.7 %pack.3 = (f32[1,2048]{1,0:T(1,128)S(1)}, bf16[512,2048]{1,0:T(8,128)(2,1)S(1)}, bf16[16,4608]{1,0:T(8,128)(2,1)S(1)}, bf16[16,4608]{1,0:T(8,128)(2,1)S(1)}, bf1...) custom-call(bf16[128,2048]{1,0:T(8,128)(2,1)} %bitcast.9, ...), custom_call_target="tpu_custom_call" | custom-call | flops 1380000000 | tf_op jit(solution)/shard_map/pack/pallas_call | solution.py:381
  6.9 1.8 %collective-permute-start.4 = (bf16[80,2048]{1,0:T(8,128)(2,1)S(1)}, bf16[80,2048]{1,0:T(8,128)(2,1)S(1)}, u32[]{:S(2)}, u32[]{:S(2)}) collective-permute-start(bf16[80,2048]{1,0:T(8,128)(2,1)S(1)} %get-tuple-element.81), channel_id=1, source_target_pairs={{0,16},{4,20},{8,24},{12,28},{16,0},{20,4},{24,8},{28,12},{1,17},{... | collective-permute-start | bytes 983048 | tf_op jit(solution)/shard_map/ppermute | solution.py:512
  8.8 1.5 %collective-permute-start.6 = (bf16[16,4608]{1,0:T(8,128)(2,1)S(1)}, bf16[16,4608]{1,0:T(8,128)(2,1)S(1)}, u32[]{:S(2)}, u32[]{:S(2)}) collective-permute-start(bf16[16,4608]{1,0:T(8,128)(2,1)S(1)} %get-tuple-element.84), channel_id=1, source_target_pairs={{0,8},{4,12},{8,0},{12,4},{16,24},{20,28},{24,16},{28,20},{1,9},{5... | collective-permute-start | bytes 442376 | tf_op jit(solution)/shard_map/ppermute | solution.py:512
  10.6 1.9 %collective-permute-done.2.refs_3_ = bf16[16,4608]{1,0:T(8,128)(2,1)S(1)} collective-permute-done((bf16[16,4608]{1,0:T(8,128)(2,1)S(1)}, bf16[16,4608]{1,0:T(8,128)(2,1)S(1)}, u32[]{:S(2)}, u32[]{:S(2)}) %collective-permute-start.2) | collective-permute-done | bytes 147488 | tf_op jit(solution)/shard_map/ppermute | solution.py:512
  12.8 0.7 %collective-permute-start.3 = (bf16[32,2048]{1,0:T(8,128)(2,1)S(1)}, bf16[32,2048]{1,0:T(8,128)(2,1)S(1)}, u32[]{:S(2)}, u32[]{:S(2)}) collective-permute-start(bf16[32,2048]{1,0:T(8,128)(2,1)S(1)} %get-tuple-element.80.refs_7_.refs_6_), channel_id=1, source_target_pairs={{3,2},{7,6},{11,10},{15,14},{19,18},{23,22},{27,26},{31,30}} | collective-permute-start | bytes 393224 | tf_op jit(solution)/shard_map/ppermute | solution.py:541
  13.5 0.7 %collective-permute-start.11 = (bf16[32,2048]{1,0:T(8,128)(2,1)S(1)}, bf16[32,2048]{1,0:T(8,128)(2,1)S(1)}, u32[]{:S(2)}, u32[]{:S(2)}) collective-permute-start(bf16[32,2048]{1,0:T(8,128)(2,1)S(1)} %get-tuple-element.87.refs_5_.refs_7_), channel_id=1, source_target_pairs={{3,2},{7,6},{11,10},{15,14},{19,18},{23,22},{27,26},{31,30}} | collective-permute-start | bytes 393224 | tf_op jit(solution)/shard_map/ppermute | solution.py:541
  14.2 1.9 %collective-permute-done.6.refs_2_ = bf16[16,4608]{1,0:T(8,128)(2,1)S(1)} collective-permute-done((bf16[16,4608]{1,0:T(8,128)(2,1)S(1)}, bf16[16,4608]{1,0:T(8,128)(2,1)S(1)}, u32[]{:S(2)}, u32[]{:S(2)}) %collective-permute-start.6) | collective-permute-done | bytes 147488 | tf_op jit(solution)/shard_map/ppermute | solution.py:512
  16.1 2.6 %collective-permute-done.7.refs_3_ = bf16[16,4608]{1,0:T(8,128)(2,1)S(1)} collective-permute-done((bf16[16,4608]{1,0:T(8,128)(2,1)S(1)}, bf16[16,4608]{1,0:T(8,128)(2,1)S(1)}, u32[]{:S(2)}, u32[]{:S(2)}) %collective-permute-start.7) | collective-permute-done | bytes 147488 | tf_op jit(solution)/shard_map/ppermute | solution.py:512
  19.8 0.7 %collective-permute-start.10 = (bf16[32,2048]{1,0:T(8,128)(2,1)S(1)}, bf16[32,2048]{1,0:T(8,128)(2,1)S(1)}, u32[]{:S(2)}, u32[]{:S(2)}) collective-permute-start(bf16[32,2048]{1,0:T(8,128)(2,1)S(1)} %get-tuple-element.93.refs_6_.refs_7_), channel_id=1, source_target_pairs={{3,2},{7,6},{11,10},{15,14},{19,18},{23,22},{27,26},{31,30}} | collective-permute-start | bytes 393224 | tf_op jit(solution)/shard_map/ppermute | solution.py:541
  21.9 0.7 %collective-permute-start.15 = (bf16[32,2048]{1,0:T(8,128)(2,1)S(1)}, bf16[32,2048]{1,0:T(8,128)(2,1)S(1)}, u32[]{:S(2)}, u32[]{:S(2)}) collective-permute-start(bf16[32,2048]{1,0:T(8,128)(2,1)S(1)} %get-tuple-element.96.refs_7_.refs_8_), channel_id=1, source_target_pairs={{2,1},{6,5},{10,9},{14,13},{18,17},{22,21},{26,25},{30,29}} | collective-permute-start | bytes 393224 | tf_op jit(solution)/shard_map/ppermute | solution.py:541
  23.5 2.6 %collective-permute-start.20 = (bf16[128,512]{1,0:T(8,128)(2,1)S(1)}, bf16[128,512]{1,0:T(8,128)(2,1)S(1)}, u32[]{:S(2)}, u32[]{:S(2)}) collective-permute-start(bf16[128,512]{1,0:T(8,128)(2,1)S(1)} %columns6.1), channel_id=1, source_target_pairs={{0,24},{4,28},{8,16},{12,20},{16,8},{20,12},{24,0},{28,4},{1,25},{... | collective-permute-start | bytes 393224 | tf_op jit(solution)/shard_map/ppermute | solution.py:512
  26.1 1.3 %collective-permute-start.12 = (bf16[32,2048]{1,0:T(8,128)(2,1)S(1)}, bf16[32,2048]{1,0:T(8,128)(2,1)S(1)}, u32[]{:S(2)}, u32[]{:S(2)}) collective-permute-start(bf16[32,2048]{1,0:T(8,128)(2,1)S(1)} %get-tuple-element.98.refs_7_.refs_10_), channel_id=1, source_target_pairs={{1,0},{5,4},{9,8},{13,12},{17,16},{21,20},{25,24},{29,28}} | collective-permute-start | bytes 393224 | tf_op jit(solution)/shard_map/ppermute | solution.py:541
  27.4 1.3 %collective-permute-start.14 = (bf16[32,2048]{1,0:T(8,128)(2,1)S(1)}, bf16[32,2048]{1,0:T(8,128)(2,1)S(1)}, u32[]{:S(2)}, u32[]{:S(2)}) collective-permute-start(bf16[32,2048]{1,0:T(8,128)(2,1)S(1)} %get-tuple-element.99.refs_6_.refs_11_), channel_id=1, source_target_pairs={{1,0},{5,4},{9,8},{13,12},{17,16},{21,20},{25,24},{29,28}} | collective-permute-start | bytes 393224 | tf_op jit(solution)/shard_map/ppermute | solution.py:541
  28.8 1.3 %collective-permute-start.18 = (bf16[32,2048]{1,0:T(8,128)(2,1)S(1)}, bf16[32,2048]{1,0:T(8,128)(2,1)S(1)}, u32[]{:S(2)}, u32[]{:S(2)}) collective-permute-start(bf16[32,2048]{1,0:T(8,128)(2,1)S(1)} %get-tuple-element.106.refs_7_.refs_10_), channel_id=1, source_target_pairs={{1,0},{5,4},{9,8},{13,12},{17,16},{21,20},{25,24},{29,28}} | collective-permute-start | bytes 393224 | tf_op jit(solution)/shard_map/ppermute | solution.py:541
  30.1 1.3 %collective-permute-start.19 = (bf16[32,2048]{1,0:T(8,128)(2,1)S(1)}, bf16[32,2048]{1,0:T(8,128)(2,1)S(1)}, u32[]{:S(2)}, u32[]{:S(2)}) collective-permute-start(bf16[32,2048]{1,0:T(8,128)(2,1)S(1)} %get-tuple-element.107.refs_12_.refs_0_.refs_11_), channel_id=1, source_target_pairs={{1,0},{5,4},{9,8},{13,12},{17,16},{21,20},{25,24},{29,28}} | collective-permute-start | bytes 393224 | tf_op jit(solution)/shard_map/ppermute | solution.py:541
  32.1 4.9 %collective-permute-done.12.refs_0_ = bf16[32,2048]{1,0:T(8,128)(2,1)S(1)} collective-permute-done((bf16[32,2048]{1,0:T(8,128)(2,1)S(1)}, bf16[32,2048]{1,0:T(8,128)(2,1)S(1)}, u32[]{:S(2)}, u32[]{:S(2)}) %collective-permute-start.12) | collective-permute-done | bytes 131104 | tf_op jit(solution)/shard_map/ppermute | solution.py:541
  37.0 0.8 %tick3_a_late.1 = (bf16[32,2048]{1,0:T(8,128)(2,1)S(1)}, bf16[32,512]{1,0:T(8,128)(2,1)S(1)}) custom-call(bf16[32,2048]{1,0:T(8,128)(2,1)S(1)} %collective-permute-done.12.refs_0_, bf16[4,32,128]{2,1,0:T(8,128)(2,1)S(1)} %get-tuple-element.75.refs_1_, f32[64,128]{1,0:T(8,128)S(1)} %get-tuple-element.76.refs_2_.refs_3_, ...), custom_call_target="tpu_custom_call" | custom-call | flops 1150000000 | tf_op jit(solution)/shard_map/tick3_a_late/pallas_call | solution.py:317
  37.8 2.0 %collective-permute-done.14.refs_1_ = bf16[32,2048]{1,0:T(8,128)(2,1)S(1)} collective-permute-done((bf16[32,2048]{1,0:T(8,128)(2,1)S(1)}, bf16[32,2048]{1,0:T(8,128)(2,1)S(1)}, u32[]{:S(2)}, u32[]{:S(2)}) %collective-permute-start.14) | collective-permute-done | bytes 131104 | tf_op jit(solution)/shard_map/ppermute | solution.py:541
  39.8 0.8 %tick3_a_early.1 = (bf16[32,2048]{1,0:T(8,128)(2,1)S(1)}, bf16[64,512]{1,0:T(8,128)(2,1)S(1)}, bf16[48,2048]{1,0:T(8,128)(2,1)S(1)}) custom-call(bf16[32,2048]{1,0:T(8,128)(2,1)S(1)} %collective-permute-done.12.refs_0_, bf16[32,2048]{1,0:T(8,128)(2,1)S(1)} %collective-permute-done.14.refs_1_, bf16[4,32,256]{2,1,0:T(8,128)(2,1)S(1)} %get-tuple-element.86.refs_2_, ...), custom_call_target="tpu_custom_call" | custom-call | flops 1150000000 | tf_op jit(solution)/shard_map/tick3_a_early/pallas_call | solution.py:317
  40.6 2.5 %collective-permute-start.22 = (bf16[64,512]{1,0:T(8,128)(2,1)S(1)}, bf16[64,512]{1,0:T(8,128)(2,1)S(1)}, u32[]{:S(2)}, u32[]{:S(2)}) collective-permute-start(bf16[64,512]{1,0:T(8,128)(2,1)S(1)} %get-tuple-element.121.refs_0_.refs_4_), channel_id=1, source_target_pairs={{0,24},{4,28},{8,16},{12,20},{16,8},{20,12},{24,0},{28,4},{1,25},{... | collective-permute-start | bytes 196616 | tf_op jit(solution)/shard_map/ppermute | solution.py:512
  44.3 0.8 %tick3_b_late.1 = (bf16[32,2048]{1,0:T(8,128)(2,1)S(1)}, bf16[32,512]{1,0:T(8,128)(2,1)S(1)}) custom-call(bf16[32,2048]{1,0:T(8,128)(2,1)S(1)} %collective-permute-done.18.refs_0_, bf16[4,32,128]{2,1,0:T(8,128)(2,1)S(1)} %get-tuple-element.91.refs_1_, f32[64,128]{1,0:T(8,128)S(1)} %get-tuple-element.89.refs_2_.refs_3_, ...), custom_call_target="tpu_custom_call" | custom-call | flops 1150000000 | tf_op jit(solution)/shard_map/tick3_b_late/pallas_call | solution.py:317
  45.1 1.4 %collective-permute-done.22.refs_19_.refs_9_ = bf16[64,512]{1,0:T(8,128)(2,1)S(1)} collective-permute-done((bf16[64,512]{1,0:T(8,128)(2,1)S(1)}, bf16[64,512]{1,0:T(8,128)(2,1)S(1)}, u32[]{:S(2)}, u32[]{:S(2)}) %collective-permute-start.22) | collective-permute-done | bytes 65568 | tf_op jit(solution)/shard_map/ppermute | solution.py:512
  46.5 0.9 %tick3_b_early.1 = (bf16[64,512]{1,0:T(8,128)(2,1)S(1)}, bf16[32,2048]{1,0:T(8,128)(2,1)S(1)}, bf16[32,2048]{1,0:T(8,128)(2,1)S(1)}, bf16[32,2048]{1,0:T(8,128)(2,1)S(1)}, bf16[16,2048]{1,0:T(8,128)(2,1)S(1)}) custom-call(bf16[32,2048]{1,0:T(8,128)(2,1)S(1)} %collective-permute-done.18.refs_0_, bf16[32,2048]{1,0:T(8,128)(2,1)S(1)} %collective-permute-done.19.refs_1_, ...), custom_call_target="tpu_custom_call" | custom-call | flops 1150000000 | tf_op jit(solution)/shard_map/tick3_b_early/pallas_call | solution.py:317
  47.3 1.7 %collective-permute-start.26 = (bf16[32,2048]{1,0:T(8,128)(2,1)S(1)}, bf16[32,2048]{1,0:T(8,128)(2,1)S(1)}, u32[]{:S(2)}, u32[]{:S(2)}) collective-permute-start(bf16[32,2048]{1,0:T(8,128)(2,1)S(1)} %get-tuple-element.126), channel_id=1, source_target_pairs={{0,8},{4,12},{8,0},{12,4},{16,24},{20,28},{24,16},{28,20},{1,9},{5... | collective-permute-start | bytes 393224 | tf_op jit(solution)/shard_map/ppermute | solution.py:512
  49.0 1.5 %collective-permute-start.28 = (bf16[64,512]{1,0:T(8,128)(2,1)S(1)}, bf16[64,512]{1,0:T(8,128)(2,1)S(1)}, u32[]{:S(2)}, u32[]{:S(2)}) collective-permute-start(bf16[64,512]{1,0:T(8,128)(2,1)S(1)} %get-tuple-element.122.refs_1_.refs_5_), channel_id=1, source_target_pairs={{0,16},{4,20},{8,24},{12,28},{16,0},{20,4},{24,8},{28,12},{1,17},{... | collective-permute-start | bytes 196616 | tf_op jit(solution)/shard_map/ppermute | solution.py:512
  51.1 1.6 %collective-permute-start.27 = (bf16[16,2048]{1,0:T(8,128)(2,1)S(1)}, bf16[16,2048]{1,0:T(8,128)(2,1)S(1)}, u32[]{:S(2)}, u32[]{:S(2)}) collective-permute-start(bf16[16,2048]{1,0:T(8,128)(2,1)S(1)} %get-tuple-element.127), channel_id=1, source_target_pairs={{0,12},{4,8},{8,4},{12,0},{16,28},{20,24},{24,20},{28,16},{1,13},{... | collective-permute-start | bytes 196616 | tf_op jit(solution)/shard_map/ppermute | solution.py:512
  52.7 0.8 %collective-permute-done.28.refs_8_ = bf16[64,512]{1,0:T(8,128)(2,1)S(1)} collective-permute-done((bf16[64,512]{1,0:T(8,128)(2,1)S(1)}, bf16[64,512]{1,0:T(8,128)(2,1)S(1)}, u32[]{:S(2)}, u32[]{:S(2)}) %collective-permute-start.28) | collective-permute-done | bytes 65568 | tf_op jit(solution)/shard_map/ppermute | solution.py:512
  53.5 2.9 %collective-permute-done.29.refs_10_ = bf16[64,512]{1,0:T(8,128)(2,1)S(1)} collective-permute-done((bf16[64,512]{1,0:T(8,128)(2,1)S(1)}, bf16[64,512]{1,0:T(8,128)(2,1)S(1)}, u32[]{:S(2)}, u32[]{:S(2)}) %collective-permute-start.29) | collective-permute-done | bytes 65568 | tf_op jit(solution)/shard_map/ppermute | solution.py:512
  57.5 0.8 %rows.1 = (bf16[128,2048]{1,0:T(8,128)(2,1)}, f32[8,128]{1,0:T(8,128)S(1)}) custom-call(bf16[48,2048]{1,0:T(8,128)(2,1)S(1)} %collective-permute-done.17.refs_0_.first_rows_ref.refs_6_, bf16[16,2048]{1,0:T(8,128)(2,1)S(1)} %collective-permute-done.24.handed_ref, bf16[32,2048]{1,0:T(8,128)(2,1)S(1)} %get-tuple-element.124.refs_0_, ...), custom_call_target="tpu_custom_call" | custom-call | flops 920000000 | tf_op jit(solution)/shard_map/rows/pallas_call | solution.py:594
  58.5 1.0 %finish.1 = (f32[256,512]{1,0:T(8,128)}, f32[1,256]{1,0:T(1,128)}) custom-call(f32[256,512]{1,0:T(8,128)S(1)} %get-tuple-element.130.own_ref, bf16[128,512]{1,0:T(8,128)(2,1)S(1)} %collective-permute-done.30.first_ref, bf16[128,512]{1,0:T(8,128)(2,1)S(1)} %collective-permute-done.31.second_ref, f32[256,512]{1,0:T(8,128)S(1)} %get-tuple-element.133.weight_ref, ...), custom_call_target="tpu_custom_call" | custom-call | tf_op jit(solution)/shard_map/finish/pallas_call | solution.py:605
  (64 shorter events, 8.2 us)
Async XLA Ops:
  2.0 6.8 %collective-permute-start = (bf16[16,4608]{1,0:T(8,128)(2,1)S(1)}, bf16[16,4608]{1,0:T(8,128)(2,1)S(1)}, u32[]{:S(2)}, u32[]{:S(2)}) collective-permute-start(bf16[16,4608]{1,0:T(8,128)(2,1)S(1)} %get-tuple-element.72), channel_id=1, source_target_pairs={{0,4},{4,0},{8,12},{12,8},{16,20},{20,16},{24,28},{28,24},{1,5},{5... | collective-permute-start | bytes 442376 | tf_op jit(solution)/shard_map/ppermute | solution.py:512
  2.5 7.7 %collective-permute-start.1 = (bf16[16,4608]{1,0:T(8,128)(2,1)S(1)}, bf16[16,4608]{1,0:T(8,128)(2,1)S(1)}, u32[]{:S(2)}, u32[]{:S(2)}) collective-permute-start(bf16[16,4608]{1,0:T(8,128)(2,1)S(1)} %get-tuple-element.73), channel_id=1, source_target_pairs={{0,8},{4,12},{8,0},{12,4},{16,24},{20,28},{24,16},{28,20},{1,9},{5... | collective-permute-start | bytes 442376 | tf_op jit(solution)/shard_map/ppermute | solution.py:512
  5.1 7.3 %collective-permute-start.2 = (bf16[16,4608]{1,0:T(8,128)(2,1)S(1)}, bf16[16,4608]{1,0:T(8,128)(2,1)S(1)}, u32[]{:S(2)}, u32[]{:S(2)}) collective-permute-start(bf16[16,4608]{1,0:T(8,128)(2,1)S(1)} %get-tuple-element.74), channel_id=1, source_target_pairs={{0,12},{4,8},{8,4},{12,0},{16,28},{20,24},{24,20},{28,16},{1,13},{... | collective-permute-start | bytes 442376 | tf_op jit(solution)/shard_map/ppermute | solution.py:512
  6.9 11.9 %collective-permute-start.4 = (bf16[80,2048]{1,0:T(8,128)(2,1)S(1)}, bf16[80,2048]{1,0:T(8,128)(2,1)S(1)}, u32[]{:S(2)}, u32[]{:S(2)}) collective-permute-start(bf16[80,2048]{1,0:T(8,128)(2,1)S(1)} %get-tuple-element.81), channel_id=1, source_target_pairs={{0,16},{4,20},{8,24},{12,28},{16,0},{20,4},{24,8},{28,12},{1,17},{... | collective-permute-start | bytes 983048 | tf_op jit(solution)/shard_map/ppermute | solution.py:512
  8.7 4.8 %collective-permute-start.5 = (bf16[16,4608]{1,0:T(8,128)(2,1)S(1)}, bf16[16,4608]{1,0:T(8,128)(2,1)S(1)}, u32[]{:S(2)}, u32[]{:S(2)}) collective-permute-start(bf16[16,4608]{1,0:T(8,128)(2,1)S(1)} %get-tuple-element.83), channel_id=1, source_target_pairs={{0,4},{4,0},{8,12},{12,8},{16,20},{20,16},{24,28},{28,24},{1,5},{5... | collective-permute-start | bytes 442376 | tf_op jit(solution)/shard_map/ppermute | solution.py:512
  8.8 7.3 %collective-permute-start.6 = (bf16[16,4608]{1,0:T(8,128)(2,1)S(1)}, bf16[16,4608]{1,0:T(8,128)(2,1)S(1)}, u32[]{:S(2)}, u32[]{:S(2)}) collective-permute-start(bf16[16,4608]{1,0:T(8,128)(2,1)S(1)} %get-tuple-element.84), channel_id=1, source_target_pairs={{0,8},{4,12},{8,0},{12,4},{16,24},{20,28},{24,16},{28,20},{1,9},{5... | collective-permute-start | bytes 442376 | tf_op jit(solution)/shard_map/ppermute | solution.py:512
  10.3 8.5 %collective-permute-start.7 = (bf16[16,4608]{1,0:T(8,128)(2,1)S(1)}, bf16[16,4608]{1,0:T(8,128)(2,1)S(1)}, u32[]{:S(2)}, u32[]{:S(2)}) collective-permute-start(bf16[16,4608]{1,0:T(8,128)(2,1)S(1)} %get-tuple-element.85), channel_id=1, source_target_pairs={{0,12},{4,8},{8,4},{12,0},{16,28},{20,24},{24,20},{28,16},{1,13},{... | collective-permute-start | bytes 442376 | tf_op jit(solution)/shard_map/ppermute | solution.py:512
  12.8 7.7 %collective-permute-start.3 = (bf16[32,2048]{1,0:T(8,128)(2,1)S(1)}, bf16[32,2048]{1,0:T(8,128)(2,1)S(1)}, u32[]{:S(2)}, u32[]{:S(2)}) collective-permute-start(bf16[32,2048]{1,0:T(8,128)(2,1)S(1)} %get-tuple-element.80.refs_7_.refs_6_), channel_id=1, source_target_pairs={{3,2},{7,6},{11,10},{15,14},{19,18},{23,22},{27,26},{31,30}} | collective-permute-start | bytes 393224 | tf_op jit(solution)/shard_map/ppermute | solution.py:541
  13.5 7.7 %collective-permute-start.11 = (bf16[32,2048]{1,0:T(8,128)(2,1)S(1)}, bf16[32,2048]{1,0:T(8,128)(2,1)S(1)}, u32[]{:S(2)}, u32[]{:S(2)}) collective-permute-start(bf16[32,2048]{1,0:T(8,128)(2,1)S(1)} %get-tuple-element.87.refs_5_.refs_7_), channel_id=1, source_target_pairs={{3,2},{7,6},{11,10},{15,14},{19,18},{23,22},{27,26},{31,30}} | collective-permute-start | bytes 393224 | tf_op jit(solution)/shard_map/ppermute | solution.py:541
  19.1 2.8 %collective-permute-start.9 = (bf16[32,2048]{1,0:T(8,128)(2,1)S(1)}, bf16[32,2048]{1,0:T(8,128)(2,1)S(1)}, u32[]{:S(2)}, u32[]{:S(2)}) collective-permute-start(bf16[32,2048]{1,0:T(8,128)(2,1)S(1)} %get-tuple-element.92.refs_7_.refs_6_), channel_id=1, source_target_pairs={{3,2},{7,6},{11,10},{15,14},{19,18},{23,22},{27,26},{31,30}} | collective-permute-start | bytes 393224 | tf_op jit(solution)/shard_map/ppermute | solution.py:541
  19.8 2.8 %collective-permute-start.10 = (bf16[32,2048]{1,0:T(8,128)(2,1)S(1)}, bf16[32,2048]{1,0:T(8,128)(2,1)S(1)}, u32[]{:S(2)}, u32[]{:S(2)}) collective-permute-start(bf16[32,2048]{1,0:T(8,128)(2,1)S(1)} %get-tuple-element.93.refs_6_.refs_7_), channel_id=1, source_target_pairs={{3,2},{7,6},{11,10},{15,14},{19,18},{23,22},{27,26},{31,30}} | collective-permute-start | bytes 393224 | tf_op jit(solution)/shard_map/ppermute | solution.py:541
  20.5 5.6 %collective-permute-start.8 = (bf16[32,2048]{1,0:T(8,128)(2,1)S(1)}, bf16[32,2048]{1,0:T(8,128)(2,1)S(1)}, u32[]{:S(2)}, u32[]{:S(2)}) collective-permute-start(bf16[32,2048]{1,0:T(8,128)(2,1)S(1)} %get-tuple-element.94.refs_7_.refs_8_), channel_id=1, source_target_pairs={{2,1},{6,5},{10,9},{14,13},{18,17},{22,21},{26,25},{30,29}} | collective-permute-start | bytes 393224 | tf_op jit(solution)/shard_map/ppermute | solution.py:541
  21.2 6.2 %collective-permute-start.13 = (bf16[32,2048]{1,0:T(8,128)(2,1)S(1)}, bf16[32,2048]{1,0:T(8,128)(2,1)S(1)}, u32[]{:S(2)}, u32[]{:S(2)}) collective-permute-start(bf16[32,2048]{1,0:T(8,128)(2,1)S(1)} %get-tuple-element.95.refs_6_.refs_9_), channel_id=1, source_target_pairs={{2,1},{6,5},{10,9},{14,13},{18,17},{22,21},{26,25},{30,29}} | collective-permute-start | bytes 393224 | tf_op jit(solution)/shard_map/ppermute | solution.py:541
  21.9 6.8 %collective-permute-start.15 = (bf16[32,2048]{1,0:T(8,128)(2,1)S(1)}, bf16[32,2048]{1,0:T(8,128)(2,1)S(1)}, u32[]{:S(2)}, u32[]{:S(2)}) collective-permute-start(bf16[32,2048]{1,0:T(8,128)(2,1)S(1)} %get-tuple-element.96.refs_7_.refs_8_), channel_id=1, source_target_pairs={{2,1},{6,5},{10,9},{14,13},{18,17},{22,21},{26,25},{30,29}} | collective-permute-start | bytes 393224 | tf_op jit(solution)/shard_map/ppermute | solution.py:541
  22.7 7.4 %collective-permute-start.16 = (bf16[32,2048]{1,0:T(8,128)(2,1)S(1)}, bf16[32,2048]{1,0:T(8,128)(2,1)S(1)}, u32[]{:S(2)}, u32[]{:S(2)}) collective-permute-start(bf16[32,2048]{1,0:T(8,128)(2,1)S(1)} %get-tuple-element.97.refs_6_.after_ref.refs_0_.refs_9_), channel_id=1, source_target_pairs={{2,1},{6,5},{10,9},{14,13},{18,17},{22,21},{26,25},{30,29}} | collective-permute-start | bytes 393224 | tf_op jit(solution)/shard_map/ppermute | solution.py:541
  23.5 7.9 %collective-permute-start.20 = (bf16[128,512]{1,0:T(8,128)(2,1)S(1)}, bf16[128,512]{1,0:T(8,128)(2,1)S(1)}, u32[]{:S(2)}, u32[]{:S(2)}) collective-permute-start(bf16[128,512]{1,0:T(8,128)(2,1)S(1)} %columns6.1), channel_id=1, source_target_pairs={{0,24},{4,28},{8,16},{12,20},{16,8},{20,12},{24,0},{28,4},{1,25},{... | collective-permute-start | bytes 393224 | tf_op jit(solution)/shard_map/ppermute | solution.py:512
  26.1 10.9 %collective-permute-start.12 = (bf16[32,2048]{1,0:T(8,128)(2,1)S(1)}, bf16[32,2048]{1,0:T(8,128)(2,1)S(1)}, u32[]{:S(2)}, u32[]{:S(2)}) collective-permute-start(bf16[32,2048]{1,0:T(8,128)(2,1)S(1)} %get-tuple-element.98.refs_7_.refs_10_), channel_id=1, source_target_pairs={{1,0},{5,4},{9,8},{13,12},{17,16},{21,20},{25,24},{29,28}} | collective-permute-start | bytes 393224 | tf_op jit(solution)/shard_map/ppermute | solution.py:541
  27.4 12.3 %collective-permute-start.14 = (bf16[32,2048]{1,0:T(8,128)(2,1)S(1)}, bf16[32,2048]{1,0:T(8,128)(2,1)S(1)}, u32[]{:S(2)}, u32[]{:S(2)}) collective-permute-start(bf16[32,2048]{1,0:T(8,128)(2,1)S(1)} %get-tuple-element.99.refs_6_.refs_11_), channel_id=1, source_target_pairs={{1,0},{5,4},{9,8},{13,12},{17,16},{21,20},{25,24},{29,28}} | collective-permute-start | bytes 393224 | tf_op jit(solution)/shard_map/ppermute | solution.py:541
  28.8 15.0 %collective-permute-start.18 = (bf16[32,2048]{1,0:T(8,128)(2,1)S(1)}, bf16[32,2048]{1,0:T(8,128)(2,1)S(1)}, u32[]{:S(2)}, u32[]{:S(2)}) collective-permute-start(bf16[32,2048]{1,0:T(8,128)(2,1)S(1)} %get-tuple-element.106.refs_7_.refs_10_), channel_id=1, source_target_pairs={{1,0},{5,4},{9,8},{13,12},{17,16},{21,20},{25,24},{29,28}} | collective-permute-start | bytes 393224 | tf_op jit(solution)/shard_map/ppermute | solution.py:541
  30.1 16.4 %collective-permute-start.19 = (bf16[32,2048]{1,0:T(8,128)(2,1)S(1)}, bf16[32,2048]{1,0:T(8,128)(2,1)S(1)}, u32[]{:S(2)}, u32[]{:S(2)}) collective-permute-start(bf16[32,2048]{1,0:T(8,128)(2,1)S(1)} %get-tuple-element.107.refs_12_.refs_0_.refs_11_), channel_id=1, source_target_pairs={{1,0},{5,4},{9,8},{13,12},{17,16},{21,20},{25,24},{29,28}} | collective-permute-start | bytes 393224 | tf_op jit(solution)/shard_map/ppermute | solution.py:541
  31.5 15.0 %collective-permute-start.21 = (bf16[128,512]{1,0:T(8,128)(2,1)S(1)}, bf16[128,512]{1,0:T(8,128)(2,1)S(1)}, u32[]{:S(2)}, u32[]{:S(2)}) collective-permute-start(bf16[128,512]{1,0:T(8,128)(2,1)S(1)} %columns2.1), channel_id=1, source_target_pairs={{0,8},{4,12},{8,0},{12,4},{16,24},{20,28},{24,16},{28,20},{1,9},{5... | collective-permute-start | bytes 393224 | tf_op jit(solution)/shard_map/ppermute | solution.py:512
  40.6 5.8 %collective-permute-start.22 = (bf16[64,512]{1,0:T(8,128)(2,1)S(1)}, bf16[64,512]{1,0:T(8,128)(2,1)S(1)}, u32[]{:S(2)}, u32[]{:S(2)}) collective-permute-start(bf16[64,512]{1,0:T(8,128)(2,1)S(1)} %get-tuple-element.121.refs_0_.refs_4_), channel_id=1, source_target_pairs={{0,24},{4,28},{8,16},{12,20},{16,8},{20,12},{24,0},{28,4},{1,25},{... | collective-permute-start | bytes 196616 | tf_op jit(solution)/shard_map/ppermute | solution.py:512
  43.2 7.9 %collective-permute-start.17 = (bf16[48,2048]{1,0:T(8,128)(2,1)S(1)}, bf16[48,2048]{1,0:T(8,128)(2,1)S(1)}, u32[]{:S(2)}, u32[]{:S(2)}) collective-permute-start(bf16[48,2048]{1,0:T(8,128)(2,1)S(1)} %get-tuple-element.110), channel_id=1, source_target_pairs={{0,8},{4,12},{8,0},{12,4},{16,24},{20,28},{24,16},{28,20},{1,9},{5... | collective-permute-start | bytes 589832 | tf_op jit(solution)/shard_map/ppermute | solution.py:512
  43.8 7.3 %collective-permute-start.23 = (bf16[192,512]{1,0:T(8,128)(2,1)S(1)}, bf16[192,512]{1,0:T(8,128)(2,1)S(1)}, u32[]{:S(2)}, u32[]{:S(2)}) collective-permute-start(bf16[192,512]{1,0:T(8,128)(2,1)S(1)} %columns4.1), channel_id=1, source_target_pairs={{0,16},{4,20},{8,24},{12,28},{16,0},{20,4},{24,8},{28,12},{1,17},{... | collective-permute-start | bytes 589832 | tf_op jit(solution)/shard_map/ppermute | solution.py:512
  47.3 9.1 %collective-permute-start.26 = (bf16[32,2048]{1,0:T(8,128)(2,1)S(1)}, bf16[32,2048]{1,0:T(8,128)(2,1)S(1)}, u32[]{:S(2)}, u32[]{:S(2)}) collective-permute-start(bf16[32,2048]{1,0:T(8,128)(2,1)S(1)} %get-tuple-element.126), channel_id=1, source_target_pairs={{0,8},{4,12},{8,0},{12,4},{16,24},{20,28},{24,16},{28,20},{1,9},{5... | collective-permute-start | bytes 393224 | tf_op jit(solution)/shard_map/ppermute | solution.py:512
  49.0 4.4 %collective-permute-start.28 = (bf16[64,512]{1,0:T(8,128)(2,1)S(1)}, bf16[64,512]{1,0:T(8,128)(2,1)S(1)}, u32[]{:S(2)}, u32[]{:S(2)}) collective-permute-start(bf16[64,512]{1,0:T(8,128)(2,1)S(1)} %get-tuple-element.122.refs_1_.refs_5_), channel_id=1, source_target_pairs={{0,16},{4,20},{8,24},{12,28},{16,0},{20,4},{24,8},{28,12},{1,17},{... | collective-permute-start | bytes 196616 | tf_op jit(solution)/shard_map/ppermute | solution.py:512
  50.6 5.8 %collective-permute-start.29 = (bf16[64,512]{1,0:T(8,128)(2,1)S(1)}, bf16[64,512]{1,0:T(8,128)(2,1)S(1)}, u32[]{:S(2)}, u32[]{:S(2)}) collective-permute-start(bf16[64,512]{1,0:T(8,128)(2,1)S(1)} %get-tuple-element.122.refs_1_.refs_5_), channel_id=1, source_target_pairs={{0,24},{4,28},{8,16},{12,20},{16,8},{20,12},{24,0},{28,4},{1,25},{... | collective-permute-start | bytes 196616 | tf_op jit(solution)/shard_map/ppermute | solution.py:512
  51.1 6.4 %collective-permute-start.25 = (bf16[32,2048]{1,0:T(8,128)(2,1)S(1)}, bf16[32,2048]{1,0:T(8,128)(2,1)S(1)}, u32[]{:S(2)}, u32[]{:S(2)}) collective-permute-start(bf16[32,2048]{1,0:T(8,128)(2,1)S(1)} %get-tuple-element.125), channel_id=1, source_target_pairs={{0,4},{4,0},{8,12},{12,8},{16,20},{20,16},{24,28},{28,24},{1,5},{5... | collective-permute-start | bytes 393224 | tf_op jit(solution)/shard_map/ppermute | solution.py:512
  51.1 6.4 %collective-permute-start.27 = (bf16[16,2048]{1,0:T(8,128)(2,1)S(1)}, bf16[16,2048]{1,0:T(8,128)(2,1)S(1)}, u32[]{:S(2)}, u32[]{:S(2)}) collective-permute-start(bf16[16,2048]{1,0:T(8,128)(2,1)S(1)} %get-tuple-element.127), channel_id=1, source_target_pairs={{0,12},{4,8},{8,4},{12,0},{16,28},{20,24},{24,20},{28,16},{1,13},{... | collective-permute-start | bytes 196616 | tf_op jit(solution)/shard_map/ppermute | solution.py:512
  53.5 4.0 %collective-permute-start.24 = (bf16[16,2048]{1,0:T(8,128)(2,1)S(1)}, bf16[16,2048]{1,0:T(8,128)(2,1)S(1)}, u32[]{:S(2)}, u32[]{:S(2)}) collective-permute-start(bf16[16,2048]{1,0:T(8,128)(2,1)S(1)} %get-tuple-element.123), channel_id=1, source_target_pairs={{0,4},{4,0},{8,12},{12,8},{16,20},{20,16},{24,28},{28,24},{1,5},{5... | collective-permute-start | bytes 196616 | tf_op jit(solution)/shard_map/ppermute | solution.py:512
  56.9 1.4 %collective-permute-start.30 = (bf16[128,512]{1,0:T(8,128)(2,1)S(1)}, bf16[128,512]{1,0:T(8,128)(2,1)S(1)}, u32[]{:S(2)}, u32[]{:S(2)}) collective-permute-start(bf16[128,512]{1,0:T(8,128)(2,1)S(1)} %get-tuple-element.131), channel_id=1, source_target_pairs={{0,4},{4,0},{8,12},{12,8},{16,20},{20,16},{24,28},{28,24},{1,5},{5... | collective-permute-start | bytes 393224 | tf_op jit(solution)/shard_map/ppermute | solution.py:512
  57.0 1.5 %collective-permute-start.31 = (bf16[128,512]{1,0:T(8,128)(2,1)S(1)}, bf16[128,512]{1,0:T(8,128)(2,1)S(1)}, u32[]{:S(2)}, u32[]{:S(2)}) collective-permute-start(bf16[128,512]{1,0:T(8,128)(2,1)S(1)} %get-tuple-element.132), channel_id=1, source_target_pairs={{0,4},{4,0},{8,12},{12,8},{16,20},{20,16},{24,28},{28,24},{1,5},{5... | collective-permute-start | bytes 393224 | tf_op jit(solution)/shard_map/ppermute | solution.py:512
  (2 other events, 9.1 us)

commit v14 on v13

--- a/solution.py
+++ b/solution.py
@@ -12,7 +12,7 @@
 UNIT = 32
 EPSILON = 1e-06
 MASKED = -1e30
-OUTS = {2: 3, 4: 5}
+OUTS = {2: 3, 5: 6}
 UNITS = ("a_late", "a_early", "b_late", "b_early")
 VMEM = pl.BlockSpec(memory_space=pltpu.VMEM)
 SMEM = pl.BlockSpec(memory_space=pltpu.SMEM)
@@ -124,7 +124,7 @@
 def unit_math(rows, grads, probs_ref, x_ref, inv_ref, turned_ref, gain_ref, scaled_ref, store, value_ref):
     kv_width, model_width = turned_ref.shape
     heads = model_width // kv_width
-    chunk = min(512, model_width)
+    chunk = min(1024, model_width)
     inv = inv_ref[rows, :1]
     values = []
     for c in range(kv_width // HEAD_FEATURES):
@@ -264,11 +264,13 @@
     blocks_ref[first_row + UNIT : first_row + BLOCK, :] = late_refs[1][...]
     outs[1 if late == 2 else 0][...] = values
     if late > 2:
-        late_a_ref, early_a_ref = late_refs[2:]
+        late_a_ref, early_a_ref, value_a_ref = late_refs[2:]
+        outs[1][:BLOCK, :] = value_a_ref[...]
+        outs[1][BLOCK:, :] = values
         blocks_ref[EARLY, :] = early_a_ref[...]
         blocks_ref[LATE, :] = late_a_ref[...]
     at = place()[1]
-    pieces = {2: outs[2]} if late == 2 else dict(enumerate(outs[1:]))
+    pieces = {2: outs[2]} if late == 2 else dict(enumerate(outs[2:]))
     piece = BLOCK * kv_width // model_width
 
     def rows_for(k, block):
@@ -311,7 +313,7 @@
         piece = BLOCK // half
         shapes = [rows, (BLOCK, kv_width), (3 * piece, model_width)]
     if len(late) > 2:
-        shapes = [(BLOCK, kv_width)]
+        shapes = [(BLOCK, kv_width), (2 * BLOCK, kv_width)]
         shapes += [(2 * piece, model_width)] * 3 + [(piece, model_width)]
     parts = [part for _, part in grads]
     return pl.pallas_call(
@@ -446,7 +448,7 @@
         beside = ref.shape[1] > kv_width
         rows = slice(first, 2 * first) if beside else slice(0, ref.shape[0])
         parts += [ref[rows, at : at + kv_width] for at in range(0, ref.shape[1], kv_width)]
-    parts.insert(len(parts) - 3, columns[2][2 * BLOCK :, :])
+    parts.insert(len(parts) - 2, columns[2][2 * BLOCK :, :])
     value = jnp.concatenate(parts, axis=0)
     mine = lax.rem(place()[2], 2)
 
@@ -562,10 +564,10 @@
             if last and u == 1:
                 late = [done[0][1], done[0][0]]
             if last and u == 3:
-                late = [done[2][1], done[2][0], done[0][0], done[1][0]]
-                first_value, first_rows = swap(done[1][1], 6), swap(done[1][2], 2)
+                late = [done[2][1], done[2][0], done[0][0], done[1][0], done[1][1]]
+                first_rows = swap(done[1][2], 2)
                 columns[4] = swap(columns_for(4, blocks, [], [done[1][1]]), 4)
-                after = after + [columns[2], first_value]
+                after = after + [columns[2]]
             done.append(
                 tick_step(
                     tick, needs, blocks[u // 2], turned, gain, kept[u] if last else (), late,
@@ -574,18 +576,17 @@
             )
             after = [done[u][0]]
             kept[u].append(done[u])
-    own_value, *rows = done[3]
-    own_first = done[1][1]
+    own_value, own_values, *rows = done[3]
     rows = [rows[0]] + [swap(rows[k], k) for k in range(1, half)]
-    last_value = swap(own_value, 6)
-    columns[0], handed = columns_for(0, blocks, [own_value, columns[4]], [first_rows])
+    far_values, across_value = swap(own_values, 6), swap(own_value, 4)
+    columns[0], handed = columns_for(0, blocks, [own_value, columns[4], far_values, across_value], [first_rows])
     handed = swap(handed, 1)
-    values = [own_first, own_value, first_rows, rows[2], swap(own_value, 4), first_value, last_value]
+    values = [own_values, first_rows, rows[2], across_value, far_values]
     own, *other = pl.pallas_call(
         functools.partial(partial_kernel, shares, piece),
         out_shape=(jax.ShapeDtypeStruct((shares, kv_width), jnp.float32),)
         + (jax.ShapeDtypeStruct((shares // 2, kv_width), bf16),) * 2,
-        in_specs=[VMEM] * 11,
+        in_specs=[VMEM] * 9,
         out_specs=(VMEM,) * 3,
         name="weight_partial",
         **params(0.0),

time: 59.8 us -> 59.1 us (0.988)
    ppermute x20 -> x19, waiting for transfers between devices: 11.9 us -> 10.8 us  [swap(): return lax.ppermute(array, 'dp', [(i, i ^ k) for i in range(replicas)])]
    ppermute x12, waiting for transfers between devices: 6.97 us -> 7.8 us  [direct(): lax.ppermute(unit[-1][0], 'section', hop)]
    ppermute x20 -> x19, starting transfers between devices: 19.4 us -> 18.9 us  [swap(): return lax.ppermute(array, 'dp', [(i, i ^ k) for i in range(replicas)])]
  transfers between devices with their start and end apart: 32 -> 31, of which waited for: 10 -> 9; matrix products, arithmetic and copies ran while one was open for 0% -> 0% of each run, Pallas kernels for 12% -> 13%
where the time goes in v14:
time: 59.1 us; the launch traced here: 58.8 us
  starting transfers between devices  29.5 us (50%)
  waiting for transfers between devices  18.6 us (31%)
  Pallas kernels  9.72 us (16%)
  between operations  1.04 us (2%)
    ppermute x19, starting transfers between devices, swap(): return lax.ppermute(array, 'dp', [(i, i ^ k) for i in range(replicas)])  18.9 us
    ppermute x19, waiting for transfers between devices, swap(): return lax.ppermute(array, 'dp', [(i, i ^ k) for i in range(replicas)])  10.8 us
    ppermute x12, starting transfers between devices, direct(): lax.ppermute(unit[-1][0], 'section', hop)  10.5 us
    ppermute x12, waiting for transfers between devices, direct(): lax.ppermute(unit[-1][0], 'section', hop)  7.8 us
    pallas_call x16, Pallas kernels, tick_step(): pl.pallas_call(functools.partial(tick_kernel, tick, EARLY if low else LAT...  3.45 us
    pallas_call x2, Pallas kernels, pack(): pl.pallas_call(functools.partial(pack_kernel, block, half, piece), out_sh...  3.06 us
  transfers between devices with their start and end apart: 31, of which 9 were waited for; matrix products, arithmetic and copies ran while one was open for 0% of the time, Pallas kernels for 13%

profile of v14, /device:TPU:0, one launch (start us, length us, event | category | flops | bytes accessed | tf_op | source)
XLA Modules:
  0.0 58.8 jit_solution(10777501951238192620)
XLA Ops:
  0.7 1.4 %pack.2 = (bf16[16,4608]{1,0:T(8,128)(2,1)S(1)}, bf16[16,4608]{1,0:T(8,128)(2,1)S(1)}, bf16[16,4608]{1,0:T(8,128)(2,1)S(1)}, bf16[16,4608]{1,0:T(8,128)(2,1)S(1)}, bf16[80,2048]{1,0:T(8,128)(2,1)S(1)}) custom-call(bf16[128,2048]{1,0:T(8,128)(2,1)} %bitcast.8, bf16[128,512]{1,0:T(8,128)(2,1)} %bitcast.13, bf16[128,2048]{1,0:T(8,128)(2,1)} %bitcast.10, ...), custom_call_target="tpu_custom_call" | custom-call | flops 1380000000 | tf_op jit(solution)/shard_map/pack/pallas_call | solution.py:383
  2.5 2.6 %collective-permute-start.1 = (bf16[16,4608]{1,0:T(8,128)(2,1)S(1)}, bf16[16,4608]{1,0:T(8,128)(2,1)S(1)}, u32[]{:S(2)}, u32[]{:S(2)}) collective-permute-start(bf16[16,4608]{1,0:T(8,128)(2,1)S(1)} %get-tuple-element.74), channel_id=1, source_target_pairs={{0,8},{4,12},{8,0},{12,4},{16,24},{20,28},{24,16},{28,20},{1,9},{5... | collective-permute-start | bytes 442376 | tf_op jit(solution)/shard_map/ppermute | solution.py:514
  5.2 1.7 %pack.3 = (f32[1,2048]{1,0:T(1,128)S(1)}, bf16[512,2048]{1,0:T(8,128)(2,1)S(1)}, bf16[16,4608]{1,0:T(8,128)(2,1)S(1)}, bf16[16,4608]{1,0:T(8,128)(2,1)S(1)}, bf1...) custom-call(bf16[128,2048]{1,0:T(8,128)(2,1)} %bitcast.9, ...), custom_call_target="tpu_custom_call" | custom-call | flops 1380000000 | tf_op jit(solution)/shard_map/pack/pallas_call | solution.py:383
  6.9 1.8 %collective-permute-start.4 = (bf16[80,2048]{1,0:T(8,128)(2,1)S(1)}, bf16[80,2048]{1,0:T(8,128)(2,1)S(1)}, u32[]{:S(2)}, u32[]{:S(2)}) collective-permute-start(bf16[80,2048]{1,0:T(8,128)(2,1)S(1)} %get-tuple-element.82), channel_id=1, source_target_pairs={{0,16},{4,20},{8,24},{12,28},{16,0},{20,4},{24,8},{28,12},{1,17},{... | collective-permute-start | bytes 983048 | tf_op jit(solution)/shard_map/ppermute | solution.py:514
  8.8 1.5 %collective-permute-start.6 = (bf16[16,4608]{1,0:T(8,128)(2,1)S(1)}, bf16[16,4608]{1,0:T(8,128)(2,1)S(1)}, u32[]{:S(2)}, u32[]{:S(2)}) collective-permute-start(bf16[16,4608]{1,0:T(8,128)(2,1)S(1)} %get-tuple-element.85), channel_id=1, source_target_pairs={{0,8},{4,12},{8,0},{12,4},{16,24},{20,28},{24,16},{28,20},{1,9},{5... | collective-permute-start | bytes 442376 | tf_op jit(solution)/shard_map/ppermute | solution.py:514
  10.6 1.9 %collective-permute-done.2.refs_3_ = bf16[16,4608]{1,0:T(8,128)(2,1)S(1)} collective-permute-done((bf16[16,4608]{1,0:T(8,128)(2,1)S(1)}, bf16[16,4608]{1,0:T(8,128)(2,1)S(1)}, u32[]{:S(2)}, u32[]{:S(2)}) %collective-permute-start.2) | collective-permute-done | bytes 147488 | tf_op jit(solution)/shard_map/ppermute | solution.py:514
  13.5 0.7 %collective-permute-start.11 = (bf16[32,2048]{1,0:T(8,128)(2,1)S(1)}, bf16[32,2048]{1,0:T(8,128)(2,1)S(1)}, u32[]{:S(2)}, u32[]{:S(2)}) collective-permute-start(bf16[32,2048]{1,0:T(8,128)(2,1)S(1)} %get-tuple-element.88.refs_5_.refs_7_), channel_id=1, source_target_pairs={{3,2},{7,6},{11,10},{15,14},{19,18},{23,22},{27,26},{31,30}} | collective-permute-start | bytes 393224 | tf_op jit(solution)/shard_map/ppermute | solution.py:543
  14.2 1.9 %collective-permute-done.6.refs_2_ = bf16[16,4608]{1,0:T(8,128)(2,1)S(1)} collective-permute-done((bf16[16,4608]{1,0:T(8,128)(2,1)S(1)}, bf16[16,4608]{1,0:T(8,128)(2,1)S(1)}, u32[]{:S(2)}, u32[]{:S(2)}) %collective-permute-start.6) | collective-permute-done | bytes 147488 | tf_op jit(solution)/shard_map/ppermute | solution.py:514
  16.1 2.6 %collective-permute-done.7.refs_3_ = bf16[16,4608]{1,0:T(8,128)(2,1)S(1)} collective-permute-done((bf16[16,4608]{1,0:T(8,128)(2,1)S(1)}, bf16[16,4608]{1,0:T(8,128)(2,1)S(1)}, u32[]{:S(2)}, u32[]{:S(2)}) %collective-permute-start.7) | collective-permute-done | bytes 147488 | tf_op jit(solution)/shard_map/ppermute | solution.py:514
  19.1 0.7 %collective-permute-start.9 = (bf16[32,2048]{1,0:T(8,128)(2,1)S(1)}, bf16[32,2048]{1,0:T(8,128)(2,1)S(1)}, u32[]{:S(2)}, u32[]{:S(2)}) collective-permute-start(bf16[32,2048]{1,0:T(8,128)(2,1)S(1)} %get-tuple-element.93.refs_7_.refs_6_), channel_id=1, source_target_pairs={{3,2},{7,6},{11,10},{15,14},{19,18},{23,22},{27,26},{31,30}} | collective-permute-start | bytes 393224 | tf_op jit(solution)/shard_map/ppermute | solution.py:543
  20.5 0.7 %collective-permute-start.8 = (bf16[32,2048]{1,0:T(8,128)(2,1)S(1)}, bf16[32,2048]{1,0:T(8,128)(2,1)S(1)}, u32[]{:S(2)}, u32[]{:S(2)}) collective-permute-start(bf16[32,2048]{1,0:T(8,128)(2,1)S(1)} %get-tuple-element.95.refs_7_.refs_8_), channel_id=1, source_target_pairs={{2,1},{6,5},{10,9},{14,13},{18,17},{22,21},{26,25},{30,29}} | collective-permute-start | bytes 393224 | tf_op jit(solution)/shard_map/ppermute | solution.py:543
  22.7 0.7 %collective-permute-start.16 = (bf16[32,2048]{1,0:T(8,128)(2,1)S(1)}, bf16[32,2048]{1,0:T(8,128)(2,1)S(1)}, u32[]{:S(2)}, u32[]{:S(2)}) collective-permute-start(bf16[32,2048]{1,0:T(8,128)(2,1)S(1)} %get-tuple-element.98.refs_6_.after_ref.refs_0_.refs_9_), channel_id=1, source_target_pairs={{2,1},{6,5},{10,9},{14,13},{18,17},{22,21},{26,25},{30,29}} | collective-permute-start | bytes 393224 | tf_op jit(solution)/shard_map/ppermute | solution.py:543
  23.5 2.6 %collective-permute-start.20 = (bf16[128,512]{1,0:T(8,128)(2,1)S(1)}, bf16[128,512]{1,0:T(8,128)(2,1)S(1)}, u32[]{:S(2)}, u32[]{:S(2)}) collective-permute-start(bf16[128,512]{1,0:T(8,128)(2,1)S(1)} %columns6.1), channel_id=1, source_target_pairs={{0,24},{4,28},{8,16},{12,20},{16,8},{20,12},{24,0},{28,4},{1,25},{... | collective-permute-start | bytes 393224 | tf_op jit(solution)/shard_map/ppermute | solution.py:514
  26.1 1.3 %collective-permute-start.12 = (bf16[32,2048]{1,0:T(8,128)(2,1)S(1)}, bf16[32,2048]{1,0:T(8,128)(2,1)S(1)}, u32[]{:S(2)}, u32[]{:S(2)}) collective-permute-start(bf16[32,2048]{1,0:T(8,128)(2,1)S(1)} %get-tuple-element.99.refs_7_.refs_10_), channel_id=1, source_target_pairs={{1,0},{5,4},{9,8},{13,12},{17,16},{21,20},{25,24},{29,28}} | collective-permute-start | bytes 393224 | tf_op jit(solution)/shard_map/ppermute | solution.py:543
  27.4 1.3 %collective-permute-start.14 = (bf16[32,2048]{1,0:T(8,128)(2,1)S(1)}, bf16[32,2048]{1,0:T(8,128)(2,1)S(1)}, u32[]{:S(2)}, u32[]{:S(2)}) collective-permute-start(bf16[32,2048]{1,0:T(8,128)(2,1)S(1)} %get-tuple-element.100.refs_6_.refs_11_), channel_id=1, source_target_pairs={{1,0},{5,4},{9,8},{13,12},{17,16},{21,20},{25,24},{29,28}} | collective-permute-start | bytes 393224 | tf_op jit(solution)/shard_map/ppermute | solution.py:543
  28.8 1.3 %collective-permute-start.18 = (bf16[32,2048]{1,0:T(8,128)(2,1)S(1)}, bf16[32,2048]{1,0:T(8,128)(2,1)S(1)}, u32[]{:S(2)}, u32[]{:S(2)}) collective-permute-start(bf16[32,2048]{1,0:T(8,128)(2,1)S(1)} %get-tuple-element.107.refs_7_.refs_10_), channel_id=1, source_target_pairs={{1,0},{5,4},{9,8},{13,12},{17,16},{21,20},{25,24},{29,28}} | collective-permute-start | bytes 393224 | tf_op jit(solution)/shard_map/ppermute | solution.py:543
  30.1 1.3 %collective-permute-start.19 = (bf16[32,2048]{1,0:T(8,128)(2,1)S(1)}, bf16[32,2048]{1,0:T(8,128)(2,1)S(1)}, u32[]{:S(2)}, u32[]{:S(2)}) collective-permute-start(bf16[32,2048]{1,0:T(8,128)(2,1)S(1)} %get-tuple-element.108.refs_12_.refs_0_.refs_11_), channel_id=1, source_target_pairs={{1,0},{5,4},{9,8},{13,12},{17,16},{21,20},{25,24},{29,28}} | collective-permute-start | bytes 393224 | tf_op jit(solution)/shard_map/ppermute | solution.py:543
  32.1 4.9 %collective-permute-done.12.refs_0_ = bf16[32,2048]{1,0:T(8,128)(2,1)S(1)} collective-permute-done((bf16[32,2048]{1,0:T(8,128)(2,1)S(1)}, bf16[32,2048]{1,0:T(8,128)(2,1)S(1)}, u32[]{:S(2)}, u32[]{:S(2)}) %collective-permute-start.12) | collective-permute-done | bytes 131104 | tf_op jit(solution)/shard_map/ppermute | solution.py:543
  37.0 0.8 %tick3_a_late.1 = (bf16[32,2048]{1,0:T(8,128)(2,1)S(1)}, bf16[32,512]{1,0:T(8,128)(2,1)S(1)}) custom-call(bf16[32,2048]{1,0:T(8,128)(2,1)S(1)} %collective-permute-done.12.refs_0_, bf16[4,32,128]{2,1,0:T(8,128)(2,1)S(1)} %get-tuple-element.76.refs_1_, f32[64,128]{1,0:T(8,128)S(1)} %get-tuple-element.77.refs_2_.refs_3_, ...), custom_call_target="tpu_custom_call" | custom-call | flops 1150000000 | tf_op jit(solution)/shard_map/tick3_a_late/pallas_call | solution.py:319
  37.8 2.0 %collective-permute-done.14.refs_1_ = bf16[32,2048]{1,0:T(8,128)(2,1)S(1)} collective-permute-done((bf16[32,2048]{1,0:T(8,128)(2,1)S(1)}, bf16[32,2048]{1,0:T(8,128)(2,1)S(1)}, u32[]{:S(2)}, u32[]{:S(2)}) %collective-permute-start.14) | collective-permute-done | bytes 131104 | tf_op jit(solution)/shard_map/ppermute | solution.py:543
  39.8 0.8 %tick3_a_early.1 = (bf16[32,2048]{1,0:T(8,128)(2,1)S(1)}, bf16[64,512]{1,0:T(8,128)(2,1)S(1)}, bf16[48,2048]{1,0:T(8,128)(2,1)S(1)}) custom-call(bf16[32,2048]{1,0:T(8,128)(2,1)S(1)} %collective-permute-done.12.refs_0_, bf16[32,2048]{1,0:T(8,128)(2,1)S(1)} %collective-permute-done.14.refs_1_, bf16[4,32,256]{2,1,0:T(8,128)(2,1)S(1)} %get-tuple-element.87.refs_2_, ...), custom_call_target="tpu_custom_call" | custom-call | flops 1150000000 | tf_op jit(solution)/shard_map/tick3_a_early/pallas_call | solution.py:319
  40.6 1.5 %collective-permute-start.17 = (bf16[48,2048]{1,0:T(8,128)(2,1)S(1)}, bf16[48,2048]{1,0:T(8,128)(2,1)S(1)}, u32[]{:S(2)}, u32[]{:S(2)}) collective-permute-start(bf16[48,2048]{1,0:T(8,128)(2,1)S(1)} %get-tuple-element.111), channel_id=1, source_target_pairs={{0,8},{4,12},{8,0},{12,4},{16,24},{20,28},{24,16},{28,20},{1,9},{5... | collective-permute-start | bytes 589832 | tf_op jit(solution)/shard_map/ppermute | solution.py:514
  42.2 1.6 %collective-permute-start.22 = (bf16[192,512]{1,0:T(8,128)(2,1)S(1)}, bf16[192,512]{1,0:T(8,128)(2,1)S(1)}, u32[]{:S(2)}, u32[]{:S(2)}) collective-permute-start(bf16[192,512]{1,0:T(8,128)(2,1)S(1)} %columns4.1), channel_id=1, source_target_pairs={{0,16},{4,20},{8,24},{12,28},{16,0},{20,4},{24,8},{28,12},{1,17},{... | collective-permute-start | bytes 589832 | tf_op jit(solution)/shard_map/ppermute | solution.py:514
  43.8 0.8 %tick3_b_late.1 = (bf16[32,2048]{1,0:T(8,128)(2,1)S(1)}, bf16[32,512]{1,0:T(8,128)(2,1)S(1)}) custom-call(bf16[32,2048]{1,0:T(8,128)(2,1)S(1)} %collective-permute-done.18.refs_0_, bf16[4,32,128]{2,1,0:T(8,128)(2,1)S(1)} %get-tuple-element.92.refs_1_, f32[64,128]{1,0:T(8,128)S(1)} %get-tuple-element.90.refs_2_.refs_3_, ...), custom_call_target="tpu_custom_call" | custom-call | flops 1150000000 | tf_op jit(solution)/shard_map/tick3_b_late/pallas_call | solution.py:319
  44.6 0.8 %collective-permute-done.19.refs_1_ = bf16[32,2048]{1,0:T(8,128)(2,1)S(1)} collective-permute-done((bf16[32,2048]{1,0:T(8,128)(2,1)S(1)}, bf16[32,2048]{1,0:T(8,128)(2,1)S(1)}, u32[]{:S(2)}, u32[]{:S(2)}) %collective-permute-start.19) | collective-permute-done | bytes 131104 | tf_op jit(solution)/shard_map/ppermute | solution.py:543
  45.4 0.9 %tick3_b_early.1 = (bf16[64,512]{1,0:T(8,128)(2,1)S(1)}, bf16[128,512]{1,0:T(8,128)(2,1)S(1)}, bf16[32,2048]{1,0:T(8,128)(2,1)S(1)}, bf16[32,2048]{1,0:T(8,128)(...) custom-call(bf16[32,2048]{1,0:T(8,128)(2,1)S(1)} %collective-permute-done.18.refs_0_, ...), custom_call_target="tpu_custom_call" | custom-call | flops 1150000000 | tf_op jit(solution)/shard_map/tick3_b_early/pallas_call | solution.py:319
  46.3 2.5 %collective-permute-start.23 = (bf16[128,512]{1,0:T(8,128)(2,1)S(1)}, bf16[128,512]{1,0:T(8,128)(2,1)S(1)}, u32[]{:S(2)}, u32[]{:S(2)}) collective-permute-start(bf16[128,512]{1,0:T(8,128)(2,1)S(1)} %get-tuple-element.124.refs_4_), channel_id=1, source_target_pairs={{0,24},{4,28},{8,16},{12,20},{16,8},{20,12},{24,0},{28,4},{1,25},{... | collective-permute-start | bytes 393224 | tf_op jit(solution)/shard_map/ppermute | solution.py:514
  49.9 1.6 %collective-permute-start.28 = (bf16[16,2048]{1,0:T(8,128)(2,1)S(1)}, bf16[16,2048]{1,0:T(8,128)(2,1)S(1)}, u32[]{:S(2)}, u32[]{:S(2)}) collective-permute-start(bf16[16,2048]{1,0:T(8,128)(2,1)S(1)} %get-tuple-element.129), channel_id=1, source_target_pairs={{0,12},{4,8},{8,4},{12,0},{16,28},{20,24},{24,20},{28,16},{1,13},{... | collective-permute-start | bytes 196616 | tf_op jit(solution)/shard_map/ppermute | solution.py:514
  51.5 2.1 %collective-permute-done.24.refs_4_.refs_7_ = bf16[64,512]{1,0:T(8,128)(2,1)S(1)} collective-permute-done((bf16[64,512]{1,0:T(8,128)(2,1)S(1)}, bf16[64,512]{1,0:T(8,128)(2,1)S(1)}, u32[]{:S(2)}, u32[]{:S(2)}) %collective-permute-start.24) | collective-permute-done | bytes 65568 | tf_op jit(solution)/shard_map/ppermute | solution.py:514
  53.7 2.1 %collective-permute-done.27.refs_2_.refs_6_ = bf16[32,2048]{1,0:T(8,128)(2,1)S(1)} collective-permute-done((bf16[32,2048]{1,0:T(8,128)(2,1)S(1)}, bf16[32,2048]{1,0:T(8,128)(2,1)S(1)}, u32[]{:S(2)}, u32[]{:S(2)}) %collective-permute-start.27) | collective-permute-done | bytes 131104 | tf_op jit(solution)/shard_map/ppermute | solution.py:514
  56.8 0.8 %rows.1 = (bf16[128,2048]{1,0:T(8,128)(2,1)}, f32[8,128]{1,0:T(8,128)S(1)}) custom-call(bf16[48,2048]{1,0:T(8,128)(2,1)S(1)} %collective-permute-done.17.refs_0_.first_rows_ref.refs_5_, bf16[16,2048]{1,0:T(8,128)(2,1)S(1)} %collective-permute-done.25.handed_ref, bf16[32,2048]{1,0:T(8,128)(2,1)S(1)} %get-tuple-element.126.refs_0_, ...), custom_call_target="tpu_custom_call" | custom-call | flops 920000000 | tf_op jit(solution)/shard_map/rows/pallas_call | solution.py:595
  57.8 1.0 %finish.1 = (f32[256,512]{1,0:T(8,128)}, f32[1,256]{1,0:T(1,128)}) custom-call(f32[256,512]{1,0:T(8,128)S(1)} %get-tuple-element.132.own_ref, bf16[128,512]{1,0:T(8,128)(2,1)S(1)} %collective-permute-done.29.first_ref, bf16[128,512]{1,0:T(8,128)(2,1)S(1)} %collective-permute-done.30.second_ref, f32[256,512]{1,0:T(8,128)S(1)} %get-tuple-element.135.weight_ref, ...), custom_call_target="tpu_custom_call" | custom-call | tf_op jit(solution)/shard_map/finish/pallas_call | solution.py:606
  (62 shorter events, 7.7 us)
Async XLA Ops:
  0.6 4.5 %copy-start = (bf16[1,2048,512]{2,1,0:T(8,128)(2,1)S(1)}, bf16[1,2048,512]{2,1,0:T(8,128)(2,1)}, u32[]{:S(2)}) copy-start(bf16[1,2048,512]{2,1,0:T(8,128)(2,1)} %param.11) | copy-start | bytes 6291460
  2.0 6.8 %collective-permute-start = (bf16[16,4608]{1,0:T(8,128)(2,1)S(1)}, bf16[16,4608]{1,0:T(8,128)(2,1)S(1)}, u32[]{:S(2)}, u32[]{:S(2)}) collective-permute-start(bf16[16,4608]{1,0:T(8,128)(2,1)S(1)} %get-tuple-element.73), channel_id=1, source_target_pairs={{0,4},{4,0},{8,12},{12,8},{16,20},{20,16},{24,28},{28,24},{1,5},{5... | collective-permute-start | bytes 442376 | tf_op jit(solution)/shard_map/ppermute | solution.py:514
  2.5 7.7 %collective-permute-start.1 = (bf16[16,4608]{1,0:T(8,128)(2,1)S(1)}, bf16[16,4608]{1,0:T(8,128)(2,1)S(1)}, u32[]{:S(2)}, u32[]{:S(2)}) collective-permute-start(bf16[16,4608]{1,0:T(8,128)(2,1)S(1)} %get-tuple-element.74), channel_id=1, source_target_pairs={{0,8},{4,12},{8,0},{12,4},{16,24},{20,28},{24,16},{28,20},{1,9},{5... | collective-permute-start | bytes 442376 | tf_op jit(solution)/shard_map/ppermute | solution.py:514
  5.1 7.3 %collective-permute-start.2 = (bf16[16,4608]{1,0:T(8,128)(2,1)S(1)}, bf16[16,4608]{1,0:T(8,128)(2,1)S(1)}, u32[]{:S(2)}, u32[]{:S(2)}) collective-permute-start(bf16[16,4608]{1,0:T(8,128)(2,1)S(1)} %get-tuple-element.75), channel_id=1, source_target_pairs={{0,12},{4,8},{8,4},{12,0},{16,28},{20,24},{24,20},{28,16},{1,13},{... | collective-permute-start | bytes 442376 | tf_op jit(solution)/shard_map/ppermute | solution.py:514
  6.9 11.9 %collective-permute-start.4 = (bf16[80,2048]{1,0:T(8,128)(2,1)S(1)}, bf16[80,2048]{1,0:T(8,128)(2,1)S(1)}, u32[]{:S(2)}, u32[]{:S(2)}) collective-permute-start(bf16[80,2048]{1,0:T(8,128)(2,1)S(1)} %get-tuple-element.82), channel_id=1, source_target_pairs={{0,16},{4,20},{8,24},{12,28},{16,0},{20,4},{24,8},{28,12},{1,17},{... | collective-permute-start | bytes 983048 | tf_op jit(solution)/shard_map/ppermute | solution.py:514
  8.7 4.8 %collective-permute-start.5 = (bf16[16,4608]{1,0:T(8,128)(2,1)S(1)}, bf16[16,4608]{1,0:T(8,128)(2,1)S(1)}, u32[]{:S(2)}, u32[]{:S(2)}) collective-permute-start(bf16[16,4608]{1,0:T(8,128)(2,1)S(1)} %get-tuple-element.84), channel_id=1, source_target_pairs={{0,4},{4,0},{8,12},{12,8},{16,20},{20,16},{24,28},{28,24},{1,5},{5... | collective-permute-start | bytes 442376 | tf_op jit(solution)/shard_map/ppermute | solution.py:514
  8.8 7.3 %collective-permute-start.6 = (bf16[16,4608]{1,0:T(8,128)(2,1)S(1)}, bf16[16,4608]{1,0:T(8,128)(2,1)S(1)}, u32[]{:S(2)}, u32[]{:S(2)}) collective-permute-start(bf16[16,4608]{1,0:T(8,128)(2,1)S(1)} %get-tuple-element.85), channel_id=1, source_target_pairs={{0,8},{4,12},{8,0},{12,4},{16,24},{20,28},{24,16},{28,20},{1,9},{5... | collective-permute-start | bytes 442376 | tf_op jit(solution)/shard_map/ppermute | solution.py:514
  10.3 8.5 %collective-permute-start.7 = (bf16[16,4608]{1,0:T(8,128)(2,1)S(1)}, bf16[16,4608]{1,0:T(8,128)(2,1)S(1)}, u32[]{:S(2)}, u32[]{:S(2)}) collective-permute-start(bf16[16,4608]{1,0:T(8,128)(2,1)S(1)} %get-tuple-element.86), channel_id=1, source_target_pairs={{0,12},{4,8},{8,4},{12,0},{16,28},{20,24},{24,20},{28,16},{1,13},{... | collective-permute-start | bytes 442376 | tf_op jit(solution)/shard_map/ppermute | solution.py:514
  12.8 7.7 %collective-permute-start.3 = (bf16[32,2048]{1,0:T(8,128)(2,1)S(1)}, bf16[32,2048]{1,0:T(8,128)(2,1)S(1)}, u32[]{:S(2)}, u32[]{:S(2)}) collective-permute-start(bf16[32,2048]{1,0:T(8,128)(2,1)S(1)} %get-tuple-element.81.refs_7_.refs_6_), channel_id=1, source_target_pairs={{3,2},{7,6},{11,10},{15,14},{19,18},{23,22},{27,26},{31,30}} | collective-permute-start | bytes 393224 | tf_op jit(solution)/shard_map/ppermute | solution.py:543
  13.5 7.7 %collective-permute-start.11 = (bf16[32,2048]{1,0:T(8,128)(2,1)S(1)}, bf16[32,2048]{1,0:T(8,128)(2,1)S(1)}, u32[]{:S(2)}, u32[]{:S(2)}) collective-permute-start(bf16[32,2048]{1,0:T(8,128)(2,1)S(1)} %get-tuple-element.88.refs_5_.refs_7_), channel_id=1, source_target_pairs={{3,2},{7,6},{11,10},{15,14},{19,18},{23,22},{27,26},{31,30}} | collective-permute-start | bytes 393224 | tf_op jit(solution)/shard_map/ppermute | solution.py:543
  19.1 2.8 %collective-permute-start.9 = (bf16[32,2048]{1,0:T(8,128)(2,1)S(1)}, bf16[32,2048]{1,0:T(8,128)(2,1)S(1)}, u32[]{:S(2)}, u32[]{:S(2)}) collective-permute-start(bf16[32,2048]{1,0:T(8,128)(2,1)S(1)} %get-tuple-element.93.refs_7_.refs_6_), channel_id=1, source_target_pairs={{3,2},{7,6},{11,10},{15,14},{19,18},{23,22},{27,26},{31,30}} | collective-permute-start | bytes 393224 | tf_op jit(solution)/shard_map/ppermute | solution.py:543
  19.8 2.8 %collective-permute-start.10 = (bf16[32,2048]{1,0:T(8,128)(2,1)S(1)}, bf16[32,2048]{1,0:T(8,128)(2,1)S(1)}, u32[]{:S(2)}, u32[]{:S(2)}) collective-permute-start(bf16[32,2048]{1,0:T(8,128)(2,1)S(1)} %get-tuple-element.94.refs_6_.refs_7_), channel_id=1, source_target_pairs={{3,2},{7,6},{11,10},{15,14},{19,18},{23,22},{27,26},{31,30}} | collective-permute-start | bytes 393224 | tf_op jit(solution)/shard_map/ppermute | solution.py:543
  20.5 5.6 %collective-permute-start.8 = (bf16[32,2048]{1,0:T(8,128)(2,1)S(1)}, bf16[32,2048]{1,0:T(8,128)(2,1)S(1)}, u32[]{:S(2)}, u32[]{:S(2)}) collective-permute-start(bf16[32,2048]{1,0:T(8,128)(2,1)S(1)} %get-tuple-element.95.refs_7_.refs_8_), channel_id=1, source_target_pairs={{2,1},{6,5},{10,9},{14,13},{18,17},{22,21},{26,25},{30,29}} | collective-permute-start | bytes 393224 | tf_op jit(solution)/shard_map/ppermute | solution.py:543
  21.2 6.2 %collective-permute-start.13 = (bf16[32,2048]{1,0:T(8,128)(2,1)S(1)}, bf16[32,2048]{1,0:T(8,128)(2,1)S(1)}, u32[]{:S(2)}, u32[]{:S(2)}) collective-permute-start(bf16[32,2048]{1,0:T(8,128)(2,1)S(1)} %get-tuple-element.96.refs_6_.refs_9_), channel_id=1, source_target_pairs={{2,1},{6,5},{10,9},{14,13},{18,17},{22,21},{26,25},{30,29}} | collective-permute-start | bytes 393224 | tf_op jit(solution)/shard_map/ppermute | solution.py:543
  21.9 6.8 %collective-permute-start.15 = (bf16[32,2048]{1,0:T(8,128)(2,1)S(1)}, bf16[32,2048]{1,0:T(8,128)(2,1)S(1)}, u32[]{:S(2)}, u32[]{:S(2)}) collective-permute-start(bf16[32,2048]{1,0:T(8,128)(2,1)S(1)} %get-tuple-element.97.refs_7_.refs_8_), channel_id=1, source_target_pairs={{2,1},{6,5},{10,9},{14,13},{18,17},{22,21},{26,25},{30,29}} | collective-permute-start | bytes 393224 | tf_op jit(solution)/shard_map/ppermute | solution.py:543
  22.7 7.4 %collective-permute-start.16 = (bf16[32,2048]{1,0:T(8,128)(2,1)S(1)}, bf16[32,2048]{1,0:T(8,128)(2,1)S(1)}, u32[]{:S(2)}, u32[]{:S(2)}) collective-permute-start(bf16[32,2048]{1,0:T(8,128)(2,1)S(1)} %get-tuple-element.98.refs_6_.after_ref.refs_0_.refs_9_), channel_id=1, source_target_pairs={{2,1},{6,5},{10,9},{14,13},{18,17},{22,21},{26,25},{30,29}} | collective-permute-start | bytes 393224 | tf_op jit(solution)/shard_map/ppermute | solution.py:543
  23.5 7.9 %collective-permute-start.20 = (bf16[128,512]{1,0:T(8,128)(2,1)S(1)}, bf16[128,512]{1,0:T(8,128)(2,1)S(1)}, u32[]{:S(2)}, u32[]{:S(2)}) collective-permute-start(bf16[128,512]{1,0:T(8,128)(2,1)S(1)} %columns6.1), channel_id=1, source_target_pairs={{0,24},{4,28},{8,16},{12,20},{16,8},{20,12},{24,0},{28,4},{1,25},{... | collective-permute-start | bytes 393224 | tf_op jit(solution)/shard_map/ppermute | solution.py:514
  26.1 10.9 %collective-permute-start.12 = (bf16[32,2048]{1,0:T(8,128)(2,1)S(1)}, bf16[32,2048]{1,0:T(8,128)(2,1)S(1)}, u32[]{:S(2)}, u32[]{:S(2)}) collective-permute-start(bf16[32,2048]{1,0:T(8,128)(2,1)S(1)} %get-tuple-element.99.refs_7_.refs_10_), channel_id=1, source_target_pairs={{1,0},{5,4},{9,8},{13,12},{17,16},{21,20},{25,24},{29,28}} | collective-permute-start | bytes 393224 | tf_op jit(solution)/shard_map/ppermute | solution.py:543
  27.4 12.4 %collective-permute-start.14 = (bf16[32,2048]{1,0:T(8,128)(2,1)S(1)}, bf16[32,2048]{1,0:T(8,128)(2,1)S(1)}, u32[]{:S(2)}, u32[]{:S(2)}) collective-permute-start(bf16[32,2048]{1,0:T(8,128)(2,1)S(1)} %get-tuple-element.100.refs_6_.refs_11_), channel_id=1, source_target_pairs={{1,0},{5,4},{9,8},{13,12},{17,16},{21,20},{25,24},{29,28}} | collective-permute-start | bytes 393224 | tf_op jit(solution)/shard_map/ppermute | solution.py:543
  28.8 15.0 %collective-permute-start.18 = (bf16[32,2048]{1,0:T(8,128)(2,1)S(1)}, bf16[32,2048]{1,0:T(8,128)(2,1)S(1)}, u32[]{:S(2)}, u32[]{:S(2)}) collective-permute-start(bf16[32,2048]{1,0:T(8,128)(2,1)S(1)} %get-tuple-element.107.refs_7_.refs_10_), channel_id=1, source_target_pairs={{1,0},{5,4},{9,8},{13,12},{17,16},{21,20},{25,24},{29,28}} | collective-permute-start | bytes 393224 | tf_op jit(solution)/shard_map/ppermute | solution.py:543
  30.1 15.3 %collective-permute-start.19 = (bf16[32,2048]{1,0:T(8,128)(2,1)S(1)}, bf16[32,2048]{1,0:T(8,128)(2,1)S(1)}, u32[]{:S(2)}, u32[]{:S(2)}) collective-permute-start(bf16[32,2048]{1,0:T(8,128)(2,1)S(1)} %get-tuple-element.108.refs_12_.refs_0_.refs_11_), channel_id=1, source_target_pairs={{1,0},{5,4},{9,8},{13,12},{17,16},{21,20},{25,24},{29,28}} | collective-permute-start | bytes 393224 | tf_op jit(solution)/shard_map/ppermute | solution.py:543
  31.5 14.0 %collective-permute-start.21 = (bf16[128,512]{1,0:T(8,128)(2,1)S(1)}, bf16[128,512]{1,0:T(8,128)(2,1)S(1)}, u32[]{:S(2)}, u32[]{:S(2)}) collective-permute-start(bf16[128,512]{1,0:T(8,128)(2,1)S(1)} %columns2.1), channel_id=1, source_target_pairs={{0,8},{4,12},{8,0},{12,4},{16,24},{20,28},{24,16},{28,20},{1,9},{5... | collective-permute-start | bytes 393224 | tf_op jit(solution)/shard_map/ppermute | solution.py:514
  40.6 9.2 %collective-permute-start.17 = (bf16[48,2048]{1,0:T(8,128)(2,1)S(1)}, bf16[48,2048]{1,0:T(8,128)(2,1)S(1)}, u32[]{:S(2)}, u32[]{:S(2)}) collective-permute-start(bf16[48,2048]{1,0:T(8,128)(2,1)S(1)} %get-tuple-element.111), channel_id=1, source_target_pairs={{0,8},{4,12},{8,0},{12,4},{16,24},{20,28},{24,16},{28,20},{1,9},{5... | collective-permute-start | bytes 589832 | tf_op jit(solution)/shard_map/ppermute | solution.py:514
  42.2 7.7 %collective-permute-start.22 = (bf16[192,512]{1,0:T(8,128)(2,1)S(1)}, bf16[192,512]{1,0:T(8,128)(2,1)S(1)}, u32[]{:S(2)}, u32[]{:S(2)}) collective-permute-start(bf16[192,512]{1,0:T(8,128)(2,1)S(1)} %columns4.1), channel_id=1, source_target_pairs={{0,16},{4,20},{8,24},{12,28},{16,0},{20,4},{24,8},{28,12},{1,17},{... | collective-permute-start | bytes 589832 | tf_op jit(solution)/shard_map/ppermute | solution.py:514
  46.3 7.2 %collective-permute-start.23 = (bf16[128,512]{1,0:T(8,128)(2,1)S(1)}, bf16[128,512]{1,0:T(8,128)(2,1)S(1)}, u32[]{:S(2)}, u32[]{:S(2)}) collective-permute-start(bf16[128,512]{1,0:T(8,128)(2,1)S(1)} %get-tuple-element.124.refs_4_), channel_id=1, source_target_pairs={{0,24},{4,28},{8,16},{12,20},{16,8},{20,12},{24,0},{28,4},{1,25},{... | collective-permute-start | bytes 393224 | tf_op jit(solution)/shard_map/ppermute | solution.py:514
  48.8 4.7 %collective-permute-start.24 = (bf16[64,512]{1,0:T(8,128)(2,1)S(1)}, bf16[64,512]{1,0:T(8,128)(2,1)S(1)}, u32[]{:S(2)}, u32[]{:S(2)}) collective-permute-start(bf16[64,512]{1,0:T(8,128)(2,1)S(1)} %get-tuple-element.123.refs_1_), channel_id=1, source_target_pairs={{0,16},{4,20},{8,24},{12,28},{16,0},{20,4},{24,8},{28,12},{1,17},{... | collective-permute-start | bytes 196616 | tf_op jit(solution)/shard_map/ppermute | solution.py:514
  49.3 6.4 %collective-permute-start.27 = (bf16[32,2048]{1,0:T(8,128)(2,1)S(1)}, bf16[32,2048]{1,0:T(8,128)(2,1)S(1)}, u32[]{:S(2)}, u32[]{:S(2)}) collective-permute-start(bf16[32,2048]{1,0:T(8,128)(2,1)S(1)} %get-tuple-element.128), channel_id=1, source_target_pairs={{0,8},{4,12},{8,0},{12,4},{16,24},{20,28},{24,16},{28,20},{1,9},{5... | collective-permute-start | bytes 393224 | tf_op jit(solution)/shard_map/ppermute | solution.py:514
  49.9 6.9 %collective-permute-start.26 = (bf16[32,2048]{1,0:T(8,128)(2,1)S(1)}, bf16[32,2048]{1,0:T(8,128)(2,1)S(1)}, u32[]{:S(2)}, u32[]{:S(2)}) collective-permute-start(bf16[32,2048]{1,0:T(8,128)(2,1)S(1)} %get-tuple-element.127), channel_id=1, source_target_pairs={{0,4},{4,0},{8,12},{12,8},{16,20},{20,16},{24,28},{28,24},{1,5},{5... | collective-permute-start | bytes 393224 | tf_op jit(solution)/shard_map/ppermute | solution.py:514
  49.9 6.9 %collective-permute-start.28 = (bf16[16,2048]{1,0:T(8,128)(2,1)S(1)}, bf16[16,2048]{1,0:T(8,128)(2,1)S(1)}, u32[]{:S(2)}, u32[]{:S(2)}) collective-permute-start(bf16[16,2048]{1,0:T(8,128)(2,1)S(1)} %get-tuple-element.129), channel_id=1, source_target_pairs={{0,12},{4,8},{8,4},{12,0},{16,28},{20,24},{24,20},{28,16},{1,13},{... | collective-permute-start | bytes 196616 | tf_op jit(solution)/shard_map/ppermute | solution.py:514
  53.6 3.2 %collective-permute-start.25 = (bf16[16,2048]{1,0:T(8,128)(2,1)S(1)}, bf16[16,2048]{1,0:T(8,128)(2,1)S(1)}, u32[]{:S(2)}, u32[]{:S(2)}) collective-permute-start(bf16[16,2048]{1,0:T(8,128)(2,1)S(1)} %get-tuple-element.125), channel_id=1, source_target_pairs={{0,4},{4,0},{8,12},{12,8},{16,20},{20,16},{24,28},{28,24},{1,5},{5... | collective-permute-start | bytes 196616 | tf_op jit(solution)/shard_map/ppermute | solution.py:514
  56.2 1.4 %collective-permute-start.29 = (bf16[128,512]{1,0:T(8,128)(2,1)S(1)}, bf16[128,512]{1,0:T(8,128)(2,1)S(1)}, u32[]{:S(2)}, u32[]{:S(2)}) collective-permute-start(bf16[128,512]{1,0:T(8,128)(2,1)S(1)} %get-tuple-element.133), channel_id=1, source_target_pairs={{0,4},{4,0},{8,12},{12,8},{16,20},{20,16},{24,28},{28,24},{1,5},{5... | collective-permute-start | bytes 393224 | tf_op jit(solution)/shard_map/ppermute | solution.py:514
  56.3 1.5 %collective-permute-start.30 = (bf16[128,512]{1,0:T(8,128)(2,1)S(1)}, bf16[128,512]{1,0:T(8,128)(2,1)S(1)}, u32[]{:S(2)}, u32[]{:S(2)}) collective-permute-start(bf16[128,512]{1,0:T(8,128)(2,1)S(1)} %get-tuple-element.134), channel_id=1, source_target_pairs={{0,4},{4,0},{8,12},{12,8},{16,20},{20,16},{24,28},{28,24},{1,5},{5... | collective-permute-start | bytes 393224 | tf_op jit(solution)/shard_map/ppermute | solution.py:514
  (1 other events, 4.5 us)

commit v15 on v14

--- a/solution.py
+++ b/solution.py
@@ -124,7 +124,7 @@
 def unit_math(rows, grads, probs_ref, x_ref, inv_ref, turned_ref, gain_ref, scaled_ref, store, value_ref):
     kv_width, model_width = turned_ref.shape
     heads = model_width // kv_width
-    chunk = min(1024, model_width)
+    chunk = min(512, model_width)
     inv = inv_ref[rows, :1]
     values = []
     for c in range(kv_width // HEAD_FEATURES):
@@ -440,9 +440,9 @@
     return pl.ds(pl.multiple_of(pair * width, width), width)
 
 
-def partial_kernel(shares, first, *refs):
-    columns, values, (own_out_ref, *other_refs) = refs[:4], refs[4:-3], refs[-3:]
-    kv_width = own_out_ref.shape[1]
+def partial_kernel(shares, first, for_other, *refs):
+    columns, values, out_ref = refs[:4], refs[4:9], refs[-1]
+    kv_width = out_ref.shape[1]
     parts = []
     for ref in values:
         beside = ref.shape[1] > kv_width
@@ -451,18 +451,26 @@
     parts.insert(len(parts) - 2, columns[2][2 * BLOCK :, :])
     value = jnp.concatenate(parts, axis=0)
     mine = lax.rem(place()[2], 2)
-
-    def share(core):
-        at = pl.ds(pl.multiple_of(core * shares, shares), shares)
-        rows = jnp.concatenate([ref[: 2 * BLOCK, at] for ref in columns], axis=0)
-        return lax.dot_general(
-            rows, value, (((0,), (0,)), ((), ())), preferred_element_type=jnp.float32
-        )
-
-    other = share(1 - mine).astype(jnp.bfloat16)
-    for part, ref in enumerate(other_refs):
-        ref[...] = other[part * (shares // 2) : (part + 1) * (shares // 2)]
-    own_out_ref[...] = share(mine)
+    core = 1 - mine if for_other else mine
+    at = pl.ds(pl.multiple_of(core * shares, shares), shares)
+    rows = jnp.concatenate([ref[: 2 * BLOCK, at] for ref in columns], axis=0)
+    out_ref[...] = lax.dot_general(
+        rows, value, (((0,), (0,)), ((), ())), preferred_element_type=jnp.float32
+    ).astype(out_ref.dtype)
+
+
+def partial_sums(shares, piece, for_other, columns, values, after=()):
+    kv_width = values[0].shape[1]
+    return pl.pallas_call(
+        functools.partial(partial_kernel, shares, piece, for_other),
+        out_shape=jax.ShapeDtypeStruct(
+            (shares, kv_width), jnp.bfloat16 if for_other else jnp.float32
+        ),
+        in_specs=[VMEM] * 9 + [ANY] * len(after),
+        out_specs=VMEM,
+        name="partial_other" if for_other else "partial_own",
+        **params(0.0 if for_other else 0.5),
+    )(*[columns[k] for k in (0, 2, 4, 6)], *values, *after)
 
 
 def diagonal(size):
@@ -490,10 +498,9 @@
 
 
 def finish_kernel(
-    own_ref, first_ref, second_ref, weight_ref, gain_ref, after_ref, out_ref, gain_out_ref
+    own_ref, other_ref, weight_ref, gain_ref, after_ref, out_ref, gain_out_ref
 ):
-    other = jnp.concatenate([first_ref[...], second_ref[...]], axis=0)
-    total = own_ref[...] + other.astype(jnp.float32)
+    total = own_ref[...] + other_ref[...].astype(jnp.float32)
     out_ref[...] = total * gain_ref[:, :1]
     sums = jnp.sum(total * weight_ref[...], axis=1, keepdims=True)
     gain_out_ref[...] = jnp.sum(
@@ -579,19 +586,12 @@
     own_value, own_values, *rows = done[3]
     rows = [rows[0]] + [swap(rows[k], k) for k in range(1, half)]
     far_values, across_value = swap(own_values, 6), swap(own_value, 4)
-    columns[0], handed = columns_for(0, blocks, [own_value, columns[4], far_values, across_value], [first_rows])
+    columns[0], handed = columns_for(0, blocks, [own_value, columns[4], across_value], [first_rows])
     handed = swap(handed, 1)
     values = [own_values, first_rows, rows[2], across_value, far_values]
-    own, *other = pl.pallas_call(
-        functools.partial(partial_kernel, shares, piece),
-        out_shape=(jax.ShapeDtypeStruct((shares, kv_width), jnp.float32),)
-        + (jax.ShapeDtypeStruct((shares // 2, kv_width), bf16),) * 2,
-        in_specs=[VMEM] * 9,
-        out_specs=(VMEM,) * 3,
-        name="weight_partial",
-        **params(0.0),
-    )(*[columns[k] for k in (0, 2, 4, 6)], *values)
-    other = [swap(part, 1) for part in other]
+    other = partial_sums(shares, piece, True, columns, values)
+    own = partial_sums(shares, piece, False, columns, values, [other])
+    other = swap(other, 1)
     input_grad, token = pl.pallas_call(
         functools.partial(rows_kernel, half),
         out_shape=(
@@ -601,7 +601,7 @@
         in_specs=[VMEM] * (2 + half),
         out_specs=(VMEM, VMEM),
         name="rows",
-        **params(0.8),
+        **params(3.0),
     )(first_rows, handed, *rows)
     weight_grad, gain_grad = pl.pallas_call(
         finish_kernel,
@@ -609,11 +609,11 @@
             jax.ShapeDtypeStruct((shares, kv_width), jnp.float32),
             jax.ShapeDtypeStruct((1, shares), jnp.float32),
         ),
-        in_specs=[VMEM] * 5 + [ANY],
+        in_specs=[VMEM] * 4 + [ANY],
         out_specs=(VMEM, VMEM),
         name="finish",
         **params(0.0),
-    )(own, *other, own_weight, own_gain, token)
+    )(own, other, own_weight, own_gain, token)
     return input_grad[None], weight_grad[None], gain_grad
 
 

time: 59.1 us -> 59.6 us (level)
  waiting for transfers between devices: 18.6 us -> 19.3 us
    ppermute x19 -> x18, waiting for transfers between devices: 10.8 us -> 11.5 us  [swap(): return lax.ppermute(array, 'dp', [(i, i ^ k) for i in range(replicas)])]
    ppermute x19 -> x18, starting transfers between devices: 18.9 us -> 18.5 us  [swap(): return lax.ppermute(array, 'dp', [(i, i ^ k) for i in range(replicas)])]
  transfers between devices with their start and end apart: 31 -> 30, of which waited for: 9 -> 9; matrix products, arithmetic and copies ran while one was open for 0% -> 0% of each run, Pallas kernels for 13% -> 13%
where the time goes in v15:
time: 59.6 us; the launch traced here: 59.2 us
  starting transfers between devices  29 us (49%)
  waiting for transfers between devices  19.3 us (32%)
  Pallas kernels  9.89 us (17%)
  between operations  1.06 us (2%)
    ppermute x18, starting transfers between devices, swap(): return lax.ppermute(array, 'dp', [(i, i ^ k) for i in range(replicas)])  18.5 us
    ppermute x18, waiting for transfers between devices, swap(): return lax.ppermute(array, 'dp', [(i, i ^ k) for i in range(replicas)])  11.5 us
    ppermute x12, starting transfers between devices, direct(): lax.ppermute(unit[-1][0], 'section', hop)  10.5 us
    ppermute x12, waiting for transfers between devices, direct(): lax.ppermute(unit[-1][0], 'section', hop)  7.8 us
    pallas_call x16, Pallas kernels, tick_step(): pl.pallas_call(functools.partial(tick_kernel, tick, EARLY if low else LAT...  3.43 us
    pallas_call x2, Pallas kernels, pack(): pl.pallas_call(functools.partial(pack_kernel, block, half, piece), out_sh...  3.06 us
  transfers between devices with their start and end apart: 30, of which 9 were waited for; matrix products, arithmetic and copies ran while one was open for 0% of the time, Pallas kernels for 13%

profile of v15, /device:TPU:0, one launch (start us, length us, event | category | flops | bytes accessed | tf_op | source)
XLA Modules:
  0.0 59.2 jit_solution(15027185998681319219)
XLA Ops:
  0.7 1.4 %pack.2 = (bf16[16,4608]{1,0:T(8,128)(2,1)S(1)}, bf16[16,4608]{1,0:T(8,128)(2,1)S(1)}, bf16[16,4608]{1,0:T(8,128)(2,1)S(1)}, bf16[16,4608]{1,0:T(8,128)(2,1)S(1)}, bf16[80,2048]{1,0:T(8,128)(2,1)S(1)}) custom-call(bf16[128,2048]{1,0:T(8,128)(2,1)} %bitcast.8, bf16[128,512]{1,0:T(8,128)(2,1)} %bitcast.13, bf16[128,2048]{1,0:T(8,128)(2,1)} %bitcast.10, ...), custom_call_target="tpu_custom_call" | custom-call | flops 1380000000 | tf_op jit(solution)/shard_map/pack/pallas_call | solution.py:383
  2.5 2.6 %collective-permute-start.1 = (bf16[16,4608]{1,0:T(8,128)(2,1)S(1)}, bf16[16,4608]{1,0:T(8,128)(2,1)S(1)}, u32[]{:S(2)}, u32[]{:S(2)}) collective-permute-start(bf16[16,4608]{1,0:T(8,128)(2,1)S(1)} %get-tuple-element.71), channel_id=1, source_target_pairs={{0,8},{4,12},{8,0},{12,4},{16,24},{20,28},{24,16},{28,20},{1,9},{5... | collective-permute-start | bytes 442376 | tf_op jit(solution)/shard_map/ppermute | solution.py:521
  5.2 1.7 %pack.3 = (f32[1,2048]{1,0:T(1,128)S(1)}, bf16[512,2048]{1,0:T(8,128)(2,1)S(1)}, bf16[16,4608]{1,0:T(8,128)(2,1)S(1)}, bf16[16,4608]{1,0:T(8,128)(2,1)S(1)}, bf1...) custom-call(bf16[128,2048]{1,0:T(8,128)(2,1)} %bitcast.9, ...), custom_call_target="tpu_custom_call" | custom-call | flops 1380000000 | tf_op jit(solution)/shard_map/pack/pallas_call | solution.py:383
  6.9 1.8 %collective-permute-start.4 = (bf16[80,2048]{1,0:T(8,128)(2,1)S(1)}, bf16[80,2048]{1,0:T(8,128)(2,1)S(1)}, u32[]{:S(2)}, u32[]{:S(2)}) collective-permute-start(bf16[80,2048]{1,0:T(8,128)(2,1)S(1)} %get-tuple-element.79), channel_id=1, source_target_pairs={{0,16},{4,20},{8,24},{12,28},{16,0},{20,4},{24,8},{28,12},{1,17},{... | collective-permute-start | bytes 983048 | tf_op jit(solution)/shard_map/ppermute | solution.py:521
  8.8 1.5 %collective-permute-start.6 = (bf16[16,4608]{1,0:T(8,128)(2,1)S(1)}, bf16[16,4608]{1,0:T(8,128)(2,1)S(1)}, u32[]{:S(2)}, u32[]{:S(2)}) collective-permute-start(bf16[16,4608]{1,0:T(8,128)(2,1)S(1)} %get-tuple-element.82), channel_id=1, source_target_pairs={{0,8},{4,12},{8,0},{12,4},{16,24},{20,28},{24,16},{28,20},{1,9},{5... | collective-permute-start | bytes 442376 | tf_op jit(solution)/shard_map/ppermute | solution.py:521
  10.6 1.9 %collective-permute-done.2.refs_3_ = bf16[16,4608]{1,0:T(8,128)(2,1)S(1)} collective-permute-done((bf16[16,4608]{1,0:T(8,128)(2,1)S(1)}, bf16[16,4608]{1,0:T(8,128)(2,1)S(1)}, u32[]{:S(2)}, u32[]{:S(2)}) %collective-permute-start.2) | collective-permute-done | bytes 147488 | tf_op jit(solution)/shard_map/ppermute | solution.py:521
  12.8 0.7 %collective-permute-start.3 = (bf16[32,2048]{1,0:T(8,128)(2,1)S(1)}, bf16[32,2048]{1,0:T(8,128)(2,1)S(1)}, u32[]{:S(2)}, u32[]{:S(2)}) collective-permute-start(bf16[32,2048]{1,0:T(8,128)(2,1)S(1)} %get-tuple-element.78.refs_7_.refs_6_), channel_id=1, source_target_pairs={{3,2},{7,6},{11,10},{15,14},{19,18},{23,22},{27,26},{31,30}} | collective-permute-start | bytes 393224 | tf_op jit(solution)/shard_map/ppermute | solution.py:550
  14.2 1.9 %collective-permute-done.6.refs_2_ = bf16[16,4608]{1,0:T(8,128)(2,1)S(1)} collective-permute-done((bf16[16,4608]{1,0:T(8,128)(2,1)S(1)}, bf16[16,4608]{1,0:T(8,128)(2,1)S(1)}, u32[]{:S(2)}, u32[]{:S(2)}) %collective-permute-start.6) | collective-permute-done | bytes 147488 | tf_op jit(solution)/shard_map/ppermute | solution.py:521
  16.1 2.6 %collective-permute-done.7.refs_3_ = bf16[16,4608]{1,0:T(8,128)(2,1)S(1)} collective-permute-done((bf16[16,4608]{1,0:T(8,128)(2,1)S(1)}, bf16[16,4608]{1,0:T(8,128)(2,1)S(1)}, u32[]{:S(2)}, u32[]{:S(2)}) %collective-permute-start.7) | collective-permute-done | bytes 147488 | tf_op jit(solution)/shard_map/ppermute | solution.py:521
  19.8 0.7 %collective-permute-start.10 = (bf16[32,2048]{1,0:T(8,128)(2,1)S(1)}, bf16[32,2048]{1,0:T(8,128)(2,1)S(1)}, u32[]{:S(2)}, u32[]{:S(2)}) collective-permute-start(bf16[32,2048]{1,0:T(8,128)(2,1)S(1)} %get-tuple-element.91.refs_6_.refs_7_), channel_id=1, source_target_pairs={{3,2},{7,6},{11,10},{15,14},{19,18},{23,22},{27,26},{31,30}} | collective-permute-start | bytes 393224 | tf_op jit(solution)/shard_map/ppermute | solution.py:550
  21.2 0.7 %collective-permute-start.13 = (bf16[32,2048]{1,0:T(8,128)(2,1)S(1)}, bf16[32,2048]{1,0:T(8,128)(2,1)S(1)}, u32[]{:S(2)}, u32[]{:S(2)}) collective-permute-start(bf16[32,2048]{1,0:T(8,128)(2,1)S(1)} %get-tuple-element.93.refs_6_.refs_9_), channel_id=1, source_target_pairs={{2,1},{6,5},{10,9},{14,13},{18,17},{22,21},{26,25},{30,29}} | collective-permute-start | bytes 393224 | tf_op jit(solution)/shard_map/ppermute | solution.py:550
  23.5 2.6 %collective-permute-start.20 = (bf16[128,512]{1,0:T(8,128)(2,1)S(1)}, bf16[128,512]{1,0:T(8,128)(2,1)S(1)}, u32[]{:S(2)}, u32[]{:S(2)}) collective-permute-start(bf16[128,512]{1,0:T(8,128)(2,1)S(1)} %columns6.1), channel_id=1, source_target_pairs={{0,24},{4,28},{8,16},{12,20},{16,8},{20,12},{24,0},{28,4},{1,25},{... | collective-permute-start | bytes 393224 | tf_op jit(solution)/shard_map/ppermute | solution.py:521
  26.1 1.3 %collective-permute-start.12 = (bf16[32,2048]{1,0:T(8,128)(2,1)S(1)}, bf16[32,2048]{1,0:T(8,128)(2,1)S(1)}, u32[]{:S(2)}, u32[]{:S(2)}) collective-permute-start(bf16[32,2048]{1,0:T(8,128)(2,1)S(1)} %get-tuple-element.96.refs_7_.refs_10_), channel_id=1, source_target_pairs={{1,0},{5,4},{9,8},{13,12},{17,16},{21,20},{25,24},{29,28}} | collective-permute-start | bytes 393224 | tf_op jit(solution)/shard_map/ppermute | solution.py:550
  27.4 1.3 %collective-permute-start.14 = (bf16[32,2048]{1,0:T(8,128)(2,1)S(1)}, bf16[32,2048]{1,0:T(8,128)(2,1)S(1)}, u32[]{:S(2)}, u32[]{:S(2)}) collective-permute-start(bf16[32,2048]{1,0:T(8,128)(2,1)S(1)} %get-tuple-element.97.refs_6_.refs_11_), channel_id=1, source_target_pairs={{1,0},{5,4},{9,8},{13,12},{17,16},{21,20},{25,24},{29,28}} | collective-permute-start | bytes 393224 | tf_op jit(solution)/shard_map/ppermute | solution.py:550
  28.8 1.3 %collective-permute-start.18 = (bf16[32,2048]{1,0:T(8,128)(2,1)S(1)}, bf16[32,2048]{1,0:T(8,128)(2,1)S(1)}, u32[]{:S(2)}, u32[]{:S(2)}) collective-permute-start(bf16[32,2048]{1,0:T(8,128)(2,1)S(1)} %get-tuple-element.104.refs_7_.refs_10_), channel_id=1, source_target_pairs={{1,0},{5,4},{9,8},{13,12},{17,16},{21,20},{25,24},{29,28}} | collective-permute-start | bytes 393224 | tf_op jit(solution)/shard_map/ppermute | solution.py:550
  30.1 1.3 %collective-permute-start.19 = (bf16[32,2048]{1,0:T(8,128)(2,1)S(1)}, bf16[32,2048]{1,0:T(8,128)(2,1)S(1)}, u32[]{:S(2)}, u32[]{:S(2)}) collective-permute-start(bf16[32,2048]{1,0:T(8,128)(2,1)S(1)} %get-tuple-element.105.refs_12_.refs_0_.refs_11_), channel_id=1, source_target_pairs={{1,0},{5,4},{9,8},{13,12},{17,16},{21,20},{25,24},{29,28}} | collective-permute-start | bytes 393224 | tf_op jit(solution)/shard_map/ppermute | solution.py:550
  32.1 4.9 %collective-permute-done.12.refs_0_ = bf16[32,2048]{1,0:T(8,128)(2,1)S(1)} collective-permute-done((bf16[32,2048]{1,0:T(8,128)(2,1)S(1)}, bf16[32,2048]{1,0:T(8,128)(2,1)S(1)}, u32[]{:S(2)}, u32[]{:S(2)}) %collective-permute-start.12) | collective-permute-done | bytes 131104 | tf_op jit(solution)/shard_map/ppermute | solution.py:550
  37.0 0.8 %tick3_a_late.1 = (bf16[32,2048]{1,0:T(8,128)(2,1)S(1)}, bf16[32,512]{1,0:T(8,128)(2,1)S(1)}) custom-call(bf16[32,2048]{1,0:T(8,128)(2,1)S(1)} %collective-permute-done.12.refs_0_, bf16[4,32,128]{2,1,0:T(8,128)(2,1)S(1)} %get-tuple-element.73.refs_1_, f32[64,128]{1,0:T(8,128)S(1)} %get-tuple-element.74.refs_2_.refs_3_, ...), custom_call_target="tpu_custom_call" | custom-call | flops 1150000000 | tf_op jit(solution)/shard_map/tick3_a_late/pallas_call | solution.py:319
  37.8 2.0 %collective-permute-done.14.refs_1_ = bf16[32,2048]{1,0:T(8,128)(2,1)S(1)} collective-permute-done((bf16[32,2048]{1,0:T(8,128)(2,1)S(1)}, bf16[32,2048]{1,0:T(8,128)(2,1)S(1)}, u32[]{:S(2)}, u32[]{:S(2)}) %collective-permute-start.14) | collective-permute-done | bytes 131104 | tf_op jit(solution)/shard_map/ppermute | solution.py:550
  39.8 0.8 %tick3_a_early.1 = (bf16[32,2048]{1,0:T(8,128)(2,1)S(1)}, bf16[64,512]{1,0:T(8,128)(2,1)S(1)}, bf16[48,2048]{1,0:T(8,128)(2,1)S(1)}) custom-call(bf16[32,2048]{1,0:T(8,128)(2,1)S(1)} %collective-permute-done.12.refs_0_, bf16[32,2048]{1,0:T(8,128)(2,1)S(1)} %collective-permute-done.14.refs_1_, bf16[4,32,256]{2,1,0:T(8,128)(2,1)S(1)} %get-tuple-element.84.refs_2_, ...), custom_call_target="tpu_custom_call" | custom-call | flops 1150000000 | tf_op jit(solution)/shard_map/tick3_a_early/pallas_call | solution.py:319
  40.6 1.6 %collective-permute-start.17 = (bf16[48,2048]{1,0:T(8,128)(2,1)S(1)}, bf16[48,2048]{1,0:T(8,128)(2,1)S(1)}, u32[]{:S(2)}, u32[]{:S(2)}) collective-permute-start(bf16[48,2048]{1,0:T(8,128)(2,1)S(1)} %get-tuple-element.108), channel_id=1, source_target_pairs={{0,8},{4,12},{8,0},{12,4},{16,24},{20,28},{24,16},{28,20},{1,9},{5... | collective-permute-start | bytes 589832 | tf_op jit(solution)/shard_map/ppermute | solution.py:521
  42.2 1.6 %collective-permute-start.22 = (bf16[192,512]{1,0:T(8,128)(2,1)S(1)}, bf16[192,512]{1,0:T(8,128)(2,1)S(1)}, u32[]{:S(2)}, u32[]{:S(2)}) collective-permute-start(bf16[192,512]{1,0:T(8,128)(2,1)S(1)} %columns4.1), channel_id=1, source_target_pairs={{0,16},{4,20},{8,24},{12,28},{16,0},{20,4},{24,8},{28,12},{1,17},{... | collective-permute-start | bytes 589832 | tf_op jit(solution)/shard_map/ppermute | solution.py:521
  43.8 0.8 %tick3_b_late.1 = (bf16[32,2048]{1,0:T(8,128)(2,1)S(1)}, bf16[32,512]{1,0:T(8,128)(2,1)S(1)}) custom-call(bf16[32,2048]{1,0:T(8,128)(2,1)S(1)} %collective-permute-done.18.refs_0_, bf16[4,32,128]{2,1,0:T(8,128)(2,1)S(1)} %get-tuple-element.89.refs_1_, f32[64,128]{1,0:T(8,128)S(1)} %get-tuple-element.87.refs_2_.refs_3_, ...), custom_call_target="tpu_custom_call" | custom-call | flops 1150000000 | tf_op jit(solution)/shard_map/tick3_b_late/pallas_call | solution.py:319
  44.6 0.8 %collective-permute-done.19.refs_1_ = bf16[32,2048]{1,0:T(8,128)(2,1)S(1)} collective-permute-done((bf16[32,2048]{1,0:T(8,128)(2,1)S(1)}, bf16[32,2048]{1,0:T(8,128)(2,1)S(1)}, u32[]{:S(2)}, u32[]{:S(2)}) %collective-permute-start.19) | collective-permute-done | bytes 131104 | tf_op jit(solution)/shard_map/ppermute | solution.py:550
  45.4 0.9 %tick3_b_early.1 = (bf16[64,512]{1,0:T(8,128)(2,1)S(1)}, bf16[128,512]{1,0:T(8,128)(2,1)S(1)}, bf16[32,2048]{1,0:T(8,128)(2,1)S(1)}, bf16[32,2048]{1,0:T(8,128)(...) custom-call(bf16[32,2048]{1,0:T(8,128)(2,1)S(1)} %collective-permute-done.18.refs_0_, ...), custom_call_target="tpu_custom_call" | custom-call | flops 1150000000 | tf_op jit(solution)/shard_map/tick3_b_early/pallas_call | solution.py:319
  46.3 1.6 %collective-permute-start.23 = (bf16[64,512]{1,0:T(8,128)(2,1)S(1)}, bf16[64,512]{1,0:T(8,128)(2,1)S(1)}, u32[]{:S(2)}, u32[]{:S(2)}) collective-permute-start(bf16[64,512]{1,0:T(8,128)(2,1)S(1)} %get-tuple-element.120.refs_1_), channel_id=1, source_target_pairs={{0,16},{4,20},{8,24},{12,28},{16,0},{20,4},{24,8},{28,12},{1,17},{... | collective-permute-start | bytes 196616 | tf_op jit(solution)/shard_map/ppermute | solution.py:521
  47.9 1.5 %collective-permute-start.26 = (bf16[32,2048]{1,0:T(8,128)(2,1)S(1)}, bf16[32,2048]{1,0:T(8,128)(2,1)S(1)}, u32[]{:S(2)}, u32[]{:S(2)}) collective-permute-start(bf16[32,2048]{1,0:T(8,128)(2,1)S(1)} %get-tuple-element.124), channel_id=1, source_target_pairs={{0,8},{4,12},{8,0},{12,4},{16,24},{20,28},{24,16},{28,20},{1,9},{5... | collective-permute-start | bytes 393224 | tf_op jit(solution)/shard_map/ppermute | solution.py:521
  49.9 1.6 %collective-permute-start.27 = (bf16[16,2048]{1,0:T(8,128)(2,1)S(1)}, bf16[16,2048]{1,0:T(8,128)(2,1)S(1)}, u32[]{:S(2)}, u32[]{:S(2)}) collective-permute-start(bf16[16,2048]{1,0:T(8,128)(2,1)S(1)} %get-tuple-element.125), channel_id=1, source_target_pairs={{0,12},{4,8},{8,4},{12,0},{16,28},{20,24},{24,20},{28,16},{1,13},{... | collective-permute-start | bytes 196616 | tf_op jit(solution)/shard_map/ppermute | solution.py:521
  51.6 2.7 %collective-permute-done.26.refs_2_.refs_6_ = bf16[32,2048]{1,0:T(8,128)(2,1)S(1)} collective-permute-done((bf16[32,2048]{1,0:T(8,128)(2,1)S(1)}, bf16[32,2048]{1,0:T(8,128)(2,1)S(1)}, u32[]{:S(2)}, u32[]{:S(2)}) %collective-permute-start.26) | collective-permute-done | bytes 131104 | tf_op jit(solution)/shard_map/ppermute | solution.py:521
  54.3 2.0 %collective-permute-done.28.refs_8_ = bf16[128,512]{1,0:T(8,128)(2,1)S(1)} collective-permute-done((bf16[128,512]{1,0:T(8,128)(2,1)S(1)}, bf16[128,512]{1,0:T(8,128)(2,1)S(1)}, u32[]{:S(2)}, u32[]{:S(2)}) %collective-permute-start.28) | collective-permute-done | bytes 131104 | tf_op jit(solution)/shard_map/ppermute | solution.py:521
  57.1 0.8 %rows.1 = (bf16[128,2048]{1,0:T(8,128)(2,1)}, f32[8,128]{1,0:T(8,128)S(1)}) custom-call(bf16[48,2048]{1,0:T(8,128)(2,1)S(1)} %collective-permute-done.17.refs_0_.first_rows_ref.refs_5_, bf16[16,2048]{1,0:T(8,128)(2,1)S(1)} %collective-permute-done.24.handed_ref, bf16[32,2048]{1,0:T(8,128)(2,1)S(1)} %get-tuple-element.122.refs_0_, ...), custom_call_target="tpu_custom_call" | custom-call | flops 3449999872 | tf_op jit(solution)/shard_map/rows/pallas_call | solution.py:595
  58.2 1.0 %finish.1 = (f32[256,512]{1,0:T(8,128)}, f32[1,256]{1,0:T(1,128)}) custom-call(f32[256,512]{1,0:T(8,128)S(1)} %partial_own.1.own_ref, bf16[256,512]{1,0:T(8,128)(2,1)S(1)} %collective-permute-done.29.other_ref, f32[256,512]{1,0:T(8,128)S(1)} %get-tuple-element.129.weight_ref, f32[256,128]{1,0:T(8,128)S(1)} %get-tuple-element.119.refs_1_.gain_ref, ...), custom_call_target="tpu_custom_call" | custom-call | tf_op jit(solution)/shard_map/finish/pallas_call | solution.py:606
  (61 shorter events, 7.7 us)
Async XLA Ops:
  0.6 4.5 %copy-start = (bf16[1,2048,512]{2,1,0:T(8,128)(2,1)S(1)}, bf16[1,2048,512]{2,1,0:T(8,128)(2,1)}, u32[]{:S(2)}) copy-start(bf16[1,2048,512]{2,1,0:T(8,128)(2,1)} %param.11) | copy-start | bytes 6291460
  0.6 4.5 %copy-start.1 = (f32[1,2048]{1,0:T(1,128)S(1)}, f32[1,2048]{1,0:T(1,128)}, u32[]{:S(2)}) copy-start(f32[1,2048]{1,0:T(1,128)} %rest_1_.1) | copy-start | bytes 24580
  2.0 6.8 %collective-permute-start = (bf16[16,4608]{1,0:T(8,128)(2,1)S(1)}, bf16[16,4608]{1,0:T(8,128)(2,1)S(1)}, u32[]{:S(2)}, u32[]{:S(2)}) collective-permute-start(bf16[16,4608]{1,0:T(8,128)(2,1)S(1)} %get-tuple-element.70), channel_id=1, source_target_pairs={{0,4},{4,0},{8,12},{12,8},{16,20},{20,16},{24,28},{28,24},{1,5},{5... | collective-permute-start | bytes 442376 | tf_op jit(solution)/shard_map/ppermute | solution.py:521
  2.5 7.7 %collective-permute-start.1 = (bf16[16,4608]{1,0:T(8,128)(2,1)S(1)}, bf16[16,4608]{1,0:T(8,128)(2,1)S(1)}, u32[]{:S(2)}, u32[]{:S(2)}) collective-permute-start(bf16[16,4608]{1,0:T(8,128)(2,1)S(1)} %get-tuple-element.71), channel_id=1, source_target_pairs={{0,8},{4,12},{8,0},{12,4},{16,24},{20,28},{24,16},{28,20},{1,9},{5... | collective-permute-start | bytes 442376 | tf_op jit(solution)/shard_map/ppermute | solution.py:521
  5.1 7.3 %collective-permute-start.2 = (bf16[16,4608]{1,0:T(8,128)(2,1)S(1)}, bf16[16,4608]{1,0:T(8,128)(2,1)S(1)}, u32[]{:S(2)}, u32[]{:S(2)}) collective-permute-start(bf16[16,4608]{1,0:T(8,128)(2,1)S(1)} %get-tuple-element.72), channel_id=1, source_target_pairs={{0,12},{4,8},{8,4},{12,0},{16,28},{20,24},{24,20},{28,16},{1,13},{... | collective-permute-start | bytes 442376 | tf_op jit(solution)/shard_map/ppermute | solution.py:521
  6.9 11.9 %collective-permute-start.4 = (bf16[80,2048]{1,0:T(8,128)(2,1)S(1)}, bf16[80,2048]{1,0:T(8,128)(2,1)S(1)}, u32[]{:S(2)}, u32[]{:S(2)}) collective-permute-start(bf16[80,2048]{1,0:T(8,128)(2,1)S(1)} %get-tuple-element.79), channel_id=1, source_target_pairs={{0,16},{4,20},{8,24},{12,28},{16,0},{20,4},{24,8},{28,12},{1,17},{... | collective-permute-start | bytes 983048 | tf_op jit(solution)/shard_map/ppermute | solution.py:521
  8.7 4.8 %collective-permute-start.5 = (bf16[16,4608]{1,0:T(8,128)(2,1)S(1)}, bf16[16,4608]{1,0:T(8,128)(2,1)S(1)}, u32[]{:S(2)}, u32[]{:S(2)}) collective-permute-start(bf16[16,4608]{1,0:T(8,128)(2,1)S(1)} %get-tuple-element.81), channel_id=1, source_target_pairs={{0,4},{4,0},{8,12},{12,8},{16,20},{20,16},{24,28},{28,24},{1,5},{5... | collective-permute-start | bytes 442376 | tf_op jit(solution)/shard_map/ppermute | solution.py:521
  8.8 7.3 %collective-permute-start.6 = (bf16[16,4608]{1,0:T(8,128)(2,1)S(1)}, bf16[16,4608]{1,0:T(8,128)(2,1)S(1)}, u32[]{:S(2)}, u32[]{:S(2)}) collective-permute-start(bf16[16,4608]{1,0:T(8,128)(2,1)S(1)} %get-tuple-element.82), channel_id=1, source_target_pairs={{0,8},{4,12},{8,0},{12,4},{16,24},{20,28},{24,16},{28,20},{1,9},{5... | collective-permute-start | bytes 442376 | tf_op jit(solution)/shard_map/ppermute | solution.py:521
  10.3 8.5 %collective-permute-start.7 = (bf16[16,4608]{1,0:T(8,128)(2,1)S(1)}, bf16[16,4608]{1,0:T(8,128)(2,1)S(1)}, u32[]{:S(2)}, u32[]{:S(2)}) collective-permute-start(bf16[16,4608]{1,0:T(8,128)(2,1)S(1)} %get-tuple-element.83), channel_id=1, source_target_pairs={{0,12},{4,8},{8,4},{12,0},{16,28},{20,24},{24,20},{28,16},{1,13},{... | collective-permute-start | bytes 442376 | tf_op jit(solution)/shard_map/ppermute | solution.py:521
  12.8 7.7 %collective-permute-start.3 = (bf16[32,2048]{1,0:T(8,128)(2,1)S(1)}, bf16[32,2048]{1,0:T(8,128)(2,1)S(1)}, u32[]{:S(2)}, u32[]{:S(2)}) collective-permute-start(bf16[32,2048]{1,0:T(8,128)(2,1)S(1)} %get-tuple-element.78.refs_7_.refs_6_), channel_id=1, source_target_pairs={{3,2},{7,6},{11,10},{15,14},{19,18},{23,22},{27,26},{31,30}} | collective-permute-start | bytes 393224 | tf_op jit(solution)/shard_map/ppermute | solution.py:550
  13.5 7.7 %collective-permute-start.11 = (bf16[32,2048]{1,0:T(8,128)(2,1)S(1)}, bf16[32,2048]{1,0:T(8,128)(2,1)S(1)}, u32[]{:S(2)}, u32[]{:S(2)}) collective-permute-start(bf16[32,2048]{1,0:T(8,128)(2,1)S(1)} %get-tuple-element.85.refs_5_.refs_7_), channel_id=1, source_target_pairs={{3,2},{7,6},{11,10},{15,14},{19,18},{23,22},{27,26},{31,30}} | collective-permute-start | bytes 393224 | tf_op jit(solution)/shard_map/ppermute | solution.py:550
  19.1 2.8 %collective-permute-start.9 = (bf16[32,2048]{1,0:T(8,128)(2,1)S(1)}, bf16[32,2048]{1,0:T(8,128)(2,1)S(1)}, u32[]{:S(2)}, u32[]{:S(2)}) collective-permute-start(bf16[32,2048]{1,0:T(8,128)(2,1)S(1)} %get-tuple-element.90.refs_7_.refs_6_), channel_id=1, source_target_pairs={{3,2},{7,6},{11,10},{15,14},{19,18},{23,22},{27,26},{31,30}} | collective-permute-start | bytes 393224 | tf_op jit(solution)/shard_map/ppermute | solution.py:550
  19.8 2.8 %collective-permute-start.10 = (bf16[32,2048]{1,0:T(8,128)(2,1)S(1)}, bf16[32,2048]{1,0:T(8,128)(2,1)S(1)}, u32[]{:S(2)}, u32[]{:S(2)}) collective-permute-start(bf16[32,2048]{1,0:T(8,128)(2,1)S(1)} %get-tuple-element.91.refs_6_.refs_7_), channel_id=1, source_target_pairs={{3,2},{7,6},{11,10},{15,14},{19,18},{23,22},{27,26},{31,30}} | collective-permute-start | bytes 393224 | tf_op jit(solution)/shard_map/ppermute | solution.py:550
  20.5 5.6 %collective-permute-start.8 = (bf16[32,2048]{1,0:T(8,128)(2,1)S(1)}, bf16[32,2048]{1,0:T(8,128)(2,1)S(1)}, u32[]{:S(2)}, u32[]{:S(2)}) collective-permute-start(bf16[32,2048]{1,0:T(8,128)(2,1)S(1)} %get-tuple-element.92.refs_7_.refs_8_), channel_id=1, source_target_pairs={{2,1},{6,5},{10,9},{14,13},{18,17},{22,21},{26,25},{30,29}} | collective-permute-start | bytes 393224 | tf_op jit(solution)/shard_map/ppermute | solution.py:550
  21.2 6.2 %collective-permute-start.13 = (bf16[32,2048]{1,0:T(8,128)(2,1)S(1)}, bf16[32,2048]{1,0:T(8,128)(2,1)S(1)}, u32[]{:S(2)}, u32[]{:S(2)}) collective-permute-start(bf16[32,2048]{1,0:T(8,128)(2,1)S(1)} %get-tuple-element.93.refs_6_.refs_9_), channel_id=1, source_target_pairs={{2,1},{6,5},{10,9},{14,13},{18,17},{22,21},{26,25},{30,29}} | collective-permute-start | bytes 393224 | tf_op jit(solution)/shard_map/ppermute | solution.py:550
  21.9 6.8 %collective-permute-start.15 = (bf16[32,2048]{1,0:T(8,128)(2,1)S(1)}, bf16[32,2048]{1,0:T(8,128)(2,1)S(1)}, u32[]{:S(2)}, u32[]{:S(2)}) collective-permute-start(bf16[32,2048]{1,0:T(8,128)(2,1)S(1)} %get-tuple-element.94.refs_7_.refs_8_), channel_id=1, source_target_pairs={{2,1},{6,5},{10,9},{14,13},{18,17},{22,21},{26,25},{30,29}} | collective-permute-start | bytes 393224 | tf_op jit(solution)/shard_map/ppermute | solution.py:550
  22.7 7.4 %collective-permute-start.16 = (bf16[32,2048]{1,0:T(8,128)(2,1)S(1)}, bf16[32,2048]{1,0:T(8,128)(2,1)S(1)}, u32[]{:S(2)}, u32[]{:S(2)}) collective-permute-start(bf16[32,2048]{1,0:T(8,128)(2,1)S(1)} %get-tuple-element.95.refs_6_.after_ref.refs_0_.refs_9_), channel_id=1, source_target_pairs={{2,1},{6,5},{10,9},{14,13},{18,17},{22,21},{26,25},{30,29}} | collective-permute-start | bytes 393224 | tf_op jit(solution)/shard_map/ppermute | solution.py:550
  23.5 7.9 %collective-permute-start.20 = (bf16[128,512]{1,0:T(8,128)(2,1)S(1)}, bf16[128,512]{1,0:T(8,128)(2,1)S(1)}, u32[]{:S(2)}, u32[]{:S(2)}) collective-permute-start(bf16[128,512]{1,0:T(8,128)(2,1)S(1)} %columns6.1), channel_id=1, source_target_pairs={{0,24},{4,28},{8,16},{12,20},{16,8},{20,12},{24,0},{28,4},{1,25},{... | collective-permute-start | bytes 393224 | tf_op jit(solution)/shard_map/ppermute | solution.py:521
  26.1 10.9 %collective-permute-start.12 = (bf16[32,2048]{1,0:T(8,128)(2,1)S(1)}, bf16[32,2048]{1,0:T(8,128)(2,1)S(1)}, u32[]{:S(2)}, u32[]{:S(2)}) collective-permute-start(bf16[32,2048]{1,0:T(8,128)(2,1)S(1)} %get-tuple-element.96.refs_7_.refs_10_), channel_id=1, source_target_pairs={{1,0},{5,4},{9,8},{13,12},{17,16},{21,20},{25,24},{29,28}} | collective-permute-start | bytes 393224 | tf_op jit(solution)/shard_map/ppermute | solution.py:550
  27.4 12.3 %collective-permute-start.14 = (bf16[32,2048]{1,0:T(8,128)(2,1)S(1)}, bf16[32,2048]{1,0:T(8,128)(2,1)S(1)}, u32[]{:S(2)}, u32[]{:S(2)}) collective-permute-start(bf16[32,2048]{1,0:T(8,128)(2,1)S(1)} %get-tuple-element.97.refs_6_.refs_11_), channel_id=1, source_target_pairs={{1,0},{5,4},{9,8},{13,12},{17,16},{21,20},{25,24},{29,28}} | collective-permute-start | bytes 393224 | tf_op jit(solution)/shard_map/ppermute | solution.py:550
  28.8 15.0 %collective-permute-start.18 = (bf16[32,2048]{1,0:T(8,128)(2,1)S(1)}, bf16[32,2048]{1,0:T(8,128)(2,1)S(1)}, u32[]{:S(2)}, u32[]{:S(2)}) collective-permute-start(bf16[32,2048]{1,0:T(8,128)(2,1)S(1)} %get-tuple-element.104.refs_7_.refs_10_), channel_id=1, source_target_pairs={{1,0},{5,4},{9,8},{13,12},{17,16},{21,20},{25,24},{29,28}} | collective-permute-start | bytes 393224 | tf_op jit(solution)/shard_map/ppermute | solution.py:550
  30.1 15.3 %collective-permute-start.19 = (bf16[32,2048]{1,0:T(8,128)(2,1)S(1)}, bf16[32,2048]{1,0:T(8,128)(2,1)S(1)}, u32[]{:S(2)}, u32[]{:S(2)}) collective-permute-start(bf16[32,2048]{1,0:T(8,128)(2,1)S(1)} %get-tuple-element.105.refs_12_.refs_0_.refs_11_), channel_id=1, source_target_pairs={{1,0},{5,4},{9,8},{13,12},{17,16},{21,20},{25,24},{29,28}} | collective-permute-start | bytes 393224 | tf_op jit(solution)/shard_map/ppermute | solution.py:550
  31.5 14.0 %collective-permute-start.21 = (bf16[128,512]{1,0:T(8,128)(2,1)S(1)}, bf16[128,512]{1,0:T(8,128)(2,1)S(1)}, u32[]{:S(2)}, u32[]{:S(2)}) collective-permute-start(bf16[128,512]{1,0:T(8,128)(2,1)S(1)} %columns2.1), channel_id=1, source_target_pairs={{0,8},{4,12},{8,0},{12,4},{16,24},{20,28},{24,16},{28,20},{1,9},{5... | collective-permute-start | bytes 393224 | tf_op jit(solution)/shard_map/ppermute | solution.py:521
  40.6 9.2 %collective-permute-start.17 = (bf16[48,2048]{1,0:T(8,128)(2,1)S(1)}, bf16[48,2048]{1,0:T(8,128)(2,1)S(1)}, u32[]{:S(2)}, u32[]{:S(2)}) collective-permute-start(bf16[48,2048]{1,0:T(8,128)(2,1)S(1)} %get-tuple-element.108), channel_id=1, source_target_pairs={{0,8},{4,12},{8,0},{12,4},{16,24},{20,28},{24,16},{28,20},{1,9},{5... | collective-permute-start | bytes 589832 | tf_op jit(solution)/shard_map/ppermute | solution.py:521
  42.2 7.7 %collective-permute-start.22 = (bf16[192,512]{1,0:T(8,128)(2,1)S(1)}, bf16[192,512]{1,0:T(8,128)(2,1)S(1)}, u32[]{:S(2)}, u32[]{:S(2)}) collective-permute-start(bf16[192,512]{1,0:T(8,128)(2,1)S(1)} %columns4.1), channel_id=1, source_target_pairs={{0,16},{4,20},{8,24},{12,28},{16,0},{20,4},{24,8},{28,12},{1,17},{... | collective-permute-start | bytes 589832 | tf_op jit(solution)/shard_map/ppermute | solution.py:521
  46.3 5.2 %collective-permute-start.23 = (bf16[64,512]{1,0:T(8,128)(2,1)S(1)}, bf16[64,512]{1,0:T(8,128)(2,1)S(1)}, u32[]{:S(2)}, u32[]{:S(2)}) collective-permute-start(bf16[64,512]{1,0:T(8,128)(2,1)S(1)} %get-tuple-element.120.refs_1_), channel_id=1, source_target_pairs={{0,16},{4,20},{8,24},{12,28},{16,0},{20,4},{24,8},{28,12},{1,17},{... | collective-permute-start | bytes 196616 | tf_op jit(solution)/shard_map/ppermute | solution.py:521
  47.9 6.4 %collective-permute-start.26 = (bf16[32,2048]{1,0:T(8,128)(2,1)S(1)}, bf16[32,2048]{1,0:T(8,128)(2,1)S(1)}, u32[]{:S(2)}, u32[]{:S(2)}) collective-permute-start(bf16[32,2048]{1,0:T(8,128)(2,1)S(1)} %get-tuple-element.124), channel_id=1, source_target_pairs={{0,8},{4,12},{8,0},{12,4},{16,24},{20,28},{24,16},{28,20},{1,9},{5... | collective-permute-start | bytes 393224 | tf_op jit(solution)/shard_map/ppermute | solution.py:521
  49.4 6.9 %collective-permute-start.28 = (bf16[128,512]{1,0:T(8,128)(2,1)S(1)}, bf16[128,512]{1,0:T(8,128)(2,1)S(1)}, u32[]{:S(2)}, u32[]{:S(2)}) collective-permute-start(bf16[128,512]{1,0:T(8,128)(2,1)S(1)} %get-tuple-element.128.refs_4_), channel_id=1, source_target_pairs={{0,24},{4,28},{8,16},{12,20},{16,8},{20,12},{24,0},{28,4},{1,25},{... | collective-permute-start | bytes 393224 | tf_op jit(solution)/shard_map/ppermute | solution.py:521
  49.8 7.2 %collective-permute-start.25 = (bf16[32,2048]{1,0:T(8,128)(2,1)S(1)}, bf16[32,2048]{1,0:T(8,128)(2,1)S(1)}, u32[]{:S(2)}, u32[]{:S(2)}) collective-permute-start(bf16[32,2048]{1,0:T(8,128)(2,1)S(1)} %get-tuple-element.123), channel_id=1, source_target_pairs={{0,4},{4,0},{8,12},{12,8},{16,20},{20,16},{24,28},{28,24},{1,5},{5... | collective-permute-start | bytes 393224 | tf_op jit(solution)/shard_map/ppermute | solution.py:521
  49.9 7.2 %collective-permute-start.27 = (bf16[16,2048]{1,0:T(8,128)(2,1)S(1)}, bf16[16,2048]{1,0:T(8,128)(2,1)S(1)}, u32[]{:S(2)}, u32[]{:S(2)}) collective-permute-start(bf16[16,2048]{1,0:T(8,128)(2,1)S(1)} %get-tuple-element.125), channel_id=1, source_target_pairs={{0,12},{4,8},{8,4},{12,0},{16,28},{20,24},{24,20},{28,16},{1,13},{... | collective-permute-start | bytes 196616 | tf_op jit(solution)/shard_map/ppermute | solution.py:521
  51.5 5.6 %collective-permute-start.24 = (bf16[16,2048]{1,0:T(8,128)(2,1)S(1)}, bf16[16,2048]{1,0:T(8,128)(2,1)S(1)}, u32[]{:S(2)}, u32[]{:S(2)}) collective-permute-start(bf16[16,2048]{1,0:T(8,128)(2,1)S(1)} %get-tuple-element.121), channel_id=1, source_target_pairs={{0,4},{4,0},{8,12},{12,8},{16,20},{20,16},{24,28},{28,24},{1,5},{5... | collective-permute-start | bytes 196616 | tf_op jit(solution)/shard_map/ppermute | solution.py:521
  56.6 1.6 %collective-permute-start.29 = (bf16[256,512]{1,0:T(8,128)(2,1)S(1)}, bf16[256,512]{1,0:T(8,128)(2,1)S(1)}, u32[]{:S(2)}, u32[]{:S(2)}) collective-permute-start(bf16[256,512]{1,0:T(8,128)(2,1)S(1)} %partial_other.1.refs_9_), channel_id=1, source_target_pairs={{0,4},{4,0},{8,12},{12,8},{16,20},{20,16},{24,28},{28,24},{1,5},{5... | collective-permute-start | bytes 786440 | tf_op jit(solution)/shard_map/ppermute | solution.py:521

commit v16 on v15

--- a/solution.py
+++ b/solution.py
@@ -422,7 +422,7 @@
         in_specs=[VMEM] * (2 + len(came)) + [ANY] * len(after),
         out_specs=(VMEM,) * len(outs),
         name=f"columns{distance}",
-        **params(0.0 if distance else 1.0),
+        **params(0.0 if distance else 2.5),
     )(blocks[0][3], blocks[1][3], *came, *after)
     return results if distance == 0 else results[0]
 
@@ -441,14 +441,14 @@
 
 
 def partial_kernel(shares, first, for_other, *refs):
-    columns, values, out_ref = refs[:4], refs[4:9], refs[-1]
+    columns, values, out_ref = refs[:4], refs[4:10], refs[-1]
     kv_width = out_ref.shape[1]
     parts = []
     for ref in values:
         beside = ref.shape[1] > kv_width
         rows = slice(first, 2 * first) if beside else slice(0, ref.shape[0])
         parts += [ref[rows, at : at + kv_width] for at in range(0, ref.shape[1], kv_width)]
-    parts.insert(len(parts) - 2, columns[2][2 * BLOCK :, :])
+    parts.insert(len(parts) - 3, columns[2][2 * BLOCK :, :])
     value = jnp.concatenate(parts, axis=0)
     mine = lax.rem(place()[2], 2)
     core = 1 - mine if for_other else mine
@@ -466,7 +466,7 @@
         out_shape=jax.ShapeDtypeStruct(
             (shares, kv_width), jnp.bfloat16 if for_other else jnp.float32
         ),
-        in_specs=[VMEM] * 9 + [ANY] * len(after),
+        in_specs=[VMEM] * 10 + [ANY] * len(after),
         out_specs=VMEM,
         name="partial_other" if for_other else "partial_own",
         **params(0.0 if for_other else 0.5),
@@ -572,7 +572,7 @@
                 late = [done[0][1], done[0][0]]
             if last and u == 3:
                 late = [done[2][1], done[2][0], done[0][0], done[1][0], done[1][1]]
-                first_rows = swap(done[1][2], 2)
+                first_rows, far_first = swap(done[1][2], 2), swap(done[1][1], 6)
                 columns[4] = swap(columns_for(4, blocks, [], [done[1][1]]), 4)
                 after = after + [columns[2]]
             done.append(
@@ -585,10 +585,10 @@
             kept[u].append(done[u])
     own_value, own_values, *rows = done[3]
     rows = [rows[0]] + [swap(rows[k], k) for k in range(1, half)]
-    far_values, across_value = swap(own_values, 6), swap(own_value, 4)
-    columns[0], handed = columns_for(0, blocks, [own_value, columns[4], across_value], [first_rows])
+    far_value, across_value = swap(own_value, 6), swap(own_value, 4)
+    columns[0], handed = columns_for(0, blocks, [own_value, columns[4], far_first, far_value], [first_rows])
     handed = swap(handed, 1)
-    values = [own_values, first_rows, rows[2], across_value, far_values]
+    values = [own_values, first_rows, rows[2], across_value, far_first, far_value]
     other = partial_sums(shares, piece, True, columns, values)
     own = partial_sums(shares, piece, False, columns, values, [other])
     other = swap(other, 1)
@@ -601,7 +601,7 @@
         in_specs=[VMEM] * (2 + half),
         out_specs=(VMEM, VMEM),
         name="rows",
-        **params(3.0),
+        **params(2.5),
     )(first_rows, handed, *rows)
     weight_grad, gain_grad = pl.pallas_call(
         finish_kernel,

time: 59.6 us -> 59.9 us (level); the launches traced: 59.2 us -> 58.9 us
  waiting for transfers between devices: 19.3 us -> 17.6 us
  starting transfers between devices: 29 us -> 30.3 us
    ppermute x18 -> x19, starting transfers between devices: 18.5 us -> 19.8 us  [swap(): return lax.ppermute(array, 'dp', [(i, i ^ k) for i in range(replicas)])]
    ppermute x18 -> x19, waiting for transfers between devices: 11.5 us -> 10.2 us  [swap(): return lax.ppermute(array, 'dp', [(i, i ^ k) for i in range(replicas)])]
  transfers between devices with their start and end apart: 30 -> 31, of which waited for: 9 -> 10; matrix products, arithmetic and copies ran while one was open for 0% -> 0% of each run, Pallas kernels for 13% -> 13%
where the time goes in v16:
time: 59.9 us; the launch traced here: 58.9 us
  starting transfers between devices  30.3 us (51%)
  waiting for transfers between devices  17.6 us (29%)
  Pallas kernels  9.89 us (17%)
  between operations  1.06 us (2%)
    ppermute x19, starting transfers between devices, swap(): return lax.ppermute(array, 'dp', [(i, i ^ k) for i in range(replicas)])  19.8 us
    ppermute x12, starting transfers between devices, direct(): lax.ppermute(unit[-1][0], 'section', hop)  10.5 us
    ppermute x19, waiting for transfers between devices, swap(): return lax.ppermute(array, 'dp', [(i, i ^ k) for i in range(replicas)])  10.2 us
    ppermute x12, waiting for transfers between devices, direct(): lax.ppermute(unit[-1][0], 'section', hop)  7.37 us
    pallas_call x16, Pallas kernels, tick_step(): pl.pallas_call(functools.partial(tick_kernel, tick, EARLY if low else LAT...  3.43 us
    pallas_call x2, Pallas kernels, pack(): pl.pallas_call(functools.partial(pack_kernel, block, half, piece), out_sh...  3.06 us
  transfers between devices with their start and end apart: 31, of which 10 were waited for; matrix products, arithmetic and copies ran while one was open for 0% of the time, Pallas kernels for 13%

profile of v16, /device:TPU:0, one launch (start us, length us, event | category | flops | bytes accessed | tf_op | source)
XLA Modules:
  0.0 58.9 jit_solution(6653777805704526392)
XLA Ops:
  0.7 1.4 %pack.2 = (bf16[16,4608]{1,0:T(8,128)(2,1)S(1)}, bf16[16,4608]{1,0:T(8,128)(2,1)S(1)}, bf16[16,4608]{1,0:T(8,128)(2,1)S(1)}, bf16[16,4608]{1,0:T(8,128)(2,1)S(1)}, bf16[80,2048]{1,0:T(8,128)(2,1)S(1)}) custom-call(bf16[128,2048]{1,0:T(8,128)(2,1)} %bitcast.8, bf16[128,512]{1,0:T(8,128)(2,1)} %bitcast.13, bf16[128,2048]{1,0:T(8,128)(2,1)} %bitcast.10, ...), custom_call_target="tpu_custom_call" | custom-call | flops 1380000000 | tf_op jit(solution)/shard_map/pack/pallas_call | solution.py:383
  2.5 2.6 %collective-permute-start.1 = (bf16[16,4608]{1,0:T(8,128)(2,1)S(1)}, bf16[16,4608]{1,0:T(8,128)(2,1)S(1)}, u32[]{:S(2)}, u32[]{:S(2)}) collective-permute-start(bf16[16,4608]{1,0:T(8,128)(2,1)S(1)} %get-tuple-element.71), channel_id=1, source_target_pairs={{0,8},{4,12},{8,0},{12,4},{16,24},{20,28},{24,16},{28,20},{1,9},{5... | collective-permute-start | bytes 442376 | tf_op jit(solution)/shard_map/ppermute | solution.py:521
  5.2 1.7 %pack.3 = (f32[1,2048]{1,0:T(1,128)S(1)}, bf16[512,2048]{1,0:T(8,128)(2,1)S(1)}, bf16[16,4608]{1,0:T(8,128)(2,1)S(1)}, bf16[16,4608]{1,0:T(8,128)(2,1)S(1)}, bf1...) custom-call(bf16[128,2048]{1,0:T(8,128)(2,1)} %bitcast.9, ...), custom_call_target="tpu_custom_call" | custom-call | flops 1380000000 | tf_op jit(solution)/shard_map/pack/pallas_call | solution.py:383
  6.9 1.8 %collective-permute-start.4 = (bf16[80,2048]{1,0:T(8,128)(2,1)S(1)}, bf16[80,2048]{1,0:T(8,128)(2,1)S(1)}, u32[]{:S(2)}, u32[]{:S(2)}) collective-permute-start(bf16[80,2048]{1,0:T(8,128)(2,1)S(1)} %get-tuple-element.79), channel_id=1, source_target_pairs={{0,16},{4,20},{8,24},{12,28},{16,0},{20,4},{24,8},{28,12},{1,17},{... | collective-permute-start | bytes 983048 | tf_op jit(solution)/shard_map/ppermute | solution.py:521
  8.8 1.5 %collective-permute-start.6 = (bf16[16,4608]{1,0:T(8,128)(2,1)S(1)}, bf16[16,4608]{1,0:T(8,128)(2,1)S(1)}, u32[]{:S(2)}, u32[]{:S(2)}) collective-permute-start(bf16[16,4608]{1,0:T(8,128)(2,1)S(1)} %get-tuple-element.82), channel_id=1, source_target_pairs={{0,8},{4,12},{8,0},{12,4},{16,24},{20,28},{24,16},{28,20},{1,9},{5... | collective-permute-start | bytes 442376 | tf_op jit(solution)/shard_map/ppermute | solution.py:521
  10.6 1.9 %collective-permute-done.2.refs_3_ = bf16[16,4608]{1,0:T(8,128)(2,1)S(1)} collective-permute-done((bf16[16,4608]{1,0:T(8,128)(2,1)S(1)}, bf16[16,4608]{1,0:T(8,128)(2,1)S(1)}, u32[]{:S(2)}, u32[]{:S(2)}) %collective-permute-start.2) | collective-permute-done | bytes 147488 | tf_op jit(solution)/shard_map/ppermute | solution.py:521
  12.8 0.7 %collective-permute-start.3 = (bf16[32,2048]{1,0:T(8,128)(2,1)S(1)}, bf16[32,2048]{1,0:T(8,128)(2,1)S(1)}, u32[]{:S(2)}, u32[]{:S(2)}) collective-permute-start(bf16[32,2048]{1,0:T(8,128)(2,1)S(1)} %get-tuple-element.78.refs_7_.refs_6_), channel_id=1, source_target_pairs={{3,2},{7,6},{11,10},{15,14},{19,18},{23,22},{27,26},{31,30}} | collective-permute-start | bytes 393224 | tf_op jit(solution)/shard_map/ppermute | solution.py:550
  13.5 0.7 %collective-permute-start.11 = (bf16[32,2048]{1,0:T(8,128)(2,1)S(1)}, bf16[32,2048]{1,0:T(8,128)(2,1)S(1)}, u32[]{:S(2)}, u32[]{:S(2)}) collective-permute-start(bf16[32,2048]{1,0:T(8,128)(2,1)S(1)} %get-tuple-element.85.refs_5_.refs_7_), channel_id=1, source_target_pairs={{3,2},{7,6},{11,10},{15,14},{19,18},{23,22},{27,26},{31,30}} | collective-permute-start | bytes 393224 | tf_op jit(solution)/shard_map/ppermute | solution.py:550
  14.2 1.9 %collective-permute-done.6.refs_2_ = bf16[16,4608]{1,0:T(8,128)(2,1)S(1)} collective-permute-done((bf16[16,4608]{1,0:T(8,128)(2,1)S(1)}, bf16[16,4608]{1,0:T(8,128)(2,1)S(1)}, u32[]{:S(2)}, u32[]{:S(2)}) %collective-permute-start.6) | collective-permute-done | bytes 147488 | tf_op jit(solution)/shard_map/ppermute | solution.py:521
  16.1 2.6 %collective-permute-done.7.refs_3_ = bf16[16,4608]{1,0:T(8,128)(2,1)S(1)} collective-permute-done((bf16[16,4608]{1,0:T(8,128)(2,1)S(1)}, bf16[16,4608]{1,0:T(8,128)(2,1)S(1)}, u32[]{:S(2)}, u32[]{:S(2)}) %collective-permute-start.7) | collective-permute-done | bytes 147488 | tf_op jit(solution)/shard_map/ppermute | solution.py:521
  19.1 0.7 %collective-permute-start.9 = (bf16[32,2048]{1,0:T(8,128)(2,1)S(1)}, bf16[32,2048]{1,0:T(8,128)(2,1)S(1)}, u32[]{:S(2)}, u32[]{:S(2)}) collective-permute-start(bf16[32,2048]{1,0:T(8,128)(2,1)S(1)} %get-tuple-element.90.refs_7_.refs_6_), channel_id=1, source_target_pairs={{3,2},{7,6},{11,10},{15,14},{19,18},{23,22},{27,26},{31,30}} | collective-permute-start | bytes 393224 | tf_op jit(solution)/shard_map/ppermute | solution.py:550
  19.8 0.7 %collective-permute-start.10 = (bf16[32,2048]{1,0:T(8,128)(2,1)S(1)}, bf16[32,2048]{1,0:T(8,128)(2,1)S(1)}, u32[]{:S(2)}, u32[]{:S(2)}) collective-permute-start(bf16[32,2048]{1,0:T(8,128)(2,1)S(1)} %get-tuple-element.91.refs_6_.refs_7_), channel_id=1, source_target_pairs={{3,2},{7,6},{11,10},{15,14},{19,18},{23,22},{27,26},{31,30}} | collective-permute-start | bytes 393224 | tf_op jit(solution)/shard_map/ppermute | solution.py:550
  21.2 0.7 %collective-permute-start.13 = (bf16[32,2048]{1,0:T(8,128)(2,1)S(1)}, bf16[32,2048]{1,0:T(8,128)(2,1)S(1)}, u32[]{:S(2)}, u32[]{:S(2)}) collective-permute-start(bf16[32,2048]{1,0:T(8,128)(2,1)S(1)} %get-tuple-element.93.refs_6_.refs_9_), channel_id=1, source_target_pairs={{2,1},{6,5},{10,9},{14,13},{18,17},{22,21},{26,25},{30,29}} | collective-permute-start | bytes 393224 | tf_op jit(solution)/shard_map/ppermute | solution.py:550
  23.5 2.6 %collective-permute-start.20 = (bf16[128,512]{1,0:T(8,128)(2,1)S(1)}, bf16[128,512]{1,0:T(8,128)(2,1)S(1)}, u32[]{:S(2)}, u32[]{:S(2)}) collective-permute-start(bf16[128,512]{1,0:T(8,128)(2,1)S(1)} %columns6.1), channel_id=1, source_target_pairs={{0,24},{4,28},{8,16},{12,20},{16,8},{20,12},{24,0},{28,4},{1,25},{... | collective-permute-start | bytes 393224 | tf_op jit(solution)/shard_map/ppermute | solution.py:521
  26.1 1.3 %collective-permute-start.12 = (bf16[32,2048]{1,0:T(8,128)(2,1)S(1)}, bf16[32,2048]{1,0:T(8,128)(2,1)S(1)}, u32[]{:S(2)}, u32[]{:S(2)}) collective-permute-start(bf16[32,2048]{1,0:T(8,128)(2,1)S(1)} %get-tuple-element.96.refs_7_.refs_10_), channel_id=1, source_target_pairs={{1,0},{5,4},{9,8},{13,12},{17,16},{21,20},{25,24},{29,28}} | collective-permute-start | bytes 393224 | tf_op jit(solution)/shard_map/ppermute | solution.py:550
  27.4 1.3 %collective-permute-start.14 = (bf16[32,2048]{1,0:T(8,128)(2,1)S(1)}, bf16[32,2048]{1,0:T(8,128)(2,1)S(1)}, u32[]{:S(2)}, u32[]{:S(2)}) collective-permute-start(bf16[32,2048]{1,0:T(8,128)(2,1)S(1)} %get-tuple-element.97.refs_6_.refs_11_), channel_id=1, source_target_pairs={{1,0},{5,4},{9,8},{13,12},{17,16},{21,20},{25,24},{29,28}} | collective-permute-start | bytes 393224 | tf_op jit(solution)/shard_map/ppermute | solution.py:550
  28.8 1.3 %collective-permute-start.18 = (bf16[32,2048]{1,0:T(8,128)(2,1)S(1)}, bf16[32,2048]{1,0:T(8,128)(2,1)S(1)}, u32[]{:S(2)}, u32[]{:S(2)}) collective-permute-start(bf16[32,2048]{1,0:T(8,128)(2,1)S(1)} %get-tuple-element.104.refs_7_.refs_10_), channel_id=1, source_target_pairs={{1,0},{5,4},{9,8},{13,12},{17,16},{21,20},{25,24},{29,28}} | collective-permute-start | bytes 393224 | tf_op jit(solution)/shard_map/ppermute | solution.py:550
  30.1 1.3 %collective-permute-start.19 = (bf16[32,2048]{1,0:T(8,128)(2,1)S(1)}, bf16[32,2048]{1,0:T(8,128)(2,1)S(1)}, u32[]{:S(2)}, u32[]{:S(2)}) collective-permute-start(bf16[32,2048]{1,0:T(8,128)(2,1)S(1)} %get-tuple-element.105.refs_12_.refs_0_.refs_11_), channel_id=1, source_target_pairs={{1,0},{5,4},{9,8},{13,12},{17,16},{21,20},{25,24},{29,28}} | collective-permute-start | bytes 393224 | tf_op jit(solution)/shard_map/ppermute | solution.py:550
  32.1 4.9 %collective-permute-done.12.refs_0_ = bf16[32,2048]{1,0:T(8,128)(2,1)S(1)} collective-permute-done((bf16[32,2048]{1,0:T(8,128)(2,1)S(1)}, bf16[32,2048]{1,0:T(8,128)(2,1)S(1)}, u32[]{:S(2)}, u32[]{:S(2)}) %collective-permute-start.12) | collective-permute-done | bytes 131104 | tf_op jit(solution)/shard_map/ppermute | solution.py:550
  37.0 0.8 %tick3_a_late.1 = (bf16[32,2048]{1,0:T(8,128)(2,1)S(1)}, bf16[32,512]{1,0:T(8,128)(2,1)S(1)}) custom-call(bf16[32,2048]{1,0:T(8,128)(2,1)S(1)} %collective-permute-done.12.refs_0_, bf16[4,32,128]{2,1,0:T(8,128)(2,1)S(1)} %get-tuple-element.73.refs_1_, f32[64,128]{1,0:T(8,128)S(1)} %get-tuple-element.74.refs_2_.refs_3_, ...), custom_call_target="tpu_custom_call" | custom-call | flops 1150000000 | tf_op jit(solution)/shard_map/tick3_a_late/pallas_call | solution.py:319
  37.8 2.0 %collective-permute-done.14.refs_1_ = bf16[32,2048]{1,0:T(8,128)(2,1)S(1)} collective-permute-done((bf16[32,2048]{1,0:T(8,128)(2,1)S(1)}, bf16[32,2048]{1,0:T(8,128)(2,1)S(1)}, u32[]{:S(2)}, u32[]{:S(2)}) %collective-permute-start.14) | collective-permute-done | bytes 131104 | tf_op jit(solution)/shard_map/ppermute | solution.py:550
  39.8 0.8 %tick3_a_early.1 = (bf16[32,2048]{1,0:T(8,128)(2,1)S(1)}, bf16[64,512]{1,0:T(8,128)(2,1)S(1)}, bf16[48,2048]{1,0:T(8,128)(2,1)S(1)}) custom-call(bf16[32,2048]{1,0:T(8,128)(2,1)S(1)} %collective-permute-done.12.refs_0_, bf16[32,2048]{1,0:T(8,128)(2,1)S(1)} %collective-permute-done.14.refs_1_, bf16[4,32,256]{2,1,0:T(8,128)(2,1)S(1)} %get-tuple-element.84.refs_2_, ...), custom_call_target="tpu_custom_call" | custom-call | flops 1150000000 | tf_op jit(solution)/shard_map/tick3_a_early/pallas_call | solution.py:319
  40.7 2.5 %collective-permute-start.23 = (bf16[64,512]{1,0:T(8,128)(2,1)S(1)}, bf16[64,512]{1,0:T(8,128)(2,1)S(1)}, u32[]{:S(2)}, u32[]{:S(2)}) collective-permute-start(bf16[64,512]{1,0:T(8,128)(2,1)S(1)} %get-tuple-element.118.refs_17_.refs_0_), channel_id=1, source_target_pairs={{0,24},{4,28},{8,16},{12,20},{16,8},{20,12},{24,0},{28,4},{1,25},{... | collective-permute-start | bytes 196616 | tf_op jit(solution)/shard_map/ppermute | solution.py:521
  44.2 0.8 %tick3_b_late.1 = (bf16[32,2048]{1,0:T(8,128)(2,1)S(1)}, bf16[32,512]{1,0:T(8,128)(2,1)S(1)}) custom-call(bf16[32,2048]{1,0:T(8,128)(2,1)S(1)} %collective-permute-done.18.refs_0_, bf16[4,32,128]{2,1,0:T(8,128)(2,1)S(1)} %get-tuple-element.89.refs_1_, f32[64,128]{1,0:T(8,128)S(1)} %get-tuple-element.87.refs_2_.refs_3_, ...), custom_call_target="tpu_custom_call" | custom-call | flops 1150000000 | tf_op jit(solution)/shard_map/tick3_b_late/pallas_call | solution.py:319
  45.4 0.9 %tick3_b_early.1 = (bf16[64,512]{1,0:T(8,128)(2,1)S(1)}, bf16[128,512]{1,0:T(8,128)(2,1)S(1)}, bf16[32,2048]{1,0:T(8,128)(2,1)S(1)}, bf16[32,2048]{1,0:T(8,128)(...) custom-call(bf16[32,2048]{1,0:T(8,128)(2,1)S(1)} %collective-permute-done.18.refs_0_, ...), custom_call_target="tpu_custom_call" | custom-call | flops 1150000000 | tf_op jit(solution)/shard_map/tick3_b_early/pallas_call | solution.py:319
  46.3 2.5 %collective-permute-start.24 = (bf16[64,512]{1,0:T(8,128)(2,1)S(1)}, bf16[64,512]{1,0:T(8,128)(2,1)S(1)}, u32[]{:S(2)}, u32[]{:S(2)}) collective-permute-start(bf16[64,512]{1,0:T(8,128)(2,1)S(1)} %get-tuple-element.120.refs_1_), channel_id=1, source_target_pairs={{0,24},{4,28},{8,16},{12,20},{16,8},{20,12},{24,0},{28,4},{1,25},{... | collective-permute-start | bytes 196616 | tf_op jit(solution)/shard_map/ppermute | solution.py:521
  49.3 0.7 %collective-permute-done.17.refs_0_.first_rows_ref.refs_5_ = bf16[48,2048]{1,0:T(8,128)(2,1)S(1)} collective-permute-done((bf16[48,2048]{1,0:T(8,128)(2,1)S(1)}, bf16[48,2048]{1,0:T(8,128)(2,1)S(1)}, u32[]{:S(2)}, u32[]{:S(2)}) %collective-permute-start.17) | collective-permute-done | bytes 196640 | tf_op jit(solution)/shard_map/ppermute | solution.py:521
  50.0 0.7 %collective-permute-start.27 = (bf16[32,2048]{1,0:T(8,128)(2,1)S(1)}, bf16[32,2048]{1,0:T(8,128)(2,1)S(1)}, u32[]{:S(2)}, u32[]{:S(2)}) collective-permute-start(bf16[32,2048]{1,0:T(8,128)(2,1)S(1)} %get-tuple-element.124), channel_id=1, source_target_pairs={{0,8},{4,12},{8,0},{12,4},{16,24},{20,28},{24,16},{28,20},{1,9},{5... | collective-permute-start | bytes 393224 | tf_op jit(solution)/shard_map/ppermute | solution.py:521
  51.6 2.0 %collective-permute-start.25 = (bf16[16,2048]{1,0:T(8,128)(2,1)S(1)}, bf16[16,2048]{1,0:T(8,128)(2,1)S(1)}, u32[]{:S(2)}, u32[]{:S(2)}) collective-permute-start(bf16[16,2048]{1,0:T(8,128)(2,1)S(1)} %get-tuple-element.121), channel_id=1, source_target_pairs={{0,4},{4,0},{8,12},{12,8},{16,20},{20,16},{24,28},{28,24},{1,5},{5... | collective-permute-start | bytes 196616 | tf_op jit(solution)/shard_map/ppermute | solution.py:521
  53.6 2.3 %collective-permute-done.27.refs_2_.refs_6_ = bf16[32,2048]{1,0:T(8,128)(2,1)S(1)} collective-permute-done((bf16[32,2048]{1,0:T(8,128)(2,1)S(1)}, bf16[32,2048]{1,0:T(8,128)(2,1)S(1)}, u32[]{:S(2)}, u32[]{:S(2)}) %collective-permute-start.27) | collective-permute-done | bytes 131104 | tf_op jit(solution)/shard_map/ppermute | solution.py:521
  56.7 0.8 %rows.1 = (bf16[128,2048]{1,0:T(8,128)(2,1)}, f32[8,128]{1,0:T(8,128)S(1)}) custom-call(bf16[48,2048]{1,0:T(8,128)(2,1)S(1)} %collective-permute-done.17.refs_0_.first_rows_ref.refs_5_, bf16[16,2048]{1,0:T(8,128)(2,1)S(1)} %collective-permute-done.25.handed_ref, bf16[32,2048]{1,0:T(8,128)(2,1)S(1)} %get-tuple-element.122.refs_0_, ...), custom_call_target="tpu_custom_call" | custom-call | flops 2875000064 | tf_op jit(solution)/shard_map/rows/pallas_call | solution.py:595
  57.9 1.0 %finish.1 = (f32[256,512]{1,0:T(8,128)}, f32[1,256]{1,0:T(1,128)}) custom-call(f32[256,512]{1,0:T(8,128)S(1)} %partial_own.1.own_ref, bf16[256,512]{1,0:T(8,128)(2,1)S(1)} %collective-permute-done.30.other_ref, f32[256,512]{1,0:T(8,128)S(1)} %get-tuple-element.129.weight_ref, f32[256,128]{1,0:T(8,128)S(1)} %get-tuple-element.119.refs_1_.gain_ref, ...), custom_call_target="tpu_custom_call" | custom-call | tf_op jit(solution)/shard_map/finish/pallas_call | solution.py:606
  (63 shorter events, 8.6 us)
Async XLA Ops:
  0.6 4.5 %copy-start = (bf16[1,2048,512]{2,1,0:T(8,128)(2,1)S(1)}, bf16[1,2048,512]{2,1,0:T(8,128)(2,1)}, u32[]{:S(2)}) copy-start(bf16[1,2048,512]{2,1,0:T(8,128)(2,1)} %param.11) | copy-start | bytes 6291460
  2.0 6.8 %collective-permute-start = (bf16[16,4608]{1,0:T(8,128)(2,1)S(1)}, bf16[16,4608]{1,0:T(8,128)(2,1)S(1)}, u32[]{:S(2)}, u32[]{:S(2)}) collective-permute-start(bf16[16,4608]{1,0:T(8,128)(2,1)S(1)} %get-tuple-element.70), channel_id=1, source_target_pairs={{0,4},{4,0},{8,12},{12,8},{16,20},{20,16},{24,28},{28,24},{1,5},{5... | collective-permute-start | bytes 442376 | tf_op jit(solution)/shard_map/ppermute | solution.py:521
  2.5 7.7 %collective-permute-start.1 = (bf16[16,4608]{1,0:T(8,128)(2,1)S(1)}, bf16[16,4608]{1,0:T(8,128)(2,1)S(1)}, u32[]{:S(2)}, u32[]{:S(2)}) collective-permute-start(bf16[16,4608]{1,0:T(8,128)(2,1)S(1)} %get-tuple-element.71), channel_id=1, source_target_pairs={{0,8},{4,12},{8,0},{12,4},{16,24},{20,28},{24,16},{28,20},{1,9},{5... | collective-permute-start | bytes 442376 | tf_op jit(solution)/shard_map/ppermute | solution.py:521
  5.1 7.3 %collective-permute-start.2 = (bf16[16,4608]{1,0:T(8,128)(2,1)S(1)}, bf16[16,4608]{1,0:T(8,128)(2,1)S(1)}, u32[]{:S(2)}, u32[]{:S(2)}) collective-permute-start(bf16[16,4608]{1,0:T(8,128)(2,1)S(1)} %get-tuple-element.72), channel_id=1, source_target_pairs={{0,12},{4,8},{8,4},{12,0},{16,28},{20,24},{24,20},{28,16},{1,13},{... | collective-permute-start | bytes 442376 | tf_op jit(solution)/shard_map/ppermute | solution.py:521
  6.9 11.9 %collective-permute-start.4 = (bf16[80,2048]{1,0:T(8,128)(2,1)S(1)}, bf16[80,2048]{1,0:T(8,128)(2,1)S(1)}, u32[]{:S(2)}, u32[]{:S(2)}) collective-permute-start(bf16[80,2048]{1,0:T(8,128)(2,1)S(1)} %get-tuple-element.79), channel_id=1, source_target_pairs={{0,16},{4,20},{8,24},{12,28},{16,0},{20,4},{24,8},{28,12},{1,17},{... | collective-permute-start | bytes 983048 | tf_op jit(solution)/shard_map/ppermute | solution.py:521
  8.7 4.8 %collective-permute-start.5 = (bf16[16,4608]{1,0:T(8,128)(2,1)S(1)}, bf16[16,4608]{1,0:T(8,128)(2,1)S(1)}, u32[]{:S(2)}, u32[]{:S(2)}) collective-permute-start(bf16[16,4608]{1,0:T(8,128)(2,1)S(1)} %get-tuple-element.81), channel_id=1, source_target_pairs={{0,4},{4,0},{8,12},{12,8},{16,20},{20,16},{24,28},{28,24},{1,5},{5... | collective-permute-start | bytes 442376 | tf_op jit(solution)/shard_map/ppermute | solution.py:521
  8.8 7.3 %collective-permute-start.6 = (bf16[16,4608]{1,0:T(8,128)(2,1)S(1)}, bf16[16,4608]{1,0:T(8,128)(2,1)S(1)}, u32[]{:S(2)}, u32[]{:S(2)}) collective-permute-start(bf16[16,4608]{1,0:T(8,128)(2,1)S(1)} %get-tuple-element.82), channel_id=1, source_target_pairs={{0,8},{4,12},{8,0},{12,4},{16,24},{20,28},{24,16},{28,20},{1,9},{5... | collective-permute-start | bytes 442376 | tf_op jit(solution)/shard_map/ppermute | solution.py:521
  10.3 8.5 %collective-permute-start.7 = (bf16[16,4608]{1,0:T(8,128)(2,1)S(1)}, bf16[16,4608]{1,0:T(8,128)(2,1)S(1)}, u32[]{:S(2)}, u32[]{:S(2)}) collective-permute-start(bf16[16,4608]{1,0:T(8,128)(2,1)S(1)} %get-tuple-element.83), channel_id=1, source_target_pairs={{0,12},{4,8},{8,4},{12,0},{16,28},{20,24},{24,20},{28,16},{1,13},{... | collective-permute-start | bytes 442376 | tf_op jit(solution)/shard_map/ppermute | solution.py:521
  12.8 7.7 %collective-permute-start.3 = (bf16[32,2048]{1,0:T(8,128)(2,1)S(1)}, bf16[32,2048]{1,0:T(8,128)(2,1)S(1)}, u32[]{:S(2)}, u32[]{:S(2)}) collective-permute-start(bf16[32,2048]{1,0:T(8,128)(2,1)S(1)} %get-tuple-element.78.refs_7_.refs_6_), channel_id=1, source_target_pairs={{3,2},{7,6},{11,10},{15,14},{19,18},{23,22},{27,26},{31,30}} | collective-permute-start | bytes 393224 | tf_op jit(solution)/shard_map/ppermute | solution.py:550
  13.5 7.7 %collective-permute-start.11 = (bf16[32,2048]{1,0:T(8,128)(2,1)S(1)}, bf16[32,2048]{1,0:T(8,128)(2,1)S(1)}, u32[]{:S(2)}, u32[]{:S(2)}) collective-permute-start(bf16[32,2048]{1,0:T(8,128)(2,1)S(1)} %get-tuple-element.85.refs_5_.refs_7_), channel_id=1, source_target_pairs={{3,2},{7,6},{11,10},{15,14},{19,18},{23,22},{27,26},{31,30}} | collective-permute-start | bytes 393224 | tf_op jit(solution)/shard_map/ppermute | solution.py:550
  19.1 2.8 %collective-permute-start.9 = (bf16[32,2048]{1,0:T(8,128)(2,1)S(1)}, bf16[32,2048]{1,0:T(8,128)(2,1)S(1)}, u32[]{:S(2)}, u32[]{:S(2)}) collective-permute-start(bf16[32,2048]{1,0:T(8,128)(2,1)S(1)} %get-tuple-element.90.refs_7_.refs_6_), channel_id=1, source_target_pairs={{3,2},{7,6},{11,10},{15,14},{19,18},{23,22},{27,26},{31,30}} | collective-permute-start | bytes 393224 | tf_op jit(solution)/shard_map/ppermute | solution.py:550
  19.8 2.8 %collective-permute-start.10 = (bf16[32,2048]{1,0:T(8,128)(2,1)S(1)}, bf16[32,2048]{1,0:T(8,128)(2,1)S(1)}, u32[]{:S(2)}, u32[]{:S(2)}) collective-permute-start(bf16[32,2048]{1,0:T(8,128)(2,1)S(1)} %get-tuple-element.91.refs_6_.refs_7_), channel_id=1, source_target_pairs={{3,2},{7,6},{11,10},{15,14},{19,18},{23,22},{27,26},{31,30}} | collective-permute-start | bytes 393224 | tf_op jit(solution)/shard_map/ppermute | solution.py:550
  20.5 5.6 %collective-permute-start.8 = (bf16[32,2048]{1,0:T(8,128)(2,1)S(1)}, bf16[32,2048]{1,0:T(8,128)(2,1)S(1)}, u32[]{:S(2)}, u32[]{:S(2)}) collective-permute-start(bf16[32,2048]{1,0:T(8,128)(2,1)S(1)} %get-tuple-element.92.refs_7_.refs_8_), channel_id=1, source_target_pairs={{2,1},{6,5},{10,9},{14,13},{18,17},{22,21},{26,25},{30,29}} | collective-permute-start | bytes 393224 | tf_op jit(solution)/shard_map/ppermute | solution.py:550
  21.2 6.2 %collective-permute-start.13 = (bf16[32,2048]{1,0:T(8,128)(2,1)S(1)}, bf16[32,2048]{1,0:T(8,128)(2,1)S(1)}, u32[]{:S(2)}, u32[]{:S(2)}) collective-permute-start(bf16[32,2048]{1,0:T(8,128)(2,1)S(1)} %get-tuple-element.93.refs_6_.refs_9_), channel_id=1, source_target_pairs={{2,1},{6,5},{10,9},{14,13},{18,17},{22,21},{26,25},{30,29}} | collective-permute-start | bytes 393224 | tf_op jit(solution)/shard_map/ppermute | solution.py:550
  21.9 6.8 %collective-permute-start.15 = (bf16[32,2048]{1,0:T(8,128)(2,1)S(1)}, bf16[32,2048]{1,0:T(8,128)(2,1)S(1)}, u32[]{:S(2)}, u32[]{:S(2)}) collective-permute-start(bf16[32,2048]{1,0:T(8,128)(2,1)S(1)} %get-tuple-element.94.refs_7_.refs_8_), channel_id=1, source_target_pairs={{2,1},{6,5},{10,9},{14,13},{18,17},{22,21},{26,25},{30,29}} | collective-permute-start | bytes 393224 | tf_op jit(solution)/shard_map/ppermute | solution.py:550
  22.7 7.4 %collective-permute-start.16 = (bf16[32,2048]{1,0:T(8,128)(2,1)S(1)}, bf16[32,2048]{1,0:T(8,128)(2,1)S(1)}, u32[]{:S(2)}, u32[]{:S(2)}) collective-permute-start(bf16[32,2048]{1,0:T(8,128)(2,1)S(1)} %get-tuple-element.95.refs_6_.after_ref.refs_0_.refs_9_), channel_id=1, source_target_pairs={{2,1},{6,5},{10,9},{14,13},{18,17},{22,21},{26,25},{30,29}} | collective-permute-start | bytes 393224 | tf_op jit(solution)/shard_map/ppermute | solution.py:550
  23.5 7.9 %collective-permute-start.20 = (bf16[128,512]{1,0:T(8,128)(2,1)S(1)}, bf16[128,512]{1,0:T(8,128)(2,1)S(1)}, u32[]{:S(2)}, u32[]{:S(2)}) collective-permute-start(bf16[128,512]{1,0:T(8,128)(2,1)S(1)} %columns6.1), channel_id=1, source_target_pairs={{0,24},{4,28},{8,16},{12,20},{16,8},{20,12},{24,0},{28,4},{1,25},{... | collective-permute-start | bytes 393224 | tf_op jit(solution)/shard_map/ppermute | solution.py:521
  26.1 10.9 %collective-permute-start.12 = (bf16[32,2048]{1,0:T(8,128)(2,1)S(1)}, bf16[32,2048]{1,0:T(8,128)(2,1)S(1)}, u32[]{:S(2)}, u32[]{:S(2)}) collective-permute-start(bf16[32,2048]{1,0:T(8,128)(2,1)S(1)} %get-tuple-element.96.refs_7_.refs_10_), channel_id=1, source_target_pairs={{1,0},{5,4},{9,8},{13,12},{17,16},{21,20},{25,24},{29,28}} | collective-permute-start | bytes 393224 | tf_op jit(solution)/shard_map/ppermute | solution.py:550
  27.4 12.3 %collective-permute-start.14 = (bf16[32,2048]{1,0:T(8,128)(2,1)S(1)}, bf16[32,2048]{1,0:T(8,128)(2,1)S(1)}, u32[]{:S(2)}, u32[]{:S(2)}) collective-permute-start(bf16[32,2048]{1,0:T(8,128)(2,1)S(1)} %get-tuple-element.97.refs_6_.refs_11_), channel_id=1, source_target_pairs={{1,0},{5,4},{9,8},{13,12},{17,16},{21,20},{25,24},{29,28}} | collective-permute-start | bytes 393224 | tf_op jit(solution)/shard_map/ppermute | solution.py:550
  28.8 14.9 %collective-permute-start.18 = (bf16[32,2048]{1,0:T(8,128)(2,1)S(1)}, bf16[32,2048]{1,0:T(8,128)(2,1)S(1)}, u32[]{:S(2)}, u32[]{:S(2)}) collective-permute-start(bf16[32,2048]{1,0:T(8,128)(2,1)S(1)} %get-tuple-element.104.refs_7_.refs_10_), channel_id=1, source_target_pairs={{1,0},{5,4},{9,8},{13,12},{17,16},{21,20},{25,24},{29,28}} | collective-permute-start | bytes 393224 | tf_op jit(solution)/shard_map/ppermute | solution.py:550
  30.1 15.3 %collective-permute-start.19 = (bf16[32,2048]{1,0:T(8,128)(2,1)S(1)}, bf16[32,2048]{1,0:T(8,128)(2,1)S(1)}, u32[]{:S(2)}, u32[]{:S(2)}) collective-permute-start(bf16[32,2048]{1,0:T(8,128)(2,1)S(1)} %get-tuple-element.105.refs_12_.refs_0_.refs_11_), channel_id=1, source_target_pairs={{1,0},{5,4},{9,8},{13,12},{17,16},{21,20},{25,24},{29,28}} | collective-permute-start | bytes 393224 | tf_op jit(solution)/shard_map/ppermute | solution.py:550
  31.5 14.0 %collective-permute-start.21 = (bf16[128,512]{1,0:T(8,128)(2,1)S(1)}, bf16[128,512]{1,0:T(8,128)(2,1)S(1)}, u32[]{:S(2)}, u32[]{:S(2)}) collective-permute-start(bf16[128,512]{1,0:T(8,128)(2,1)S(1)} %columns2.1), channel_id=1, source_target_pairs={{0,8},{4,12},{8,0},{12,4},{16,24},{20,28},{24,16},{28,20},{1,9},{5... | collective-permute-start | bytes 393224 | tf_op jit(solution)/shard_map/ppermute | solution.py:521
  40.7 8.7 %collective-permute-start.23 = (bf16[64,512]{1,0:T(8,128)(2,1)S(1)}, bf16[64,512]{1,0:T(8,128)(2,1)S(1)}, u32[]{:S(2)}, u32[]{:S(2)}) collective-permute-start(bf16[64,512]{1,0:T(8,128)(2,1)S(1)} %get-tuple-element.118.refs_17_.refs_0_), channel_id=1, source_target_pairs={{0,24},{4,28},{8,16},{12,20},{16,8},{20,12},{24,0},{28,4},{1,25},{... | collective-permute-start | bytes 196616 | tf_op jit(solution)/shard_map/ppermute | solution.py:521
  43.2 6.8 %collective-permute-start.17 = (bf16[48,2048]{1,0:T(8,128)(2,1)S(1)}, bf16[48,2048]{1,0:T(8,128)(2,1)S(1)}, u32[]{:S(2)}, u32[]{:S(2)}) collective-permute-start(bf16[48,2048]{1,0:T(8,128)(2,1)S(1)} %get-tuple-element.108), channel_id=1, source_target_pairs={{0,8},{4,12},{8,0},{12,4},{16,24},{20,28},{24,16},{28,20},{1,9},{5... | collective-permute-start | bytes 589832 | tf_op jit(solution)/shard_map/ppermute | solution.py:521
  43.7 7.0 %collective-permute-start.22 = (bf16[192,512]{1,0:T(8,128)(2,1)S(1)}, bf16[192,512]{1,0:T(8,128)(2,1)S(1)}, u32[]{:S(2)}, u32[]{:S(2)}) collective-permute-start(bf16[192,512]{1,0:T(8,128)(2,1)S(1)} %columns4.1), channel_id=1, source_target_pairs={{0,16},{4,20},{8,24},{12,28},{16,0},{20,4},{24,8},{28,12},{1,17},{... | collective-permute-start | bytes 589832 | tf_op jit(solution)/shard_map/ppermute | solution.py:521
  46.3 5.3 %collective-permute-start.24 = (bf16[64,512]{1,0:T(8,128)(2,1)S(1)}, bf16[64,512]{1,0:T(8,128)(2,1)S(1)}, u32[]{:S(2)}, u32[]{:S(2)}) collective-permute-start(bf16[64,512]{1,0:T(8,128)(2,1)S(1)} %get-tuple-element.120.refs_1_), channel_id=1, source_target_pairs={{0,24},{4,28},{8,16},{12,20},{16,8},{20,12},{24,0},{28,4},{1,25},{... | collective-permute-start | bytes 196616 | tf_op jit(solution)/shard_map/ppermute | solution.py:521
  48.8 4.8 %collective-permute-start.29 = (bf16[64,512]{1,0:T(8,128)(2,1)S(1)}, bf16[64,512]{1,0:T(8,128)(2,1)S(1)}, u32[]{:S(2)}, u32[]{:S(2)}) collective-permute-start(bf16[64,512]{1,0:T(8,128)(2,1)S(1)} %get-tuple-element.120.refs_1_), channel_id=1, source_target_pairs={{0,16},{4,20},{8,24},{12,28},{16,0},{20,4},{24,8},{28,12},{1,17},{... | collective-permute-start | bytes 196616 | tf_op jit(solution)/shard_map/ppermute | solution.py:521
  49.3 7.4 %collective-permute-start.26 = (bf16[32,2048]{1,0:T(8,128)(2,1)S(1)}, bf16[32,2048]{1,0:T(8,128)(2,1)S(1)}, u32[]{:S(2)}, u32[]{:S(2)}) collective-permute-start(bf16[32,2048]{1,0:T(8,128)(2,1)S(1)} %get-tuple-element.123), channel_id=1, source_target_pairs={{0,4},{4,0},{8,12},{12,8},{16,20},{20,16},{24,28},{28,24},{1,5},{5... | collective-permute-start | bytes 393224 | tf_op jit(solution)/shard_map/ppermute | solution.py:521
  50.0 5.9 %collective-permute-start.27 = (bf16[32,2048]{1,0:T(8,128)(2,1)S(1)}, bf16[32,2048]{1,0:T(8,128)(2,1)S(1)}, u32[]{:S(2)}, u32[]{:S(2)}) collective-permute-start(bf16[32,2048]{1,0:T(8,128)(2,1)S(1)} %get-tuple-element.124), channel_id=1, source_target_pairs={{0,8},{4,12},{8,0},{12,4},{16,24},{20,28},{24,16},{28,20},{1,9},{5... | collective-permute-start | bytes 393224 | tf_op jit(solution)/shard_map/ppermute | solution.py:521
  50.7 6.0 %collective-permute-start.28 = (bf16[16,2048]{1,0:T(8,128)(2,1)S(1)}, bf16[16,2048]{1,0:T(8,128)(2,1)S(1)}, u32[]{:S(2)}, u32[]{:S(2)}) collective-permute-start(bf16[16,2048]{1,0:T(8,128)(2,1)S(1)} %get-tuple-element.125), channel_id=1, source_target_pairs={{0,12},{4,8},{8,4},{12,0},{16,28},{20,24},{24,20},{28,16},{1,13},{... | collective-permute-start | bytes 196616 | tf_op jit(solution)/shard_map/ppermute | solution.py:521
  51.6 5.1 %collective-permute-start.25 = (bf16[16,2048]{1,0:T(8,128)(2,1)S(1)}, bf16[16,2048]{1,0:T(8,128)(2,1)S(1)}, u32[]{:S(2)}, u32[]{:S(2)}) collective-permute-start(bf16[16,2048]{1,0:T(8,128)(2,1)S(1)} %get-tuple-element.121), channel_id=1, source_target_pairs={{0,4},{4,0},{8,12},{12,8},{16,20},{20,16},{24,28},{28,24},{1,5},{5... | collective-permute-start | bytes 196616 | tf_op jit(solution)/shard_map/ppermute | solution.py:521
  56.3 1.6 %collective-permute-start.30 = (bf16[256,512]{1,0:T(8,128)(2,1)S(1)}, bf16[256,512]{1,0:T(8,128)(2,1)S(1)}, u32[]{:S(2)}, u32[]{:S(2)}) collective-permute-start(bf16[256,512]{1,0:T(8,128)(2,1)S(1)} %partial_other.1.refs_10_), channel_id=1, source_target_pairs={{0,4},{4,0},{8,12},{12,8},{16,20},{20,16},{24,28},{28,24},{1,5},{5... | collective-permute-start | bytes 786440 | tf_op jit(solution)/shard_map/ppermute | solution.py:521
  (1 other events, 4.5 us)

commit v17 on v16

--- a/solution.py
+++ b/solution.py
@@ -422,7 +422,7 @@
         in_specs=[VMEM] * (2 + len(came)) + [ANY] * len(after),
         out_specs=(VMEM,) * len(outs),
         name=f"columns{distance}",
-        **params(0.0 if distance else 2.5),
+        **params(0.0 if distance else 1.0),
     )(blocks[0][3], blocks[1][3], *came, *after)
     return results if distance == 0 else results[0]
 
@@ -586,7 +586,7 @@
     own_value, own_values, *rows = done[3]
     rows = [rows[0]] + [swap(rows[k], k) for k in range(1, half)]
     far_value, across_value = swap(own_value, 6), swap(own_value, 4)
-    columns[0], handed = columns_for(0, blocks, [own_value, columns[4], far_first, far_value], [first_rows])
+    columns[0], handed = columns_for(0, blocks, [own_value, columns[4], far_first], [first_rows])
     handed = swap(handed, 1)
     values = [own_values, first_rows, rows[2], across_value, far_first, far_value]
     other = partial_sums(shares, piece, True, columns, values)

time: 59.9 us -> 58.9 us (0.983)
  starting transfers between devices: 30.3 us -> 28.3 us
  waiting for transfers between devices: 17.6 us -> 18.9 us
    ppermute x19, starting transfers between devices: 19.8 us -> 17.8 us  [swap(): return lax.ppermute(array, 'dp', [(i, i ^ k) for i in range(replicas)])]
    ppermute x19, waiting for transfers between devices: 10.2 us -> 11.5 us  [swap(): return lax.ppermute(array, 'dp', [(i, i ^ k) for i in range(replicas)])]
where the time goes in v17:
time: 58.9 us; the launch traced here: 58.2 us
  starting transfers between devices  28.3 us (48%)
  waiting for transfers between devices  18.9 us (32%)
  Pallas kernels  9.89 us (17%)
  between operations  1.06 us (2%)
    ppermute x19, starting transfers between devices, swap(): return lax.ppermute(array, 'dp', [(i, i ^ k) for i in range(replicas)])  17.8 us
    ppermute x19, waiting for transfers between devices, swap(): return lax.ppermute(array, 'dp', [(i, i ^ k) for i in range(replicas)])  11.5 us
    ppermute x12, starting transfers between devices, direct(): lax.ppermute(unit[-1][0], 'section', hop)  10.5 us
    ppermute x12, waiting for transfers between devices, direct(): lax.ppermute(unit[-1][0], 'section', hop)  7.37 us
    pallas_call x16, Pallas kernels, tick_step(): pl.pallas_call(functools.partial(tick_kernel, tick, EARLY if low else LAT...  3.43 us
    pallas_call x2, Pallas kernels, pack(): pl.pallas_call(functools.partial(pack_kernel, block, half, piece), out_sh...  3.06 us
  transfers between devices with their start and end apart: 31, of which 10 were waited for; matrix products, arithmetic and copies ran while one was open for 0% of the time, Pallas kernels for 13%

profile of v17, /device:TPU:0, one launch (start us, length us, event | category | flops | bytes accessed | tf_op | source)
XLA Modules:
  0.0 58.2 jit_solution(13139801076827726479)
XLA Ops:
  0.7 1.4 %pack.2 = (bf16[16,4608]{1,0:T(8,128)(2,1)S(1)}, bf16[16,4608]{1,0:T(8,128)(2,1)S(1)}, bf16[16,4608]{1,0:T(8,128)(2,1)S(1)}, bf16[16,4608]{1,0:T(8,128)(2,1)S(1)}, bf16[80,2048]{1,0:T(8,128)(2,1)S(1)}) custom-call(bf16[128,2048]{1,0:T(8,128)(2,1)} %bitcast.8, bf16[128,512]{1,0:T(8,128)(2,1)} %bitcast.13, bf16[128,2048]{1,0:T(8,128)(2,1)} %bitcast.10, ...), custom_call_target="tpu_custom_call" | custom-call | flops 1380000000 | tf_op jit(solution)/shard_map/pack/pallas_call | solution.py:383
  2.5 2.6 %collective-permute-start.1 = (bf16[16,4608]{1,0:T(8,128)(2,1)S(1)}, bf16[16,4608]{1,0:T(8,128)(2,1)S(1)}, u32[]{:S(2)}, u32[]{:S(2)}) collective-permute-start(bf16[16,4608]{1,0:T(8,128)(2,1)S(1)} %get-tuple-element.71), channel_id=1, source_target_pairs={{0,8},{4,12},{8,0},{12,4},{16,24},{20,28},{24,16},{28,20},{1,9},{5... | collective-permute-start | bytes 442376 | tf_op jit(solution)/shard_map/ppermute | solution.py:521
  5.2 1.7 %pack.3 = (f32[1,2048]{1,0:T(1,128)S(1)}, bf16[512,2048]{1,0:T(8,128)(2,1)S(1)}, bf16[16,4608]{1,0:T(8,128)(2,1)S(1)}, bf16[16,4608]{1,0:T(8,128)(2,1)S(1)}, bf1...) custom-call(bf16[128,2048]{1,0:T(8,128)(2,1)} %bitcast.9, ...), custom_call_target="tpu_custom_call" | custom-call | flops 1380000000 | tf_op jit(solution)/shard_map/pack/pallas_call | solution.py:383
  6.9 1.8 %collective-permute-start.4 = (bf16[80,2048]{1,0:T(8,128)(2,1)S(1)}, bf16[80,2048]{1,0:T(8,128)(2,1)S(1)}, u32[]{:S(2)}, u32[]{:S(2)}) collective-permute-start(bf16[80,2048]{1,0:T(8,128)(2,1)S(1)} %get-tuple-element.79), channel_id=1, source_target_pairs={{0,16},{4,20},{8,24},{12,28},{16,0},{20,4},{24,8},{28,12},{1,17},{... | collective-permute-start | bytes 983048 | tf_op jit(solution)/shard_map/ppermute | solution.py:521
  8.8 1.5 %collective-permute-start.6 = (bf16[16,4608]{1,0:T(8,128)(2,1)S(1)}, bf16[16,4608]{1,0:T(8,128)(2,1)S(1)}, u32[]{:S(2)}, u32[]{:S(2)}) collective-permute-start(bf16[16,4608]{1,0:T(8,128)(2,1)S(1)} %get-tuple-element.82), channel_id=1, source_target_pairs={{0,8},{4,12},{8,0},{12,4},{16,24},{20,28},{24,16},{28,20},{1,9},{5... | collective-permute-start | bytes 442376 | tf_op jit(solution)/shard_map/ppermute | solution.py:521
  10.6 1.9 %collective-permute-done.2.refs_3_ = bf16[16,4608]{1,0:T(8,128)(2,1)S(1)} collective-permute-done((bf16[16,4608]{1,0:T(8,128)(2,1)S(1)}, bf16[16,4608]{1,0:T(8,128)(2,1)S(1)}, u32[]{:S(2)}, u32[]{:S(2)}) %collective-permute-start.2) | collective-permute-done | bytes 147488 | tf_op jit(solution)/shard_map/ppermute | solution.py:521
  12.8 0.7 %collective-permute-start.3 = (bf16[32,2048]{1,0:T(8,128)(2,1)S(1)}, bf16[32,2048]{1,0:T(8,128)(2,1)S(1)}, u32[]{:S(2)}, u32[]{:S(2)}) collective-permute-start(bf16[32,2048]{1,0:T(8,128)(2,1)S(1)} %get-tuple-element.78.refs_7_.refs_6_), channel_id=1, source_target_pairs={{3,2},{7,6},{11,10},{15,14},{19,18},{23,22},{27,26},{31,30}} | collective-permute-start | bytes 393224 | tf_op jit(solution)/shard_map/ppermute | solution.py:550
  13.5 0.7 %collective-permute-start.11 = (bf16[32,2048]{1,0:T(8,128)(2,1)S(1)}, bf16[32,2048]{1,0:T(8,128)(2,1)S(1)}, u32[]{:S(2)}, u32[]{:S(2)}) collective-permute-start(bf16[32,2048]{1,0:T(8,128)(2,1)S(1)} %get-tuple-element.85.refs_5_.refs_7_), channel_id=1, source_target_pairs={{3,2},{7,6},{11,10},{15,14},{19,18},{23,22},{27,26},{31,30}} | collective-permute-start | bytes 393224 | tf_op jit(solution)/shard_map/ppermute | solution.py:550
  14.2 1.9 %collective-permute-done.6.refs_2_ = bf16[16,4608]{1,0:T(8,128)(2,1)S(1)} collective-permute-done((bf16[16,4608]{1,0:T(8,128)(2,1)S(1)}, bf16[16,4608]{1,0:T(8,128)(2,1)S(1)}, u32[]{:S(2)}, u32[]{:S(2)}) %collective-permute-start.6) | collective-permute-done | bytes 147488 | tf_op jit(solution)/shard_map/ppermute | solution.py:521
  16.1 2.6 %collective-permute-done.7.refs_3_ = bf16[16,4608]{1,0:T(8,128)(2,1)S(1)} collective-permute-done((bf16[16,4608]{1,0:T(8,128)(2,1)S(1)}, bf16[16,4608]{1,0:T(8,128)(2,1)S(1)}, u32[]{:S(2)}, u32[]{:S(2)}) %collective-permute-start.7) | collective-permute-done | bytes 147488 | tf_op jit(solution)/shard_map/ppermute | solution.py:521
  19.1 0.7 %collective-permute-start.9 = (bf16[32,2048]{1,0:T(8,128)(2,1)S(1)}, bf16[32,2048]{1,0:T(8,128)(2,1)S(1)}, u32[]{:S(2)}, u32[]{:S(2)}) collective-permute-start(bf16[32,2048]{1,0:T(8,128)(2,1)S(1)} %get-tuple-element.90.refs_7_.refs_6_), channel_id=1, source_target_pairs={{3,2},{7,6},{11,10},{15,14},{19,18},{23,22},{27,26},{31,30}} | collective-permute-start | bytes 393224 | tf_op jit(solution)/shard_map/ppermute | solution.py:550
  19.8 0.7 %collective-permute-start.10 = (bf16[32,2048]{1,0:T(8,128)(2,1)S(1)}, bf16[32,2048]{1,0:T(8,128)(2,1)S(1)}, u32[]{:S(2)}, u32[]{:S(2)}) collective-permute-start(bf16[32,2048]{1,0:T(8,128)(2,1)S(1)} %get-tuple-element.91.refs_6_.refs_7_), channel_id=1, source_target_pairs={{3,2},{7,6},{11,10},{15,14},{19,18},{23,22},{27,26},{31,30}} | collective-permute-start | bytes 393224 | tf_op jit(solution)/shard_map/ppermute | solution.py:550
  21.2 0.7 %collective-permute-start.13 = (bf16[32,2048]{1,0:T(8,128)(2,1)S(1)}, bf16[32,2048]{1,0:T(8,128)(2,1)S(1)}, u32[]{:S(2)}, u32[]{:S(2)}) collective-permute-start(bf16[32,2048]{1,0:T(8,128)(2,1)S(1)} %get-tuple-element.93.refs_6_.refs_9_), channel_id=1, source_target_pairs={{2,1},{6,5},{10,9},{14,13},{18,17},{22,21},{26,25},{30,29}} | collective-permute-start | bytes 393224 | tf_op jit(solution)/shard_map/ppermute | solution.py:550
  23.5 2.6 %collective-permute-start.20 = (bf16[128,512]{1,0:T(8,128)(2,1)S(1)}, bf16[128,512]{1,0:T(8,128)(2,1)S(1)}, u32[]{:S(2)}, u32[]{:S(2)}) collective-permute-start(bf16[128,512]{1,0:T(8,128)(2,1)S(1)} %columns6.1), channel_id=1, source_target_pairs={{0,24},{4,28},{8,16},{12,20},{16,8},{20,12},{24,0},{28,4},{1,25},{... | collective-permute-start | bytes 393224 | tf_op jit(solution)/shard_map/ppermute | solution.py:521
  26.1 1.3 %collective-permute-start.12 = (bf16[32,2048]{1,0:T(8,128)(2,1)S(1)}, bf16[32,2048]{1,0:T(8,128)(2,1)S(1)}, u32[]{:S(2)}, u32[]{:S(2)}) collective-permute-start(bf16[32,2048]{1,0:T(8,128)(2,1)S(1)} %get-tuple-element.96.refs_7_.refs_10_), channel_id=1, source_target_pairs={{1,0},{5,4},{9,8},{13,12},{17,16},{21,20},{25,24},{29,28}} | collective-permute-start | bytes 393224 | tf_op jit(solution)/shard_map/ppermute | solution.py:550
  27.4 1.3 %collective-permute-start.14 = (bf16[32,2048]{1,0:T(8,128)(2,1)S(1)}, bf16[32,2048]{1,0:T(8,128)(2,1)S(1)}, u32[]{:S(2)}, u32[]{:S(2)}) collective-permute-start(bf16[32,2048]{1,0:T(8,128)(2,1)S(1)} %get-tuple-element.97.refs_6_.refs_11_), channel_id=1, source_target_pairs={{1,0},{5,4},{9,8},{13,12},{17,16},{21,20},{25,24},{29,28}} | collective-permute-start | bytes 393224 | tf_op jit(solution)/shard_map/ppermute | solution.py:550
  28.8 1.3 %collective-permute-start.18 = (bf16[32,2048]{1,0:T(8,128)(2,1)S(1)}, bf16[32,2048]{1,0:T(8,128)(2,1)S(1)}, u32[]{:S(2)}, u32[]{:S(2)}) collective-permute-start(bf16[32,2048]{1,0:T(8,128)(2,1)S(1)} %get-tuple-element.104.refs_7_.refs_10_), channel_id=1, source_target_pairs={{1,0},{5,4},{9,8},{13,12},{17,16},{21,20},{25,24},{29,28}} | collective-permute-start | bytes 393224 | tf_op jit(solution)/shard_map/ppermute | solution.py:550
  30.1 1.3 %collective-permute-start.19 = (bf16[32,2048]{1,0:T(8,128)(2,1)S(1)}, bf16[32,2048]{1,0:T(8,128)(2,1)S(1)}, u32[]{:S(2)}, u32[]{:S(2)}) collective-permute-start(bf16[32,2048]{1,0:T(8,128)(2,1)S(1)} %get-tuple-element.105.refs_12_.refs_0_.refs_11_), channel_id=1, source_target_pairs={{1,0},{5,4},{9,8},{13,12},{17,16},{21,20},{25,24},{29,28}} | collective-permute-start | bytes 393224 | tf_op jit(solution)/shard_map/ppermute | solution.py:550
  32.1 4.9 %collective-permute-done.12.refs_0_ = bf16[32,2048]{1,0:T(8,128)(2,1)S(1)} collective-permute-done((bf16[32,2048]{1,0:T(8,128)(2,1)S(1)}, bf16[32,2048]{1,0:T(8,128)(2,1)S(1)}, u32[]{:S(2)}, u32[]{:S(2)}) %collective-permute-start.12) | collective-permute-done | bytes 131104 | tf_op jit(solution)/shard_map/ppermute | solution.py:550
  37.0 0.8 %tick3_a_late.1 = (bf16[32,2048]{1,0:T(8,128)(2,1)S(1)}, bf16[32,512]{1,0:T(8,128)(2,1)S(1)}) custom-call(bf16[32,2048]{1,0:T(8,128)(2,1)S(1)} %collective-permute-done.12.refs_0_, bf16[4,32,128]{2,1,0:T(8,128)(2,1)S(1)} %get-tuple-element.73.refs_1_, f32[64,128]{1,0:T(8,128)S(1)} %get-tuple-element.74.refs_2_.refs_3_, ...), custom_call_target="tpu_custom_call" | custom-call | flops 1150000000 | tf_op jit(solution)/shard_map/tick3_a_late/pallas_call | solution.py:319
  37.8 2.0 %collective-permute-done.14.refs_1_ = bf16[32,2048]{1,0:T(8,128)(2,1)S(1)} collective-permute-done((bf16[32,2048]{1,0:T(8,128)(2,1)S(1)}, bf16[32,2048]{1,0:T(8,128)(2,1)S(1)}, u32[]{:S(2)}, u32[]{:S(2)}) %collective-permute-start.14) | collective-permute-done | bytes 131104 | tf_op jit(solution)/shard_map/ppermute | solution.py:550
  39.8 0.8 %tick3_a_early.1 = (bf16[32,2048]{1,0:T(8,128)(2,1)S(1)}, bf16[64,512]{1,0:T(8,128)(2,1)S(1)}, bf16[48,2048]{1,0:T(8,128)(2,1)S(1)}) custom-call(bf16[32,2048]{1,0:T(8,128)(2,1)S(1)} %collective-permute-done.12.refs_0_, bf16[32,2048]{1,0:T(8,128)(2,1)S(1)} %collective-permute-done.14.refs_1_, bf16[4,32,256]{2,1,0:T(8,128)(2,1)S(1)} %get-tuple-element.84.refs_2_, ...), custom_call_target="tpu_custom_call" | custom-call | flops 1150000000 | tf_op jit(solution)/shard_map/tick3_a_early/pallas_call | solution.py:319
  40.7 2.5 %collective-permute-start.23 = (bf16[64,512]{1,0:T(8,128)(2,1)S(1)}, bf16[64,512]{1,0:T(8,128)(2,1)S(1)}, u32[]{:S(2)}, u32[]{:S(2)}) collective-permute-start(bf16[64,512]{1,0:T(8,128)(2,1)S(1)} %get-tuple-element.118.refs_17_.refs_0_), channel_id=1, source_target_pairs={{0,24},{4,28},{8,16},{12,20},{16,8},{20,12},{24,0},{28,4},{1,25},{... | collective-permute-start | bytes 196616 | tf_op jit(solution)/shard_map/ppermute | solution.py:521
  44.2 0.8 %tick3_b_late.1 = (bf16[32,2048]{1,0:T(8,128)(2,1)S(1)}, bf16[32,512]{1,0:T(8,128)(2,1)S(1)}) custom-call(bf16[32,2048]{1,0:T(8,128)(2,1)S(1)} %collective-permute-done.18.refs_0_, bf16[4,32,128]{2,1,0:T(8,128)(2,1)S(1)} %get-tuple-element.89.refs_1_, f32[64,128]{1,0:T(8,128)S(1)} %get-tuple-element.87.refs_2_.refs_3_, ...), custom_call_target="tpu_custom_call" | custom-call | flops 1150000000 | tf_op jit(solution)/shard_map/tick3_b_late/pallas_call | solution.py:319
  45.4 0.9 %tick3_b_early.1 = (bf16[64,512]{1,0:T(8,128)(2,1)S(1)}, bf16[128,512]{1,0:T(8,128)(2,1)S(1)}, bf16[32,2048]{1,0:T(8,128)(2,1)S(1)}, bf16[32,2048]{1,0:T(8,128)(...) custom-call(bf16[32,2048]{1,0:T(8,128)(2,1)S(1)} %collective-permute-done.18.refs_0_, ...), custom_call_target="tpu_custom_call" | custom-call | flops 1150000000 | tf_op jit(solution)/shard_map/tick3_b_early/pallas_call | solution.py:319
  46.3 1.6 %collective-permute-start.26 = (bf16[32,2048]{1,0:T(8,128)(2,1)S(1)}, bf16[32,2048]{1,0:T(8,128)(2,1)S(1)}, u32[]{:S(2)}, u32[]{:S(2)}) collective-permute-start(bf16[32,2048]{1,0:T(8,128)(2,1)S(1)} %get-tuple-element.124), channel_id=1, source_target_pairs={{0,8},{4,12},{8,0},{12,4},{16,24},{20,28},{24,16},{28,20},{1,9},{5... | collective-permute-start | bytes 393224 | tf_op jit(solution)/shard_map/ppermute | solution.py:521
  47.8 1.5 %collective-permute-start.28 = (bf16[64,512]{1,0:T(8,128)(2,1)S(1)}, bf16[64,512]{1,0:T(8,128)(2,1)S(1)}, u32[]{:S(2)}, u32[]{:S(2)}) collective-permute-start(bf16[64,512]{1,0:T(8,128)(2,1)S(1)} %get-tuple-element.120.refs_1_), channel_id=1, source_target_pairs={{0,16},{4,20},{8,24},{12,28},{16,0},{20,4},{24,8},{28,12},{1,17},{... | collective-permute-start | bytes 196616 | tf_op jit(solution)/shard_map/ppermute | solution.py:521
  49.8 1.2 %collective-permute-done.17.refs_0_.first_rows_ref.refs_5_ = bf16[48,2048]{1,0:T(8,128)(2,1)S(1)} collective-permute-done((bf16[48,2048]{1,0:T(8,128)(2,1)S(1)}, bf16[48,2048]{1,0:T(8,128)(2,1)S(1)}, u32[]{:S(2)}, u32[]{:S(2)}) %collective-permute-start.17) | collective-permute-done | bytes 196640 | tf_op jit(solution)/shard_map/ppermute | solution.py:521
  51.6 0.9 %collective-permute-done.28.refs_7_ = bf16[64,512]{1,0:T(8,128)(2,1)S(1)} collective-permute-done((bf16[64,512]{1,0:T(8,128)(2,1)S(1)}, bf16[64,512]{1,0:T(8,128)(2,1)S(1)}, u32[]{:S(2)}, u32[]{:S(2)}) %collective-permute-start.28) | collective-permute-done | bytes 65568 | tf_op jit(solution)/shard_map/ppermute | solution.py:521
  52.5 2.7 %collective-permute-done.29.refs_9_ = bf16[64,512]{1,0:T(8,128)(2,1)S(1)} collective-permute-done((bf16[64,512]{1,0:T(8,128)(2,1)S(1)}, bf16[64,512]{1,0:T(8,128)(2,1)S(1)}, u32[]{:S(2)}, u32[]{:S(2)}) %collective-permute-start.29) | collective-permute-done | bytes 65568 | tf_op jit(solution)/shard_map/ppermute | solution.py:521
  56.0 0.8 %rows.1 = (bf16[128,2048]{1,0:T(8,128)(2,1)}, f32[8,128]{1,0:T(8,128)S(1)}) custom-call(bf16[48,2048]{1,0:T(8,128)(2,1)S(1)} %collective-permute-done.17.refs_0_.first_rows_ref.refs_5_, bf16[16,2048]{1,0:T(8,128)(2,1)S(1)} %collective-permute-done.24.handed_ref, bf16[32,2048]{1,0:T(8,128)(2,1)S(1)} %get-tuple-element.122.refs_0_, ...), custom_call_target="tpu_custom_call" | custom-call | flops 2875000064 | tf_op jit(solution)/shard_map/rows/pallas_call | solution.py:595
  57.2 1.0 %finish.1 = (f32[256,512]{1,0:T(8,128)}, f32[1,256]{1,0:T(1,128)}) custom-call(f32[256,512]{1,0:T(8,128)S(1)} %partial_own.1.own_ref, bf16[256,512]{1,0:T(8,128)(2,1)S(1)} %collective-permute-done.30.other_ref, f32[256,512]{1,0:T(8,128)S(1)} %get-tuple-element.129.weight_ref, f32[256,128]{1,0:T(8,128)S(1)} %get-tuple-element.119.refs_1_.gain_ref, ...), custom_call_target="tpu_custom_call" | custom-call | tf_op jit(solution)/shard_map/finish/pallas_call | solution.py:606
  (63 shorter events, 8.2 us)
Async XLA Ops:
  0.6 4.5 %copy-start = (bf16[1,2048,512]{2,1,0:T(8,128)(2,1)S(1)}, bf16[1,2048,512]{2,1,0:T(8,128)(2,1)}, u32[]{:S(2)}) copy-start(bf16[1,2048,512]{2,1,0:T(8,128)(2,1)} %param.11) | copy-start | bytes 6291460
  2.0 6.8 %collective-permute-start = (bf16[16,4608]{1,0:T(8,128)(2,1)S(1)}, bf16[16,4608]{1,0:T(8,128)(2,1)S(1)}, u32[]{:S(2)}, u32[]{:S(2)}) collective-permute-start(bf16[16,4608]{1,0:T(8,128)(2,1)S(1)} %get-tuple-element.70), channel_id=1, source_target_pairs={{0,4},{4,0},{8,12},{12,8},{16,20},{20,16},{24,28},{28,24},{1,5},{5... | collective-permute-start | bytes 442376 | tf_op jit(solution)/shard_map/ppermute | solution.py:521
  2.5 7.7 %collective-permute-start.1 = (bf16[16,4608]{1,0:T(8,128)(2,1)S(1)}, bf16[16,4608]{1,0:T(8,128)(2,1)S(1)}, u32[]{:S(2)}, u32[]{:S(2)}) collective-permute-start(bf16[16,4608]{1,0:T(8,128)(2,1)S(1)} %get-tuple-element.71), channel_id=1, source_target_pairs={{0,8},{4,12},{8,0},{12,4},{16,24},{20,28},{24,16},{28,20},{1,9},{5... | collective-permute-start | bytes 442376 | tf_op jit(solution)/shard_map/ppermute | solution.py:521
  5.1 7.3 %collective-permute-start.2 = (bf16[16,4608]{1,0:T(8,128)(2,1)S(1)}, bf16[16,4608]{1,0:T(8,128)(2,1)S(1)}, u32[]{:S(2)}, u32[]{:S(2)}) collective-permute-start(bf16[16,4608]{1,0:T(8,128)(2,1)S(1)} %get-tuple-element.72), channel_id=1, source_target_pairs={{0,12},{4,8},{8,4},{12,0},{16,28},{20,24},{24,20},{28,16},{1,13},{... | collective-permute-start | bytes 442376 | tf_op jit(solution)/shard_map/ppermute | solution.py:521
  6.9 11.9 %collective-permute-start.4 = (bf16[80,2048]{1,0:T(8,128)(2,1)S(1)}, bf16[80,2048]{1,0:T(8,128)(2,1)S(1)}, u32[]{:S(2)}, u32[]{:S(2)}) collective-permute-start(bf16[80,2048]{1,0:T(8,128)(2,1)S(1)} %get-tuple-element.79), channel_id=1, source_target_pairs={{0,16},{4,20},{8,24},{12,28},{16,0},{20,4},{24,8},{28,12},{1,17},{... | collective-permute-start | bytes 983048 | tf_op jit(solution)/shard_map/ppermute | solution.py:521
  8.7 4.8 %collective-permute-start.5 = (bf16[16,4608]{1,0:T(8,128)(2,1)S(1)}, bf16[16,4608]{1,0:T(8,128)(2,1)S(1)}, u32[]{:S(2)}, u32[]{:S(2)}) collective-permute-start(bf16[16,4608]{1,0:T(8,128)(2,1)S(1)} %get-tuple-element.81), channel_id=1, source_target_pairs={{0,4},{4,0},{8,12},{12,8},{16,20},{20,16},{24,28},{28,24},{1,5},{5... | collective-permute-start | bytes 442376 | tf_op jit(solution)/shard_map/ppermute | solution.py:521
  8.8 7.3 %collective-permute-start.6 = (bf16[16,4608]{1,0:T(8,128)(2,1)S(1)}, bf16[16,4608]{1,0:T(8,128)(2,1)S(1)}, u32[]{:S(2)}, u32[]{:S(2)}) collective-permute-start(bf16[16,4608]{1,0:T(8,128)(2,1)S(1)} %get-tuple-element.82), channel_id=1, source_target_pairs={{0,8},{4,12},{8,0},{12,4},{16,24},{20,28},{24,16},{28,20},{1,9},{5... | collective-permute-start | bytes 442376 | tf_op jit(solution)/shard_map/ppermute | solution.py:521
  10.3 8.5 %collective-permute-start.7 = (bf16[16,4608]{1,0:T(8,128)(2,1)S(1)}, bf16[16,4608]{1,0:T(8,128)(2,1)S(1)}, u32[]{:S(2)}, u32[]{:S(2)}) collective-permute-start(bf16[16,4608]{1,0:T(8,128)(2,1)S(1)} %get-tuple-element.83), channel_id=1, source_target_pairs={{0,12},{4,8},{8,4},{12,0},{16,28},{20,24},{24,20},{28,16},{1,13},{... | collective-permute-start | bytes 442376 | tf_op jit(solution)/shard_map/ppermute | solution.py:521
  12.8 7.7 %collective-permute-start.3 = (bf16[32,2048]{1,0:T(8,128)(2,1)S(1)}, bf16[32,2048]{1,0:T(8,128)(2,1)S(1)}, u32[]{:S(2)}, u32[]{:S(2)}) collective-permute-start(bf16[32,2048]{1,0:T(8,128)(2,1)S(1)} %get-tuple-element.78.refs_7_.refs_6_), channel_id=1, source_target_pairs={{3,2},{7,6},{11,10},{15,14},{19,18},{23,22},{27,26},{31,30}} | collective-permute-start | bytes 393224 | tf_op jit(solution)/shard_map/ppermute | solution.py:550
  13.5 7.7 %collective-permute-start.11 = (bf16[32,2048]{1,0:T(8,128)(2,1)S(1)}, bf16[32,2048]{1,0:T(8,128)(2,1)S(1)}, u32[]{:S(2)}, u32[]{:S(2)}) collective-permute-start(bf16[32,2048]{1,0:T(8,128)(2,1)S(1)} %get-tuple-element.85.refs_5_.refs_7_), channel_id=1, source_target_pairs={{3,2},{7,6},{11,10},{15,14},{19,18},{23,22},{27,26},{31,30}} | collective-permute-start | bytes 393224 | tf_op jit(solution)/shard_map/ppermute | solution.py:550
  19.1 2.8 %collective-permute-start.9 = (bf16[32,2048]{1,0:T(8,128)(2,1)S(1)}, bf16[32,2048]{1,0:T(8,128)(2,1)S(1)}, u32[]{:S(2)}, u32[]{:S(2)}) collective-permute-start(bf16[32,2048]{1,0:T(8,128)(2,1)S(1)} %get-tuple-element.90.refs_7_.refs_6_), channel_id=1, source_target_pairs={{3,2},{7,6},{11,10},{15,14},{19,18},{23,22},{27,26},{31,30}} | collective-permute-start | bytes 393224 | tf_op jit(solution)/shard_map/ppermute | solution.py:550
  19.8 2.8 %collective-permute-start.10 = (bf16[32,2048]{1,0:T(8,128)(2,1)S(1)}, bf16[32,2048]{1,0:T(8,128)(2,1)S(1)}, u32[]{:S(2)}, u32[]{:S(2)}) collective-permute-start(bf16[32,2048]{1,0:T(8,128)(2,1)S(1)} %get-tuple-element.91.refs_6_.refs_7_), channel_id=1, source_target_pairs={{3,2},{7,6},{11,10},{15,14},{19,18},{23,22},{27,26},{31,30}} | collective-permute-start | bytes 393224 | tf_op jit(solution)/shard_map/ppermute | solution.py:550
  20.5 5.6 %collective-permute-start.8 = (bf16[32,2048]{1,0:T(8,128)(2,1)S(1)}, bf16[32,2048]{1,0:T(8,128)(2,1)S(1)}, u32[]{:S(2)}, u32[]{:S(2)}) collective-permute-start(bf16[32,2048]{1,0:T(8,128)(2,1)S(1)} %get-tuple-element.92.refs_7_.refs_8_), channel_id=1, source_target_pairs={{2,1},{6,5},{10,9},{14,13},{18,17},{22,21},{26,25},{30,29}} | collective-permute-start | bytes 393224 | tf_op jit(solution)/shard_map/ppermute | solution.py:550
  21.2 6.2 %collective-permute-start.13 = (bf16[32,2048]{1,0:T(8,128)(2,1)S(1)}, bf16[32,2048]{1,0:T(8,128)(2,1)S(1)}, u32[]{:S(2)}, u32[]{:S(2)}) collective-permute-start(bf16[32,2048]{1,0:T(8,128)(2,1)S(1)} %get-tuple-element.93.refs_6_.refs_9_), channel_id=1, source_target_pairs={{2,1},{6,5},{10,9},{14,13},{18,17},{22,21},{26,25},{30,29}} | collective-permute-start | bytes 393224 | tf_op jit(solution)/shard_map/ppermute | solution.py:550
  21.9 6.8 %collective-permute-start.15 = (bf16[32,2048]{1,0:T(8,128)(2,1)S(1)}, bf16[32,2048]{1,0:T(8,128)(2,1)S(1)}, u32[]{:S(2)}, u32[]{:S(2)}) collective-permute-start(bf16[32,2048]{1,0:T(8,128)(2,1)S(1)} %get-tuple-element.94.refs_7_.refs_8_), channel_id=1, source_target_pairs={{2,1},{6,5},{10,9},{14,13},{18,17},{22,21},{26,25},{30,29}} | collective-permute-start | bytes 393224 | tf_op jit(solution)/shard_map/ppermute | solution.py:550
  22.7 7.4 %collective-permute-start.16 = (bf16[32,2048]{1,0:T(8,128)(2,1)S(1)}, bf16[32,2048]{1,0:T(8,128)(2,1)S(1)}, u32[]{:S(2)}, u32[]{:S(2)}) collective-permute-start(bf16[32,2048]{1,0:T(8,128)(2,1)S(1)} %get-tuple-element.95.refs_6_.after_ref.refs_0_.refs_9_), channel_id=1, source_target_pairs={{2,1},{6,5},{10,9},{14,13},{18,17},{22,21},{26,25},{30,29}} | collective-permute-start | bytes 393224 | tf_op jit(solution)/shard_map/ppermute | solution.py:550
  23.5 7.9 %collective-permute-start.20 = (bf16[128,512]{1,0:T(8,128)(2,1)S(1)}, bf16[128,512]{1,0:T(8,128)(2,1)S(1)}, u32[]{:S(2)}, u32[]{:S(2)}) collective-permute-start(bf16[128,512]{1,0:T(8,128)(2,1)S(1)} %columns6.1), channel_id=1, source_target_pairs={{0,24},{4,28},{8,16},{12,20},{16,8},{20,12},{24,0},{28,4},{1,25},{... | collective-permute-start | bytes 393224 | tf_op jit(solution)/shard_map/ppermute | solution.py:521
  26.1 10.9 %collective-permute-start.12 = (bf16[32,2048]{1,0:T(8,128)(2,1)S(1)}, bf16[32,2048]{1,0:T(8,128)(2,1)S(1)}, u32[]{:S(2)}, u32[]{:S(2)}) collective-permute-start(bf16[32,2048]{1,0:T(8,128)(2,1)S(1)} %get-tuple-element.96.refs_7_.refs_10_), channel_id=1, source_target_pairs={{1,0},{5,4},{9,8},{13,12},{17,16},{21,20},{25,24},{29,28}} | collective-permute-start | bytes 393224 | tf_op jit(solution)/shard_map/ppermute | solution.py:550
  27.4 12.3 %collective-permute-start.14 = (bf16[32,2048]{1,0:T(8,128)(2,1)S(1)}, bf16[32,2048]{1,0:T(8,128)(2,1)S(1)}, u32[]{:S(2)}, u32[]{:S(2)}) collective-permute-start(bf16[32,2048]{1,0:T(8,128)(2,1)S(1)} %get-tuple-element.97.refs_6_.refs_11_), channel_id=1, source_target_pairs={{1,0},{5,4},{9,8},{13,12},{17,16},{21,20},{25,24},{29,28}} | collective-permute-start | bytes 393224 | tf_op jit(solution)/shard_map/ppermute | solution.py:550
  28.8 14.9 %collective-permute-start.18 = (bf16[32,2048]{1,0:T(8,128)(2,1)S(1)}, bf16[32,2048]{1,0:T(8,128)(2,1)S(1)}, u32[]{:S(2)}, u32[]{:S(2)}) collective-permute-start(bf16[32,2048]{1,0:T(8,128)(2,1)S(1)} %get-tuple-element.104.refs_7_.refs_10_), channel_id=1, source_target_pairs={{1,0},{5,4},{9,8},{13,12},{17,16},{21,20},{25,24},{29,28}} | collective-permute-start | bytes 393224 | tf_op jit(solution)/shard_map/ppermute | solution.py:550
  30.1 15.3 %collective-permute-start.19 = (bf16[32,2048]{1,0:T(8,128)(2,1)S(1)}, bf16[32,2048]{1,0:T(8,128)(2,1)S(1)}, u32[]{:S(2)}, u32[]{:S(2)}) collective-permute-start(bf16[32,2048]{1,0:T(8,128)(2,1)S(1)} %get-tuple-element.105.refs_12_.refs_0_.refs_11_), channel_id=1, source_target_pairs={{1,0},{5,4},{9,8},{13,12},{17,16},{21,20},{25,24},{29,28}} | collective-permute-start | bytes 393224 | tf_op jit(solution)/shard_map/ppermute | solution.py:550
  31.5 14.0 %collective-permute-start.21 = (bf16[128,512]{1,0:T(8,128)(2,1)S(1)}, bf16[128,512]{1,0:T(8,128)(2,1)S(1)}, u32[]{:S(2)}, u32[]{:S(2)}) collective-permute-start(bf16[128,512]{1,0:T(8,128)(2,1)S(1)} %columns2.1), channel_id=1, source_target_pairs={{0,8},{4,12},{8,0},{12,4},{16,24},{20,28},{24,16},{28,20},{1,9},{5... | collective-permute-start | bytes 393224 | tf_op jit(solution)/shard_map/ppermute | solution.py:521
  40.7 8.7 %collective-permute-start.23 = (bf16[64,512]{1,0:T(8,128)(2,1)S(1)}, bf16[64,512]{1,0:T(8,128)(2,1)S(1)}, u32[]{:S(2)}, u32[]{:S(2)}) collective-permute-start(bf16[64,512]{1,0:T(8,128)(2,1)S(1)} %get-tuple-element.118.refs_17_.refs_0_), channel_id=1, source_target_pairs={{0,24},{4,28},{8,16},{12,20},{16,8},{20,12},{24,0},{28,4},{1,25},{... | collective-permute-start | bytes 196616 | tf_op jit(solution)/shard_map/ppermute | solution.py:521
  43.2 7.8 %collective-permute-start.17 = (bf16[48,2048]{1,0:T(8,128)(2,1)S(1)}, bf16[48,2048]{1,0:T(8,128)(2,1)S(1)}, u32[]{:S(2)}, u32[]{:S(2)}) collective-permute-start(bf16[48,2048]{1,0:T(8,128)(2,1)S(1)} %get-tuple-element.108), channel_id=1, source_target_pairs={{0,8},{4,12},{8,0},{12,4},{16,24},{20,28},{24,16},{28,20},{1,9},{5... | collective-permute-start | bytes 589832 | tf_op jit(solution)/shard_map/ppermute | solution.py:521
  43.7 7.3 %collective-permute-start.22 = (bf16[192,512]{1,0:T(8,128)(2,1)S(1)}, bf16[192,512]{1,0:T(8,128)(2,1)S(1)}, u32[]{:S(2)}, u32[]{:S(2)}) collective-permute-start(bf16[192,512]{1,0:T(8,128)(2,1)S(1)} %columns4.1), channel_id=1, source_target_pairs={{0,16},{4,20},{8,24},{12,28},{16,0},{20,4},{24,8},{28,12},{1,17},{... | collective-permute-start | bytes 589832 | tf_op jit(solution)/shard_map/ppermute | solution.py:521
  46.3 8.9 %collective-permute-start.26 = (bf16[32,2048]{1,0:T(8,128)(2,1)S(1)}, bf16[32,2048]{1,0:T(8,128)(2,1)S(1)}, u32[]{:S(2)}, u32[]{:S(2)}) collective-permute-start(bf16[32,2048]{1,0:T(8,128)(2,1)S(1)} %get-tuple-element.124), channel_id=1, source_target_pairs={{0,8},{4,12},{8,0},{12,4},{16,24},{20,28},{24,16},{28,20},{1,9},{5... | collective-permute-start | bytes 393224 | tf_op jit(solution)/shard_map/ppermute | solution.py:521
  47.8 4.6 %collective-permute-start.28 = (bf16[64,512]{1,0:T(8,128)(2,1)S(1)}, bf16[64,512]{1,0:T(8,128)(2,1)S(1)}, u32[]{:S(2)}, u32[]{:S(2)}) collective-permute-start(bf16[64,512]{1,0:T(8,128)(2,1)S(1)} %get-tuple-element.120.refs_1_), channel_id=1, source_target_pairs={{0,16},{4,20},{8,24},{12,28},{16,0},{20,4},{24,8},{28,12},{1,17},{... | collective-permute-start | bytes 196616 | tf_op jit(solution)/shard_map/ppermute | solution.py:521
  49.4 5.8 %collective-permute-start.29 = (bf16[64,512]{1,0:T(8,128)(2,1)S(1)}, bf16[64,512]{1,0:T(8,128)(2,1)S(1)}, u32[]{:S(2)}, u32[]{:S(2)}) collective-permute-start(bf16[64,512]{1,0:T(8,128)(2,1)S(1)} %get-tuple-element.120.refs_1_), channel_id=1, source_target_pairs={{0,24},{4,28},{8,16},{12,20},{16,8},{20,12},{24,0},{28,4},{1,25},{... | collective-permute-start | bytes 196616 | tf_op jit(solution)/shard_map/ppermute | solution.py:521
  51.0 5.0 %collective-permute-start.25 = (bf16[32,2048]{1,0:T(8,128)(2,1)S(1)}, bf16[32,2048]{1,0:T(8,128)(2,1)S(1)}, u32[]{:S(2)}, u32[]{:S(2)}) collective-permute-start(bf16[32,2048]{1,0:T(8,128)(2,1)S(1)} %get-tuple-element.123), channel_id=1, source_target_pairs={{0,4},{4,0},{8,12},{12,8},{16,20},{20,16},{24,28},{28,24},{1,5},{5... | collective-permute-start | bytes 393224 | tf_op jit(solution)/shard_map/ppermute | solution.py:521
  51.0 5.0 %collective-permute-start.27 = (bf16[16,2048]{1,0:T(8,128)(2,1)S(1)}, bf16[16,2048]{1,0:T(8,128)(2,1)S(1)}, u32[]{:S(2)}, u32[]{:S(2)}) collective-permute-start(bf16[16,2048]{1,0:T(8,128)(2,1)S(1)} %get-tuple-element.125), channel_id=1, source_target_pairs={{0,12},{4,8},{8,4},{12,0},{16,28},{20,24},{24,20},{28,16},{1,13},{... | collective-permute-start | bytes 196616 | tf_op jit(solution)/shard_map/ppermute | solution.py:521
  52.5 3.5 %collective-permute-start.24 = (bf16[16,2048]{1,0:T(8,128)(2,1)S(1)}, bf16[16,2048]{1,0:T(8,128)(2,1)S(1)}, u32[]{:S(2)}, u32[]{:S(2)}) collective-permute-start(bf16[16,2048]{1,0:T(8,128)(2,1)S(1)} %get-tuple-element.121), channel_id=1, source_target_pairs={{0,4},{4,0},{8,12},{12,8},{16,20},{20,16},{24,28},{28,24},{1,5},{5... | collective-permute-start | bytes 196616 | tf_op jit(solution)/shard_map/ppermute | solution.py:521
  55.5 1.6 %collective-permute-start.30 = (bf16[256,512]{1,0:T(8,128)(2,1)S(1)}, bf16[256,512]{1,0:T(8,128)(2,1)S(1)}, u32[]{:S(2)}, u32[]{:S(2)}) collective-permute-start(bf16[256,512]{1,0:T(8,128)(2,1)S(1)} %partial_other.1.refs_10_), channel_id=1, source_target_pairs={{0,4},{4,0},{8,12},{12,8},{16,20},{20,16},{24,28},{28,24},{1,5},{5... | collective-permute-start | bytes 786440 | tf_op jit(solution)/shard_map/ppermute | solution.py:521
  (1 other events, 4.5 us)

commit v18 on v16

--- a/solution.py
+++ b/solution.py
@@ -422,7 +422,7 @@
         in_specs=[VMEM] * (2 + len(came)) + [ANY] * len(after),
         out_specs=(VMEM,) * len(outs),
         name=f"columns{distance}",
-        **params(0.0 if distance else 2.5),
+        **params(0.0 if distance else 0.8),
     )(blocks[0][3], blocks[1][3], *came, *after)
     return results if distance == 0 else results[0]
 

time: 59.9 us -> 58.3 us (0.973)
  starting transfers between devices: 30.3 us -> 28.6 us
    ppermute x19, starting transfers between devices: 19.8 us -> 18.1 us  [swap(): return lax.ppermute(array, 'dp', [(i, i ^ k) for i in range(replicas)])]
  transfers between devices with their start and end apart: 31 -> 31, of which waited for: 10 -> 12; matrix products, arithmetic and copies ran while one was open for 0% -> 0% of each run, Pallas kernels for 13% -> 13%
where the time goes in v18:
time: 58.3 us; the launch traced here: 57.4 us
  starting transfers between devices  28.6 us (49%)
  waiting for transfers between devices  17.8 us (31%)
  Pallas kernels  9.89 us (17%)
  between operations  1.06 us (2%)
    ppermute x19, starting transfers between devices, swap(): return lax.ppermute(array, 'dp', [(i, i ^ k) for i in range(replicas)])  18.1 us
    ppermute x12, starting transfers between devices, direct(): lax.ppermute(unit[-1][0], 'section', hop)  10.5 us
    ppermute x19, waiting for transfers between devices, swap(): return lax.ppermute(array, 'dp', [(i, i ^ k) for i in range(replicas)])  10.5 us
    ppermute x12, waiting for transfers between devices, direct(): lax.ppermute(unit[-1][0], 'section', hop)  7.37 us
    pallas_call x16, Pallas kernels, tick_step(): pl.pallas_call(functools.partial(tick_kernel, tick, EARLY if low else LAT...  3.43 us
    pallas_call x2, Pallas kernels, pack(): pl.pallas_call(functools.partial(pack_kernel, block, half, piece), out_sh...  3.06 us
  transfers between devices with their start and end apart: 31, of which 12 were waited for; matrix products, arithmetic and copies ran while one was open for 0% of the time, Pallas kernels for 13%

profile of v18, /device:TPU:0, one launch (start us, length us, event | category | flops | bytes accessed | tf_op | source)
XLA Modules:
  0.0 57.4 jit_solution(9189503468786010980)
XLA Ops:
  0.7 1.4 %pack.2 = (bf16[16,4608]{1,0:T(8,128)(2,1)S(1)}, bf16[16,4608]{1,0:T(8,128)(2,1)S(1)}, bf16[16,4608]{1,0:T(8,128)(2,1)S(1)}, bf16[16,4608]{1,0:T(8,128)(2,1)S(1)}, bf16[80,2048]{1,0:T(8,128)(2,1)S(1)}) custom-call(bf16[128,2048]{1,0:T(8,128)(2,1)} %bitcast.8, bf16[128,512]{1,0:T(8,128)(2,1)} %bitcast.13, bf16[128,2048]{1,0:T(8,128)(2,1)} %bitcast.10, ...), custom_call_target="tpu_custom_call" | custom-call | flops 1380000000 | tf_op jit(solution)/shard_map/pack/pallas_call | solution.py:383
  2.5 2.6 %collective-permute-start.1 = (bf16[16,4608]{1,0:T(8,128)(2,1)S(1)}, bf16[16,4608]{1,0:T(8,128)(2,1)S(1)}, u32[]{:S(2)}, u32[]{:S(2)}) collective-permute-start(bf16[16,4608]{1,0:T(8,128)(2,1)S(1)} %get-tuple-element.71), channel_id=1, source_target_pairs={{0,8},{4,12},{8,0},{12,4},{16,24},{20,28},{24,16},{28,20},{1,9},{5... | collective-permute-start | bytes 442376 | tf_op jit(solution)/shard_map/ppermute | solution.py:521
  5.2 1.7 %pack.3 = (f32[1,2048]{1,0:T(1,128)S(1)}, bf16[512,2048]{1,0:T(8,128)(2,1)S(1)}, bf16[16,4608]{1,0:T(8,128)(2,1)S(1)}, bf16[16,4608]{1,0:T(8,128)(2,1)S(1)}, bf1...) custom-call(bf16[128,2048]{1,0:T(8,128)(2,1)} %bitcast.9, ...), custom_call_target="tpu_custom_call" | custom-call | flops 1380000000 | tf_op jit(solution)/shard_map/pack/pallas_call | solution.py:383
  6.9 1.8 %collective-permute-start.4 = (bf16[80,2048]{1,0:T(8,128)(2,1)S(1)}, bf16[80,2048]{1,0:T(8,128)(2,1)S(1)}, u32[]{:S(2)}, u32[]{:S(2)}) collective-permute-start(bf16[80,2048]{1,0:T(8,128)(2,1)S(1)} %get-tuple-element.79), channel_id=1, source_target_pairs={{0,16},{4,20},{8,24},{12,28},{16,0},{20,4},{24,8},{28,12},{1,17},{... | collective-permute-start | bytes 983048 | tf_op jit(solution)/shard_map/ppermute | solution.py:521
  8.8 1.5 %collective-permute-start.6 = (bf16[16,4608]{1,0:T(8,128)(2,1)S(1)}, bf16[16,4608]{1,0:T(8,128)(2,1)S(1)}, u32[]{:S(2)}, u32[]{:S(2)}) collective-permute-start(bf16[16,4608]{1,0:T(8,128)(2,1)S(1)} %get-tuple-element.82), channel_id=1, source_target_pairs={{0,8},{4,12},{8,0},{12,4},{16,24},{20,28},{24,16},{28,20},{1,9},{5... | collective-permute-start | bytes 442376 | tf_op jit(solution)/shard_map/ppermute | solution.py:521
  10.6 1.9 %collective-permute-done.2.refs_3_ = bf16[16,4608]{1,0:T(8,128)(2,1)S(1)} collective-permute-done((bf16[16,4608]{1,0:T(8,128)(2,1)S(1)}, bf16[16,4608]{1,0:T(8,128)(2,1)S(1)}, u32[]{:S(2)}, u32[]{:S(2)}) %collective-permute-start.2) | collective-permute-done | bytes 147488 | tf_op jit(solution)/shard_map/ppermute | solution.py:521
  12.8 0.7 %collective-permute-start.3 = (bf16[32,2048]{1,0:T(8,128)(2,1)S(1)}, bf16[32,2048]{1,0:T(8,128)(2,1)S(1)}, u32[]{:S(2)}, u32[]{:S(2)}) collective-permute-start(bf16[32,2048]{1,0:T(8,128)(2,1)S(1)} %get-tuple-element.78.refs_7_.refs_6_), channel_id=1, source_target_pairs={{3,2},{7,6},{11,10},{15,14},{19,18},{23,22},{27,26},{31,30}} | collective-permute-start | bytes 393224 | tf_op jit(solution)/shard_map/ppermute | solution.py:550
  13.5 0.7 %collective-permute-start.11 = (bf16[32,2048]{1,0:T(8,128)(2,1)S(1)}, bf16[32,2048]{1,0:T(8,128)(2,1)S(1)}, u32[]{:S(2)}, u32[]{:S(2)}) collective-permute-start(bf16[32,2048]{1,0:T(8,128)(2,1)S(1)} %get-tuple-element.85.refs_5_.refs_7_), channel_id=1, source_target_pairs={{3,2},{7,6},{11,10},{15,14},{19,18},{23,22},{27,26},{31,30}} | collective-permute-start | bytes 393224 | tf_op jit(solution)/shard_map/ppermute | solution.py:550
  14.2 1.9 %collective-permute-done.6.refs_2_ = bf16[16,4608]{1,0:T(8,128)(2,1)S(1)} collective-permute-done((bf16[16,4608]{1,0:T(8,128)(2,1)S(1)}, bf16[16,4608]{1,0:T(8,128)(2,1)S(1)}, u32[]{:S(2)}, u32[]{:S(2)}) %collective-permute-start.6) | collective-permute-done | bytes 147488 | tf_op jit(solution)/shard_map/ppermute | solution.py:521
  16.1 2.6 %collective-permute-done.7.refs_3_ = bf16[16,4608]{1,0:T(8,128)(2,1)S(1)} collective-permute-done((bf16[16,4608]{1,0:T(8,128)(2,1)S(1)}, bf16[16,4608]{1,0:T(8,128)(2,1)S(1)}, u32[]{:S(2)}, u32[]{:S(2)}) %collective-permute-start.7) | collective-permute-done | bytes 147488 | tf_op jit(solution)/shard_map/ppermute | solution.py:521
  19.8 0.7 %collective-permute-start.10 = (bf16[32,2048]{1,0:T(8,128)(2,1)S(1)}, bf16[32,2048]{1,0:T(8,128)(2,1)S(1)}, u32[]{:S(2)}, u32[]{:S(2)}) collective-permute-start(bf16[32,2048]{1,0:T(8,128)(2,1)S(1)} %get-tuple-element.91.refs_6_.refs_7_), channel_id=1, source_target_pairs={{3,2},{7,6},{11,10},{15,14},{19,18},{23,22},{27,26},{31,30}} | collective-permute-start | bytes 393224 | tf_op jit(solution)/shard_map/ppermute | solution.py:550
  21.9 0.7 %collective-permute-start.15 = (bf16[32,2048]{1,0:T(8,128)(2,1)S(1)}, bf16[32,2048]{1,0:T(8,128)(2,1)S(1)}, u32[]{:S(2)}, u32[]{:S(2)}) collective-permute-start(bf16[32,2048]{1,0:T(8,128)(2,1)S(1)} %get-tuple-element.94.refs_7_.refs_8_), channel_id=1, source_target_pairs={{2,1},{6,5},{10,9},{14,13},{18,17},{22,21},{26,25},{30,29}} | collective-permute-start | bytes 393224 | tf_op jit(solution)/shard_map/ppermute | solution.py:550
  23.5 2.6 %collective-permute-start.20 = (bf16[128,512]{1,0:T(8,128)(2,1)S(1)}, bf16[128,512]{1,0:T(8,128)(2,1)S(1)}, u32[]{:S(2)}, u32[]{:S(2)}) collective-permute-start(bf16[128,512]{1,0:T(8,128)(2,1)S(1)} %columns6.1), channel_id=1, source_target_pairs={{0,24},{4,28},{8,16},{12,20},{16,8},{20,12},{24,0},{28,4},{1,25},{... | collective-permute-start | bytes 393224 | tf_op jit(solution)/shard_map/ppermute | solution.py:521
  26.1 1.3 %collective-permute-start.12 = (bf16[32,2048]{1,0:T(8,128)(2,1)S(1)}, bf16[32,2048]{1,0:T(8,128)(2,1)S(1)}, u32[]{:S(2)}, u32[]{:S(2)}) collective-permute-start(bf16[32,2048]{1,0:T(8,128)(2,1)S(1)} %get-tuple-element.96.refs_7_.refs_10_), channel_id=1, source_target_pairs={{1,0},{5,4},{9,8},{13,12},{17,16},{21,20},{25,24},{29,28}} | collective-permute-start | bytes 393224 | tf_op jit(solution)/shard_map/ppermute | solution.py:550
  27.4 1.3 %collective-permute-start.14 = (bf16[32,2048]{1,0:T(8,128)(2,1)S(1)}, bf16[32,2048]{1,0:T(8,128)(2,1)S(1)}, u32[]{:S(2)}, u32[]{:S(2)}) collective-permute-start(bf16[32,2048]{1,0:T(8,128)(2,1)S(1)} %get-tuple-element.97.refs_6_.refs_11_), channel_id=1, source_target_pairs={{1,0},{5,4},{9,8},{13,12},{17,16},{21,20},{25,24},{29,28}} | collective-permute-start | bytes 393224 | tf_op jit(solution)/shard_map/ppermute | solution.py:550
  28.8 1.3 %collective-permute-start.18 = (bf16[32,2048]{1,0:T(8,128)(2,1)S(1)}, bf16[32,2048]{1,0:T(8,128)(2,1)S(1)}, u32[]{:S(2)}, u32[]{:S(2)}) collective-permute-start(bf16[32,2048]{1,0:T(8,128)(2,1)S(1)} %get-tuple-element.104.refs_7_.refs_10_), channel_id=1, source_target_pairs={{1,0},{5,4},{9,8},{13,12},{17,16},{21,20},{25,24},{29,28}} | collective-permute-start | bytes 393224 | tf_op jit(solution)/shard_map/ppermute | solution.py:550
  30.1 1.3 %collective-permute-start.19 = (bf16[32,2048]{1,0:T(8,128)(2,1)S(1)}, bf16[32,2048]{1,0:T(8,128)(2,1)S(1)}, u32[]{:S(2)}, u32[]{:S(2)}) collective-permute-start(bf16[32,2048]{1,0:T(8,128)(2,1)S(1)} %get-tuple-element.105.refs_12_.refs_0_.refs_11_), channel_id=1, source_target_pairs={{1,0},{5,4},{9,8},{13,12},{17,16},{21,20},{25,24},{29,28}} | collective-permute-start | bytes 393224 | tf_op jit(solution)/shard_map/ppermute | solution.py:550
  32.1 4.9 %collective-permute-done.12.refs_0_ = bf16[32,2048]{1,0:T(8,128)(2,1)S(1)} collective-permute-done((bf16[32,2048]{1,0:T(8,128)(2,1)S(1)}, bf16[32,2048]{1,0:T(8,128)(2,1)S(1)}, u32[]{:S(2)}, u32[]{:S(2)}) %collective-permute-start.12) | collective-permute-done | bytes 131104 | tf_op jit(solution)/shard_map/ppermute | solution.py:550
  37.0 0.8 %tick3_a_late.1 = (bf16[32,2048]{1,0:T(8,128)(2,1)S(1)}, bf16[32,512]{1,0:T(8,128)(2,1)S(1)}) custom-call(bf16[32,2048]{1,0:T(8,128)(2,1)S(1)} %collective-permute-done.12.refs_0_, bf16[4,32,128]{2,1,0:T(8,128)(2,1)S(1)} %get-tuple-element.73.refs_1_, f32[64,128]{1,0:T(8,128)S(1)} %get-tuple-element.74.refs_2_.refs_3_, ...), custom_call_target="tpu_custom_call" | custom-call | flops 1150000000 | tf_op jit(solution)/shard_map/tick3_a_late/pallas_call | solution.py:319
  37.8 2.0 %collective-permute-done.14.refs_1_ = bf16[32,2048]{1,0:T(8,128)(2,1)S(1)} collective-permute-done((bf16[32,2048]{1,0:T(8,128)(2,1)S(1)}, bf16[32,2048]{1,0:T(8,128)(2,1)S(1)}, u32[]{:S(2)}, u32[]{:S(2)}) %collective-permute-start.14) | collective-permute-done | bytes 131104 | tf_op jit(solution)/shard_map/ppermute | solution.py:550
  39.8 0.8 %tick3_a_early.1 = (bf16[32,2048]{1,0:T(8,128)(2,1)S(1)}, bf16[64,512]{1,0:T(8,128)(2,1)S(1)}, bf16[48,2048]{1,0:T(8,128)(2,1)S(1)}) custom-call(bf16[32,2048]{1,0:T(8,128)(2,1)S(1)} %collective-permute-done.12.refs_0_, bf16[32,2048]{1,0:T(8,128)(2,1)S(1)} %collective-permute-done.14.refs_1_, bf16[4,32,256]{2,1,0:T(8,128)(2,1)S(1)} %get-tuple-element.84.refs_2_, ...), custom_call_target="tpu_custom_call" | custom-call | flops 1150000000 | tf_op jit(solution)/shard_map/tick3_a_early/pallas_call | solution.py:319
  40.7 2.5 %collective-permute-start.23 = (bf16[64,512]{1,0:T(8,128)(2,1)S(1)}, bf16[64,512]{1,0:T(8,128)(2,1)S(1)}, u32[]{:S(2)}, u32[]{:S(2)}) collective-permute-start(bf16[64,512]{1,0:T(8,128)(2,1)S(1)} %get-tuple-element.118.refs_17_.refs_0_), channel_id=1, source_target_pairs={{0,24},{4,28},{8,16},{12,20},{16,8},{20,12},{24,0},{28,4},{1,25},{... | collective-permute-start | bytes 196616 | tf_op jit(solution)/shard_map/ppermute | solution.py:521
  44.2 0.8 %tick3_b_late.1 = (bf16[32,2048]{1,0:T(8,128)(2,1)S(1)}, bf16[32,512]{1,0:T(8,128)(2,1)S(1)}) custom-call(bf16[32,2048]{1,0:T(8,128)(2,1)S(1)} %collective-permute-done.18.refs_0_, bf16[4,32,128]{2,1,0:T(8,128)(2,1)S(1)} %get-tuple-element.89.refs_1_, f32[64,128]{1,0:T(8,128)S(1)} %get-tuple-element.87.refs_2_.refs_3_, ...), custom_call_target="tpu_custom_call" | custom-call | flops 1150000000 | tf_op jit(solution)/shard_map/tick3_b_late/pallas_call | solution.py:319
  45.4 0.9 %tick3_b_early.1 = (bf16[64,512]{1,0:T(8,128)(2,1)S(1)}, bf16[128,512]{1,0:T(8,128)(2,1)S(1)}, bf16[32,2048]{1,0:T(8,128)(2,1)S(1)}, bf16[32,2048]{1,0:T(8,128)(...) custom-call(bf16[32,2048]{1,0:T(8,128)(2,1)S(1)} %collective-permute-done.18.refs_0_, ...), custom_call_target="tpu_custom_call" | custom-call | flops 1150000000 | tf_op jit(solution)/shard_map/tick3_b_early/pallas_call | solution.py:319
  46.3 2.5 %collective-permute-start.24 = (bf16[64,512]{1,0:T(8,128)(2,1)S(1)}, bf16[64,512]{1,0:T(8,128)(2,1)S(1)}, u32[]{:S(2)}, u32[]{:S(2)}) collective-permute-start(bf16[64,512]{1,0:T(8,128)(2,1)S(1)} %get-tuple-element.120.refs_1_), channel_id=1, source_target_pairs={{0,24},{4,28},{8,16},{12,20},{16,8},{20,12},{24,0},{28,4},{1,25},{... | collective-permute-start | bytes 196616 | tf_op jit(solution)/shard_map/ppermute | solution.py:521
  50.0 0.7 %collective-permute-done.22.refs_2_ = bf16[192,512]{1,0:T(8,128)(2,1)S(1)} collective-permute-done((bf16[192,512]{1,0:T(8,128)(2,1)S(1)}, bf16[192,512]{1,0:T(8,128)(2,1)S(1)}, u32[]{:S(2)}, u32[]{:S(2)}) %collective-permute-start.22) | collective-permute-done | bytes 196640 | tf_op jit(solution)/shard_map/ppermute | solution.py:521
  50.7 0.8 %collective-permute-start.28 = (bf16[16,2048]{1,0:T(8,128)(2,1)S(1)}, bf16[16,2048]{1,0:T(8,128)(2,1)S(1)}, u32[]{:S(2)}, u32[]{:S(2)}) collective-permute-start(bf16[16,2048]{1,0:T(8,128)(2,1)S(1)} %get-tuple-element.125), channel_id=1, source_target_pairs={{0,12},{4,8},{8,4},{12,0},{16,28},{20,24},{24,20},{28,16},{1,13},{... | collective-permute-start | bytes 196616 | tf_op jit(solution)/shard_map/ppermute | solution.py:521
  51.5 0.8 %collective-permute-done.24.refs_4_.refs_9_ = bf16[64,512]{1,0:T(8,128)(2,1)S(1)} collective-permute-done((bf16[64,512]{1,0:T(8,128)(2,1)S(1)}, bf16[64,512]{1,0:T(8,128)(2,1)S(1)}, u32[]{:S(2)}, u32[]{:S(2)}) %collective-permute-start.24) | collective-permute-done | bytes 65568 | tf_op jit(solution)/shard_map/ppermute | solution.py:521
  52.4 1.2 %collective-permute-done.29.refs_7_ = bf16[64,512]{1,0:T(8,128)(2,1)S(1)} collective-permute-done((bf16[64,512]{1,0:T(8,128)(2,1)S(1)}, bf16[64,512]{1,0:T(8,128)(2,1)S(1)}, u32[]{:S(2)}, u32[]{:S(2)}) %collective-permute-start.29) | collective-permute-done | bytes 65568 | tf_op jit(solution)/shard_map/ppermute | solution.py:521
  53.6 0.9 %collective-permute-done.27.refs_2_.refs_6_ = bf16[32,2048]{1,0:T(8,128)(2,1)S(1)} collective-permute-done((bf16[32,2048]{1,0:T(8,128)(2,1)S(1)}, bf16[32,2048]{1,0:T(8,128)(2,1)S(1)}, u32[]{:S(2)}, u32[]{:S(2)}) %collective-permute-start.27) | collective-permute-done | bytes 131104 | tf_op jit(solution)/shard_map/ppermute | solution.py:521
  55.3 0.8 %rows.1 = (bf16[128,2048]{1,0:T(8,128)(2,1)}, f32[8,128]{1,0:T(8,128)S(1)}) custom-call(bf16[48,2048]{1,0:T(8,128)(2,1)S(1)} %collective-permute-done.17.refs_0_.first_rows_ref.refs_5_, bf16[16,2048]{1,0:T(8,128)(2,1)S(1)} %collective-permute-done.25.handed_ref, bf16[32,2048]{1,0:T(8,128)(2,1)S(1)} %get-tuple-element.122.refs_0_, ...), custom_call_target="tpu_custom_call" | custom-call | flops 2875000064 | tf_op jit(solution)/shard_map/rows/pallas_call | solution.py:595
  56.4 1.0 %finish.1 = (f32[256,512]{1,0:T(8,128)}, f32[1,256]{1,0:T(1,128)}) custom-call(f32[256,512]{1,0:T(8,128)S(1)} %partial_own.1.own_ref, bf16[256,512]{1,0:T(8,128)(2,1)S(1)} %collective-permute-done.30.other_ref, f32[256,512]{1,0:T(8,128)S(1)} %get-tuple-element.129.weight_ref, f32[256,128]{1,0:T(8,128)S(1)} %get-tuple-element.119.refs_1_.gain_ref, ...), custom_call_target="tpu_custom_call" | custom-call | tf_op jit(solution)/shard_map/finish/pallas_call | solution.py:606
  (63 shorter events, 9.2 us)
Async XLA Ops:
  0.6 4.5 %copy-start = (bf16[1,2048,512]{2,1,0:T(8,128)(2,1)S(1)}, bf16[1,2048,512]{2,1,0:T(8,128)(2,1)}, u32[]{:S(2)}) copy-start(bf16[1,2048,512]{2,1,0:T(8,128)(2,1)} %param.11) | copy-start | bytes 6291460
  2.0 6.8 %collective-permute-start = (bf16[16,4608]{1,0:T(8,128)(2,1)S(1)}, bf16[16,4608]{1,0:T(8,128)(2,1)S(1)}, u32[]{:S(2)}, u32[]{:S(2)}) collective-permute-start(bf16[16,4608]{1,0:T(8,128)(2,1)S(1)} %get-tuple-element.70), channel_id=1, source_target_pairs={{0,4},{4,0},{8,12},{12,8},{16,20},{20,16},{24,28},{28,24},{1,5},{5... | collective-permute-start | bytes 442376 | tf_op jit(solution)/shard_map/ppermute | solution.py:521
  2.5 7.7 %collective-permute-start.1 = (bf16[16,4608]{1,0:T(8,128)(2,1)S(1)}, bf16[16,4608]{1,0:T(8,128)(2,1)S(1)}, u32[]{:S(2)}, u32[]{:S(2)}) collective-permute-start(bf16[16,4608]{1,0:T(8,128)(2,1)S(1)} %get-tuple-element.71), channel_id=1, source_target_pairs={{0,8},{4,12},{8,0},{12,4},{16,24},{20,28},{24,16},{28,20},{1,9},{5... | collective-permute-start | bytes 442376 | tf_op jit(solution)/shard_map/ppermute | solution.py:521
  5.1 7.3 %collective-permute-start.2 = (bf16[16,4608]{1,0:T(8,128)(2,1)S(1)}, bf16[16,4608]{1,0:T(8,128)(2,1)S(1)}, u32[]{:S(2)}, u32[]{:S(2)}) collective-permute-start(bf16[16,4608]{1,0:T(8,128)(2,1)S(1)} %get-tuple-element.72), channel_id=1, source_target_pairs={{0,12},{4,8},{8,4},{12,0},{16,28},{20,24},{24,20},{28,16},{1,13},{... | collective-permute-start | bytes 442376 | tf_op jit(solution)/shard_map/ppermute | solution.py:521
  6.9 11.9 %collective-permute-start.4 = (bf16[80,2048]{1,0:T(8,128)(2,1)S(1)}, bf16[80,2048]{1,0:T(8,128)(2,1)S(1)}, u32[]{:S(2)}, u32[]{:S(2)}) collective-permute-start(bf16[80,2048]{1,0:T(8,128)(2,1)S(1)} %get-tuple-element.79), channel_id=1, source_target_pairs={{0,16},{4,20},{8,24},{12,28},{16,0},{20,4},{24,8},{28,12},{1,17},{... | collective-permute-start | bytes 983048 | tf_op jit(solution)/shard_map/ppermute | solution.py:521
  8.7 4.8 %collective-permute-start.5 = (bf16[16,4608]{1,0:T(8,128)(2,1)S(1)}, bf16[16,4608]{1,0:T(8,128)(2,1)S(1)}, u32[]{:S(2)}, u32[]{:S(2)}) collective-permute-start(bf16[16,4608]{1,0:T(8,128)(2,1)S(1)} %get-tuple-element.81), channel_id=1, source_target_pairs={{0,4},{4,0},{8,12},{12,8},{16,20},{20,16},{24,28},{28,24},{1,5},{5... | collective-permute-start | bytes 442376 | tf_op jit(solution)/shard_map/ppermute | solution.py:521
  8.8 7.3 %collective-permute-start.6 = (bf16[16,4608]{1,0:T(8,128)(2,1)S(1)}, bf16[16,4608]{1,0:T(8,128)(2,1)S(1)}, u32[]{:S(2)}, u32[]{:S(2)}) collective-permute-start(bf16[16,4608]{1,0:T(8,128)(2,1)S(1)} %get-tuple-element.82), channel_id=1, source_target_pairs={{0,8},{4,12},{8,0},{12,4},{16,24},{20,28},{24,16},{28,20},{1,9},{5... | collective-permute-start | bytes 442376 | tf_op jit(solution)/shard_map/ppermute | solution.py:521
  10.3 8.5 %collective-permute-start.7 = (bf16[16,4608]{1,0:T(8,128)(2,1)S(1)}, bf16[16,4608]{1,0:T(8,128)(2,1)S(1)}, u32[]{:S(2)}, u32[]{:S(2)}) collective-permute-start(bf16[16,4608]{1,0:T(8,128)(2,1)S(1)} %get-tuple-element.83), channel_id=1, source_target_pairs={{0,12},{4,8},{8,4},{12,0},{16,28},{20,24},{24,20},{28,16},{1,13},{... | collective-permute-start | bytes 442376 | tf_op jit(solution)/shard_map/ppermute | solution.py:521
  12.8 7.7 %collective-permute-start.3 = (bf16[32,2048]{1,0:T(8,128)(2,1)S(1)}, bf16[32,2048]{1,0:T(8,128)(2,1)S(1)}, u32[]{:S(2)}, u32[]{:S(2)}) collective-permute-start(bf16[32,2048]{1,0:T(8,128)(2,1)S(1)} %get-tuple-element.78.refs_7_.refs_6_), channel_id=1, source_target_pairs={{3,2},{7,6},{11,10},{15,14},{19,18},{23,22},{27,26},{31,30}} | collective-permute-start | bytes 393224 | tf_op jit(solution)/shard_map/ppermute | solution.py:550
  13.5 7.7 %collective-permute-start.11 = (bf16[32,2048]{1,0:T(8,128)(2,1)S(1)}, bf16[32,2048]{1,0:T(8,128)(2,1)S(1)}, u32[]{:S(2)}, u32[]{:S(2)}) collective-permute-start(bf16[32,2048]{1,0:T(8,128)(2,1)S(1)} %get-tuple-element.85.refs_5_.refs_7_), channel_id=1, source_target_pairs={{3,2},{7,6},{11,10},{15,14},{19,18},{23,22},{27,26},{31,30}} | collective-permute-start | bytes 393224 | tf_op jit(solution)/shard_map/ppermute | solution.py:550
  19.1 2.8 %collective-permute-start.9 = (bf16[32,2048]{1,0:T(8,128)(2,1)S(1)}, bf16[32,2048]{1,0:T(8,128)(2,1)S(1)}, u32[]{:S(2)}, u32[]{:S(2)}) collective-permute-start(bf16[32,2048]{1,0:T(8,128)(2,1)S(1)} %get-tuple-element.90.refs_7_.refs_6_), channel_id=1, source_target_pairs={{3,2},{7,6},{11,10},{15,14},{19,18},{23,22},{27,26},{31,30}} | collective-permute-start | bytes 393224 | tf_op jit(solution)/shard_map/ppermute | solution.py:550
  19.8 2.8 %collective-permute-start.10 = (bf16[32,2048]{1,0:T(8,128)(2,1)S(1)}, bf16[32,2048]{1,0:T(8,128)(2,1)S(1)}, u32[]{:S(2)}, u32[]{:S(2)}) collective-permute-start(bf16[32,2048]{1,0:T(8,128)(2,1)S(1)} %get-tuple-element.91.refs_6_.refs_7_), channel_id=1, source_target_pairs={{3,2},{7,6},{11,10},{15,14},{19,18},{23,22},{27,26},{31,30}} | collective-permute-start | bytes 393224 | tf_op jit(solution)/shard_map/ppermute | solution.py:550
  20.5 5.6 %collective-permute-start.8 = (bf16[32,2048]{1,0:T(8,128)(2,1)S(1)}, bf16[32,2048]{1,0:T(8,128)(2,1)S(1)}, u32[]{:S(2)}, u32[]{:S(2)}) collective-permute-start(bf16[32,2048]{1,0:T(8,128)(2,1)S(1)} %get-tuple-element.92.refs_7_.refs_8_), channel_id=1, source_target_pairs={{2,1},{6,5},{10,9},{14,13},{18,17},{22,21},{26,25},{30,29}} | collective-permute-start | bytes 393224 | tf_op jit(solution)/shard_map/ppermute | solution.py:550
  21.2 6.2 %collective-permute-start.13 = (bf16[32,2048]{1,0:T(8,128)(2,1)S(1)}, bf16[32,2048]{1,0:T(8,128)(2,1)S(1)}, u32[]{:S(2)}, u32[]{:S(2)}) collective-permute-start(bf16[32,2048]{1,0:T(8,128)(2,1)S(1)} %get-tuple-element.93.refs_6_.refs_9_), channel_id=1, source_target_pairs={{2,1},{6,5},{10,9},{14,13},{18,17},{22,21},{26,25},{30,29}} | collective-permute-start | bytes 393224 | tf_op jit(solution)/shard_map/ppermute | solution.py:550
  21.9 6.8 %collective-permute-start.15 = (bf16[32,2048]{1,0:T(8,128)(2,1)S(1)}, bf16[32,2048]{1,0:T(8,128)(2,1)S(1)}, u32[]{:S(2)}, u32[]{:S(2)}) collective-permute-start(bf16[32,2048]{1,0:T(8,128)(2,1)S(1)} %get-tuple-element.94.refs_7_.refs_8_), channel_id=1, source_target_pairs={{2,1},{6,5},{10,9},{14,13},{18,17},{22,21},{26,25},{30,29}} | collective-permute-start | bytes 393224 | tf_op jit(solution)/shard_map/ppermute | solution.py:550
  22.7 7.4 %collective-permute-start.16 = (bf16[32,2048]{1,0:T(8,128)(2,1)S(1)}, bf16[32,2048]{1,0:T(8,128)(2,1)S(1)}, u32[]{:S(2)}, u32[]{:S(2)}) collective-permute-start(bf16[32,2048]{1,0:T(8,128)(2,1)S(1)} %get-tuple-element.95.refs_6_.after_ref.refs_0_.refs_9_), channel_id=1, source_target_pairs={{2,1},{6,5},{10,9},{14,13},{18,17},{22,21},{26,25},{30,29}} | collective-permute-start | bytes 393224 | tf_op jit(solution)/shard_map/ppermute | solution.py:550
  23.5 7.9 %collective-permute-start.20 = (bf16[128,512]{1,0:T(8,128)(2,1)S(1)}, bf16[128,512]{1,0:T(8,128)(2,1)S(1)}, u32[]{:S(2)}, u32[]{:S(2)}) collective-permute-start(bf16[128,512]{1,0:T(8,128)(2,1)S(1)} %columns6.1), channel_id=1, source_target_pairs={{0,24},{4,28},{8,16},{12,20},{16,8},{20,12},{24,0},{28,4},{1,25},{... | collective-permute-start | bytes 393224 | tf_op jit(solution)/shard_map/ppermute | solution.py:521
  26.1 10.9 %collective-permute-start.12 = (bf16[32,2048]{1,0:T(8,128)(2,1)S(1)}, bf16[32,2048]{1,0:T(8,128)(2,1)S(1)}, u32[]{:S(2)}, u32[]{:S(2)}) collective-permute-start(bf16[32,2048]{1,0:T(8,128)(2,1)S(1)} %get-tuple-element.96.refs_7_.refs_10_), channel_id=1, source_target_pairs={{1,0},{5,4},{9,8},{13,12},{17,16},{21,20},{25,24},{29,28}} | collective-permute-start | bytes 393224 | tf_op jit(solution)/shard_map/ppermute | solution.py:550
  27.4 12.3 %collective-permute-start.14 = (bf16[32,2048]{1,0:T(8,128)(2,1)S(1)}, bf16[32,2048]{1,0:T(8,128)(2,1)S(1)}, u32[]{:S(2)}, u32[]{:S(2)}) collective-permute-start(bf16[32,2048]{1,0:T(8,128)(2,1)S(1)} %get-tuple-element.97.refs_6_.refs_11_), channel_id=1, source_target_pairs={{1,0},{5,4},{9,8},{13,12},{17,16},{21,20},{25,24},{29,28}} | collective-permute-start | bytes 393224 | tf_op jit(solution)/shard_map/ppermute | solution.py:550
  28.8 14.9 %collective-permute-start.18 = (bf16[32,2048]{1,0:T(8,128)(2,1)S(1)}, bf16[32,2048]{1,0:T(8,128)(2,1)S(1)}, u32[]{:S(2)}, u32[]{:S(2)}) collective-permute-start(bf16[32,2048]{1,0:T(8,128)(2,1)S(1)} %get-tuple-element.104.refs_7_.refs_10_), channel_id=1, source_target_pairs={{1,0},{5,4},{9,8},{13,12},{17,16},{21,20},{25,24},{29,28}} | collective-permute-start | bytes 393224 | tf_op jit(solution)/shard_map/ppermute | solution.py:550
  30.1 15.3 %collective-permute-start.19 = (bf16[32,2048]{1,0:T(8,128)(2,1)S(1)}, bf16[32,2048]{1,0:T(8,128)(2,1)S(1)}, u32[]{:S(2)}, u32[]{:S(2)}) collective-permute-start(bf16[32,2048]{1,0:T(8,128)(2,1)S(1)} %get-tuple-element.105.refs_12_.refs_0_.refs_11_), channel_id=1, source_target_pairs={{1,0},{5,4},{9,8},{13,12},{17,16},{21,20},{25,24},{29,28}} | collective-permute-start | bytes 393224 | tf_op jit(solution)/shard_map/ppermute | solution.py:550
  31.5 14.0 %collective-permute-start.21 = (bf16[128,512]{1,0:T(8,128)(2,1)S(1)}, bf16[128,512]{1,0:T(8,128)(2,1)S(1)}, u32[]{:S(2)}, u32[]{:S(2)}) collective-permute-start(bf16[128,512]{1,0:T(8,128)(2,1)S(1)} %columns2.1), channel_id=1, source_target_pairs={{0,8},{4,12},{8,0},{12,4},{16,24},{20,28},{24,16},{28,20},{1,9},{5... | collective-permute-start | bytes 393224 | tf_op jit(solution)/shard_map/ppermute | solution.py:521
  40.7 8.7 %collective-permute-start.23 = (bf16[64,512]{1,0:T(8,128)(2,1)S(1)}, bf16[64,512]{1,0:T(8,128)(2,1)S(1)}, u32[]{:S(2)}, u32[]{:S(2)}) collective-permute-start(bf16[64,512]{1,0:T(8,128)(2,1)S(1)} %get-tuple-element.118.refs_17_.refs_0_), channel_id=1, source_target_pairs={{0,24},{4,28},{8,16},{12,20},{16,8},{20,12},{24,0},{28,4},{1,25},{... | collective-permute-start | bytes 196616 | tf_op jit(solution)/shard_map/ppermute | solution.py:521
  43.2 6.8 %collective-permute-start.17 = (bf16[48,2048]{1,0:T(8,128)(2,1)S(1)}, bf16[48,2048]{1,0:T(8,128)(2,1)S(1)}, u32[]{:S(2)}, u32[]{:S(2)}) collective-permute-start(bf16[48,2048]{1,0:T(8,128)(2,1)S(1)} %get-tuple-element.108), channel_id=1, source_target_pairs={{0,8},{4,12},{8,0},{12,4},{16,24},{20,28},{24,16},{28,20},{1,9},{5... | collective-permute-start | bytes 589832 | tf_op jit(solution)/shard_map/ppermute | solution.py:521
  43.7 7.0 %collective-permute-start.22 = (bf16[192,512]{1,0:T(8,128)(2,1)S(1)}, bf16[192,512]{1,0:T(8,128)(2,1)S(1)}, u32[]{:S(2)}, u32[]{:S(2)}) collective-permute-start(bf16[192,512]{1,0:T(8,128)(2,1)S(1)} %columns4.1), channel_id=1, source_target_pairs={{0,16},{4,20},{8,24},{12,28},{16,0},{20,4},{24,8},{28,12},{1,17},{... | collective-permute-start | bytes 589832 | tf_op jit(solution)/shard_map/ppermute | solution.py:521
  46.3 5.9 %collective-permute-start.24 = (bf16[64,512]{1,0:T(8,128)(2,1)S(1)}, bf16[64,512]{1,0:T(8,128)(2,1)S(1)}, u32[]{:S(2)}, u32[]{:S(2)}) collective-permute-start(bf16[64,512]{1,0:T(8,128)(2,1)S(1)} %get-tuple-element.120.refs_1_), channel_id=1, source_target_pairs={{0,24},{4,28},{8,16},{12,20},{16,8},{20,12},{24,0},{28,4},{1,25},{... | collective-permute-start | bytes 196616 | tf_op jit(solution)/shard_map/ppermute | solution.py:521
  48.8 5.7 %collective-permute-start.27 = (bf16[32,2048]{1,0:T(8,128)(2,1)S(1)}, bf16[32,2048]{1,0:T(8,128)(2,1)S(1)}, u32[]{:S(2)}, u32[]{:S(2)}) collective-permute-start(bf16[32,2048]{1,0:T(8,128)(2,1)S(1)} %get-tuple-element.124), channel_id=1, source_target_pairs={{0,8},{4,12},{8,0},{12,4},{16,24},{20,28},{24,16},{28,20},{1,9},{5... | collective-permute-start | bytes 393224 | tf_op jit(solution)/shard_map/ppermute | solution.py:521
  49.3 4.3 %collective-permute-start.29 = (bf16[64,512]{1,0:T(8,128)(2,1)S(1)}, bf16[64,512]{1,0:T(8,128)(2,1)S(1)}, u32[]{:S(2)}, u32[]{:S(2)}) collective-permute-start(bf16[64,512]{1,0:T(8,128)(2,1)S(1)} %get-tuple-element.120.refs_1_), channel_id=1, source_target_pairs={{0,16},{4,20},{8,24},{12,28},{16,0},{20,4},{24,8},{28,12},{1,17},{... | collective-permute-start | bytes 196616 | tf_op jit(solution)/shard_map/ppermute | solution.py:521
  50.0 5.2 %collective-permute-start.26 = (bf16[32,2048]{1,0:T(8,128)(2,1)S(1)}, bf16[32,2048]{1,0:T(8,128)(2,1)S(1)}, u32[]{:S(2)}, u32[]{:S(2)}) collective-permute-start(bf16[32,2048]{1,0:T(8,128)(2,1)S(1)} %get-tuple-element.123), channel_id=1, source_target_pairs={{0,4},{4,0},{8,12},{12,8},{16,20},{20,16},{24,28},{28,24},{1,5},{5... | collective-permute-start | bytes 393224 | tf_op jit(solution)/shard_map/ppermute | solution.py:521
  50.7 4.5 %collective-permute-start.28 = (bf16[16,2048]{1,0:T(8,128)(2,1)S(1)}, bf16[16,2048]{1,0:T(8,128)(2,1)S(1)}, u32[]{:S(2)}, u32[]{:S(2)}) collective-permute-start(bf16[16,2048]{1,0:T(8,128)(2,1)S(1)} %get-tuple-element.125), channel_id=1, source_target_pairs={{0,12},{4,8},{8,4},{12,0},{16,28},{20,24},{24,20},{28,16},{1,13},{... | collective-permute-start | bytes 196616 | tf_op jit(solution)/shard_map/ppermute | solution.py:521
  52.2 3.0 %collective-permute-start.25 = (bf16[16,2048]{1,0:T(8,128)(2,1)S(1)}, bf16[16,2048]{1,0:T(8,128)(2,1)S(1)}, u32[]{:S(2)}, u32[]{:S(2)}) collective-permute-start(bf16[16,2048]{1,0:T(8,128)(2,1)S(1)} %get-tuple-element.121), channel_id=1, source_target_pairs={{0,4},{4,0},{8,12},{12,8},{16,20},{20,16},{24,28},{28,24},{1,5},{5... | collective-permute-start | bytes 196616 | tf_op jit(solution)/shard_map/ppermute | solution.py:521
  54.8 1.6 %collective-permute-start.30 = (bf16[256,512]{1,0:T(8,128)(2,1)S(1)}, bf16[256,512]{1,0:T(8,128)(2,1)S(1)}, u32[]{:S(2)}, u32[]{:S(2)}) collective-permute-start(bf16[256,512]{1,0:T(8,128)(2,1)S(1)} %partial_other.1.refs_10_), channel_id=1, source_target_pairs={{0,4},{4,0},{8,12},{12,8},{16,20},{20,16},{24,28},{28,24},{1,5},{5... | collective-permute-start | bytes 786440 | tf_op jit(solution)/shard_map/ppermute | solution.py:521
  (1 other events, 4.5 us)

commit v19 on v18

--- a/solution.py
+++ b/solution.py
@@ -325,7 +325,7 @@
         out_specs=(VMEM,) * len(shapes),
         scratch_shapes=scratch,
         name=f"tick{tick}_{name}",
-        **params(1.0 if kept else 0.0),
+        **params(1.0 if kept else 1.5 if tick == 1 and name in UNITS[2:] else 0.0),
     )(*operands, *after)
 
 
@@ -562,10 +562,10 @@
                 name="own",
                 **params(0.0),
             )(near(weight), near(gain), *after)
-            columns = {6: swap(columns_for(6, blocks, after + [own_gain]), 6)}
-        if last:
-            columns[2] = swap(columns_for(2, blocks, after + [columns[6]]), 2)
+            columns[6] = swap(columns_for(6, blocks, after + [own_gain, columns[2]]), 6)
         for u in range(4):
+            if last and u == 0:
+                after = after + [columns[6]]
             needs = grads[u - 1 : u + 1] if u % 2 else grads[u : u + 1]
             late = []
             if last and u == 1:
@@ -574,7 +574,6 @@
                 late = [done[2][1], done[2][0], done[0][0], done[1][0], done[1][1]]
                 first_rows, far_first = swap(done[1][2], 2), swap(done[1][1], 6)
                 columns[4] = swap(columns_for(4, blocks, [], [done[1][1]]), 4)
-                after = after + [columns[2]]
             done.append(
                 tick_step(
                     tick, needs, blocks[u // 2], turned, gain, kept[u] if last else (), late,
@@ -583,6 +582,8 @@
             )
             after = [done[u][0]]
             kept[u].append(done[u])
+            if tick == layers - 3 and u == 1:
+                columns = {2: swap(columns_for(2, blocks, after), 2)}
     own_value, own_values, *rows = done[3]
     rows = [rows[0]] + [swap(rows[k], k) for k in range(1, half)]
     far_value, across_value = swap(own_value, 6), swap(own_value, 4)

time: 58.3 us -> 59.7 us (1.024)
  waiting for transfers between devices: 17.8 us -> 19.3 us
  starting transfers between devices: 28.6 us -> 29.2 us
    ppermute x19, waiting for transfers between devices: 10.5 us -> 13.9 us  [swap(): return lax.ppermute(array, 'dp', [(i, i ^ k) for i in range(replicas)])]
    ppermute x12, waiting for transfers between devices: 7.37 us -> 5.41 us  [direct(): lax.ppermute(unit[-1][0], 'section', hop)]
  transfers between devices with their start and end apart: 31 -> 31, of which waited for: 12 -> 9; matrix products, arithmetic and copies ran while one was open for 0% -> 0% of each run, Pallas kernels for 13% -> 13%
where the time goes in v19:
time: 59.7 us; the launch traced here: 59.4 us
  starting transfers between devices  29.2 us (49%)
  waiting for transfers between devices  19.3 us (32%)
  Pallas kernels  9.88 us (17%)
  between operations  1.02 us (2%)
    ppermute x19, starting transfers between devices, swap(): return lax.ppermute(array, 'dp', [(i, i ^ k) for i in range(replicas)])  18.7 us
    ppermute x19, waiting for transfers between devices, swap(): return lax.ppermute(array, 'dp', [(i, i ^ k) for i in range(replicas)])  13.9 us
    ppermute x12, starting transfers between devices, direct(): lax.ppermute(unit[-1][0], 'section', hop)  10.5 us
    ppermute x12, waiting for transfers between devices, direct(): lax.ppermute(unit[-1][0], 'section', hop)  5.41 us
    pallas_call x16, Pallas kernels, tick_step(): pl.pallas_call(functools.partial(tick_kernel, tick, EARLY if low else LAT...  3.43 us
    pallas_call x2, Pallas kernels, pack(): pl.pallas_call(functools.partial(pack_kernel, block, half, piece), out_sh...  3.06 us
  transfers between devices with their start and end apart: 31, of which 9 were waited for; matrix products, arithmetic and copies ran while one was open for 0% of the time, Pallas kernels for 13%

profile of v19, /device:TPU:0, one launch (start us, length us, event | category | flops | bytes accessed | tf_op | source)
XLA Modules:
  0.0 59.4 jit_solution(13836592708346179545)
XLA Ops:
  0.7 1.4 %pack.2 = (bf16[16,4608]{1,0:T(8,128)(2,1)S(1)}, bf16[16,4608]{1,0:T(8,128)(2,1)S(1)}, bf16[16,4608]{1,0:T(8,128)(2,1)S(1)}, bf16[16,4608]{1,0:T(8,128)(2,1)S(1)}, bf16[80,2048]{1,0:T(8,128)(2,1)S(1)}) custom-call(bf16[128,2048]{1,0:T(8,128)(2,1)} %bitcast.8, bf16[128,512]{1,0:T(8,128)(2,1)} %bitcast.13, bf16[128,2048]{1,0:T(8,128)(2,1)} %bitcast.10, ...), custom_call_target="tpu_custom_call" | custom-call | flops 1380000000 | tf_op jit(solution)/shard_map/pack/pallas_call | solution.py:383
  2.5 2.6 %collective-permute-start.1 = (bf16[16,4608]{1,0:T(8,128)(2,1)S(1)}, bf16[16,4608]{1,0:T(8,128)(2,1)S(1)}, u32[]{:S(2)}, u32[]{:S(2)}) collective-permute-start(bf16[16,4608]{1,0:T(8,128)(2,1)S(1)} %get-tuple-element.71), channel_id=1, source_target_pairs={{0,8},{4,12},{8,0},{12,4},{16,24},{20,28},{24,16},{28,20},{1,9},{5... | collective-permute-start | bytes 442376 | tf_op jit(solution)/shard_map/ppermute | solution.py:521
  5.2 1.7 %pack.3 = (f32[1,2048]{1,0:T(1,128)S(1)}, bf16[512,2048]{1,0:T(8,128)(2,1)S(1)}, bf16[16,4608]{1,0:T(8,128)(2,1)S(1)}, bf16[16,4608]{1,0:T(8,128)(2,1)S(1)}, bf1...) custom-call(bf16[128,2048]{1,0:T(8,128)(2,1)} %bitcast.9, ...), custom_call_target="tpu_custom_call" | custom-call | flops 1380000000 | tf_op jit(solution)/shard_map/pack/pallas_call | solution.py:383
  6.9 1.8 %collective-permute-start.4 = (bf16[80,2048]{1,0:T(8,128)(2,1)S(1)}, bf16[80,2048]{1,0:T(8,128)(2,1)S(1)}, u32[]{:S(2)}, u32[]{:S(2)}) collective-permute-start(bf16[80,2048]{1,0:T(8,128)(2,1)S(1)} %get-tuple-element.79), channel_id=1, source_target_pairs={{0,16},{4,20},{8,24},{12,28},{16,0},{20,4},{24,8},{28,12},{1,17},{... | collective-permute-start | bytes 983048 | tf_op jit(solution)/shard_map/ppermute | solution.py:521
  8.8 1.5 %collective-permute-start.6 = (bf16[16,4608]{1,0:T(8,128)(2,1)S(1)}, bf16[16,4608]{1,0:T(8,128)(2,1)S(1)}, u32[]{:S(2)}, u32[]{:S(2)}) collective-permute-start(bf16[16,4608]{1,0:T(8,128)(2,1)S(1)} %get-tuple-element.82), channel_id=1, source_target_pairs={{0,8},{4,12},{8,0},{12,4},{16,24},{20,28},{24,16},{28,20},{1,9},{5... | collective-permute-start | bytes 442376 | tf_op jit(solution)/shard_map/ppermute | solution.py:521
  10.6 1.9 %collective-permute-done.2.refs_3_ = bf16[16,4608]{1,0:T(8,128)(2,1)S(1)} collective-permute-done((bf16[16,4608]{1,0:T(8,128)(2,1)S(1)}, bf16[16,4608]{1,0:T(8,128)(2,1)S(1)}, u32[]{:S(2)}, u32[]{:S(2)}) %collective-permute-start.2) | collective-permute-done | bytes 147488 | tf_op jit(solution)/shard_map/ppermute | solution.py:521
  13.5 0.7 %collective-permute-start.11 = (bf16[32,2048]{1,0:T(8,128)(2,1)S(1)}, bf16[32,2048]{1,0:T(8,128)(2,1)S(1)}, u32[]{:S(2)}, u32[]{:S(2)}) collective-permute-start(bf16[32,2048]{1,0:T(8,128)(2,1)S(1)} %get-tuple-element.85.refs_5_.refs_7_), channel_id=1, source_target_pairs={{3,2},{7,6},{11,10},{15,14},{19,18},{23,22},{27,26},{31,30}} | collective-permute-start | bytes 393224 | tf_op jit(solution)/shard_map/ppermute | solution.py:550
  14.2 1.9 %collective-permute-done.6.refs_2_ = bf16[16,4608]{1,0:T(8,128)(2,1)S(1)} collective-permute-done((bf16[16,4608]{1,0:T(8,128)(2,1)S(1)}, bf16[16,4608]{1,0:T(8,128)(2,1)S(1)}, u32[]{:S(2)}, u32[]{:S(2)}) %collective-permute-start.6) | collective-permute-done | bytes 147488 | tf_op jit(solution)/shard_map/ppermute | solution.py:521
  16.1 2.6 %collective-permute-done.7.refs_3_ = bf16[16,4608]{1,0:T(8,128)(2,1)S(1)} collective-permute-done((bf16[16,4608]{1,0:T(8,128)(2,1)S(1)}, bf16[16,4608]{1,0:T(8,128)(2,1)S(1)}, u32[]{:S(2)}, u32[]{:S(2)}) %collective-permute-start.7) | collective-permute-done | bytes 147488 | tf_op jit(solution)/shard_map/ppermute | solution.py:521
  19.1 0.7 %collective-permute-start.9 = (bf16[32,2048]{1,0:T(8,128)(2,1)S(1)}, bf16[32,2048]{1,0:T(8,128)(2,1)S(1)}, u32[]{:S(2)}, u32[]{:S(2)}) collective-permute-start(bf16[32,2048]{1,0:T(8,128)(2,1)S(1)} %get-tuple-element.90.refs_7_.refs_6_), channel_id=1, source_target_pairs={{3,2},{7,6},{11,10},{15,14},{19,18},{23,22},{27,26},{31,30}} | collective-permute-start | bytes 393224 | tf_op jit(solution)/shard_map/ppermute | solution.py:550
  20.5 0.7 %collective-permute-start.8 = (bf16[32,2048]{1,0:T(8,128)(2,1)S(1)}, bf16[32,2048]{1,0:T(8,128)(2,1)S(1)}, u32[]{:S(2)}, u32[]{:S(2)}) collective-permute-start(bf16[32,2048]{1,0:T(8,128)(2,1)S(1)} %get-tuple-element.92.refs_7_.refs_8_), channel_id=1, source_target_pairs={{2,1},{6,5},{10,9},{14,13},{18,17},{22,21},{26,25},{30,29}} | collective-permute-start | bytes 393224 | tf_op jit(solution)/shard_map/ppermute | solution.py:550
  21.9 1.6 %collective-permute-start.17 = (bf16[128,512]{1,0:T(8,128)(2,1)S(1)}, bf16[128,512]{1,0:T(8,128)(2,1)S(1)}, u32[]{:S(2)}, u32[]{:S(2)}) collective-permute-start(bf16[128,512]{1,0:T(8,128)(2,1)S(1)} %columns2.1), channel_id=1, source_target_pairs={{0,8},{4,12},{8,0},{12,4},{16,24},{20,28},{24,16},{28,20},{1,9},{5... | collective-permute-start | bytes 393224 | tf_op jit(solution)/shard_map/ppermute | solution.py:521
  25.1 2.4 %collective-permute-done.17.refs_2_.refs_1_ = bf16[128,512]{1,0:T(8,128)(2,1)S(1)} collective-permute-done((bf16[128,512]{1,0:T(8,128)(2,1)S(1)}, bf16[128,512]{1,0:T(8,128)(2,1)S(1)}, u32[]{:S(2)}, u32[]{:S(2)}) %collective-permute-start.17) | collective-permute-done | bytes 131104 | tf_op jit(solution)/shard_map/ppermute | solution.py:521
  27.5 2.7 %collective-permute-start.18 = (bf16[128,512]{1,0:T(8,128)(2,1)S(1)}, bf16[128,512]{1,0:T(8,128)(2,1)S(1)}, u32[]{:S(2)}, u32[]{:S(2)}) collective-permute-start(bf16[128,512]{1,0:T(8,128)(2,1)S(1)} %columns6.1), channel_id=1, source_target_pairs={{0,24},{4,28},{8,16},{12,20},{16,8},{20,12},{24,0},{28,4},{1,25},{... | collective-permute-start | bytes 393224 | tf_op jit(solution)/shard_map/ppermute | solution.py:521
  30.3 1.3 %collective-permute-start.12 = (bf16[32,2048]{1,0:T(8,128)(2,1)S(1)}, bf16[32,2048]{1,0:T(8,128)(2,1)S(1)}, u32[]{:S(2)}, u32[]{:S(2)}) collective-permute-start(bf16[32,2048]{1,0:T(8,128)(2,1)S(1)} %get-tuple-element.96.refs_7_.refs_10_), channel_id=1, source_target_pairs={{1,0},{5,4},{9,8},{13,12},{17,16},{21,20},{25,24},{29,28}} | collective-permute-start | bytes 393224 | tf_op jit(solution)/shard_map/ppermute | solution.py:550
  31.6 1.3 %collective-permute-start.14 = (bf16[32,2048]{1,0:T(8,128)(2,1)S(1)}, bf16[32,2048]{1,0:T(8,128)(2,1)S(1)}, u32[]{:S(2)}, u32[]{:S(2)}) collective-permute-start(bf16[32,2048]{1,0:T(8,128)(2,1)S(1)} %get-tuple-element.97.refs_6_.refs_11_), channel_id=1, source_target_pairs={{1,0},{5,4},{9,8},{13,12},{17,16},{21,20},{25,24},{29,28}} | collective-permute-start | bytes 393224 | tf_op jit(solution)/shard_map/ppermute | solution.py:550
  33.0 1.3 %collective-permute-start.20 = (bf16[32,2048]{1,0:T(8,128)(2,1)S(1)}, bf16[32,2048]{1,0:T(8,128)(2,1)S(1)}, u32[]{:S(2)}, u32[]{:S(2)}) collective-permute-start(bf16[32,2048]{1,0:T(8,128)(2,1)S(1)} %get-tuple-element.104.refs_7_.refs_10_), channel_id=1, source_target_pairs={{1,0},{5,4},{9,8},{13,12},{17,16},{21,20},{25,24},{29,28}} | collective-permute-start | bytes 393224 | tf_op jit(solution)/shard_map/ppermute | solution.py:550
  34.3 1.3 %collective-permute-start.21 = (bf16[32,2048]{1,0:T(8,128)(2,1)S(1)}, bf16[32,2048]{1,0:T(8,128)(2,1)S(1)}, u32[]{:S(2)}, u32[]{:S(2)}) collective-permute-start(bf16[32,2048]{1,0:T(8,128)(2,1)S(1)} %get-tuple-element.105.refs_12_.refs_11_), channel_id=1, source_target_pairs={{1,0},{5,4},{9,8},{13,12},{17,16},{21,20},{25,24},{29,28}} | collective-permute-start | bytes 393224 | tf_op jit(solution)/shard_map/ppermute | solution.py:550
  35.6 3.4 %collective-permute-done.12.refs_0_ = bf16[32,2048]{1,0:T(8,128)(2,1)S(1)} collective-permute-done((bf16[32,2048]{1,0:T(8,128)(2,1)S(1)}, bf16[32,2048]{1,0:T(8,128)(2,1)S(1)}, u32[]{:S(2)}, u32[]{:S(2)}) %collective-permute-start.12) | collective-permute-done | bytes 131104 | tf_op jit(solution)/shard_map/ppermute | solution.py:550
  39.0 0.8 %tick3_a_late.1 = (bf16[32,2048]{1,0:T(8,128)(2,1)S(1)}, bf16[32,512]{1,0:T(8,128)(2,1)S(1)}) custom-call(bf16[32,2048]{1,0:T(8,128)(2,1)S(1)} %collective-permute-done.12.refs_0_, bf16[4,32,128]{2,1,0:T(8,128)(2,1)S(1)} %get-tuple-element.73.refs_1_, f32[64,128]{1,0:T(8,128)S(1)} %get-tuple-element.74.refs_2_.refs_3_, ...), custom_call_target="tpu_custom_call" | custom-call | flops 1150000000 | tf_op jit(solution)/shard_map/tick3_a_late/pallas_call | solution.py:319
  39.8 2.0 %collective-permute-done.14.refs_1_ = bf16[32,2048]{1,0:T(8,128)(2,1)S(1)} collective-permute-done((bf16[32,2048]{1,0:T(8,128)(2,1)S(1)}, bf16[32,2048]{1,0:T(8,128)(2,1)S(1)}, u32[]{:S(2)}, u32[]{:S(2)}) %collective-permute-start.14) | collective-permute-done | bytes 131104 | tf_op jit(solution)/shard_map/ppermute | solution.py:550
  41.8 0.8 %tick3_a_early.1 = (bf16[32,2048]{1,0:T(8,128)(2,1)S(1)}, bf16[64,512]{1,0:T(8,128)(2,1)S(1)}, bf16[48,2048]{1,0:T(8,128)(2,1)S(1)}) custom-call(bf16[32,2048]{1,0:T(8,128)(2,1)S(1)} %collective-permute-done.12.refs_0_, bf16[32,2048]{1,0:T(8,128)(2,1)S(1)} %collective-permute-done.14.refs_1_, bf16[4,32,256]{2,1,0:T(8,128)(2,1)S(1)} %get-tuple-element.84.refs_2_, ...), custom_call_target="tpu_custom_call" | custom-call | flops 1150000000 | tf_op jit(solution)/shard_map/tick3_a_early/pallas_call | solution.py:319
  43.2 0.8 %collective-permute-start.22 = (bf16[192,512]{1,0:T(8,128)(2,1)S(1)}, bf16[192,512]{1,0:T(8,128)(2,1)S(1)}, u32[]{:S(2)}, u32[]{:S(2)}) collective-permute-start(bf16[192,512]{1,0:T(8,128)(2,1)S(1)} %columns4.1), channel_id=1, source_target_pairs={{0,16},{4,20},{8,24},{12,28},{16,0},{20,4},{24,8},{28,12},{1,17},{... | collective-permute-start | bytes 589832 | tf_op jit(solution)/shard_map/ppermute | solution.py:521
  44.0 2.2 %collective-permute-start.19 = (bf16[48,2048]{1,0:T(8,128)(2,1)S(1)}, bf16[48,2048]{1,0:T(8,128)(2,1)S(1)}, u32[]{:S(2)}, u32[]{:S(2)}) collective-permute-start(bf16[48,2048]{1,0:T(8,128)(2,1)S(1)} %get-tuple-element.109), channel_id=1, source_target_pairs={{0,8},{4,12},{8,0},{12,4},{16,24},{20,28},{24,16},{28,20},{1,9},{5... | collective-permute-start | bytes 589832 | tf_op jit(solution)/shard_map/ppermute | solution.py:521
  46.2 0.8 %tick3_b_late.1 = (bf16[32,2048]{1,0:T(8,128)(2,1)S(1)}, bf16[32,512]{1,0:T(8,128)(2,1)S(1)}) custom-call(bf16[32,2048]{1,0:T(8,128)(2,1)S(1)} %collective-permute-done.20.refs_0_, bf16[4,32,128]{2,1,0:T(8,128)(2,1)S(1)} %get-tuple-element.89.refs_1_, f32[64,128]{1,0:T(8,128)S(1)} %get-tuple-element.87.refs_2_.refs_3_, ...), custom_call_target="tpu_custom_call" | custom-call | flops 1150000000 | tf_op jit(solution)/shard_map/tick3_b_late/pallas_call | solution.py:319
  47.0 0.9 %tick3_b_early.1 = (bf16[64,512]{1,0:T(8,128)(2,1)S(1)}, bf16[128,512]{1,0:T(8,128)(2,1)S(1)}, bf16[32,2048]{1,0:T(8,128)(2,1)S(1)}, bf16[32,2048]{1,0:T(8,128)(...) custom-call(bf16[32,2048]{1,0:T(8,128)(2,1)S(1)} %collective-permute-done.20.refs_0_, ...), custom_call_target="tpu_custom_call" | custom-call | flops 1150000000 | tf_op jit(solution)/shard_map/tick3_b_early/pallas_call | solution.py:319
  47.9 0.9 %collective-permute-start.24 = (bf16[64,512]{1,0:T(8,128)(2,1)S(1)}, bf16[64,512]{1,0:T(8,128)(2,1)S(1)}, u32[]{:S(2)}, u32[]{:S(2)}) collective-permute-start(bf16[64,512]{1,0:T(8,128)(2,1)S(1)} %get-tuple-element.120.refs_1_), channel_id=1, source_target_pairs={{0,24},{4,28},{8,16},{12,20},{16,8},{20,12},{24,0},{28,4},{1,25},{... | collective-permute-start | bytes 196616 | tf_op jit(solution)/shard_map/ppermute | solution.py:521
  49.5 2.0 %collective-permute-start.29 = (bf16[64,512]{1,0:T(8,128)(2,1)S(1)}, bf16[64,512]{1,0:T(8,128)(2,1)S(1)}, u32[]{:S(2)}, u32[]{:S(2)}) collective-permute-start(bf16[64,512]{1,0:T(8,128)(2,1)S(1)} %get-tuple-element.120.refs_1_), channel_id=1, source_target_pairs={{0,16},{4,20},{8,24},{12,28},{16,0},{20,4},{24,8},{28,12},{1,17},{... | collective-permute-start | bytes 196616 | tf_op jit(solution)/shard_map/ppermute | solution.py:521
  51.4 2.4 %collective-permute-done.24.refs_4_.refs_9_ = bf16[64,512]{1,0:T(8,128)(2,1)S(1)} collective-permute-done((bf16[64,512]{1,0:T(8,128)(2,1)S(1)}, bf16[64,512]{1,0:T(8,128)(2,1)S(1)}, u32[]{:S(2)}, u32[]{:S(2)}) %collective-permute-start.24) | collective-permute-done | bytes 65568 | tf_op jit(solution)/shard_map/ppermute | solution.py:521
  55.2 2.3 %collective-permute-done.28.refs_3_ = bf16[16,2048]{1,0:T(8,128)(2,1)S(1)} collective-permute-done((bf16[16,2048]{1,0:T(8,128)(2,1)S(1)}, bf16[16,2048]{1,0:T(8,128)(2,1)S(1)}, u32[]{:S(2)}, u32[]{:S(2)}) %collective-permute-start.28) | collective-permute-done | bytes 65568 | tf_op jit(solution)/shard_map/ppermute | solution.py:521
  57.5 0.8 %rows.1 = (bf16[128,2048]{1,0:T(8,128)(2,1)}, f32[8,128]{1,0:T(8,128)S(1)}) custom-call(bf16[48,2048]{1,0:T(8,128)(2,1)S(1)} %collective-permute-done.19.refs_0_.first_rows_ref.refs_5_, bf16[16,2048]{1,0:T(8,128)(2,1)S(1)} %collective-permute-done.25.handed_ref, bf16[32,2048]{1,0:T(8,128)(2,1)S(1)} %get-tuple-element.122.refs_0_, ...), custom_call_target="tpu_custom_call" | custom-call | flops 2875000064 | tf_op jit(solution)/shard_map/rows/pallas_call | solution.py:596
  58.4 1.0 %finish.1 = (f32[256,512]{1,0:T(8,128)}, f32[1,256]{1,0:T(1,128)}) custom-call(f32[256,512]{1,0:T(8,128)S(1)} %partial_own.1.own_ref, bf16[256,512]{1,0:T(8,128)(2,1)S(1)} %collective-permute-done.30.other_ref, f32[256,512]{1,0:T(8,128)S(1)} %get-tuple-element.129.weight_ref, f32[256,128]{1,0:T(8,128)S(1)} %get-tuple-element.106.refs_1_.gain_ref, ...), custom_call_target="tpu_custom_call" | custom-call | tf_op jit(solution)/shard_map/finish/pallas_call | solution.py:607
  (63 shorter events, 7.9 us)
Async XLA Ops:
  0.6 4.5 %copy-start = (bf16[1,2048,512]{2,1,0:T(8,128)(2,1)S(1)}, bf16[1,2048,512]{2,1,0:T(8,128)(2,1)}, u32[]{:S(2)}) copy-start(bf16[1,2048,512]{2,1,0:T(8,128)(2,1)} %param.11) | copy-start | bytes 6291460
  2.0 6.8 %collective-permute-start = (bf16[16,4608]{1,0:T(8,128)(2,1)S(1)}, bf16[16,4608]{1,0:T(8,128)(2,1)S(1)}, u32[]{:S(2)}, u32[]{:S(2)}) collective-permute-start(bf16[16,4608]{1,0:T(8,128)(2,1)S(1)} %get-tuple-element.70), channel_id=1, source_target_pairs={{0,4},{4,0},{8,12},{12,8},{16,20},{20,16},{24,28},{28,24},{1,5},{5... | collective-permute-start | bytes 442376 | tf_op jit(solution)/shard_map/ppermute | solution.py:521
  2.5 7.7 %collective-permute-start.1 = (bf16[16,4608]{1,0:T(8,128)(2,1)S(1)}, bf16[16,4608]{1,0:T(8,128)(2,1)S(1)}, u32[]{:S(2)}, u32[]{:S(2)}) collective-permute-start(bf16[16,4608]{1,0:T(8,128)(2,1)S(1)} %get-tuple-element.71), channel_id=1, source_target_pairs={{0,8},{4,12},{8,0},{12,4},{16,24},{20,28},{24,16},{28,20},{1,9},{5... | collective-permute-start | bytes 442376 | tf_op jit(solution)/shard_map/ppermute | solution.py:521
  5.1 7.3 %collective-permute-start.2 = (bf16[16,4608]{1,0:T(8,128)(2,1)S(1)}, bf16[16,4608]{1,0:T(8,128)(2,1)S(1)}, u32[]{:S(2)}, u32[]{:S(2)}) collective-permute-start(bf16[16,4608]{1,0:T(8,128)(2,1)S(1)} %get-tuple-element.72), channel_id=1, source_target_pairs={{0,12},{4,8},{8,4},{12,0},{16,28},{20,24},{24,20},{28,16},{1,13},{... | collective-permute-start | bytes 442376 | tf_op jit(solution)/shard_map/ppermute | solution.py:521
  6.9 11.9 %collective-permute-start.4 = (bf16[80,2048]{1,0:T(8,128)(2,1)S(1)}, bf16[80,2048]{1,0:T(8,128)(2,1)S(1)}, u32[]{:S(2)}, u32[]{:S(2)}) collective-permute-start(bf16[80,2048]{1,0:T(8,128)(2,1)S(1)} %get-tuple-element.79), channel_id=1, source_target_pairs={{0,16},{4,20},{8,24},{12,28},{16,0},{20,4},{24,8},{28,12},{1,17},{... | collective-permute-start | bytes 983048 | tf_op jit(solution)/shard_map/ppermute | solution.py:521
  8.7 4.8 %collective-permute-start.5 = (bf16[16,4608]{1,0:T(8,128)(2,1)S(1)}, bf16[16,4608]{1,0:T(8,128)(2,1)S(1)}, u32[]{:S(2)}, u32[]{:S(2)}) collective-permute-start(bf16[16,4608]{1,0:T(8,128)(2,1)S(1)} %get-tuple-element.81), channel_id=1, source_target_pairs={{0,4},{4,0},{8,12},{12,8},{16,20},{20,16},{24,28},{28,24},{1,5},{5... | collective-permute-start | bytes 442376 | tf_op jit(solution)/shard_map/ppermute | solution.py:521
  8.8 7.3 %collective-permute-start.6 = (bf16[16,4608]{1,0:T(8,128)(2,1)S(1)}, bf16[16,4608]{1,0:T(8,128)(2,1)S(1)}, u32[]{:S(2)}, u32[]{:S(2)}) collective-permute-start(bf16[16,4608]{1,0:T(8,128)(2,1)S(1)} %get-tuple-element.82), channel_id=1, source_target_pairs={{0,8},{4,12},{8,0},{12,4},{16,24},{20,28},{24,16},{28,20},{1,9},{5... | collective-permute-start | bytes 442376 | tf_op jit(solution)/shard_map/ppermute | solution.py:521
  10.3 8.5 %collective-permute-start.7 = (bf16[16,4608]{1,0:T(8,128)(2,1)S(1)}, bf16[16,4608]{1,0:T(8,128)(2,1)S(1)}, u32[]{:S(2)}, u32[]{:S(2)}) collective-permute-start(bf16[16,4608]{1,0:T(8,128)(2,1)S(1)} %get-tuple-element.83), channel_id=1, source_target_pairs={{0,12},{4,8},{8,4},{12,0},{16,28},{20,24},{24,20},{28,16},{1,13},{... | collective-permute-start | bytes 442376 | tf_op jit(solution)/shard_map/ppermute | solution.py:521
  12.8 7.7 %collective-permute-start.3 = (bf16[32,2048]{1,0:T(8,128)(2,1)S(1)}, bf16[32,2048]{1,0:T(8,128)(2,1)S(1)}, u32[]{:S(2)}, u32[]{:S(2)}) collective-permute-start(bf16[32,2048]{1,0:T(8,128)(2,1)S(1)} %get-tuple-element.78.refs_7_.refs_6_), channel_id=1, source_target_pairs={{3,2},{7,6},{11,10},{15,14},{19,18},{23,22},{27,26},{31,30}} | collective-permute-start | bytes 393224 | tf_op jit(solution)/shard_map/ppermute | solution.py:550
  13.5 7.7 %collective-permute-start.11 = (bf16[32,2048]{1,0:T(8,128)(2,1)S(1)}, bf16[32,2048]{1,0:T(8,128)(2,1)S(1)}, u32[]{:S(2)}, u32[]{:S(2)}) collective-permute-start(bf16[32,2048]{1,0:T(8,128)(2,1)S(1)} %get-tuple-element.85.refs_5_.refs_7_), channel_id=1, source_target_pairs={{3,2},{7,6},{11,10},{15,14},{19,18},{23,22},{27,26},{31,30}} | collective-permute-start | bytes 393224 | tf_op jit(solution)/shard_map/ppermute | solution.py:550
  19.1 4.5 %collective-permute-start.9 = (bf16[32,2048]{1,0:T(8,128)(2,1)S(1)}, bf16[32,2048]{1,0:T(8,128)(2,1)S(1)}, u32[]{:S(2)}, u32[]{:S(2)}) collective-permute-start(bf16[32,2048]{1,0:T(8,128)(2,1)S(1)} %get-tuple-element.90.refs_7_.refs_6_), channel_id=1, source_target_pairs={{3,2},{7,6},{11,10},{15,14},{19,18},{23,22},{27,26},{31,30}} | collective-permute-start | bytes 393224 | tf_op jit(solution)/shard_map/ppermute | solution.py:550
  19.8 4.4 %collective-permute-start.10 = (bf16[32,2048]{1,0:T(8,128)(2,1)S(1)}, bf16[32,2048]{1,0:T(8,128)(2,1)S(1)}, u32[]{:S(2)}, u32[]{:S(2)}) collective-permute-start(bf16[32,2048]{1,0:T(8,128)(2,1)S(1)} %get-tuple-element.91.refs_6_.refs_7_), channel_id=1, source_target_pairs={{3,2},{7,6},{11,10},{15,14},{19,18},{23,22},{27,26},{31,30}} | collective-permute-start | bytes 393224 | tf_op jit(solution)/shard_map/ppermute | solution.py:550
  20.5 9.8 %collective-permute-start.8 = (bf16[32,2048]{1,0:T(8,128)(2,1)S(1)}, bf16[32,2048]{1,0:T(8,128)(2,1)S(1)}, u32[]{:S(2)}, u32[]{:S(2)}) collective-permute-start(bf16[32,2048]{1,0:T(8,128)(2,1)S(1)} %get-tuple-element.92.refs_7_.refs_8_), channel_id=1, source_target_pairs={{2,1},{6,5},{10,9},{14,13},{18,17},{22,21},{26,25},{30,29}} | collective-permute-start | bytes 393224 | tf_op jit(solution)/shard_map/ppermute | solution.py:550
  21.3 10.3 %collective-permute-start.13 = (bf16[32,2048]{1,0:T(8,128)(2,1)S(1)}, bf16[32,2048]{1,0:T(8,128)(2,1)S(1)}, u32[]{:S(2)}, u32[]{:S(2)}) collective-permute-start(bf16[32,2048]{1,0:T(8,128)(2,1)S(1)} %get-tuple-element.93.refs_6_.refs_0_.refs_9_), channel_id=1, source_target_pairs={{2,1},{6,5},{10,9},{14,13},{18,17},{22,21},{26,25},{30,29}} | collective-permute-start | bytes 393224 | tf_op jit(solution)/shard_map/ppermute | solution.py:550
  21.9 5.6 %collective-permute-start.17 = (bf16[128,512]{1,0:T(8,128)(2,1)S(1)}, bf16[128,512]{1,0:T(8,128)(2,1)S(1)}, u32[]{:S(2)}, u32[]{:S(2)}) collective-permute-start(bf16[128,512]{1,0:T(8,128)(2,1)S(1)} %columns2.1), channel_id=1, source_target_pairs={{0,8},{4,12},{8,0},{12,4},{16,24},{20,28},{24,16},{28,20},{1,9},{5... | collective-permute-start | bytes 393224 | tf_op jit(solution)/shard_map/ppermute | solution.py:521
  23.6 9.3 %collective-permute-start.15 = (bf16[32,2048]{1,0:T(8,128)(2,1)S(1)}, bf16[32,2048]{1,0:T(8,128)(2,1)S(1)}, u32[]{:S(2)}, u32[]{:S(2)}) collective-permute-start(bf16[32,2048]{1,0:T(8,128)(2,1)S(1)} %get-tuple-element.94.refs_7_.refs_8_), channel_id=1, source_target_pairs={{2,1},{6,5},{10,9},{14,13},{18,17},{22,21},{26,25},{30,29}} | collective-permute-start | bytes 393224 | tf_op jit(solution)/shard_map/ppermute | solution.py:550
  24.4 9.8 %collective-permute-start.16 = (bf16[32,2048]{1,0:T(8,128)(2,1)S(1)}, bf16[32,2048]{1,0:T(8,128)(2,1)S(1)}, u32[]{:S(2)}, u32[]{:S(2)}) collective-permute-start(bf16[32,2048]{1,0:T(8,128)(2,1)S(1)} %get-tuple-element.95.refs_6_.after_ref.refs_0_.refs_9_), channel_id=1, source_target_pairs={{2,1},{6,5},{10,9},{14,13},{18,17},{22,21},{26,25},{30,29}} | collective-permute-start | bytes 393224 | tf_op jit(solution)/shard_map/ppermute | solution.py:550
  27.5 8.0 %collective-permute-start.18 = (bf16[128,512]{1,0:T(8,128)(2,1)S(1)}, bf16[128,512]{1,0:T(8,128)(2,1)S(1)}, u32[]{:S(2)}, u32[]{:S(2)}) collective-permute-start(bf16[128,512]{1,0:T(8,128)(2,1)S(1)} %columns6.1), channel_id=1, source_target_pairs={{0,24},{4,28},{8,16},{12,20},{16,8},{20,12},{24,0},{28,4},{1,25},{... | collective-permute-start | bytes 393224 | tf_op jit(solution)/shard_map/ppermute | solution.py:521
  30.3 8.7 %collective-permute-start.12 = (bf16[32,2048]{1,0:T(8,128)(2,1)S(1)}, bf16[32,2048]{1,0:T(8,128)(2,1)S(1)}, u32[]{:S(2)}, u32[]{:S(2)}) collective-permute-start(bf16[32,2048]{1,0:T(8,128)(2,1)S(1)} %get-tuple-element.96.refs_7_.refs_10_), channel_id=1, source_target_pairs={{1,0},{5,4},{9,8},{13,12},{17,16},{21,20},{25,24},{29,28}} | collective-permute-start | bytes 393224 | tf_op jit(solution)/shard_map/ppermute | solution.py:550
  31.6 10.2 %collective-permute-start.14 = (bf16[32,2048]{1,0:T(8,128)(2,1)S(1)}, bf16[32,2048]{1,0:T(8,128)(2,1)S(1)}, u32[]{:S(2)}, u32[]{:S(2)}) collective-permute-start(bf16[32,2048]{1,0:T(8,128)(2,1)S(1)} %get-tuple-element.97.refs_6_.refs_11_), channel_id=1, source_target_pairs={{1,0},{5,4},{9,8},{13,12},{17,16},{21,20},{25,24},{29,28}} | collective-permute-start | bytes 393224 | tf_op jit(solution)/shard_map/ppermute | solution.py:550
  33.0 13.2 %collective-permute-start.20 = (bf16[32,2048]{1,0:T(8,128)(2,1)S(1)}, bf16[32,2048]{1,0:T(8,128)(2,1)S(1)}, u32[]{:S(2)}, u32[]{:S(2)}) collective-permute-start(bf16[32,2048]{1,0:T(8,128)(2,1)S(1)} %get-tuple-element.104.refs_7_.refs_10_), channel_id=1, source_target_pairs={{1,0},{5,4},{9,8},{13,12},{17,16},{21,20},{25,24},{29,28}} | collective-permute-start | bytes 393224 | tf_op jit(solution)/shard_map/ppermute | solution.py:550
  34.3 12.7 %collective-permute-start.21 = (bf16[32,2048]{1,0:T(8,128)(2,1)S(1)}, bf16[32,2048]{1,0:T(8,128)(2,1)S(1)}, u32[]{:S(2)}, u32[]{:S(2)}) collective-permute-start(bf16[32,2048]{1,0:T(8,128)(2,1)S(1)} %get-tuple-element.105.refs_12_.refs_11_), channel_id=1, source_target_pairs={{1,0},{5,4},{9,8},{13,12},{17,16},{21,20},{25,24},{29,28}} | collective-permute-start | bytes 393224 | tf_op jit(solution)/shard_map/ppermute | solution.py:550
  42.6 6.8 %collective-permute-start.23 = (bf16[64,512]{1,0:T(8,128)(2,1)S(1)}, bf16[64,512]{1,0:T(8,128)(2,1)S(1)}, u32[]{:S(2)}, u32[]{:S(2)}) collective-permute-start(bf16[64,512]{1,0:T(8,128)(2,1)S(1)} %get-tuple-element.119.refs_17_.refs_0_), channel_id=1, source_target_pairs={{0,24},{4,28},{8,16},{12,20},{16,8},{20,12},{24,0},{28,4},{1,25},{... | collective-permute-start | bytes 196616 | tf_op jit(solution)/shard_map/ppermute | solution.py:521
  43.2 8.3 %collective-permute-start.22 = (bf16[192,512]{1,0:T(8,128)(2,1)S(1)}, bf16[192,512]{1,0:T(8,128)(2,1)S(1)}, u32[]{:S(2)}, u32[]{:S(2)}) collective-permute-start(bf16[192,512]{1,0:T(8,128)(2,1)S(1)} %columns4.1), channel_id=1, source_target_pairs={{0,16},{4,20},{8,24},{12,28},{16,0},{20,4},{24,8},{28,12},{1,17},{... | collective-permute-start | bytes 589832 | tf_op jit(solution)/shard_map/ppermute | solution.py:521
  44.0 9.9 %collective-permute-start.19 = (bf16[48,2048]{1,0:T(8,128)(2,1)S(1)}, bf16[48,2048]{1,0:T(8,128)(2,1)S(1)}, u32[]{:S(2)}, u32[]{:S(2)}) collective-permute-start(bf16[48,2048]{1,0:T(8,128)(2,1)S(1)} %get-tuple-element.109), channel_id=1, source_target_pairs={{0,8},{4,12},{8,0},{12,4},{16,24},{20,28},{24,16},{28,20},{1,9},{5... | collective-permute-start | bytes 589832 | tf_op jit(solution)/shard_map/ppermute | solution.py:521
  47.9 6.0 %collective-permute-start.24 = (bf16[64,512]{1,0:T(8,128)(2,1)S(1)}, bf16[64,512]{1,0:T(8,128)(2,1)S(1)}, u32[]{:S(2)}, u32[]{:S(2)}) collective-permute-start(bf16[64,512]{1,0:T(8,128)(2,1)S(1)} %get-tuple-element.120.refs_1_), channel_id=1, source_target_pairs={{0,24},{4,28},{8,16},{12,20},{16,8},{20,12},{24,0},{28,4},{1,25},{... | collective-permute-start | bytes 196616 | tf_op jit(solution)/shard_map/ppermute | solution.py:521
  48.8 5.6 %collective-permute-start.27 = (bf16[32,2048]{1,0:T(8,128)(2,1)S(1)}, bf16[32,2048]{1,0:T(8,128)(2,1)S(1)}, u32[]{:S(2)}, u32[]{:S(2)}) collective-permute-start(bf16[32,2048]{1,0:T(8,128)(2,1)S(1)} %get-tuple-element.124), channel_id=1, source_target_pairs={{0,8},{4,12},{8,0},{12,4},{16,24},{20,28},{24,16},{28,20},{1,9},{5... | collective-permute-start | bytes 393224 | tf_op jit(solution)/shard_map/ppermute | solution.py:521
  49.5 4.7 %collective-permute-start.29 = (bf16[64,512]{1,0:T(8,128)(2,1)S(1)}, bf16[64,512]{1,0:T(8,128)(2,1)S(1)}, u32[]{:S(2)}, u32[]{:S(2)}) collective-permute-start(bf16[64,512]{1,0:T(8,128)(2,1)S(1)} %get-tuple-element.120.refs_1_), channel_id=1, source_target_pairs={{0,16},{4,20},{8,24},{12,28},{16,0},{20,4},{24,8},{28,12},{1,17},{... | collective-permute-start | bytes 196616 | tf_op jit(solution)/shard_map/ppermute | solution.py:521
  51.4 6.1 %collective-permute-start.26 = (bf16[32,2048]{1,0:T(8,128)(2,1)S(1)}, bf16[32,2048]{1,0:T(8,128)(2,1)S(1)}, u32[]{:S(2)}, u32[]{:S(2)}) collective-permute-start(bf16[32,2048]{1,0:T(8,128)(2,1)S(1)} %get-tuple-element.123), channel_id=1, source_target_pairs={{0,4},{4,0},{8,12},{12,8},{16,20},{20,16},{24,28},{28,24},{1,5},{5... | collective-permute-start | bytes 393224 | tf_op jit(solution)/shard_map/ppermute | solution.py:521
  53.8 3.7 %collective-permute-start.28 = (bf16[16,2048]{1,0:T(8,128)(2,1)S(1)}, bf16[16,2048]{1,0:T(8,128)(2,1)S(1)}, u32[]{:S(2)}, u32[]{:S(2)}) collective-permute-start(bf16[16,2048]{1,0:T(8,128)(2,1)S(1)} %get-tuple-element.125), channel_id=1, source_target_pairs={{0,12},{4,8},{8,4},{12,0},{16,28},{20,24},{24,20},{28,16},{1,13},{... | collective-permute-start | bytes 196616 | tf_op jit(solution)/shard_map/ppermute | solution.py:521
  53.9 3.7 %collective-permute-start.25 = (bf16[16,2048]{1,0:T(8,128)(2,1)S(1)}, bf16[16,2048]{1,0:T(8,128)(2,1)S(1)}, u32[]{:S(2)}, u32[]{:S(2)}) collective-permute-start(bf16[16,2048]{1,0:T(8,128)(2,1)S(1)} %get-tuple-element.121), channel_id=1, source_target_pairs={{0,4},{4,0},{8,12},{12,8},{16,20},{20,16},{24,28},{28,24},{1,5},{5... | collective-permute-start | bytes 196616 | tf_op jit(solution)/shard_map/ppermute | solution.py:521
  54.8 3.6 %collective-permute-start.30 = (bf16[256,512]{1,0:T(8,128)(2,1)S(1)}, bf16[256,512]{1,0:T(8,128)(2,1)S(1)}, u32[]{:S(2)}, u32[]{:S(2)}) collective-permute-start(bf16[256,512]{1,0:T(8,128)(2,1)S(1)} %partial_other.1.refs_10_), channel_id=1, source_target_pairs={{0,4},{4,0},{8,12},{12,8},{16,20},{20,16},{24,28},{28,24},{1,5},{5... | collective-permute-start | bytes 786440 | tf_op jit(solution)/shard_map/ppermute | solution.py:521
  (1 other events, 4.5 us)

commit v20 on v18

--- a/solution.py
+++ b/solution.py
@@ -400,8 +400,6 @@
     if distance == 0:
         came_ref, out_ref, handed_ref = refs[0], refs[-2], refs[-1]
         handed_ref[...] = came_ref[came_ref.shape[0] - handed_ref.shape[0] :, :]
-    if distance == 4:
-        out_ref[2 * BLOCK :, :] = refs[0][...]
     there = lax.div(lax.bitwise_xor(place()[2], distance), 2)
     out_ref[:BLOCK, :] = first_ref[:, columns_of(there, width)]
     out_ref[BLOCK : 2 * BLOCK, :] = second_ref[:, columns_of(there, width)]
@@ -413,8 +411,6 @@
     shapes = [(2 * BLOCK, width)]
     if distance == 0:
         shapes.append((came[0].shape[0] // 3, model_width))
-    if distance == 4:
-        shapes = [(3 * BLOCK, width)]
     outs = [jax.ShapeDtypeStruct(shape, jnp.bfloat16) for shape in shapes]
     results = pl.pallas_call(
         functools.partial(columns_kernel, width, distance),
@@ -448,7 +444,6 @@
         beside = ref.shape[1] > kv_width
         rows = slice(first, 2 * first) if beside else slice(0, ref.shape[0])
         parts += [ref[rows, at : at + kv_width] for at in range(0, ref.shape[1], kv_width)]
-    parts.insert(len(parts) - 3, columns[2][2 * BLOCK :, :])
     value = jnp.concatenate(parts, axis=0)
     mine = lax.rem(place()[2], 2)
     core = 1 - mine if for_other else mine
@@ -573,7 +568,7 @@
             if last and u == 3:
                 late = [done[2][1], done[2][0], done[0][0], done[1][0], done[1][1]]
                 first_rows, far_first = swap(done[1][2], 2), swap(done[1][1], 6)
-                columns[4] = swap(columns_for(4, blocks, [], [done[1][1]]), 4)
+                columns[4] = swap(columns_for(4, blocks, [done[1][0]]), 4)
                 after = after + [columns[2]]
             done.append(
                 tick_step(
@@ -585,7 +580,7 @@
             kept[u].append(done[u])
     own_value, own_values, *rows = done[3]
     rows = [rows[0]] + [swap(rows[k], k) for k in range(1, half)]
-    far_value, across_value = swap(own_value, 6), swap(own_value, 4)
+    far_value, across_value = swap(own_value, 6), swap(own_values, 4)
     columns[0], handed = columns_for(0, blocks, [own_value, columns[4], far_first, far_value], [first_rows])
     handed = swap(handed, 1)
     values = [own_values, first_rows, rows[2], across_value, far_first, far_value]

time: 58.3 us -> 60.4 us (1.036)
  the two profiles are of different devices: /device:TPU:0 before, /device:TPU:11 now
where the time goes in v20:
time: 60.4 us; the launch traced here: 60.1 us
  starting transfers between devices  33.1 us (55%)
  waiting for transfers between devices  16.1 us (27%)
  Pallas kernels  9.87 us (16%)
  between operations  1.04 us (2%)
    ppermute x19, starting transfers between devices, swap(): return lax.ppermute(array, 'dp', [(i, i ^ k) for i in range(replicas)])  20 us
    ppermute x12, starting transfers between devices, direct(): lax.ppermute(unit[-1][0], 'section', hop)  13 us
    ppermute x19, waiting for transfers between devices, swap(): return lax.ppermute(array, 'dp', [(i, i ^ k) for i in range(replicas)])  11.9 us
    ppermute x12, waiting for transfers between devices, direct(): lax.ppermute(unit[-1][0], 'section', hop)  4.22 us
    pallas_call x16, Pallas kernels, tick_step(): pl.pallas_call(functools.partial(tick_kernel, tick, EARLY if low else LAT...  3.41 us
    pallas_call x2, Pallas kernels, pack(): pl.pallas_call(functools.partial(pack_kernel, block, half, piece), out_sh...  3.06 us
  transfers between devices with their start and end apart: 31, of which 10 were waited for; matrix products, arithmetic and copies ran while one was open for 0% of the time, Pallas kernels for 12%

profile of v20, /device:TPU:11, one launch (start us, length us, event | category | flops | bytes accessed | tf_op | source)
XLA Modules:
  0.0 60.1 jit_solution(3125574258615595656)
XLA Ops:
  0.7 1.4 %pack.2 = (bf16[16,4608]{1,0:T(8,128)(2,1)S(1)}, bf16[16,4608]{1,0:T(8,128)(2,1)S(1)}, bf16[16,4608]{1,0:T(8,128)(2,1)S(1)}, bf16[16,4608]{1,0:T(8,128)(2,1)S(1)}, bf16[80,2048]{1,0:T(8,128)(2,1)S(1)}) custom-call(bf16[128,2048]{1,0:T(8,128)(2,1)} %bitcast.8, bf16[128,512]{1,0:T(8,128)(2,1)} %bitcast.13, bf16[128,2048]{1,0:T(8,128)(2,1)} %bitcast.10, ...), custom_call_target="tpu_custom_call" | custom-call | flops 1380000000 | tf_op jit(solution)/shard_map/pack/pallas_call | solution.py:383
  2.0 0.7 %collective-permute-start = (bf16[16,4608]{1,0:T(8,128)(2,1)S(1)}, bf16[16,4608]{1,0:T(8,128)(2,1)S(1)}, u32[]{:S(2)}, u32[]{:S(2)}) collective-permute-start(bf16[16,4608]{1,0:T(8,128)(2,1)S(1)} %get-tuple-element.70), channel_id=1, source_target_pairs={{0,4},{4,0},{8,12},{12,8},{16,20},{20,16},{24,28},{28,24},{1,5},{5... | collective-permute-start | bytes 442376 | tf_op jit(solution)/shard_map/ppermute | solution.py:516
  3.0 1.4 %collective-permute-start.2 = (bf16[16,4608]{1,0:T(8,128)(2,1)S(1)}, bf16[16,4608]{1,0:T(8,128)(2,1)S(1)}, u32[]{:S(2)}, u32[]{:S(2)}) collective-permute-start(bf16[16,4608]{1,0:T(8,128)(2,1)S(1)} %get-tuple-element.72), channel_id=1, source_target_pairs={{0,12},{4,8},{8,4},{12,0},{16,28},{20,24},{24,20},{28,16},{1,13},{... | collective-permute-start | bytes 442376 | tf_op jit(solution)/shard_map/ppermute | solution.py:516
  4.5 1.7 %pack.3 = (f32[1,2048]{1,0:T(1,128)S(1)}, bf16[512,2048]{1,0:T(8,128)(2,1)S(1)}, bf16[16,4608]{1,0:T(8,128)(2,1)S(1)}, bf16[16,4608]{1,0:T(8,128)(2,1)S(1)}, bf1...) custom-call(bf16[128,2048]{1,0:T(8,128)(2,1)} %bitcast.9, ...), custom_call_target="tpu_custom_call" | custom-call | flops 1380000000 | tf_op jit(solution)/shard_map/pack/pallas_call | solution.py:383
  6.2 1.3 %collective-permute-start.4 = (bf16[80,2048]{1,0:T(8,128)(2,1)S(1)}, bf16[80,2048]{1,0:T(8,128)(2,1)S(1)}, u32[]{:S(2)}, u32[]{:S(2)}) collective-permute-start(bf16[80,2048]{1,0:T(8,128)(2,1)S(1)} %get-tuple-element.79), channel_id=1, source_target_pairs={{0,16},{4,20},{8,24},{12,28},{16,0},{20,4},{24,8},{28,12},{1,17},{... | collective-permute-start | bytes 983048 | tf_op jit(solution)/shard_map/ppermute | solution.py:516
  8.2 1.4 %collective-permute-start.7 = (bf16[16,4608]{1,0:T(8,128)(2,1)S(1)}, bf16[16,4608]{1,0:T(8,128)(2,1)S(1)}, u32[]{:S(2)}, u32[]{:S(2)}) collective-permute-start(bf16[16,4608]{1,0:T(8,128)(2,1)S(1)} %get-tuple-element.83), channel_id=1, source_target_pairs={{0,12},{4,8},{8,4},{12,0},{16,28},{20,24},{24,20},{28,16},{1,13},{... | collective-permute-start | bytes 442376 | tf_op jit(solution)/shard_map/ppermute | solution.py:516
  9.6 2.6 %collective-permute-done.2.refs_3_ = bf16[16,4608]{1,0:T(8,128)(2,1)S(1)} collective-permute-done((bf16[16,4608]{1,0:T(8,128)(2,1)S(1)}, bf16[16,4608]{1,0:T(8,128)(2,1)S(1)}, u32[]{:S(2)}, u32[]{:S(2)}) %collective-permute-start.2) | collective-permute-done | bytes 147488 | tf_op jit(solution)/shard_map/ppermute | solution.py:516
  14.5 3.3 %collective-permute-done.7.refs_3_ = bf16[16,4608]{1,0:T(8,128)(2,1)S(1)} collective-permute-done((bf16[16,4608]{1,0:T(8,128)(2,1)S(1)}, bf16[16,4608]{1,0:T(8,128)(2,1)S(1)}, u32[]{:S(2)}, u32[]{:S(2)}) %collective-permute-start.7) | collective-permute-done | bytes 147488 | tf_op jit(solution)/shard_map/ppermute | solution.py:516
  19.6 1.3 %collective-permute-start.8 = (bf16[32,2048]{1,0:T(8,128)(2,1)S(1)}, bf16[32,2048]{1,0:T(8,128)(2,1)S(1)}, u32[]{:S(2)}, u32[]{:S(2)}) collective-permute-start(bf16[32,2048]{1,0:T(8,128)(2,1)S(1)} %get-tuple-element.92.refs_7_.refs_8_), channel_id=1, source_target_pairs={{2,1},{6,5},{10,9},{14,13},{18,17},{22,21},{26,25},{30,29}} | collective-permute-start | bytes 393224 | tf_op jit(solution)/shard_map/ppermute | solution.py:545
  20.9 1.3 %collective-permute-start.13 = (bf16[32,2048]{1,0:T(8,128)(2,1)S(1)}, bf16[32,2048]{1,0:T(8,128)(2,1)S(1)}, u32[]{:S(2)}, u32[]{:S(2)}) collective-permute-start(bf16[32,2048]{1,0:T(8,128)(2,1)S(1)} %get-tuple-element.93.refs_6_.refs_9_), channel_id=1, source_target_pairs={{2,1},{6,5},{10,9},{14,13},{18,17},{22,21},{26,25},{30,29}} | collective-permute-start | bytes 393224 | tf_op jit(solution)/shard_map/ppermute | solution.py:545
  22.3 1.3 %collective-permute-start.15 = (bf16[32,2048]{1,0:T(8,128)(2,1)S(1)}, bf16[32,2048]{1,0:T(8,128)(2,1)S(1)}, u32[]{:S(2)}, u32[]{:S(2)}) collective-permute-start(bf16[32,2048]{1,0:T(8,128)(2,1)S(1)} %get-tuple-element.94.refs_7_.refs_8_), channel_id=1, source_target_pairs={{2,1},{6,5},{10,9},{14,13},{18,17},{22,21},{26,25},{30,29}} | collective-permute-start | bytes 393224 | tf_op jit(solution)/shard_map/ppermute | solution.py:545
  23.6 1.3 %collective-permute-start.16 = (bf16[32,2048]{1,0:T(8,128)(2,1)S(1)}, bf16[32,2048]{1,0:T(8,128)(2,1)S(1)}, u32[]{:S(2)}, u32[]{:S(2)}) collective-permute-start(bf16[32,2048]{1,0:T(8,128)(2,1)S(1)} %get-tuple-element.95.refs_6_.after_ref.refs_0_.refs_9_), channel_id=1, source_target_pairs={{2,1},{6,5},{10,9},{14,13},{18,17},{22,21},{26,25},{30,29}} | collective-permute-start | bytes 393224 | tf_op jit(solution)/shard_map/ppermute | solution.py:545
  25.1 1.3 %collective-permute-start.20 = (bf16[128,512]{1,0:T(8,128)(2,1)S(1)}, bf16[128,512]{1,0:T(8,128)(2,1)S(1)}, u32[]{:S(2)}, u32[]{:S(2)}) collective-permute-start(bf16[128,512]{1,0:T(8,128)(2,1)S(1)} %columns6.1), channel_id=1, source_target_pairs={{0,24},{4,28},{8,16},{12,20},{16,8},{20,12},{24,0},{28,4},{1,25},{... | collective-permute-start | bytes 393224 | tf_op jit(solution)/shard_map/ppermute | solution.py:516
  26.4 2.0 %collective-permute-done.8.refs_0_ = bf16[32,2048]{1,0:T(8,128)(2,1)S(1)} collective-permute-done((bf16[32,2048]{1,0:T(8,128)(2,1)S(1)}, bf16[32,2048]{1,0:T(8,128)(2,1)S(1)}, u32[]{:S(2)}, u32[]{:S(2)}) %collective-permute-start.8) | collective-permute-done | bytes 131104 | tf_op jit(solution)/shard_map/ppermute | solution.py:545
  28.4 0.8 %tick2_a_late.1 = (bf16[32,2048]{1,0:T(8,128)(2,1)S(1)}, bf16[32,512]{1,0:T(8,128)(2,1)S(1)}) custom-call(bf16[32,2048]{1,0:T(8,128)(2,1)S(1)} %collective-permute-done.8.refs_0_, bf16[4,32,128]{2,1,0:T(8,128)(2,1)S(1)} %get-tuple-element.73.refs_1_, f32[64,128]{1,0:T(8,128)S(1)} %get-tuple-element.74.refs_2_.refs_3_, ...), custom_call_target="tpu_custom_call" | custom-call | tf_op jit(solution)/shard_map/tick2_a_late/pallas_call | solution.py:319
  29.2 1.3 %collective-permute-start.12 = (bf16[32,2048]{1,0:T(8,128)(2,1)S(1)}, bf16[32,2048]{1,0:T(8,128)(2,1)S(1)}, u32[]{:S(2)}, u32[]{:S(2)}) collective-permute-start(bf16[32,2048]{1,0:T(8,128)(2,1)S(1)} %get-tuple-element.96.refs_7_.refs_10_), channel_id=1, source_target_pairs={{1,0},{5,4},{9,8},{13,12},{17,16},{21,20},{25,24},{29,28}} | collective-permute-start | bytes 393224 | tf_op jit(solution)/shard_map/ppermute | solution.py:545
  31.2 0.8 %tick2_a_early.1 = (bf16[32,2048]{1,0:T(8,128)(2,1)S(1)}, bf16[32,512]{1,0:T(8,128)(2,1)S(1)}) custom-call(bf16[32,2048]{1,0:T(8,128)(2,1)S(1)} %collective-permute-done.8.refs_0_, bf16[32,2048]{1,0:T(8,128)(2,1)S(1)} %collective-permute-done.13.refs_1_, bf16[4,32,256]{2,1,0:T(8,128)(2,1)S(1)} %get-tuple-element.84.refs_2_, ...), custom_call_target="tpu_custom_call" | custom-call | tf_op jit(solution)/shard_map/tick2_a_early/pallas_call | solution.py:319
  32.0 1.3 %collective-permute-start.14 = (bf16[32,2048]{1,0:T(8,128)(2,1)S(1)}, bf16[32,2048]{1,0:T(8,128)(2,1)S(1)}, u32[]{:S(2)}, u32[]{:S(2)}) collective-permute-start(bf16[32,2048]{1,0:T(8,128)(2,1)S(1)} %get-tuple-element.97.refs_6_.refs_11_), channel_id=1, source_target_pairs={{1,0},{5,4},{9,8},{13,12},{17,16},{21,20},{25,24},{29,28}} | collective-permute-start | bytes 393224 | tf_op jit(solution)/shard_map/ppermute | solution.py:545
  34.0 0.8 %tick2_b_late.1 = (bf16[32,2048]{1,0:T(8,128)(2,1)S(1)}, bf16[32,512]{1,0:T(8,128)(2,1)S(1)}) custom-call(bf16[32,2048]{1,0:T(8,128)(2,1)S(1)} %collective-permute-done.15.refs_0_, bf16[4,32,128]{2,1,0:T(8,128)(2,1)S(1)} %get-tuple-element.89.refs_1_, f32[64,128]{1,0:T(8,128)S(1)} %get-tuple-element.87.refs_2_.refs_3_, ...), custom_call_target="tpu_custom_call" | custom-call | tf_op jit(solution)/shard_map/tick2_b_late/pallas_call | solution.py:319
  34.8 1.3 %collective-permute-start.18 = (bf16[32,2048]{1,0:T(8,128)(2,1)S(1)}, bf16[32,2048]{1,0:T(8,128)(2,1)S(1)}, u32[]{:S(2)}, u32[]{:S(2)}) collective-permute-start(bf16[32,2048]{1,0:T(8,128)(2,1)S(1)} %get-tuple-element.104.refs_7_.refs_10_), channel_id=1, source_target_pairs={{1,0},{5,4},{9,8},{13,12},{17,16},{21,20},{25,24},{29,28}} | collective-permute-start | bytes 393224 | tf_op jit(solution)/shard_map/ppermute | solution.py:545
  36.8 0.8 %tick2_b_early.1 = (bf16[32,2048]{1,0:T(8,128)(2,1)S(1)}, bf16[32,512]{1,0:T(8,128)(2,1)S(1)}) custom-call(bf16[32,2048]{1,0:T(8,128)(2,1)S(1)} %collective-permute-done.15.refs_0_, bf16[32,2048]{1,0:T(8,128)(2,1)S(1)} %collective-permute-done.16.refs_1_, bf16[4,32,256]{2,1,0:T(8,128)(2,1)S(1)} %get-tuple-element.86.refs_2_, ...), custom_call_target="tpu_custom_call" | custom-call | tf_op jit(solution)/shard_map/tick2_b_early/pallas_call | solution.py:319
  37.6 1.3 %collective-permute-start.19 = (bf16[32,2048]{1,0:T(8,128)(2,1)S(1)}, bf16[32,2048]{1,0:T(8,128)(2,1)S(1)}, u32[]{:S(2)}, u32[]{:S(2)}) collective-permute-start(bf16[32,2048]{1,0:T(8,128)(2,1)S(1)} %get-tuple-element.105.refs_12_.refs_0_.refs_11_), channel_id=1, source_target_pairs={{1,0},{5,4},{9,8},{13,12},{17,16},{21,20},{25,24},{29,28}} | collective-permute-start | bytes 393224 | tf_op jit(solution)/shard_map/ppermute | solution.py:545
  39.4 1.3 %collective-permute-start.17 = (bf16[48,2048]{1,0:T(8,128)(2,1)S(1)}, bf16[48,2048]{1,0:T(8,128)(2,1)S(1)}, u32[]{:S(2)}, u32[]{:S(2)}) collective-permute-start(bf16[48,2048]{1,0:T(8,128)(2,1)S(1)} %get-tuple-element.108), channel_id=1, source_target_pairs={{0,8},{4,12},{8,0},{12,4},{16,24},{20,28},{24,16},{28,20},{1,9},{5... | collective-permute-start | bytes 589832 | tf_op jit(solution)/shard_map/ppermute | solution.py:516
  40.7 1.3 %collective-permute-start.22 = (bf16[128,512]{1,0:T(8,128)(2,1)S(1)}, bf16[128,512]{1,0:T(8,128)(2,1)S(1)}, u32[]{:S(2)}, u32[]{:S(2)}) collective-permute-start(bf16[128,512]{1,0:T(8,128)(2,1)S(1)} %columns4.1), channel_id=1, source_target_pairs={{0,16},{4,20},{8,24},{12,28},{16,0},{20,4},{24,8},{28,12},{1,17},{... | collective-permute-start | bytes 393224 | tf_op jit(solution)/shard_map/ppermute | solution.py:516
  42.2 1.3 %collective-permute-done.21.refs_19_.refs_1_ = bf16[128,512]{1,0:T(8,128)(2,1)S(1)} collective-permute-done((bf16[128,512]{1,0:T(8,128)(2,1)S(1)}, bf16[128,512]{1,0:T(8,128)(2,1)S(1)}, u32[]{:S(2)}, u32[]{:S(2)}) %collective-permute-start.21) | collective-permute-done | bytes 131104 | tf_op jit(solution)/shard_map/ppermute | solution.py:516
  43.7 1.3 %collective-permute-start.24 = (bf16[64,512]{1,0:T(8,128)(2,1)S(1)}, bf16[64,512]{1,0:T(8,128)(2,1)S(1)}, u32[]{:S(2)}, u32[]{:S(2)}) collective-permute-start(bf16[64,512]{1,0:T(8,128)(2,1)S(1)} %get-tuple-element.120.refs_1_), channel_id=1, source_target_pairs={{0,24},{4,28},{8,16},{12,20},{16,8},{20,12},{24,0},{28,4},{1,25},{... | collective-permute-start | bytes 196616 | tf_op jit(solution)/shard_map/ppermute | solution.py:516
  44.9 1.2 %collective-permute-start.27 = (bf16[32,2048]{1,0:T(8,128)(2,1)S(1)}, bf16[32,2048]{1,0:T(8,128)(2,1)S(1)}, u32[]{:S(2)}, u32[]{:S(2)}) collective-permute-start(bf16[32,2048]{1,0:T(8,128)(2,1)S(1)} %get-tuple-element.124), channel_id=1, source_target_pairs={{0,8},{4,12},{8,0},{12,4},{16,24},{20,28},{24,16},{28,20},{1,9},{5... | collective-permute-start | bytes 393224 | tf_op jit(solution)/shard_map/ppermute | solution.py:516
  46.2 3.7 %collective-permute-done.23.refs_3_.refs_8_ = bf16[64,512]{1,0:T(8,128)(2,1)S(1)} collective-permute-done((bf16[64,512]{1,0:T(8,128)(2,1)S(1)}, bf16[64,512]{1,0:T(8,128)(2,1)S(1)}, u32[]{:S(2)}, u32[]{:S(2)}) %collective-permute-start.23) | collective-permute-done | bytes 65568 | tf_op jit(solution)/shard_map/ppermute | solution.py:516
  50.1 2.9 %collective-permute-start.26 = (bf16[32,2048]{1,0:T(8,128)(2,1)S(1)}, bf16[32,2048]{1,0:T(8,128)(2,1)S(1)}, u32[]{:S(2)}, u32[]{:S(2)}) collective-permute-start(bf16[32,2048]{1,0:T(8,128)(2,1)S(1)} %get-tuple-element.123), channel_id=1, source_target_pairs={{0,4},{4,0},{8,12},{12,8},{16,20},{20,16},{24,28},{28,24},{1,5},{5... | collective-permute-start | bytes 393224 | tf_op jit(solution)/shard_map/ppermute | solution.py:516
  54.7 3.1 %collective-permute-start.30 = (bf16[256,512]{1,0:T(8,128)(2,1)S(1)}, bf16[256,512]{1,0:T(8,128)(2,1)S(1)}, u32[]{:S(2)}, u32[]{:S(2)}) collective-permute-start(bf16[256,512]{1,0:T(8,128)(2,1)S(1)} %partial_other.1.refs_10_), channel_id=1, source_target_pairs={{0,4},{4,0},{8,12},{12,8},{16,20},{20,16},{24,28},{28,24},{1,5},{5... | collective-permute-start | bytes 786440 | tf_op jit(solution)/shard_map/ppermute | solution.py:516
  58.2 0.8 %rows.1 = (bf16[128,2048]{1,0:T(8,128)(2,1)}, f32[8,128]{1,0:T(8,128)S(1)}) custom-call(bf16[48,2048]{1,0:T(8,128)(2,1)S(1)} %collective-permute-done.17.refs_0_.first_rows_ref.refs_5_, bf16[16,2048]{1,0:T(8,128)(2,1)S(1)} %collective-permute-done.25.handed_ref, bf16[32,2048]{1,0:T(8,128)(2,1)S(1)} %get-tuple-element.122.refs_0_, ...), custom_call_target="tpu_custom_call" | custom-call | flops 2875000064 | tf_op jit(solution)/shard_map/rows/pallas_call | solution.py:590
  59.1 1.0 %finish.1 = (f32[256,512]{1,0:T(8,128)}, f32[1,256]{1,0:T(1,128)}) custom-call(f32[256,512]{1,0:T(8,128)S(1)} %partial_own.1.own_ref, bf16[256,512]{1,0:T(8,128)(2,1)S(1)} %collective-permute-done.30.other_ref, f32[256,512]{1,0:T(8,128)S(1)} %get-tuple-element.129.weight_ref, f32[256,128]{1,0:T(8,128)S(1)} %get-tuple-element.119.refs_1_.gain_ref, ...), custom_call_target="tpu_custom_call" | custom-call | tf_op jit(solution)/shard_map/finish/pallas_call | solution.py:601
  (63 shorter events, 10.3 us)
Async XLA Ops:
  0.6 3.8 %copy-start = (bf16[1,2048,512]{2,1,0:T(8,128)(2,1)S(1)}, bf16[1,2048,512]{2,1,0:T(8,128)(2,1)}, u32[]{:S(2)}) copy-start(bf16[1,2048,512]{2,1,0:T(8,128)(2,1)} %param.11) | copy-start | bytes 6291460
  2.0 5.9 %collective-permute-start = (bf16[16,4608]{1,0:T(8,128)(2,1)S(1)}, bf16[16,4608]{1,0:T(8,128)(2,1)S(1)}, u32[]{:S(2)}, u32[]{:S(2)}) collective-permute-start(bf16[16,4608]{1,0:T(8,128)(2,1)S(1)} %get-tuple-element.70), channel_id=1, source_target_pairs={{0,4},{4,0},{8,12},{12,8},{16,20},{20,16},{24,28},{28,24},{1,5},{5... | collective-permute-start | bytes 442376 | tf_op jit(solution)/shard_map/ppermute | solution.py:516
  2.8 5.4 %collective-permute-start.1 = (bf16[16,4608]{1,0:T(8,128)(2,1)S(1)}, bf16[16,4608]{1,0:T(8,128)(2,1)S(1)}, u32[]{:S(2)}, u32[]{:S(2)}) collective-permute-start(bf16[16,4608]{1,0:T(8,128)(2,1)S(1)} %get-tuple-element.71), channel_id=1, source_target_pairs={{0,8},{4,12},{8,0},{12,4},{16,24},{20,28},{24,16},{28,20},{1,9},{5... | collective-permute-start | bytes 442376 | tf_op jit(solution)/shard_map/ppermute | solution.py:516
  3.0 9.2 %collective-permute-start.2 = (bf16[16,4608]{1,0:T(8,128)(2,1)S(1)}, bf16[16,4608]{1,0:T(8,128)(2,1)S(1)}, u32[]{:S(2)}, u32[]{:S(2)}) collective-permute-start(bf16[16,4608]{1,0:T(8,128)(2,1)S(1)} %get-tuple-element.72), channel_id=1, source_target_pairs={{0,12},{4,8},{8,4},{12,0},{16,28},{20,24},{24,20},{28,16},{1,13},{... | collective-permute-start | bytes 442376 | tf_op jit(solution)/shard_map/ppermute | solution.py:516
  6.2 11.6 %collective-permute-start.4 = (bf16[80,2048]{1,0:T(8,128)(2,1)S(1)}, bf16[80,2048]{1,0:T(8,128)(2,1)S(1)}, u32[]{:S(2)}, u32[]{:S(2)}) collective-permute-start(bf16[80,2048]{1,0:T(8,128)(2,1)S(1)} %get-tuple-element.79), channel_id=1, source_target_pairs={{0,16},{4,20},{8,24},{12,28},{16,0},{20,4},{24,8},{28,12},{1,17},{... | collective-permute-start | bytes 983048 | tf_op jit(solution)/shard_map/ppermute | solution.py:516
  7.5 5.8 %collective-permute-start.5 = (bf16[16,4608]{1,0:T(8,128)(2,1)S(1)}, bf16[16,4608]{1,0:T(8,128)(2,1)S(1)}, u32[]{:S(2)}, u32[]{:S(2)}) collective-permute-start(bf16[16,4608]{1,0:T(8,128)(2,1)S(1)} %get-tuple-element.81), channel_id=1, source_target_pairs={{0,4},{4,0},{8,12},{12,8},{16,20},{20,16},{24,28},{28,24},{1,5},{5... | collective-permute-start | bytes 442376 | tf_op jit(solution)/shard_map/ppermute | solution.py:516
  7.9 6.6 %collective-permute-start.6 = (bf16[16,4608]{1,0:T(8,128)(2,1)S(1)}, bf16[16,4608]{1,0:T(8,128)(2,1)S(1)}, u32[]{:S(2)}, u32[]{:S(2)}) collective-permute-start(bf16[16,4608]{1,0:T(8,128)(2,1)S(1)} %get-tuple-element.82), channel_id=1, source_target_pairs={{0,8},{4,12},{8,0},{12,4},{16,24},{20,28},{24,16},{28,20},{1,9},{5... | collective-permute-start | bytes 442376 | tf_op jit(solution)/shard_map/ppermute | solution.py:516
  8.2 9.6 %collective-permute-start.7 = (bf16[16,4608]{1,0:T(8,128)(2,1)S(1)}, bf16[16,4608]{1,0:T(8,128)(2,1)S(1)}, u32[]{:S(2)}, u32[]{:S(2)}) collective-permute-start(bf16[16,4608]{1,0:T(8,128)(2,1)S(1)} %get-tuple-element.83), channel_id=1, source_target_pairs={{0,12},{4,8},{8,4},{12,0},{16,28},{20,24},{24,20},{28,16},{1,13},{... | collective-permute-start | bytes 442376 | tf_op jit(solution)/shard_map/ppermute | solution.py:516
  12.6 7.0 %collective-permute-start.3 = (bf16[32,2048]{1,0:T(8,128)(2,1)S(1)}, bf16[32,2048]{1,0:T(8,128)(2,1)S(1)}, u32[]{:S(2)}, u32[]{:S(2)}) collective-permute-start(bf16[32,2048]{1,0:T(8,128)(2,1)S(1)} %get-tuple-element.78.refs_7_.refs_6_), channel_id=1, source_target_pairs={{3,2},{7,6},{11,10},{15,14},{19,18},{23,22},{27,26},{31,30}} | collective-permute-start | bytes 393224 | tf_op jit(solution)/shard_map/ppermute | solution.py:545
  13.3 7.6 %collective-permute-start.11 = (bf16[32,2048]{1,0:T(8,128)(2,1)S(1)}, bf16[32,2048]{1,0:T(8,128)(2,1)S(1)}, u32[]{:S(2)}, u32[]{:S(2)}) collective-permute-start(bf16[32,2048]{1,0:T(8,128)(2,1)S(1)} %get-tuple-element.85.refs_5_.refs_7_), channel_id=1, source_target_pairs={{3,2},{7,6},{11,10},{15,14},{19,18},{23,22},{27,26},{31,30}} | collective-permute-start | bytes 393224 | tf_op jit(solution)/shard_map/ppermute | solution.py:545
  18.2 4.0 %collective-permute-start.9 = (bf16[32,2048]{1,0:T(8,128)(2,1)S(1)}, bf16[32,2048]{1,0:T(8,128)(2,1)S(1)}, u32[]{:S(2)}, u32[]{:S(2)}) collective-permute-start(bf16[32,2048]{1,0:T(8,128)(2,1)S(1)} %get-tuple-element.90.refs_7_.refs_6_), channel_id=1, source_target_pairs={{3,2},{7,6},{11,10},{15,14},{19,18},{23,22},{27,26},{31,30}} | collective-permute-start | bytes 393224 | tf_op jit(solution)/shard_map/ppermute | solution.py:545
  18.9 4.7 %collective-permute-start.10 = (bf16[32,2048]{1,0:T(8,128)(2,1)S(1)}, bf16[32,2048]{1,0:T(8,128)(2,1)S(1)}, u32[]{:S(2)}, u32[]{:S(2)}) collective-permute-start(bf16[32,2048]{1,0:T(8,128)(2,1)S(1)} %get-tuple-element.91.refs_6_.refs_7_), channel_id=1, source_target_pairs={{3,2},{7,6},{11,10},{15,14},{19,18},{23,22},{27,26},{31,30}} | collective-permute-start | bytes 393224 | tf_op jit(solution)/shard_map/ppermute | solution.py:545
  19.6 8.8 %collective-permute-start.8 = (bf16[32,2048]{1,0:T(8,128)(2,1)S(1)}, bf16[32,2048]{1,0:T(8,128)(2,1)S(1)}, u32[]{:S(2)}, u32[]{:S(2)}) collective-permute-start(bf16[32,2048]{1,0:T(8,128)(2,1)S(1)} %get-tuple-element.92.refs_7_.refs_8_), channel_id=1, source_target_pairs={{2,1},{6,5},{10,9},{14,13},{18,17},{22,21},{26,25},{30,29}} | collective-permute-start | bytes 393224 | tf_op jit(solution)/shard_map/ppermute | solution.py:545
  20.9 10.3 %collective-permute-start.13 = (bf16[32,2048]{1,0:T(8,128)(2,1)S(1)}, bf16[32,2048]{1,0:T(8,128)(2,1)S(1)}, u32[]{:S(2)}, u32[]{:S(2)}) collective-permute-start(bf16[32,2048]{1,0:T(8,128)(2,1)S(1)} %get-tuple-element.93.refs_6_.refs_9_), channel_id=1, source_target_pairs={{2,1},{6,5},{10,9},{14,13},{18,17},{22,21},{26,25},{30,29}} | collective-permute-start | bytes 393224 | tf_op jit(solution)/shard_map/ppermute | solution.py:545
  22.3 11.8 %collective-permute-start.15 = (bf16[32,2048]{1,0:T(8,128)(2,1)S(1)}, bf16[32,2048]{1,0:T(8,128)(2,1)S(1)}, u32[]{:S(2)}, u32[]{:S(2)}) collective-permute-start(bf16[32,2048]{1,0:T(8,128)(2,1)S(1)} %get-tuple-element.94.refs_7_.refs_8_), channel_id=1, source_target_pairs={{2,1},{6,5},{10,9},{14,13},{18,17},{22,21},{26,25},{30,29}} | collective-permute-start | bytes 393224 | tf_op jit(solution)/shard_map/ppermute | solution.py:545
  23.6 13.2 %collective-permute-start.16 = (bf16[32,2048]{1,0:T(8,128)(2,1)S(1)}, bf16[32,2048]{1,0:T(8,128)(2,1)S(1)}, u32[]{:S(2)}, u32[]{:S(2)}) collective-permute-start(bf16[32,2048]{1,0:T(8,128)(2,1)S(1)} %get-tuple-element.95.refs_6_.after_ref.refs_0_.refs_9_), channel_id=1, source_target_pairs={{2,1},{6,5},{10,9},{14,13},{18,17},{22,21},{26,25},{30,29}} | collective-permute-start | bytes 393224 | tf_op jit(solution)/shard_map/ppermute | solution.py:545
  25.1 13.8 %collective-permute-start.20 = (bf16[128,512]{1,0:T(8,128)(2,1)S(1)}, bf16[128,512]{1,0:T(8,128)(2,1)S(1)}, u32[]{:S(2)}, u32[]{:S(2)}) collective-permute-start(bf16[128,512]{1,0:T(8,128)(2,1)S(1)} %columns6.1), channel_id=1, source_target_pairs={{0,24},{4,28},{8,16},{12,20},{16,8},{20,12},{24,0},{28,4},{1,25},{... | collective-permute-start | bytes 393224 | tf_op jit(solution)/shard_map/ppermute | solution.py:516
  29.2 10.1 %collective-permute-start.12 = (bf16[32,2048]{1,0:T(8,128)(2,1)S(1)}, bf16[32,2048]{1,0:T(8,128)(2,1)S(1)}, u32[]{:S(2)}, u32[]{:S(2)}) collective-permute-start(bf16[32,2048]{1,0:T(8,128)(2,1)S(1)} %get-tuple-element.96.refs_7_.refs_10_), channel_id=1, source_target_pairs={{1,0},{5,4},{9,8},{13,12},{17,16},{21,20},{25,24},{29,28}} | collective-permute-start | bytes 393224 | tf_op jit(solution)/shard_map/ppermute | solution.py:545
  32.0 7.3 %collective-permute-start.14 = (bf16[32,2048]{1,0:T(8,128)(2,1)S(1)}, bf16[32,2048]{1,0:T(8,128)(2,1)S(1)}, u32[]{:S(2)}, u32[]{:S(2)}) collective-permute-start(bf16[32,2048]{1,0:T(8,128)(2,1)S(1)} %get-tuple-element.97.refs_6_.refs_11_), channel_id=1, source_target_pairs={{1,0},{5,4},{9,8},{13,12},{17,16},{21,20},{25,24},{29,28}} | collective-permute-start | bytes 393224 | tf_op jit(solution)/shard_map/ppermute | solution.py:545
  34.8 7.2 %collective-permute-start.18 = (bf16[32,2048]{1,0:T(8,128)(2,1)S(1)}, bf16[32,2048]{1,0:T(8,128)(2,1)S(1)}, u32[]{:S(2)}, u32[]{:S(2)}) collective-permute-start(bf16[32,2048]{1,0:T(8,128)(2,1)S(1)} %get-tuple-element.104.refs_7_.refs_10_), channel_id=1, source_target_pairs={{1,0},{5,4},{9,8},{13,12},{17,16},{21,20},{25,24},{29,28}} | collective-permute-start | bytes 393224 | tf_op jit(solution)/shard_map/ppermute | solution.py:545
  37.6 4.6 %collective-permute-start.19 = (bf16[32,2048]{1,0:T(8,128)(2,1)S(1)}, bf16[32,2048]{1,0:T(8,128)(2,1)S(1)}, u32[]{:S(2)}, u32[]{:S(2)}) collective-permute-start(bf16[32,2048]{1,0:T(8,128)(2,1)S(1)} %get-tuple-element.105.refs_12_.refs_0_.refs_11_), channel_id=1, source_target_pairs={{1,0},{5,4},{9,8},{13,12},{17,16},{21,20},{25,24},{29,28}} | collective-permute-start | bytes 393224 | tf_op jit(solution)/shard_map/ppermute | solution.py:545
  39.0 4.6 %collective-permute-start.21 = (bf16[128,512]{1,0:T(8,128)(2,1)S(1)}, bf16[128,512]{1,0:T(8,128)(2,1)S(1)}, u32[]{:S(2)}, u32[]{:S(2)}) collective-permute-start(bf16[128,512]{1,0:T(8,128)(2,1)S(1)} %columns2.1), channel_id=1, source_target_pairs={{0,8},{4,12},{8,0},{12,4},{16,24},{20,28},{24,16},{28,20},{1,9},{5... | collective-permute-start | bytes 393224 | tf_op jit(solution)/shard_map/ppermute | solution.py:516
  39.4 13.6 %collective-permute-start.17 = (bf16[48,2048]{1,0:T(8,128)(2,1)S(1)}, bf16[48,2048]{1,0:T(8,128)(2,1)S(1)}, u32[]{:S(2)}, u32[]{:S(2)}) collective-permute-start(bf16[48,2048]{1,0:T(8,128)(2,1)S(1)} %get-tuple-element.108), channel_id=1, source_target_pairs={{0,8},{4,12},{8,0},{12,4},{16,24},{20,28},{24,16},{28,20},{1,9},{5... | collective-permute-start | bytes 589832 | tf_op jit(solution)/shard_map/ppermute | solution.py:516
  40.7 9.4 %collective-permute-start.22 = (bf16[128,512]{1,0:T(8,128)(2,1)S(1)}, bf16[128,512]{1,0:T(8,128)(2,1)S(1)}, u32[]{:S(2)}, u32[]{:S(2)}) collective-permute-start(bf16[128,512]{1,0:T(8,128)(2,1)S(1)} %columns4.1), channel_id=1, source_target_pairs={{0,16},{4,20},{8,24},{12,28},{16,0},{20,4},{24,8},{28,12},{1,17},{... | collective-permute-start | bytes 393224 | tf_op jit(solution)/shard_map/ppermute | solution.py:516
  42.0 7.9 %collective-permute-start.23 = (bf16[64,512]{1,0:T(8,128)(2,1)S(1)}, bf16[64,512]{1,0:T(8,128)(2,1)S(1)}, u32[]{:S(2)}, u32[]{:S(2)}) collective-permute-start(bf16[64,512]{1,0:T(8,128)(2,1)S(1)} %get-tuple-element.118.refs_17_), channel_id=1, source_target_pairs={{0,24},{4,28},{8,16},{12,20},{16,8},{20,12},{24,0},{28,4},{1,25},{... | collective-permute-start | bytes 196616 | tf_op jit(solution)/shard_map/ppermute | solution.py:516
  43.7 9.6 %collective-permute-start.24 = (bf16[64,512]{1,0:T(8,128)(2,1)S(1)}, bf16[64,512]{1,0:T(8,128)(2,1)S(1)}, u32[]{:S(2)}, u32[]{:S(2)}) collective-permute-start(bf16[64,512]{1,0:T(8,128)(2,1)S(1)} %get-tuple-element.120.refs_1_), channel_id=1, source_target_pairs={{0,24},{4,28},{8,16},{12,20},{16,8},{20,12},{24,0},{28,4},{1,25},{... | collective-permute-start | bytes 196616 | tf_op jit(solution)/shard_map/ppermute | solution.py:516
  44.9 9.0 %collective-permute-start.27 = (bf16[32,2048]{1,0:T(8,128)(2,1)S(1)}, bf16[32,2048]{1,0:T(8,128)(2,1)S(1)}, u32[]{:S(2)}, u32[]{:S(2)}) collective-permute-start(bf16[32,2048]{1,0:T(8,128)(2,1)S(1)} %get-tuple-element.124), channel_id=1, source_target_pairs={{0,8},{4,12},{8,0},{12,4},{16,24},{20,28},{24,16},{28,20},{1,9},{5... | collective-permute-start | bytes 393224 | tf_op jit(solution)/shard_map/ppermute | solution.py:516
  49.9 4.5 %collective-permute-start.29 = (bf16[128,512]{1,0:T(8,128)(2,1)S(1)}, bf16[128,512]{1,0:T(8,128)(2,1)S(1)}, u32[]{:S(2)}, u32[]{:S(2)}) collective-permute-start(bf16[128,512]{1,0:T(8,128)(2,1)S(1)} %get-tuple-element.128.refs_4_), channel_id=1, source_target_pairs={{0,16},{4,20},{8,24},{12,28},{16,0},{20,4},{24,8},{28,12},{1,17},{... | collective-permute-start | bytes 393224 | tf_op jit(solution)/shard_map/ppermute | solution.py:516
  50.1 8.2 %collective-permute-start.26 = (bf16[32,2048]{1,0:T(8,128)(2,1)S(1)}, bf16[32,2048]{1,0:T(8,128)(2,1)S(1)}, u32[]{:S(2)}, u32[]{:S(2)}) collective-permute-start(bf16[32,2048]{1,0:T(8,128)(2,1)S(1)} %get-tuple-element.123), channel_id=1, source_target_pairs={{0,4},{4,0},{8,12},{12,8},{16,20},{20,16},{24,28},{28,24},{1,5},{5... | collective-permute-start | bytes 393224 | tf_op jit(solution)/shard_map/ppermute | solution.py:516
  53.0 5.2 %collective-permute-start.28 = (bf16[16,2048]{1,0:T(8,128)(2,1)S(1)}, bf16[16,2048]{1,0:T(8,128)(2,1)S(1)}, u32[]{:S(2)}, u32[]{:S(2)}) collective-permute-start(bf16[16,2048]{1,0:T(8,128)(2,1)S(1)} %get-tuple-element.125), channel_id=1, source_target_pairs={{0,12},{4,8},{8,4},{12,0},{16,28},{20,24},{24,20},{28,16},{1,13},{... | collective-permute-start | bytes 196616 | tf_op jit(solution)/shard_map/ppermute | solution.py:516
  53.2 5.0 %collective-permute-start.25 = (bf16[16,2048]{1,0:T(8,128)(2,1)S(1)}, bf16[16,2048]{1,0:T(8,128)(2,1)S(1)}, u32[]{:S(2)}, u32[]{:S(2)}) collective-permute-start(bf16[16,2048]{1,0:T(8,128)(2,1)S(1)} %get-tuple-element.121), channel_id=1, source_target_pairs={{0,4},{4,0},{8,12},{12,8},{16,20},{20,16},{24,28},{28,24},{1,5},{5... | collective-permute-start | bytes 196616 | tf_op jit(solution)/shard_map/ppermute | solution.py:516
  54.7 4.4 %collective-permute-start.30 = (bf16[256,512]{1,0:T(8,128)(2,1)S(1)}, bf16[256,512]{1,0:T(8,128)(2,1)S(1)}, u32[]{:S(2)}, u32[]{:S(2)}) collective-permute-start(bf16[256,512]{1,0:T(8,128)(2,1)S(1)} %partial_other.1.refs_10_), channel_id=1, source_target_pairs={{0,4},{4,0},{8,12},{12,8},{16,20},{20,16},{24,28},{28,24},{1,5},{5... | collective-permute-start | bytes 786440 | tf_op jit(solution)/shard_map/ppermute | solution.py:516
  (1 other events, 3.8 us)

commit v21 on v18

--- a/solution.py
+++ b/solution.py
@@ -351,7 +351,7 @@
     copy(up_ref.at[rows], up_out_ref.at[pl.ds(0, BLOCK)])
     up_out_ref[BLOCK:, :] = jnp.zeros((16, up_out_ref.shape[1]), jnp.bfloat16)
     if block == 1:
-        rest[2][...] = rest[1][...]
+        copy(rest[1], rest[2])
         turn_kernel(rest[0], rest[3])
     for made in copies[:4]:
         made.wait()
@@ -362,7 +362,8 @@
     for k in range(half):
         first = pl.multiple_of(lax.bitwise_xor(at, k) * piece, piece)
         packed[k][...] = rows_ref[pl.ds(first, piece), :]
-    copies[4].wait()
+    for made in copies[4:]:
+        made.wait()
 
 
 def pack(block, half, piece, sources, weight=None, gain=None):
@@ -374,8 +375,8 @@
     outs = [jax.ShapeDtypeStruct((piece, width), bf16)] * half
     outs.append(jax.ShapeDtypeStruct((BLOCK + 16, model_width), bf16))
     if weight is not None:
-        operands += [near(weight), gain]
-        specs += [VMEM, VMEM]
+        operands += [near(weight), pltpu.with_memory_space_constraint(gain, pltpu.HBM)]
+        specs += [VMEM, pl.BlockSpec(memory_space=pltpu.HBM)]
         outs = [
             jax.ShapeDtypeStruct(gain.shape, gain.dtype),
             jax.ShapeDtypeStruct(weight.shape[::-1], bf16),
@@ -388,7 +389,7 @@
         scratch_shapes=[
             pltpu.VMEM(sources[-1].shape, jnp.int32),
             pltpu.VMEM((BLOCK, width), bf16),
-            pltpu.SemaphoreType.DMA((5,)),
+            pltpu.SemaphoreType.DMA((6,)),
         ],
         name="pack",
         **params(1.2),

time: 58.3 us -> 58.3 us (level)
  transfers between devices with their start and end apart: 31 -> 31, of which waited for: 12 -> 12; matrix products, arithmetic and copies ran while one was open for 0% -> 0% of each run, Pallas kernels for 13% -> 12%
where the time goes in v21:
time: 58.3 us; the launch traced here: 57.4 us
  starting transfers between devices  29.1 us (50%)
  waiting for transfers between devices  17.8 us (31%)
  Pallas kernels  9.44 us (16%)
  between operations  1.05 us (2%)
    ppermute x19, starting transfers between devices, swap(): return lax.ppermute(array, 'dp', [(i, i ^ k) for i in range(replicas)])  18.6 us
    ppermute x12, starting transfers between devices, direct(): lax.ppermute(unit[-1][0], 'section', hop)  10.5 us
    ppermute x19, waiting for transfers between devices, swap(): return lax.ppermute(array, 'dp', [(i, i ^ k) for i in range(replicas)])  10.5 us
    ppermute x12, waiting for transfers between devices, direct(): lax.ppermute(unit[-1][0], 'section', hop)  7.37 us
    pallas_call x16, Pallas kernels, tick_step(): pl.pallas_call(functools.partial(tick_kernel, tick, EARLY if low else LAT...  3.43 us
    pallas_call x2, Pallas kernels, pack(): pl.pallas_call(functools.partial(pack_kernel, block, half, piece), out_sh...  2.6 us
  transfers between devices with their start and end apart: 31, of which 12 were waited for; matrix products, arithmetic and copies ran while one was open for 0% of the time, Pallas kernels for 12%

profile of v21, /device:TPU:0, one launch (start us, length us, event | category | flops | bytes accessed | tf_op | source)
XLA Modules:
  0.0 57.4 jit_solution(9780009435647421835)
XLA Ops:
  0.6 1.4 %pack.2 = (bf16[16,4608]{1,0:T(8,128)(2,1)S(1)}, bf16[16,4608]{1,0:T(8,128)(2,1)S(1)}, bf16[16,4608]{1,0:T(8,128)(2,1)S(1)}, bf16[16,4608]{1,0:T(8,128)(2,1)S(1)}, bf16[80,2048]{1,0:T(8,128)(2,1)S(1)}) custom-call(bf16[128,2048]{1,0:T(8,128)(2,1)} %bitcast.8, bf16[128,512]{1,0:T(8,128)(2,1)} %bitcast.13, bf16[128,2048]{1,0:T(8,128)(2,1)} %bitcast.10, ...), custom_call_target="tpu_custom_call" | custom-call | flops 1380000000 | tf_op jit(solution)/shard_map/pack/pallas_call | solution.py:384
  2.5 2.6 %collective-permute-start.1 = (bf16[16,4608]{1,0:T(8,128)(2,1)S(1)}, bf16[16,4608]{1,0:T(8,128)(2,1)S(1)}, u32[]{:S(2)}, u32[]{:S(2)}) collective-permute-start(bf16[16,4608]{1,0:T(8,128)(2,1)S(1)} %get-tuple-element.71), channel_id=1, source_target_pairs={{0,8},{4,12},{8,0},{12,4},{16,24},{20,28},{24,16},{28,20},{1,9},{5... | collective-permute-start | bytes 442376 | tf_op jit(solution)/shard_map/ppermute | solution.py:522
  5.2 1.2 %pack.3 = (f32[1,2048]{1,0:T(1,128)S(1)}, bf16[512,2048]{1,0:T(8,128)(2,1)S(1)}, bf16[16,4608]{1,0:T(8,128)(2,1)S(1)}, bf16[16,4608]{1,0:T(8,128)(2,1)S(1)}, bf1...) custom-call(bf16[128,2048]{1,0:T(8,128)(2,1)} %bitcast.9, ...), custom_call_target="tpu_custom_call" | custom-call | flops 1380000000 | tf_op jit(solution)/shard_map/pack/pallas_call | solution.py:384
  6.4 1.8 %collective-permute-start.4 = (bf16[80,2048]{1,0:T(8,128)(2,1)S(1)}, bf16[80,2048]{1,0:T(8,128)(2,1)S(1)}, u32[]{:S(2)}, u32[]{:S(2)}) collective-permute-start(bf16[80,2048]{1,0:T(8,128)(2,1)S(1)} %get-tuple-element.79), channel_id=1, source_target_pairs={{0,16},{4,20},{8,24},{12,28},{16,0},{20,4},{24,8},{28,12},{1,17},{... | collective-permute-start | bytes 983048 | tf_op jit(solution)/shard_map/ppermute | solution.py:522
  8.3 1.5 %collective-permute-start.6 = (bf16[16,4608]{1,0:T(8,128)(2,1)S(1)}, bf16[16,4608]{1,0:T(8,128)(2,1)S(1)}, u32[]{:S(2)}, u32[]{:S(2)}) collective-permute-start(bf16[16,4608]{1,0:T(8,128)(2,1)S(1)} %get-tuple-element.82), channel_id=1, source_target_pairs={{0,8},{4,12},{8,0},{12,4},{16,24},{20,28},{24,16},{28,20},{1,9},{5... | collective-permute-start | bytes 442376 | tf_op jit(solution)/shard_map/ppermute | solution.py:522
  9.8 0.8 %collective-permute-start.7 = (bf16[16,4608]{1,0:T(8,128)(2,1)S(1)}, bf16[16,4608]{1,0:T(8,128)(2,1)S(1)}, u32[]{:S(2)}, u32[]{:S(2)}) collective-permute-start(bf16[16,4608]{1,0:T(8,128)(2,1)S(1)} %get-tuple-element.83), channel_id=1, source_target_pairs={{0,12},{4,8},{8,4},{12,0},{16,28},{20,24},{24,20},{28,16},{1,13},{... | collective-permute-start | bytes 442376 | tf_op jit(solution)/shard_map/ppermute | solution.py:522
  10.6 1.9 %collective-permute-done.2.refs_3_ = bf16[16,4608]{1,0:T(8,128)(2,1)S(1)} collective-permute-done((bf16[16,4608]{1,0:T(8,128)(2,1)S(1)}, bf16[16,4608]{1,0:T(8,128)(2,1)S(1)}, u32[]{:S(2)}, u32[]{:S(2)}) %collective-permute-start.2) | collective-permute-done | bytes 147488 | tf_op jit(solution)/shard_map/ppermute | solution.py:522
  12.8 0.7 %collective-permute-start.3 = (bf16[32,2048]{1,0:T(8,128)(2,1)S(1)}, bf16[32,2048]{1,0:T(8,128)(2,1)S(1)}, u32[]{:S(2)}, u32[]{:S(2)}) collective-permute-start(bf16[32,2048]{1,0:T(8,128)(2,1)S(1)} %get-tuple-element.78.refs_7_.refs_6_), channel_id=1, source_target_pairs={{3,2},{7,6},{11,10},{15,14},{19,18},{23,22},{27,26},{31,30}} | collective-permute-start | bytes 393224 | tf_op jit(solution)/shard_map/ppermute | solution.py:551
  13.5 0.7 %collective-permute-start.11 = (bf16[32,2048]{1,0:T(8,128)(2,1)S(1)}, bf16[32,2048]{1,0:T(8,128)(2,1)S(1)}, u32[]{:S(2)}, u32[]{:S(2)}) collective-permute-start(bf16[32,2048]{1,0:T(8,128)(2,1)S(1)} %get-tuple-element.85.refs_5_.refs_7_), channel_id=1, source_target_pairs={{3,2},{7,6},{11,10},{15,14},{19,18},{23,22},{27,26},{31,30}} | collective-permute-start | bytes 393224 | tf_op jit(solution)/shard_map/ppermute | solution.py:551
  14.2 1.9 %collective-permute-done.6.refs_2_ = bf16[16,4608]{1,0:T(8,128)(2,1)S(1)} collective-permute-done((bf16[16,4608]{1,0:T(8,128)(2,1)S(1)}, bf16[16,4608]{1,0:T(8,128)(2,1)S(1)}, u32[]{:S(2)}, u32[]{:S(2)}) %collective-permute-start.6) | collective-permute-done | bytes 147488 | tf_op jit(solution)/shard_map/ppermute | solution.py:522
  16.1 2.6 %collective-permute-done.7.refs_3_ = bf16[16,4608]{1,0:T(8,128)(2,1)S(1)} collective-permute-done((bf16[16,4608]{1,0:T(8,128)(2,1)S(1)}, bf16[16,4608]{1,0:T(8,128)(2,1)S(1)}, u32[]{:S(2)}, u32[]{:S(2)}) %collective-permute-start.7) | collective-permute-done | bytes 147488 | tf_op jit(solution)/shard_map/ppermute | solution.py:522
  19.1 0.7 %collective-permute-start.9 = (bf16[32,2048]{1,0:T(8,128)(2,1)S(1)}, bf16[32,2048]{1,0:T(8,128)(2,1)S(1)}, u32[]{:S(2)}, u32[]{:S(2)}) collective-permute-start(bf16[32,2048]{1,0:T(8,128)(2,1)S(1)} %get-tuple-element.90.refs_7_.refs_6_), channel_id=1, source_target_pairs={{3,2},{7,6},{11,10},{15,14},{19,18},{23,22},{27,26},{31,30}} | collective-permute-start | bytes 393224 | tf_op jit(solution)/shard_map/ppermute | solution.py:551
  21.2 0.7 %collective-permute-start.13 = (bf16[32,2048]{1,0:T(8,128)(2,1)S(1)}, bf16[32,2048]{1,0:T(8,128)(2,1)S(1)}, u32[]{:S(2)}, u32[]{:S(2)}) collective-permute-start(bf16[32,2048]{1,0:T(8,128)(2,1)S(1)} %get-tuple-element.93.refs_6_.refs_9_), channel_id=1, source_target_pairs={{2,1},{6,5},{10,9},{14,13},{18,17},{22,21},{26,25},{30,29}} | collective-permute-start | bytes 393224 | tf_op jit(solution)/shard_map/ppermute | solution.py:551
  23.5 2.6 %collective-permute-start.20 = (bf16[128,512]{1,0:T(8,128)(2,1)S(1)}, bf16[128,512]{1,0:T(8,128)(2,1)S(1)}, u32[]{:S(2)}, u32[]{:S(2)}) collective-permute-start(bf16[128,512]{1,0:T(8,128)(2,1)S(1)} %columns6.1), channel_id=1, source_target_pairs={{0,24},{4,28},{8,16},{12,20},{16,8},{20,12},{24,0},{28,4},{1,25},{... | collective-permute-start | bytes 393224 | tf_op jit(solution)/shard_map/ppermute | solution.py:522
  26.1 1.3 %collective-permute-start.12 = (bf16[32,2048]{1,0:T(8,128)(2,1)S(1)}, bf16[32,2048]{1,0:T(8,128)(2,1)S(1)}, u32[]{:S(2)}, u32[]{:S(2)}) collective-permute-start(bf16[32,2048]{1,0:T(8,128)(2,1)S(1)} %get-tuple-element.96.refs_7_.refs_10_), channel_id=1, source_target_pairs={{1,0},{5,4},{9,8},{13,12},{17,16},{21,20},{25,24},{29,28}} | collective-permute-start | bytes 393224 | tf_op jit(solution)/shard_map/ppermute | solution.py:551
  27.5 1.3 %collective-permute-start.14 = (bf16[32,2048]{1,0:T(8,128)(2,1)S(1)}, bf16[32,2048]{1,0:T(8,128)(2,1)S(1)}, u32[]{:S(2)}, u32[]{:S(2)}) collective-permute-start(bf16[32,2048]{1,0:T(8,128)(2,1)S(1)} %get-tuple-element.97.refs_6_.refs_11_), channel_id=1, source_target_pairs={{1,0},{5,4},{9,8},{13,12},{17,16},{21,20},{25,24},{29,28}} | collective-permute-start | bytes 393224 | tf_op jit(solution)/shard_map/ppermute | solution.py:551
  28.8 1.3 %collective-permute-start.18 = (bf16[32,2048]{1,0:T(8,128)(2,1)S(1)}, bf16[32,2048]{1,0:T(8,128)(2,1)S(1)}, u32[]{:S(2)}, u32[]{:S(2)}) collective-permute-start(bf16[32,2048]{1,0:T(8,128)(2,1)S(1)} %get-tuple-element.104.refs_7_.refs_10_), channel_id=1, source_target_pairs={{1,0},{5,4},{9,8},{13,12},{17,16},{21,20},{25,24},{29,28}} | collective-permute-start | bytes 393224 | tf_op jit(solution)/shard_map/ppermute | solution.py:551
  30.1 1.3 %collective-permute-start.19 = (bf16[32,2048]{1,0:T(8,128)(2,1)S(1)}, bf16[32,2048]{1,0:T(8,128)(2,1)S(1)}, u32[]{:S(2)}, u32[]{:S(2)}) collective-permute-start(bf16[32,2048]{1,0:T(8,128)(2,1)S(1)} %get-tuple-element.105.refs_12_.refs_0_.refs_11_), channel_id=1, source_target_pairs={{1,0},{5,4},{9,8},{13,12},{17,16},{21,20},{25,24},{29,28}} | collective-permute-start | bytes 393224 | tf_op jit(solution)/shard_map/ppermute | solution.py:551
  32.1 4.9 %collective-permute-done.12.refs_0_ = bf16[32,2048]{1,0:T(8,128)(2,1)S(1)} collective-permute-done((bf16[32,2048]{1,0:T(8,128)(2,1)S(1)}, bf16[32,2048]{1,0:T(8,128)(2,1)S(1)}, u32[]{:S(2)}, u32[]{:S(2)}) %collective-permute-start.12) | collective-permute-done | bytes 131104 | tf_op jit(solution)/shard_map/ppermute | solution.py:551
  37.0 0.8 %tick3_a_late.1 = (bf16[32,2048]{1,0:T(8,128)(2,1)S(1)}, bf16[32,512]{1,0:T(8,128)(2,1)S(1)}) custom-call(bf16[32,2048]{1,0:T(8,128)(2,1)S(1)} %collective-permute-done.12.refs_0_, bf16[4,32,128]{2,1,0:T(8,128)(2,1)S(1)} %get-tuple-element.73.refs_1_, f32[64,128]{1,0:T(8,128)S(1)} %get-tuple-element.74.refs_2_.refs_3_, ...), custom_call_target="tpu_custom_call" | custom-call | flops 1150000000 | tf_op jit(solution)/shard_map/tick3_a_late/pallas_call | solution.py:319
  37.8 2.0 %collective-permute-done.14.refs_1_ = bf16[32,2048]{1,0:T(8,128)(2,1)S(1)} collective-permute-done((bf16[32,2048]{1,0:T(8,128)(2,1)S(1)}, bf16[32,2048]{1,0:T(8,128)(2,1)S(1)}, u32[]{:S(2)}, u32[]{:S(2)}) %collective-permute-start.14) | collective-permute-done | bytes 131104 | tf_op jit(solution)/shard_map/ppermute | solution.py:551
  39.8 0.8 %tick3_a_early.1 = (bf16[32,2048]{1,0:T(8,128)(2,1)S(1)}, bf16[64,512]{1,0:T(8,128)(2,1)S(1)}, bf16[48,2048]{1,0:T(8,128)(2,1)S(1)}) custom-call(bf16[32,2048]{1,0:T(8,128)(2,1)S(1)} %collective-permute-done.12.refs_0_, bf16[32,2048]{1,0:T(8,128)(2,1)S(1)} %collective-permute-done.14.refs_1_, bf16[4,32,256]{2,1,0:T(8,128)(2,1)S(1)} %get-tuple-element.84.refs_2_, ...), custom_call_target="tpu_custom_call" | custom-call | flops 1150000000 | tf_op jit(solution)/shard_map/tick3_a_early/pallas_call | solution.py:319
  40.7 2.5 %collective-permute-start.23 = (bf16[64,512]{1,0:T(8,128)(2,1)S(1)}, bf16[64,512]{1,0:T(8,128)(2,1)S(1)}, u32[]{:S(2)}, u32[]{:S(2)}) collective-permute-start(bf16[64,512]{1,0:T(8,128)(2,1)S(1)} %get-tuple-element.118.refs_17_.refs_0_), channel_id=1, source_target_pairs={{0,24},{4,28},{8,16},{12,20},{16,8},{20,12},{24,0},{28,4},{1,25},{... | collective-permute-start | bytes 196616 | tf_op jit(solution)/shard_map/ppermute | solution.py:522
  44.2 0.8 %tick3_b_late.1 = (bf16[32,2048]{1,0:T(8,128)(2,1)S(1)}, bf16[32,512]{1,0:T(8,128)(2,1)S(1)}) custom-call(bf16[32,2048]{1,0:T(8,128)(2,1)S(1)} %collective-permute-done.18.refs_0_, bf16[4,32,128]{2,1,0:T(8,128)(2,1)S(1)} %get-tuple-element.89.refs_1_, f32[64,128]{1,0:T(8,128)S(1)} %get-tuple-element.87.refs_2_.refs_3_, ...), custom_call_target="tpu_custom_call" | custom-call | flops 1150000000 | tf_op jit(solution)/shard_map/tick3_b_late/pallas_call | solution.py:319
  45.4 0.9 %tick3_b_early.1 = (bf16[64,512]{1,0:T(8,128)(2,1)S(1)}, bf16[128,512]{1,0:T(8,128)(2,1)S(1)}, bf16[32,2048]{1,0:T(8,128)(2,1)S(1)}, bf16[32,2048]{1,0:T(8,128)(...) custom-call(bf16[32,2048]{1,0:T(8,128)(2,1)S(1)} %collective-permute-done.18.refs_0_, ...), custom_call_target="tpu_custom_call" | custom-call | flops 1150000000 | tf_op jit(solution)/shard_map/tick3_b_early/pallas_call | solution.py:319
  46.3 2.5 %collective-permute-start.24 = (bf16[64,512]{1,0:T(8,128)(2,1)S(1)}, bf16[64,512]{1,0:T(8,128)(2,1)S(1)}, u32[]{:S(2)}, u32[]{:S(2)}) collective-permute-start(bf16[64,512]{1,0:T(8,128)(2,1)S(1)} %get-tuple-element.120.refs_1_), channel_id=1, source_target_pairs={{0,24},{4,28},{8,16},{12,20},{16,8},{20,12},{24,0},{28,4},{1,25},{... | collective-permute-start | bytes 196616 | tf_op jit(solution)/shard_map/ppermute | solution.py:522
  50.7 0.8 %collective-permute-start.28 = (bf16[16,2048]{1,0:T(8,128)(2,1)S(1)}, bf16[16,2048]{1,0:T(8,128)(2,1)S(1)}, u32[]{:S(2)}, u32[]{:S(2)}) collective-permute-start(bf16[16,2048]{1,0:T(8,128)(2,1)S(1)} %get-tuple-element.125), channel_id=1, source_target_pairs={{0,12},{4,8},{8,4},{12,0},{16,28},{20,24},{24,20},{28,16},{1,13},{... | collective-permute-start | bytes 196616 | tf_op jit(solution)/shard_map/ppermute | solution.py:522
  51.5 0.8 %collective-permute-done.24.refs_4_.refs_9_ = bf16[64,512]{1,0:T(8,128)(2,1)S(1)} collective-permute-done((bf16[64,512]{1,0:T(8,128)(2,1)S(1)}, bf16[64,512]{1,0:T(8,128)(2,1)S(1)}, u32[]{:S(2)}, u32[]{:S(2)}) %collective-permute-start.24) | collective-permute-done | bytes 65568 | tf_op jit(solution)/shard_map/ppermute | solution.py:522
  52.4 1.2 %collective-permute-done.29.refs_7_ = bf16[64,512]{1,0:T(8,128)(2,1)S(1)} collective-permute-done((bf16[64,512]{1,0:T(8,128)(2,1)S(1)}, bf16[64,512]{1,0:T(8,128)(2,1)S(1)}, u32[]{:S(2)}, u32[]{:S(2)}) %collective-permute-start.29) | collective-permute-done | bytes 65568 | tf_op jit(solution)/shard_map/ppermute | solution.py:522
  53.6 0.8 %collective-permute-done.27.refs_2_.refs_6_ = bf16[32,2048]{1,0:T(8,128)(2,1)S(1)} collective-permute-done((bf16[32,2048]{1,0:T(8,128)(2,1)S(1)}, bf16[32,2048]{1,0:T(8,128)(2,1)S(1)}, u32[]{:S(2)}, u32[]{:S(2)}) %collective-permute-start.27) | collective-permute-done | bytes 131104 | tf_op jit(solution)/shard_map/ppermute | solution.py:522
  55.3 0.8 %rows.1 = (bf16[128,2048]{1,0:T(8,128)(2,1)}, f32[8,128]{1,0:T(8,128)S(1)}) custom-call(bf16[48,2048]{1,0:T(8,128)(2,1)S(1)} %collective-permute-done.17.refs_0_.first_rows_ref.refs_5_, bf16[16,2048]{1,0:T(8,128)(2,1)S(1)} %collective-permute-done.25.handed_ref, bf16[32,2048]{1,0:T(8,128)(2,1)S(1)} %get-tuple-element.122.refs_0_, ...), custom_call_target="tpu_custom_call" | custom-call | flops 2875000064 | tf_op jit(solution)/shard_map/rows/pallas_call | solution.py:596
  56.4 1.0 %finish.1 = (f32[256,512]{1,0:T(8,128)}, f32[1,256]{1,0:T(1,128)}) custom-call(f32[256,512]{1,0:T(8,128)S(1)} %partial_own.1.own_ref, bf16[256,512]{1,0:T(8,128)(2,1)S(1)} %collective-permute-done.30.other_ref, f32[256,512]{1,0:T(8,128)S(1)} %get-tuple-element.129.weight_ref, f32[256,128]{1,0:T(8,128)S(1)} %get-tuple-element.119.refs_1_.gain_ref, ...), custom_call_target="tpu_custom_call" | custom-call | tf_op jit(solution)/shard_map/finish/pallas_call | solution.py:607
  (61 shorter events, 9.6 us)
Async XLA Ops:
  0.6 4.5 %copy-start = (bf16[1,2048,512]{2,1,0:T(8,128)(2,1)S(1)}, bf16[1,2048,512]{2,1,0:T(8,128)(2,1)}, u32[]{:S(2)}) copy-start(bf16[1,2048,512]{2,1,0:T(8,128)(2,1)} %param.11) | copy-start | bytes 6291460
  2.0 6.3 %collective-permute-start = (bf16[16,4608]{1,0:T(8,128)(2,1)S(1)}, bf16[16,4608]{1,0:T(8,128)(2,1)S(1)}, u32[]{:S(2)}, u32[]{:S(2)}) collective-permute-start(bf16[16,4608]{1,0:T(8,128)(2,1)S(1)} %get-tuple-element.70), channel_id=1, source_target_pairs={{0,4},{4,0},{8,12},{12,8},{16,20},{20,16},{24,28},{28,24},{1,5},{5... | collective-permute-start | bytes 442376 | tf_op jit(solution)/shard_map/ppermute | solution.py:522
  2.5 7.3 %collective-permute-start.1 = (bf16[16,4608]{1,0:T(8,128)(2,1)S(1)}, bf16[16,4608]{1,0:T(8,128)(2,1)S(1)}, u32[]{:S(2)}, u32[]{:S(2)}) collective-permute-start(bf16[16,4608]{1,0:T(8,128)(2,1)S(1)} %get-tuple-element.71), channel_id=1, source_target_pairs={{0,8},{4,12},{8,0},{12,4},{16,24},{20,28},{24,16},{28,20},{1,9},{5... | collective-permute-start | bytes 442376 | tf_op jit(solution)/shard_map/ppermute | solution.py:522
  5.1 7.3 %collective-permute-start.2 = (bf16[16,4608]{1,0:T(8,128)(2,1)S(1)}, bf16[16,4608]{1,0:T(8,128)(2,1)S(1)}, u32[]{:S(2)}, u32[]{:S(2)}) collective-permute-start(bf16[16,4608]{1,0:T(8,128)(2,1)S(1)} %get-tuple-element.72), channel_id=1, source_target_pairs={{0,12},{4,8},{8,4},{12,0},{16,28},{20,24},{24,20},{28,16},{1,13},{... | collective-permute-start | bytes 442376 | tf_op jit(solution)/shard_map/ppermute | solution.py:522
  6.4 12.4 %collective-permute-start.4 = (bf16[80,2048]{1,0:T(8,128)(2,1)S(1)}, bf16[80,2048]{1,0:T(8,128)(2,1)S(1)}, u32[]{:S(2)}, u32[]{:S(2)}) collective-permute-start(bf16[80,2048]{1,0:T(8,128)(2,1)S(1)} %get-tuple-element.79), channel_id=1, source_target_pairs={{0,16},{4,20},{8,24},{12,28},{16,0},{20,4},{24,8},{28,12},{1,17},{... | collective-permute-start | bytes 983048 | tf_op jit(solution)/shard_map/ppermute | solution.py:522
  8.2 5.3 %collective-permute-start.5 = (bf16[16,4608]{1,0:T(8,128)(2,1)S(1)}, bf16[16,4608]{1,0:T(8,128)(2,1)S(1)}, u32[]{:S(2)}, u32[]{:S(2)}) collective-permute-start(bf16[16,4608]{1,0:T(8,128)(2,1)S(1)} %get-tuple-element.81), channel_id=1, source_target_pairs={{0,4},{4,0},{8,12},{12,8},{16,20},{20,16},{24,28},{28,24},{1,5},{5... | collective-permute-start | bytes 442376 | tf_op jit(solution)/shard_map/ppermute | solution.py:522
  8.3 7.8 %collective-permute-start.6 = (bf16[16,4608]{1,0:T(8,128)(2,1)S(1)}, bf16[16,4608]{1,0:T(8,128)(2,1)S(1)}, u32[]{:S(2)}, u32[]{:S(2)}) collective-permute-start(bf16[16,4608]{1,0:T(8,128)(2,1)S(1)} %get-tuple-element.82), channel_id=1, source_target_pairs={{0,8},{4,12},{8,0},{12,4},{16,24},{20,28},{24,16},{28,20},{1,9},{5... | collective-permute-start | bytes 442376 | tf_op jit(solution)/shard_map/ppermute | solution.py:522
  9.8 9.0 %collective-permute-start.7 = (bf16[16,4608]{1,0:T(8,128)(2,1)S(1)}, bf16[16,4608]{1,0:T(8,128)(2,1)S(1)}, u32[]{:S(2)}, u32[]{:S(2)}) collective-permute-start(bf16[16,4608]{1,0:T(8,128)(2,1)S(1)} %get-tuple-element.83), channel_id=1, source_target_pairs={{0,12},{4,8},{8,4},{12,0},{16,28},{20,24},{24,20},{28,16},{1,13},{... | collective-permute-start | bytes 442376 | tf_op jit(solution)/shard_map/ppermute | solution.py:522
  12.8 7.7 %collective-permute-start.3 = (bf16[32,2048]{1,0:T(8,128)(2,1)S(1)}, bf16[32,2048]{1,0:T(8,128)(2,1)S(1)}, u32[]{:S(2)}, u32[]{:S(2)}) collective-permute-start(bf16[32,2048]{1,0:T(8,128)(2,1)S(1)} %get-tuple-element.78.refs_7_.refs_6_), channel_id=1, source_target_pairs={{3,2},{7,6},{11,10},{15,14},{19,18},{23,22},{27,26},{31,30}} | collective-permute-start | bytes 393224 | tf_op jit(solution)/shard_map/ppermute | solution.py:551
  13.5 7.7 %collective-permute-start.11 = (bf16[32,2048]{1,0:T(8,128)(2,1)S(1)}, bf16[32,2048]{1,0:T(8,128)(2,1)S(1)}, u32[]{:S(2)}, u32[]{:S(2)}) collective-permute-start(bf16[32,2048]{1,0:T(8,128)(2,1)S(1)} %get-tuple-element.85.refs_5_.refs_7_), channel_id=1, source_target_pairs={{3,2},{7,6},{11,10},{15,14},{19,18},{23,22},{27,26},{31,30}} | collective-permute-start | bytes 393224 | tf_op jit(solution)/shard_map/ppermute | solution.py:551
  19.1 2.8 %collective-permute-start.9 = (bf16[32,2048]{1,0:T(8,128)(2,1)S(1)}, bf16[32,2048]{1,0:T(8,128)(2,1)S(1)}, u32[]{:S(2)}, u32[]{:S(2)}) collective-permute-start(bf16[32,2048]{1,0:T(8,128)(2,1)S(1)} %get-tuple-element.90.refs_7_.refs_6_), channel_id=1, source_target_pairs={{3,2},{7,6},{11,10},{15,14},{19,18},{23,22},{27,26},{31,30}} | collective-permute-start | bytes 393224 | tf_op jit(solution)/shard_map/ppermute | solution.py:551
  19.8 2.8 %collective-permute-start.10 = (bf16[32,2048]{1,0:T(8,128)(2,1)S(1)}, bf16[32,2048]{1,0:T(8,128)(2,1)S(1)}, u32[]{:S(2)}, u32[]{:S(2)}) collective-permute-start(bf16[32,2048]{1,0:T(8,128)(2,1)S(1)} %get-tuple-element.91.refs_6_.refs_7_), channel_id=1, source_target_pairs={{3,2},{7,6},{11,10},{15,14},{19,18},{23,22},{27,26},{31,30}} | collective-permute-start | bytes 393224 | tf_op jit(solution)/shard_map/ppermute | solution.py:551
  20.5 5.6 %collective-permute-start.8 = (bf16[32,2048]{1,0:T(8,128)(2,1)S(1)}, bf16[32,2048]{1,0:T(8,128)(2,1)S(1)}, u32[]{:S(2)}, u32[]{:S(2)}) collective-permute-start(bf16[32,2048]{1,0:T(8,128)(2,1)S(1)} %get-tuple-element.92.refs_7_.refs_8_), channel_id=1, source_target_pairs={{2,1},{6,5},{10,9},{14,13},{18,17},{22,21},{26,25},{30,29}} | collective-permute-start | bytes 393224 | tf_op jit(solution)/shard_map/ppermute | solution.py:551
  21.2 6.2 %collective-permute-start.13 = (bf16[32,2048]{1,0:T(8,128)(2,1)S(1)}, bf16[32,2048]{1,0:T(8,128)(2,1)S(1)}, u32[]{:S(2)}, u32[]{:S(2)}) collective-permute-start(bf16[32,2048]{1,0:T(8,128)(2,1)S(1)} %get-tuple-element.93.refs_6_.refs_9_), channel_id=1, source_target_pairs={{2,1},{6,5},{10,9},{14,13},{18,17},{22,21},{26,25},{30,29}} | collective-permute-start | bytes 393224 | tf_op jit(solution)/shard_map/ppermute | solution.py:551
  21.9 6.8 %collective-permute-start.15 = (bf16[32,2048]{1,0:T(8,128)(2,1)S(1)}, bf16[32,2048]{1,0:T(8,128)(2,1)S(1)}, u32[]{:S(2)}, u32[]{:S(2)}) collective-permute-start(bf16[32,2048]{1,0:T(8,128)(2,1)S(1)} %get-tuple-element.94.refs_7_.refs_8_), channel_id=1, source_target_pairs={{2,1},{6,5},{10,9},{14,13},{18,17},{22,21},{26,25},{30,29}} | collective-permute-start | bytes 393224 | tf_op jit(solution)/shard_map/ppermute | solution.py:551
  22.7 7.4 %collective-permute-start.16 = (bf16[32,2048]{1,0:T(8,128)(2,1)S(1)}, bf16[32,2048]{1,0:T(8,128)(2,1)S(1)}, u32[]{:S(2)}, u32[]{:S(2)}) collective-permute-start(bf16[32,2048]{1,0:T(8,128)(2,1)S(1)} %get-tuple-element.95.refs_6_.after_ref.refs_0_.refs_9_), channel_id=1, source_target_pairs={{2,1},{6,5},{10,9},{14,13},{18,17},{22,21},{26,25},{30,29}} | collective-permute-start | bytes 393224 | tf_op jit(solution)/shard_map/ppermute | solution.py:551
  23.5 7.9 %collective-permute-start.20 = (bf16[128,512]{1,0:T(8,128)(2,1)S(1)}, bf16[128,512]{1,0:T(8,128)(2,1)S(1)}, u32[]{:S(2)}, u32[]{:S(2)}) collective-permute-start(bf16[128,512]{1,0:T(8,128)(2,1)S(1)} %columns6.1), channel_id=1, source_target_pairs={{0,24},{4,28},{8,16},{12,20},{16,8},{20,12},{24,0},{28,4},{1,25},{... | collective-permute-start | bytes 393224 | tf_op jit(solution)/shard_map/ppermute | solution.py:522
  26.1 10.9 %collective-permute-start.12 = (bf16[32,2048]{1,0:T(8,128)(2,1)S(1)}, bf16[32,2048]{1,0:T(8,128)(2,1)S(1)}, u32[]{:S(2)}, u32[]{:S(2)}) collective-permute-start(bf16[32,2048]{1,0:T(8,128)(2,1)S(1)} %get-tuple-element.96.refs_7_.refs_10_), channel_id=1, source_target_pairs={{1,0},{5,4},{9,8},{13,12},{17,16},{21,20},{25,24},{29,28}} | collective-permute-start | bytes 393224 | tf_op jit(solution)/shard_map/ppermute | solution.py:551
  27.5 12.3 %collective-permute-start.14 = (bf16[32,2048]{1,0:T(8,128)(2,1)S(1)}, bf16[32,2048]{1,0:T(8,128)(2,1)S(1)}, u32[]{:S(2)}, u32[]{:S(2)}) collective-permute-start(bf16[32,2048]{1,0:T(8,128)(2,1)S(1)} %get-tuple-element.97.refs_6_.refs_11_), channel_id=1, source_target_pairs={{1,0},{5,4},{9,8},{13,12},{17,16},{21,20},{25,24},{29,28}} | collective-permute-start | bytes 393224 | tf_op jit(solution)/shard_map/ppermute | solution.py:551
  28.8 14.9 %collective-permute-start.18 = (bf16[32,2048]{1,0:T(8,128)(2,1)S(1)}, bf16[32,2048]{1,0:T(8,128)(2,1)S(1)}, u32[]{:S(2)}, u32[]{:S(2)}) collective-permute-start(bf16[32,2048]{1,0:T(8,128)(2,1)S(1)} %get-tuple-element.104.refs_7_.refs_10_), channel_id=1, source_target_pairs={{1,0},{5,4},{9,8},{13,12},{17,16},{21,20},{25,24},{29,28}} | collective-permute-start | bytes 393224 | tf_op jit(solution)/shard_map/ppermute | solution.py:551
  30.1 15.3 %collective-permute-start.19 = (bf16[32,2048]{1,0:T(8,128)(2,1)S(1)}, bf16[32,2048]{1,0:T(8,128)(2,1)S(1)}, u32[]{:S(2)}, u32[]{:S(2)}) collective-permute-start(bf16[32,2048]{1,0:T(8,128)(2,1)S(1)} %get-tuple-element.105.refs_12_.refs_0_.refs_11_), channel_id=1, source_target_pairs={{1,0},{5,4},{9,8},{13,12},{17,16},{21,20},{25,24},{29,28}} | collective-permute-start | bytes 393224 | tf_op jit(solution)/shard_map/ppermute | solution.py:551
  31.5 14.0 %collective-permute-start.21 = (bf16[128,512]{1,0:T(8,128)(2,1)S(1)}, bf16[128,512]{1,0:T(8,128)(2,1)S(1)}, u32[]{:S(2)}, u32[]{:S(2)}) collective-permute-start(bf16[128,512]{1,0:T(8,128)(2,1)S(1)} %columns2.1), channel_id=1, source_target_pairs={{0,8},{4,12},{8,0},{12,4},{16,24},{20,28},{24,16},{28,20},{1,9},{5... | collective-permute-start | bytes 393224 | tf_op jit(solution)/shard_map/ppermute | solution.py:522
  40.7 8.7 %collective-permute-start.23 = (bf16[64,512]{1,0:T(8,128)(2,1)S(1)}, bf16[64,512]{1,0:T(8,128)(2,1)S(1)}, u32[]{:S(2)}, u32[]{:S(2)}) collective-permute-start(bf16[64,512]{1,0:T(8,128)(2,1)S(1)} %get-tuple-element.118.refs_17_.refs_0_), channel_id=1, source_target_pairs={{0,24},{4,28},{8,16},{12,20},{16,8},{20,12},{24,0},{28,4},{1,25},{... | collective-permute-start | bytes 196616 | tf_op jit(solution)/shard_map/ppermute | solution.py:522
  43.2 6.9 %collective-permute-start.17 = (bf16[48,2048]{1,0:T(8,128)(2,1)S(1)}, bf16[48,2048]{1,0:T(8,128)(2,1)S(1)}, u32[]{:S(2)}, u32[]{:S(2)}) collective-permute-start(bf16[48,2048]{1,0:T(8,128)(2,1)S(1)} %get-tuple-element.108), channel_id=1, source_target_pairs={{0,8},{4,12},{8,0},{12,4},{16,24},{20,28},{24,16},{28,20},{1,9},{5... | collective-permute-start | bytes 589832 | tf_op jit(solution)/shard_map/ppermute | solution.py:522
  43.7 7.0 %collective-permute-start.22 = (bf16[192,512]{1,0:T(8,128)(2,1)S(1)}, bf16[192,512]{1,0:T(8,128)(2,1)S(1)}, u32[]{:S(2)}, u32[]{:S(2)}) collective-permute-start(bf16[192,512]{1,0:T(8,128)(2,1)S(1)} %columns4.1), channel_id=1, source_target_pairs={{0,16},{4,20},{8,24},{12,28},{16,0},{20,4},{24,8},{28,12},{1,17},{... | collective-permute-start | bytes 589832 | tf_op jit(solution)/shard_map/ppermute | solution.py:522
  46.3 5.9 %collective-permute-start.24 = (bf16[64,512]{1,0:T(8,128)(2,1)S(1)}, bf16[64,512]{1,0:T(8,128)(2,1)S(1)}, u32[]{:S(2)}, u32[]{:S(2)}) collective-permute-start(bf16[64,512]{1,0:T(8,128)(2,1)S(1)} %get-tuple-element.120.refs_1_), channel_id=1, source_target_pairs={{0,24},{4,28},{8,16},{12,20},{16,8},{20,12},{24,0},{28,4},{1,25},{... | collective-permute-start | bytes 196616 | tf_op jit(solution)/shard_map/ppermute | solution.py:522
  48.8 5.7 %collective-permute-start.27 = (bf16[32,2048]{1,0:T(8,128)(2,1)S(1)}, bf16[32,2048]{1,0:T(8,128)(2,1)S(1)}, u32[]{:S(2)}, u32[]{:S(2)}) collective-permute-start(bf16[32,2048]{1,0:T(8,128)(2,1)S(1)} %get-tuple-element.124), channel_id=1, source_target_pairs={{0,8},{4,12},{8,0},{12,4},{16,24},{20,28},{24,16},{28,20},{1,9},{5... | collective-permute-start | bytes 393224 | tf_op jit(solution)/shard_map/ppermute | solution.py:522
  49.3 4.3 %collective-permute-start.29 = (bf16[64,512]{1,0:T(8,128)(2,1)S(1)}, bf16[64,512]{1,0:T(8,128)(2,1)S(1)}, u32[]{:S(2)}, u32[]{:S(2)}) collective-permute-start(bf16[64,512]{1,0:T(8,128)(2,1)S(1)} %get-tuple-element.120.refs_1_), channel_id=1, source_target_pairs={{0,16},{4,20},{8,24},{12,28},{16,0},{20,4},{24,8},{28,12},{1,17},{... | collective-permute-start | bytes 196616 | tf_op jit(solution)/shard_map/ppermute | solution.py:522
  50.0 5.2 %collective-permute-start.26 = (bf16[32,2048]{1,0:T(8,128)(2,1)S(1)}, bf16[32,2048]{1,0:T(8,128)(2,1)S(1)}, u32[]{:S(2)}, u32[]{:S(2)}) collective-permute-start(bf16[32,2048]{1,0:T(8,128)(2,1)S(1)} %get-tuple-element.123), channel_id=1, source_target_pairs={{0,4},{4,0},{8,12},{12,8},{16,20},{20,16},{24,28},{28,24},{1,5},{5... | collective-permute-start | bytes 393224 | tf_op jit(solution)/shard_map/ppermute | solution.py:522
  50.7 4.5 %collective-permute-start.28 = (bf16[16,2048]{1,0:T(8,128)(2,1)S(1)}, bf16[16,2048]{1,0:T(8,128)(2,1)S(1)}, u32[]{:S(2)}, u32[]{:S(2)}) collective-permute-start(bf16[16,2048]{1,0:T(8,128)(2,1)S(1)} %get-tuple-element.125), channel_id=1, source_target_pairs={{0,12},{4,8},{8,4},{12,0},{16,28},{20,24},{24,20},{28,16},{1,13},{... | collective-permute-start | bytes 196616 | tf_op jit(solution)/shard_map/ppermute | solution.py:522
  52.2 3.0 %collective-permute-start.25 = (bf16[16,2048]{1,0:T(8,128)(2,1)S(1)}, bf16[16,2048]{1,0:T(8,128)(2,1)S(1)}, u32[]{:S(2)}, u32[]{:S(2)}) collective-permute-start(bf16[16,2048]{1,0:T(8,128)(2,1)S(1)} %get-tuple-element.121), channel_id=1, source_target_pairs={{0,4},{4,0},{8,12},{12,8},{16,20},{20,16},{24,28},{28,24},{1,5},{5... | collective-permute-start | bytes 196616 | tf_op jit(solution)/shard_map/ppermute | solution.py:522
  54.8 1.6 %collective-permute-start.30 = (bf16[256,512]{1,0:T(8,128)(2,1)S(1)}, bf16[256,512]{1,0:T(8,128)(2,1)S(1)}, u32[]{:S(2)}, u32[]{:S(2)}) collective-permute-start(bf16[256,512]{1,0:T(8,128)(2,1)S(1)} %partial_other.1.refs_10_), channel_id=1, source_target_pairs={{0,4},{4,0},{8,12},{12,8},{16,20},{20,16},{24,28},{28,24},{1,5},{5... | collective-permute-start | bytes 786440 | tf_op jit(solution)/shard_map/ppermute | solution.py:522
